TPU v7x, 32 devices: a whole 2x2x4 slice. The times are simulated.
32 devices in a mesh: dom: 2 (over x), col: 4 (over y, core), row: 4 (over z).
Axes of the slice: x: 2, y: 2, z: 4, core: 2. Of those that a mesh axis runs over, the one named last changes fastest.
Arguments:
- vectors: bfloat16 [4096, 512], P(('col', 'row'), 'dom'), parts along dimension 1, may hold values from -6 to 6
- blocks: bfloat16 [8, 4, 16, 128, 128], P(('dom', 'col'), 'row'), parts along dimension 0, may hold values from -0.0625 to 0.0625
- cols: int32 [8, 4, 16], P(('dom', 'col'), 'row'), parts along dimension 0, may hold values from 0 to 7
Outputs:
- last: float32 [4096, 512], P(('col', 'row'), 'dom'), parts along dimension 1
- before: float32 [4096, 512], P(('col', 'row'), 'dom'), parts along dimension 1
There are 2 independent parts, one for each index of `dom`. A program takes and returns all parts, laid end to end along the dimension named above; each array names one. Nothing has to cross between parts.
All inputs are finite; a program needn't handle non-finite values.
Results may differ from a plain program's by a relative error of at most 0.025.
Values may be sent and summed in bfloat16 or wider, within the bound.
No kernel may reach another device: no remote copies, remote signals or barrier semaphores. Data moves between devices by JAX's collectives and lax.ppermute only.
A program may use at most 64 MiB of HBM per device.

v0:
```python
import jax
import jax.numpy as jnp
from jax import lax
from jax.sharding import PartitionSpec as P

PER_ROW = 2
DEG = 4


def onehot_sum(selected, high_part, low_part):
    first = jnp.einsum("su,sok->uok", selected, high_part, preferred_element_type=jnp.float32)
    second = jnp.einsum("su,sok->uok", selected, low_part, preferred_element_type=jnp.float32)
    return first + second


def apply_pair(send, grouped, col_ids, onehot):
    tile_rows, per_row, orb, _ = grouped.shape
    piece_rows, width = send.shape
    tile_cols = onehot.shape[1]
    wide = lax.all_gather(send, "col", axis=0, tiled=True).reshape(tile_cols, orb, width)
    picked = jnp.take(wide, col_ids, axis=0).reshape(tile_rows, per_row, orb, width)
    direct = jnp.einsum("tpio,tpok->tik", grouped, picked, preferred_element_type=jnp.float32)
    part_rows = lax.psum_scatter(
        direct.reshape(tile_rows * orb, width).astype(jnp.bfloat16),
        "row",
        scatter_dimension=0,
        tiled=True,
    ).astype(jnp.float32)
    tall = lax.all_gather(send, "row", axis=0, tiled=True).reshape(tile_rows, orb, width)
    mirrored = jnp.einsum("tpio,tik->tpok", grouped, tall, preferred_element_type=jnp.float32)
    mirrored = mirrored.reshape(tile_rows * per_row, orb, width)
    high_part = mirrored.astype(jnp.bfloat16)
    low_part = (mirrored - high_part.astype(jnp.float32)).astype(jnp.bfloat16)
    summed = onehot_sum(onehot, high_part, low_part)
    part_cols = lax.psum_scatter(
        summed.reshape(tile_cols * orb, width).astype(jnp.bfloat16),
        "col",
        scatter_dimension=0,
        tiled=True,
    ).astype(jnp.float32)
    return part_rows + part_cols


def per_device(vectors, blocks, cols):
    tiles = blocks[0, 0]
    col_ids = cols[0, 0]
    slots, orb, _ = tiles.shape
    tile_rows = slots // PER_ROW
    tile_cols = lax.axis_size("col") * (vectors.shape[0] // orb)
    grouped = tiles.reshape(tile_rows, PER_ROW, orb, orb)
    onehot = (col_ids[:, None] == jnp.arange(tile_cols, dtype=jnp.int32)[None, :]).astype(
        jnp.bfloat16
    )
    prev = vectors.astype(jnp.float32)
    now = apply_pair(vectors, grouped, col_ids, onehot)
    for step in range(DEG - 1):
        nxt = 2.0 * apply_pair(now.astype(jnp.bfloat16), grouped, col_ids, onehot) - prev
        prev, now = (now, nxt)
    return (now, prev)


def solution(mesh):
    return jax.shard_map(
        per_device,
        mesh=mesh,
        in_specs=(
            P(("col", "row"), "dom"),
            P(("dom", "col"), "row", None, None, None),
            P(("dom", "col"), "row", None),
        ),
        out_specs=(P(("col", "row"), "dom"), P(("col", "row"), "dom")),
        check_vma=False,
    )
```

profile of v0, /device:TPU:0, one launch (start us, length us, event | category | flops | bytes accessed | tf_op | source)
XLA Modules:
  0.0 253.9 jit_solution(9700152727667451719)
XLA Ops:
  8.6 8.8 %all_gather.24 = bf16[1024,256]{1,0:T(8,128)(2,1)S(1)} all-gather(bf16[256,256]{1,0:T(8,128)(2,1)} %param.5), channel_id=1, replica_groups=mesh['dom'=2,'col'=4,'row'=4] {'col'}, dimensions={0}, use_global_device_ids=true | all-gather | bytes 655360 | tf_op jit(solution)/shard_map/all_gather | solution.py:20
  19.5 21.2 %all_gather.25 = bf16[1024,256]{1,0:T(8,128)(2,1)S(1)} all-gather(bf16[256,256]{1,0:T(8,128)(2,1)S(1)} %copy-done.1), channel_id=1, replica_groups=mesh['dom'=2,'col'=4,'row'=4] {'row'}, dimensions={0}, use_global_device_ids=true | all-gather | bytes 655360 | tf_op jit(solution)/shard_map/all_gather | solution.py:29
  41.2 1.2 fusion.10
  42.4 1.2 fusion.2
  45.0 23.7 %reduce-scatter.11.cloned.1.call-done = bf16[256,256]{1,0:T(8,128)(2,1)} async-done(((bf16[1024,256]{1,0:T(8,128)(2,1)}), bf16[256,256]{1,0:T(8,128)(2,1)}) %reduce-scatter.11.cloned.1.call-update) | async-done | bytes 131088 | tf_op jit(solution)/shard_map/reduce_scatter | solution.py:35
  69.7 6.8 %all_gather.26 = bf16[1024,256]{1,0:T(8,128)(2,1)S(1)} all-gather(bf16[256,256]{1,0:T(8,128)(2,1)S(1)} %fusion.20), channel_id=1, replica_groups=mesh['dom'=2,'col'=4,'row'=4] {'col'}, dimensions={0}, use_global_device_ids=true | all-gather | bytes 655360 | tf_op jit(solution)/shard_map/all_gather | solution.py:20
  77.3 1.2 fusion.7
  78.5 21.1 %all_gather.27 = bf16[1024,256]{1,0:T(8,128)(2,1)S(1)} all-gather(bf16[256,256]{1,0:T(8,128)(2,1)S(1)} %fusion.20), channel_id=1, replica_groups=mesh['dom'=2,'col'=4,'row'=4] {'row'}, dimensions={0}, use_global_device_ids=true | all-gather | bytes 655360 | tf_op jit(solution)/shard_map/all_gather | solution.py:29
  99.7 1.8 fusion.41
  101.5 2.2 copy.19
  105.4 22.0 %reduce-scatter.15.cloned.1.call-done = bf16[256,256]{1,0:T(8,128)(2,1)} async-done(((bf16[1024,256]{1,0:T(8,128)(2,1)}), bf16[256,256]{1,0:T(8,128)(2,1)}) %reduce-scatter.15.cloned.1.call-update) | async-done | bytes 131088 | tf_op jit(solution)/shard_map/reduce_scatter | solution.py:35
  128.4 6.8 %all_gather.28 = bf16[1024,256]{1,0:T(8,128)(2,1)S(1)} all-gather(bf16[256,256]{1,0:T(8,128)(2,1)S(1)} %fusion.21), channel_id=1, replica_groups=mesh['dom'=2,'col'=4,'row'=4] {'col'}, dimensions={0}, use_global_device_ids=true | all-gather | bytes 655360 | tf_op jit(solution)/shard_map/all_gather | solution.py:20
  137.2 21.2 %all_gather.29 = bf16[1024,256]{1,0:T(8,128)(2,1)S(1)} all-gather(bf16[256,256]{1,0:T(8,128)(2,1)S(1)} %fusion.21), channel_id=1, replica_groups=mesh['dom'=2,'col'=4,'row'=4] {'row'}, dimensions={0}, use_global_device_ids=true | all-gather | bytes 655360 | tf_op jit(solution)/shard_map/all_gather | solution.py:29
  158.4 1.8 fusion.42
  160.2 2.2 copy.23
  164.1 21.8 %reduce-scatter.19.cloned.1.call-done = bf16[256,256]{1,0:T(8,128)(2,1)} async-done(((bf16[1024,256]{1,0:T(8,128)(2,1)}), bf16[256,256]{1,0:T(8,128)(2,1)}) %reduce-scatter.19.cloned.1.call-update) | async-done | bytes 131088 | tf_op jit(solution)/shard_map/reduce_scatter | solution.py:35
  185.8 1.7 fusion.39
  187.6 6.7 %all_gather.30 = bf16[1024,256]{1,0:T(8,128)(2,1)S(1)} all-gather(bf16[256,256]{1,0:T(8,128)(2,1)S(1)} %get-tuple-element.3), channel_id=1, replica_groups=mesh['dom'=2,'col'=4,'row'=4] {'col'}, dimensions={0}, use_global_device_ids=true | all-gather | bytes 655360 | tf_op jit(solution)/shard_map/all_gather | solution.py:20
  195.1 1.2 fusion.9
  196.3 21.1 %all_gather.31 = bf16[1024,256]{1,0:T(8,128)(2,1)S(1)} all-gather(bf16[256,256]{1,0:T(8,128)(2,1)S(1)} %get-tuple-element.3), channel_id=1, replica_groups=mesh['dom'=2,'col'=4,'row'=4] {'row'}, dimensions={0}, use_global_device_ids=true | all-gather | bytes 655360 | tf_op jit(solution)/shard_map/all_gather | solution.py:29
  217.5 1.8 fusion.43
  219.3 2.2 copy.27
  223.1 22.2 %reduce-scatter.23.cloned.1.call-done = bf16[256,256]{1,0:T(8,128)(2,1)} async-done(((bf16[1024,256]{1,0:T(8,128)(2,1)}), bf16[256,256]{1,0:T(8,128)(2,1)}) %reduce-scatter.23.cloned.1.call-update) | async-done | bytes 131088 | tf_op jit(solution)/shard_map/reduce_scatter | solution.py:35
  245.3 1.8 multiply_subtract_fusion
  (60 shorter events, 15.6 us)
Async XLA Ops:
  7.2 11.1 %copy-start = (bf16[1,1,16,128,128]{4,3,2,1,0:T(8,128)(2,1)S(1)}, bf16[1,1,16,128,128]{4,3,2,1,0:T(8,128)(2,1)}, u32[]{:S(2)}) copy-start(bf16[1,1,16,128,128]{4,3,2,1,0:T(8,128)(2,1)} %param.6) | copy-start | bytes 1572868
  7.2 37.8 %reduce-scatter.9.cloned.1.call-start = ((), (), s32[]{:S(2)}) async-start(), calls=%async_computation.8 | async-start | bytes 655360 | tf_op jit(solution)/shard_map/reduce_scatter | solution.py:23
  18.1 1.4 copy-start.1
  19.4 21.8 %copy-start.6 = (s32[1,1,16]{2,1,0:T(1,128)S(1)}, s32[1,1,16]{2,1,0:T(1,128)}, u32[]{:S(2)}) copy-start(s32[1,1,16]{2,1,0:T(1,128)} %param.7) | copy-start | bytes 196
  19.4 49.3 %reduce-scatter.11.cloned.1.call-start = ((), (), s32[]{:S(2)}) async-start(), calls=%async_computation.9 | async-start | bytes 655360 | tf_op jit(solution)/shard_map/reduce_scatter | solution.py:35
  44.6 60.8 %reduce-scatter.13.cloned.1.call-start = ((), (), s32[]{:S(2)}) async-start(), calls=%async_computation.10 | async-start | bytes 655360 | tf_op jit(solution)/shard_map/reduce_scatter | solution.py:23
  78.5 48.9 %reduce-scatter.15.cloned.1.call-start = ((), (), s32[]{:S(2)}) async-start(), calls=%async_computation.11 | async-start | bytes 655360 | tf_op jit(solution)/shard_map/reduce_scatter | solution.py:35
  105.3 58.8 %reduce-scatter.17.cloned.1.call-start = ((), (), s32[]{:S(2)}) async-start(), calls=%async_computation.12 | async-start | bytes 655360 | tf_op jit(solution)/shard_map/reduce_scatter | solution.py:23
  137.1 48.7 %reduce-scatter.19.cloned.1.call-start = ((), (), s32[]{:S(2)}) async-start(), calls=%async_computation.13 | async-start | bytes 655360 | tf_op jit(solution)/shard_map/reduce_scatter | solution.py:35
  162.7 23.1 %copy-start.2 = (bf16[256,256]{1,0:T(8,128)(2,1)S(1)}, bf16[256,256]{1,0:T(8,128)(2,1)}, u32[]{:S(2)}) copy-start(bf16[256,256]{1,0:T(8,128)(2,1)} %reduce-scatter.9.cloned.1.call-done) | copy-start | bytes 393220
  162.7 23.1 %copy-start.3 = (bf16[256,256]{1,0:T(8,128)(2,1)S(1)}, bf16[256,256]{1,0:T(8,128)(2,1)}, u32[]{:S(2)}) copy-start(bf16[256,256]{1,0:T(8,128)(2,1)} %reduce-scatter.11.cloned.1.call-done) | copy-start | bytes 393220
  164.0 59.1 %reduce-scatter.21.cloned.1.call-start = ((), (), s32[]{:S(2)}) async-start(), calls=%async_computation.14 | async-start | bytes 655360 | tf_op jit(solution)/shard_map/reduce_scatter | solution.py:23
  196.3 49.0 %reduce-scatter.23.cloned.1.call-start = ((), (), s32[]{:S(2)}) async-start(), calls=%async_computation.15 | async-start | bytes 655360 | tf_op jit(solution)/shard_map/reduce_scatter | solution.py:35
  221.8 23.5 %copy-start.4 = (bf16[256,256]{1,0:T(8,128)(2,1)S(1)}, bf16[256,256]{1,0:T(8,128)(2,1)}, u32[]{:S(2)}) copy-start(bf16[256,256]{1,0:T(8,128)(2,1)} %reduce-scatter.13.cloned.1.call-done) | copy-start | bytes 393220
  221.8 23.5 %copy-start.5 = (bf16[256,256]{1,0:T(8,128)(2,1)S(1)}, bf16[256,256]{1,0:T(8,128)(2,1)}, u32[]{:S(2)}) copy-start(bf16[256,256]{1,0:T(8,128)(2,1)} %reduce-scatter.15.cloned.1.call-done) | copy-start | bytes 393220
Sparse Core Ops, SparseCore 0:
  19.6 25.3 reduce-scatter.8
  47.5 21.2 reduce-scatter.10
  78.6 24.8 reduce-scatter.12
  106.0 21.2 reduce-scatter.14
  137.3 24.8 reduce-scatter.16
  164.5 21.2 reduce-scatter.18
  196.4 24.8 reduce-scatter.20
  224.0 21.2 reduce-scatter.22
where the time goes:
time: 254 us
  blocking collectives  114 us (45%)
  waiting for transfers between devices  90.3 us (36%)
  matrix products  14.7 us (6%)
  between operations  14.4 us (6%)
  local copies, waits for them, and re-layouts  12.8 us (5%)
  other arithmetic  7.56 us (3%)
    reduce_scatter x4, waiting for transfers between devices, apply_pair(): lax.psum_scatter(summed.reshape(tile_cols * orb, width).astype(jnp.bfloat...  89.7 us
    all_gather x4, blocking collectives, apply_pair(): lax.all_gather(send, 'row', axis=0, tiled=True)  84.7 us
    all_gather x4, blocking collectives, apply_pair(): lax.all_gather(send, 'col', axis=0, tiled=True)  29.2 us
    reshape x3, local copies, waits for them, and re-layouts, apply_pair(): mirrored = mirrored.reshape(tile_rows * per_row, orb, width)  6.73 us
    dot_general x4, matrix products, apply_pair(): jnp.einsum('tpio,tik->tpok', grouped, tall, preferred_element_type=jnp.fl...  5.97 us
  transfers between devices with their start and end apart: 8, of which 5 were waited for; matrix products, arithmetic and copies ran while one was open for 8% of the time, Pallas kernels for 0%

commit v1 on v0

--- a/solution.py
+++ b/solution.py
@@ -1,10 +1,16 @@
+import functools
+
 import jax
 import jax.numpy as jnp
 from jax import lax
+from jax.experimental import pallas as pl
+from jax.experimental.pallas import tpu as pltpu
 from jax.sharding import PartitionSpec as P
 
 PER_ROW = 2
 DEG = 4
+GATHER_LIMIT = 12 * 2**20
+LANES = ("col", "row")
 
 
 def onehot_sum(selected, high_part, low_part):
@@ -41,7 +47,7 @@
     return part_rows + part_cols
 
 
-def per_device(vectors, blocks, cols):
+def spread_plan(vectors, blocks, cols):
     tiles = blocks[0, 0]
     col_ids = cols[0, 0]
     slots, orb, _ = tiles.shape
@@ -59,6 +65,106 @@
     return (now, prev)
 
 
+def filter_kernel(n_row, per_piece, cols_ref, zt_ref, s_ref, out_ref, z, acc, now, prev):
+    tiles, slots = s_ref.shape[:2]
+    orb = s_ref.shape[2]
+    tile_rows = slots // PER_ROW
+    pieces = zt_ref.shape[0]
+
+    for p in range(pieces):
+        for b in range(per_piece):
+            own = zt_ref[p, :, b * orb : (b + 1) * orb]
+            z[p * per_piece + b] = own
+            prev[p * per_piece + b] = own.astype(jnp.float32)
+
+    def tile_step(tile, carry):
+        across = tile // n_row
+        down = tile % n_row
+
+        def block_of(slot):
+            u = cols_ref[tile, slot]
+            return (u // per_piece * n_row + down) * per_piece + u % per_piece
+
+        direct, mirrored, places = [], [], []
+        for t in range(tile_rows):
+            pair = jnp.concatenate([s_ref[tile, t * PER_ROW + p] for p in range(PER_ROW)], axis=1)
+            where = [block_of(t * PER_ROW + p) for p in range(PER_ROW)]
+            wide = jnp.concatenate([z[g] for g in where], axis=1)
+            tall = z[across * tile_rows + t]
+            direct.append(
+                lax.dot_general(wide, pair, (((1,), (1,)), ((), ())), preferred_element_type=jnp.float32)
+            )
+            both = jnp.dot(tall, pair, preferred_element_type=jnp.float32)
+            for p in range(PER_ROW):
+                places.append(where[p])
+                mirrored.append(both[:, p * orb : (p + 1) * orb])
+        for t in range(tile_rows):
+            acc[across * tile_rows + t] += direct[t]
+        for g, term in zip(places, mirrored):
+            acc[g] += term
+        return carry
+
+    for step in range(DEG):
+        acc[...] = jnp.zeros_like(acc)
+        lax.fori_loop(0, tiles, tile_step, 0)
+        if step == 0:
+            now[...] = acc[...]
+        else:
+            nxt = 2.0 * acc[...] - prev[...]
+            prev[...] = now[...]
+            now[...] = nxt
+        if step < DEG - 1:
+            z[...] = now[...].astype(z.dtype)
+    for p in range(pieces):
+        for b in range(per_piece):
+            g = p * per_piece + b
+            out_ref[p, 0, :, b * orb : (b + 1) * orb] = now[g].astype(out_ref.dtype)
+            out_ref[p, 1, :, b * orb : (b + 1) * orb] = prev[g].astype(out_ref.dtype)
+
+
+def gather_plan(vectors, blocks, cols):
+    n_dev = lax.axis_size(LANES)
+    n_row = lax.axis_size("row")
+    rows, width = vectors.shape
+    slots, orb = blocks.shape[2:4]
+    share = width // n_dev
+    per_piece = rows // orb
+
+    tiles = lax.all_gather(blocks[0, 0], LANES, axis=0)
+    ids = lax.all_gather(cols[0, 0], LANES, axis=0)
+    turned = vectors.T.reshape(n_dev, share, rows)
+    zt = lax.all_to_all(turned, LANES, split_axis=0, concat_axis=0, tiled=True)
+
+    n_blocks = n_dev * per_piece
+    done = pl.pallas_call(
+        functools.partial(filter_kernel, n_row, per_piece),
+        out_shape=jax.ShapeDtypeStruct((n_dev, 2, share, rows), jnp.bfloat16),
+        in_specs=[
+            pl.BlockSpec(memory_space=pltpu.SMEM),
+            pl.BlockSpec(memory_space=pltpu.VMEM),
+            pl.BlockSpec(memory_space=pltpu.VMEM),
+        ],
+        out_specs=pl.BlockSpec(memory_space=pltpu.VMEM),
+        scratch_shapes=[
+            pltpu.VMEM((n_blocks, share, orb), jnp.bfloat16),
+            pltpu.VMEM((n_blocks, share, orb), jnp.float32),
+            pltpu.VMEM((n_blocks, share, orb), jnp.float32),
+            pltpu.VMEM((n_blocks, share, orb), jnp.float32),
+        ],
+        compiler_params=pltpu.CompilerParams(vmem_limit_bytes=32 * 2**20),
+    )(ids, zt, tiles)
+    back = lax.all_to_all(done, LANES, split_axis=0, concat_axis=0, tiled=True)
+    outs = jnp.transpose(back, (1, 3, 0, 2)).reshape(2, rows, width).astype(jnp.float32)
+    return outs[0], outs[1]
+
+
+def per_device(vectors, blocks, cols):
+    n_dev = lax.axis_size(LANES)
+    if n_dev * blocks.size * blocks.dtype.itemsize <= GATHER_LIMIT:
+        return gather_plan(vectors, blocks, cols)
+    return spread_plan(vectors, blocks, cols)
+
+
 def solution(mesh):
     return jax.shard_map(
         per_device,

time: 254 us -> 138 us (0.54)
  blocking collectives: 114 us -> 45.9 us
  waiting for transfers between devices: 90.3 us -> 38.6 us
  Pallas kernels: 0 us -> 25.4 us
  matrix products: 14.7 us -> 0 us
  other arithmetic: 7.56 us -> 0.05 us
  starting transfers between devices: 0.33 us -> 7.42 us
  local copies, waits for them, and re-layouts: 12.8 us -> 6.75 us
    reduce_scatter x8 -> x0, waiting for transfers between devices: 90.1 us -> none  [the longest x4 89.7 us: apply_pair(): lax.psum_scatter(summed.reshape(tile_cols * orb, width).astype(jnp.bfloat...]
    all_gather x8 -> x1, blocking collectives: 114 us -> 33.1 us  [gather_plan(): ids = lax.all_gather(cols[0, 0], LANES, axis=0)]
    all_gather x0 -> x1, waiting for transfers between devices: none -> 37.9 us  [gather_plan(): tiles = lax.all_gather(blocks[0, 0], LANES, axis=0)]
    pallas_call x0 -> x1, Pallas kernels: none -> 25.4 us  [gather_plan(): pl.pallas_call(functools.partial(filter_kernel, n_row, per_piece), out_sh...]
    dot_general x16 -> x0, matrix products: 14.7 us -> none  [the longest x4 5.97 us: apply_pair(): jnp.einsum('tpio,tik->tpok', grouped, tall, preferred_element_type=jnp.fl...]
    all_to_all x0 -> x1, blocking collectives: none -> 12.9 us  [gather_plan(): back = lax.all_to_all(done, LANES, split_axis=0, concat_axis=0, tiled=True)]
    all_to_all x0 -> x1, starting transfers between devices: none -> 7.39 us  [gather_plan(): zt = lax.all_to_all(turned, LANES, split_axis=0, concat_axis=0, tiled=True)]
    reshape x3 -> x0, local copies, waits for them, and re-layouts: 6.73 us -> none  [apply_pair(): mirrored = mirrored.reshape(tile_rows * per_row, orb, width)]
  transfers between devices with their start and end apart: 8 -> 2, of which waited for: 5 -> 1; matrix products, arithmetic and copies ran while one was open for 8% -> 1% of each run, Pallas kernels for 0% -> 0%
where the time goes in v1:
time: 138 us
  blocking collectives  45.9 us (33%)
  waiting for transfers between devices  38.6 us (28%)
  Pallas kernels  25.4 us (18%)
  between operations  14.1 us (10%)
  starting transfers between devices  7.42 us (5%)
  local copies, waits for them, and re-layouts  6.75 us (5%)
    all_gather x1, waiting for transfers between devices, gather_plan(): tiles = lax.all_gather(blocks[0, 0], LANES, axis=0)  37.9 us
    all_gather x1, blocking collectives, gather_plan(): ids = lax.all_gather(cols[0, 0], LANES, axis=0)  33.1 us
    pallas_call x1, Pallas kernels, gather_plan(): pl.pallas_call(functools.partial(filter_kernel, n_row, per_piece), out_sh...  25.4 us
    all_to_all x1, blocking collectives, gather_plan(): back = lax.all_to_all(done, LANES, split_axis=0, concat_axis=0, tiled=True)  12.9 us
    all_to_all x1, starting transfers between devices, gather_plan(): zt = lax.all_to_all(turned, LANES, split_axis=0, concat_axis=0, tiled=True)  7.39 us
    unnamed x4, local copies, waits for them, and re-layouts  5.05 us
  transfers between devices with their start and end apart: 2, of which 1 were waited for; matrix products, arithmetic and copies ran while one was open for 1% of the time, Pallas kernels for 0%

profile of v1, /device:TPU:0, one launch (start us, length us, event | category | flops | bytes accessed | tf_op | source)
XLA Modules:
  0.0 138.3 jit_solution(7476439224283624596)
XLA Ops:
  7.2 0.0 all-gather.4.cloned.1.call-start
  7.2 0.7 all-gather.4.cloned.1.call-update
  7.9 1.7 %copy.10 = bf16[256,256]{1,0:T(8,128)(2,1)} copy(bf16[256,256]{0,1:T(8,128)(2,1)} %bitcast.12) | data formatting | bytes 262144 | tf_op jit(solution)/shard_map/transpose | solution.py:135
  9.6 7.4 %all-to-all-start = ((bf16[16,16,256]{2,1,0:T(8,128)(2,1)}), bf16[16,16,256]{2,1,0:T(8,128)(2,1)S(1)}, u32[]{:S(2)}, u32[]{:S(2)}) async-start(bf16[16,16,256]{2,1,0:T(8,128)(2,1)} %bitcast.2), calls=%async_computation | async-start | bytes 262144 | tf_op jit(solution)/shard_map/all_to_all | solution.py:136
  17.0 33.1 %all-gather = s32[16,1,16]{2,1,0:T(1,128)S(1)} all-gather(s32[1,1,16]{2,1,0:T(1,128)} %param.5), channel_id=2, replica_groups=mesh['dom'=2,'col'=4,'row'=4] {'col','row'}, dimensions={0}, use_global_device_ids=true | all-gather | bytes 1088 | tf_op jit(solution)/shard_map/all_gather | solution.py:134
  50.0 0.0 all-to-all-done.zt_ref
  50.0 37.9 %all-gather.4.cloned.1.call-done = bf16[16,1,16,128,128]{4,3,2,1,0:T(8,128)(2,1)} async-done(((bf16[1,1,16,128,128]{4,3,2,1,0:T(8,128)(2,1)}), bf16[16,1,16,128,128]{4,3,2,1,0:T(8,128)(2,1)}) %all-gather.4.cloned.1.call-update) | async-done | bytes 8388624 | tf_op jit(solution)/shard_map/all_gather | solution.py:133
  88.0 0.0 copy-start
  88.0 3.4 %copy-done = bf16[16,1,16,128,128]{4,3,2,1,0:T(8,128)(2,1)S(1)} copy-done((bf16[16,1,16,128,128]{4,3,2,1,0:T(8,128)(2,1)S(1)}, bf16[16,1,16,128,128]{4,3,2,1,0:T(8,128)(2,1)}, u32[]{:S(2)}) %copy-start) | copy-done | bytes 8388632
  91.3 25.4 %shard_map.50 = bf16[16,2,16,256]{3,2,1,0:T(8,128)(2,1)S(1)} custom-call(s32[16,16]{1,0:T(8,128)S(1)} %bitcast.9, bf16[16,16,256]{2,1,0:T(8,128)(2,1)S(1)} %all-to-all-done.zt_ref, bf16[16,16,128,128]{3,2,1,0:T(8,128)(2,1)S(1)} %bitcast.8), custom_call_target="tpu_custom_call" | custom-call | tf_op jit(solution)/shard_map/pallas_call | solution.py:139
  116.8 12.9 %all_to_all.10 = bf16[16,2,16,256]{3,2,1,0:T(8,128)(2,1)S(1)} all-to-all(bf16[16,2,16,256]{3,2,1,0:T(8,128)(2,1)S(1)} %shard_map.50), channel_id=1, replica_groups=mesh['dom'=2,'col'=4,'row'=4] {'col','row'}, dimensions={0} | all-to-all | bytes 524288 | tf_op jit(solution)/shard_map/all_to_all | solution.py:156
  129.8 0.8 copy.12
  130.6 0.8 copy.11
  (2 shorter events, 0.1 us)
Async XLA Ops:
  7.2 80.8 %all-gather.4.cloned.1.call-start = ((), (), s32[]{:S(2)}) async-start(), calls=%async_computation.2 | async-start | bytes 8912896 | tf_op jit(solution)/shard_map/all_gather | solution.py:133
  9.6 40.5 %all-to-all-start = ((bf16[16,16,256]{2,1,0:T(8,128)(2,1)}), bf16[16,16,256]{2,1,0:T(8,128)(2,1)S(1)}, u32[]{:S(2)}, u32[]{:S(2)}) async-start(bf16[16,16,256]{2,1,0:T(8,128)(2,1)} %bitcast.2), calls=%async_computation | async-start | bytes 262144 | tf_op jit(solution)/shard_map/all_to_all | solution.py:136
  88.0 3.4 %copy-start = (bf16[16,1,16,128,128]{4,3,2,1,0:T(8,128)(2,1)S(1)}, bf16[16,1,16,128,128]{4,3,2,1,0:T(8,128)(2,1)}, u32[]{:S(2)}) copy-start(bf16[16,1,16,128,128]{4,3,2,1,0:T(8,128)(2,1)} %all-gather.4.cloned.1.call-done) | copy-start | bytes 25165828
Sparse Core Ops, SparseCore 0:
  10.2 77.6 all-gather.3

commit v2 on v1

--- a/solution.py
+++ b/solution.py
@@ -65,11 +65,20 @@
     return (now, prev)
 
 
-def filter_kernel(n_row, per_piece, cols_ref, zt_ref, s_ref, out_ref, z, acc, now, prev):
+def filter_kernel(per_piece, sources, ids_ref, where_ref, zt_ref, *refs):
+    bufs, (out_ref, s_ref, z, acc, now, prev, sems) = refs[:sources], refs[sources:]
     tiles, slots = s_ref.shape[:2]
     orb = s_ref.shape[2]
     tile_rows = slots // PER_ROW
     pieces = zt_ref.shape[0]
+    n_row = tile_rows // per_piece
+
+    for i, buf in enumerate(bufs):
+        tile = where_ref[i]
+
+        @pl.when(tile >= 0)
+        def _():
+            pltpu.make_async_copy(buf, s_ref.at[tile], sems.at[tile]).start()
 
     for p in range(pieces):
         for b in range(per_piece):
@@ -77,20 +86,17 @@
             z[p * per_piece + b] = own
             prev[p * per_piece + b] = own.astype(jnp.float32)
 
-    def tile_step(tile, carry):
-        across = tile // n_row
-        down = tile % n_row
-
-        def block_of(slot):
-            u = cols_ref[tile, slot]
-            return (u // per_piece * n_row + down) * per_piece + u % per_piece
+    def tile_step(first, tile, carry):
+        if first:
+            pltpu.make_async_copy(bufs[0], s_ref.at[tile], sems.at[tile]).wait()
+        row_base = tile // n_row * tile_rows
 
         direct, mirrored, places = [], [], []
         for t in range(tile_rows):
             pair = jnp.concatenate([s_ref[tile, t * PER_ROW + p] for p in range(PER_ROW)], axis=1)
-            where = [block_of(t * PER_ROW + p) for p in range(PER_ROW)]
+            where = [ids_ref[tile, t * PER_ROW + p] for p in range(PER_ROW)]
             wide = jnp.concatenate([z[g] for g in where], axis=1)
-            tall = z[across * tile_rows + t]
+            tall = z[row_base + t]
             direct.append(
                 lax.dot_general(wide, pair, (((1,), (1,)), ((), ())), preferred_element_type=jnp.float32)
             )
@@ -99,14 +105,14 @@
                 places.append(where[p])
                 mirrored.append(both[:, p * orb : (p + 1) * orb])
         for t in range(tile_rows):
-            acc[across * tile_rows + t] += direct[t]
+            acc[row_base + t] += direct[t]
         for g, term in zip(places, mirrored):
             acc[g] += term
         return carry
 
     for step in range(DEG):
         acc[...] = jnp.zeros_like(acc)
-        lax.fori_loop(0, tiles, tile_step, 0)
+        lax.fori_loop(0, tiles, functools.partial(tile_step, step == 0), 0)
         if step == 0:
             now[...] = acc[...]
         else:
@@ -122,37 +128,85 @@
             out_ref[p, 1, :, b * orb : (b + 1) * orb] = prev[g].astype(out_ref.dtype)
 
 
+def gather_tiles(own, n_col, n_row):
+    col, row = lax.axis_index("col"), lax.axis_index("row")
+    index = lambda c, r: c * n_row + r
+
+    def send(buf, pairs):
+        return lax.ppermute(buf, LANES, pairs)
+
+    held = [(own, 0, 0)]
+    for sign in (1, -1):
+        buf = own
+        for hop in range(1, n_row):
+            pairs = []
+            for r in range(n_row):
+                source = r - sign * (hop - 1)
+                if 0 <= r + sign < n_row and 0 <= source < n_row:
+                    pairs += [(index(c, r), index(c, r + sign)) for c in range(n_col)]
+            buf = send(buf, pairs)
+            held.append((buf, -sign * hop, 0))
+    held.sort(key=lambda item: abs(item[1]))
+    bit = n_col // 2
+    while bit:
+        for buf, shift, flips in list(held):
+            pairs = [
+                (index(c, r), index(c ^ bit, r))
+                for c in range(n_col)
+                for r in range(n_row)
+                if 0 <= r + shift < n_row
+            ]
+            held.append((send(buf, pairs), shift, flips | bit))
+        bit //= 2
+    where = []
+    for _, shift, flips in held:
+        r = row + shift
+        where.append(jnp.where((r >= 0) & (r < n_row), (col ^ flips) * n_row + r, -1))
+    return [buf for buf, _, _ in held], jnp.stack(where).astype(jnp.int32)
+
+
 def gather_plan(vectors, blocks, cols):
     n_dev = lax.axis_size(LANES)
-    n_row = lax.axis_size("row")
+    n_col, n_row = lax.axis_size("col"), lax.axis_size("row")
     rows, width = vectors.shape
     slots, orb = blocks.shape[2:4]
     share = width // n_dev
     per_piece = rows // orb
-
-    tiles = lax.all_gather(blocks[0, 0], LANES, axis=0)
-    ids = lax.all_gather(cols[0, 0], LANES, axis=0)
+    n_blocks = n_dev * per_piece
+
+    bufs, where = gather_tiles(blocks[0, 0], n_col, n_row)
+
     turned = vectors.T.reshape(n_dev, share, rows)
-    zt = lax.all_to_all(turned, LANES, split_axis=0, concat_axis=0, tiled=True)
-
-    n_blocks = n_dev * per_piece
+    own_ids = jnp.pad(cols[0, 0].astype(jnp.bfloat16), (0, rows - slots))
+    own_ids = jnp.broadcast_to(own_ids, (n_dev, share, rows))
+    both = lax.all_to_all(
+        jnp.concatenate([turned, own_ids], axis=1), LANES, split_axis=0, concat_axis=0, tiled=True
+    )
+    zt = both[:, :share]
+    local = both[:, share, :slots].astype(jnp.int32)
+    down = (jnp.arange(n_dev, dtype=jnp.int32) % n_row)[:, None]
+    ids = (local // per_piece * n_row + down) * per_piece + local % per_piece
+
     done = pl.pallas_call(
-        functools.partial(filter_kernel, n_row, per_piece),
+        functools.partial(filter_kernel, per_piece, len(bufs)),
         out_shape=jax.ShapeDtypeStruct((n_dev, 2, share, rows), jnp.bfloat16),
         in_specs=[
             pl.BlockSpec(memory_space=pltpu.SMEM),
+            pl.BlockSpec(memory_space=pltpu.SMEM),
             pl.BlockSpec(memory_space=pltpu.VMEM),
-            pl.BlockSpec(memory_space=pltpu.VMEM),
-        ],
+        ]
+        + [pl.BlockSpec(memory_space=pl.ANY)] * len(bufs),
         out_specs=pl.BlockSpec(memory_space=pltpu.VMEM),
         scratch_shapes=[
+            pltpu.VMEM((n_dev, slots, orb, orb), blocks.dtype),
             pltpu.VMEM((n_blocks, share, orb), jnp.bfloat16),
             pltpu.VMEM((n_blocks, share, orb), jnp.float32),
             pltpu.VMEM((n_blocks, share, orb), jnp.float32),
             pltpu.VMEM((n_blocks, share, orb), jnp.float32),
+            pltpu.SemaphoreType.DMA((n_dev,)),
         ],
         compiler_params=pltpu.CompilerParams(vmem_limit_bytes=32 * 2**20),
-    )(ids, zt, tiles)
+    )(ids, where, zt, *bufs)
     back = lax.all_to_all(done, LANES, split_axis=0, concat_axis=0, tiled=True)
     outs = jnp.transpose(back, (1, 3, 0, 2)).reshape(2, rows, width).astype(jnp.float32)
     return outs[0], outs[1]

time: 138 us -> 145 us (1.051)
  starting transfers between devices: 7.42 us -> 52.4 us
  blocking collectives: 45.9 us -> 18.8 us
  between operations: 14.1 us -> 1.14 us
  waiting for transfers between devices: 38.6 us -> 27.6 us
  local copies, waits for them, and re-layouts: 6.75 us -> 17.7 us
    ppermute x0 -> x27, starting transfers between devices: none -> 44.8 us  [send(): return lax.ppermute(buf, LANES, pairs)]
    all_gather x1 -> x0, waiting for transfers between devices: 37.9 us -> none  [gather_plan(): tiles = lax.all_gather(blocks[0, 0], LANES, axis=0)]
    all_gather x1 -> x0, blocking collectives: 33.1 us -> none  [gather_plan(): ids = lax.all_gather(cols[0, 0], LANES, axis=0)]
    ppermute x0 -> x27, waiting for transfers between devices: none -> 26.5 us  [send(): return lax.ppermute(buf, LANES, pairs)]
    unnamed x4 -> x38, local copies, waits for them, and re-layouts: 5.05 us -> 16.5 us
    all_to_all x1, blocking collectives: 12.9 us -> 18.8 us  [gather_plan(): back = lax.all_to_all(done, LANES, split_axis=0, concat_axis=0, tiled=True)]
  transfers between devices with their start and end apart: 2 -> 28, of which waited for: 1 -> 6; matrix products, arithmetic and copies ran while one was open for 1% -> 1% of each run, Pallas kernels for 0% -> 0%
where the time goes in v2:
time: 145 us; the launch traced here: 144 us
  starting transfers between devices  52.4 us (36%)
  waiting for transfers between devices  27.6 us (19%)
  Pallas kernels  25.9 us (18%)
  blocking collectives  18.8 us (13%)
  local copies, waits for them, and re-layouts  17.7 us (12%)
    ppermute x27, starting transfers between devices, send(): return lax.ppermute(buf, LANES, pairs)  44.8 us
    ppermute x27, waiting for transfers between devices, send(): return lax.ppermute(buf, LANES, pairs)  26.5 us
    pallas_call x1, Pallas kernels, gather_plan(): pl.pallas_call(functools.partial(filter_kernel, per_piece, len(bufs)), ou...  25.9 us
    all_to_all x1, blocking collectives, gather_plan(): back = lax.all_to_all(done, LANES, split_axis=0, concat_axis=0, tiled=True)  18.8 us
    unnamed x38, local copies, waits for them, and re-layouts  16.5 us
    all_to_all x1, starting transfers between devices, gather_plan(): lax.all_to_all(jnp.concatenate([turned, own_ids], axis=1), LANES, split_a...  7.58 us
  transfers between devices with their start and end apart: 28, of which 6 were waited for; matrix products, arithmetic and copies ran while one was open for 1% of the time, Pallas kernels for 0%

profile of v2, /device:TPU:0, one launch (start us, length us, event | category | flops | bytes accessed | tf_op | source)
XLA Modules:
  0.0 144.3 jit_solution(14775993079911128550)
XLA Ops:
  0.6 3.0 %collective-permute-start.6 = (bf16[16,128,128]{2,1,0:T(8,128)(2,1)}, bf16[16,128,128]{2,1,0:T(8,128)(2,1)S(1)}, u32[]{:S(2)}, u32[]{:S(2)}) collective-permute-start(bf16[16,128,128]{2,1,0:T(8,128)(2,1)} %bitcast.38), channel_id=1, source_target_pairs={{0,8},{1,9},{2,10},{3,11},{4,12},{5,13},{6,14},{7,15},{8,0},{9,1},... | collective-permute-start | bytes 1572872 | tf_op jit(solution)/shard_map/ppermute | solution.py:136
  5.0 4.6 %collective-permute-start = (bf16[16,128,128]{2,1,0:T(8,128)(2,1)}, bf16[16,128,128]{2,1,0:T(8,128)(2,1)S(1)}, u32[]{:S(2)}, u32[]{:S(2)}) collective-permute-start(bf16[16,128,128]{2,1,0:T(8,128)(2,1)} %bitcast.41), channel_id=1, source_target_pairs={{0,1},{4,5},{8,9},{12,13},{1,2},{5,6},{9,10},{13,14},{2,3},{6,7},{... | collective-permute-start | bytes 1572872 | tf_op jit(solution)/shard_map/ppermute | solution.py:136
  9.6 6.2 %collective-permute-done.6.refs_7_ = bf16[16,128,128]{2,1,0:T(8,128)(2,1)S(1)} collective-permute-done((bf16[16,128,128]{2,1,0:T(8,128)(2,1)}, bf16[16,128,128]{2,1,0:T(8,128)(2,1)S(1)}, u32[]{:S(2)}, u32[]{:S(2)}) %collective-permute-start.6) | collective-permute-done | bytes 524320 | tf_op jit(solution)/shard_map/ppermute | solution.py:136
  15.8 3.3 %collective-permute-done.1.refs_2_ = bf16[16,128,128]{2,1,0:T(8,128)(2,1)S(1)} collective-permute-done((bf16[16,128,128]{2,1,0:T(8,128)(2,1)}, bf16[16,128,128]{2,1,0:T(8,128)(2,1)S(1)}, u32[]{:S(2)}, u32[]{:S(2)}) %collective-permute-start.1) | collective-permute-done | bytes 524320 | tf_op jit(solution)/shard_map/ppermute | solution.py:136
  19.1 1.9 %collective-permute-start.15 = (bf16[16,128,128]{2,1,0:T(8,128)(2,1)S(1)}, bf16[16,128,128]{2,1,0:T(8,128)(2,1)S(1)}, u32[]{:S(2)}, u32[]{:S(2)}) collective-permute-start(bf16[16,128,128]{2,1,0:T(8,128)(2,1)S(1)} %collective-permute-done.1.refs_2_), channel_id=1, source_target_pairs={{0,4},{1,5},{2,6},{4,0},{5,1},{6,2},{8,12},{9,13},{10,14},{12,8},{... | collective-permute-start | bytes 1572872 | tf_op jit(solution)/shard_map/ppermute | solution.py:136
  21.1 2.3 %collective-permute-start.8 = (bf16[16,128,128]{2,1,0:T(8,128)(2,1)S(1)}, bf16[16,128,128]{2,1,0:T(8,128)(2,1)S(1)}, u32[]{:S(2)}, u32[]{:S(2)}) collective-permute-start(bf16[16,128,128]{2,1,0:T(8,128)(2,1)S(1)} %collective-permute-done.1.refs_2_), channel_id=1, source_target_pairs={{0,8},{1,9},{2,10},{4,12},{5,13},{6,14},{8,0},{9,1},{10,2},{12,4},... | collective-permute-start | bytes 1572872 | tf_op jit(solution)/shard_map/ppermute | solution.py:136
  28.3 8.9 %collective-permute-done.8.refs_9_ = bf16[16,128,128]{2,1,0:T(8,128)(2,1)S(1)} collective-permute-done((bf16[16,128,128]{2,1,0:T(8,128)(2,1)S(1)}, bf16[16,128,128]{2,1,0:T(8,128)(2,1)S(1)}, u32[]{:S(2)}, u32[]{:S(2)}) %collective-permute-start.8) | collective-permute-done | bytes 524320 | tf_op jit(solution)/shard_map/ppermute | solution.py:136
  37.3 1.9 %collective-permute-start.22 = (bf16[16,128,128]{2,1,0:T(8,128)(2,1)S(1)}, bf16[16,128,128]{2,1,0:T(8,128)(2,1)S(1)}, u32[]{:S(2)}, u32[]{:S(2)}) collective-permute-start(bf16[16,128,128]{2,1,0:T(8,128)(2,1)S(1)} %collective-permute-done.8.refs_9_), channel_id=1, source_target_pairs={{0,4},{1,5},{2,6},{4,0},{5,1},{6,2},{8,12},{9,13},{10,14},{12,8},{... | collective-permute-start | bytes 1572872 | tf_op jit(solution)/shard_map/ppermute | solution.py:136
  40.0 2.4 %collective-permute-start.17 = (bf16[16,128,128]{2,1,0:T(8,128)(2,1)S(1)}, bf16[16,128,128]{2,1,0:T(8,128)(2,1)S(1)}, u32[]{:S(2)}, u32[]{:S(2)}) collective-permute-start(bf16[16,128,128]{2,1,0:T(8,128)(2,1)S(1)} %collective-permute-done.3.refs_4_), channel_id=1, source_target_pairs={{0,4},{1,5},{4,0},{5,1},{8,12},{9,13},{12,8},{13,9},{16,20},{17,21... | collective-permute-start | bytes 1572872 | tf_op jit(solution)/shard_map/ppermute | solution.py:136
  43.3 2.4 %collective-permute-start.10 = (bf16[16,128,128]{2,1,0:T(8,128)(2,1)S(1)}, bf16[16,128,128]{2,1,0:T(8,128)(2,1)}, u32[]{:S(2)}, u32[]{:S(2)}) collective-permute-start(bf16[16,128,128]{2,1,0:T(8,128)(2,1)S(1)} %collective-permute-done.3.refs_4_), channel_id=1, source_target_pairs={{0,8},{1,9},{4,12},{5,13},{8,0},{9,1},{12,4},{13,5},{16,24},{17,25... | collective-permute-start | bytes 1572872 | tf_op jit(solution)/shard_map/ppermute | solution.py:136
  50.1 1.5 %collective-permute-start.4 = (bf16[16,128,128]{2,1,0:T(8,128)(2,1)}, bf16[16,128,128]{2,1,0:T(8,128)(2,1)}, u32[]{:S(2)}, u32[]{:S(2)}) collective-permute-start(bf16[16,128,128]{2,1,0:T(8,128)(2,1)} %collective-permute-done.2.refs_3_), channel_id=1, source_target_pairs={{2,3},{6,7},{10,11},{14,15},{18,19},{22,23},{26,27},{30,31}} | collective-permute-start | bytes 1572872 | tf_op jit(solution)/shard_map/ppermute | solution.py:136
  53.8 5.3 %collective-permute-done.10.refs_11_ = bf16[16,128,128]{2,1,0:T(8,128)(2,1)} collective-permute-done((bf16[16,128,128]{2,1,0:T(8,128)(2,1)S(1)}, bf16[16,128,128]{2,1,0:T(8,128)(2,1)}, u32[]{:S(2)}, u32[]{:S(2)}) %collective-permute-start.10) | collective-permute-done | bytes 524320 | tf_op jit(solution)/shard_map/ppermute | solution.py:136
  59.1 1.5 %collective-permute-start.9 = (bf16[16,128,128]{2,1,0:T(8,128)(2,1)}, bf16[16,128,128]{2,1,0:T(8,128)(2,1)}, u32[]{:S(2)}, u32[]{:S(2)}) collective-permute-start(bf16[16,128,128]{2,1,0:T(8,128)(2,1)} %collective-permute-done.2.refs_3_), channel_id=1, source_target_pairs={{2,10},{3,11},{6,14},{7,15},{10,2},{11,3},{14,6},{15,7},{18,26},{1... | collective-permute-start | bytes 1572872 | tf_op jit(solution)/shard_map/ppermute | solution.py:136
  60.6 2.7 %collective-permute-done.5.refs_6_ = bf16[16,128,128]{2,1,0:T(8,128)(2,1)} collective-permute-done((bf16[16,128,128]{2,1,0:T(8,128)(2,1)S(1)}, bf16[16,128,128]{2,1,0:T(8,128)(2,1)}, u32[]{:S(2)}, u32[]{:S(2)}) %collective-permute-start.5) | collective-permute-done | bytes 524320 | tf_op jit(solution)/shard_map/ppermute | solution.py:136
  63.3 1.9 %collective-permute-start.24 = (bf16[16,128,128]{2,1,0:T(8,128)(2,1)}, bf16[16,128,128]{2,1,0:T(8,128)(2,1)}, u32[]{:S(2)}, u32[]{:S(2)}) collective-permute-start(bf16[16,128,128]{2,1,0:T(8,128)(2,1)} %collective-permute-done.10.refs_11_), channel_id=1, source_target_pairs={{0,4},{1,5},{4,0},{5,1},{8,12},{9,13},{12,8},{13,9},{16,20},{17,21... | collective-permute-start | bytes 1572872 | tf_op jit(solution)/shard_map/ppermute | solution.py:136
  66.0 2.4 %collective-permute-start.12 = (bf16[16,128,128]{2,1,0:T(8,128)(2,1)}, bf16[16,128,128]{2,1,0:T(8,128)(2,1)}, u32[]{:S(2)}, u32[]{:S(2)}) collective-permute-start(bf16[16,128,128]{2,1,0:T(8,128)(2,1)} %collective-permute-done.5.refs_6_), channel_id=1, source_target_pairs={{0,8},{4,12},{8,0},{12,4},{16,24},{20,28},{24,16},{28,20}} | collective-permute-start | bytes 1572872 | tf_op jit(solution)/shard_map/ppermute | solution.py:136
  68.4 1.5 %collective-permute-start.11 = (bf16[16,128,128]{2,1,0:T(8,128)(2,1)}, bf16[16,128,128]{2,1,0:T(8,128)(2,1)}, u32[]{:S(2)}, u32[]{:S(2)}) collective-permute-start(bf16[16,128,128]{2,1,0:T(8,128)(2,1)} %collective-permute-done.4.refs_5_), channel_id=1, source_target_pairs={{3,11},{7,15},{11,3},{15,7},{19,27},{23,31},{27,19},{31,23}} | collective-permute-start | bytes 1572872 | tf_op jit(solution)/shard_map/ppermute | solution.py:136
  71.7 7.6 %all-to-all-start = ((bf16[16,32,256]{2,1,0:T(8,128)(2,1)}), bf16[16,32,256]{2,1,0:T(8,128)(2,1)S(1)}, u32[]{:S(2)}, u32[]{:S(2)}) async-start(bf16[16,32,256]{2,1,0:T(8,128)(2,1)} %pad_maximum_fusion), calls=%async_computation | async-start | bytes 524288 | tf_op jit(solution)/shard_map/all_to_all | solution.py:182
  79.5 2.2 %collective-permute-start.19 = (bf16[16,128,128]{2,1,0:T(8,128)(2,1)}, bf16[16,128,128]{2,1,0:T(8,128)(2,1)}, u32[]{:S(2)}, u32[]{:S(2)}) collective-permute-start(bf16[16,128,128]{2,1,0:T(8,128)(2,1)} %collective-permute-done.5.refs_6_), channel_id=1, source_target_pairs={{0,4},{4,0},{8,12},{12,8},{16,20},{20,16},{24,28},{28,24}} | collective-permute-start | bytes 1572872 | tf_op jit(solution)/shard_map/ppermute | solution.py:136
  81.7 1.5 %collective-permute-start.18 = (bf16[16,128,128]{2,1,0:T(8,128)(2,1)}, bf16[16,128,128]{2,1,0:T(8,128)(2,1)}, u32[]{:S(2)}, u32[]{:S(2)}) collective-permute-start(bf16[16,128,128]{2,1,0:T(8,128)(2,1)} %collective-permute-done.4.refs_5_), channel_id=1, source_target_pairs={{3,7},{7,3},{11,15},{15,11},{19,23},{23,19},{27,31},{31,27}} | collective-permute-start | bytes 1572872 | tf_op jit(solution)/shard_map/ppermute | solution.py:136
  84.7 2.1 %collective-permute-start.26 = (bf16[16,128,128]{2,1,0:T(8,128)(2,1)}, bf16[16,128,128]{2,1,0:T(8,128)(2,1)}, u32[]{:S(2)}, u32[]{:S(2)}) collective-permute-start(bf16[16,128,128]{2,1,0:T(8,128)(2,1)} %collective-permute-done.12.refs_13_), channel_id=1, source_target_pairs={{0,4},{4,0},{8,12},{12,8},{16,20},{20,16},{24,28},{28,24}} | collective-permute-start | bytes 1572872 | tf_op jit(solution)/shard_map/ppermute | solution.py:136
  86.8 1.5 %collective-permute-start.25 = (bf16[16,128,128]{2,1,0:T(8,128)(2,1)}, bf16[16,128,128]{2,1,0:T(8,128)(2,1)}, u32[]{:S(2)}, u32[]{:S(2)}) collective-permute-start(bf16[16,128,128]{2,1,0:T(8,128)(2,1)} %collective-permute-done.11.refs_12_), channel_id=1, source_target_pairs={{3,7},{7,3},{11,15},{15,11},{19,23},{23,19},{27,31},{31,27}} | collective-permute-start | bytes 1572872 | tf_op jit(solution)/shard_map/ppermute | solution.py:136
  97.8 25.9 %shard_map.50 = bf16[16,2,16,256]{3,2,1,0:T(8,128)(2,1)S(1)} custom-call(s32[16,16]{1,0:T(8,128)S(1)} %fusion.3.ids_ref, s32[28]{0:T(128)S(1)} %stack.115.where_ref, bf16[16,16,256]{2,1,0:T(8,128)(2,1)S(1)} %slice.19.zt_ref, bf16[16,128,128]{2,1,0:T(8,128)(2,1)S(1)} %bitcast.42, bf16[16,128,128]{2,1,0:T(8,128)(2,1)S(1)} %collective-permute-done.refs_1_, ...), custom_call_target="tpu_custom_call" | custom-call | tf_op jit(solution)/shard_map/pallas_call | solution.py:190
  123.8 18.8 %all_to_all.10 = bf16[16,2,16,256]{3,2,1,0:T(8,128)(2,1)S(1)} all-to-all(bf16[16,2,16,256]{3,2,1,0:T(8,128)(2,1)S(1)} %shard_map.50), channel_id=1, replica_groups=mesh['dom'=2,'col'=4,'row'=4] {'col','row'}, dimensions={0} | all-to-all | bytes 524288 | tf_op jit(solution)/shard_map/all_to_all | solution.py:210
  (84 shorter events, 30.1 us)
Async XLA Ops:
  0.6 15.2 %collective-permute-start.6 = (bf16[16,128,128]{2,1,0:T(8,128)(2,1)}, bf16[16,128,128]{2,1,0:T(8,128)(2,1)S(1)}, u32[]{:S(2)}, u32[]{:S(2)}) collective-permute-start(bf16[16,128,128]{2,1,0:T(8,128)(2,1)} %bitcast.38), channel_id=1, source_target_pairs={{0,8},{1,9},{2,10},{3,11},{4,12},{5,13},{6,14},{7,15},{8,0},{9,1},... | collective-permute-start | bytes 1572872 | tf_op jit(solution)/shard_map/ppermute | solution.py:136
  3.7 15.5 %collective-permute-start.1 = (bf16[16,128,128]{2,1,0:T(8,128)(2,1)}, bf16[16,128,128]{2,1,0:T(8,128)(2,1)S(1)}, u32[]{:S(2)}, u32[]{:S(2)}) collective-permute-start(bf16[16,128,128]{2,1,0:T(8,128)(2,1)} %bitcast.39), channel_id=1, source_target_pairs={{1,0},{5,4},{9,8},{13,12},{2,1},{6,5},{10,9},{14,13},{3,2},{7,6},{... | collective-permute-start | bytes 1572872 | tf_op jit(solution)/shard_map/ppermute | solution.py:136
  5.0 18.4 %collective-permute-start.13 = (bf16[16,128,128]{2,1,0:T(8,128)(2,1)}, bf16[16,128,128]{2,1,0:T(8,128)(2,1)S(1)}, u32[]{:S(2)}, u32[]{:S(2)}) collective-permute-start(bf16[16,128,128]{2,1,0:T(8,128)(2,1)} %bitcast.40), channel_id=1, source_target_pairs={{0,4},{1,5},{2,6},{3,7},{4,0},{5,1},{6,2},{7,3},{8,12},{9,13},{10,... | collective-permute-start | bytes 1572872 | tf_op jit(solution)/shard_map/ppermute | solution.py:136
  5.0 19.6 %collective-permute-start = (bf16[16,128,128]{2,1,0:T(8,128)(2,1)}, bf16[16,128,128]{2,1,0:T(8,128)(2,1)S(1)}, u32[]{:S(2)}, u32[]{:S(2)}) collective-permute-start(bf16[16,128,128]{2,1,0:T(8,128)(2,1)} %bitcast.41), channel_id=1, source_target_pairs={{0,1},{4,5},{8,9},{12,13},{1,2},{5,6},{9,10},{13,14},{2,3},{6,7},{... | collective-permute-start | bytes 1572872 | tf_op jit(solution)/shard_map/ppermute | solution.py:136
  15.8 9.6 %collective-permute-start.20 = (bf16[16,128,128]{2,1,0:T(8,128)(2,1)S(1)}, bf16[16,128,128]{2,1,0:T(8,128)(2,1)S(1)}, u32[]{:S(2)}, u32[]{:S(2)}) collective-permute-start(bf16[16,128,128]{2,1,0:T(8,128)(2,1)S(1)} %collective-permute-done.6.refs_7_), channel_id=1, source_target_pairs={{0,4},{1,5},{2,6},{3,7},{4,0},{5,1},{6,2},{7,3},{8,12},{9,13},{10,... | collective-permute-start | bytes 1572872 | tf_op jit(solution)/shard_map/ppermute | solution.py:136
  21.1 16.2 %collective-permute-start.8 = (bf16[16,128,128]{2,1,0:T(8,128)(2,1)S(1)}, bf16[16,128,128]{2,1,0:T(8,128)(2,1)S(1)}, u32[]{:S(2)}, u32[]{:S(2)}) collective-permute-start(bf16[16,128,128]{2,1,0:T(8,128)(2,1)S(1)} %collective-permute-done.1.refs_2_), channel_id=1, source_target_pairs={{0,8},{1,9},{2,10},{4,12},{5,13},{6,14},{8,0},{9,1},{10,2},{12,4},... | collective-permute-start | bytes 1572872 | tf_op jit(solution)/shard_map/ppermute | solution.py:136
  23.3 16.7 %collective-permute-start.3 = (bf16[16,128,128]{2,1,0:T(8,128)(2,1)S(1)}, bf16[16,128,128]{2,1,0:T(8,128)(2,1)S(1)}, u32[]{:S(2)}, u32[]{:S(2)}) collective-permute-start(bf16[16,128,128]{2,1,0:T(8,128)(2,1)S(1)} %collective-permute-done.1.refs_2_), channel_id=1, source_target_pairs={{1,0},{5,4},{9,8},{13,12},{2,1},{6,5},{10,9},{14,13},{17,16},{21,2... | collective-permute-start | bytes 1572872 | tf_op jit(solution)/shard_map/ppermute | solution.py:136
  24.7 17.8 %collective-permute-start.14 = (bf16[16,128,128]{2,1,0:T(8,128)(2,1)S(1)}, bf16[16,128,128]{2,1,0:T(8,128)(2,1)S(1)}, u32[]{:S(2)}, u32[]{:S(2)}) collective-permute-start(bf16[16,128,128]{2,1,0:T(8,128)(2,1)S(1)} %collective-permute-done.refs_1_), channel_id=1, source_target_pairs={{1,5},{2,6},{3,7},{5,1},{6,2},{7,3},{9,13},{10,14},{11,15},{13,9},... | collective-permute-start | bytes 1572872 | tf_op jit(solution)/shard_map/ppermute | solution.py:136
  25.4 20.3 %collective-permute-start.7 = (bf16[16,128,128]{2,1,0:T(8,128)(2,1)S(1)}, bf16[16,128,128]{2,1,0:T(8,128)(2,1)S(1)}, u32[]{:S(2)}, u32[]{:S(2)}) collective-permute-start(bf16[16,128,128]{2,1,0:T(8,128)(2,1)S(1)} %collective-permute-done.refs_1_), channel_id=1, source_target_pairs={{1,9},{2,10},{3,11},{5,13},{6,14},{7,15},{9,1},{10,2},{11,3},{13,5... | collective-permute-start | bytes 1572872 | tf_op jit(solution)/shard_map/ppermute | solution.py:136
  26.9 20.9 %collective-permute-start.2 = (bf16[16,128,128]{2,1,0:T(8,128)(2,1)S(1)}, bf16[16,128,128]{2,1,0:T(8,128)(2,1)}, u32[]{:S(2)}, u32[]{:S(2)}) collective-permute-start(bf16[16,128,128]{2,1,0:T(8,128)(2,1)S(1)} %collective-permute-done.refs_1_), channel_id=1, source_target_pairs={{1,2},{5,6},{9,10},{13,14},{2,3},{6,7},{10,11},{14,15},{17,18},{21... | collective-permute-start | bytes 1572872 | tf_op jit(solution)/shard_map/ppermute | solution.py:136
  37.3 12.0 %collective-permute-start.22 = (bf16[16,128,128]{2,1,0:T(8,128)(2,1)S(1)}, bf16[16,128,128]{2,1,0:T(8,128)(2,1)S(1)}, u32[]{:S(2)}, u32[]{:S(2)}) collective-permute-start(bf16[16,128,128]{2,1,0:T(8,128)(2,1)S(1)} %collective-permute-done.8.refs_9_), channel_id=1, source_target_pairs={{0,4},{1,5},{2,6},{4,0},{5,1},{6,2},{8,12},{9,13},{10,14},{12,8},{... | collective-permute-start | bytes 1572872 | tf_op jit(solution)/shard_map/ppermute | solution.py:136
  40.0 11.5 %collective-permute-start.17 = (bf16[16,128,128]{2,1,0:T(8,128)(2,1)S(1)}, bf16[16,128,128]{2,1,0:T(8,128)(2,1)S(1)}, u32[]{:S(2)}, u32[]{:S(2)}) collective-permute-start(bf16[16,128,128]{2,1,0:T(8,128)(2,1)S(1)} %collective-permute-done.3.refs_4_), channel_id=1, source_target_pairs={{0,4},{1,5},{4,0},{5,1},{8,12},{9,13},{12,8},{13,9},{16,20},{17,21... | collective-permute-start | bytes 1572872 | tf_op jit(solution)/shard_map/ppermute | solution.py:136
  43.3 15.8 %collective-permute-start.10 = (bf16[16,128,128]{2,1,0:T(8,128)(2,1)S(1)}, bf16[16,128,128]{2,1,0:T(8,128)(2,1)}, u32[]{:S(2)}, u32[]{:S(2)}) collective-permute-start(bf16[16,128,128]{2,1,0:T(8,128)(2,1)S(1)} %collective-permute-done.3.refs_4_), channel_id=1, source_target_pairs={{0,8},{1,9},{4,12},{5,13},{8,0},{9,1},{12,4},{13,5},{16,24},{17,25... | collective-permute-start | bytes 1572872 | tf_op jit(solution)/shard_map/ppermute | solution.py:136
  45.6 17.6 %collective-permute-start.5 = (bf16[16,128,128]{2,1,0:T(8,128)(2,1)S(1)}, bf16[16,128,128]{2,1,0:T(8,128)(2,1)}, u32[]{:S(2)}, u32[]{:S(2)}) collective-permute-start(bf16[16,128,128]{2,1,0:T(8,128)(2,1)S(1)} %collective-permute-done.3.refs_4_), channel_id=1, source_target_pairs={{1,0},{5,4},{9,8},{13,12},{17,16},{21,20},{25,24},{29,28}} | collective-permute-start | bytes 1572872 | tf_op jit(solution)/shard_map/ppermute | solution.py:136
  47.8 17.4 %collective-permute-start.21 = (bf16[16,128,128]{2,1,0:T(8,128)(2,1)S(1)}, bf16[16,128,128]{2,1,0:T(8,128)(2,1)S(1)}, u32[]{:S(2)}, u32[]{:S(2)}) collective-permute-start(bf16[16,128,128]{2,1,0:T(8,128)(2,1)S(1)} %collective-permute-done.7.refs_8_), channel_id=1, source_target_pairs={{1,5},{2,6},{3,7},{5,1},{6,2},{7,3},{9,13},{10,14},{11,15},{13,9},... | collective-permute-start | bytes 1572872 | tf_op jit(solution)/shard_map/ppermute | solution.py:136
  50.1 18.4 %collective-permute-start.4 = (bf16[16,128,128]{2,1,0:T(8,128)(2,1)}, bf16[16,128,128]{2,1,0:T(8,128)(2,1)}, u32[]{:S(2)}, u32[]{:S(2)}) collective-permute-start(bf16[16,128,128]{2,1,0:T(8,128)(2,1)} %collective-permute-done.2.refs_3_), channel_id=1, source_target_pairs={{2,3},{6,7},{10,11},{14,15},{18,19},{22,23},{26,27},{30,31}} | collective-permute-start | bytes 1572872 | tf_op jit(solution)/shard_map/ppermute | solution.py:136
  52.4 27.1 %collective-permute-start.16 = (bf16[16,128,128]{2,1,0:T(8,128)(2,1)}, bf16[16,128,128]{2,1,0:T(8,128)(2,1)}, u32[]{:S(2)}, u32[]{:S(2)}) collective-permute-start(bf16[16,128,128]{2,1,0:T(8,128)(2,1)} %collective-permute-done.2.refs_3_), channel_id=1, source_target_pairs={{2,6},{3,7},{6,2},{7,3},{10,14},{11,15},{14,10},{15,11},{18,22},{1... | collective-permute-start | bytes 1572872 | tf_op jit(solution)/shard_map/ppermute | solution.py:136
  59.1 22.6 %collective-permute-start.9 = (bf16[16,128,128]{2,1,0:T(8,128)(2,1)}, bf16[16,128,128]{2,1,0:T(8,128)(2,1)}, u32[]{:S(2)}, u32[]{:S(2)}) collective-permute-start(bf16[16,128,128]{2,1,0:T(8,128)(2,1)} %collective-permute-done.2.refs_3_), channel_id=1, source_target_pairs={{2,10},{3,11},{6,14},{7,15},{10,2},{11,3},{14,6},{15,7},{18,26},{1... | collective-permute-start | bytes 1572872 | tf_op jit(solution)/shard_map/ppermute | solution.py:136
  63.3 19.9 %collective-permute-start.24 = (bf16[16,128,128]{2,1,0:T(8,128)(2,1)}, bf16[16,128,128]{2,1,0:T(8,128)(2,1)}, u32[]{:S(2)}, u32[]{:S(2)}) collective-permute-start(bf16[16,128,128]{2,1,0:T(8,128)(2,1)} %collective-permute-done.10.refs_11_), channel_id=1, source_target_pairs={{0,4},{1,5},{4,0},{5,1},{8,12},{9,13},{12,8},{13,9},{16,20},{17,21... | collective-permute-start | bytes 1572872 | tf_op jit(solution)/shard_map/ppermute | solution.py:136
  66.0 18.6 %collective-permute-start.12 = (bf16[16,128,128]{2,1,0:T(8,128)(2,1)}, bf16[16,128,128]{2,1,0:T(8,128)(2,1)}, u32[]{:S(2)}, u32[]{:S(2)}) collective-permute-start(bf16[16,128,128]{2,1,0:T(8,128)(2,1)} %collective-permute-done.5.refs_6_), channel_id=1, source_target_pairs={{0,8},{4,12},{8,0},{12,4},{16,24},{20,28},{24,16},{28,20}} | collective-permute-start | bytes 1572872 | tf_op jit(solution)/shard_map/ppermute | solution.py:136
  68.4 18.3 %collective-permute-start.11 = (bf16[16,128,128]{2,1,0:T(8,128)(2,1)}, bf16[16,128,128]{2,1,0:T(8,128)(2,1)}, u32[]{:S(2)}, u32[]{:S(2)}) collective-permute-start(bf16[16,128,128]{2,1,0:T(8,128)(2,1)} %collective-permute-done.4.refs_5_), channel_id=1, source_target_pairs={{3,11},{7,15},{11,3},{15,7},{19,27},{23,31},{27,19},{31,23}} | collective-permute-start | bytes 1572872 | tf_op jit(solution)/shard_map/ppermute | solution.py:136
  71.7 17.7 %all-to-all-start = ((bf16[16,32,256]{2,1,0:T(8,128)(2,1)}), bf16[16,32,256]{2,1,0:T(8,128)(2,1)S(1)}, u32[]{:S(2)}, u32[]{:S(2)}) async-start(bf16[16,32,256]{2,1,0:T(8,128)(2,1)} %pad_maximum_fusion), calls=%async_computation | async-start | bytes 524288 | tf_op jit(solution)/shard_map/all_to_all | solution.py:182
  79.5 10.0 %collective-permute-start.19 = (bf16[16,128,128]{2,1,0:T(8,128)(2,1)}, bf16[16,128,128]{2,1,0:T(8,128)(2,1)}, u32[]{:S(2)}, u32[]{:S(2)}) collective-permute-start(bf16[16,128,128]{2,1,0:T(8,128)(2,1)} %collective-permute-done.5.refs_6_), channel_id=1, source_target_pairs={{0,4},{4,0},{8,12},{12,8},{16,20},{20,16},{24,28},{28,24}} | collective-permute-start | bytes 1572872 | tf_op jit(solution)/shard_map/ppermute | solution.py:136
  81.7 7.7 %collective-permute-start.18 = (bf16[16,128,128]{2,1,0:T(8,128)(2,1)}, bf16[16,128,128]{2,1,0:T(8,128)(2,1)}, u32[]{:S(2)}, u32[]{:S(2)}) collective-permute-start(bf16[16,128,128]{2,1,0:T(8,128)(2,1)} %collective-permute-done.4.refs_5_), channel_id=1, source_target_pairs={{3,7},{7,3},{11,15},{15,11},{19,23},{23,19},{27,31},{31,27}} | collective-permute-start | bytes 1572872 | tf_op jit(solution)/shard_map/ppermute | solution.py:136
  (22 other events, 122.6 us)

commit v3 on v2

--- a/solution.py
+++ b/solution.py
@@ -9,6 +9,7 @@
 
 PER_ROW = 2
 DEG = 4
+SPLIT = 4
 GATHER_LIMIT = 12 * 2**20
 LANES = ("col", "row")
 
@@ -65,13 +66,12 @@
     return (now, prev)
 
 
-def filter_kernel(per_piece, sources, ids_ref, where_ref, zt_ref, *refs):
-    bufs, (out_ref, s_ref, z, acc, now, prev, sems) = refs[:sources], refs[sources:]
+def filter_kernel(per_piece, n_row, sources, ids_ref, where_ref, zt_ref, *refs):
+    bufs, (out_ref, s_ref, z, now, prev, straight, *scattered, sems) = refs[:sources], refs[sources:]
     tiles, slots = s_ref.shape[:2]
     orb = s_ref.shape[2]
     tile_rows = slots // PER_ROW
     pieces = zt_ref.shape[0]
-    n_row = tile_rows // per_piece
 
     for i, buf in enumerate(bufs):
         tile = where_ref[i]
@@ -84,43 +84,46 @@
         for b in range(per_piece):
             own = zt_ref[p, :, b * orb : (b + 1) * orb]
             z[p * per_piece + b] = own
-            prev[p * per_piece + b] = own.astype(jnp.float32)
-
-    def tile_step(first, tile, carry):
-        if first:
-            pltpu.make_async_copy(bufs[0], s_ref.at[tile], sems.at[tile]).wait()
-        row_base = tile // n_row * tile_rows
-
-        direct, mirrored, places = [], [], []
+            now[p * per_piece + b] = own.astype(jnp.float32)
+    prev[...] = jnp.zeros_like(prev)
+
+    def row_group(step, across, carry):
+        group = [across * n_row + r for r in range(n_row)]
+
+        @pl.when(step == 0)
+        def _():
+            for tile in group:
+                pltpu.make_async_copy(bufs[0], s_ref.at[tile], sems.at[tile]).wait()
+
         for t in range(tile_rows):
-            pair = jnp.concatenate([s_ref[tile, t * PER_ROW + p] for p in range(PER_ROW)], axis=1)
-            where = [ids_ref[tile, t * PER_ROW + p] for p in range(PER_ROW)]
+            places = [(tile, t * PER_ROW + p) for tile in group for p in range(PER_ROW)]
+            strip = jnp.concatenate([s_ref[tile, slot] for tile, slot in places], axis=1)
+            where = [ids_ref[tile, slot] for tile, slot in places]
             wide = jnp.concatenate([z[g] for g in where], axis=1)
-            tall = z[row_base + t]
-            direct.append(
-                lax.dot_general(wide, pair, (((1,), (1,)), ((), ())), preferred_element_type=jnp.float32)
+            tall = z[across * tile_rows + t]
+            straight[across * tile_rows + t] = lax.dot_general(
+                wide, strip, (((1,), (1,)), ((), ())), preferred_element_type=jnp.float32
             )
-            both = jnp.dot(tall, pair, preferred_element_type=jnp.float32)
-            for p in range(PER_ROW):
-                places.append(where[p])
-                mirrored.append(both[:, p * orb : (p + 1) * orb])
-        for t in range(tile_rows):
-            acc[row_base + t] += direct[t]
-        for g, term in zip(places, mirrored):
-            acc[g] += term
+            turned = jnp.dot(tall, strip, preferred_element_type=jnp.float32)
+            for i, g in enumerate(where):
+                scattered[i % len(scattered)][g] += turned[:, i * orb : (i + 1) * orb]
         return carry
 
-    for step in range(DEG):
-        acc[...] = jnp.zeros_like(acc)
-        lax.fori_loop(0, tiles, functools.partial(tile_step, step == 0), 0)
-        if step == 0:
-            now[...] = acc[...]
-        else:
-            nxt = 2.0 * acc[...] - prev[...]
-            prev[...] = now[...]
-            now[...] = nxt
-        if step < DEG - 1:
-            z[...] = now[...].astype(z.dtype)
+    def one_step(step, carry):
+        for ref in scattered:
+            ref[...] = jnp.zeros_like(ref)
+        lax.fori_loop(0, tiles // n_row, functools.partial(row_group, step), 0)
+        total = straight[...]
+        for ref in scattered:
+            total += ref[...]
+        later = step > 0
+        total = jnp.where(later, 2.0, 1.0) * total - jnp.where(later, 1.0, 0.0) * prev[...]
+        prev[...] = now[...]
+        now[...] = total
+        z[...] = total.astype(z.dtype)
+        return carry
+
+    lax.fori_loop(0, DEG, one_step, 0)
     for p in range(pieces):
         for b in range(per_piece):
             g = p * per_piece + b
@@ -188,7 +191,7 @@
     ids = (local // per_piece * n_row + down) * per_piece + local % per_piece
 
     done = pl.pallas_call(
-        functools.partial(filter_kernel, per_piece, len(bufs)),
+        functools.partial(filter_kernel, per_piece, n_row, len(bufs)),
         out_shape=jax.ShapeDtypeStruct((n_dev, 2, share, rows), jnp.bfloat16),
         in_specs=[
             pl.BlockSpec(memory_space=pltpu.SMEM),
@@ -200,9 +203,7 @@
         scratch_shapes=[
             pltpu.VMEM((n_dev, slots, orb, orb), blocks.dtype),
             pltpu.VMEM((n_blocks, share, orb), jnp.bfloat16),
-            pltpu.VMEM((n_blocks, share, orb), jnp.float32),
-            pltpu.VMEM((n_blocks, share, orb), jnp.float32),
-            pltpu.VMEM((n_blocks, share, orb), jnp.float32),
+            *[pltpu.VMEM((n_blocks, share, orb), jnp.float32)] * (3 + SPLIT),
             pltpu.SemaphoreType.DMA((n_dev,)),
         ],
         compiler_params=pltpu.CompilerParams(vmem_limit_bytes=32 * 2**20),

time: 145 us -> 137 us (0.945)
  Pallas kernels: 25.9 us -> 17.7 us
    pallas_call x1, Pallas kernels: 25.9 us -> 17.7 us  [gather_plan(): pl.pallas_call(functools.partial(filter_kernel, per_piece, n_row, len(buf...]
where the time goes in v3:
time: 137 us; the launch traced here: 135 us
  starting transfers between devices  52.4 us (38%)
  waiting for transfers between devices  27.6 us (20%)
  blocking collectives  18.1 us (13%)
  local copies, waits for them, and re-layouts  17.7 us (13%)
  Pallas kernels  17.7 us (13%)
    ppermute x27, starting transfers between devices, send(): return lax.ppermute(buf, LANES, pairs)  44.8 us
    ppermute x27, waiting for transfers between devices, send(): return lax.ppermute(buf, LANES, pairs)  26.5 us
    all_to_all x1, blocking collectives, gather_plan(): back = lax.all_to_all(done, LANES, split_axis=0, concat_axis=0, tiled=True)  18.1 us
    pallas_call x1, Pallas kernels, gather_plan(): pl.pallas_call(functools.partial(filter_kernel, per_piece, n_row, len(buf...  17.7 us
    unnamed x38, local copies, waits for them, and re-layouts  16.5 us
    all_to_all x1, starting transfers between devices, gather_plan(): lax.all_to_all(jnp.concatenate([turned, own_ids], axis=1), LANES, split_a...  7.58 us
  transfers between devices with their start and end apart: 28, of which 6 were waited for; matrix products, arithmetic and copies ran while one was open for 1% of the time, Pallas kernels for 0%

profile of v3, /device:TPU:0, one launch (start us, length us, event | category | flops | bytes accessed | tf_op | source)
XLA Modules:
  0.0 135.4 jit_solution(17093105290658733083)
XLA Ops:
  0.6 3.0 %collective-permute-start.6 = (bf16[16,128,128]{2,1,0:T(8,128)(2,1)}, bf16[16,128,128]{2,1,0:T(8,128)(2,1)S(1)}, u32[]{:S(2)}, u32[]{:S(2)}) collective-permute-start(bf16[16,128,128]{2,1,0:T(8,128)(2,1)} %bitcast.38), channel_id=1, source_target_pairs={{0,8},{1,9},{2,10},{3,11},{4,12},{5,13},{6,14},{7,15},{8,0},{9,1},... | collective-permute-start | bytes 1572872 | tf_op jit(solution)/shard_map/ppermute | solution.py:139
  5.0 4.6 %collective-permute-start = (bf16[16,128,128]{2,1,0:T(8,128)(2,1)}, bf16[16,128,128]{2,1,0:T(8,128)(2,1)S(1)}, u32[]{:S(2)}, u32[]{:S(2)}) collective-permute-start(bf16[16,128,128]{2,1,0:T(8,128)(2,1)} %bitcast.41), channel_id=1, source_target_pairs={{0,1},{4,5},{8,9},{12,13},{1,2},{5,6},{9,10},{13,14},{2,3},{6,7},{... | collective-permute-start | bytes 1572872 | tf_op jit(solution)/shard_map/ppermute | solution.py:139
  9.6 6.2 %collective-permute-done.6.refs_7_ = bf16[16,128,128]{2,1,0:T(8,128)(2,1)S(1)} collective-permute-done((bf16[16,128,128]{2,1,0:T(8,128)(2,1)}, bf16[16,128,128]{2,1,0:T(8,128)(2,1)S(1)}, u32[]{:S(2)}, u32[]{:S(2)}) %collective-permute-start.6) | collective-permute-done | bytes 524320 | tf_op jit(solution)/shard_map/ppermute | solution.py:139
  15.8 3.3 %collective-permute-done.1.refs_2_ = bf16[16,128,128]{2,1,0:T(8,128)(2,1)S(1)} collective-permute-done((bf16[16,128,128]{2,1,0:T(8,128)(2,1)}, bf16[16,128,128]{2,1,0:T(8,128)(2,1)S(1)}, u32[]{:S(2)}, u32[]{:S(2)}) %collective-permute-start.1) | collective-permute-done | bytes 524320 | tf_op jit(solution)/shard_map/ppermute | solution.py:139
  19.1 1.9 %collective-permute-start.15 = (bf16[16,128,128]{2,1,0:T(8,128)(2,1)S(1)}, bf16[16,128,128]{2,1,0:T(8,128)(2,1)S(1)}, u32[]{:S(2)}, u32[]{:S(2)}) collective-permute-start(bf16[16,128,128]{2,1,0:T(8,128)(2,1)S(1)} %collective-permute-done.1.refs_2_), channel_id=1, source_target_pairs={{0,4},{1,5},{2,6},{4,0},{5,1},{6,2},{8,12},{9,13},{10,14},{12,8},{... | collective-permute-start | bytes 1572872 | tf_op jit(solution)/shard_map/ppermute | solution.py:139
  21.1 2.3 %collective-permute-start.8 = (bf16[16,128,128]{2,1,0:T(8,128)(2,1)S(1)}, bf16[16,128,128]{2,1,0:T(8,128)(2,1)S(1)}, u32[]{:S(2)}, u32[]{:S(2)}) collective-permute-start(bf16[16,128,128]{2,1,0:T(8,128)(2,1)S(1)} %collective-permute-done.1.refs_2_), channel_id=1, source_target_pairs={{0,8},{1,9},{2,10},{4,12},{5,13},{6,14},{8,0},{9,1},{10,2},{12,4},... | collective-permute-start | bytes 1572872 | tf_op jit(solution)/shard_map/ppermute | solution.py:139
  28.3 8.9 %collective-permute-done.8.refs_9_ = bf16[16,128,128]{2,1,0:T(8,128)(2,1)S(1)} collective-permute-done((bf16[16,128,128]{2,1,0:T(8,128)(2,1)S(1)}, bf16[16,128,128]{2,1,0:T(8,128)(2,1)S(1)}, u32[]{:S(2)}, u32[]{:S(2)}) %collective-permute-start.8) | collective-permute-done | bytes 524320 | tf_op jit(solution)/shard_map/ppermute | solution.py:139
  37.3 1.9 %collective-permute-start.22 = (bf16[16,128,128]{2,1,0:T(8,128)(2,1)S(1)}, bf16[16,128,128]{2,1,0:T(8,128)(2,1)S(1)}, u32[]{:S(2)}, u32[]{:S(2)}) collective-permute-start(bf16[16,128,128]{2,1,0:T(8,128)(2,1)S(1)} %collective-permute-done.8.refs_9_), channel_id=1, source_target_pairs={{0,4},{1,5},{2,6},{4,0},{5,1},{6,2},{8,12},{9,13},{10,14},{12,8},{... | collective-permute-start | bytes 1572872 | tf_op jit(solution)/shard_map/ppermute | solution.py:139
  40.0 2.4 %collective-permute-start.17 = (bf16[16,128,128]{2,1,0:T(8,128)(2,1)S(1)}, bf16[16,128,128]{2,1,0:T(8,128)(2,1)S(1)}, u32[]{:S(2)}, u32[]{:S(2)}) collective-permute-start(bf16[16,128,128]{2,1,0:T(8,128)(2,1)S(1)} %collective-permute-done.3.refs_4_), channel_id=1, source_target_pairs={{0,4},{1,5},{4,0},{5,1},{8,12},{9,13},{12,8},{13,9},{16,20},{17,21... | collective-permute-start | bytes 1572872 | tf_op jit(solution)/shard_map/ppermute | solution.py:139
  43.3 2.4 %collective-permute-start.10 = (bf16[16,128,128]{2,1,0:T(8,128)(2,1)S(1)}, bf16[16,128,128]{2,1,0:T(8,128)(2,1)}, u32[]{:S(2)}, u32[]{:S(2)}) collective-permute-start(bf16[16,128,128]{2,1,0:T(8,128)(2,1)S(1)} %collective-permute-done.3.refs_4_), channel_id=1, source_target_pairs={{0,8},{1,9},{4,12},{5,13},{8,0},{9,1},{12,4},{13,5},{16,24},{17,25... | collective-permute-start | bytes 1572872 | tf_op jit(solution)/shard_map/ppermute | solution.py:139
  50.1 1.5 %collective-permute-start.4 = (bf16[16,128,128]{2,1,0:T(8,128)(2,1)}, bf16[16,128,128]{2,1,0:T(8,128)(2,1)}, u32[]{:S(2)}, u32[]{:S(2)}) collective-permute-start(bf16[16,128,128]{2,1,0:T(8,128)(2,1)} %collective-permute-done.2.refs_3_), channel_id=1, source_target_pairs={{2,3},{6,7},{10,11},{14,15},{18,19},{22,23},{26,27},{30,31}} | collective-permute-start | bytes 1572872 | tf_op jit(solution)/shard_map/ppermute | solution.py:139
  53.8 5.3 %collective-permute-done.10.refs_11_ = bf16[16,128,128]{2,1,0:T(8,128)(2,1)} collective-permute-done((bf16[16,128,128]{2,1,0:T(8,128)(2,1)S(1)}, bf16[16,128,128]{2,1,0:T(8,128)(2,1)}, u32[]{:S(2)}, u32[]{:S(2)}) %collective-permute-start.10) | collective-permute-done | bytes 524320 | tf_op jit(solution)/shard_map/ppermute | solution.py:139
  59.1 1.5 %collective-permute-start.9 = (bf16[16,128,128]{2,1,0:T(8,128)(2,1)}, bf16[16,128,128]{2,1,0:T(8,128)(2,1)}, u32[]{:S(2)}, u32[]{:S(2)}) collective-permute-start(bf16[16,128,128]{2,1,0:T(8,128)(2,1)} %collective-permute-done.2.refs_3_), channel_id=1, source_target_pairs={{2,10},{3,11},{6,14},{7,15},{10,2},{11,3},{14,6},{15,7},{18,26},{1... | collective-permute-start | bytes 1572872 | tf_op jit(solution)/shard_map/ppermute | solution.py:139
  60.6 2.7 %collective-permute-done.5.refs_6_ = bf16[16,128,128]{2,1,0:T(8,128)(2,1)} collective-permute-done((bf16[16,128,128]{2,1,0:T(8,128)(2,1)S(1)}, bf16[16,128,128]{2,1,0:T(8,128)(2,1)}, u32[]{:S(2)}, u32[]{:S(2)}) %collective-permute-start.5) | collective-permute-done | bytes 524320 | tf_op jit(solution)/shard_map/ppermute | solution.py:139
  63.3 1.9 %collective-permute-start.24 = (bf16[16,128,128]{2,1,0:T(8,128)(2,1)}, bf16[16,128,128]{2,1,0:T(8,128)(2,1)}, u32[]{:S(2)}, u32[]{:S(2)}) collective-permute-start(bf16[16,128,128]{2,1,0:T(8,128)(2,1)} %collective-permute-done.10.refs_11_), channel_id=1, source_target_pairs={{0,4},{1,5},{4,0},{5,1},{8,12},{9,13},{12,8},{13,9},{16,20},{17,21... | collective-permute-start | bytes 1572872 | tf_op jit(solution)/shard_map/ppermute | solution.py:139
  66.0 2.4 %collective-permute-start.12 = (bf16[16,128,128]{2,1,0:T(8,128)(2,1)}, bf16[16,128,128]{2,1,0:T(8,128)(2,1)}, u32[]{:S(2)}, u32[]{:S(2)}) collective-permute-start(bf16[16,128,128]{2,1,0:T(8,128)(2,1)} %collective-permute-done.5.refs_6_), channel_id=1, source_target_pairs={{0,8},{4,12},{8,0},{12,4},{16,24},{20,28},{24,16},{28,20}} | collective-permute-start | bytes 1572872 | tf_op jit(solution)/shard_map/ppermute | solution.py:139
  68.4 1.5 %collective-permute-start.11 = (bf16[16,128,128]{2,1,0:T(8,128)(2,1)}, bf16[16,128,128]{2,1,0:T(8,128)(2,1)}, u32[]{:S(2)}, u32[]{:S(2)}) collective-permute-start(bf16[16,128,128]{2,1,0:T(8,128)(2,1)} %collective-permute-done.4.refs_5_), channel_id=1, source_target_pairs={{3,11},{7,15},{11,3},{15,7},{19,27},{23,31},{27,19},{31,23}} | collective-permute-start | bytes 1572872 | tf_op jit(solution)/shard_map/ppermute | solution.py:139
  71.7 7.6 %all-to-all-start = ((bf16[16,32,256]{2,1,0:T(8,128)(2,1)}), bf16[16,32,256]{2,1,0:T(8,128)(2,1)S(1)}, u32[]{:S(2)}, u32[]{:S(2)}) async-start(bf16[16,32,256]{2,1,0:T(8,128)(2,1)} %pad_maximum_fusion), calls=%async_computation | async-start | bytes 524288 | tf_op jit(solution)/shard_map/all_to_all | solution.py:185
  79.5 2.2 %collective-permute-start.19 = (bf16[16,128,128]{2,1,0:T(8,128)(2,1)}, bf16[16,128,128]{2,1,0:T(8,128)(2,1)}, u32[]{:S(2)}, u32[]{:S(2)}) collective-permute-start(bf16[16,128,128]{2,1,0:T(8,128)(2,1)} %collective-permute-done.5.refs_6_), channel_id=1, source_target_pairs={{0,4},{4,0},{8,12},{12,8},{16,20},{20,16},{24,28},{28,24}} | collective-permute-start | bytes 1572872 | tf_op jit(solution)/shard_map/ppermute | solution.py:139
  81.7 1.5 %collective-permute-start.18 = (bf16[16,128,128]{2,1,0:T(8,128)(2,1)}, bf16[16,128,128]{2,1,0:T(8,128)(2,1)}, u32[]{:S(2)}, u32[]{:S(2)}) collective-permute-start(bf16[16,128,128]{2,1,0:T(8,128)(2,1)} %collective-permute-done.4.refs_5_), channel_id=1, source_target_pairs={{3,7},{7,3},{11,15},{15,11},{19,23},{23,19},{27,31},{31,27}} | collective-permute-start | bytes 1572872 | tf_op jit(solution)/shard_map/ppermute | solution.py:139
  84.7 2.1 %collective-permute-start.26 = (bf16[16,128,128]{2,1,0:T(8,128)(2,1)}, bf16[16,128,128]{2,1,0:T(8,128)(2,1)}, u32[]{:S(2)}, u32[]{:S(2)}) collective-permute-start(bf16[16,128,128]{2,1,0:T(8,128)(2,1)} %collective-permute-done.12.refs_13_), channel_id=1, source_target_pairs={{0,4},{4,0},{8,12},{12,8},{16,20},{20,16},{24,28},{28,24}} | collective-permute-start | bytes 1572872 | tf_op jit(solution)/shard_map/ppermute | solution.py:139
  86.8 1.5 %collective-permute-start.25 = (bf16[16,128,128]{2,1,0:T(8,128)(2,1)}, bf16[16,128,128]{2,1,0:T(8,128)(2,1)}, u32[]{:S(2)}, u32[]{:S(2)}) collective-permute-start(bf16[16,128,128]{2,1,0:T(8,128)(2,1)} %collective-permute-done.11.refs_12_), channel_id=1, source_target_pairs={{3,7},{7,3},{11,15},{15,11},{19,23},{23,19},{27,31},{31,27}} | collective-permute-start | bytes 1572872 | tf_op jit(solution)/shard_map/ppermute | solution.py:139
  97.8 17.7 %shard_map.50 = bf16[16,2,16,256]{3,2,1,0:T(8,128)(2,1)S(1)} custom-call(s32[16,16]{1,0:T(8,128)S(1)} %fusion.3.ids_ref, s32[28]{0:T(128)S(1)} %stack.115.where_ref, bf16[16,16,256]{2,1,0:T(8,128)(2,1)S(1)} %slice.19.zt_ref, bf16[16,128,128]{2,1,0:T(8,128)(2,1)S(1)} %bitcast.42, bf16[16,128,128]{2,1,0:T(8,128)(2,1)S(1)} %collective-permute-done.refs_1_, ...), custom_call_target="tpu_custom_call" | custom-call | tf_op jit(solution)/shard_map/pallas_call | solution.py:193
  115.6 18.1 %all_to_all.10 = bf16[16,2,16,256]{3,2,1,0:T(8,128)(2,1)S(1)} all-to-all(bf16[16,2,16,256]{3,2,1,0:T(8,128)(2,1)S(1)} %shard_map.50), channel_id=1, replica_groups=mesh['dom'=2,'col'=4,'row'=4] {'col','row'}, dimensions={0} | all-to-all | bytes 524288 | tf_op jit(solution)/shard_map/all_to_all | solution.py:211
  (84 shorter events, 30.1 us)
Async XLA Ops:
  0.6 15.2 %collective-permute-start.6 = (bf16[16,128,128]{2,1,0:T(8,128)(2,1)}, bf16[16,128,128]{2,1,0:T(8,128)(2,1)S(1)}, u32[]{:S(2)}, u32[]{:S(2)}) collective-permute-start(bf16[16,128,128]{2,1,0:T(8,128)(2,1)} %bitcast.38), channel_id=1, source_target_pairs={{0,8},{1,9},{2,10},{3,11},{4,12},{5,13},{6,14},{7,15},{8,0},{9,1},... | collective-permute-start | bytes 1572872 | tf_op jit(solution)/shard_map/ppermute | solution.py:139
  3.7 15.5 %collective-permute-start.1 = (bf16[16,128,128]{2,1,0:T(8,128)(2,1)}, bf16[16,128,128]{2,1,0:T(8,128)(2,1)S(1)}, u32[]{:S(2)}, u32[]{:S(2)}) collective-permute-start(bf16[16,128,128]{2,1,0:T(8,128)(2,1)} %bitcast.39), channel_id=1, source_target_pairs={{1,0},{5,4},{9,8},{13,12},{2,1},{6,5},{10,9},{14,13},{3,2},{7,6},{... | collective-permute-start | bytes 1572872 | tf_op jit(solution)/shard_map/ppermute | solution.py:139
  5.0 18.4 %collective-permute-start.13 = (bf16[16,128,128]{2,1,0:T(8,128)(2,1)}, bf16[16,128,128]{2,1,0:T(8,128)(2,1)S(1)}, u32[]{:S(2)}, u32[]{:S(2)}) collective-permute-start(bf16[16,128,128]{2,1,0:T(8,128)(2,1)} %bitcast.40), channel_id=1, source_target_pairs={{0,4},{1,5},{2,6},{3,7},{4,0},{5,1},{6,2},{7,3},{8,12},{9,13},{10,... | collective-permute-start | bytes 1572872 | tf_op jit(solution)/shard_map/ppermute | solution.py:139
  5.0 19.6 %collective-permute-start = (bf16[16,128,128]{2,1,0:T(8,128)(2,1)}, bf16[16,128,128]{2,1,0:T(8,128)(2,1)S(1)}, u32[]{:S(2)}, u32[]{:S(2)}) collective-permute-start(bf16[16,128,128]{2,1,0:T(8,128)(2,1)} %bitcast.41), channel_id=1, source_target_pairs={{0,1},{4,5},{8,9},{12,13},{1,2},{5,6},{9,10},{13,14},{2,3},{6,7},{... | collective-permute-start | bytes 1572872 | tf_op jit(solution)/shard_map/ppermute | solution.py:139
  15.8 9.6 %collective-permute-start.20 = (bf16[16,128,128]{2,1,0:T(8,128)(2,1)S(1)}, bf16[16,128,128]{2,1,0:T(8,128)(2,1)S(1)}, u32[]{:S(2)}, u32[]{:S(2)}) collective-permute-start(bf16[16,128,128]{2,1,0:T(8,128)(2,1)S(1)} %collective-permute-done.6.refs_7_), channel_id=1, source_target_pairs={{0,4},{1,5},{2,6},{3,7},{4,0},{5,1},{6,2},{7,3},{8,12},{9,13},{10,... | collective-permute-start | bytes 1572872 | tf_op jit(solution)/shard_map/ppermute | solution.py:139
  21.1 16.2 %collective-permute-start.8 = (bf16[16,128,128]{2,1,0:T(8,128)(2,1)S(1)}, bf16[16,128,128]{2,1,0:T(8,128)(2,1)S(1)}, u32[]{:S(2)}, u32[]{:S(2)}) collective-permute-start(bf16[16,128,128]{2,1,0:T(8,128)(2,1)S(1)} %collective-permute-done.1.refs_2_), channel_id=1, source_target_pairs={{0,8},{1,9},{2,10},{4,12},{5,13},{6,14},{8,0},{9,1},{10,2},{12,4},... | collective-permute-start | bytes 1572872 | tf_op jit(solution)/shard_map/ppermute | solution.py:139
  23.3 16.7 %collective-permute-start.3 = (bf16[16,128,128]{2,1,0:T(8,128)(2,1)S(1)}, bf16[16,128,128]{2,1,0:T(8,128)(2,1)S(1)}, u32[]{:S(2)}, u32[]{:S(2)}) collective-permute-start(bf16[16,128,128]{2,1,0:T(8,128)(2,1)S(1)} %collective-permute-done.1.refs_2_), channel_id=1, source_target_pairs={{1,0},{5,4},{9,8},{13,12},{2,1},{6,5},{10,9},{14,13},{17,16},{21,2... | collective-permute-start | bytes 1572872 | tf_op jit(solution)/shard_map/ppermute | solution.py:139
  24.7 17.8 %collective-permute-start.14 = (bf16[16,128,128]{2,1,0:T(8,128)(2,1)S(1)}, bf16[16,128,128]{2,1,0:T(8,128)(2,1)S(1)}, u32[]{:S(2)}, u32[]{:S(2)}) collective-permute-start(bf16[16,128,128]{2,1,0:T(8,128)(2,1)S(1)} %collective-permute-done.refs_1_), channel_id=1, source_target_pairs={{1,5},{2,6},{3,7},{5,1},{6,2},{7,3},{9,13},{10,14},{11,15},{13,9},... | collective-permute-start | bytes 1572872 | tf_op jit(solution)/shard_map/ppermute | solution.py:139
  25.4 20.3 %collective-permute-start.7 = (bf16[16,128,128]{2,1,0:T(8,128)(2,1)S(1)}, bf16[16,128,128]{2,1,0:T(8,128)(2,1)S(1)}, u32[]{:S(2)}, u32[]{:S(2)}) collective-permute-start(bf16[16,128,128]{2,1,0:T(8,128)(2,1)S(1)} %collective-permute-done.refs_1_), channel_id=1, source_target_pairs={{1,9},{2,10},{3,11},{5,13},{6,14},{7,15},{9,1},{10,2},{11,3},{13,5... | collective-permute-start | bytes 1572872 | tf_op jit(solution)/shard_map/ppermute | solution.py:139
  26.9 20.9 %collective-permute-start.2 = (bf16[16,128,128]{2,1,0:T(8,128)(2,1)S(1)}, bf16[16,128,128]{2,1,0:T(8,128)(2,1)}, u32[]{:S(2)}, u32[]{:S(2)}) collective-permute-start(bf16[16,128,128]{2,1,0:T(8,128)(2,1)S(1)} %collective-permute-done.refs_1_), channel_id=1, source_target_pairs={{1,2},{5,6},{9,10},{13,14},{2,3},{6,7},{10,11},{14,15},{17,18},{21... | collective-permute-start | bytes 1572872 | tf_op jit(solution)/shard_map/ppermute | solution.py:139
  37.3 12.0 %collective-permute-start.22 = (bf16[16,128,128]{2,1,0:T(8,128)(2,1)S(1)}, bf16[16,128,128]{2,1,0:T(8,128)(2,1)S(1)}, u32[]{:S(2)}, u32[]{:S(2)}) collective-permute-start(bf16[16,128,128]{2,1,0:T(8,128)(2,1)S(1)} %collective-permute-done.8.refs_9_), channel_id=1, source_target_pairs={{0,4},{1,5},{2,6},{4,0},{5,1},{6,2},{8,12},{9,13},{10,14},{12,8},{... | collective-permute-start | bytes 1572872 | tf_op jit(solution)/shard_map/ppermute | solution.py:139
  40.0 11.5 %collective-permute-start.17 = (bf16[16,128,128]{2,1,0:T(8,128)(2,1)S(1)}, bf16[16,128,128]{2,1,0:T(8,128)(2,1)S(1)}, u32[]{:S(2)}, u32[]{:S(2)}) collective-permute-start(bf16[16,128,128]{2,1,0:T(8,128)(2,1)S(1)} %collective-permute-done.3.refs_4_), channel_id=1, source_target_pairs={{0,4},{1,5},{4,0},{5,1},{8,12},{9,13},{12,8},{13,9},{16,20},{17,21... | collective-permute-start | bytes 1572872 | tf_op jit(solution)/shard_map/ppermute | solution.py:139
  43.3 15.8 %collective-permute-start.10 = (bf16[16,128,128]{2,1,0:T(8,128)(2,1)S(1)}, bf16[16,128,128]{2,1,0:T(8,128)(2,1)}, u32[]{:S(2)}, u32[]{:S(2)}) collective-permute-start(bf16[16,128,128]{2,1,0:T(8,128)(2,1)S(1)} %collective-permute-done.3.refs_4_), channel_id=1, source_target_pairs={{0,8},{1,9},{4,12},{5,13},{8,0},{9,1},{12,4},{13,5},{16,24},{17,25... | collective-permute-start | bytes 1572872 | tf_op jit(solution)/shard_map/ppermute | solution.py:139
  45.6 17.6 %collective-permute-start.5 = (bf16[16,128,128]{2,1,0:T(8,128)(2,1)S(1)}, bf16[16,128,128]{2,1,0:T(8,128)(2,1)}, u32[]{:S(2)}, u32[]{:S(2)}) collective-permute-start(bf16[16,128,128]{2,1,0:T(8,128)(2,1)S(1)} %collective-permute-done.3.refs_4_), channel_id=1, source_target_pairs={{1,0},{5,4},{9,8},{13,12},{17,16},{21,20},{25,24},{29,28}} | collective-permute-start | bytes 1572872 | tf_op jit(solution)/shard_map/ppermute | solution.py:139
  47.8 17.4 %collective-permute-start.21 = (bf16[16,128,128]{2,1,0:T(8,128)(2,1)S(1)}, bf16[16,128,128]{2,1,0:T(8,128)(2,1)S(1)}, u32[]{:S(2)}, u32[]{:S(2)}) collective-permute-start(bf16[16,128,128]{2,1,0:T(8,128)(2,1)S(1)} %collective-permute-done.7.refs_8_), channel_id=1, source_target_pairs={{1,5},{2,6},{3,7},{5,1},{6,2},{7,3},{9,13},{10,14},{11,15},{13,9},... | collective-permute-start | bytes 1572872 | tf_op jit(solution)/shard_map/ppermute | solution.py:139
  50.1 18.4 %collective-permute-start.4 = (bf16[16,128,128]{2,1,0:T(8,128)(2,1)}, bf16[16,128,128]{2,1,0:T(8,128)(2,1)}, u32[]{:S(2)}, u32[]{:S(2)}) collective-permute-start(bf16[16,128,128]{2,1,0:T(8,128)(2,1)} %collective-permute-done.2.refs_3_), channel_id=1, source_target_pairs={{2,3},{6,7},{10,11},{14,15},{18,19},{22,23},{26,27},{30,31}} | collective-permute-start | bytes 1572872 | tf_op jit(solution)/shard_map/ppermute | solution.py:139
  52.4 27.1 %collective-permute-start.16 = (bf16[16,128,128]{2,1,0:T(8,128)(2,1)}, bf16[16,128,128]{2,1,0:T(8,128)(2,1)}, u32[]{:S(2)}, u32[]{:S(2)}) collective-permute-start(bf16[16,128,128]{2,1,0:T(8,128)(2,1)} %collective-permute-done.2.refs_3_), channel_id=1, source_target_pairs={{2,6},{3,7},{6,2},{7,3},{10,14},{11,15},{14,10},{15,11},{18,22},{1... | collective-permute-start | bytes 1572872 | tf_op jit(solution)/shard_map/ppermute | solution.py:139
  59.1 22.6 %collective-permute-start.9 = (bf16[16,128,128]{2,1,0:T(8,128)(2,1)}, bf16[16,128,128]{2,1,0:T(8,128)(2,1)}, u32[]{:S(2)}, u32[]{:S(2)}) collective-permute-start(bf16[16,128,128]{2,1,0:T(8,128)(2,1)} %collective-permute-done.2.refs_3_), channel_id=1, source_target_pairs={{2,10},{3,11},{6,14},{7,15},{10,2},{11,3},{14,6},{15,7},{18,26},{1... | collective-permute-start | bytes 1572872 | tf_op jit(solution)/shard_map/ppermute | solution.py:139
  63.3 19.9 %collective-permute-start.24 = (bf16[16,128,128]{2,1,0:T(8,128)(2,1)}, bf16[16,128,128]{2,1,0:T(8,128)(2,1)}, u32[]{:S(2)}, u32[]{:S(2)}) collective-permute-start(bf16[16,128,128]{2,1,0:T(8,128)(2,1)} %collective-permute-done.10.refs_11_), channel_id=1, source_target_pairs={{0,4},{1,5},{4,0},{5,1},{8,12},{9,13},{12,8},{13,9},{16,20},{17,21... | collective-permute-start | bytes 1572872 | tf_op jit(solution)/shard_map/ppermute | solution.py:139
  66.0 18.6 %collective-permute-start.12 = (bf16[16,128,128]{2,1,0:T(8,128)(2,1)}, bf16[16,128,128]{2,1,0:T(8,128)(2,1)}, u32[]{:S(2)}, u32[]{:S(2)}) collective-permute-start(bf16[16,128,128]{2,1,0:T(8,128)(2,1)} %collective-permute-done.5.refs_6_), channel_id=1, source_target_pairs={{0,8},{4,12},{8,0},{12,4},{16,24},{20,28},{24,16},{28,20}} | collective-permute-start | bytes 1572872 | tf_op jit(solution)/shard_map/ppermute | solution.py:139
  68.4 18.3 %collective-permute-start.11 = (bf16[16,128,128]{2,1,0:T(8,128)(2,1)}, bf16[16,128,128]{2,1,0:T(8,128)(2,1)}, u32[]{:S(2)}, u32[]{:S(2)}) collective-permute-start(bf16[16,128,128]{2,1,0:T(8,128)(2,1)} %collective-permute-done.4.refs_5_), channel_id=1, source_target_pairs={{3,11},{7,15},{11,3},{15,7},{19,27},{23,31},{27,19},{31,23}} | collective-permute-start | bytes 1572872 | tf_op jit(solution)/shard_map/ppermute | solution.py:139
  71.7 17.7 %all-to-all-start = ((bf16[16,32,256]{2,1,0:T(8,128)(2,1)}), bf16[16,32,256]{2,1,0:T(8,128)(2,1)S(1)}, u32[]{:S(2)}, u32[]{:S(2)}) async-start(bf16[16,32,256]{2,1,0:T(8,128)(2,1)} %pad_maximum_fusion), calls=%async_computation | async-start | bytes 524288 | tf_op jit(solution)/shard_map/all_to_all | solution.py:185
  79.5 10.0 %collective-permute-start.19 = (bf16[16,128,128]{2,1,0:T(8,128)(2,1)}, bf16[16,128,128]{2,1,0:T(8,128)(2,1)}, u32[]{:S(2)}, u32[]{:S(2)}) collective-permute-start(bf16[16,128,128]{2,1,0:T(8,128)(2,1)} %collective-permute-done.5.refs_6_), channel_id=1, source_target_pairs={{0,4},{4,0},{8,12},{12,8},{16,20},{20,16},{24,28},{28,24}} | collective-permute-start | bytes 1572872 | tf_op jit(solution)/shard_map/ppermute | solution.py:139
  81.7 7.7 %collective-permute-start.18 = (bf16[16,128,128]{2,1,0:T(8,128)(2,1)}, bf16[16,128,128]{2,1,0:T(8,128)(2,1)}, u32[]{:S(2)}, u32[]{:S(2)}) collective-permute-start(bf16[16,128,128]{2,1,0:T(8,128)(2,1)} %collective-permute-done.4.refs_5_), channel_id=1, source_target_pairs={{3,7},{7,3},{11,15},{15,11},{19,23},{23,19},{27,31},{31,27}} | collective-permute-start | bytes 1572872 | tf_op jit(solution)/shard_map/ppermute | solution.py:139
  (22 other events, 122.6 us)

commit v4 on v3

--- a/solution.py
+++ b/solution.py
@@ -66,19 +66,18 @@
     return (now, prev)
 
 
-def filter_kernel(per_piece, n_row, sources, ids_ref, where_ref, zt_ref, *refs):
-    bufs, (out_ref, s_ref, z, now, prev, straight, *scattered, sems) = refs[:sources], refs[sources:]
+def filter_kernel(per_piece, n_row, starts, ids_ref, where_ref, zt_ref, *refs):
+    bufs, (out_ref, s_ref, z, now, prev, straight, *scattered, sems) = refs[: len(starts)], refs[len(starts) :]
     tiles, slots = s_ref.shape[:2]
     orb = s_ref.shape[2]
     tile_rows = slots // PER_ROW
     pieces = zt_ref.shape[0]
 
-    for i, buf in enumerate(bufs):
-        tile = where_ref[i]
-
-        @pl.when(tile >= 0)
-        def _():
-            pltpu.make_async_copy(buf, s_ref.at[tile], sems.at[tile]).start()
+    copies = []
+    for i, (buf, start) in enumerate(zip(bufs, starts)):
+        place = s_ref.at[where_ref[i], pl.ds(start, buf.shape[0])]
+        copies.append(pltpu.make_async_copy(buf, place, sems.at[i]))
+        copies[-1].start()
 
     for p in range(pieces):
         for b in range(per_piece):
@@ -87,14 +86,11 @@
             now[p * per_piece + b] = own.astype(jnp.float32)
     prev[...] = jnp.zeros_like(prev)
 
-    def row_group(step, across, carry):
+    for copy in copies:
+        copy.wait()
+
+    def row_group(across, carry):
         group = [across * n_row + r for r in range(n_row)]
-
-        @pl.when(step == 0)
-        def _():
-            for tile in group:
-                pltpu.make_async_copy(bufs[0], s_ref.at[tile], sems.at[tile]).wait()
-
         for t in range(tile_rows):
             places = [(tile, t * PER_ROW + p) for tile in group for p in range(PER_ROW)]
             strip = jnp.concatenate([s_ref[tile, slot] for tile, slot in places], axis=1)
@@ -112,7 +108,7 @@
     def one_step(step, carry):
         for ref in scattered:
             ref[...] = jnp.zeros_like(ref)
-        lax.fori_loop(0, tiles // n_row, functools.partial(row_group, step), 0)
+        lax.fori_loop(0, tiles // n_row, row_group, 0)
         total = straight[...]
         for ref in scattered:
             total += ref[...]
@@ -133,39 +129,38 @@
 
 def gather_tiles(own, n_col, n_row):
     col, row = lax.axis_index("col"), lax.axis_index("row")
-    index = lambda c, r: c * n_row + r
-
-    def send(buf, pairs):
+    half = own.shape[0] // 2
+
+    def send(buf, flip_col, flip_row):
+        pairs = [
+            (c * n_row + r, (c ^ flip_col) * n_row + (r ^ flip_row))
+            for c in range(n_col)
+            for r in range(n_row)
+        ]
         return lax.ppermute(buf, LANES, pairs)
 
-    held = [(own, 0, 0)]
-    for sign in (1, -1):
-        buf = own
-        for hop in range(1, n_row):
-            pairs = []
-            for r in range(n_row):
-                source = r - sign * (hop - 1)
-                if 0 <= r + sign < n_row and 0 <= source < n_row:
-                    pairs += [(index(c, r), index(c, r + sign)) for c in range(n_col)]
-            buf = send(buf, pairs)
-            held.append((buf, -sign * hop, 0))
-    held.sort(key=lambda item: abs(item[1]))
-    bit = n_col // 2
-    while bit:
-        for buf, shift, flips in list(held):
-            pairs = [
-                (index(c, r), index(c ^ bit, r))
-                for c in range(n_col)
-                for r in range(n_row)
-                if 0 <= r + shift < n_row
-            ]
-            held.append((send(buf, pairs), shift, flips | bit))
-        bit //= 2
-    where = []
-    for _, shift, flips in held:
-        r = row + shift
-        where.append(jnp.where((r >= 0) & (r < n_row), (col ^ flips) * n_row + r, -1))
-    return [buf for buf, _, _ in held], jnp.stack(where).astype(jnp.int32)
+    near = send(own, 0, 1)
+    over_own = send(own, 2, 0)
+    far = send(own, 0, 3)
+    over_near = send(near, 2, 0)
+    last = send(far, 0, 1)
+    over_far = send(far, 2, 0)
+    over_last = send(last[:half], 2, 0)
+    side_last = send(over_far[half:], 0, 1)
+    held = [
+        (own, 0, 0, 0),
+        (near, 0, 1, 0),
+        (over_own, 2, 0, 0),
+        (far, 0, 3, 0),
+        (over_near, 2, 1, 0),
+        (last, 0, 2, 0),
+        (over_far, 2, 3, 0),
+        (over_last, 2, 2, 0),
+        (side_last, 2, 2, half),
+    ]
+    held += [(send(buf, 1, 0), c ^ 1, r, slot) for buf, c, r, slot in held]
+    where = jnp.stack([(col ^ c) * n_row + (row ^ r) for _, c, r, _ in held]).astype(jnp.int32)
+    return [buf for buf, _, _, _ in held], [slot for _, _, _, slot in held], where
 
 
 def gather_plan(vectors, blocks, cols):
@@ -177,7 +172,7 @@
     per_piece = rows // orb
     n_blocks = n_dev * per_piece
 
-    bufs, where = gather_tiles(blocks[0, 0], n_col, n_row)
+    bufs, starts, where = gather_tiles(blocks[0, 0], n_col, n_row)
 
     turned = vectors.T.reshape(n_dev, share, rows)
     own_ids = jnp.pad(cols[0, 0].astype(jnp.bfloat16), (0, rows - slots))
@@ -191,7 +186,7 @@
     ids = (local // per_piece * n_row + down) * per_piece + local % per_piece
 
     done = pl.pallas_call(
-        functools.partial(filter_kernel, per_piece, n_row, len(bufs)),
+        functools.partial(filter_kernel, per_piece, n_row, starts),
         out_shape=jax.ShapeDtypeStruct((n_dev, 2, share, rows), jnp.bfloat16),
         in_specs=[
             pl.BlockSpec(memory_space=pltpu.SMEM),
@@ -204,7 +199,7 @@
             pltpu.VMEM((n_dev, slots, orb, orb), blocks.dtype),
             pltpu.VMEM((n_blocks, share, orb), jnp.bfloat16),
             *[pltpu.VMEM((n_blocks, share, orb), jnp.float32)] * (3 + SPLIT),
-            pltpu.SemaphoreType.DMA((n_dev,)),
+            pltpu.SemaphoreType.DMA((len(bufs),)),
         ],
         compiler_params=pltpu.CompilerParams(vmem_limit_bytes=32 * 2**20),
     )(ids, where, zt, *bufs)
@@ -215,7 +210,8 @@
 
 def per_device(vectors, blocks, cols):
     n_dev = lax.axis_size(LANES)
-    if n_dev * blocks.size * blocks.dtype.itemsize <= GATHER_LIMIT:
+    line_of_four = lax.axis_size("col") == 4 and lax.axis_size("row") == 4
+    if line_of_four and n_dev * blocks.size * blocks.dtype.itemsize <= GATHER_LIMIT:
         return gather_plan(vectors, blocks, cols)
     return spread_plan(vectors, blocks, cols)
 

time: 137 us -> 98.6 us (0.72)
  starting transfers between devices: 52.4 us -> 29 us
  local copies, waits for them, and re-layouts: 17.7 us -> 5.2 us
  blocking collectives: 18.1 us -> 14.4 us
  Pallas kernels: 17.7 us -> 19.2 us
    ppermute x27 -> x17, starting transfers between devices: 44.8 us -> 24.6 us  [send(): return lax.ppermute(buf, LANES, pairs)]
    unnamed x38 -> x6, local copies, waits for them, and re-layouts: 16.5 us -> 1.68 us
    all_to_all x1, blocking collectives: 18.1 us -> 14.4 us  [gather_plan(): back = lax.all_to_all(done, LANES, split_axis=0, concat_axis=0, tiled=True)]
    all_to_all x1, starting transfers between devices: 7.58 us -> 4.4 us  [gather_plan(): lax.all_to_all(jnp.concatenate([turned, own_ids], axis=1), LANES, split_a...]
    ppermute x27 -> x17, waiting for transfers between devices: 26.5 us -> 28 us  [send(): return lax.ppermute(buf, LANES, pairs)]
    slice x0 -> x2, local copies, waits for them, and re-layouts: none -> 1.45 us  [the longest x1 0.73 us: gather_tiles(): side_last = send(over_far[half:], 0, 1)]
    pallas_call x1, Pallas kernels: 17.7 us -> 19.2 us  [gather_plan(): pl.pallas_call(functools.partial(filter_kernel, per_piece, n_row, starts)...]
  transfers between devices with their start and end apart: 28 -> 18, of which waited for: 6 -> 4; matrix products, arithmetic and copies ran while one was open for 1% -> 5% of each run, Pallas kernels for 0% -> 0%
where the time goes in v4:
time: 98.6 us; the launch traced here: 98.2 us
  starting transfers between devices  29 us (29%)
  waiting for transfers between devices  28 us (28%)
  Pallas kernels  19.2 us (19%)
  blocking collectives  14.4 us (15%)
  local copies, waits for them, and re-layouts  5.2 us (5%)
  other arithmetic  1.63 us (2%)
    ppermute x17, waiting for transfers between devices, send(): return lax.ppermute(buf, LANES, pairs)  28 us
    ppermute x17, starting transfers between devices, send(): return lax.ppermute(buf, LANES, pairs)  24.6 us
    pallas_call x1, Pallas kernels, gather_plan(): pl.pallas_call(functools.partial(filter_kernel, per_piece, n_row, starts)...  19.2 us
    all_to_all x1, blocking collectives, gather_plan(): back = lax.all_to_all(done, LANES, split_axis=0, concat_axis=0, tiled=True)  14.4 us
    all_to_all x1, starting transfers between devices, gather_plan(): lax.all_to_all(jnp.concatenate([turned, own_ids], axis=1), LANES, split_a...  4.4 us
  transfers between devices with their start and end apart: 18, of which 4 were waited for; matrix products, arithmetic and copies ran while one was open for 5% of the time, Pallas kernels for 0%

profile of v4, /device:TPU:0, one launch (start us, length us, event | category | flops | bytes accessed | tf_op | source)
XLA Modules:
  0.0 98.2 jit_solution(11969040801897608759)
XLA Ops:
  0.6 5.1 %collective-permute-start.2 = (bf16[16,128,128]{2,1,0:T(8,128)(2,1)}, bf16[16,128,128]{2,1,0:T(8,128)(2,1)S(1)}, u32[]{:S(2)}, u32[]{:S(2)}) collective-permute-start(bf16[16,128,128]{2,1,0:T(8,128)(2,1)} %bitcast.26), channel_id=1, source_target_pairs={{0,3},{1,2},{2,1},{3,0},{4,7},{5,6},{6,5},{7,4},{8,11},{9,10},{10,... | collective-permute-start | bytes 1572872 | tf_op jit(solution)/shard_map/ppermute | solution.py:140
  5.8 1.5 %collective-permute-start.1 = (bf16[16,128,128]{2,1,0:T(8,128)(2,1)}, bf16[16,128,128]{2,1,0:T(8,128)(2,1)S(1)}, u32[]{:S(2)}, u32[]{:S(2)}) collective-permute-start(bf16[16,128,128]{2,1,0:T(8,128)(2,1)} %bitcast.27), channel_id=1, source_target_pairs={{0,8},{1,9},{2,10},{3,11},{4,12},{5,13},{6,14},{7,15},{8,0},{9,1},... | collective-permute-start | bytes 1572872 | tf_op jit(solution)/shard_map/ppermute | solution.py:140
  7.3 11.5 %collective-permute-done.2.refs_3_ = bf16[16,128,128]{2,1,0:T(8,128)(2,1)S(1)} collective-permute-done((bf16[16,128,128]{2,1,0:T(8,128)(2,1)}, bf16[16,128,128]{2,1,0:T(8,128)(2,1)S(1)}, u32[]{:S(2)}, u32[]{:S(2)}) %collective-permute-start.2) | collective-permute-done | bytes 524320 | tf_op jit(solution)/shard_map/ppermute | solution.py:140
  18.8 1.7 %collective-permute-start.5 = (bf16[16,128,128]{2,1,0:T(8,128)(2,1)S(1)}, bf16[16,128,128]{2,1,0:T(8,128)(2,1)S(1)}, u32[]{:S(2)}, u32[]{:S(2)}) collective-permute-start(bf16[16,128,128]{2,1,0:T(8,128)(2,1)S(1)} %collective-permute-done.2.refs_3_), channel_id=1, source_target_pairs={{0,8},{1,9},{2,10},{3,11},{4,12},{5,13},{6,14},{7,15},{8,0},{9,1},... | collective-permute-start | bytes 1572872 | tf_op jit(solution)/shard_map/ppermute | solution.py:140
  20.5 9.8 %collective-permute-start.4 = (bf16[16,128,128]{2,1,0:T(8,128)(2,1)S(1)}, bf16[16,128,128]{2,1,0:T(8,128)(2,1)S(1)}, u32[]{:S(2)}, u32[]{:S(2)}) collective-permute-start(bf16[16,128,128]{2,1,0:T(8,128)(2,1)S(1)} %collective-permute-done.2.refs_3_), channel_id=1, source_target_pairs={{0,1},{1,0},{2,3},{3,2},{4,5},{5,4},{6,7},{7,6},{8,9},{9,8},{10,11... | collective-permute-start | bytes 1572872 | tf_op jit(solution)/shard_map/ppermute | solution.py:140
  30.4 0.5 collective-permute-start.11
  31.1 1.3 %collective-permute-start.3 = (bf16[16,128,128]{2,1,0:T(8,128)(2,1)S(1)}, bf16[16,128,128]{2,1,0:T(8,128)(2,1)}, u32[]{:S(2)}, u32[]{:S(2)}) collective-permute-start(bf16[16,128,128]{2,1,0:T(8,128)(2,1)S(1)} %collective-permute-done.refs_1_), channel_id=1, source_target_pairs={{0,8},{1,9},{2,10},{3,11},{4,12},{5,13},{6,14},{7,15},{8,0},{9,1},... | collective-permute-start | bytes 1572872 | tf_op jit(solution)/shard_map/ppermute | solution.py:140
  32.4 8.9 %collective-permute-done.4.refs_5_ = bf16[16,128,128]{2,1,0:T(8,128)(2,1)S(1)} collective-permute-done((bf16[16,128,128]{2,1,0:T(8,128)(2,1)S(1)}, bf16[16,128,128]{2,1,0:T(8,128)(2,1)S(1)}, u32[]{:S(2)}, u32[]{:S(2)}) %collective-permute-start.4) | collective-permute-done | bytes 524320 | tf_op jit(solution)/shard_map/ppermute | solution.py:140
  41.3 1.0 %copy.5 = bf16[256,256]{1,0:T(8,128)(2,1)S(1)} copy(bf16[256,256]{0,1:T(8,128)(2,1)} %bitcast.34) | data formatting | bytes 262144 | tf_op jit(solution)/shard_map/transpose | solution.py:177
  42.4 0.7 pad_maximum_fusion
  43.1 4.4 %all-to-all-start = ((bf16[16,32,256]{2,1,0:T(8,128)(2,1)}), bf16[16,32,256]{2,1,0:T(8,128)(2,1)}, u32[]{:S(2)}, u32[]{:S(2)}) async-start(bf16[16,32,256]{2,1,0:T(8,128)(2,1)} %pad_maximum_fusion), calls=%async_computation | async-start | bytes 524288 | tf_op jit(solution)/shard_map/all_to_all | solution.py:180
  47.5 0.7 slice.29
  48.2 0.7 slice.28
  49.0 1.9 %collective-permute-start.7 = (bf16[8,128,128]{2,1,0:T(8,128)(2,1)}, bf16[8,128,128]{2,1,0:T(8,128)(2,1)S(1)}, u32[]{:S(2)}, u32[]{:S(2)}) collective-permute-start(bf16[8,128,128]{2,1,0:T(8,128)(2,1)} %slice.29), channel_id=1, source_target_pairs={{0,1},{1,0},{2,3},{3,2},{4,5},{5,4},{6,7},{7,6},{8,9},{9,8},{10,11... | collective-permute-start | bytes 786440 | tf_op jit(solution)/shard_map/ppermute | solution.py:140
  50.8 1.5 %collective-permute-start.6 = (bf16[8,128,128]{2,1,0:T(8,128)(2,1)}, bf16[8,128,128]{2,1,0:T(8,128)(2,1)}, u32[]{:S(2)}, u32[]{:S(2)}) collective-permute-start(bf16[8,128,128]{2,1,0:T(8,128)(2,1)} %slice.28), channel_id=1, source_target_pairs={{0,8},{1,9},{2,10},{3,11},{4,12},{5,13},{6,14},{7,15},{8,0},{9,1},... | collective-permute-start | bytes 786440 | tf_op jit(solution)/shard_map/ppermute | solution.py:140
  52.5 0.5 collective-permute-start.13
  53.1 7.4 %collective-permute-done.7.refs_8_ = bf16[8,128,128]{2,1,0:T(8,128)(2,1)S(1)} collective-permute-done((bf16[8,128,128]{2,1,0:T(8,128)(2,1)}, bf16[8,128,128]{2,1,0:T(8,128)(2,1)S(1)}, u32[]{:S(2)}, u32[]{:S(2)}) %collective-permute-start.7) | collective-permute-done | bytes 262176 | tf_op jit(solution)/shard_map/ppermute | solution.py:140
  60.5 0.5 collective-permute-start.15
  61.0 0.8 slice_convert_fusion
  61.8 0.9 slice.27.zt_ref
  62.8 19.2 %shard_map.50 = bf16[16,2,16,256]{3,2,1,0:T(8,128)(2,1)S(1)} custom-call(s32[16,16]{1,0:T(8,128)S(1)} %fusion.3.ids_ref, s32[18]{0:T(128)S(1)} %stack.69.where_ref, bf16[16,16,256]{2,1,0:T(8,128)(2,1)S(1)} %slice.27.zt_ref, bf16[16,128,128]{2,1,0:T(8,128)(2,1)S(1)} %bitcast.30, bf16[16,128,128]{2,1,0:T(8,128)(2,1)S(1)} %collective-permute-done.refs_1_, ...), custom_call_target="tpu_custom_call" | custom-call | tf_op jit(solution)/shard_map/pallas_call | solution.py:188
  82.0 14.4 %all_to_all.10 = bf16[16,2,16,256]{3,2,1,0:T(8,128)(2,1)S(1)} all-to-all(bf16[16,2,16,256]{3,2,1,0:T(8,128)(2,1)S(1)} %shard_map.50), channel_id=1, replica_groups=mesh['dom'=2,'col'=4,'row'=4] {'col','row'}, dimensions={0} | all-to-all | bytes 524288 | tf_op jit(solution)/shard_map/all_to_all | solution.py:206
  96.5 0.8 copy.7
  97.4 0.8 copy.6
  (34 shorter events, 0.7 us)
Async XLA Ops:
  0.6 40.7 %copy-start.1 = (s32[1,1,16]{2,1,0:T(1,128)S(1)}, s32[1,1,16]{2,1,0:T(1,128)}, u32[]{:S(2)}) copy-start(s32[1,1,16]{2,1,0:T(1,128)} %param.5) | copy-start | bytes 196
  0.6 18.2 %collective-permute-start.2 = (bf16[16,128,128]{2,1,0:T(8,128)(2,1)}, bf16[16,128,128]{2,1,0:T(8,128)(2,1)S(1)}, u32[]{:S(2)}, u32[]{:S(2)}) collective-permute-start(bf16[16,128,128]{2,1,0:T(8,128)(2,1)} %bitcast.26), channel_id=1, source_target_pairs={{0,3},{1,2},{2,1},{3,0},{4,7},{5,6},{6,5},{7,4},{8,11},{9,10},{10,... | collective-permute-start | bytes 1572872 | tf_op jit(solution)/shard_map/ppermute | solution.py:140
  5.8 24.6 %collective-permute-start.1 = (bf16[16,128,128]{2,1,0:T(8,128)(2,1)}, bf16[16,128,128]{2,1,0:T(8,128)(2,1)S(1)}, u32[]{:S(2)}, u32[]{:S(2)}) collective-permute-start(bf16[16,128,128]{2,1,0:T(8,128)(2,1)} %bitcast.27), channel_id=1, source_target_pairs={{0,8},{1,9},{2,10},{3,11},{4,12},{5,13},{6,14},{7,15},{8,0},{9,1},... | collective-permute-start | bytes 1572872 | tf_op jit(solution)/shard_map/ppermute | solution.py:140
  7.3 23.6 %collective-permute-start = (bf16[16,128,128]{2,1,0:T(8,128)(2,1)}, bf16[16,128,128]{2,1,0:T(8,128)(2,1)S(1)}, u32[]{:S(2)}, u32[]{:S(2)}) collective-permute-start(bf16[16,128,128]{2,1,0:T(8,128)(2,1)} %bitcast.28), channel_id=1, source_target_pairs={{0,1},{1,0},{2,3},{3,2},{4,5},{5,4},{6,7},{7,6},{8,9},{9,8},{10,11... | collective-permute-start | bytes 1572872 | tf_op jit(solution)/shard_map/ppermute | solution.py:140
  18.8 12.3 %collective-permute-start.5 = (bf16[16,128,128]{2,1,0:T(8,128)(2,1)S(1)}, bf16[16,128,128]{2,1,0:T(8,128)(2,1)S(1)}, u32[]{:S(2)}, u32[]{:S(2)}) collective-permute-start(bf16[16,128,128]{2,1,0:T(8,128)(2,1)S(1)} %collective-permute-done.2.refs_3_), channel_id=1, source_target_pairs={{0,8},{1,9},{2,10},{3,11},{4,12},{5,13},{6,14},{7,15},{8,0},{9,1},... | collective-permute-start | bytes 1572872 | tf_op jit(solution)/shard_map/ppermute | solution.py:140
  20.5 20.8 %collective-permute-start.4 = (bf16[16,128,128]{2,1,0:T(8,128)(2,1)S(1)}, bf16[16,128,128]{2,1,0:T(8,128)(2,1)S(1)}, u32[]{:S(2)}, u32[]{:S(2)}) collective-permute-start(bf16[16,128,128]{2,1,0:T(8,128)(2,1)S(1)} %collective-permute-done.2.refs_3_), channel_id=1, source_target_pairs={{0,1},{1,0},{2,3},{3,2},{4,5},{5,4},{6,7},{7,6},{8,9},{9,8},{10,11... | collective-permute-start | bytes 1572872 | tf_op jit(solution)/shard_map/ppermute | solution.py:140
  30.4 18.6 %collective-permute-start.8 = (bf16[16,128,128]{2,1,0:T(8,128)(2,1)}, bf16[16,128,128]{2,1,0:T(8,128)(2,1)}, u32[]{:S(2)}, u32[]{:S(2)}) collective-permute-start(bf16[16,128,128]{2,1,0:T(8,128)(2,1)} %bitcast.29), channel_id=1, source_target_pairs={{0,4},{1,5},{2,6},{3,7},{4,0},{5,1},{6,2},{7,3},{8,12},{9,13},{10,... | collective-permute-start | bytes 1572872 | tf_op jit(solution)/shard_map/ppermute | solution.py:140
  30.4 20.5 %collective-permute-start.11 = (bf16[16,128,128]{2,1,0:T(8,128)(2,1)S(1)}, bf16[16,128,128]{2,1,0:T(8,128)(2,1)}, u32[]{:S(2)}, u32[]{:S(2)}) collective-permute-start(bf16[16,128,128]{2,1,0:T(8,128)(2,1)S(1)} %collective-permute-done.2.refs_3_), channel_id=1, source_target_pairs={{0,4},{1,5},{2,6},{3,7},{4,0},{5,1},{6,2},{7,3},{8,12},{9,13},{10,... | collective-permute-start | bytes 1572872 | tf_op jit(solution)/shard_map/ppermute | solution.py:140
  30.9 21.6 %collective-permute-start.9 = (bf16[16,128,128]{2,1,0:T(8,128)(2,1)S(1)}, bf16[16,128,128]{2,1,0:T(8,128)(2,1)}, u32[]{:S(2)}, u32[]{:S(2)}) collective-permute-start(bf16[16,128,128]{2,1,0:T(8,128)(2,1)S(1)} %collective-permute-done.refs_1_), channel_id=1, source_target_pairs={{0,4},{1,5},{2,6},{3,7},{4,0},{5,1},{6,2},{7,3},{8,12},{9,13},{10,... | collective-permute-start | bytes 1572872 | tf_op jit(solution)/shard_map/ppermute | solution.py:140
  31.1 21.9 %collective-permute-start.3 = (bf16[16,128,128]{2,1,0:T(8,128)(2,1)S(1)}, bf16[16,128,128]{2,1,0:T(8,128)(2,1)}, u32[]{:S(2)}, u32[]{:S(2)}) collective-permute-start(bf16[16,128,128]{2,1,0:T(8,128)(2,1)S(1)} %collective-permute-done.refs_1_), channel_id=1, source_target_pairs={{0,8},{1,9},{2,10},{3,11},{4,12},{5,13},{6,14},{7,15},{8,0},{9,1},... | collective-permute-start | bytes 1572872 | tf_op jit(solution)/shard_map/ppermute | solution.py:140
  41.3 11.1 %collective-permute-start.10 = (bf16[16,128,128]{2,1,0:T(8,128)(2,1)S(1)}, bf16[16,128,128]{2,1,0:T(8,128)(2,1)}, u32[]{:S(2)}, u32[]{:S(2)}) collective-permute-start(bf16[16,128,128]{2,1,0:T(8,128)(2,1)S(1)} %collective-permute-done.1.refs_2_), channel_id=1, source_target_pairs={{0,4},{1,5},{2,6},{3,7},{4,0},{5,1},{6,2},{7,3},{8,12},{9,13},{10,... | collective-permute-start | bytes 1572872 | tf_op jit(solution)/shard_map/ppermute | solution.py:140
  43.1 17.9 %all-to-all-start = ((bf16[16,32,256]{2,1,0:T(8,128)(2,1)}), bf16[16,32,256]{2,1,0:T(8,128)(2,1)}, u32[]{:S(2)}, u32[]{:S(2)}) async-start(bf16[16,32,256]{2,1,0:T(8,128)(2,1)} %pad_maximum_fusion), calls=%async_computation | async-start | bytes 524288 | tf_op jit(solution)/shard_map/all_to_all | solution.py:180
  48.2 14.6 %copy-start = (bf16[1,1,16,128,128]{4,3,2,1,0:T(8,128)(2,1)S(1)}, bf16[1,1,16,128,128]{4,3,2,1,0:T(8,128)(2,1)}, u32[]{:S(2)}) copy-start(bf16[1,1,16,128,128]{4,3,2,1,0:T(8,128)(2,1)} %param.4) | copy-start | bytes 1572868
  49.0 11.6 %collective-permute-start.7 = (bf16[8,128,128]{2,1,0:T(8,128)(2,1)}, bf16[8,128,128]{2,1,0:T(8,128)(2,1)S(1)}, u32[]{:S(2)}, u32[]{:S(2)}) collective-permute-start(bf16[8,128,128]{2,1,0:T(8,128)(2,1)} %slice.29), channel_id=1, source_target_pairs={{0,1},{1,0},{2,3},{3,2},{4,5},{5,4},{6,7},{7,6},{8,9},{9,8},{10,11... | collective-permute-start | bytes 786440 | tf_op jit(solution)/shard_map/ppermute | solution.py:140
  50.8 9.7 %collective-permute-start.6 = (bf16[8,128,128]{2,1,0:T(8,128)(2,1)}, bf16[8,128,128]{2,1,0:T(8,128)(2,1)}, u32[]{:S(2)}, u32[]{:S(2)}) collective-permute-start(bf16[8,128,128]{2,1,0:T(8,128)(2,1)} %slice.28), channel_id=1, source_target_pairs={{0,8},{1,9},{2,10},{3,11},{4,12},{5,13},{6,14},{7,15},{8,0},{9,1},... | collective-permute-start | bytes 786440 | tf_op jit(solution)/shard_map/ppermute | solution.py:140
  52.4 10.4 %collective-permute-start.14 = (bf16[16,128,128]{2,1,0:T(8,128)(2,1)S(1)}, bf16[16,128,128]{2,1,0:T(8,128)(2,1)}, u32[]{:S(2)}, u32[]{:S(2)}) collective-permute-start(bf16[16,128,128]{2,1,0:T(8,128)(2,1)S(1)} %collective-permute-done.5.refs_6_), channel_id=1, source_target_pairs={{0,4},{1,5},{2,6},{3,7},{4,0},{5,1},{6,2},{7,3},{8,12},{9,13},{10,... | collective-permute-start | bytes 1572872 | tf_op jit(solution)/shard_map/ppermute | solution.py:140
  52.5 10.3 %collective-permute-start.13 = (bf16[16,128,128]{2,1,0:T(8,128)(2,1)S(1)}, bf16[16,128,128]{2,1,0:T(8,128)(2,1)}, u32[]{:S(2)}, u32[]{:S(2)}) collective-permute-start(bf16[16,128,128]{2,1,0:T(8,128)(2,1)S(1)} %collective-permute-done.4.refs_5_), channel_id=1, source_target_pairs={{0,4},{1,5},{2,6},{3,7},{4,0},{5,1},{6,2},{7,3},{8,12},{9,13},{10,... | collective-permute-start | bytes 1572872 | tf_op jit(solution)/shard_map/ppermute | solution.py:140
  53.0 9.8 %collective-permute-start.12 = (bf16[16,128,128]{2,1,0:T(8,128)(2,1)}, bf16[16,128,128]{2,1,0:T(8,128)(2,1)}, u32[]{:S(2)}, u32[]{:S(2)}) collective-permute-start(bf16[16,128,128]{2,1,0:T(8,128)(2,1)} %collective-permute-done.3.refs_4_), channel_id=1, source_target_pairs={{0,4},{1,5},{2,6},{3,7},{4,0},{5,1},{6,2},{7,3},{8,12},{9,13},{10,... | collective-permute-start | bytes 1572872 | tf_op jit(solution)/shard_map/ppermute | solution.py:140
  60.5 2.3 %collective-permute-start.16 = (bf16[8,128,128]{2,1,0:T(8,128)(2,1)S(1)}, bf16[8,128,128]{2,1,0:T(8,128)(2,1)}, u32[]{:S(2)}, u32[]{:S(2)}) collective-permute-start(bf16[8,128,128]{2,1,0:T(8,128)(2,1)S(1)} %collective-permute-done.7.refs_8_), channel_id=1, source_target_pairs={{0,4},{1,5},{2,6},{3,7},{4,0},{5,1},{6,2},{7,3},{8,12},{9,13},{10,... | collective-permute-start | bytes 786440 | tf_op jit(solution)/shard_map/ppermute | solution.py:140
  60.5 2.3 %collective-permute-start.15 = (bf16[8,128,128]{2,1,0:T(8,128)(2,1)}, bf16[8,128,128]{2,1,0:T(8,128)(2,1)}, u32[]{:S(2)}, u32[]{:S(2)}) collective-permute-start(bf16[8,128,128]{2,1,0:T(8,128)(2,1)} %collective-permute-done.6.refs_7_), channel_id=1, source_target_pairs={{0,4},{1,5},{2,6},{3,7},{4,0},{5,1},{6,2},{7,3},{8,12},{9,13},{10,... | collective-permute-start | bytes 786440 | tf_op jit(solution)/shard_map/ppermute | solution.py:140

commit v5 on v4

--- a/solution.py
+++ b/solution.py
@@ -127,7 +127,22 @@
             out_ref[p, 1, :, b * orb : (b + 1) * orb] = prev[g].astype(out_ref.dtype)
 
 
-def gather_tiles(own, n_col, n_row):
+def nothing(*refs):
+    pass
+
+
+def after(value, *others):
+    return pl.pallas_call(
+        nothing,
+        out_shape=jax.ShapeDtypeStruct(value.shape, value.dtype),
+        in_specs=[pl.BlockSpec(memory_space=pl.ANY)] * (1 + len(others)),
+        out_specs=pl.BlockSpec(memory_space=pl.ANY),
+        input_output_aliases={0: 0},
+        compiler_params=pltpu.CompilerParams(vmem_limit_bytes=2**20),
+    )(value, *others)
+
+
+def gather_tiles(own, n_col, n_row, meanwhile):
     col, row = lax.axis_index("col"), lax.axis_index("row")
     half = own.shape[0] // 2
 
@@ -139,14 +154,24 @@
         ]
         return lax.ppermute(buf, LANES, pairs)
 
+    def to_mate(*bufs):
+        return [send(buf, 1, 0) for buf in bufs]
+
+    over_own = send(own, 2, 0)
     near = send(own, 0, 1)
-    over_own = send(own, 2, 0)
     far = send(own, 0, 3)
+    near = after(near, over_own)
     over_near = send(near, 2, 0)
+    mates = to_mate(own, near, over_own)
+    far = after(far, over_near, *mates)
+    over_far = send(far, 2, 0)
     last = send(far, 0, 1)
-    over_far = send(far, 2, 0)
+    mates += to_mate(far, over_near)
+    other = meanwhile(over_near)
+    last = after(last, over_far, other, *mates[3:])
     over_last = send(last[:half], 2, 0)
     side_last = send(over_far[half:], 0, 1)
+    mates += to_mate(last, over_far, over_last, side_last)
     held = [
         (own, 0, 0, 0),
         (near, 0, 1, 0),
@@ -158,9 +183,9 @@
         (over_last, 2, 2, 0),
         (side_last, 2, 2, half),
     ]
-    held += [(send(buf, 1, 0), c ^ 1, r, slot) for buf, c, r, slot in held]
+    held += [(buf, c ^ 1, r, slot) for buf, (_, c, r, slot) in zip(mates, held)]
     where = jnp.stack([(col ^ c) * n_row + (row ^ r) for _, c, r, _ in held]).astype(jnp.int32)
-    return [buf for buf, _, _, _ in held], [slot for _, _, _, slot in held], where
+    return [buf for buf, _, _, _ in held], [slot for _, _, _, slot in held], where, other
 
 
 def gather_plan(vectors, blocks, cols):
@@ -172,14 +197,14 @@
     per_piece = rows // orb
     n_blocks = n_dev * per_piece
 
-    bufs, starts, where = gather_tiles(blocks[0, 0], n_col, n_row)
-
-    turned = vectors.T.reshape(n_dev, share, rows)
-    own_ids = jnp.pad(cols[0, 0].astype(jnp.bfloat16), (0, rows - slots))
-    own_ids = jnp.broadcast_to(own_ids, (n_dev, share, rows))
-    both = lax.all_to_all(
-        jnp.concatenate([turned, own_ids], axis=1), LANES, split_axis=0, concat_axis=0, tiled=True
-    )
+    def exchange(ready):
+        turned = after(vectors, ready).T.reshape(n_dev, share, rows)
+        own_ids = jnp.pad(cols[0, 0].astype(jnp.bfloat16), (0, rows - slots))
+        own_ids = jnp.broadcast_to(own_ids, (n_dev, share, rows))
+        both = jnp.concatenate([turned, own_ids], axis=1)
+        return lax.all_to_all(both, LANES, split_axis=0, concat_axis=0, tiled=True)
+
+    bufs, starts, where, both = gather_tiles(blocks[0, 0], n_col, n_row, exchange)
     zt = both[:, :share]
     local = both[:, share, :slots].astype(jnp.int32)
     down = (jnp.arange(n_dev, dtype=jnp.int32) % n_row)[:, None]

time: 98.6 us -> 114 us (1.16)
  waiting for transfers between devices: 28 us -> 41.7 us
  local copies, waits for them, and re-layouts: 5.2 us -> 7.41 us
    all_to_all x1, starting transfers between devices: 4.4 us -> 14.8 us  [exchange(): return lax.all_to_all(both, LANES, split_axis=0, concat_axis=0, tiled=True)]
    ppermute x17, starting transfers between devices: 24.6 us -> 14.7 us  [send(): return lax.ppermute(buf, LANES, pairs)]
    all_to_all x1, waiting for transfers between devices: 0.01 us -> 9.77 us  [exchange(): return lax.all_to_all(both, LANES, split_axis=0, concat_axis=0, tiled=True)]
    unnamed x6 -> x15, local copies, waits for them, and re-layouts: 1.68 us -> 5.71 us
    ppermute x17, waiting for transfers between devices: 28 us -> 32 us  [send(): return lax.ppermute(buf, LANES, pairs)]
  transfers between devices with their start and end apart: 18 -> 18, of which waited for: 4 -> 7; matrix products, arithmetic and copies ran while one was open for 5% -> 2% of each run, Pallas kernels for 0% -> 0%
where the time goes in v5:
time: 114 us; the launch traced here: 113 us
  waiting for transfers between devices  41.7 us (37%)
  starting transfers between devices  29.5 us (26%)
  Pallas kernels  18.3 us (16%)
  blocking collectives  14.7 us (13%)
  local copies, waits for them, and re-layouts  7.41 us (6%)
    ppermute x17, waiting for transfers between devices, send(): return lax.ppermute(buf, LANES, pairs)  32 us
    pallas_call x1, Pallas kernels, gather_plan(): pl.pallas_call(functools.partial(filter_kernel, per_piece, n_row, starts)...  18.3 us
    all_to_all x1, starting transfers between devices, exchange(): return lax.all_to_all(both, LANES, split_axis=0, concat_axis=0, tiled=True)  14.8 us
    ppermute x17, starting transfers between devices, send(): return lax.ppermute(buf, LANES, pairs)  14.7 us
    all_to_all x1, blocking collectives, gather_plan(): back = lax.all_to_all(done, LANES, split_axis=0, concat_axis=0, tiled=True)  14.7 us
    all_to_all x1, waiting for transfers between devices, exchange(): return lax.all_to_all(both, LANES, split_axis=0, concat_axis=0, tiled=True)  9.77 us
    unnamed x15, local copies, waits for them, and re-layouts  5.71 us
  transfers between devices with their start and end apart: 18, of which 7 were waited for; matrix products, arithmetic and copies ran while one was open for 2% of the time, Pallas kernels for 0%

profile of v5, /device:TPU:0, one launch (start us, length us, event | category | flops | bytes accessed | tf_op | source)
XLA Modules:
  0.0 113.3 jit_solution(2336710044432546713)
XLA Ops:
  0.6 0.9 copy.17.refs_0_
  1.5 3.0 %collective-permute-start.1 = (bf16[16,128,128]{2,1,0:T(8,128)(2,1)}, bf16[16,128,128]{2,1,0:T(8,128)(2,1)S(1)}, u32[]{:S(2)}, u32[]{:S(2)}) collective-permute-start(bf16[16,128,128]{2,1,0:T(8,128)(2,1)} %bitcast.27), channel_id=1, source_target_pairs={{0,8},{1,9},{2,10},{3,11},{4,12},{5,13},{6,14},{7,15},{8,0},{9,1},... | collective-permute-start | bytes 1572872 | tf_op jit(solution)/shard_map/ppermute | solution.py:155
  4.5 1.6 %collective-permute-start = (bf16[16,128,128]{2,1,0:T(8,128)(2,1)}, bf16[16,128,128]{2,1,0:T(8,128)(2,1)S(1)}, u32[]{:S(2)}, u32[]{:S(2)}) collective-permute-start(bf16[16,128,128]{2,1,0:T(8,128)(2,1)} %bitcast.28), channel_id=1, source_target_pairs={{0,1},{1,0},{2,3},{3,2},{4,5},{5,4},{6,7},{7,6},{8,9},{9,8},{10,11... | collective-permute-start | bytes 1572872 | tf_op jit(solution)/shard_map/ppermute | solution.py:155
  6.1 2.5 %collective-permute-start.3 = (bf16[16,128,128]{2,1,0:T(8,128)(2,1)}, bf16[16,128,128]{2,1,0:T(8,128)(2,1)}, u32[]{:S(2)}, u32[]{:S(2)}) collective-permute-start(bf16[16,128,128]{2,1,0:T(8,128)(2,1)} %bitcast.30), channel_id=1, source_target_pairs={{0,3},{1,2},{2,1},{3,0},{4,7},{5,6},{6,5},{7,4},{8,11},{9,10},{10,... | collective-permute-start | bytes 1572872 | tf_op jit(solution)/shard_map/ppermute | solution.py:155
  8.6 8.1 %collective-permute-done.1.refs_1_.refs_2_ = bf16[16,128,128]{2,1,0:T(8,128)(2,1)S(1)} collective-permute-done((bf16[16,128,128]{2,1,0:T(8,128)(2,1)}, bf16[16,128,128]{2,1,0:T(8,128)(2,1)S(1)}, u32[]{:S(2)}, u32[]{:S(2)}) %collective-permute-start.1) | collective-permute-done | bytes 524320 | tf_op jit(solution)/shard_map/ppermute | solution.py:155
  16.6 2.1 %collective-permute-done.refs_0_ = bf16[16,128,128]{2,1,0:T(8,128)(2,1)S(1)} collective-permute-done((bf16[16,128,128]{2,1,0:T(8,128)(2,1)}, bf16[16,128,128]{2,1,0:T(8,128)(2,1)S(1)}, u32[]{:S(2)}, u32[]{:S(2)}) %collective-permute-start) | collective-permute-done | bytes 524320 | tf_op jit(solution)/shard_map/ppermute | solution.py:155
  19.3 12.3 %collective-permute-done.3.refs_0_ = bf16[16,128,128]{2,1,0:T(8,128)(2,1)} collective-permute-done((bf16[16,128,128]{2,1,0:T(8,128)(2,1)}, bf16[16,128,128]{2,1,0:T(8,128)(2,1)}, u32[]{:S(2)}, u32[]{:S(2)}) %collective-permute-start.3) | collective-permute-done | bytes 524320 | tf_op jit(solution)/shard_map/ppermute | solution.py:155
  31.6 1.5 %collective-permute-done.2.refs_1_.refs_4_ = bf16[16,128,128]{2,1,0:T(8,128)(2,1)S(1)} collective-permute-done((bf16[16,128,128]{2,1,0:T(8,128)(2,1)S(1)}, bf16[16,128,128]{2,1,0:T(8,128)(2,1)S(1)}, u32[]{:S(2)}, u32[]{:S(2)}) %collective-permute-start.2) | collective-permute-done | bytes 524320 | tf_op jit(solution)/shard_map/ppermute | solution.py:155
  33.7 2.4 %collective-permute-start.7 = (bf16[16,128,128]{2,1,0:T(8,128)(2,1)}, bf16[16,128,128]{2,1,0:T(8,128)(2,1)S(1)}, u32[]{:S(2)}, u32[]{:S(2)}) collective-permute-start(bf16[16,128,128]{2,1,0:T(8,128)(2,1)} %shard_map.52.refs_3_), channel_id=1, source_target_pairs={{0,1},{1,0},{2,3},{3,2},{4,5},{5,4},{6,7},{7,6},{8,9},{9,8},{10,11... | collective-permute-start | bytes 1572872 | tf_op jit(solution)/shard_map/ppermute | solution.py:155
  36.3 0.7 pad_maximum_fusion
  37.0 14.8 %all-to-all-start = ((bf16[16,32,256]{2,1,0:T(8,128)(2,1)}), bf16[16,32,256]{2,1,0:T(8,128)(2,1)S(1)}, u32[]{:S(2)}, u32[]{:S(2)}) async-start(bf16[16,32,256]{2,1,0:T(8,128)(2,1)} %pad_maximum_fusion), calls=%async_computation | async-start | bytes 524288 | tf_op jit(solution)/shard_map/all_to_all | solution.py:205
  52.5 1.9 %collective-permute-start.12 = (bf16[8,128,128]{2,1,0:T(8,128)(2,1)}, bf16[8,128,128]{2,1,0:T(8,128)(2,1)}, u32[]{:S(2)}, u32[]{:S(2)}) collective-permute-start(bf16[8,128,128]{2,1,0:T(8,128)(2,1)} %slice.29), channel_id=1, source_target_pairs={{0,1},{1,0},{2,3},{3,2},{4,5},{5,4},{6,7},{7,6},{8,9},{9,8},{10,11... | collective-permute-start | bytes 786440 | tf_op jit(solution)/shard_map/ppermute | solution.py:155
  54.5 9.8 %all-to-all-done.refs_2_ = bf16[16,32,256]{2,1,0:T(8,128)(2,1)S(1)} async-done(((bf16[16,32,256]{2,1,0:T(8,128)(2,1)}), bf16[16,32,256]{2,1,0:T(8,128)(2,1)S(1)}, u32[]{:S(2)}, u32[]{:S(2)}) %all-to-all-start) | async-done | bytes 262176 | tf_op jit(solution)/shard_map/all_to_all | solution.py:205
  64.3 0.7 slice.28
  65.0 1.6 %collective-permute-start.11 = (bf16[8,128,128]{2,1,0:T(8,128)(2,1)}, bf16[8,128,128]{2,1,0:T(8,128)(2,1)}, u32[]{:S(2)}, u32[]{:S(2)}) collective-permute-start(bf16[8,128,128]{2,1,0:T(8,128)(2,1)} %slice.28), channel_id=1, source_target_pairs={{0,8},{1,9},{2,10},{3,11},{4,12},{5,13},{6,14},{7,15},{8,0},{9,1},... | collective-permute-start | bytes 786440 | tf_op jit(solution)/shard_map/ppermute | solution.py:155
  67.4 6.3 %collective-permute-done.11.refs_7_ = bf16[8,128,128]{2,1,0:T(8,128)(2,1)} collective-permute-done((bf16[8,128,128]{2,1,0:T(8,128)(2,1)}, bf16[8,128,128]{2,1,0:T(8,128)(2,1)}, u32[]{:S(2)}, u32[]{:S(2)}) %collective-permute-start.11) | collective-permute-done | bytes 262176 | tf_op jit(solution)/shard_map/ppermute | solution.py:155
  73.8 1.6 %collective-permute-done.15.refs_16_ = bf16[8,128,128]{2,1,0:T(8,128)(2,1)S(1)} collective-permute-done((bf16[8,128,128]{2,1,0:T(8,128)(2,1)}, bf16[8,128,128]{2,1,0:T(8,128)(2,1)S(1)}, u32[]{:S(2)}, u32[]{:S(2)}) %collective-permute-start.15) | collective-permute-done | bytes 262176 | tf_op jit(solution)/shard_map/ppermute | solution.py:155
  75.4 1.0 copy-done.1
  76.5 1.0 copy-done.3
  77.5 1.0 copy-done.4
  78.6 18.3 %shard_map.54 = bf16[16,2,16,256]{3,2,1,0:T(8,128)(2,1)S(1)} custom-call(s32[16,16]{1,0:T(8,128)S(1)} %fusion.3.ids_ref, s32[18]{0:T(128)S(1)} %stack.69.where_ref, bf16[16,16,256]{2,1,0:T(8,128)(2,1)S(1)} %slice.27.zt_ref, bf16[16,128,128]{2,1,0:T(8,128)(2,1)S(1)} %bitcast.31, bf16[16,128,128]{2,1,0:T(8,128)(2,1)S(1)} %shard_map.50.refs_1_, ...), custom_call_target="tpu_custom_call" | custom-call | tf_op jit(solution)/shard_map/pallas_call | solution.py:213
  96.9 14.7 %all_to_all.10 = bf16[16,2,16,256]{3,2,1,0:T(8,128)(2,1)S(1)} all-to-all(bf16[16,2,16,256]{3,2,1,0:T(8,128)(2,1)S(1)} %shard_map.54), channel_id=1, replica_groups=mesh['dom'=2,'col'=4,'row'=4] {'col','row'}, dimensions={0} | all-to-all | bytes 524288 | tf_op jit(solution)/shard_map/all_to_all | solution.py:231
  111.6 0.8 copy.11
  112.5 0.8 copy.10
  (47 shorter events, 3.0 us)
Async XLA Ops:
  1.5 17.7 %copy-start.5 = (s32[1,1,16]{2,1,0:T(1,128)S(1)}, s32[1,1,16]{2,1,0:T(1,128)}, u32[]{:S(2)}) copy-start(s32[1,1,16]{2,1,0:T(1,128)} %param.5) | copy-start | bytes 196
  1.5 15.1 %collective-permute-start.1 = (bf16[16,128,128]{2,1,0:T(8,128)(2,1)}, bf16[16,128,128]{2,1,0:T(8,128)(2,1)S(1)}, u32[]{:S(2)}, u32[]{:S(2)}) collective-permute-start(bf16[16,128,128]{2,1,0:T(8,128)(2,1)} %bitcast.27), channel_id=1, source_target_pairs={{0,8},{1,9},{2,10},{3,11},{4,12},{5,13},{6,14},{7,15},{8,0},{9,1},... | collective-permute-start | bytes 1572872 | tf_op jit(solution)/shard_map/ppermute | solution.py:155
  4.5 14.3 %collective-permute-start = (bf16[16,128,128]{2,1,0:T(8,128)(2,1)}, bf16[16,128,128]{2,1,0:T(8,128)(2,1)S(1)}, u32[]{:S(2)}, u32[]{:S(2)}) collective-permute-start(bf16[16,128,128]{2,1,0:T(8,128)(2,1)} %bitcast.28), channel_id=1, source_target_pairs={{0,1},{1,0},{2,3},{3,2},{4,5},{5,4},{6,7},{7,6},{8,9},{9,8},{10,11... | collective-permute-start | bytes 1572872 | tf_op jit(solution)/shard_map/ppermute | solution.py:155
  6.1 13.2 %collective-permute-start.4 = (bf16[16,128,128]{2,1,0:T(8,128)(2,1)}, bf16[16,128,128]{2,1,0:T(8,128)(2,1)S(1)}, u32[]{:S(2)}, u32[]{:S(2)}) collective-permute-start(bf16[16,128,128]{2,1,0:T(8,128)(2,1)} %bitcast.29), channel_id=1, source_target_pairs={{0,4},{1,5},{2,6},{3,7},{4,0},{5,1},{6,2},{7,3},{8,12},{9,13},{10,... | collective-permute-start | bytes 1572872 | tf_op jit(solution)/shard_map/ppermute | solution.py:155
  6.1 25.5 %collective-permute-start.3 = (bf16[16,128,128]{2,1,0:T(8,128)(2,1)}, bf16[16,128,128]{2,1,0:T(8,128)(2,1)}, u32[]{:S(2)}, u32[]{:S(2)}) collective-permute-start(bf16[16,128,128]{2,1,0:T(8,128)(2,1)} %bitcast.30), channel_id=1, source_target_pairs={{0,3},{1,2},{2,1},{3,0},{4,7},{5,6},{6,5},{7,4},{8,11},{9,10},{10,... | collective-permute-start | bytes 1572872 | tf_op jit(solution)/shard_map/ppermute | solution.py:155
  16.6 14.9 %collective-permute-start.6 = (bf16[16,128,128]{2,1,0:T(8,128)(2,1)S(1)}, bf16[16,128,128]{2,1,0:T(8,128)(2,1)S(1)}, u32[]{:S(2)}, u32[]{:S(2)}) collective-permute-start(bf16[16,128,128]{2,1,0:T(8,128)(2,1)S(1)} %collective-permute-done.1.refs_1_.refs_2_), channel_id=1, source_target_pairs={{0,4},{1,5},{2,6},{3,7},{4,0},{5,1},{6,2},{7,3},{8,12},{9,13},{10,... | collective-permute-start | bytes 1572872 | tf_op jit(solution)/shard_map/ppermute | solution.py:155
  18.8 12.8 %collective-permute-start.5 = (bf16[16,128,128]{2,1,0:T(8,128)(2,1)S(1)}, bf16[16,128,128]{2,1,0:T(8,128)(2,1)S(1)}, u32[]{:S(2)}, u32[]{:S(2)}) collective-permute-start(bf16[16,128,128]{2,1,0:T(8,128)(2,1)S(1)} %shard_map.50.refs_1_), channel_id=1, source_target_pairs={{0,4},{1,5},{2,6},{3,7},{4,0},{5,1},{6,2},{7,3},{8,12},{9,13},{10,... | collective-permute-start | bytes 1572872 | tf_op jit(solution)/shard_map/ppermute | solution.py:155
  18.8 14.3 %collective-permute-start.2 = (bf16[16,128,128]{2,1,0:T(8,128)(2,1)S(1)}, bf16[16,128,128]{2,1,0:T(8,128)(2,1)S(1)}, u32[]{:S(2)}, u32[]{:S(2)}) collective-permute-start(bf16[16,128,128]{2,1,0:T(8,128)(2,1)S(1)} %shard_map.50.refs_1_), channel_id=1, source_target_pairs={{0,8},{1,9},{2,10},{3,11},{4,12},{5,13},{6,14},{7,15},{8,0},{9,1},... | collective-permute-start | bytes 1572872 | tf_op jit(solution)/shard_map/ppermute | solution.py:155
  31.6 1.5 %copy-start = (bf16[16,128,128]{2,1,0:T(8,128)(2,1)}, bf16[16,128,128]{2,1,0:T(8,128)(2,1)S(1)}, u32[]{:S(2)}) copy-start(bf16[16,128,128]{2,1,0:T(8,128)(2,1)S(1)} %collective-permute-done.6.refs_4_.refs_11_) | copy-start | bytes 1572868
  31.6 1.5 %copy-start.2 = (bf16[16,128,128]{2,1,0:T(8,128)(2,1)}, bf16[16,128,128]{2,1,0:T(8,128)(2,1)S(1)}, u32[]{:S(2)}) copy-start(bf16[16,128,128]{2,1,0:T(8,128)(2,1)S(1)} %collective-permute-done.5.refs_3_.refs_10_) | copy-start | bytes 1572868
  33.1 31.1 %collective-permute-start.9 = (bf16[16,128,128]{2,1,0:T(8,128)(2,1)}, bf16[16,128,128]{2,1,0:T(8,128)(2,1)}, u32[]{:S(2)}, u32[]{:S(2)}) collective-permute-start(bf16[16,128,128]{2,1,0:T(8,128)(2,1)} %shard_map.52.refs_3_), channel_id=1, source_target_pairs={{0,4},{1,5},{2,6},{3,7},{4,0},{5,1},{6,2},{7,3},{8,12},{9,13},{10,... | collective-permute-start | bytes 1572872 | tf_op jit(solution)/shard_map/ppermute | solution.py:155
  33.1 18.7 %collective-permute-start.8 = (bf16[16,128,128]{2,1,0:T(8,128)(2,1)}, bf16[16,128,128]{2,1,0:T(8,128)(2,1)S(1)}, u32[]{:S(2)}, u32[]{:S(2)}) collective-permute-start(bf16[16,128,128]{2,1,0:T(8,128)(2,1)} %shard_map.52.refs_3_), channel_id=1, source_target_pairs={{0,8},{1,9},{2,10},{3,11},{4,12},{5,13},{6,14},{7,15},{8,0},{9,1},... | collective-permute-start | bytes 1572872 | tf_op jit(solution)/shard_map/ppermute | solution.py:155
  33.7 30.5 %collective-permute-start.7 = (bf16[16,128,128]{2,1,0:T(8,128)(2,1)}, bf16[16,128,128]{2,1,0:T(8,128)(2,1)S(1)}, u32[]{:S(2)}, u32[]{:S(2)}) collective-permute-start(bf16[16,128,128]{2,1,0:T(8,128)(2,1)} %shard_map.52.refs_3_), channel_id=1, source_target_pairs={{0,1},{1,0},{2,3},{3,2},{4,5},{5,4},{6,7},{7,6},{8,9},{9,8},{10,11... | collective-permute-start | bytes 1572872 | tf_op jit(solution)/shard_map/ppermute | solution.py:155
  36.2 28.1 %collective-permute-start.10 = (bf16[16,128,128]{2,1,0:T(8,128)(2,1)S(1)}, bf16[16,128,128]{2,1,0:T(8,128)(2,1)}, u32[]{:S(2)}, u32[]{:S(2)}) collective-permute-start(bf16[16,128,128]{2,1,0:T(8,128)(2,1)S(1)} %collective-permute-done.2.refs_1_.refs_4_), channel_id=1, source_target_pairs={{0,4},{1,5},{2,6},{3,7},{4,0},{5,1},{6,2},{7,3},{8,12},{9,13},{10,... | collective-permute-start | bytes 1572872 | tf_op jit(solution)/shard_map/ppermute | solution.py:155
  37.0 27.2 %all-to-all-start = ((bf16[16,32,256]{2,1,0:T(8,128)(2,1)}), bf16[16,32,256]{2,1,0:T(8,128)(2,1)S(1)}, u32[]{:S(2)}, u32[]{:S(2)}) async-start(bf16[16,32,256]{2,1,0:T(8,128)(2,1)} %pad_maximum_fusion), calls=%async_computation | async-start | bytes 524288 | tf_op jit(solution)/shard_map/all_to_all | solution.py:205
  52.5 14.7 %collective-permute-start.12 = (bf16[8,128,128]{2,1,0:T(8,128)(2,1)}, bf16[8,128,128]{2,1,0:T(8,128)(2,1)}, u32[]{:S(2)}, u32[]{:S(2)}) collective-permute-start(bf16[8,128,128]{2,1,0:T(8,128)(2,1)} %slice.29), channel_id=1, source_target_pairs={{0,1},{1,0},{2,3},{3,2},{4,5},{5,4},{6,7},{7,6},{8,9},{9,8},{10,11... | collective-permute-start | bytes 786440 | tf_op jit(solution)/shard_map/ppermute | solution.py:155
  65.0 8.7 %collective-permute-start.11 = (bf16[8,128,128]{2,1,0:T(8,128)(2,1)}, bf16[8,128,128]{2,1,0:T(8,128)(2,1)}, u32[]{:S(2)}, u32[]{:S(2)}) collective-permute-start(bf16[8,128,128]{2,1,0:T(8,128)(2,1)} %slice.28), channel_id=1, source_target_pairs={{0,8},{1,9},{2,10},{3,11},{4,12},{5,13},{6,14},{7,15},{8,0},{9,1},... | collective-permute-start | bytes 786440 | tf_op jit(solution)/shard_map/ppermute | solution.py:155
  66.7 8.7 %collective-permute-start.13 = (bf16[16,128,128]{2,1,0:T(8,128)(2,1)S(1)}, bf16[16,128,128]{2,1,0:T(8,128)(2,1)S(1)}, u32[]{:S(2)}, u32[]{:S(2)}) collective-permute-start(bf16[16,128,128]{2,1,0:T(8,128)(2,1)S(1)} %shard_map.53.refs_5_), channel_id=1, source_target_pairs={{0,4},{1,5},{2,6},{3,7},{4,0},{5,1},{6,2},{7,3},{8,12},{9,13},{10,... | collective-permute-start | bytes 1572872 | tf_op jit(solution)/shard_map/ppermute | solution.py:155
  66.8 8.7 %collective-permute-start.14 = (bf16[16,128,128]{2,1,0:T(8,128)(2,1)S(1)}, bf16[16,128,128]{2,1,0:T(8,128)(2,1)S(1)}, u32[]{:S(2)}, u32[]{:S(2)}) collective-permute-start(bf16[16,128,128]{2,1,0:T(8,128)(2,1)S(1)} %collective-permute-done.8.refs_1_.refs_6_), channel_id=1, source_target_pairs={{0,4},{1,5},{2,6},{3,7},{4,0},{5,1},{6,2},{7,3},{8,12},{9,13},{10,... | collective-permute-start | bytes 1572872 | tf_op jit(solution)/shard_map/ppermute | solution.py:155
  67.3 6.5 %collective-permute-start.16 = (bf16[8,128,128]{2,1,0:T(8,128)(2,1)}, bf16[8,128,128]{2,1,0:T(8,128)(2,1)S(1)}, u32[]{:S(2)}, u32[]{:S(2)}) collective-permute-start(bf16[8,128,128]{2,1,0:T(8,128)(2,1)} %collective-permute-done.12.refs_8_), channel_id=1, source_target_pairs={{0,4},{1,5},{2,6},{3,7},{4,0},{5,1},{6,2},{7,3},{8,12},{9,13},{10,... | collective-permute-start | bytes 786440 | tf_op jit(solution)/shard_map/ppermute | solution.py:155
  73.7 1.7 %collective-permute-start.15 = (bf16[8,128,128]{2,1,0:T(8,128)(2,1)}, bf16[8,128,128]{2,1,0:T(8,128)(2,1)S(1)}, u32[]{:S(2)}, u32[]{:S(2)}) collective-permute-start(bf16[8,128,128]{2,1,0:T(8,128)(2,1)} %collective-permute-done.11.refs_7_), channel_id=1, source_target_pairs={{0,4},{1,5},{2,6},{3,7},{4,0},{5,1},{6,2},{7,3},{8,12},{9,13},{10,... | collective-permute-start | bytes 786440 | tf_op jit(solution)/shard_map/ppermute | solution.py:155
  75.4 1.0 copy-start.1
  76.5 1.0 copy-start.3
  77.5 1.0 copy-start.4

commit v6 on v4

--- a/solution.py
+++ b/solution.py
@@ -70,14 +70,13 @@
     bufs, (out_ref, s_ref, z, now, prev, straight, *scattered, sems) = refs[: len(starts)], refs[len(starts) :]
     tiles, slots = s_ref.shape[:2]
     orb = s_ref.shape[2]
+    share = z.shape[1]
     tile_rows = slots // PER_ROW
     pieces = zt_ref.shape[0]
 
-    copies = []
-    for i, (buf, start) in enumerate(zip(bufs, starts)):
-        place = s_ref.at[where_ref[i], pl.ds(start, buf.shape[0])]
-        copies.append(pltpu.make_async_copy(buf, place, sems.at[i]))
-        copies[-1].start()
+    for buf, start, i in zip(bufs, starts, range(len(bufs))):
+        tile = where_ref[i]
+        pltpu.make_async_copy(buf, s_ref.at[tile, pl.ds(start, buf.shape[0])], sems.at[tile]).start()
 
     for p in range(pieces):
         for b in range(per_piece):
@@ -86,29 +85,47 @@
             now[p * per_piece + b] = own.astype(jnp.float32)
     prev[...] = jnp.zeros_like(prev)
 
-    for copy in copies:
-        copy.wait()
-
-    def row_group(across, carry):
+    def row_group(step, across, carry):
         group = [across * n_row + r for r in range(n_row)]
-        for t in range(tile_rows):
-            places = [(tile, t * PER_ROW + p) for tile in group for p in range(PER_ROW)]
-            strip = jnp.concatenate([s_ref[tile, slot] for tile, slot in places], axis=1)
-            where = [ids_ref[tile, slot] for tile, slot in places]
-            wide = jnp.concatenate([z[g] for g in where], axis=1)
-            tall = z[across * tile_rows + t]
-            straight[across * tile_rows + t] = lax.dot_general(
+
+        @pl.when(step == 0)
+        def _():
+            for tile in group:
+                pltpu.make_async_copy(s_ref.at[tile], s_ref.at[tile], sems.at[tile]).wait()
+
+        for t in range(0, tile_rows, 2):
+            strips, wides, where = [], [], []
+            for row in (t, t + 1):
+                places = [(tile, row * PER_ROW + p) for tile in group for p in range(PER_ROW)]
+                strips.append(jnp.concatenate([s_ref[tile, slot] for tile, slot in places], axis=1))
+                where.append([ids_ref[tile, slot] for tile, slot in places])
+                wides.append(jnp.concatenate([z[g] for g in where[-1]], axis=1))
+            strip = jnp.concatenate(strips, axis=0)
+            wide = jnp.concatenate(wides, axis=0)
+            base = across * tile_rows + t
+            none = jnp.zeros((share, orb), z.dtype)
+            tall = jnp.concatenate(
+                [
+                    jnp.concatenate([z[base], none], axis=1),
+                    jnp.concatenate([none, z[base + 1]], axis=1),
+                ],
+                axis=0,
+            )
+            direct = lax.dot_general(
                 wide, strip, (((1,), (1,)), ((), ())), preferred_element_type=jnp.float32
             )
             turned = jnp.dot(tall, strip, preferred_element_type=jnp.float32)
-            for i, g in enumerate(where):
-                scattered[i % len(scattered)][g] += turned[:, i * orb : (i + 1) * orb]
+            for k in range(2):
+                rows = slice(k * share, (k + 1) * share)
+                straight[base + k] = direct[rows, k * orb : (k + 1) * orb]
+                for i, g in enumerate(where[k]):
+                    scattered[i % len(scattered)][g] += turned[rows, i * orb : (i + 1) * orb]
         return carry
 
     def one_step(step, carry):
         for ref in scattered:
             ref[...] = jnp.zeros_like(ref)
-        lax.fori_loop(0, tiles // n_row, row_group, 0)
+        lax.fori_loop(0, tiles // n_row, functools.partial(row_group, step), 0)
         total = straight[...]
         for ref in scattered:
             total += ref[...]
@@ -199,7 +216,7 @@
             pltpu.VMEM((n_dev, slots, orb, orb), blocks.dtype),
             pltpu.VMEM((n_blocks, share, orb), jnp.bfloat16),
             *[pltpu.VMEM((n_blocks, share, orb), jnp.float32)] * (3 + SPLIT),
-            pltpu.SemaphoreType.DMA((len(bufs),)),
+            pltpu.SemaphoreType.DMA((n_dev,)),
         ],
         compiler_params=pltpu.CompilerParams(vmem_limit_bytes=32 * 2**20),
     )(ids, where, zt, *bufs)

time: 98.6 us -> 100 us (1.014)
  blocking collectives: 14.4 us -> 15.7 us
    all_to_all x1, blocking collectives: 14.4 us -> 15.7 us  [gather_plan(): back = lax.all_to_all(done, LANES, split_axis=0, concat_axis=0, tiled=True)]
where the time goes in v6:
time: 100 us; the launch traced here: 99.8 us
  starting transfers between devices  29 us (29%)
  waiting for transfers between devices  28 us (28%)
  Pallas kernels  19.4 us (19%)
  blocking collectives  15.7 us (16%)
  local copies, waits for them, and re-layouts  5.2 us (5%)
  other arithmetic  1.63 us (2%)
    ppermute x17, waiting for transfers between devices, send(): return lax.ppermute(buf, LANES, pairs)  28 us
    ppermute x17, starting transfers between devices, send(): return lax.ppermute(buf, LANES, pairs)  24.6 us
    pallas_call x1, Pallas kernels, gather_plan(): pl.pallas_call(functools.partial(filter_kernel, per_piece, n_row, starts)...  19.4 us
    all_to_all x1, blocking collectives, gather_plan(): back = lax.all_to_all(done, LANES, split_axis=0, concat_axis=0, tiled=True)  15.7 us
    all_to_all x1, starting transfers between devices, gather_plan(): lax.all_to_all(jnp.concatenate([turned, own_ids], axis=1), LANES, split_a...  4.4 us
  transfers between devices with their start and end apart: 18, of which 4 were waited for; matrix products, arithmetic and copies ran while one was open for 5% of the time, Pallas kernels for 0%

profile of v6, /device:TPU:0, one launch (start us, length us, event | category | flops | bytes accessed | tf_op | source)
XLA Modules:
  0.0 99.8 jit_solution(3698698571707534834)
XLA Ops:
  0.6 5.1 %collective-permute-start.2 = (bf16[16,128,128]{2,1,0:T(8,128)(2,1)}, bf16[16,128,128]{2,1,0:T(8,128)(2,1)S(1)}, u32[]{:S(2)}, u32[]{:S(2)}) collective-permute-start(bf16[16,128,128]{2,1,0:T(8,128)(2,1)} %bitcast.26), channel_id=1, source_target_pairs={{0,3},{1,2},{2,1},{3,0},{4,7},{5,6},{6,5},{7,4},{8,11},{9,10},{10,... | collective-permute-start | bytes 1572872 | tf_op jit(solution)/shard_map/ppermute | solution.py:157
  5.8 1.5 %collective-permute-start.1 = (bf16[16,128,128]{2,1,0:T(8,128)(2,1)}, bf16[16,128,128]{2,1,0:T(8,128)(2,1)S(1)}, u32[]{:S(2)}, u32[]{:S(2)}) collective-permute-start(bf16[16,128,128]{2,1,0:T(8,128)(2,1)} %bitcast.27), channel_id=1, source_target_pairs={{0,8},{1,9},{2,10},{3,11},{4,12},{5,13},{6,14},{7,15},{8,0},{9,1},... | collective-permute-start | bytes 1572872 | tf_op jit(solution)/shard_map/ppermute | solution.py:157
  7.3 11.5 %collective-permute-done.2.refs_3_ = bf16[16,128,128]{2,1,0:T(8,128)(2,1)S(1)} collective-permute-done((bf16[16,128,128]{2,1,0:T(8,128)(2,1)}, bf16[16,128,128]{2,1,0:T(8,128)(2,1)S(1)}, u32[]{:S(2)}, u32[]{:S(2)}) %collective-permute-start.2) | collective-permute-done | bytes 524320 | tf_op jit(solution)/shard_map/ppermute | solution.py:157
  18.8 1.7 %collective-permute-start.5 = (bf16[16,128,128]{2,1,0:T(8,128)(2,1)S(1)}, bf16[16,128,128]{2,1,0:T(8,128)(2,1)S(1)}, u32[]{:S(2)}, u32[]{:S(2)}) collective-permute-start(bf16[16,128,128]{2,1,0:T(8,128)(2,1)S(1)} %collective-permute-done.2.refs_3_), channel_id=1, source_target_pairs={{0,8},{1,9},{2,10},{3,11},{4,12},{5,13},{6,14},{7,15},{8,0},{9,1},... | collective-permute-start | bytes 1572872 | tf_op jit(solution)/shard_map/ppermute | solution.py:157
  20.5 9.8 %collective-permute-start.4 = (bf16[16,128,128]{2,1,0:T(8,128)(2,1)S(1)}, bf16[16,128,128]{2,1,0:T(8,128)(2,1)S(1)}, u32[]{:S(2)}, u32[]{:S(2)}) collective-permute-start(bf16[16,128,128]{2,1,0:T(8,128)(2,1)S(1)} %collective-permute-done.2.refs_3_), channel_id=1, source_target_pairs={{0,1},{1,0},{2,3},{3,2},{4,5},{5,4},{6,7},{7,6},{8,9},{9,8},{10,11... | collective-permute-start | bytes 1572872 | tf_op jit(solution)/shard_map/ppermute | solution.py:157
  30.4 0.5 collective-permute-start.11
  31.1 1.3 %collective-permute-start.3 = (bf16[16,128,128]{2,1,0:T(8,128)(2,1)S(1)}, bf16[16,128,128]{2,1,0:T(8,128)(2,1)}, u32[]{:S(2)}, u32[]{:S(2)}) collective-permute-start(bf16[16,128,128]{2,1,0:T(8,128)(2,1)S(1)} %collective-permute-done.refs_1_), channel_id=1, source_target_pairs={{0,8},{1,9},{2,10},{3,11},{4,12},{5,13},{6,14},{7,15},{8,0},{9,1},... | collective-permute-start | bytes 1572872 | tf_op jit(solution)/shard_map/ppermute | solution.py:157
  32.4 8.9 %collective-permute-done.4.refs_5_ = bf16[16,128,128]{2,1,0:T(8,128)(2,1)S(1)} collective-permute-done((bf16[16,128,128]{2,1,0:T(8,128)(2,1)S(1)}, bf16[16,128,128]{2,1,0:T(8,128)(2,1)S(1)}, u32[]{:S(2)}, u32[]{:S(2)}) %collective-permute-start.4) | collective-permute-done | bytes 524320 | tf_op jit(solution)/shard_map/ppermute | solution.py:157
  41.3 1.0 %copy.5 = bf16[256,256]{1,0:T(8,128)(2,1)S(1)} copy(bf16[256,256]{0,1:T(8,128)(2,1)} %bitcast.34) | data formatting | bytes 262144 | tf_op jit(solution)/shard_map/transpose | solution.py:194
  42.4 0.7 pad_maximum_fusion
  43.1 4.4 %all-to-all-start = ((bf16[16,32,256]{2,1,0:T(8,128)(2,1)}), bf16[16,32,256]{2,1,0:T(8,128)(2,1)}, u32[]{:S(2)}, u32[]{:S(2)}) async-start(bf16[16,32,256]{2,1,0:T(8,128)(2,1)} %pad_maximum_fusion), calls=%async_computation | async-start | bytes 524288 | tf_op jit(solution)/shard_map/all_to_all | solution.py:197
  47.5 0.7 slice.29
  48.2 0.7 slice.28
  49.0 1.9 %collective-permute-start.7 = (bf16[8,128,128]{2,1,0:T(8,128)(2,1)}, bf16[8,128,128]{2,1,0:T(8,128)(2,1)S(1)}, u32[]{:S(2)}, u32[]{:S(2)}) collective-permute-start(bf16[8,128,128]{2,1,0:T(8,128)(2,1)} %slice.29), channel_id=1, source_target_pairs={{0,1},{1,0},{2,3},{3,2},{4,5},{5,4},{6,7},{7,6},{8,9},{9,8},{10,11... | collective-permute-start | bytes 786440 | tf_op jit(solution)/shard_map/ppermute | solution.py:157
  50.8 1.5 %collective-permute-start.6 = (bf16[8,128,128]{2,1,0:T(8,128)(2,1)}, bf16[8,128,128]{2,1,0:T(8,128)(2,1)}, u32[]{:S(2)}, u32[]{:S(2)}) collective-permute-start(bf16[8,128,128]{2,1,0:T(8,128)(2,1)} %slice.28), channel_id=1, source_target_pairs={{0,8},{1,9},{2,10},{3,11},{4,12},{5,13},{6,14},{7,15},{8,0},{9,1},... | collective-permute-start | bytes 786440 | tf_op jit(solution)/shard_map/ppermute | solution.py:157
  52.5 0.5 collective-permute-start.13
  53.1 7.4 %collective-permute-done.7.refs_8_ = bf16[8,128,128]{2,1,0:T(8,128)(2,1)S(1)} collective-permute-done((bf16[8,128,128]{2,1,0:T(8,128)(2,1)}, bf16[8,128,128]{2,1,0:T(8,128)(2,1)S(1)}, u32[]{:S(2)}, u32[]{:S(2)}) %collective-permute-start.7) | collective-permute-done | bytes 262176 | tf_op jit(solution)/shard_map/ppermute | solution.py:157
  60.5 0.5 collective-permute-start.15
  61.0 0.8 slice_convert_fusion
  61.8 0.9 slice.27.zt_ref
  62.8 19.4 %shard_map.50 = bf16[16,2,16,256]{3,2,1,0:T(8,128)(2,1)S(1)} custom-call(s32[16,16]{1,0:T(8,128)S(1)} %fusion.3.ids_ref, s32[18]{0:T(128)S(1)} %stack.69.where_ref, bf16[16,16,256]{2,1,0:T(8,128)(2,1)S(1)} %slice.27.zt_ref, bf16[16,128,128]{2,1,0:T(8,128)(2,1)S(1)} %bitcast.30, bf16[16,128,128]{2,1,0:T(8,128)(2,1)S(1)} %collective-permute-done.refs_1_, ...), custom_call_target="tpu_custom_call" | custom-call | tf_op jit(solution)/shard_map/pallas_call | solution.py:205
  82.3 15.7 %all_to_all.10 = bf16[16,2,16,256]{3,2,1,0:T(8,128)(2,1)S(1)} all-to-all(bf16[16,2,16,256]{3,2,1,0:T(8,128)(2,1)S(1)} %shard_map.50), channel_id=1, replica_groups=mesh['dom'=2,'col'=4,'row'=4] {'col','row'}, dimensions={0} | all-to-all | bytes 524288 | tf_op jit(solution)/shard_map/all_to_all | solution.py:223
  98.1 0.8 copy.7
  98.9 0.8 copy.6
  (34 shorter events, 0.7 us)
Async XLA Ops:
  0.6 40.7 %copy-start.1 = (s32[1,1,16]{2,1,0:T(1,128)S(1)}, s32[1,1,16]{2,1,0:T(1,128)}, u32[]{:S(2)}) copy-start(s32[1,1,16]{2,1,0:T(1,128)} %param.5) | copy-start | bytes 196
  0.6 18.2 %collective-permute-start.2 = (bf16[16,128,128]{2,1,0:T(8,128)(2,1)}, bf16[16,128,128]{2,1,0:T(8,128)(2,1)S(1)}, u32[]{:S(2)}, u32[]{:S(2)}) collective-permute-start(bf16[16,128,128]{2,1,0:T(8,128)(2,1)} %bitcast.26), channel_id=1, source_target_pairs={{0,3},{1,2},{2,1},{3,0},{4,7},{5,6},{6,5},{7,4},{8,11},{9,10},{10,... | collective-permute-start | bytes 1572872 | tf_op jit(solution)/shard_map/ppermute | solution.py:157
  5.8 24.6 %collective-permute-start.1 = (bf16[16,128,128]{2,1,0:T(8,128)(2,1)}, bf16[16,128,128]{2,1,0:T(8,128)(2,1)S(1)}, u32[]{:S(2)}, u32[]{:S(2)}) collective-permute-start(bf16[16,128,128]{2,1,0:T(8,128)(2,1)} %bitcast.27), channel_id=1, source_target_pairs={{0,8},{1,9},{2,10},{3,11},{4,12},{5,13},{6,14},{7,15},{8,0},{9,1},... | collective-permute-start | bytes 1572872 | tf_op jit(solution)/shard_map/ppermute | solution.py:157
  7.3 23.6 %collective-permute-start = (bf16[16,128,128]{2,1,0:T(8,128)(2,1)}, bf16[16,128,128]{2,1,0:T(8,128)(2,1)S(1)}, u32[]{:S(2)}, u32[]{:S(2)}) collective-permute-start(bf16[16,128,128]{2,1,0:T(8,128)(2,1)} %bitcast.28), channel_id=1, source_target_pairs={{0,1},{1,0},{2,3},{3,2},{4,5},{5,4},{6,7},{7,6},{8,9},{9,8},{10,11... | collective-permute-start | bytes 1572872 | tf_op jit(solution)/shard_map/ppermute | solution.py:157
  18.8 12.3 %collective-permute-start.5 = (bf16[16,128,128]{2,1,0:T(8,128)(2,1)S(1)}, bf16[16,128,128]{2,1,0:T(8,128)(2,1)S(1)}, u32[]{:S(2)}, u32[]{:S(2)}) collective-permute-start(bf16[16,128,128]{2,1,0:T(8,128)(2,1)S(1)} %collective-permute-done.2.refs_3_), channel_id=1, source_target_pairs={{0,8},{1,9},{2,10},{3,11},{4,12},{5,13},{6,14},{7,15},{8,0},{9,1},... | collective-permute-start | bytes 1572872 | tf_op jit(solution)/shard_map/ppermute | solution.py:157
  20.5 20.8 %collective-permute-start.4 = (bf16[16,128,128]{2,1,0:T(8,128)(2,1)S(1)}, bf16[16,128,128]{2,1,0:T(8,128)(2,1)S(1)}, u32[]{:S(2)}, u32[]{:S(2)}) collective-permute-start(bf16[16,128,128]{2,1,0:T(8,128)(2,1)S(1)} %collective-permute-done.2.refs_3_), channel_id=1, source_target_pairs={{0,1},{1,0},{2,3},{3,2},{4,5},{5,4},{6,7},{7,6},{8,9},{9,8},{10,11... | collective-permute-start | bytes 1572872 | tf_op jit(solution)/shard_map/ppermute | solution.py:157
  30.4 18.6 %collective-permute-start.8 = (bf16[16,128,128]{2,1,0:T(8,128)(2,1)}, bf16[16,128,128]{2,1,0:T(8,128)(2,1)}, u32[]{:S(2)}, u32[]{:S(2)}) collective-permute-start(bf16[16,128,128]{2,1,0:T(8,128)(2,1)} %bitcast.29), channel_id=1, source_target_pairs={{0,4},{1,5},{2,6},{3,7},{4,0},{5,1},{6,2},{7,3},{8,12},{9,13},{10,... | collective-permute-start | bytes 1572872 | tf_op jit(solution)/shard_map/ppermute | solution.py:157
  30.4 20.5 %collective-permute-start.11 = (bf16[16,128,128]{2,1,0:T(8,128)(2,1)S(1)}, bf16[16,128,128]{2,1,0:T(8,128)(2,1)}, u32[]{:S(2)}, u32[]{:S(2)}) collective-permute-start(bf16[16,128,128]{2,1,0:T(8,128)(2,1)S(1)} %collective-permute-done.2.refs_3_), channel_id=1, source_target_pairs={{0,4},{1,5},{2,6},{3,7},{4,0},{5,1},{6,2},{7,3},{8,12},{9,13},{10,... | collective-permute-start | bytes 1572872 | tf_op jit(solution)/shard_map/ppermute | solution.py:157
  30.9 21.6 %collective-permute-start.9 = (bf16[16,128,128]{2,1,0:T(8,128)(2,1)S(1)}, bf16[16,128,128]{2,1,0:T(8,128)(2,1)}, u32[]{:S(2)}, u32[]{:S(2)}) collective-permute-start(bf16[16,128,128]{2,1,0:T(8,128)(2,1)S(1)} %collective-permute-done.refs_1_), channel_id=1, source_target_pairs={{0,4},{1,5},{2,6},{3,7},{4,0},{5,1},{6,2},{7,3},{8,12},{9,13},{10,... | collective-permute-start | bytes 1572872 | tf_op jit(solution)/shard_map/ppermute | solution.py:157
  31.1 21.9 %collective-permute-start.3 = (bf16[16,128,128]{2,1,0:T(8,128)(2,1)S(1)}, bf16[16,128,128]{2,1,0:T(8,128)(2,1)}, u32[]{:S(2)}, u32[]{:S(2)}) collective-permute-start(bf16[16,128,128]{2,1,0:T(8,128)(2,1)S(1)} %collective-permute-done.refs_1_), channel_id=1, source_target_pairs={{0,8},{1,9},{2,10},{3,11},{4,12},{5,13},{6,14},{7,15},{8,0},{9,1},... | collective-permute-start | bytes 1572872 | tf_op jit(solution)/shard_map/ppermute | solution.py:157
  41.3 11.1 %collective-permute-start.10 = (bf16[16,128,128]{2,1,0:T(8,128)(2,1)S(1)}, bf16[16,128,128]{2,1,0:T(8,128)(2,1)}, u32[]{:S(2)}, u32[]{:S(2)}) collective-permute-start(bf16[16,128,128]{2,1,0:T(8,128)(2,1)S(1)} %collective-permute-done.1.refs_2_), channel_id=1, source_target_pairs={{0,4},{1,5},{2,6},{3,7},{4,0},{5,1},{6,2},{7,3},{8,12},{9,13},{10,... | collective-permute-start | bytes 1572872 | tf_op jit(solution)/shard_map/ppermute | solution.py:157
  43.1 17.9 %all-to-all-start = ((bf16[16,32,256]{2,1,0:T(8,128)(2,1)}), bf16[16,32,256]{2,1,0:T(8,128)(2,1)}, u32[]{:S(2)}, u32[]{:S(2)}) async-start(bf16[16,32,256]{2,1,0:T(8,128)(2,1)} %pad_maximum_fusion), calls=%async_computation | async-start | bytes 524288 | tf_op jit(solution)/shard_map/all_to_all | solution.py:197
  48.2 14.6 %copy-start = (bf16[1,1,16,128,128]{4,3,2,1,0:T(8,128)(2,1)S(1)}, bf16[1,1,16,128,128]{4,3,2,1,0:T(8,128)(2,1)}, u32[]{:S(2)}) copy-start(bf16[1,1,16,128,128]{4,3,2,1,0:T(8,128)(2,1)} %param.4) | copy-start | bytes 1572868
  49.0 11.6 %collective-permute-start.7 = (bf16[8,128,128]{2,1,0:T(8,128)(2,1)}, bf16[8,128,128]{2,1,0:T(8,128)(2,1)S(1)}, u32[]{:S(2)}, u32[]{:S(2)}) collective-permute-start(bf16[8,128,128]{2,1,0:T(8,128)(2,1)} %slice.29), channel_id=1, source_target_pairs={{0,1},{1,0},{2,3},{3,2},{4,5},{5,4},{6,7},{7,6},{8,9},{9,8},{10,11... | collective-permute-start | bytes 786440 | tf_op jit(solution)/shard_map/ppermute | solution.py:157
  50.8 9.7 %collective-permute-start.6 = (bf16[8,128,128]{2,1,0:T(8,128)(2,1)}, bf16[8,128,128]{2,1,0:T(8,128)(2,1)}, u32[]{:S(2)}, u32[]{:S(2)}) collective-permute-start(bf16[8,128,128]{2,1,0:T(8,128)(2,1)} %slice.28), channel_id=1, source_target_pairs={{0,8},{1,9},{2,10},{3,11},{4,12},{5,13},{6,14},{7,15},{8,0},{9,1},... | collective-permute-start | bytes 786440 | tf_op jit(solution)/shard_map/ppermute | solution.py:157
  52.4 10.4 %collective-permute-start.14 = (bf16[16,128,128]{2,1,0:T(8,128)(2,1)S(1)}, bf16[16,128,128]{2,1,0:T(8,128)(2,1)}, u32[]{:S(2)}, u32[]{:S(2)}) collective-permute-start(bf16[16,128,128]{2,1,0:T(8,128)(2,1)S(1)} %collective-permute-done.5.refs_6_), channel_id=1, source_target_pairs={{0,4},{1,5},{2,6},{3,7},{4,0},{5,1},{6,2},{7,3},{8,12},{9,13},{10,... | collective-permute-start | bytes 1572872 | tf_op jit(solution)/shard_map/ppermute | solution.py:157
  52.5 10.3 %collective-permute-start.13 = (bf16[16,128,128]{2,1,0:T(8,128)(2,1)S(1)}, bf16[16,128,128]{2,1,0:T(8,128)(2,1)}, u32[]{:S(2)}, u32[]{:S(2)}) collective-permute-start(bf16[16,128,128]{2,1,0:T(8,128)(2,1)S(1)} %collective-permute-done.4.refs_5_), channel_id=1, source_target_pairs={{0,4},{1,5},{2,6},{3,7},{4,0},{5,1},{6,2},{7,3},{8,12},{9,13},{10,... | collective-permute-start | bytes 1572872 | tf_op jit(solution)/shard_map/ppermute | solution.py:157
  53.0 9.8 %collective-permute-start.12 = (bf16[16,128,128]{2,1,0:T(8,128)(2,1)}, bf16[16,128,128]{2,1,0:T(8,128)(2,1)}, u32[]{:S(2)}, u32[]{:S(2)}) collective-permute-start(bf16[16,128,128]{2,1,0:T(8,128)(2,1)} %collective-permute-done.3.refs_4_), channel_id=1, source_target_pairs={{0,4},{1,5},{2,6},{3,7},{4,0},{5,1},{6,2},{7,3},{8,12},{9,13},{10,... | collective-permute-start | bytes 1572872 | tf_op jit(solution)/shard_map/ppermute | solution.py:157
  60.5 2.3 %collective-permute-start.16 = (bf16[8,128,128]{2,1,0:T(8,128)(2,1)S(1)}, bf16[8,128,128]{2,1,0:T(8,128)(2,1)}, u32[]{:S(2)}, u32[]{:S(2)}) collective-permute-start(bf16[8,128,128]{2,1,0:T(8,128)(2,1)S(1)} %collective-permute-done.7.refs_8_), channel_id=1, source_target_pairs={{0,4},{1,5},{2,6},{3,7},{4,0},{5,1},{6,2},{7,3},{8,12},{9,13},{10,... | collective-permute-start | bytes 786440 | tf_op jit(solution)/shard_map/ppermute | solution.py:157
  60.5 2.3 %collective-permute-start.15 = (bf16[8,128,128]{2,1,0:T(8,128)(2,1)}, bf16[8,128,128]{2,1,0:T(8,128)(2,1)}, u32[]{:S(2)}, u32[]{:S(2)}) collective-permute-start(bf16[8,128,128]{2,1,0:T(8,128)(2,1)} %collective-permute-done.6.refs_7_), channel_id=1, source_target_pairs={{0,4},{1,5},{2,6},{3,7},{4,0},{5,1},{6,2},{7,3},{8,12},{9,13},{10,... | collective-permute-start | bytes 786440 | tf_op jit(solution)/shard_map/ppermute | solution.py:157

commit v7 on v4

--- a/solution.py
+++ b/solution.py
@@ -67,17 +67,15 @@
 
 
 def filter_kernel(per_piece, n_row, starts, ids_ref, where_ref, zt_ref, *refs):
-    bufs, (out_ref, s_ref, z, now, prev, straight, *scattered, sems) = refs[: len(starts)], refs[len(starts) :]
+    bufs, (out_ref, s_ref, st_ref, z, now, prev, straight, *scattered, sems) = refs[: len(starts)], refs[len(starts) :]
     tiles, slots = s_ref.shape[:2]
     orb = s_ref.shape[2]
     tile_rows = slots // PER_ROW
     pieces = zt_ref.shape[0]
 
-    copies = []
-    for i, (buf, start) in enumerate(zip(bufs, starts)):
-        place = s_ref.at[where_ref[i], pl.ds(start, buf.shape[0])]
-        copies.append(pltpu.make_async_copy(buf, place, sems.at[i]))
-        copies[-1].start()
+    for buf, start, i in zip(bufs, starts, range(len(bufs))):
+        tile = where_ref[i]
+        pltpu.make_async_copy(buf, s_ref.at[tile, pl.ds(start, buf.shape[0])], sems.at[tile]).start()
 
     for p in range(pieces):
         for b in range(per_piece):
@@ -86,19 +84,25 @@
             now[p * per_piece + b] = own.astype(jnp.float32)
     prev[...] = jnp.zeros_like(prev)
 
-    for copy in copies:
-        copy.wait()
-
-    def row_group(across, carry):
+    def row_group(step, across, carry):
         group = [across * n_row + r for r in range(n_row)]
+
+        @pl.when(step == 0)
+        def _():
+            for tile in group:
+                pltpu.make_async_copy(s_ref.at[tile], s_ref.at[tile], sems.at[tile]).wait()
+                for slot in range(slots):
+                    st_ref[tile, slot] = s_ref[tile, slot].T
+
         for t in range(tile_rows):
             places = [(tile, t * PER_ROW + p) for tile in group for p in range(PER_ROW)]
             strip = jnp.concatenate([s_ref[tile, slot] for tile, slot in places], axis=1)
+            turned_strip = jnp.concatenate([st_ref[tile, slot] for tile, slot in places], axis=0)
             where = [ids_ref[tile, slot] for tile, slot in places]
             wide = jnp.concatenate([z[g] for g in where], axis=1)
             tall = z[across * tile_rows + t]
-            straight[across * tile_rows + t] = lax.dot_general(
-                wide, strip, (((1,), (1,)), ((), ())), preferred_element_type=jnp.float32
+            straight[across * tile_rows + t] = jnp.dot(
+                wide, turned_strip, preferred_element_type=jnp.float32
             )
             turned = jnp.dot(tall, strip, preferred_element_type=jnp.float32)
             for i, g in enumerate(where):
@@ -108,7 +112,7 @@
     def one_step(step, carry):
         for ref in scattered:
             ref[...] = jnp.zeros_like(ref)
-        lax.fori_loop(0, tiles // n_row, row_group, 0)
+        lax.fori_loop(0, tiles // n_row, functools.partial(row_group, step), 0)
         total = straight[...]
         for ref in scattered:
             total += ref[...]
@@ -197,9 +201,10 @@
         out_specs=pl.BlockSpec(memory_space=pltpu.VMEM),
         scratch_shapes=[
             pltpu.VMEM((n_dev, slots, orb, orb), blocks.dtype),
+            pltpu.VMEM((n_dev, slots, orb, orb), blocks.dtype),
             pltpu.VMEM((n_blocks, share, orb), jnp.bfloat16),
             *[pltpu.VMEM((n_blocks, share, orb), jnp.float32)] * (3 + SPLIT),
-            pltpu.SemaphoreType.DMA((len(bufs),)),
+            pltpu.SemaphoreType.DMA((n_dev,)),
         ],
         compiler_params=pltpu.CompilerParams(vmem_limit_bytes=32 * 2**20),
     )(ids, where, zt, *bufs)

time: 98.6 us -> 97.4 us (0.988)
  Pallas kernels: 19.2 us -> 15.9 us
  blocking collectives: 14.4 us -> 16.5 us
    pallas_call x1, Pallas kernels: 19.2 us -> 15.9 us  [gather_plan(): pl.pallas_call(functools.partial(filter_kernel, per_piece, n_row, starts)...]
    all_to_all x1, blocking collectives: 14.4 us -> 16.5 us  [gather_plan(): back = lax.all_to_all(done, LANES, split_axis=0, concat_axis=0, tiled=True)]
where the time goes in v7:
time: 97.4 us; the launch traced here: 97 us
  starting transfers between devices  29 us (30%)
  waiting for transfers between devices  28 us (29%)
  blocking collectives  16.5 us (17%)
  Pallas kernels  15.9 us (16%)
  local copies, waits for them, and re-layouts  5.2 us (5%)
  other arithmetic  1.63 us (2%)
    ppermute x17, waiting for transfers between devices, send(): return lax.ppermute(buf, LANES, pairs)  28 us
    ppermute x17, starting transfers between devices, send(): return lax.ppermute(buf, LANES, pairs)  24.6 us
    all_to_all x1, blocking collectives, gather_plan(): back = lax.all_to_all(done, LANES, split_axis=0, concat_axis=0, tiled=True)  16.5 us
    pallas_call x1, Pallas kernels, gather_plan(): pl.pallas_call(functools.partial(filter_kernel, per_piece, n_row, starts)...  15.9 us
    all_to_all x1, starting transfers between devices, gather_plan(): lax.all_to_all(jnp.concatenate([turned, own_ids], axis=1), LANES, split_a...  4.4 us
  transfers between devices with their start and end apart: 18, of which 4 were waited for; matrix products, arithmetic and copies ran while one was open for 5% of the time, Pallas kernels for 0%

profile of v7, /device:TPU:0, one launch (start us, length us, event | category | flops | bytes accessed | tf_op | source)
XLA Modules:
  0.0 97.0 jit_solution(12991018110195909238)
XLA Ops:
  0.6 5.1 %collective-permute-start.2 = (bf16[16,128,128]{2,1,0:T(8,128)(2,1)}, bf16[16,128,128]{2,1,0:T(8,128)(2,1)S(1)}, u32[]{:S(2)}, u32[]{:S(2)}) collective-permute-start(bf16[16,128,128]{2,1,0:T(8,128)(2,1)} %bitcast.26), channel_id=1, source_target_pairs={{0,3},{1,2},{2,1},{3,0},{4,7},{5,6},{6,5},{7,4},{8,11},{9,10},{10,... | collective-permute-start | bytes 1572872 | tf_op jit(solution)/shard_map/ppermute | solution.py:144
  5.8 1.5 %collective-permute-start.1 = (bf16[16,128,128]{2,1,0:T(8,128)(2,1)}, bf16[16,128,128]{2,1,0:T(8,128)(2,1)S(1)}, u32[]{:S(2)}, u32[]{:S(2)}) collective-permute-start(bf16[16,128,128]{2,1,0:T(8,128)(2,1)} %bitcast.27), channel_id=1, source_target_pairs={{0,8},{1,9},{2,10},{3,11},{4,12},{5,13},{6,14},{7,15},{8,0},{9,1},... | collective-permute-start | bytes 1572872 | tf_op jit(solution)/shard_map/ppermute | solution.py:144
  7.3 11.5 %collective-permute-done.2.refs_3_ = bf16[16,128,128]{2,1,0:T(8,128)(2,1)S(1)} collective-permute-done((bf16[16,128,128]{2,1,0:T(8,128)(2,1)}, bf16[16,128,128]{2,1,0:T(8,128)(2,1)S(1)}, u32[]{:S(2)}, u32[]{:S(2)}) %collective-permute-start.2) | collective-permute-done | bytes 524320 | tf_op jit(solution)/shard_map/ppermute | solution.py:144
  18.8 1.7 %collective-permute-start.5 = (bf16[16,128,128]{2,1,0:T(8,128)(2,1)S(1)}, bf16[16,128,128]{2,1,0:T(8,128)(2,1)S(1)}, u32[]{:S(2)}, u32[]{:S(2)}) collective-permute-start(bf16[16,128,128]{2,1,0:T(8,128)(2,1)S(1)} %collective-permute-done.2.refs_3_), channel_id=1, source_target_pairs={{0,8},{1,9},{2,10},{3,11},{4,12},{5,13},{6,14},{7,15},{8,0},{9,1},... | collective-permute-start | bytes 1572872 | tf_op jit(solution)/shard_map/ppermute | solution.py:144
  20.5 9.8 %collective-permute-start.4 = (bf16[16,128,128]{2,1,0:T(8,128)(2,1)S(1)}, bf16[16,128,128]{2,1,0:T(8,128)(2,1)S(1)}, u32[]{:S(2)}, u32[]{:S(2)}) collective-permute-start(bf16[16,128,128]{2,1,0:T(8,128)(2,1)S(1)} %collective-permute-done.2.refs_3_), channel_id=1, source_target_pairs={{0,1},{1,0},{2,3},{3,2},{4,5},{5,4},{6,7},{7,6},{8,9},{9,8},{10,11... | collective-permute-start | bytes 1572872 | tf_op jit(solution)/shard_map/ppermute | solution.py:144
  30.4 0.5 collective-permute-start.11
  31.1 1.3 %collective-permute-start.3 = (bf16[16,128,128]{2,1,0:T(8,128)(2,1)S(1)}, bf16[16,128,128]{2,1,0:T(8,128)(2,1)}, u32[]{:S(2)}, u32[]{:S(2)}) collective-permute-start(bf16[16,128,128]{2,1,0:T(8,128)(2,1)S(1)} %collective-permute-done.refs_1_), channel_id=1, source_target_pairs={{0,8},{1,9},{2,10},{3,11},{4,12},{5,13},{6,14},{7,15},{8,0},{9,1},... | collective-permute-start | bytes 1572872 | tf_op jit(solution)/shard_map/ppermute | solution.py:144
  32.4 8.9 %collective-permute-done.4.refs_5_ = bf16[16,128,128]{2,1,0:T(8,128)(2,1)S(1)} collective-permute-done((bf16[16,128,128]{2,1,0:T(8,128)(2,1)S(1)}, bf16[16,128,128]{2,1,0:T(8,128)(2,1)S(1)}, u32[]{:S(2)}, u32[]{:S(2)}) %collective-permute-start.4) | collective-permute-done | bytes 524320 | tf_op jit(solution)/shard_map/ppermute | solution.py:144
  41.3 1.0 %copy.5 = bf16[256,256]{1,0:T(8,128)(2,1)S(1)} copy(bf16[256,256]{0,1:T(8,128)(2,1)} %bitcast.34) | data formatting | bytes 262144 | tf_op jit(solution)/shard_map/transpose | solution.py:181
  42.4 0.7 pad_maximum_fusion
  43.1 4.4 %all-to-all-start = ((bf16[16,32,256]{2,1,0:T(8,128)(2,1)}), bf16[16,32,256]{2,1,0:T(8,128)(2,1)}, u32[]{:S(2)}, u32[]{:S(2)}) async-start(bf16[16,32,256]{2,1,0:T(8,128)(2,1)} %pad_maximum_fusion), calls=%async_computation | async-start | bytes 524288 | tf_op jit(solution)/shard_map/all_to_all | solution.py:184
  47.5 0.7 slice.29
  48.2 0.7 slice.28
  49.0 1.9 %collective-permute-start.7 = (bf16[8,128,128]{2,1,0:T(8,128)(2,1)}, bf16[8,128,128]{2,1,0:T(8,128)(2,1)S(1)}, u32[]{:S(2)}, u32[]{:S(2)}) collective-permute-start(bf16[8,128,128]{2,1,0:T(8,128)(2,1)} %slice.29), channel_id=1, source_target_pairs={{0,1},{1,0},{2,3},{3,2},{4,5},{5,4},{6,7},{7,6},{8,9},{9,8},{10,11... | collective-permute-start | bytes 786440 | tf_op jit(solution)/shard_map/ppermute | solution.py:144
  50.8 1.5 %collective-permute-start.6 = (bf16[8,128,128]{2,1,0:T(8,128)(2,1)}, bf16[8,128,128]{2,1,0:T(8,128)(2,1)}, u32[]{:S(2)}, u32[]{:S(2)}) collective-permute-start(bf16[8,128,128]{2,1,0:T(8,128)(2,1)} %slice.28), channel_id=1, source_target_pairs={{0,8},{1,9},{2,10},{3,11},{4,12},{5,13},{6,14},{7,15},{8,0},{9,1},... | collective-permute-start | bytes 786440 | tf_op jit(solution)/shard_map/ppermute | solution.py:144
  52.5 0.5 collective-permute-start.13
  53.1 7.4 %collective-permute-done.7.refs_8_ = bf16[8,128,128]{2,1,0:T(8,128)(2,1)S(1)} collective-permute-done((bf16[8,128,128]{2,1,0:T(8,128)(2,1)}, bf16[8,128,128]{2,1,0:T(8,128)(2,1)S(1)}, u32[]{:S(2)}, u32[]{:S(2)}) %collective-permute-start.7) | collective-permute-done | bytes 262176 | tf_op jit(solution)/shard_map/ppermute | solution.py:144
  60.5 0.5 collective-permute-start.15
  61.0 0.8 slice_convert_fusion
  61.8 0.9 slice.27.zt_ref
  62.8 15.9 %shard_map.50 = bf16[16,2,16,256]{3,2,1,0:T(8,128)(2,1)S(1)} custom-call(s32[16,16]{1,0:T(8,128)S(1)} %fusion.3.ids_ref, s32[18]{0:T(128)S(1)} %stack.69.where_ref, bf16[16,16,256]{2,1,0:T(8,128)(2,1)S(1)} %slice.27.zt_ref, bf16[16,128,128]{2,1,0:T(8,128)(2,1)S(1)} %bitcast.30, bf16[16,128,128]{2,1,0:T(8,128)(2,1)S(1)} %collective-permute-done.refs_1_, ...), custom_call_target="tpu_custom_call" | custom-call | tf_op jit(solution)/shard_map/pallas_call | solution.py:192
  78.8 16.5 %all_to_all.10 = bf16[16,2,16,256]{3,2,1,0:T(8,128)(2,1)S(1)} all-to-all(bf16[16,2,16,256]{3,2,1,0:T(8,128)(2,1)S(1)} %shard_map.50), channel_id=1, replica_groups=mesh['dom'=2,'col'=4,'row'=4] {'col','row'}, dimensions={0} | all-to-all | bytes 524288 | tf_op jit(solution)/shard_map/all_to_all | solution.py:211
  95.3 0.8 copy.7
  96.2 0.8 copy.6
  (34 shorter events, 0.7 us)
Async XLA Ops:
  0.6 40.7 %copy-start.1 = (s32[1,1,16]{2,1,0:T(1,128)S(1)}, s32[1,1,16]{2,1,0:T(1,128)}, u32[]{:S(2)}) copy-start(s32[1,1,16]{2,1,0:T(1,128)} %param.5) | copy-start | bytes 196
  0.6 18.2 %collective-permute-start.2 = (bf16[16,128,128]{2,1,0:T(8,128)(2,1)}, bf16[16,128,128]{2,1,0:T(8,128)(2,1)S(1)}, u32[]{:S(2)}, u32[]{:S(2)}) collective-permute-start(bf16[16,128,128]{2,1,0:T(8,128)(2,1)} %bitcast.26), channel_id=1, source_target_pairs={{0,3},{1,2},{2,1},{3,0},{4,7},{5,6},{6,5},{7,4},{8,11},{9,10},{10,... | collective-permute-start | bytes 1572872 | tf_op jit(solution)/shard_map/ppermute | solution.py:144
  5.8 24.6 %collective-permute-start.1 = (bf16[16,128,128]{2,1,0:T(8,128)(2,1)}, bf16[16,128,128]{2,1,0:T(8,128)(2,1)S(1)}, u32[]{:S(2)}, u32[]{:S(2)}) collective-permute-start(bf16[16,128,128]{2,1,0:T(8,128)(2,1)} %bitcast.27), channel_id=1, source_target_pairs={{0,8},{1,9},{2,10},{3,11},{4,12},{5,13},{6,14},{7,15},{8,0},{9,1},... | collective-permute-start | bytes 1572872 | tf_op jit(solution)/shard_map/ppermute | solution.py:144
  7.3 23.6 %collective-permute-start = (bf16[16,128,128]{2,1,0:T(8,128)(2,1)}, bf16[16,128,128]{2,1,0:T(8,128)(2,1)S(1)}, u32[]{:S(2)}, u32[]{:S(2)}) collective-permute-start(bf16[16,128,128]{2,1,0:T(8,128)(2,1)} %bitcast.28), channel_id=1, source_target_pairs={{0,1},{1,0},{2,3},{3,2},{4,5},{5,4},{6,7},{7,6},{8,9},{9,8},{10,11... | collective-permute-start | bytes 1572872 | tf_op jit(solution)/shard_map/ppermute | solution.py:144
  18.8 12.3 %collective-permute-start.5 = (bf16[16,128,128]{2,1,0:T(8,128)(2,1)S(1)}, bf16[16,128,128]{2,1,0:T(8,128)(2,1)S(1)}, u32[]{:S(2)}, u32[]{:S(2)}) collective-permute-start(bf16[16,128,128]{2,1,0:T(8,128)(2,1)S(1)} %collective-permute-done.2.refs_3_), channel_id=1, source_target_pairs={{0,8},{1,9},{2,10},{3,11},{4,12},{5,13},{6,14},{7,15},{8,0},{9,1},... | collective-permute-start | bytes 1572872 | tf_op jit(solution)/shard_map/ppermute | solution.py:144
  20.5 20.8 %collective-permute-start.4 = (bf16[16,128,128]{2,1,0:T(8,128)(2,1)S(1)}, bf16[16,128,128]{2,1,0:T(8,128)(2,1)S(1)}, u32[]{:S(2)}, u32[]{:S(2)}) collective-permute-start(bf16[16,128,128]{2,1,0:T(8,128)(2,1)S(1)} %collective-permute-done.2.refs_3_), channel_id=1, source_target_pairs={{0,1},{1,0},{2,3},{3,2},{4,5},{5,4},{6,7},{7,6},{8,9},{9,8},{10,11... | collective-permute-start | bytes 1572872 | tf_op jit(solution)/shard_map/ppermute | solution.py:144
  30.4 18.6 %collective-permute-start.8 = (bf16[16,128,128]{2,1,0:T(8,128)(2,1)}, bf16[16,128,128]{2,1,0:T(8,128)(2,1)}, u32[]{:S(2)}, u32[]{:S(2)}) collective-permute-start(bf16[16,128,128]{2,1,0:T(8,128)(2,1)} %bitcast.29), channel_id=1, source_target_pairs={{0,4},{1,5},{2,6},{3,7},{4,0},{5,1},{6,2},{7,3},{8,12},{9,13},{10,... | collective-permute-start | bytes 1572872 | tf_op jit(solution)/shard_map/ppermute | solution.py:144
  30.4 20.5 %collective-permute-start.11 = (bf16[16,128,128]{2,1,0:T(8,128)(2,1)S(1)}, bf16[16,128,128]{2,1,0:T(8,128)(2,1)}, u32[]{:S(2)}, u32[]{:S(2)}) collective-permute-start(bf16[16,128,128]{2,1,0:T(8,128)(2,1)S(1)} %collective-permute-done.2.refs_3_), channel_id=1, source_target_pairs={{0,4},{1,5},{2,6},{3,7},{4,0},{5,1},{6,2},{7,3},{8,12},{9,13},{10,... | collective-permute-start | bytes 1572872 | tf_op jit(solution)/shard_map/ppermute | solution.py:144
  30.9 21.6 %collective-permute-start.9 = (bf16[16,128,128]{2,1,0:T(8,128)(2,1)S(1)}, bf16[16,128,128]{2,1,0:T(8,128)(2,1)}, u32[]{:S(2)}, u32[]{:S(2)}) collective-permute-start(bf16[16,128,128]{2,1,0:T(8,128)(2,1)S(1)} %collective-permute-done.refs_1_), channel_id=1, source_target_pairs={{0,4},{1,5},{2,6},{3,7},{4,0},{5,1},{6,2},{7,3},{8,12},{9,13},{10,... | collective-permute-start | bytes 1572872 | tf_op jit(solution)/shard_map/ppermute | solution.py:144
  31.1 21.9 %collective-permute-start.3 = (bf16[16,128,128]{2,1,0:T(8,128)(2,1)S(1)}, bf16[16,128,128]{2,1,0:T(8,128)(2,1)}, u32[]{:S(2)}, u32[]{:S(2)}) collective-permute-start(bf16[16,128,128]{2,1,0:T(8,128)(2,1)S(1)} %collective-permute-done.refs_1_), channel_id=1, source_target_pairs={{0,8},{1,9},{2,10},{3,11},{4,12},{5,13},{6,14},{7,15},{8,0},{9,1},... | collective-permute-start | bytes 1572872 | tf_op jit(solution)/shard_map/ppermute | solution.py:144
  41.3 11.1 %collective-permute-start.10 = (bf16[16,128,128]{2,1,0:T(8,128)(2,1)S(1)}, bf16[16,128,128]{2,1,0:T(8,128)(2,1)}, u32[]{:S(2)}, u32[]{:S(2)}) collective-permute-start(bf16[16,128,128]{2,1,0:T(8,128)(2,1)S(1)} %collective-permute-done.1.refs_2_), channel_id=1, source_target_pairs={{0,4},{1,5},{2,6},{3,7},{4,0},{5,1},{6,2},{7,3},{8,12},{9,13},{10,... | collective-permute-start | bytes 1572872 | tf_op jit(solution)/shard_map/ppermute | solution.py:144
  43.1 17.9 %all-to-all-start = ((bf16[16,32,256]{2,1,0:T(8,128)(2,1)}), bf16[16,32,256]{2,1,0:T(8,128)(2,1)}, u32[]{:S(2)}, u32[]{:S(2)}) async-start(bf16[16,32,256]{2,1,0:T(8,128)(2,1)} %pad_maximum_fusion), calls=%async_computation | async-start | bytes 524288 | tf_op jit(solution)/shard_map/all_to_all | solution.py:184
  48.2 14.6 %copy-start = (bf16[1,1,16,128,128]{4,3,2,1,0:T(8,128)(2,1)S(1)}, bf16[1,1,16,128,128]{4,3,2,1,0:T(8,128)(2,1)}, u32[]{:S(2)}) copy-start(bf16[1,1,16,128,128]{4,3,2,1,0:T(8,128)(2,1)} %param.4) | copy-start | bytes 1572868
  49.0 11.6 %collective-permute-start.7 = (bf16[8,128,128]{2,1,0:T(8,128)(2,1)}, bf16[8,128,128]{2,1,0:T(8,128)(2,1)S(1)}, u32[]{:S(2)}, u32[]{:S(2)}) collective-permute-start(bf16[8,128,128]{2,1,0:T(8,128)(2,1)} %slice.29), channel_id=1, source_target_pairs={{0,1},{1,0},{2,3},{3,2},{4,5},{5,4},{6,7},{7,6},{8,9},{9,8},{10,11... | collective-permute-start | bytes 786440 | tf_op jit(solution)/shard_map/ppermute | solution.py:144
  50.8 9.7 %collective-permute-start.6 = (bf16[8,128,128]{2,1,0:T(8,128)(2,1)}, bf16[8,128,128]{2,1,0:T(8,128)(2,1)}, u32[]{:S(2)}, u32[]{:S(2)}) collective-permute-start(bf16[8,128,128]{2,1,0:T(8,128)(2,1)} %slice.28), channel_id=1, source_target_pairs={{0,8},{1,9},{2,10},{3,11},{4,12},{5,13},{6,14},{7,15},{8,0},{9,1},... | collective-permute-start | bytes 786440 | tf_op jit(solution)/shard_map/ppermute | solution.py:144
  52.4 10.4 %collective-permute-start.14 = (bf16[16,128,128]{2,1,0:T(8,128)(2,1)S(1)}, bf16[16,128,128]{2,1,0:T(8,128)(2,1)}, u32[]{:S(2)}, u32[]{:S(2)}) collective-permute-start(bf16[16,128,128]{2,1,0:T(8,128)(2,1)S(1)} %collective-permute-done.5.refs_6_), channel_id=1, source_target_pairs={{0,4},{1,5},{2,6},{3,7},{4,0},{5,1},{6,2},{7,3},{8,12},{9,13},{10,... | collective-permute-start | bytes 1572872 | tf_op jit(solution)/shard_map/ppermute | solution.py:144
  52.5 10.3 %collective-permute-start.13 = (bf16[16,128,128]{2,1,0:T(8,128)(2,1)S(1)}, bf16[16,128,128]{2,1,0:T(8,128)(2,1)}, u32[]{:S(2)}, u32[]{:S(2)}) collective-permute-start(bf16[16,128,128]{2,1,0:T(8,128)(2,1)S(1)} %collective-permute-done.4.refs_5_), channel_id=1, source_target_pairs={{0,4},{1,5},{2,6},{3,7},{4,0},{5,1},{6,2},{7,3},{8,12},{9,13},{10,... | collective-permute-start | bytes 1572872 | tf_op jit(solution)/shard_map/ppermute | solution.py:144
  53.0 9.8 %collective-permute-start.12 = (bf16[16,128,128]{2,1,0:T(8,128)(2,1)}, bf16[16,128,128]{2,1,0:T(8,128)(2,1)}, u32[]{:S(2)}, u32[]{:S(2)}) collective-permute-start(bf16[16,128,128]{2,1,0:T(8,128)(2,1)} %collective-permute-done.3.refs_4_), channel_id=1, source_target_pairs={{0,4},{1,5},{2,6},{3,7},{4,0},{5,1},{6,2},{7,3},{8,12},{9,13},{10,... | collective-permute-start | bytes 1572872 | tf_op jit(solution)/shard_map/ppermute | solution.py:144
  60.5 2.3 %collective-permute-start.16 = (bf16[8,128,128]{2,1,0:T(8,128)(2,1)S(1)}, bf16[8,128,128]{2,1,0:T(8,128)(2,1)}, u32[]{:S(2)}, u32[]{:S(2)}) collective-permute-start(bf16[8,128,128]{2,1,0:T(8,128)(2,1)S(1)} %collective-permute-done.7.refs_8_), channel_id=1, source_target_pairs={{0,4},{1,5},{2,6},{3,7},{4,0},{5,1},{6,2},{7,3},{8,12},{9,13},{10,... | collective-permute-start | bytes 786440 | tf_op jit(solution)/shard_map/ppermute | solution.py:144
  60.5 2.3 %collective-permute-start.15 = (bf16[8,128,128]{2,1,0:T(8,128)(2,1)}, bf16[8,128,128]{2,1,0:T(8,128)(2,1)}, u32[]{:S(2)}, u32[]{:S(2)}) collective-permute-start(bf16[8,128,128]{2,1,0:T(8,128)(2,1)} %collective-permute-done.6.refs_7_), channel_id=1, source_target_pairs={{0,4},{1,5},{2,6},{3,7},{4,0},{5,1},{6,2},{7,3},{8,12},{9,13},{10,... | collective-permute-start | bytes 786440 | tf_op jit(solution)/shard_map/ppermute | solution.py:144

commit v8 on v0

--- a/solution.py
+++ b/solution.py
@@ -1,10 +1,17 @@
+import functools
+
 import jax
 import jax.numpy as jnp
 from jax import lax
+from jax.experimental import pallas as pl
+from jax.experimental.pallas import tpu as pltpu
 from jax.sharding import PartitionSpec as P
 
 PER_ROW = 2
 DEG = 4
+SPLIT = 4
+GATHER_LIMIT = 12 * 2**20
+LANES = ("col", "row")
 
 
 def onehot_sum(selected, high_part, low_part):
@@ -41,7 +48,7 @@
     return part_rows + part_cols
 
 
-def per_device(vectors, blocks, cols):
+def spread_plan(vectors, blocks, cols):
     tiles = blocks[0, 0]
     col_ids = cols[0, 0]
     slots, orb, _ = tiles.shape
@@ -59,6 +66,193 @@
     return (now, prev)
 
 
+def vmem(count=1):
+    return [pl.BlockSpec(memory_space=pltpu.VMEM)] * count
+
+
+def smem(count=1):
+    return [pl.BlockSpec(memory_space=pltpu.SMEM)] * count
+
+
+def anywhere(count=1):
+    return [pl.BlockSpec(memory_space=pl.ANY)] * count
+
+
+def nothing(*refs):
+    pass
+
+
+def after(value, *others, rank=0):
+    return pl.pallas_call(
+        nothing,
+        out_shape=jax.ShapeDtypeStruct(value.shape, value.dtype),
+        in_specs=anywhere(1 + len(others)),
+        out_specs=anywhere()[0],
+        input_output_aliases={0: 0},
+        compiler_params=pltpu.CompilerParams(vmem_limit_bytes=2**20),
+        cost_estimate=pl.CostEstimate(flops=0, bytes_accessed=rank * 2**26, transcendentals=0),
+    )(value, *others)
+
+
+def multiply(t, groups, across_ref, down_ref, ids_ref, z, straight, scattered):
+    tile_rows = z.shape[0] // len(groups)
+    n_row = ids_ref.shape[0] // len(groups)
+    orb = z.shape[2]
+    for g, group in enumerate(groups):
+        if not group:
+            continue
+        here = across_ref[g] * tile_rows + t
+        places = [(tile, t * PER_ROW + p) for tile in group for p in range(PER_ROW)]
+        strip = jnp.concatenate([s[i, slot] for (_, s, _, i), slot in places], axis=1)
+        turned = jnp.concatenate([st[i, slot] for (_, _, st, i), slot in places], axis=0)
+        where = [ids_ref[across_ref[g] * n_row + down_ref[f], slot] for (f, _, _, _), slot in places]
+        wide = jnp.concatenate([z[u] for u in where], axis=1)
+        straight[here] = jnp.dot(wide, turned, preferred_element_type=jnp.float32)
+        mirrored = jnp.dot(z[here], strip, preferred_element_type=jnp.float32)
+        for i, u in enumerate(where):
+            scattered[i % len(scattered)][u] += mirrored[:, i * orb : (i + 1) * orb]
+
+
+def clear(refs):
+    for ref in refs:
+        ref[...] = jnp.zeros_like(ref)
+
+
+def filter_kernel(order, n_col, n_row, across_ref, down_ref, ids_ref, zt_ref, *refs):
+    bufs, (out_ref, s_ref, st_ref, z, now, prev, straight, *scattered, sems) = (
+        refs[: len(order)],
+        refs[len(order) :],
+    )
+    n_blocks, share, orb = z.shape
+    slots = s_ref.shape[1]
+    per_piece = n_blocks // (n_col * n_row)
+    tile_rows = slots // PER_ROW
+
+    copies = []
+    for i, (buf, (g, f, start)) in enumerate(zip(bufs, order)):
+        place = s_ref.at[g * n_row + f, pl.ds(start, buf.shape[0])]
+        copies.append(pltpu.make_async_copy(buf, place, sems.at[i]))
+        copies[-1].start()
+    for p in range(n_col * n_row):
+        for b in range(per_piece):
+            own = zt_ref[p, :, b * orb : (b + 1) * orb]
+            z[p * per_piece + b] = own
+            now[p * per_piece + b] = own.astype(jnp.float32)
+    clear([prev])
+    for copy, (g, f, start) in zip(copies, order):
+        copy.wait()
+        tile = g * n_row + f
+        for slot in range(start, start + copy.src_ref.shape[0]):
+            st_ref[tile, slot] = s_ref[tile, slot].T
+
+    groups = [[(f, s_ref, st_ref, g * n_row + f) for f in range(n_row)] for g in range(n_col)]
+
+    def one_step(step, carry):
+        clear(scattered)
+
+        def block_row(t, carry):
+            multiply(t, groups, across_ref, down_ref, ids_ref, z, straight, scattered)
+            return carry
+
+        lax.fori_loop(0, tile_rows, block_row, 0)
+        total = straight[...]
+        for ref in scattered:
+            total += ref[...]
+        later = step > 0
+        total = jnp.where(later, 2.0, 1.0) * total - jnp.where(later, 1.0, 0.0) * prev[...]
+        prev[...] = now[...]
+        now[...] = total
+        z[...] = total.astype(z.dtype)
+        return carry
+
+    lax.fori_loop(0, DEG, one_step, 0)
+    for p in range(n_col * n_row):
+        for b in range(per_piece):
+            u = p * per_piece + b
+            out_ref[p, 0, :, b * orb : (b + 1) * orb] = now[u].astype(out_ref.dtype)
+            out_ref[p, 1, :, b * orb : (b + 1) * orb] = prev[u].astype(out_ref.dtype)
+
+
+def gather_plan(vectors, blocks, cols):
+    n_dev = lax.axis_size(LANES)
+    n_col, n_row = lax.axis_size("col"), lax.axis_size("row")
+    rows, width = vectors.shape
+    slots, orb = blocks.shape[2:4]
+    share = width // n_dev
+    per_piece = rows // orb
+    n_blocks = n_dev * per_piece
+    half = slots // 2
+    across = lax.axis_index("col") ^ jnp.arange(n_col, dtype=jnp.int32)
+    down = lax.axis_index("row") ^ jnp.arange(n_row, dtype=jnp.int32)
+
+    def send(buf, flip_col, flip_row):
+        pairs = [
+            (c * n_row + r, (c ^ flip_col) * n_row + (r ^ flip_row))
+            for c in range(n_col)
+            for r in range(n_row)
+        ]
+        return lax.ppermute(buf, LANES, pairs)
+
+    def to_mate(*bufs):
+        return [send(buf, 1, 0) for buf in bufs]
+
+    own = blocks[0, 0]
+    far = send(own, 0, 3)
+    near = send(own, 0, 1)
+    over_own = send(own, 2, 0)
+
+    near = after(near, over_own)
+    over_near = send(near, 2, 0)
+    mates = to_mate(own, near, over_own)
+    far = after(after(far, rank=1), over_near, *mates[1:])
+    over_far = send(far, 2, 0)
+    last = send(far, 0, 1)
+
+    mates += to_mate(far, over_near)
+    last = after(last, over_far, mates[0], *mates[3:])
+    over_last = send(last[:half], 2, 0)
+    side_last = send(over_far[half:], 0, 1)
+    mates += to_mate(last, over_far, over_last, side_last)
+
+    turned = vectors.T.reshape(n_dev, share, rows)
+    own_ids = jnp.pad(cols[0, 0].astype(vectors.dtype), (0, rows - slots))
+    own_ids = jnp.broadcast_to(own_ids, (n_dev, share, rows))
+    payload = after(jnp.concatenate([turned, own_ids], axis=1), last)
+    both = lax.all_to_all(payload, LANES, split_axis=0, concat_axis=0, tiled=True)
+    local = both[:, share, :slots].astype(jnp.int32)
+    at_row = (jnp.arange(n_dev, dtype=jnp.int32) % n_row)[:, None]
+    ids = (local // per_piece * n_row + at_row) * per_piece + local % per_piece
+
+    bufs = [own, near, over_own, far, over_near, last, over_far, over_last, side_last]
+    order = [(0, 0, 0), (0, 1, 0), (2, 0, 0), (0, 3, 0), (2, 1, 0), (0, 2, 0), (2, 3, 0), (2, 2, 0), (2, 2, half)]
+    order += [(g ^ 1, f, slot) for g, f, slot in order]
+    bufs += mates
+    done = pl.pallas_call(
+        functools.partial(filter_kernel, order, n_col, n_row),
+        out_shape=jax.ShapeDtypeStruct((n_dev, 2, share, rows), jnp.bfloat16),
+        in_specs=smem(3) + vmem() + anywhere(len(bufs)),
+        out_specs=vmem()[0],
+        scratch_shapes=[
+            *[pltpu.VMEM((n_dev, slots, orb, orb), blocks.dtype)] * 2,
+            pltpu.VMEM((n_blocks, share, orb), jnp.bfloat16),
+            *[pltpu.VMEM((n_blocks, share, orb), jnp.float32)] * (3 + SPLIT),
+            pltpu.SemaphoreType.DMA((len(bufs),)),
+        ],
+        compiler_params=pltpu.CompilerParams(vmem_limit_bytes=32 * 2**20),
+    )(across, down, ids, both[:, :share], *bufs)
+    back = lax.all_to_all(done, LANES, split_axis=0, concat_axis=0, tiled=True)
+    outs = jnp.transpose(back, (1, 3, 0, 2)).reshape(2, rows, width).astype(jnp.float32)
+    return outs[0], outs[1]
+
+
+def per_device(vectors, blocks, cols):
+    n_dev = lax.axis_size(LANES)
+    line_of_four = lax.axis_size("col") == 4 and lax.axis_size("row") == 4
+    if line_of_four and n_dev * blocks.size * blocks.dtype.itemsize <= GATHER_LIMIT:
+        return gather_plan(vectors, blocks, cols)
+    return spread_plan(vectors, blocks, cols)
+
+
 def solution(mesh):
     return jax.shard_map(
         per_device,

time: 254 us -> 112 us (0.44)
  blocking collectives: 114 us -> 14.5 us
  waiting for transfers between devices: 90.3 us -> 40.9 us
  starting transfers between devices: 0.33 us -> 27.3 us
  Pallas kernels: 0 us -> 18.5 us
  matrix products: 14.7 us -> 0 us
  between operations: 14.4 us -> 0.78 us
  other arithmetic: 7.56 us -> 1.63 us
  local copies, waits for them, and re-layouts: 12.8 us -> 7.59 us
    all_gather x8 -> x0, blocking collectives: 114 us -> none  [the longest x4 84.7 us: apply_pair(): lax.all_gather(send, 'row', axis=0, tiled=True)]
    reduce_scatter x8 -> x0, waiting for transfers between devices: 90.1 us -> none  [the longest x4 89.7 us: apply_pair(): lax.psum_scatter(summed.reshape(tile_cols * orb, width).astype(jnp.bfloat...]
    ppermute x0 -> x17, waiting for transfers between devices: none -> 40.9 us  [send(): return lax.ppermute(buf, LANES, pairs)]
    pallas_call x0 -> x6, Pallas kernels: none -> 18.5 us  [the longest x1 18.5 us: gather_plan(): pl.pallas_call(functools.partial(filter_kernel, order, n_col, n_row), out...]
    dot_general x16 -> x0, matrix products: 14.7 us -> none  [the longest x4 5.97 us: apply_pair(): jnp.einsum('tpio,tik->tpok', grouped, tall, preferred_element_type=jnp.fl...]
    all_to_all x0 -> x1, blocking collectives: none -> 14.5 us  [gather_plan(): back = lax.all_to_all(done, LANES, split_axis=0, concat_axis=0, tiled=True)]
    ppermute x0 -> x17, starting transfers between devices: none -> 14.2 us  [send(): return lax.ppermute(buf, LANES, pairs)]
    all_to_all x0 -> x1, starting transfers between devices: none -> 13 us  [gather_plan(): lax.all_to_all(payload, LANES, split_axis=0, concat_axis=0, tiled=True)]
  transfers between devices with their start and end apart: 8 -> 18, of which waited for: 5 -> 6; matrix products, arithmetic and copies ran while one was open for 8% -> 4% of each run, Pallas kernels for 0% -> 0%
where the time goes in v8:
time: 112 us; the launch traced here: 111 us
  waiting for transfers between devices  40.9 us (37%)
  starting transfers between devices  27.3 us (24%)
  Pallas kernels  18.5 us (17%)
  blocking collectives  14.5 us (13%)
  local copies, waits for them, and re-layouts  7.59 us (7%)
  other arithmetic  1.63 us (1%)
    ppermute x17, waiting for transfers between devices, send(): return lax.ppermute(buf, LANES, pairs)  40.9 us
    pallas_call x1, Pallas kernels, gather_plan(): pl.pallas_call(functools.partial(filter_kernel, order, n_col, n_row), out...  18.5 us
    all_to_all x1, blocking collectives, gather_plan(): back = lax.all_to_all(done, LANES, split_axis=0, concat_axis=0, tiled=True)  14.5 us
    ppermute x17, starting transfers between devices, send(): return lax.ppermute(buf, LANES, pairs)  14.2 us
    all_to_all x1, starting transfers between devices, gather_plan(): lax.all_to_all(payload, LANES, split_axis=0, concat_axis=0, tiled=True)  13 us
    unnamed x14, local copies, waits for them, and re-layouts  5.08 us
  transfers between devices with their start and end apart: 18, of which 6 were waited for; matrix products, arithmetic and copies ran while one was open for 4% of the time, Pallas kernels for 0%

profile of v8, /device:TPU:0, one launch (start us, length us, event | category | flops | bytes accessed | tf_op | source)
XLA Modules:
  0.0 111.1 jit_solution(8691015249035601961)
XLA Ops:
  0.6 3.0 %collective-permute-start.2 = (bf16[16,128,128]{2,1,0:T(8,128)(2,1)}, bf16[16,128,128]{2,1,0:T(8,128)(2,1)S(1)}, u32[]{:S(2)}, u32[]{:S(2)}) collective-permute-start(bf16[16,128,128]{2,1,0:T(8,128)(2,1)} %bitcast.3.refs_0_), channel_id=1, source_target_pairs={{0,8},{1,9},{2,10},{3,11},{4,12},{5,13},{6,14},{7,15},{8,0},{9,1},... | collective-permute-start | bytes 1572872 | tf_op jit(solution)/shard_map/ppermute | solution.py:194
  3.7 1.6 %collective-permute-start.1 = (bf16[16,128,128]{2,1,0:T(8,128)(2,1)}, bf16[16,128,128]{2,1,0:T(8,128)(2,1)S(1)}, u32[]{:S(2)}, u32[]{:S(2)}) collective-permute-start(bf16[16,128,128]{2,1,0:T(8,128)(2,1)} %bitcast.3.refs_0_), channel_id=1, source_target_pairs={{0,1},{1,0},{2,3},{3,2},{4,5},{5,4},{6,7},{7,6},{8,9},{9,8},{10,11... | collective-permute-start | bytes 1572872 | tf_op jit(solution)/shard_map/ppermute | solution.py:194
  5.2 2.5 %collective-permute-start = (bf16[16,128,128]{2,1,0:T(8,128)(2,1)}, bf16[16,128,128]{2,1,0:T(8,128)(2,1)S(1)}, u32[]{:S(2)}, u32[]{:S(2)}) collective-permute-start(bf16[16,128,128]{2,1,0:T(8,128)(2,1)} %bitcast.3.refs_0_), channel_id=1, source_target_pairs={{0,3},{1,2},{2,1},{3,0},{4,7},{5,6},{6,5},{7,4},{8,11},{9,10},{10,... | collective-permute-start | bytes 1572872 | tf_op jit(solution)/shard_map/ppermute | solution.py:194
  7.7 8.1 %collective-permute-done.2.refs_1_.refs_2_ = bf16[16,128,128]{2,1,0:T(8,128)(2,1)S(1)} collective-permute-done((bf16[16,128,128]{2,1,0:T(8,128)(2,1)}, bf16[16,128,128]{2,1,0:T(8,128)(2,1)S(1)}, u32[]{:S(2)}, u32[]{:S(2)}) %collective-permute-start.2) | collective-permute-done | bytes 524320 | tf_op jit(solution)/shard_map/ppermute | solution.py:194
  15.8 2.1 %collective-permute-done.1.refs_0_ = bf16[16,128,128]{2,1,0:T(8,128)(2,1)S(1)} collective-permute-done((bf16[16,128,128]{2,1,0:T(8,128)(2,1)}, bf16[16,128,128]{2,1,0:T(8,128)(2,1)S(1)}, u32[]{:S(2)}, u32[]{:S(2)}) %collective-permute-start.1) | collective-permute-done | bytes 524320 | tf_op jit(solution)/shard_map/ppermute | solution.py:194
  18.9 11.7 %collective-permute-done.refs_0_ = bf16[16,128,128]{2,1,0:T(8,128)(2,1)S(1)} collective-permute-done((bf16[16,128,128]{2,1,0:T(8,128)(2,1)}, bf16[16,128,128]{2,1,0:T(8,128)(2,1)S(1)}, u32[]{:S(2)}, u32[]{:S(2)}) %collective-permute-start) | collective-permute-done | bytes 524320 | tf_op jit(solution)/shard_map/ppermute | solution.py:194
  30.7 0.8 copy-done
  32.5 0.8 collective-permute-start.6
  33.9 0.7 pad_maximum_fusion.refs_0_
  34.7 11.1 %collective-permute-done.7.refs_1_.refs_6_ = bf16[16,128,128]{2,1,0:T(8,128)(2,1)S(1)} collective-permute-done((bf16[16,128,128]{2,1,0:T(8,128)(2,1)S(1)}, bf16[16,128,128]{2,1,0:T(8,128)(2,1)S(1)}, u32[]{:S(2)}, u32[]{:S(2)}) %collective-permute-start.7) | collective-permute-done | bytes 524320 | tf_op jit(solution)/shard_map/ppermute | solution.py:194
  46.0 13.0 %all-to-all-start = ((bf16[16,32,256]{2,1,0:T(8,128)(2,1)}), bf16[16,32,256]{2,1,0:T(8,128)(2,1)}, u32[]{:S(2)}, u32[]{:S(2)}) async-start(bf16[16,32,256]{2,1,0:T(8,128)(2,1)} %shard_map.54), calls=%async_computation | async-start | bytes 524288 | tf_op jit(solution)/shard_map/all_to_all | solution.py:221
  59.1 0.7 slice.29
  59.8 1.9 %collective-permute-start.12 = (bf16[8,128,128]{2,1,0:T(8,128)(2,1)}, bf16[8,128,128]{2,1,0:T(8,128)(2,1)S(1)}, u32[]{:S(2)}, u32[]{:S(2)}) collective-permute-start(bf16[8,128,128]{2,1,0:T(8,128)(2,1)} %slice.29), channel_id=1, source_target_pairs={{0,1},{1,0},{2,3},{3,2},{4,5},{5,4},{6,7},{7,6},{8,9},{9,8},{10,11... | collective-permute-start | bytes 786440 | tf_op jit(solution)/shard_map/ppermute | solution.py:194
  61.6 0.7 slice.28
  62.4 1.5 %collective-permute-start.11 = (bf16[8,128,128]{2,1,0:T(8,128)(2,1)}, bf16[8,128,128]{2,1,0:T(8,128)(2,1)}, u32[]{:S(2)}, u32[]{:S(2)}) collective-permute-start(bf16[8,128,128]{2,1,0:T(8,128)(2,1)} %slice.28), channel_id=1, source_target_pairs={{0,8},{1,9},{2,10},{3,11},{4,12},{5,13},{6,14},{7,15},{8,0},{9,1},... | collective-permute-start | bytes 786440 | tf_op jit(solution)/shard_map/ppermute | solution.py:194
  64.4 7.6 %collective-permute-done.12.refs_8_ = bf16[8,128,128]{2,1,0:T(8,128)(2,1)S(1)} collective-permute-done((bf16[8,128,128]{2,1,0:T(8,128)(2,1)}, bf16[8,128,128]{2,1,0:T(8,128)(2,1)S(1)}, u32[]{:S(2)}, u32[]{:S(2)}) %collective-permute-start.12) | collective-permute-done | bytes 262176 | tf_op jit(solution)/shard_map/ppermute | solution.py:194
  72.5 0.8 slice_convert_fusion
  73.3 0.9 slice.27.zt_ref
  74.3 1.0 copy-done.1
  75.3 1.0 copy-done.3
  76.4 18.5 %shard_map.55 = bf16[16,2,16,256]{3,2,1,0:T(8,128)(2,1)S(1)} custom-call(s32[4]{0:T(128)S(1)} %get-tuple-element.7.across_ref, s32[4]{0:T(128)S(1)} %get-tuple-element.6.down_ref, s32[16,16]{1,0:T(8,128)S(1)} %fusion.3.ids_ref, bf16[16,16,256]{2,1,0:T(8,128)(2,1)S(1)} %slice.27.zt_ref, bf16[16,128,128]{2,1,0:T(8,128)(2,1)} %bitcast.3.refs_0_, ...), custom_call_target="tpu_custom_call" | custom-call | tf_op jit(solution)/shard_map/pallas_call | solution.py:230
  94.8 14.5 %all_to_all.10 = bf16[16,2,16,256]{3,2,1,0:T(8,128)(2,1)S(1)} all-to-all(bf16[16,2,16,256]{3,2,1,0:T(8,128)(2,1)S(1)} %shard_map.55), channel_id=1, replica_groups=mesh['dom'=2,'col'=4,'row'=4] {'col','row'}, dimensions={0} | all-to-all | bytes 524288 | tf_op jit(solution)/shard_map/all_to_all | solution.py:243
  109.5 0.8 copy.12
  110.3 0.8 copy.11
  (47 shorter events, 4.2 us)
Async XLA Ops:
  0.6 15.2 %collective-permute-start.2 = (bf16[16,128,128]{2,1,0:T(8,128)(2,1)}, bf16[16,128,128]{2,1,0:T(8,128)(2,1)S(1)}, u32[]{:S(2)}, u32[]{:S(2)}) collective-permute-start(bf16[16,128,128]{2,1,0:T(8,128)(2,1)} %bitcast.3.refs_0_), channel_id=1, source_target_pairs={{0,8},{1,9},{2,10},{3,11},{4,12},{5,13},{6,14},{7,15},{8,0},{9,1},... | collective-permute-start | bytes 1572872 | tf_op jit(solution)/shard_map/ppermute | solution.py:194
  3.7 14.3 %collective-permute-start.1 = (bf16[16,128,128]{2,1,0:T(8,128)(2,1)}, bf16[16,128,128]{2,1,0:T(8,128)(2,1)S(1)}, u32[]{:S(2)}, u32[]{:S(2)}) collective-permute-start(bf16[16,128,128]{2,1,0:T(8,128)(2,1)} %bitcast.3.refs_0_), channel_id=1, source_target_pairs={{0,1},{1,0},{2,3},{3,2},{4,5},{5,4},{6,7},{7,6},{8,9},{9,8},{10,11... | collective-permute-start | bytes 1572872 | tf_op jit(solution)/shard_map/ppermute | solution.py:194
  5.2 25.4 %collective-permute-start = (bf16[16,128,128]{2,1,0:T(8,128)(2,1)}, bf16[16,128,128]{2,1,0:T(8,128)(2,1)S(1)}, u32[]{:S(2)}, u32[]{:S(2)}) collective-permute-start(bf16[16,128,128]{2,1,0:T(8,128)(2,1)} %bitcast.3.refs_0_), channel_id=1, source_target_pairs={{0,3},{1,2},{2,1},{3,0},{4,7},{5,6},{6,5},{7,4},{8,11},{9,10},{10,... | collective-permute-start | bytes 1572872 | tf_op jit(solution)/shard_map/ppermute | solution.py:194
  17.9 12.8 %copy-start.2 = (bf16[16,128,128]{2,1,0:T(8,128)(2,1)}, bf16[16,128,128]{2,1,0:T(8,128)(2,1)S(1)}, u32[]{:S(2)}) copy-start(bf16[16,128,128]{2,1,0:T(8,128)(2,1)S(1)} %shard_map.51.refs_1_) | copy-start | bytes 1572868
  17.9 12.7 %collective-permute-start.3 = (bf16[16,128,128]{2,1,0:T(8,128)(2,1)S(1)}, bf16[16,128,128]{2,1,0:T(8,128)(2,1)S(1)}, u32[]{:S(2)}, u32[]{:S(2)}) collective-permute-start(bf16[16,128,128]{2,1,0:T(8,128)(2,1)S(1)} %shard_map.51.refs_1_), channel_id=1, source_target_pairs={{0,8},{1,9},{2,10},{3,11},{4,12},{5,13},{6,14},{7,15},{8,0},{9,1},... | collective-permute-start | bytes 1572872 | tf_op jit(solution)/shard_map/ppermute | solution.py:194
  18.4 12.2 %collective-permute-start.5 = (bf16[16,128,128]{2,1,0:T(8,128)(2,1)S(1)}, bf16[16,128,128]{2,1,0:T(8,128)(2,1)S(1)}, u32[]{:S(2)}, u32[]{:S(2)}) collective-permute-start(bf16[16,128,128]{2,1,0:T(8,128)(2,1)S(1)} %collective-permute-done.2.refs_1_.refs_2_), channel_id=1, source_target_pairs={{0,4},{1,5},{2,6},{3,7},{4,0},{5,1},{6,2},{7,3},{8,12},{9,13},{10,... | collective-permute-start | bytes 1572872 | tf_op jit(solution)/shard_map/ppermute | solution.py:194
  18.4 12.2 %collective-permute-start.4 = (bf16[16,128,128]{2,1,0:T(8,128)(2,1)S(1)}, bf16[16,128,128]{2,1,0:T(8,128)(2,1)S(1)}, u32[]{:S(2)}, u32[]{:S(2)}) collective-permute-start(bf16[16,128,128]{2,1,0:T(8,128)(2,1)S(1)} %shard_map.51.refs_1_), channel_id=1, source_target_pairs={{0,4},{1,5},{2,6},{3,7},{4,0},{5,1},{6,2},{7,3},{8,12},{9,13},{10,... | collective-permute-start | bytes 1572872 | tf_op jit(solution)/shard_map/ppermute | solution.py:194
  18.9 15.7 %collective-permute-start.8 = (bf16[16,128,128]{2,1,0:T(8,128)(2,1)}, bf16[16,128,128]{2,1,0:T(8,128)(2,1)}, u32[]{:S(2)}, u32[]{:S(2)}) collective-permute-start(bf16[16,128,128]{2,1,0:T(8,128)(2,1)} %bitcast.3.refs_0_), channel_id=1, source_target_pairs={{0,4},{1,5},{2,6},{3,7},{4,0},{5,1},{6,2},{7,3},{8,12},{9,13},{10,... | collective-permute-start | bytes 1572872 | tf_op jit(solution)/shard_map/ppermute | solution.py:194
  30.6 2.6 %copy-start.4 = (bf16[256,256]{1,0:T(8,128)(2,1)S(1)}, bf16[256,256]{1,0:T(8,128)(2,1)}, u32[]{:S(2)}) copy-start(bf16[256,256]{1,0:T(8,128)(2,1)} %param.3) | copy-start | bytes 393220
  30.6 4.0 %collective-permute-start.10 = (bf16[16,128,128]{2,1,0:T(8,128)(2,1)S(1)}, bf16[16,128,128]{2,1,0:T(8,128)(2,1)}, u32[]{:S(2)}, u32[]{:S(2)}) collective-permute-start(bf16[16,128,128]{2,1,0:T(8,128)(2,1)S(1)} %collective-permute-done.3.refs_1_.refs_4_), channel_id=1, source_target_pairs={{0,4},{1,5},{2,6},{3,7},{4,0},{5,1},{6,2},{7,3},{8,12},{9,13},{10,... | collective-permute-start | bytes 1572872 | tf_op jit(solution)/shard_map/ppermute | solution.py:194
  30.7 0.8 copy-start
  31.5 3.2 %collective-permute-start.9 = (bf16[16,128,128]{2,1,0:T(8,128)(2,1)S(1)}, bf16[16,128,128]{2,1,0:T(8,128)(2,1)}, u32[]{:S(2)}, u32[]{:S(2)}) collective-permute-start(bf16[16,128,128]{2,1,0:T(8,128)(2,1)S(1)} %shard_map.52.refs_3_), channel_id=1, source_target_pairs={{0,4},{1,5},{2,6},{3,7},{4,0},{5,1},{6,2},{7,3},{8,12},{9,13},{10,... | collective-permute-start | bytes 1572872 | tf_op jit(solution)/shard_map/ppermute | solution.py:194
  31.9 13.9 %collective-permute-start.7 = (bf16[16,128,128]{2,1,0:T(8,128)(2,1)S(1)}, bf16[16,128,128]{2,1,0:T(8,128)(2,1)S(1)}, u32[]{:S(2)}, u32[]{:S(2)}) collective-permute-start(bf16[16,128,128]{2,1,0:T(8,128)(2,1)S(1)} %shard_map.52.refs_3_), channel_id=1, source_target_pairs={{0,8},{1,9},{2,10},{3,11},{4,12},{5,13},{6,14},{7,15},{8,0},{9,1},... | collective-permute-start | bytes 1572872 | tf_op jit(solution)/shard_map/ppermute | solution.py:194
  32.5 13.6 %collective-permute-start.6 = (bf16[16,128,128]{2,1,0:T(8,128)(2,1)S(1)}, bf16[16,128,128]{2,1,0:T(8,128)(2,1)S(1)}, u32[]{:S(2)}, u32[]{:S(2)}) collective-permute-start(bf16[16,128,128]{2,1,0:T(8,128)(2,1)S(1)} %shard_map.52.refs_3_), channel_id=1, source_target_pairs={{0,1},{1,0},{2,3},{3,2},{4,5},{5,4},{6,7},{7,6},{8,9},{9,8},{10,11... | collective-permute-start | bytes 1572872 | tf_op jit(solution)/shard_map/ppermute | solution.py:194
  33.2 0.7 copy-start.5
  46.0 26.5 %all-to-all-start = ((bf16[16,32,256]{2,1,0:T(8,128)(2,1)}), bf16[16,32,256]{2,1,0:T(8,128)(2,1)}, u32[]{:S(2)}, u32[]{:S(2)}) async-start(bf16[16,32,256]{2,1,0:T(8,128)(2,1)} %shard_map.54), calls=%async_computation | async-start | bytes 524288 | tf_op jit(solution)/shard_map/all_to_all | solution.py:221
  59.8 12.2 %collective-permute-start.12 = (bf16[8,128,128]{2,1,0:T(8,128)(2,1)}, bf16[8,128,128]{2,1,0:T(8,128)(2,1)S(1)}, u32[]{:S(2)}, u32[]{:S(2)}) collective-permute-start(bf16[8,128,128]{2,1,0:T(8,128)(2,1)} %slice.29), channel_id=1, source_target_pairs={{0,1},{1,0},{2,3},{3,2},{4,5},{5,4},{6,7},{7,6},{8,9},{9,8},{10,11... | collective-permute-start | bytes 786440 | tf_op jit(solution)/shard_map/ppermute | solution.py:194
  62.4 9.6 %collective-permute-start.11 = (bf16[8,128,128]{2,1,0:T(8,128)(2,1)}, bf16[8,128,128]{2,1,0:T(8,128)(2,1)}, u32[]{:S(2)}, u32[]{:S(2)}) collective-permute-start(bf16[8,128,128]{2,1,0:T(8,128)(2,1)} %slice.28), channel_id=1, source_target_pairs={{0,8},{1,9},{2,10},{3,11},{4,12},{5,13},{6,14},{7,15},{8,0},{9,1},... | collective-permute-start | bytes 786440 | tf_op jit(solution)/shard_map/ppermute | solution.py:194
  63.8 10.4 %collective-permute-start.13 = (bf16[16,128,128]{2,1,0:T(8,128)(2,1)S(1)}, bf16[16,128,128]{2,1,0:T(8,128)(2,1)}, u32[]{:S(2)}, u32[]{:S(2)}) collective-permute-start(bf16[16,128,128]{2,1,0:T(8,128)(2,1)S(1)} %shard_map.53.refs_1_.refs_5_), channel_id=1, source_target_pairs={{0,4},{1,5},{2,6},{3,7},{4,0},{5,1},{6,2},{7,3},{8,12},{9,13},{10,... | collective-permute-start | bytes 1572872 | tf_op jit(solution)/shard_map/ppermute | solution.py:194
  63.8 10.4 %collective-permute-start.14 = (bf16[16,128,128]{2,1,0:T(8,128)(2,1)S(1)}, bf16[16,128,128]{2,1,0:T(8,128)(2,1)}, u32[]{:S(2)}, u32[]{:S(2)}) collective-permute-start(bf16[16,128,128]{2,1,0:T(8,128)(2,1)S(1)} %collective-permute-done.7.refs_1_.refs_6_), channel_id=1, source_target_pairs={{0,4},{1,5},{2,6},{3,7},{4,0},{5,1},{6,2},{7,3},{8,12},{9,13},{10,... | collective-permute-start | bytes 1572872 | tf_op jit(solution)/shard_map/ppermute | solution.py:194
  72.0 2.3 %collective-permute-start.16 = (bf16[8,128,128]{2,1,0:T(8,128)(2,1)S(1)}, bf16[8,128,128]{2,1,0:T(8,128)(2,1)}, u32[]{:S(2)}, u32[]{:S(2)}) collective-permute-start(bf16[8,128,128]{2,1,0:T(8,128)(2,1)S(1)} %collective-permute-done.12.refs_8_), channel_id=1, source_target_pairs={{0,4},{1,5},{2,6},{3,7},{4,0},{5,1},{6,2},{7,3},{8,12},{9,13},{10,... | collective-permute-start | bytes 786440 | tf_op jit(solution)/shard_map/ppermute | solution.py:194
  72.0 2.3 %collective-permute-start.15 = (bf16[8,128,128]{2,1,0:T(8,128)(2,1)}, bf16[8,128,128]{2,1,0:T(8,128)(2,1)}, u32[]{:S(2)}, u32[]{:S(2)}) collective-permute-start(bf16[8,128,128]{2,1,0:T(8,128)(2,1)} %collective-permute-done.11.refs_7_), channel_id=1, source_target_pairs={{0,4},{1,5},{2,6},{3,7},{4,0},{5,1},{6,2},{7,3},{8,12},{9,13},{10,... | collective-permute-start | bytes 786440 | tf_op jit(solution)/shard_map/ppermute | solution.py:194
  74.3 1.0 copy-start.1
  75.3 1.0 copy-start.3

commit v9 on v8

--- a/solution.py
+++ b/solution.py
@@ -82,7 +82,7 @@
     pass
 
 
-def after(value, *others, rank=0):
+def after(value, *others):
     return pl.pallas_call(
         nothing,
         out_shape=jax.ShapeDtypeStruct(value.shape, value.dtype),
@@ -90,13 +90,53 @@
         out_specs=anywhere()[0],
         input_output_aliases={0: 0},
         compiler_params=pltpu.CompilerParams(vmem_limit_bytes=2**20),
-        cost_estimate=pl.CostEstimate(flops=0, bytes_accessed=rank * 2**26, transcendentals=0),
     )(value, *others)
 
 
-def multiply(t, groups, across_ref, down_ref, ids_ref, z, straight, scattered):
+def pick_kernel(first_ref, one_ref, other_ref, *refs):
+    out_ref, sem = refs[-2:]
+
+    @pl.when(first_ref[0] != 0)
+    def _():
+        copy = pltpu.make_async_copy(one_ref, out_ref, sem)
+        copy.start()
+        copy.wait()
+
+    @pl.when(first_ref[0] == 0)
+    def _():
+        copy = pltpu.make_async_copy(other_ref, out_ref, sem)
+        copy.start()
+        copy.wait()
+
+
+def pick(first, one, other, *others):
+    return pl.pallas_call(
+        pick_kernel,
+        out_shape=jax.ShapeDtypeStruct(one.shape, one.dtype),
+        in_specs=smem() + anywhere(2 + len(others)),
+        out_specs=anywhere()[0],
+        scratch_shapes=[pltpu.SemaphoreType.DMA(())],
+        compiler_params=pltpu.CompilerParams(vmem_limit_bytes=2**20),
+    )(first, one, other, *others)
+
+
+def split_kernel(peers_ref, vectors_ref, ids_ref, keep_ref, go_ref, turned):
+    count, share, rows = turned.shape
+    whole = vectors_ref[...].T
+    for d in range(count):
+        turned[d] = whole[d * share : (d + 1) * share]
+    for k in range(count):
+        out_ref = (keep_ref, go_ref)[k // (count // 2)]
+        out_ref[k % (count // 2), :, :rows] = turned[peers_ref[k]]
+        out_ref[k % (count // 2), :, rows:] = ids_ref[...]
+
+
+def place(g, f):
+    return (f >> 1) * 8 + ((f & 1) ^ (f >> 1)) * 4 + g
+
+
+def multiply(t, groups, across_ref, ids_ref, z, straight, scattered):
     tile_rows = z.shape[0] // len(groups)
-    n_row = ids_ref.shape[0] // len(groups)
     orb = z.shape[2]
     for g, group in enumerate(groups):
         if not group:
@@ -105,7 +145,7 @@
         places = [(tile, t * PER_ROW + p) for tile in group for p in range(PER_ROW)]
         strip = jnp.concatenate([s[i, slot] for (_, s, _, i), slot in places], axis=1)
         turned = jnp.concatenate([st[i, slot] for (_, _, st, i), slot in places], axis=0)
-        where = [ids_ref[across_ref[g] * n_row + down_ref[f], slot] for (f, _, _, _), slot in places]
+        where = [ids_ref[place(g, f), slot] for (f, _, _, _), slot in places]
         wide = jnp.concatenate([z[u] for u in where], axis=1)
         straight[here] = jnp.dot(wide, turned, preferred_element_type=jnp.float32)
         mirrored = jnp.dot(z[here], strip, preferred_element_type=jnp.float32)
@@ -130,14 +170,16 @@
 
     copies = []
     for i, (buf, (g, f, start)) in enumerate(zip(bufs, order)):
-        place = s_ref.at[g * n_row + f, pl.ds(start, buf.shape[0])]
-        copies.append(pltpu.make_async_copy(buf, place, sems.at[i]))
+        target = s_ref.at[g * n_row + f, pl.ds(start, buf.shape[0])]
+        copies.append(pltpu.make_async_copy(buf, target, sems.at[i]))
         copies[-1].start()
-    for p in range(n_col * n_row):
-        for b in range(per_piece):
-            own = zt_ref[p, :, b * orb : (b + 1) * orb]
-            z[p * per_piece + b] = own
-            now[p * per_piece + b] = own.astype(jnp.float32)
+    for g in range(n_col):
+        for f in range(n_row):
+            for b in range(per_piece):
+                u = (across_ref[g] * n_row + down_ref[f]) * per_piece + b
+                own = zt_ref[place(g, f), :, b * orb : (b + 1) * orb]
+                z[u] = own
+                now[u] = own.astype(jnp.float32)
     clear([prev])
     for copy, (g, f, start) in zip(copies, order):
         copy.wait()
@@ -151,7 +193,7 @@
         clear(scattered)
 
         def block_row(t, carry):
-            multiply(t, groups, across_ref, down_ref, ids_ref, z, straight, scattered)
+            multiply(t, groups, across_ref, ids_ref, z, straight, scattered)
             return carry
 
         lax.fori_loop(0, tile_rows, block_row, 0)
@@ -185,11 +227,11 @@
     across = lax.axis_index("col") ^ jnp.arange(n_col, dtype=jnp.int32)
     down = lax.axis_index("row") ^ jnp.arange(n_row, dtype=jnp.int32)
 
-    def send(buf, flip_col, flip_row):
+    def send(buf, flip_col, flip_row, from_rows=range(n_row)):
         pairs = [
             (c * n_row + r, (c ^ flip_col) * n_row + (r ^ flip_row))
             for c in range(n_col)
-            for r in range(n_row)
+            for r in from_rows
         ]
         return lax.ppermute(buf, LANES, pairs)
 
@@ -197,30 +239,55 @@
         return [send(buf, 1, 0) for buf in bufs]
 
     own = blocks[0, 0]
-    far = send(own, 0, 3)
     near = send(own, 0, 1)
+    inner = send(own, 0, 3, (1, 2))
     over_own = send(own, 2, 0)
 
+    peers = [
+        (across[core + 2 * y] * n_row + down[one ^ 3 * three])
+        for core in range(2)
+        for y in range(2)
+        for one in range(2)
+        for three in range(2)
+    ]
+    own_ids = jnp.pad(cols[0, 0], (0, orb - slots)).astype(vectors.dtype)
+    keep, go = pl.pallas_call(
+        split_kernel,
+        out_shape=[jax.ShapeDtypeStruct((n_dev // 2, share, rows + orb), vectors.dtype)] * 2,
+        in_specs=smem() + vmem(2),
+        out_specs=vmem(2),
+        scratch_shapes=[pltpu.VMEM((n_dev, share, rows), vectors.dtype)],
+        compiler_params=pltpu.CompilerParams(vmem_limit_bytes=4 * 2**20),
+    )(jnp.stack(peers), vectors, jnp.broadcast_to(own_ids, (share, orb)))
+    parts = jnp.stack([keep, send(go, 1, 0)])
+
+    def swap(parts, flip_col, flip_row, *others):
+        count = parts.shape[1] // 2
+        go = parts[:, count:]
+        go = after(go, *others) if others else go
+        return jnp.concatenate([parts[:, :count], send(go, flip_col, flip_row)])
+
+    parts = swap(parts, 2, 0)
+
     near = after(near, over_own)
+    outer = send(after(own, near), 0, 3, (0, 3))
     over_near = send(near, 2, 0)
+    parts = swap(parts, 0, 1, near)
     mates = to_mate(own, near, over_own)
-    far = after(after(far, rank=1), over_near, *mates[1:])
+    inside = (lax.axis_index("row") == 1) | (lax.axis_index("row") == 2)
+    far = pick(inside.astype(jnp.int32)[None], inner, outer, over_near, *mates)
     over_far = send(far, 2, 0)
     last = send(far, 0, 1)
-
+    parts = swap(parts, 0, 3, far)[:, 0]
     mates += to_mate(far, over_near)
-    last = after(last, over_far, mates[0], *mates[3:])
+    last = after(last, over_far, *mates[3:])
     over_last = send(last[:half], 2, 0)
     side_last = send(over_far[half:], 0, 1)
     mates += to_mate(last, over_far, over_last, side_last)
 
-    turned = vectors.T.reshape(n_dev, share, rows)
-    own_ids = jnp.pad(cols[0, 0].astype(vectors.dtype), (0, rows - slots))
-    own_ids = jnp.broadcast_to(own_ids, (n_dev, share, rows))
-    payload = after(jnp.concatenate([turned, own_ids], axis=1), last)
-    both = lax.all_to_all(payload, LANES, split_axis=0, concat_axis=0, tiled=True)
-    local = both[:, share, :slots].astype(jnp.int32)
-    at_row = (jnp.arange(n_dev, dtype=jnp.int32) % n_row)[:, None]
+    local = parts[:, 0, rows : rows + slots].astype(jnp.int32)
+    at_row = {place(g, f): down[f] for g in range(n_col) for f in range(n_row)}
+    at_row = jnp.stack([at_row[k] for k in range(n_dev)])[:, None]
     ids = (local // per_piece * n_row + at_row) * per_piece + local % per_piece
 
     bufs = [own, near, over_own, far, over_near, last, over_far, over_last, side_last]
@@ -239,7 +306,7 @@
             pltpu.SemaphoreType.DMA((len(bufs),)),
         ],
         compiler_params=pltpu.CompilerParams(vmem_limit_bytes=32 * 2**20),
-    )(across, down, ids, both[:, :share], *bufs)
+    )(across, down, ids, parts, *bufs)
     back = lax.all_to_all(done, LANES, split_axis=0, concat_axis=0, tiled=True)
     outs = jnp.transpose(back, (1, 3, 0, 2)).reshape(2, rows, width).astype(jnp.float32)
     return outs[0], outs[1]

time: 112 us -> 117 us (1.045)
  waiting for transfers between devices: 40.9 us -> 24.4 us
  local copies, waits for them, and re-layouts: 7.59 us -> 21 us
  between operations: 0.78 us -> 13.2 us
  starting transfers between devices: 27.3 us -> 20.5 us
  Pallas kernels: 18.5 us -> 20 us
  blocking collectives: 14.5 us -> 15.7 us
    ppermute x17 -> x22, waiting for transfers between devices: 40.9 us -> 24.4 us  [send(): return lax.ppermute(buf, LANES, pairs)]
    all_to_all x1 -> x0, starting transfers between devices: 13 us -> none  [gather_plan(): lax.all_to_all(payload, LANES, split_axis=0, concat_axis=0, tiled=True)]
    another operation x0 -> x2, local copies, waits for them, and re-layouts: none -> 8.7 us  [the longest x1 8.59 us: gather_plan(): at_row = jnp.stack([at_row[k] for k in range(n_dev)])[:, None]]
    ppermute x17 -> x22, starting transfers between devices: 14.2 us -> 20.5 us  [send(): return lax.ppermute(buf, LANES, pairs)]
    unnamed x14 -> x25, local copies, waits for them, and re-layouts: 5.08 us -> 9.53 us
    pallas_call x0 -> x2, Pallas kernels: none -> 2.05 us  [the longest x1 1.42 us: pick(): pl.pallas_call(pick_kernel, out_shape=jax.ShapeDtypeStruct(one.shape, one...]
    all_to_all x1, blocking collectives: 14.5 us -> 15.7 us  [gather_plan(): back = lax.all_to_all(done, LANES, split_axis=0, concat_axis=0, tiled=True)]
  transfers between devices with their start and end apart: 18 -> 22, of which waited for: 6 -> 5; matrix products, arithmetic and copies ran while one was open for 4% -> 12% of each run, Pallas kernels for 0% -> 2%
where the time goes in v9:
time: 117 us
  waiting for transfers between devices  24.4 us (21%)
  local copies, waits for them, and re-layouts  21 us (18%)
  starting transfers between devices  20.5 us (18%)
  Pallas kernels  20 us (17%)
  blocking collectives  15.7 us (13%)
  between operations  13.2 us (11%)
  other arithmetic  1.83 us (2%)
    ppermute x22, waiting for transfers between devices, send(): return lax.ppermute(buf, LANES, pairs)  24.4 us
    ppermute x22, starting transfers between devices, send(): return lax.ppermute(buf, LANES, pairs)  20.5 us
    pallas_call x1, Pallas kernels, gather_plan(): pl.pallas_call(functools.partial(filter_kernel, order, n_col, n_row), out...  17.9 us
    all_to_all x1, blocking collectives, gather_plan(): back = lax.all_to_all(done, LANES, split_axis=0, concat_axis=0, tiled=True)  15.7 us
    unnamed x25, local copies, waits for them, and re-layouts  9.53 us
    another operation x1, local copies, waits for them, and re-layouts, gather_plan(): at_row = jnp.stack([at_row[k] for k in range(n_dev)])[:, None]  8.59 us
  transfers between devices with their start and end apart: 22, of which 5 were waited for; matrix products, arithmetic and copies ran while one was open for 12% of the time, Pallas kernels for 2%

profile of v9, /device:TPU:0, one launch (start us, length us, event | category | flops | bytes accessed | tf_op | source)
XLA Modules:
  0.0 116.6 jit_solution(9844813843900085856)
XLA Ops:
  0.6 3.0 %collective-permute-start.3 = (bf16[16,128,128]{2,1,0:T(8,128)(2,1)}, bf16[16,128,128]{2,1,0:T(8,128)(2,1)S(1)}, u32[]{:S(2)}, u32[]{:S(2)}) collective-permute-start(bf16[16,128,128]{2,1,0:T(8,128)(2,1)} %bitcast.17), channel_id=1, source_target_pairs={{0,8},{1,9},{2,10},{3,11},{4,12},{5,13},{6,14},{7,15},{8,0},{9,1},... | collective-permute-start | bytes 1572872 | tf_op jit(solution)/shard_map/ppermute | solution.py:236
  3.7 1.6 %collective-permute-start.2 = (bf16[16,128,128]{2,1,0:T(8,128)(2,1)}, bf16[16,128,128]{2,1,0:T(8,128)(2,1)S(1)}, u32[]{:S(2)}, u32[]{:S(2)}) collective-permute-start(bf16[16,128,128]{2,1,0:T(8,128)(2,1)} %bitcast.18), channel_id=1, source_target_pairs={{0,1},{1,0},{2,3},{3,2},{4,5},{5,4},{6,7},{7,6},{8,9},{9,8},{10,11... | collective-permute-start | bytes 1572872 | tf_op jit(solution)/shard_map/ppermute | solution.py:236
  5.2 1.5 %collective-permute-start.5 = (bf16[16,128,128]{2,1,0:T(8,128)(2,1)}, bf16[16,128,128]{2,1,0:T(8,128)(2,1)}, u32[]{:S(2)}, u32[]{:S(2)}) collective-permute-start(bf16[16,128,128]{2,1,0:T(8,128)(2,1)} %bitcast.20), channel_id=1, source_target_pairs={{1,2},{2,1},{5,6},{6,5},{9,10},{10,9},{13,14},{14,13},{17,18},{18,... | collective-permute-start | bytes 1572872 | tf_op jit(solution)/shard_map/ppermute | solution.py:236
  6.7 1.0 copy.18.refs_0_
  7.8 8.0 %collective-permute-done.3.refs_1_.refs_2_ = bf16[16,128,128]{2,1,0:T(8,128)(2,1)S(1)} collective-permute-done((bf16[16,128,128]{2,1,0:T(8,128)(2,1)}, bf16[16,128,128]{2,1,0:T(8,128)(2,1)S(1)}, u32[]{:S(2)}, u32[]{:S(2)}) %collective-permute-start.3) | collective-permute-done | bytes 524320 | tf_op jit(solution)/shard_map/ppermute | solution.py:236
  15.8 1.5 %collective-permute-done.2.refs_0_ = bf16[16,128,128]{2,1,0:T(8,128)(2,1)S(1)} collective-permute-done((bf16[16,128,128]{2,1,0:T(8,128)(2,1)}, bf16[16,128,128]{2,1,0:T(8,128)(2,1)S(1)}, u32[]{:S(2)}, u32[]{:S(2)}) %collective-permute-start.2) | collective-permute-done | bytes 524320 | tf_op jit(solution)/shard_map/ppermute | solution.py:236
  17.6 5.8 %collective-permute-start.6 = (bf16[16,128,128]{2,1,0:T(8,128)(2,1)S(1)}, bf16[16,128,128]{2,1,0:T(8,128)(2,1)}, u32[]{:S(2)}, u32[]{:S(2)}) collective-permute-start(bf16[16,128,128]{2,1,0:T(8,128)(2,1)S(1)} %shard_map.53), channel_id=1, source_target_pairs={{0,3},{3,0},{4,7},{7,4},{8,11},{11,8},{12,15},{15,12},{16,19},{19,... | collective-permute-start | bytes 1572872 | tf_op jit(solution)/shard_map/ppermute | solution.py:236
  38.5 1.4 %shard_map.54.refs_1_.refs_3_ = bf16[16,128,128]{2,1,0:T(8,128)(2,1)S(1)} custom-call(s32[1]{0:T(128)} %bitcast.5.first_ref, bf16[16,128,128]{2,1,0:T(8,128)(2,1)} %collective-permute-done.5.one_ref, bf16[16,128,128]{2,1,0:T(8,128)(2,1)} %collective-permute-done.6.other_ref, bf16[16,128,128]{2,1,0:T(8,128)(2,1)S(1)} %collective-permute-done.7.refs_0_.refs_4_, ...), custom_call_target="tpu_custom_call" | custom-call | tf_op jit(solution)/shard_map/pallas_call | solution.py:113
  40.7 1.5 %collective-permute-start.13 = (bf16[16,128,128]{2,1,0:T(8,128)(2,1)S(1)}, bf16[16,128,128]{2,1,0:T(8,128)(2,1)S(1)}, u32[]{:S(2)}, u32[]{:S(2)}) collective-permute-start(bf16[16,128,128]{2,1,0:T(8,128)(2,1)S(1)} %shard_map.54.refs_1_.refs_3_), channel_id=1, source_target_pairs={{0,8},{1,9},{2,10},{3,11},{4,12},{5,13},{6,14},{7,15},{8,0},{9,1},... | collective-permute-start | bytes 1572872 | tf_op jit(solution)/shard_map/ppermute | solution.py:236
  43.4 13.3 %collective-permute-done.1 = bf16[2,4,16,384]{3,2,0,1:T(8,128)(2,1)S(1)} collective-permute-done((bf16[2,4,16,384]{3,2,0,1:T(8,128)(2,1)S(1)}, bf16[2,4,16,384]{3,2,0,1:T(8,128)(2,1)S(1)}, u32[]{:S(2)}, u32[]{:S(2)}) %collective-permute-start.1) | collective-permute-done | bytes 98336 | tf_op jit(solution)/shard_map/ppermute | solution.py:236
  57.6 2.0 %collective-permute-start.17 = (bf16[8,128,128]{2,1,0:T(8,128)(2,1)}, bf16[8,128,128]{2,1,0:T(8,128)(2,1)S(1)}, u32[]{:S(2)}, u32[]{:S(2)}) collective-permute-start(bf16[8,128,128]{2,1,0:T(8,128)(2,1)} %slice.130), channel_id=1, source_target_pairs={{0,1},{1,0},{2,3},{3,2},{4,5},{5,4},{6,7},{7,6},{8,9},{9,8},{10,11... | collective-permute-start | bytes 786440 | tf_op jit(solution)/shard_map/ppermute | solution.py:236
  61.1 1.5 %collective-permute-start.16 = (bf16[8,128,128]{2,1,0:T(8,128)(2,1)}, bf16[8,128,128]{2,1,0:T(8,128)(2,1)}, u32[]{:S(2)}, u32[]{:S(2)}) collective-permute-start(bf16[8,128,128]{2,1,0:T(8,128)(2,1)} %slice.129), channel_id=1, source_target_pairs={{0,8},{1,9},{2,10},{3,11},{4,12},{5,13},{6,14},{7,15},{8,0},{9,1},... | collective-permute-start | bytes 786440 | tf_op jit(solution)/shard_map/ppermute | solution.py:236
  63.6 8.6 %stack.15 = s32[16]{0:T(128)S(1)} concatenate(s32[1]{0:T(128)} %get-tuple-element.23, s32[1]{0:T(128)} %get-tuple-element.23, s32[1]{0:T(128)} %get-tuple-element.23, s32[2]{0:T(128)S(1)} %bitcast.25, s32[1]{0:T(128)} %get-tuple-element.21, s32[1]{0:T(128)} %get-tuple-element.21, s32[1]{0:T(128)} %get-tuple-element.21, s32[1]{0:T(128)} %get-tuple-element.22, ...), dimensions={0} | concatenate | bytes 128 | tf_op jit(solution)/shard_map/stack | solution.py:290
  72.8 1.0 maximum_bitcast_fusion.zt_ref
  74.4 0.9 collective-permute-done.21.refs_17_
  76.0 1.0 copy-done.1
  77.0 1.0 copy-done.2
  78.0 1.0 copy-done.4
  79.1 1.0 copy-done.6
  80.1 1.0 copy-done.8
  81.2 17.9 %shard_map.57 = bf16[16,2,16,256]{3,2,1,0:T(8,128)(2,1)S(1)} custom-call(s32[4]{0:T(128)S(1)} %get-tuple-element.25.across_ref, s32[4]{0:T(128)S(1)} %get-tuple-element.24.down_ref, s32[16,16]{1,0:T(8,128)S(1)} %fusion.7.ids_ref, bf16[16,16,384]{2,1,0:T(8,128)(2,1)S(1)} %maximum_bitcast_fusion.zt_ref, bf16[16,128,128]{2,1,0:T(8,128)(2,1)S(1)} %bitcast.22, ...), custom_call_target="tpu_custom_call" | custom-call | tf_op jit(solution)/shard_map/pallas_call | solution.py:297
  99.1 15.7 %all_to_all.5 = bf16[16,2,16,256]{3,2,1,0:T(8,128)(2,1)S(1)} all-to-all(bf16[16,2,16,256]{3,2,1,0:T(8,128)(2,1)S(1)} %shard_map.57), channel_id=1, replica_groups=mesh['dom'=2,'col'=4,'row'=4] {'col','row'}, dimensions={0} | all-to-all | bytes 524288 | tf_op jit(solution)/shard_map/all_to_all | solution.py:310
  114.9 0.8 copy.15
  115.8 0.8 copy.14
  (74 shorter events, 10.2 us)
Async XLA Ops:
  0.6 15.2 %collective-permute-start.3 = (bf16[16,128,128]{2,1,0:T(8,128)(2,1)}, bf16[16,128,128]{2,1,0:T(8,128)(2,1)S(1)}, u32[]{:S(2)}, u32[]{:S(2)}) collective-permute-start(bf16[16,128,128]{2,1,0:T(8,128)(2,1)} %bitcast.17), channel_id=1, source_target_pairs={{0,8},{1,9},{2,10},{3,11},{4,12},{5,13},{6,14},{7,15},{8,0},{9,1},... | collective-permute-start | bytes 1572872 | tf_op jit(solution)/shard_map/ppermute | solution.py:236
  3.7 13.6 %collective-permute-start.2 = (bf16[16,128,128]{2,1,0:T(8,128)(2,1)}, bf16[16,128,128]{2,1,0:T(8,128)(2,1)S(1)}, u32[]{:S(2)}, u32[]{:S(2)}) collective-permute-start(bf16[16,128,128]{2,1,0:T(8,128)(2,1)} %bitcast.18), channel_id=1, source_target_pairs={{0,1},{1,0},{2,3},{3,2},{4,5},{5,4},{6,7},{7,6},{8,9},{9,8},{10,11... | collective-permute-start | bytes 1572872 | tf_op jit(solution)/shard_map/ppermute | solution.py:236
  5.2 18.2 %collective-permute-start.8 = (bf16[16,128,128]{2,1,0:T(8,128)(2,1)}, bf16[16,128,128]{2,1,0:T(8,128)(2,1)S(1)}, u32[]{:S(2)}, u32[]{:S(2)}) collective-permute-start(bf16[16,128,128]{2,1,0:T(8,128)(2,1)} %bitcast.19), channel_id=1, source_target_pairs={{0,4},{1,5},{2,6},{3,7},{4,0},{5,1},{6,2},{7,3},{8,12},{9,13},{10,... | collective-permute-start | bytes 1572872 | tf_op jit(solution)/shard_map/ppermute | solution.py:236
  5.2 32.6 %collective-permute-start.5 = (bf16[16,128,128]{2,1,0:T(8,128)(2,1)}, bf16[16,128,128]{2,1,0:T(8,128)(2,1)}, u32[]{:S(2)}, u32[]{:S(2)}) collective-permute-start(bf16[16,128,128]{2,1,0:T(8,128)(2,1)} %bitcast.20), channel_id=1, source_target_pairs={{1,2},{2,1},{5,6},{6,5},{9,10},{10,9},{13,14},{14,13},{17,18},{18,... | collective-permute-start | bytes 1572872 | tf_op jit(solution)/shard_map/ppermute | solution.py:236
  17.3 21.2 %collective-permute-start.9 = (bf16[16,128,128]{2,1,0:T(8,128)(2,1)S(1)}, bf16[16,128,128]{2,1,0:T(8,128)(2,1)S(1)}, u32[]{:S(2)}, u32[]{:S(2)}) collective-permute-start(bf16[16,128,128]{2,1,0:T(8,128)(2,1)S(1)} %shard_map.51.refs_1_), channel_id=1, source_target_pairs={{0,4},{1,5},{2,6},{3,7},{4,0},{5,1},{6,2},{7,3},{8,12},{9,13},{10,... | collective-permute-start | bytes 1572872 | tf_op jit(solution)/shard_map/ppermute | solution.py:236
  17.3 21.2 %collective-permute-start.7 = (bf16[16,128,128]{2,1,0:T(8,128)(2,1)S(1)}, bf16[16,128,128]{2,1,0:T(8,128)(2,1)S(1)}, u32[]{:S(2)}, u32[]{:S(2)}) collective-permute-start(bf16[16,128,128]{2,1,0:T(8,128)(2,1)S(1)} %shard_map.51.refs_1_), channel_id=1, source_target_pairs={{0,8},{1,9},{2,10},{3,11},{4,12},{5,13},{6,14},{7,15},{8,0},{9,1},... | collective-permute-start | bytes 1572872 | tf_op jit(solution)/shard_map/ppermute | solution.py:236
  17.6 19.6 %copy-start.9 = (bf16[256,256]{1,0:T(8,128)(2,1)S(1)}, bf16[256,256]{1,0:T(8,128)(2,1)}, u32[]{:S(2)}) copy-start(bf16[256,256]{1,0:T(8,128)(2,1)} %vectors_ref.1) | copy-start | bytes 393220
  17.6 20.8 %collective-permute-start.6 = (bf16[16,128,128]{2,1,0:T(8,128)(2,1)S(1)}, bf16[16,128,128]{2,1,0:T(8,128)(2,1)}, u32[]{:S(2)}, u32[]{:S(2)}) collective-permute-start(bf16[16,128,128]{2,1,0:T(8,128)(2,1)S(1)} %shard_map.53), channel_id=1, source_target_pairs={{0,3},{3,0},{4,7},{7,4},{8,11},{11,8},{12,15},{15,12},{16,19},{19,... | collective-permute-start | bytes 1572872 | tf_op jit(solution)/shard_map/ppermute | solution.py:236
  23.4 15.0 %collective-permute-start.10 = (bf16[16,128,128]{2,1,0:T(8,128)(2,1)S(1)}, bf16[16,128,128]{2,1,0:T(8,128)(2,1)}, u32[]{:S(2)}, u32[]{:S(2)}) collective-permute-start(bf16[16,128,128]{2,1,0:T(8,128)(2,1)S(1)} %collective-permute-done.3.refs_1_.refs_2_), channel_id=1, source_target_pairs={{0,4},{1,5},{2,6},{3,7},{4,0},{5,1},{6,2},{7,3},{8,12},{9,13},{10,... | collective-permute-start | bytes 1572872 | tf_op jit(solution)/shard_map/ppermute | solution.py:236
  37.9 4.9 %collective-permute-start = (bf16[8,16,384]{2,1,0:T(8,128)(2,1)S(1)}, bf16[8,16,384]{2,1,0:T(8,128)(2,1)S(1)}, u32[]{:S(2)}, u32[]{:S(2)}) collective-permute-start(bf16[8,16,384]{2,1,0:T(8,128)(2,1)S(1)} %get-tuple-element.5), channel_id=1, source_target_pairs={{0,4},{1,5},{2,6},{3,7},{4,0},{5,1},{6,2},{7,3},{8,12},{9,13},{10,... | collective-permute-start | bytes 294920 | tf_op jit(solution)/shard_map/ppermute | solution.py:236
  38.5 1.5 %copy-start.5 = (bf16[16,128,128]{2,1,0:T(8,128)(2,1)}, bf16[16,128,128]{2,1,0:T(8,128)(2,1)S(1)}, u32[]{:S(2)}) copy-start(bf16[16,128,128]{2,1,0:T(8,128)(2,1)S(1)} %collective-permute-done.9.refs_2_.refs_10_) | copy-start | bytes 1572868
  40.7 16.1 %collective-permute-start.13 = (bf16[16,128,128]{2,1,0:T(8,128)(2,1)S(1)}, bf16[16,128,128]{2,1,0:T(8,128)(2,1)S(1)}, u32[]{:S(2)}, u32[]{:S(2)}) collective-permute-start(bf16[16,128,128]{2,1,0:T(8,128)(2,1)S(1)} %shard_map.54.refs_1_.refs_3_), channel_id=1, source_target_pairs={{0,8},{1,9},{2,10},{3,11},{4,12},{5,13},{6,14},{7,15},{8,0},{9,1},... | collective-permute-start | bytes 1572872 | tf_op jit(solution)/shard_map/ppermute | solution.py:236
  42.3 17.4 %collective-permute-start.14 = (bf16[16,128,128]{2,1,0:T(8,128)(2,1)S(1)}, bf16[16,128,128]{2,1,0:T(8,128)(2,1)S(1)}, u32[]{:S(2)}, u32[]{:S(2)}) collective-permute-start(bf16[16,128,128]{2,1,0:T(8,128)(2,1)S(1)} %shard_map.54.refs_1_.refs_3_), channel_id=1, source_target_pairs={{0,4},{1,5},{2,6},{3,7},{4,0},{5,1},{6,2},{7,3},{8,12},{9,13},{10,... | collective-permute-start | bytes 1572872 | tf_op jit(solution)/shard_map/ppermute | solution.py:236
  42.3 17.4 %collective-permute-start.12 = (bf16[16,128,128]{2,1,0:T(8,128)(2,1)S(1)}, bf16[16,128,128]{2,1,0:T(8,128)(2,1)S(1)}, u32[]{:S(2)}, u32[]{:S(2)}) collective-permute-start(bf16[16,128,128]{2,1,0:T(8,128)(2,1)S(1)} %shard_map.54.refs_1_.refs_3_), channel_id=1, source_target_pairs={{0,1},{1,0},{2,3},{3,2},{4,5},{5,4},{6,7},{7,6},{8,9},{9,8},{10,11... | collective-permute-start | bytes 1572872 | tf_op jit(solution)/shard_map/ppermute | solution.py:236
  42.3 17.4 %collective-permute-start.15 = (bf16[16,128,128]{2,1,0:T(8,128)(2,1)}, bf16[16,128,128]{2,1,0:T(8,128)(2,1)S(1)}, u32[]{:S(2)}, u32[]{:S(2)}) collective-permute-start(bf16[16,128,128]{2,1,0:T(8,128)(2,1)} %copy-done.7), channel_id=1, source_target_pairs={{0,4},{1,5},{2,6},{3,7},{4,0},{5,1},{6,2},{7,3},{8,12},{9,13},{10,... | collective-permute-start | bytes 1572872 | tf_op jit(solution)/shard_map/ppermute | solution.py:236
  42.8 13.9 %collective-permute-start.1 = (bf16[2,4,16,384]{3,2,0,1:T(8,128)(2,1)S(1)}, bf16[2,4,16,384]{3,2,0,1:T(8,128)(2,1)S(1)}, u32[]{:S(2)}, u32[]{:S(2)}) collective-permute-start(bf16[2,4,16,384]{3,2,0,1:T(8,128)(2,1)S(1)} %get-tuple-element.15), channel_id=1, source_target_pairs={{0,8},{1,9},{2,10},{3,11},{4,12},{5,13},{6,14},{7,15},{8,0},{9,1},... | collective-permute-start | bytes 294920 | tf_op jit(solution)/shard_map/ppermute | solution.py:236
  56.8 5.9 %collective-permute-start.4 = (bf16[4,2,16,384]{3,2,0,1:T(8,128)(2,1)S(1)}, bf16[4,2,16,384]{3,2,0,1:T(8,128)(2,1)S(1)}, u32[]{:S(2)}, u32[]{:S(2)}) collective-permute-start(bf16[4,2,16,384]{3,2,0,1:T(8,128)(2,1)S(1)} %copy.11), channel_id=1, source_target_pairs={{0,1},{1,0},{2,3},{3,2},{4,5},{5,4},{6,7},{7,6},{8,9},{9,8},{10,11... | collective-permute-start | bytes 294920 | tf_op jit(solution)/shard_map/ppermute | solution.py:236
  57.6 16.1 %collective-permute-start.17 = (bf16[8,128,128]{2,1,0:T(8,128)(2,1)}, bf16[8,128,128]{2,1,0:T(8,128)(2,1)S(1)}, u32[]{:S(2)}, u32[]{:S(2)}) collective-permute-start(bf16[8,128,128]{2,1,0:T(8,128)(2,1)} %slice.130), channel_id=1, source_target_pairs={{0,1},{1,0},{2,3},{3,2},{4,5},{5,4},{6,7},{7,6},{8,9},{9,8},{10,11... | collective-permute-start | bytes 786440 | tf_op jit(solution)/shard_map/ppermute | solution.py:236
  61.1 12.8 %collective-permute-start.16 = (bf16[8,128,128]{2,1,0:T(8,128)(2,1)}, bf16[8,128,128]{2,1,0:T(8,128)(2,1)}, u32[]{:S(2)}, u32[]{:S(2)}) collective-permute-start(bf16[8,128,128]{2,1,0:T(8,128)(2,1)} %slice.129), channel_id=1, source_target_pairs={{0,8},{1,9},{2,10},{3,11},{4,12},{5,13},{6,14},{7,15},{8,0},{9,1},... | collective-permute-start | bytes 786440 | tf_op jit(solution)/shard_map/ppermute | solution.py:236
  63.3 9.4 %collective-permute-start.11 = (bf16[8,1,16,384]{3,2,0,1:T(8,128)(2,1)S(1)}, bf16[8,1,16,384]{3,2,0,1:T(8,128)(2,1)}, u32[]{:S(2)}, u32[]{:S(2)}) collective-permute-start(bf16[8,1,16,384]{3,2,0,1:T(8,128)(2,1)S(1)} %bitcast.23), channel_id=1, source_target_pairs={{0,3},{1,2},{2,1},{3,0},{4,7},{5,6},{6,5},{7,4},{8,11},{9,10},{10,... | collective-permute-start | bytes 294920 | tf_op jit(solution)/shard_map/ppermute | solution.py:236
  72.2 3.8 %collective-permute-start.18 = (bf16[16,128,128]{2,1,0:T(8,128)(2,1)S(1)}, bf16[16,128,128]{2,1,0:T(8,128)(2,1)S(1)}, u32[]{:S(2)}, u32[]{:S(2)}) collective-permute-start(bf16[16,128,128]{2,1,0:T(8,128)(2,1)S(1)} %shard_map.56.refs_5_), channel_id=1, source_target_pairs={{0,4},{1,5},{2,6},{3,7},{4,0},{5,1},{6,2},{7,3},{8,12},{9,13},{10,... | collective-permute-start | bytes 1572872 | tf_op jit(solution)/shard_map/ppermute | solution.py:236
  72.3 3.7 %collective-permute-start.19 = (bf16[16,128,128]{2,1,0:T(8,128)(2,1)S(1)}, bf16[16,128,128]{2,1,0:T(8,128)(2,1)S(1)}, u32[]{:S(2)}, u32[]{:S(2)}) collective-permute-start(bf16[16,128,128]{2,1,0:T(8,128)(2,1)S(1)} %collective-permute-done.13.refs_1_.refs_6_), channel_id=1, source_target_pairs={{0,4},{1,5},{2,6},{3,7},{4,0},{5,1},{6,2},{7,3},{8,12},{9,13},{10,... | collective-permute-start | bytes 1572872 | tf_op jit(solution)/shard_map/ppermute | solution.py:236
  73.8 1.6 %collective-permute-start.21 = (bf16[8,128,128]{2,1,0:T(8,128)(2,1)S(1)}, bf16[8,128,128]{2,1,0:T(8,128)(2,1)S(1)}, u32[]{:S(2)}, u32[]{:S(2)}) collective-permute-start(bf16[8,128,128]{2,1,0:T(8,128)(2,1)S(1)} %collective-permute-done.17.refs_8_), channel_id=1, source_target_pairs={{0,4},{1,5},{2,6},{3,7},{4,0},{5,1},{6,2},{7,3},{8,12},{9,13},{10,... | collective-permute-start | bytes 786440 | tf_op jit(solution)/shard_map/ppermute | solution.py:236
  73.9 2.0 %collective-permute-start.20 = (bf16[8,128,128]{2,1,0:T(8,128)(2,1)}, bf16[8,128,128]{2,1,0:T(8,128)(2,1)S(1)}, u32[]{:S(2)}, u32[]{:S(2)}) collective-permute-start(bf16[8,128,128]{2,1,0:T(8,128)(2,1)} %collective-permute-done.16.refs_7_), channel_id=1, source_target_pairs={{0,4},{1,5},{2,6},{3,7},{4,0},{5,1},{6,2},{7,3},{8,12},{9,13},{10,... | collective-permute-start | bytes 786440 | tf_op jit(solution)/shard_map/ppermute | solution.py:236
  (9 other events, 9.0 us)

commit v10 on v9

--- a/solution.py
+++ b/solution.py
@@ -2,6 +2,7 @@
 
 import jax
 import jax.numpy as jnp
+import numpy
 from jax import lax
 from jax.experimental import pallas as pl
 from jax.experimental.pallas import tpu as pltpu
@@ -93,6 +94,24 @@
     )(value, *others)
 
 
+def copy_kernel(value_ref, *refs):
+    out_ref, sem = refs[-2:]
+    copy = pltpu.make_async_copy(value_ref, out_ref, sem)
+    copy.start()
+    copy.wait()
+
+
+def copy_after(value, *others):
+    return pl.pallas_call(
+        copy_kernel,
+        out_shape=jax.ShapeDtypeStruct(value.shape, value.dtype),
+        in_specs=anywhere(1 + len(others)),
+        out_specs=anywhere()[0],
+        scratch_shapes=[pltpu.SemaphoreType.DMA(())],
+        compiler_params=pltpu.CompilerParams(vmem_limit_bytes=2**20),
+    )(value, *others)
+
+
 def pick_kernel(first_ref, one_ref, other_ref, *refs):
     out_ref, sem = refs[-2:]
 
@@ -158,19 +177,53 @@
         ref[...] = jnp.zeros_like(ref)
 
 
-def filter_kernel(order, n_col, n_row, across_ref, down_ref, ids_ref, zt_ref, *refs):
+def turn(s_ref, st_ref, i, start, count):
+    def four(k, carry):
+        for m in range(4):
+            st_ref[i, start + 4 * k + m] = s_ref[i, start + 4 * k + m].T
+        return carry
+
+    lax.fori_loop(0, count // 4, four, 0)
+
+
+def load_kernel(count, *refs):
+    bufs, (s_ref, st_ref, sems) = refs[:count], refs[count:]
+    copies = [pltpu.make_async_copy(buf, s_ref.at[i], sems.at[i]) for i, buf in enumerate(bufs)]
+    for copy in copies:
+        copy.start()
+    for i, copy in enumerate(copies):
+        copy.wait()
+        turn(s_ref, st_ref, i, 0, s_ref.shape[1])
+
+
+def load(bufs):
+    out = jax.ShapeDtypeStruct((len(bufs), *bufs[0].shape), bufs[0].dtype)
+    size = len(bufs) * bufs[0].size
+    return pl.pallas_call(
+        functools.partial(load_kernel, len(bufs)),
+        out_shape=[out, out],
+        in_specs=anywhere(len(bufs)),
+        out_specs=vmem(2),
+        scratch_shapes=[pltpu.SemaphoreType.DMA((len(bufs),))],
+        compiler_params=pltpu.CompilerParams(vmem_limit_bytes=2**20),
+        cost_estimate=pl.CostEstimate(flops=0, bytes_accessed=6 * size, transcendentals=0),
+    )(*bufs)
+
+
+def filter_kernel(early, late, n_col, n_row, across_ref, down_ref, ids_ref, zt_ref, se_ref, ste_ref, *refs):
     bufs, (out_ref, s_ref, st_ref, z, now, prev, straight, *scattered, sems) = (
-        refs[: len(order)],
-        refs[len(order) :],
+        refs[: len(late)],
+        refs[len(late) :],
     )
     n_blocks, share, orb = z.shape
     slots = s_ref.shape[1]
     per_piece = n_blocks // (n_col * n_row)
     tile_rows = slots // PER_ROW
+    rest = sorted({(g, f) for g, f, _ in late})
 
     copies = []
-    for i, (buf, (g, f, start)) in enumerate(zip(bufs, order)):
-        target = s_ref.at[g * n_row + f, pl.ds(start, buf.shape[0])]
+    for i, (buf, (g, f, start)) in enumerate(zip(bufs, late)):
+        target = s_ref.at[rest.index((g, f)), pl.ds(start, buf.shape[0])]
         copies.append(pltpu.make_async_copy(buf, target, sems.at[i]))
         copies[-1].start()
     for g in range(n_col):
@@ -181,13 +234,13 @@
                 z[u] = own
                 now[u] = own.astype(jnp.float32)
     clear([prev])
-    for copy, (g, f, start) in zip(copies, order):
+    for copy, buf, (g, f, start) in zip(copies, bufs, late):
         copy.wait()
-        tile = g * n_row + f
-        for slot in range(start, start + copy.src_ref.shape[0]):
-            st_ref[tile, slot] = s_ref[tile, slot].T
-
-    groups = [[(f, s_ref, st_ref, g * n_row + f) for f in range(n_row)] for g in range(n_col)]
+        turn(s_ref, st_ref, rest.index((g, f)), start, buf.shape[0])
+
+    tiles = {at: (se_ref, ste_ref, i) for i, at in enumerate(early)}
+    tiles.update({at: (s_ref, st_ref, i) for i, at in enumerate(rest)})
+    groups = [[(f, *tiles[g, f]) for f in range(n_row)] for g in range(n_col)]
 
     def one_step(step, carry):
         clear(scattered)
@@ -243,13 +296,9 @@
     inner = send(own, 0, 3, (1, 2))
     over_own = send(own, 2, 0)
 
-    peers = [
-        (across[core + 2 * y] * n_row + down[one ^ 3 * three])
-        for core in range(2)
-        for y in range(2)
-        for one in range(2)
-        for three in range(2)
-    ]
+    g_of = numpy.array([core + 2 * y for core in range(2) for y in range(2) for _ in range(4)])
+    f_of = numpy.array([one ^ 3 * three for _ in range(4) for one in range(2) for three in range(2)])
+    peers = (lax.axis_index("col") ^ g_of) * n_row + (lax.axis_index("row") ^ f_of)
     own_ids = jnp.pad(cols[0, 0], (0, orb - slots)).astype(vectors.dtype)
     keep, go = pl.pallas_call(
         split_kernel,
@@ -258,55 +307,56 @@
         out_specs=vmem(2),
         scratch_shapes=[pltpu.VMEM((n_dev, share, rows), vectors.dtype)],
         compiler_params=pltpu.CompilerParams(vmem_limit_bytes=4 * 2**20),
-    )(jnp.stack(peers), vectors, jnp.broadcast_to(own_ids, (share, orb)))
+    )(peers.astype(jnp.int32), vectors, jnp.broadcast_to(own_ids, (share, orb)))
     parts = jnp.stack([keep, send(go, 1, 0)])
 
-    def swap(parts, flip_col, flip_row, *others):
+    def swap(parts, flip_col, flip_row):
         count = parts.shape[1] // 2
-        go = parts[:, count:]
-        go = after(go, *others) if others else go
-        return jnp.concatenate([parts[:, :count], send(go, flip_col, flip_row)])
+        return jnp.concatenate([parts[:, :count], send(parts[:, count:], flip_col, flip_row)])
 
     parts = swap(parts, 2, 0)
 
-    near = after(near, over_own)
-    outer = send(after(own, near), 0, 3, (0, 3))
+    near = after(near, over_own, parts)
+    outer = send(copy_after(own, near), 0, 3, (0, 3))
     over_near = send(near, 2, 0)
-    parts = swap(parts, 0, 1, near)
+    parts = swap(parts, 0, 1)
     mates = to_mate(own, near, over_own)
     inside = (lax.axis_index("row") == 1) | (lax.axis_index("row") == 2)
-    far = pick(inside.astype(jnp.int32)[None], inner, outer, over_near, *mates)
+    far = pick(inside.astype(jnp.int32)[None], inner, outer, over_near, parts, *mates)
     over_far = send(far, 2, 0)
     last = send(far, 0, 1)
-    parts = swap(parts, 0, 3, far)[:, 0]
+    parts = swap(parts, 0, 3)[:, 0]
     mates += to_mate(far, over_near)
-    last = after(last, over_far, *mates[3:])
+    last = after(last, over_far, parts, *mates[3:])
     over_last = send(last[:half], 2, 0)
     side_last = send(over_far[half:], 0, 1)
-    mates += to_mate(last, over_far, over_last, side_last)
+    mates += to_mate(last, over_far)
+    early = [(0, 0), (0, 1), (2, 0), (0, 3), (2, 1), (0, 2), (2, 3)]
+    early += [(g ^ 1, f) for g, f in early]
+    se, ste = load([own, near, over_own, far, over_near, last, over_far, *mates])
+    over_last, side_last = after(over_last, se), after(side_last, se)
+    late_bufs = [over_last, side_last, *to_mate(over_last, side_last)]
+    late = [(2, 2, 0), (2, 2, half), (3, 2, 0), (3, 2, half)]
 
     local = parts[:, 0, rows : rows + slots].astype(jnp.int32)
-    at_row = {place(g, f): down[f] for g in range(n_col) for f in range(n_row)}
-    at_row = jnp.stack([at_row[k] for k in range(n_dev)])[:, None]
+    f_at = {place(g, f): f for g in range(n_col) for f in range(n_row)}
+    f_at = numpy.array([f_at[k] for k in range(n_dev)], numpy.int32)
+    at_row = (lax.axis_index("row") ^ f_at)[:, None]
     ids = (local // per_piece * n_row + at_row) * per_piece + local % per_piece
 
-    bufs = [own, near, over_own, far, over_near, last, over_far, over_last, side_last]
-    order = [(0, 0, 0), (0, 1, 0), (2, 0, 0), (0, 3, 0), (2, 1, 0), (0, 2, 0), (2, 3, 0), (2, 2, 0), (2, 2, half)]
-    order += [(g ^ 1, f, slot) for g, f, slot in order]
-    bufs += mates
     done = pl.pallas_call(
-        functools.partial(filter_kernel, order, n_col, n_row),
+        functools.partial(filter_kernel, early, late, n_col, n_row),
         out_shape=jax.ShapeDtypeStruct((n_dev, 2, share, rows), jnp.bfloat16),
-        in_specs=smem(3) + vmem() + anywhere(len(bufs)),
+        in_specs=smem(3) + vmem(3) + anywhere(len(late)),
         out_specs=vmem()[0],
         scratch_shapes=[
-            *[pltpu.VMEM((n_dev, slots, orb, orb), blocks.dtype)] * 2,
+            *[pltpu.VMEM((n_dev - len(early), slots, orb, orb), blocks.dtype)] * 2,
             pltpu.VMEM((n_blocks, share, orb), jnp.bfloat16),
             *[pltpu.VMEM((n_blocks, share, orb), jnp.float32)] * (3 + SPLIT),
-            pltpu.SemaphoreType.DMA((len(bufs),)),
+            pltpu.SemaphoreType.DMA((len(late),)),
         ],
-        compiler_params=pltpu.CompilerParams(vmem_limit_bytes=32 * 2**20),
-    )(across, down, ids, parts, *bufs)
+        compiler_params=pltpu.CompilerParams(vmem_limit_bytes=12 * 2**20),
+    )(across, down, ids, parts, se, ste, *late_bufs)
     back = lax.all_to_all(done, LANES, split_axis=0, concat_axis=0, tiled=True)
     outs = jnp.transpose(back, (1, 3, 0, 2)).reshape(2, rows, width).astype(jnp.float32)
     return outs[0], outs[1]

time: 117 us -> 101 us (0.86)
  local copies, waits for them, and re-layouts: 21 us -> 3.75 us
  waiting for transfers between devices: 24.4 us -> 38 us
  between operations: 13.2 us -> 0.91 us
  Pallas kernels: 20 us -> 23 us
  blocking collectives: 15.7 us -> 12.9 us
    ppermute x22, waiting for transfers between devices: 24.4 us -> 38 us  [send(): return lax.ppermute(buf, LANES, pairs)]
    another operation x2 -> x0, local copies, waits for them, and re-layouts: 8.7 us -> none  [the longest x1 8.59 us: gather_plan(): at_row = jnp.stack([at_row[k] for k in range(n_dev)])[:, None]]
    unnamed x25 -> x10, local copies, waits for them, and re-layouts: 9.53 us -> 3.62 us
    pallas_call x1 -> x3, Pallas kernels: 17.9 us -> 21.3 us  [the longest x1 15 us: gather_plan(): pl.pallas_call(functools.partial(filter_kernel, early, late, n_col, n_row...]
    all_to_all x1, blocking collectives: 15.7 us -> 12.9 us  [gather_plan(): back = lax.all_to_all(done, LANES, split_axis=0, concat_axis=0, tiled=True)]
    slice x3 -> x0, local copies, waits for them, and re-layouts: 1.3 us -> none  [the longest x1 0.67 us: gather_plan(): down[one ^ 3 * three]]
  transfers between devices with their start and end apart: 22 -> 22, of which waited for: 5 -> 9; matrix products, arithmetic and copies ran while one was open for 12% -> 0% of each run, Pallas kernels for 2% -> 6%
where the time goes in v10:
time: 101 us
  waiting for transfers between devices  38 us (38%)
  Pallas kernels  23 us (23%)
  starting transfers between devices  20.5 us (20%)
  blocking collectives  12.9 us (13%)
  local copies, waits for them, and re-layouts  3.75 us (4%)
  other arithmetic  1.68 us (2%)
    ppermute x22, waiting for transfers between devices, send(): return lax.ppermute(buf, LANES, pairs)  38 us
    ppermute x22, starting transfers between devices, send(): return lax.ppermute(buf, LANES, pairs)  20.5 us
    pallas_call x1, Pallas kernels, gather_plan(): pl.pallas_call(functools.partial(filter_kernel, early, late, n_col, n_row...  15 us
    all_to_all x1, blocking collectives, gather_plan(): back = lax.all_to_all(done, LANES, split_axis=0, concat_axis=0, tiled=True)  12.9 us
    pallas_call x1, Pallas kernels, load(): pl.pallas_call(functools.partial(load_kernel, len(bufs)), out_shape=[out,...  5.53 us
    unnamed x10, local copies, waits for them, and re-layouts  3.62 us
  transfers between devices with their start and end apart: 22, of which 9 were waited for; matrix products, arithmetic and copies ran while one was open for 0% of the time, Pallas kernels for 6%

profile of v10, /device:TPU:0, one launch (start us, length us, event | category | flops | bytes accessed | tf_op | source)
XLA Modules:
  0.0 100.8 jit_solution(5354588587855087069)
XLA Ops:
  0.6 0.7 convert_bitcast_fusion.1
  2.1 0.9 copy-done.2
  4.1 2.6 %collective-permute-start.5 = (bf16[16,128,128]{2,1,0:T(8,128)(2,1)}, bf16[16,128,128]{2,1,0:T(8,128)(2,1)S(1)}, u32[]{:S(2)}, u32[]{:S(2)}) collective-permute-start(bf16[16,128,128]{2,1,0:T(8,128)(2,1)} %bitcast.13), channel_id=1, source_target_pairs={{0,8},{1,9},{2,10},{3,11},{4,12},{5,13},{6,14},{7,15},{8,0},{9,1},... | collective-permute-start | bytes 1572872 | tf_op jit(solution)/shard_map/ppermute | solution.py:289
  6.7 1.6 %collective-permute-start.4 = (bf16[16,128,128]{2,1,0:T(8,128)(2,1)}, bf16[16,128,128]{2,1,0:T(8,128)(2,1)S(1)}, u32[]{:S(2)}, u32[]{:S(2)}) collective-permute-start(bf16[16,128,128]{2,1,0:T(8,128)(2,1)} %bitcast.14), channel_id=1, source_target_pairs={{0,1},{1,0},{2,3},{3,2},{4,5},{5,4},{6,7},{7,6},{8,9},{9,8},{10,11... | collective-permute-start | bytes 1572872 | tf_op jit(solution)/shard_map/ppermute | solution.py:289
  8.9 1.5 %collective-permute-start.6 = (bf16[16,128,128]{2,1,0:T(8,128)(2,1)}, bf16[16,128,128]{2,1,0:T(8,128)(2,1)}, u32[]{:S(2)}, u32[]{:S(2)}) collective-permute-start(bf16[16,128,128]{2,1,0:T(8,128)(2,1)} %bitcast.16), channel_id=1, source_target_pairs={{1,2},{2,1},{5,6},{6,5},{9,10},{10,9},{13,14},{14,13},{17,18},{18,... | collective-permute-start | bytes 1572872 | tf_op jit(solution)/shard_map/ppermute | solution.py:289
  10.4 11.2 %collective-permute-done.1 = bf16[2,4,16,384]{3,2,0,1:T(8,128)(2,1)S(1)} collective-permute-done((bf16[2,4,16,384]{3,2,0,1:T(8,128)(2,1)S(1)}, bf16[2,4,16,384]{3,2,0,1:T(8,128)(2,1)S(1)}, u32[]{:S(2)}, u32[]{:S(2)}) %collective-permute-start.1) | collective-permute-done | bytes 98336 | tf_op jit(solution)/shard_map/ppermute | solution.py:289
  21.6 1.9 %collective-permute-start.2 = (bf16[4,2,16,384]{3,2,0,1:T(8,128)(2,1)S(1)}, bf16[4,2,16,384]{3,2,0,1:T(8,128)(2,1)S(1)}, u32[]{:S(2)}, u32[]{:S(2)}) collective-permute-start(bf16[4,2,16,384]{3,2,0,1:T(8,128)(2,1)S(1)} %get-tuple-element.16), channel_id=1, source_target_pairs={{0,1},{1,0},{2,3},{3,2},{4,5},{5,4},{6,7},{7,6},{8,9},{9,8},{10,11... | collective-permute-start | bytes 294920 | tf_op jit(solution)/shard_map/ppermute | solution.py:289
  23.6 1.0 %copy-done = bf16[1,1,16,128,128]{4,3,2,1,0:T(8,128)(2,1)S(1)} copy-done((bf16[1,1,16,128,128]{4,3,2,1,0:T(8,128)(2,1)S(1)}, bf16[1,1,16,128,128]{4,3,2,1,0:T(8,128)(2,1)}, u32[]{:S(2)}) %copy-start) | copy-done | bytes 524312
  24.6 0.8 shard_map.79
  25.4 1.6 %collective-permute-start.8 = (bf16[16,128,128]{2,1,0:T(8,128)(2,1)S(1)}, bf16[16,128,128]{2,1,0:T(8,128)(2,1)S(1)}, u32[]{:S(2)}, u32[]{:S(2)}) collective-permute-start(bf16[16,128,128]{2,1,0:T(8,128)(2,1)S(1)} %shard_map.78.refs_0_.refs_1_), channel_id=1, source_target_pairs={{0,8},{1,9},{2,10},{3,11},{4,12},{5,13},{6,14},{7,15},{8,0},{9,1},... | collective-permute-start | bytes 1572872 | tf_op jit(solution)/shard_map/ppermute | solution.py:289
  27.0 4.4 %collective-permute-start.7 = (bf16[16,128,128]{2,1,0:T(8,128)(2,1)}, bf16[16,128,128]{2,1,0:T(8,128)(2,1)}, u32[]{:S(2)}, u32[]{:S(2)}) collective-permute-start(bf16[16,128,128]{2,1,0:T(8,128)(2,1)} %shard_map.79), channel_id=1, source_target_pairs={{0,3},{3,0},{4,7},{7,4},{8,11},{11,8},{12,15},{15,12},{16,19},{19,... | collective-permute-start | bytes 1572872 | tf_op jit(solution)/shard_map/ppermute | solution.py:289
  32.0 12.0 %collective-permute-done.7.other_ref = bf16[16,128,128]{2,1,0:T(8,128)(2,1)} collective-permute-done((bf16[16,128,128]{2,1,0:T(8,128)(2,1)}, bf16[16,128,128]{2,1,0:T(8,128)(2,1)}, u32[]{:S(2)}, u32[]{:S(2)}) %collective-permute-start.7) | collective-permute-done | bytes 524320 | tf_op jit(solution)/shard_map/ppermute | solution.py:289
  44.0 1.1 %shard_map.80.refs_3_ = bf16[16,128,128]{2,1,0:T(8,128)(2,1)S(1)} custom-call(s32[1]{0:T(128)} %bitcast.6.first_ref, bf16[16,128,128]{2,1,0:T(8,128)(2,1)} %collective-permute-done.6.one_ref, bf16[16,128,128]{2,1,0:T(8,128)(2,1)} %collective-permute-done.7.other_ref, bf16[16,128,128]{2,1,0:T(8,128)(2,1)S(1)} %collective-permute-done.8.refs_0_.refs_4_, ...), custom_call_target="tpu_custom_call" | custom-call | tf_op jit(solution)/shard_map/pallas_call | solution.py:132
  46.3 2.5 %collective-permute-start.3 = (bf16[8,1,16,384]{3,2,0,1:T(8,128)(2,1)S(1)}, bf16[8,1,16,384]{3,2,0,1:T(8,128)(2,1)S(1)}, u32[]{:S(2)}, u32[]{:S(2)}) collective-permute-start(bf16[8,1,16,384]{3,2,0,1:T(8,128)(2,1)S(1)} %get-tuple-element.15), channel_id=1, source_target_pairs={{0,3},{1,2},{2,1},{3,0},{4,7},{5,6},{6,5},{7,4},{8,11},{9,10},{10,... | collective-permute-start | bytes 294920 | tf_op jit(solution)/shard_map/ppermute | solution.py:289
  48.8 11.3 %collective-permute-done.3 = bf16[8,1,16,384]{3,2,0,1:T(8,128)(2,1)S(1)} collective-permute-done((bf16[8,1,16,384]{3,2,0,1:T(8,128)(2,1)S(1)}, bf16[8,1,16,384]{3,2,0,1:T(8,128)(2,1)S(1)}, u32[]{:S(2)}, u32[]{:S(2)}) %collective-permute-start.3) | collective-permute-done | bytes 98336 | tf_op jit(solution)/shard_map/ppermute | solution.py:289
  61.5 0.7 collective-permute-done.16.refs_12_
  62.2 0.7 collective-permute-done.17.refs_13_
  62.9 5.5 %shard_map.82 = (bf16[14,16,128,128]{3,2,1,0:T(8,128)(2,1)S(1)}, bf16[14,16,128,128]{3,2,1,0:T(8,128)(2,1)S(1)}) custom-call(bf16[16,128,128]{2,1,0:T(8,128)(2,1)S(1)} %bitcast.18, bf16[16,128,128]{2,1,0:T(8,128)(2,1)S(1)} %shard_map.78.refs_0_.refs_1_, bf16[16,128,128]{2,1,0:T(8,128)(2,1)S(1)} %collective-permute-done.5.refs_1_.refs_2_, ...), custom_call_target="tpu_custom_call" | custom-call | bytes 22020096 | tf_op jit(solution)/shard_map/pallas_call | solution.py:202
  68.5 0.7 collective-permute-done.19.refs_0_
  69.8 0.9 collective-permute-done.21.refs_3_
  71.1 15.0 %shard_map.85 = bf16[16,2,16,256]{3,2,1,0:T(8,128)(2,1)S(1)} custom-call(s32[4]{0:T(128)S(1)} %get-tuple-element.21.across_ref, s32[4]{0:T(128)S(1)} %get-tuple-element.20.down_ref, s32[16,16]{1,0:T(8,128)S(1)} %fusion.8.ids_ref, bf16[16,16,384]{2,1,0:T(8,128)(2,1)S(1)} %maximum_bitcast_fusion.refs_2_.zt_ref, ...), custom_call_target="tpu_custom_call" | custom-call | tf_op jit(solution)/shard_map/pallas_call | solution.py:347
  86.1 12.9 %all_to_all.5 = bf16[16,2,16,256]{3,2,1,0:T(8,128)(2,1)S(1)} all-to-all(bf16[16,2,16,256]{3,2,1,0:T(8,128)(2,1)S(1)} %shard_map.85), channel_id=1, replica_groups=mesh['dom'=2,'col'=4,'row'=4] {'col','row'}, dimensions={0} | all-to-all | bytes 524288 | tf_op jit(solution)/shard_map/all_to_all | solution.py:360
  99.1 0.8 copy.14
  99.9 0.8 copy.15
  (60 shorter events, 6.7 us)
Async XLA Ops:
  0.6 62.3 %copy-start.1 = (bf16[1,1,16,128,128]{4,3,2,1,0:T(8,128)(2,1)S(1)}, bf16[1,1,16,128,128]{4,3,2,1,0:T(8,128)(2,1)}, u32[]{:S(2)}) copy-start(bf16[1,1,16,128,128]{4,3,2,1,0:T(8,128)(2,1)} %param.7) | copy-start | bytes 1572868
  3.0 58.5 %copy-start.3 = (s32[16]{0:T(128)S(1)}, s32[16]{0:T(128)}, u32[]{:S(2)}) copy-start(s32[16]{0:T(128)} %constant.49.clone) | copy-start | bytes 196
  3.6 4.7 %collective-permute-start = (bf16[8,16,384]{2,1,0:T(8,128)(2,1)S(1)}, bf16[8,16,384]{2,1,0:T(8,128)(2,1)S(1)}, u32[]{:S(2)}, u32[]{:S(2)}) collective-permute-start(bf16[8,16,384]{2,1,0:T(8,128)(2,1)S(1)} %get-tuple-element.7), channel_id=1, source_target_pairs={{0,4},{1,5},{2,6},{3,7},{4,0},{5,1},{6,2},{7,3},{8,12},{9,13},{10,... | collective-permute-start | bytes 294920 | tf_op jit(solution)/shard_map/ppermute | solution.py:289
  4.1 19.4 %collective-permute-start.5 = (bf16[16,128,128]{2,1,0:T(8,128)(2,1)}, bf16[16,128,128]{2,1,0:T(8,128)(2,1)S(1)}, u32[]{:S(2)}, u32[]{:S(2)}) collective-permute-start(bf16[16,128,128]{2,1,0:T(8,128)(2,1)} %bitcast.13), channel_id=1, source_target_pairs={{0,8},{1,9},{2,10},{3,11},{4,12},{5,13},{6,14},{7,15},{8,0},{9,1},... | collective-permute-start | bytes 1572872 | tf_op jit(solution)/shard_map/ppermute | solution.py:289
  6.7 16.8 %collective-permute-start.4 = (bf16[16,128,128]{2,1,0:T(8,128)(2,1)}, bf16[16,128,128]{2,1,0:T(8,128)(2,1)S(1)}, u32[]{:S(2)}, u32[]{:S(2)}) collective-permute-start(bf16[16,128,128]{2,1,0:T(8,128)(2,1)} %bitcast.14), channel_id=1, source_target_pairs={{0,1},{1,0},{2,3},{3,2},{4,5},{5,4},{6,7},{7,6},{8,9},{9,8},{10,11... | collective-permute-start | bytes 1572872 | tf_op jit(solution)/shard_map/ppermute | solution.py:289
  8.3 23.2 %collective-permute-start.9 = (bf16[16,128,128]{2,1,0:T(8,128)(2,1)}, bf16[16,128,128]{2,1,0:T(8,128)(2,1)S(1)}, u32[]{:S(2)}, u32[]{:S(2)}) collective-permute-start(bf16[16,128,128]{2,1,0:T(8,128)(2,1)} %bitcast.15), channel_id=1, source_target_pairs={{0,4},{1,5},{2,6},{3,7},{4,0},{5,1},{6,2},{7,3},{8,12},{9,13},{10,... | collective-permute-start | bytes 1572872 | tf_op jit(solution)/shard_map/ppermute | solution.py:289
  8.3 13.2 %collective-permute-start.1 = (bf16[2,4,16,384]{3,2,0,1:T(8,128)(2,1)S(1)}, bf16[2,4,16,384]{3,2,0,1:T(8,128)(2,1)S(1)}, u32[]{:S(2)}, u32[]{:S(2)}) collective-permute-start(bf16[2,4,16,384]{3,2,0,1:T(8,128)(2,1)S(1)} %get-tuple-element.18), channel_id=1, source_target_pairs={{0,8},{1,9},{2,10},{3,11},{4,12},{5,13},{6,14},{7,15},{8,0},{9,1},... | collective-permute-start | bytes 294920 | tf_op jit(solution)/shard_map/ppermute | solution.py:289
  8.9 23.1 %collective-permute-start.6 = (bf16[16,128,128]{2,1,0:T(8,128)(2,1)}, bf16[16,128,128]{2,1,0:T(8,128)(2,1)}, u32[]{:S(2)}, u32[]{:S(2)}) collective-permute-start(bf16[16,128,128]{2,1,0:T(8,128)(2,1)} %bitcast.16), channel_id=1, source_target_pairs={{1,2},{2,1},{5,6},{6,5},{9,10},{10,9},{13,14},{14,13},{17,18},{18,... | collective-permute-start | bytes 1572872 | tf_op jit(solution)/shard_map/ppermute | solution.py:289
  21.6 9.8 %collective-permute-start.2 = (bf16[4,2,16,384]{3,2,0,1:T(8,128)(2,1)S(1)}, bf16[4,2,16,384]{3,2,0,1:T(8,128)(2,1)S(1)}, u32[]{:S(2)}, u32[]{:S(2)}) collective-permute-start(bf16[4,2,16,384]{3,2,0,1:T(8,128)(2,1)S(1)} %get-tuple-element.16), channel_id=1, source_target_pairs={{0,1},{1,0},{2,3},{3,2},{4,5},{5,4},{6,7},{7,6},{8,9},{9,8},{10,11... | collective-permute-start | bytes 294920 | tf_op jit(solution)/shard_map/ppermute | solution.py:289
  25.4 18.6 %collective-permute-start.8 = (bf16[16,128,128]{2,1,0:T(8,128)(2,1)S(1)}, bf16[16,128,128]{2,1,0:T(8,128)(2,1)S(1)}, u32[]{:S(2)}, u32[]{:S(2)}) collective-permute-start(bf16[16,128,128]{2,1,0:T(8,128)(2,1)S(1)} %shard_map.78.refs_0_.refs_1_), channel_id=1, source_target_pairs={{0,8},{1,9},{2,10},{3,11},{4,12},{5,13},{6,14},{7,15},{8,0},{9,1},... | collective-permute-start | bytes 1572872 | tf_op jit(solution)/shard_map/ppermute | solution.py:289
  27.0 17.0 %collective-permute-start.7 = (bf16[16,128,128]{2,1,0:T(8,128)(2,1)}, bf16[16,128,128]{2,1,0:T(8,128)(2,1)}, u32[]{:S(2)}, u32[]{:S(2)}) collective-permute-start(bf16[16,128,128]{2,1,0:T(8,128)(2,1)} %shard_map.79), channel_id=1, source_target_pairs={{0,3},{3,0},{4,7},{7,4},{8,11},{11,8},{12,15},{15,12},{16,19},{19,... | collective-permute-start | bytes 1572872 | tf_op jit(solution)/shard_map/ppermute | solution.py:289
  31.4 12.6 %collective-permute-start.10 = (bf16[16,128,128]{2,1,0:T(8,128)(2,1)S(1)}, bf16[16,128,128]{2,1,0:T(8,128)(2,1)S(1)}, u32[]{:S(2)}, u32[]{:S(2)}) collective-permute-start(bf16[16,128,128]{2,1,0:T(8,128)(2,1)S(1)} %shard_map.78.refs_0_.refs_1_), channel_id=1, source_target_pairs={{0,4},{1,5},{2,6},{3,7},{4,0},{5,1},{6,2},{7,3},{8,12},{9,13},{10,... | collective-permute-start | bytes 1572872 | tf_op jit(solution)/shard_map/ppermute | solution.py:289
  31.5 12.6 %collective-permute-start.11 = (bf16[16,128,128]{2,1,0:T(8,128)(2,1)S(1)}, bf16[16,128,128]{2,1,0:T(8,128)(2,1)}, u32[]{:S(2)}, u32[]{:S(2)}) collective-permute-start(bf16[16,128,128]{2,1,0:T(8,128)(2,1)S(1)} %collective-permute-done.5.refs_1_.refs_2_), channel_id=1, source_target_pairs={{0,4},{1,5},{2,6},{3,7},{4,0},{5,1},{6,2},{7,3},{8,12},{9,13},{10,... | collective-permute-start | bytes 1572872 | tf_op jit(solution)/shard_map/ppermute | solution.py:289
  45.1 15.1 %collective-permute-start.12 = (bf16[16,128,128]{2,1,0:T(8,128)(2,1)S(1)}, bf16[16,128,128]{2,1,0:T(8,128)(2,1)S(1)}, u32[]{:S(2)}, u32[]{:S(2)}) collective-permute-start(bf16[16,128,128]{2,1,0:T(8,128)(2,1)S(1)} %shard_map.80.refs_3_), channel_id=1, source_target_pairs={{0,1},{1,0},{2,3},{3,2},{4,5},{5,4},{6,7},{7,6},{8,9},{9,8},{10,11... | collective-permute-start | bytes 1572872 | tf_op jit(solution)/shard_map/ppermute | solution.py:289
  45.2 15.0 %collective-permute-start.13 = (bf16[16,128,128]{2,1,0:T(8,128)(2,1)S(1)}, bf16[16,128,128]{2,1,0:T(8,128)(2,1)S(1)}, u32[]{:S(2)}, u32[]{:S(2)}) collective-permute-start(bf16[16,128,128]{2,1,0:T(8,128)(2,1)S(1)} %shard_map.80.refs_3_), channel_id=1, source_target_pairs={{0,8},{1,9},{2,10},{3,11},{4,12},{5,13},{6,14},{7,15},{8,0},{9,1},... | collective-permute-start | bytes 1572872 | tf_op jit(solution)/shard_map/ppermute | solution.py:289
  45.7 14.4 %collective-permute-start.14 = (bf16[16,128,128]{2,1,0:T(8,128)(2,1)S(1)}, bf16[16,128,128]{2,1,0:T(8,128)(2,1)S(1)}, u32[]{:S(2)}, u32[]{:S(2)}) collective-permute-start(bf16[16,128,128]{2,1,0:T(8,128)(2,1)S(1)} %shard_map.80.refs_3_), channel_id=1, source_target_pairs={{0,4},{1,5},{2,6},{3,7},{4,0},{5,1},{6,2},{7,3},{8,12},{9,13},{10,... | collective-permute-start | bytes 1572872 | tf_op jit(solution)/shard_map/ppermute | solution.py:289
  45.8 14.4 %collective-permute-start.15 = (bf16[16,128,128]{2,1,0:T(8,128)(2,1)S(1)}, bf16[16,128,128]{2,1,0:T(8,128)(2,1)S(1)}, u32[]{:S(2)}, u32[]{:S(2)}) collective-permute-start(bf16[16,128,128]{2,1,0:T(8,128)(2,1)S(1)} %collective-permute-done.8.refs_0_.refs_4_), channel_id=1, source_target_pairs={{0,4},{1,5},{2,6},{3,7},{4,0},{5,1},{6,2},{7,3},{8,12},{9,13},{10,... | collective-permute-start | bytes 1572872 | tf_op jit(solution)/shard_map/ppermute | solution.py:289
  46.3 13.8 %collective-permute-start.3 = (bf16[8,1,16,384]{3,2,0,1:T(8,128)(2,1)S(1)}, bf16[8,1,16,384]{3,2,0,1:T(8,128)(2,1)S(1)}, u32[]{:S(2)}, u32[]{:S(2)}) collective-permute-start(bf16[8,1,16,384]{3,2,0,1:T(8,128)(2,1)S(1)} %get-tuple-element.15), channel_id=1, source_target_pairs={{0,3},{1,2},{2,1},{3,0},{4,7},{5,6},{6,5},{7,4},{8,11},{9,10},{10,... | collective-permute-start | bytes 294920 | tf_op jit(solution)/shard_map/ppermute | solution.py:289
  60.2 2.0 %collective-permute-start.16 = (bf16[16,128,128]{2,1,0:T(8,128)(2,1)S(1)}, bf16[16,128,128]{2,1,0:T(8,128)(2,1)S(1)}, u32[]{:S(2)}, u32[]{:S(2)}) collective-permute-start(bf16[16,128,128]{2,1,0:T(8,128)(2,1)S(1)} %shard_map.81.refs_5_), channel_id=1, source_target_pairs={{0,4},{1,5},{2,6},{3,7},{4,0},{5,1},{6,2},{7,3},{8,12},{9,13},{10,... | collective-permute-start | bytes 1572872 | tf_op jit(solution)/shard_map/ppermute | solution.py:289
  60.3 2.6 %collective-permute-start.17 = (bf16[16,128,128]{2,1,0:T(8,128)(2,1)S(1)}, bf16[16,128,128]{2,1,0:T(8,128)(2,1)S(1)}, u32[]{:S(2)}, u32[]{:S(2)}) collective-permute-start(bf16[16,128,128]{2,1,0:T(8,128)(2,1)S(1)} %collective-permute-done.13.refs_1_.refs_6_), channel_id=1, source_target_pairs={{0,4},{1,5},{2,6},{3,7},{4,0},{5,1},{6,2},{7,3},{8,12},{9,13},{10,... | collective-permute-start | bytes 1572872 | tf_op jit(solution)/shard_map/ppermute | solution.py:289
  60.8 8.4 %collective-permute-start.19 = (bf16[8,128,128]{2,1,0:T(8,128)(2,1)S(1)}, bf16[8,128,128]{2,1,0:T(8,128)(2,1)S(1)}, u32[]{:S(2)}, u32[]{:S(2)}) collective-permute-start(bf16[8,128,128]{2,1,0:T(8,128)(2,1)S(1)} %slice.58), channel_id=1, source_target_pairs={{0,1},{1,0},{2,3},{3,2},{4,5},{5,4},{6,7},{7,6},{8,9},{9,8},{10,11... | collective-permute-start | bytes 786440 | tf_op jit(solution)/shard_map/ppermute | solution.py:289
  60.9 8.4 %collective-permute-start.18 = (bf16[8,128,128]{2,1,0:T(8,128)(2,1)S(1)}, bf16[8,128,128]{2,1,0:T(8,128)(2,1)S(1)}, u32[]{:S(2)}, u32[]{:S(2)}) collective-permute-start(bf16[8,128,128]{2,1,0:T(8,128)(2,1)S(1)} %slice.57), channel_id=1, source_target_pairs={{0,8},{1,9},{2,10},{3,11},{4,12},{5,13},{6,14},{7,15},{8,0},{9,1},... | collective-permute-start | bytes 786440 | tf_op jit(solution)/shard_map/ppermute | solution.py:289
  69.2 1.5 %collective-permute-start.21 = (bf16[8,128,128]{2,1,0:T(8,128)(2,1)S(1)}, bf16[8,128,128]{2,1,0:T(8,128)(2,1)S(1)}, u32[]{:S(2)}, u32[]{:S(2)}) collective-permute-start(bf16[8,128,128]{2,1,0:T(8,128)(2,1)S(1)} %shard_map.84.refs_1_), channel_id=1, source_target_pairs={{0,4},{1,5},{2,6},{3,7},{4,0},{5,1},{6,2},{7,3},{8,12},{9,13},{10,... | collective-permute-start | bytes 786440 | tf_op jit(solution)/shard_map/ppermute | solution.py:289
  69.3 1.8 %collective-permute-start.20 = (bf16[8,128,128]{2,1,0:T(8,128)(2,1)S(1)}, bf16[8,128,128]{2,1,0:T(8,128)(2,1)S(1)}, u32[]{:S(2)}, u32[]{:S(2)}) collective-permute-start(bf16[8,128,128]{2,1,0:T(8,128)(2,1)S(1)} %shard_map.83.refs_0_), channel_id=1, source_target_pairs={{0,4},{1,5},{2,6},{3,7},{4,0},{5,1},{6,2},{7,3},{8,12},{9,13},{10,... | collective-permute-start | bytes 786440 | tf_op jit(solution)/shard_map/ppermute | solution.py:289
  (2 other events, 1.9 us)

commit v11 on v10

--- a/solution.py
+++ b/solution.py
@@ -2,7 +2,6 @@
 
 import jax
 import jax.numpy as jnp
-import numpy
 from jax import lax
 from jax.experimental import pallas as pl
 from jax.experimental.pallas import tpu as pltpu
@@ -105,66 +104,79 @@
     return pl.pallas_call(
         copy_kernel,
         out_shape=jax.ShapeDtypeStruct(value.shape, value.dtype),
-        in_specs=anywhere(1 + len(others)),
+        in_specs=[pl.BlockSpec(memory_space=pltpu.HBM)] + anywhere(len(others)),
         out_specs=anywhere()[0],
         scratch_shapes=[pltpu.SemaphoreType.DMA(())],
         compiler_params=pltpu.CompilerParams(vmem_limit_bytes=2**20),
     )(value, *others)
 
 
-def pick_kernel(first_ref, one_ref, other_ref, *refs):
+def pick_kernel(rows, one_ref, other_ref, *refs):
     out_ref, sem = refs[-2:]
-
-    @pl.when(first_ref[0] != 0)
+    row = lax.axis_index("row")
+    first = (row == rows[0]) | (row == rows[1])
+
+    @pl.when(first)
     def _():
         copy = pltpu.make_async_copy(one_ref, out_ref, sem)
         copy.start()
         copy.wait()
 
-    @pl.when(first_ref[0] == 0)
+    @pl.when(jnp.logical_not(first))
     def _():
         copy = pltpu.make_async_copy(other_ref, out_ref, sem)
         copy.start()
         copy.wait()
 
 
-def pick(first, one, other, *others):
+def pick(rows, one, other, *others):
     return pl.pallas_call(
-        pick_kernel,
+        functools.partial(pick_kernel, rows),
         out_shape=jax.ShapeDtypeStruct(one.shape, one.dtype),
-        in_specs=smem() + anywhere(2 + len(others)),
+        in_specs=anywhere(2 + len(others)),
         out_specs=anywhere()[0],
         scratch_shapes=[pltpu.SemaphoreType.DMA(())],
         compiler_params=pltpu.CompilerParams(vmem_limit_bytes=2**20),
-    )(first, one, other, *others)
-
-
-def split_kernel(peers_ref, vectors_ref, ids_ref, keep_ref, go_ref, turned):
+    )(one, other, *others)
+
+
+def split_kernel(n_col, n_row, vectors_ref, cols_ref, keep_ref, go_ref, known_ref, turned):
+    col, row = lax.axis_index("col"), lax.axis_index("row")
     count, share, rows = turned.shape
+    orb = keep_ref.shape[2]
+    per_piece = rows // orb
     whole = vectors_ref[...].T
     for d in range(count):
         turned[d] = whole[d * share : (d + 1) * share]
-    for k in range(count):
-        out_ref = (keep_ref, go_ref)[k // (count // 2)]
-        out_ref[k % (count // 2), :, :rows] = turned[peers_ref[k]]
-        out_ref[k % (count // 2), :, rows:] = ids_ref[...]
+    orders = [(y, one, three) for y in range(2) for one in range(2) for three in range(2)]
+    for core, out_ref in enumerate((keep_ref, go_ref)):
+        for k, (y, one, three) in enumerate(orders):
+            peer = (col ^ (core + 2 * y)) * n_row + (row ^ one ^ 3 * three)
+            for b in range(per_piece):
+                out_ref[k * per_piece + b] = turned[peer, :, b * orb : (b + 1) * orb]
+    ids = cols_ref[...]
+    piece = jnp.zeros_like(ids)
+    for c in range(1, n_col):
+        piece += (ids >= c * per_piece).astype(jnp.int32)
+    ids = ids - piece * per_piece + (piece * n_row + row) * per_piece
+    known_ref[0] = ids.astype(jnp.float32).astype(known_ref.dtype)
 
 
 def place(g, f):
     return (f >> 1) * 8 + ((f & 1) ^ (f >> 1)) * 4 + g
 
 
-def multiply(t, groups, across_ref, ids_ref, z, straight, scattered):
+def multiply(t, groups, across, ids_ref, z, straight, scattered):
     tile_rows = z.shape[0] // len(groups)
     orb = z.shape[2]
     for g, group in enumerate(groups):
         if not group:
             continue
-        here = across_ref[g] * tile_rows + t
+        here = across[g] * tile_rows + t
         places = [(tile, t * PER_ROW + p) for tile in group for p in range(PER_ROW)]
-        strip = jnp.concatenate([s[i, slot] for (_, s, _, i), slot in places], axis=1)
-        turned = jnp.concatenate([st[i, slot] for (_, _, st, i), slot in places], axis=0)
-        where = [ids_ref[place(g, f), slot] for (f, _, _, _), slot in places]
+        strip = jnp.concatenate([s[i, slot] for (_, s, i, _, _), slot in places], axis=1)
+        turned = jnp.concatenate([st[i, slot] for (_, _, _, st, i), slot in places], axis=0)
+        where = [ids_ref[place(g, f), slot] for (f, *_), slot in places]
         wide = jnp.concatenate([z[u] for u in where], axis=1)
         straight[here] = jnp.dot(wide, turned, preferred_element_type=jnp.float32)
         mirrored = jnp.dot(z[here], strip, preferred_element_type=jnp.float32)
@@ -210,7 +222,7 @@
     )(*bufs)
 
 
-def filter_kernel(early, late, n_col, n_row, across_ref, down_ref, ids_ref, zt_ref, se_ref, ste_ref, *refs):
+def filter_kernel(early, late, n_col, n_row, ids_ref, zt_ref, se_ref, ste_ref, *refs):
     bufs, (out_ref, s_ref, st_ref, z, now, prev, straight, *scattered, sems) = (
         refs[: len(late)],
         refs[len(late) :],
@@ -219,6 +231,8 @@
     slots = s_ref.shape[1]
     per_piece = n_blocks // (n_col * n_row)
     tile_rows = slots // PER_ROW
+    across = [lax.axis_index("col") ^ g for g in range(n_col)]
+    down = [lax.axis_index("row") ^ f for f in range(n_row)]
     rest = sorted({(g, f) for g, f, _ in late})
 
     copies = []
@@ -229,8 +243,8 @@
     for g in range(n_col):
         for f in range(n_row):
             for b in range(per_piece):
-                u = (across_ref[g] * n_row + down_ref[f]) * per_piece + b
-                own = zt_ref[place(g, f), :, b * orb : (b + 1) * orb]
+                u = (across[g] * n_row + down[f]) * per_piece + b
+                own = zt_ref[place(g, f), b]
                 z[u] = own
                 now[u] = own.astype(jnp.float32)
     clear([prev])
@@ -238,15 +252,15 @@
         copy.wait()
         turn(s_ref, st_ref, rest.index((g, f)), start, buf.shape[0])
 
-    tiles = {at: (se_ref, ste_ref, i) for i, at in enumerate(early)}
-    tiles.update({at: (s_ref, st_ref, i) for i, at in enumerate(rest)})
+    tiles = {at: (se_ref, i, ste_ref, i) for i, at in enumerate(early)}
+    tiles.update({at: (s_ref, i, st_ref, i) for i, at in enumerate(rest)})
     groups = [[(f, *tiles[g, f]) for f in range(n_row)] for g in range(n_col)]
 
     def one_step(step, carry):
         clear(scattered)
 
         def block_row(t, carry):
-            multiply(t, groups, across_ref, ids_ref, z, straight, scattered)
+            multiply(t, groups, across, ids_ref, z, straight, scattered)
             return carry
 
         lax.fori_loop(0, tile_rows, block_row, 0)
@@ -277,8 +291,6 @@
     per_piece = rows // orb
     n_blocks = n_dev * per_piece
     half = slots // 2
-    across = lax.axis_index("col") ^ jnp.arange(n_col, dtype=jnp.int32)
-    down = lax.axis_index("row") ^ jnp.arange(n_row, dtype=jnp.int32)
 
     def send(buf, flip_col, flip_row, from_rows=range(n_row)):
         pairs = [
@@ -296,58 +308,62 @@
     inner = send(own, 0, 3, (1, 2))
     over_own = send(own, 2, 0)
 
-    g_of = numpy.array([core + 2 * y for core in range(2) for y in range(2) for _ in range(4)])
-    f_of = numpy.array([one ^ 3 * three for _ in range(4) for one in range(2) for three in range(2)])
-    peers = (lax.axis_index("col") ^ g_of) * n_row + (lax.axis_index("row") ^ f_of)
-    own_ids = jnp.pad(cols[0, 0], (0, orb - slots)).astype(vectors.dtype)
-    keep, go = pl.pallas_call(
-        split_kernel,
-        out_shape=[jax.ShapeDtypeStruct((n_dev // 2, share, rows + orb), vectors.dtype)] * 2,
-        in_specs=smem() + vmem(2),
-        out_specs=vmem(2),
+    own_cols = jnp.broadcast_to(jnp.pad(cols[0, 0], (0, orb - slots)), (share, orb))
+    shares = jax.ShapeDtypeStruct((n_dev // 2 * per_piece, share, orb), vectors.dtype)
+    keep, go, known = pl.pallas_call(
+        functools.partial(split_kernel, n_col, n_row),
+        out_shape=[shares, shares, jax.ShapeDtypeStruct((1, share, orb), vectors.dtype)],
+        in_specs=vmem(2),
+        out_specs=vmem(3),
         scratch_shapes=[pltpu.VMEM((n_dev, share, rows), vectors.dtype)],
         compiler_params=pltpu.CompilerParams(vmem_limit_bytes=4 * 2**20),
-    )(peers.astype(jnp.int32), vectors, jnp.broadcast_to(own_ids, (share, orb)))
-    parts = jnp.stack([keep, send(go, 1, 0)])
-
-    def swap(parts, flip_col, flip_row):
-        count = parts.shape[1] // 2
-        return jnp.concatenate([parts[:, :count], send(parts[:, count:], flip_col, flip_row)])
-
-    parts = swap(parts, 2, 0)
-
-    near = after(near, over_own, parts)
+    )(vectors, own_cols)
+
+    def swap(keep, go, flip_col, flip_row):
+        (keep, known), count = keep, go.shape[0]
+        came = send(jnp.concatenate([go, known]), flip_col, flip_row)
+        return jnp.concatenate([keep, came[:count]]), jnp.concatenate([known, came[count:]])
+
+    parts = swap((keep, known), go, 1, 0)
+
+    near = after(near, over_own, parts[0])
     outer = send(copy_after(own, near), 0, 3, (0, 3))
     over_near = send(near, 2, 0)
-    parts = swap(parts, 0, 1)
+    mine, known = parts
+    mine = mine.reshape(2, 2, -1, share, orb)
+    parts = swap((mine[:, 0].reshape(-1, share, orb), known), mine[:, 1].reshape(-1, share, orb), 2, 0)
     mates = to_mate(own, near, over_own)
-    inside = (lax.axis_index("row") == 1) | (lax.axis_index("row") == 2)
-    far = pick(inside.astype(jnp.int32)[None], inner, outer, over_near, parts, *mates)
+    far = pick((1, 2), inner, outer, over_near, parts[0], *mates)
+
     over_far = send(far, 2, 0)
     last = send(far, 0, 1)
-    parts = swap(parts, 0, 3)[:, 0]
+    mine, known = parts
+    mine = mine.reshape(n_col, n_row, -1, share, orb)
+    parts = [(mine[:, 0].reshape(-1, share, orb), known)]
+    for one, three in ((1, 0), (0, 1), (1, 1)):
+        go = mine[:, 2 * one + three].reshape(-1, share, orb)
+        came = send(jnp.concatenate([go, known]), 0, one ^ 3 * three)
+        parts.append((came[: go.shape[0]], came[go.shape[0] :]))
+    mine = jnp.concatenate([part for part, _ in parts])
+    ids = jnp.concatenate([known[:, 0, :slots].astype(jnp.int32) for _, known in parts])
     mates += to_mate(far, over_near)
-    last = after(last, over_far, parts, *mates[3:])
+    last = after(last, over_far, mine, *mates[3:])
+
     over_last = send(last[:half], 2, 0)
     side_last = send(over_far[half:], 0, 1)
     mates += to_mate(last, over_far)
+    se, ste = load([own, near, over_own, far, over_near, last, over_far, *mates])
+    over_last, side_last = after(over_last, se), after(side_last, se)
+
     early = [(0, 0), (0, 1), (2, 0), (0, 3), (2, 1), (0, 2), (2, 3)]
     early += [(g ^ 1, f) for g, f in early]
-    se, ste = load([own, near, over_own, far, over_near, last, over_far, *mates])
-    over_last, side_last = after(over_last, se), after(side_last, se)
+    late = [(2, 2, 0), (2, 2, half), (3, 2, 0), (3, 2, half)]
     late_bufs = [over_last, side_last, *to_mate(over_last, side_last)]
-    late = [(2, 2, 0), (2, 2, half), (3, 2, 0), (3, 2, half)]
-
-    local = parts[:, 0, rows : rows + slots].astype(jnp.int32)
-    f_at = {place(g, f): f for g in range(n_col) for f in range(n_row)}
-    f_at = numpy.array([f_at[k] for k in range(n_dev)], numpy.int32)
-    at_row = (lax.axis_index("row") ^ f_at)[:, None]
-    ids = (local // per_piece * n_row + at_row) * per_piece + local % per_piece
 
     done = pl.pallas_call(
         functools.partial(filter_kernel, early, late, n_col, n_row),
         out_shape=jax.ShapeDtypeStruct((n_dev, 2, share, rows), jnp.bfloat16),
-        in_specs=smem(3) + vmem(3) + anywhere(len(late)),
+        in_specs=smem() + vmem(3) + anywhere(len(late)),
         out_specs=vmem()[0],
         scratch_shapes=[
             *[pltpu.VMEM((n_dev - len(early), slots, orb, orb), blocks.dtype)] * 2,
@@ -356,7 +372,13 @@
             pltpu.SemaphoreType.DMA((len(late),)),
         ],
         compiler_params=pltpu.CompilerParams(vmem_limit_bytes=12 * 2**20),
-    )(across, down, ids, parts, se, ste, *late_bufs)
+    )(
+        ids,
+        mine.reshape(n_dev, per_piece, share, orb),
+        se,
+        ste,
+        *late_bufs,
+    )
     back = lax.all_to_all(done, LANES, split_axis=0, concat_axis=0, tiled=True)
     outs = jnp.transpose(back, (1, 3, 0, 2)).reshape(2, rows, width).astype(jnp.float32)
     return outs[0], outs[1]

time: 101 us -> 103 us (1.020)
  starting transfers between devices: 20.5 us -> 23.4 us
  Pallas kernels: 23 us -> 20.8 us
  other arithmetic: 1.68 us -> 0.16 us
  blocking collectives: 12.9 us -> 14.1 us
    ppermute x22 -> x23, starting transfers between devices: 20.5 us -> 23.4 us  [send(): return lax.ppermute(buf, LANES, pairs)]
    pallas_call x2, Pallas kernels: 1.69 us -> 0.17 us  [the longest x1 0.11 us: gather_plan(): pl.pallas_call(functools.partial(split_kernel, n_col, n_row), out_shape=[...]
    all_to_all x1, blocking collectives: 12.9 us -> 14.1 us  [gather_plan(): back = lax.all_to_all(done, LANES, split_axis=0, concat_axis=0, tiled=True)]
    ppermute x22 -> x23, waiting for transfers between devices: 38 us -> 38.5 us  [send(): return lax.ppermute(buf, LANES, pairs)]
    unnamed x10 -> x12, local copies, waits for them, and re-layouts: 3.62 us -> 3.64 us
  transfers between devices with their start and end apart: 22 -> 23, of which waited for: 9 -> 11; matrix products, arithmetic and copies ran while one was open for 0% -> 0% of each run, Pallas kernels for 6% -> 5%
where the time goes in v11:
time: 103 us; the launch traced here: 102 us
  waiting for transfers between devices  38.5 us (37%)
  starting transfers between devices  23.4 us (23%)
  Pallas kernels  20.8 us (20%)
  blocking collectives  14.1 us (14%)
  local copies, waits for them, and re-layouts  4.5 us (4%)
    ppermute x23, waiting for transfers between devices, send(): return lax.ppermute(buf, LANES, pairs)  38.5 us
    ppermute x23, starting transfers between devices, send(): return lax.ppermute(buf, LANES, pairs)  23.4 us
    pallas_call x1, Pallas kernels, gather_plan(): pl.pallas_call(functools.partial(filter_kernel, early, late, n_col, n_row...  15 us
    all_to_all x1, blocking collectives, gather_plan(): back = lax.all_to_all(done, LANES, split_axis=0, concat_axis=0, tiled=True)  14.1 us
    pallas_call x1, Pallas kernels, load(): pl.pallas_call(functools.partial(load_kernel, len(bufs)), out_shape=[out,...  5.57 us
    unnamed x12, local copies, waits for them, and re-layouts  3.64 us
  transfers between devices with their start and end apart: 23, of which 11 were waited for; matrix products, arithmetic and copies ran while one was open for 0% of the time, Pallas kernels for 5%

profile of v11, /device:TPU:0, one launch (start us, length us, event | category | flops | bytes accessed | tf_op | source)
XLA Modules:
  0.0 102.4 jit_solution(9686572120227615192)
XLA Ops:
  0.6 0.7 pad.4
  1.4 0.9 copy-done.2
  2.9 2.6 %collective-permute-start.5 = (bf16[16,128,128]{2,1,0:T(8,128)(2,1)}, bf16[16,128,128]{2,1,0:T(8,128)(2,1)S(1)}, u32[]{:S(2)}, u32[]{:S(2)}) collective-permute-start(bf16[16,128,128]{2,1,0:T(8,128)(2,1)} %bitcast.27), channel_id=1, source_target_pairs={{0,1},{1,0},{2,3},{3,2},{4,5},{5,4},{6,7},{7,6},{8,9},{9,8},{10,11... | collective-permute-start | bytes 1572872 | tf_op jit(solution)/shard_map/ppermute | solution.py:301
  5.6 1.5 %collective-permute-start.6 = (bf16[16,128,128]{2,1,0:T(8,128)(2,1)}, bf16[16,128,128]{2,1,0:T(8,128)(2,1)S(1)}, u32[]{:S(2)}, u32[]{:S(2)}) collective-permute-start(bf16[16,128,128]{2,1,0:T(8,128)(2,1)} %bitcast.28), channel_id=1, source_target_pairs={{0,8},{1,9},{2,10},{3,11},{4,12},{5,13},{6,14},{7,15},{8,0},{9,1},... | collective-permute-start | bytes 1572872 | tf_op jit(solution)/shard_map/ppermute | solution.py:301
  7.1 0.7 collective-permute-start.7
  8.5 9.8 %collective-permute-done.5.refs_0_ = bf16[16,128,128]{2,1,0:T(8,128)(2,1)S(1)} collective-permute-done((bf16[16,128,128]{2,1,0:T(8,128)(2,1)}, bf16[16,128,128]{2,1,0:T(8,128)(2,1)S(1)}, u32[]{:S(2)}, u32[]{:S(2)}) %collective-permute-start.5) | collective-permute-done | bytes 524320 | tf_op jit(solution)/shard_map/ppermute | solution.py:301
  18.3 2.3 %collective-permute-done.6.refs_1_.refs_2_ = bf16[16,128,128]{2,1,0:T(8,128)(2,1)S(1)} collective-permute-done((bf16[16,128,128]{2,1,0:T(8,128)(2,1)}, bf16[16,128,128]{2,1,0:T(8,128)(2,1)S(1)}, u32[]{:S(2)}, u32[]{:S(2)}) %collective-permute-start.6) | collective-permute-done | bytes 524320 | tf_op jit(solution)/shard_map/ppermute | solution.py:301
  20.6 1.0 %copy-done = bf16[1,1,16,128,128]{4,3,2,1,0:T(8,128)(2,1)S(1)} copy-done((bf16[1,1,16,128,128]{4,3,2,1,0:T(8,128)(2,1)S(1)}, bf16[1,1,16,128,128]{4,3,2,1,0:T(8,128)(2,1)}, u32[]{:S(2)}) %copy-start) | copy-done | bytes 524312
  21.6 1.6 %collective-permute-start.9 = (bf16[16,128,128]{2,1,0:T(8,128)(2,1)S(1)}, bf16[16,128,128]{2,1,0:T(8,128)(2,1)S(1)}, u32[]{:S(2)}, u32[]{:S(2)}) collective-permute-start(bf16[16,128,128]{2,1,0:T(8,128)(2,1)S(1)} %shard_map.51.refs_0_.refs_1_), channel_id=1, source_target_pairs={{0,8},{1,9},{2,10},{3,11},{4,12},{5,13},{6,14},{7,15},{8,0},{9,1},... | collective-permute-start | bytes 1572872 | tf_op jit(solution)/shard_map/ppermute | solution.py:301
  23.2 4.4 %collective-permute-start.8 = (bf16[16,128,128]{2,1,0:T(8,128)(2,1)S(1)}, bf16[16,128,128]{2,1,0:T(8,128)(2,1)S(1)}, u32[]{:S(2)}, u32[]{:S(2)}) collective-permute-start(bf16[16,128,128]{2,1,0:T(8,128)(2,1)S(1)} %shard_map.52), channel_id=1, source_target_pairs={{0,3},{3,0},{4,7},{7,4},{8,11},{11,8},{12,15},{15,12},{16,19},{19,... | collective-permute-start | bytes 1572872 | tf_op jit(solution)/shard_map/ppermute | solution.py:301
  28.2 10.8 %collective-permute-done.8.other_ref = bf16[16,128,128]{2,1,0:T(8,128)(2,1)S(1)} collective-permute-done((bf16[16,128,128]{2,1,0:T(8,128)(2,1)S(1)}, bf16[16,128,128]{2,1,0:T(8,128)(2,1)S(1)}, u32[]{:S(2)}, u32[]{:S(2)}) %collective-permute-start.8) | collective-permute-done | bytes 524320 | tf_op jit(solution)/shard_map/ppermute | solution.py:301
  40.3 3.6 %collective-permute-start.4 = (bf16[12,16,128]{2,1,0:T(8,128)(2,1)S(1)}, bf16[12,16,128]{2,1,0:T(8,128)(2,1)S(1)}, u32[]{:S(2)}, u32[]{:S(2)}) collective-permute-start(bf16[12,16,128]{2,1,0:T(8,128)(2,1)S(1)} %get-tuple-element.26), channel_id=1, source_target_pairs={{0,2},{1,3},{2,0},{3,1},{4,6},{5,7},{6,4},{7,5},{8,10},{9,11},{10,... | collective-permute-start | bytes 147464 | tf_op jit(solution)/shard_map/ppermute | solution.py:301
  43.9 6.3 %collective-permute-done.4 = bf16[12,16,128]{2,1,0:T(8,128)(2,1)S(1)} collective-permute-done((bf16[12,16,128]{2,1,0:T(8,128)(2,1)S(1)}, bf16[12,16,128]{2,1,0:T(8,128)(2,1)S(1)}, u32[]{:S(2)}, u32[]{:S(2)}) %collective-permute-start.4) | collective-permute-done | bytes 49184 | tf_op jit(solution)/shard_map/ppermute | solution.py:301
  50.2 2.3 %collective-permute-start.3 = (bf16[12,16,128]{2,1,0:T(8,128)(2,1)S(1)}, bf16[12,16,128]{2,1,0:T(8,128)(2,1)S(1)}, u32[]{:S(2)}, u32[]{:S(2)}) collective-permute-start(bf16[12,16,128]{2,1,0:T(8,128)(2,1)S(1)} %get-tuple-element.25), channel_id=1, source_target_pairs={{0,3},{1,2},{2,1},{3,0},{4,7},{5,6},{6,5},{7,4},{8,11},{9,10},{10,... | collective-permute-start | bytes 147464 | tf_op jit(solution)/shard_map/ppermute | solution.py:301
  52.5 3.9 %collective-permute-done.3 = bf16[12,16,128]{2,1,0:T(8,128)(2,1)S(1)} collective-permute-done((bf16[12,16,128]{2,1,0:T(8,128)(2,1)S(1)}, bf16[12,16,128]{2,1,0:T(8,128)(2,1)S(1)}, u32[]{:S(2)}, u32[]{:S(2)}) %collective-permute-start.3) | collective-permute-done | bytes 49184 | tf_op jit(solution)/shard_map/ppermute | solution.py:301
  56.4 1.2 %collective-permute-start.2 = (bf16[12,16,128]{2,1,0:T(8,128)(2,1)S(1)}, bf16[12,16,128]{2,1,0:T(8,128)(2,1)S(1)}, u32[]{:S(2)}, u32[]{:S(2)}) collective-permute-start(bf16[12,16,128]{2,1,0:T(8,128)(2,1)S(1)} %get-tuple-element.24), channel_id=1, source_target_pairs={{0,1},{1,0},{2,3},{3,2},{4,5},{5,4},{6,7},{7,6},{8,9},{9,8},{10,11... | collective-permute-start | bytes 147464 | tf_op jit(solution)/shard_map/ppermute | solution.py:301
  57.7 2.9 %collective-permute-done.2 = bf16[12,16,128]{2,1,0:T(8,128)(2,1)S(1)} collective-permute-done((bf16[12,16,128]{2,1,0:T(8,128)(2,1)S(1)}, bf16[12,16,128]{2,1,0:T(8,128)(2,1)S(1)}, u32[]{:S(2)}, u32[]{:S(2)}) %collective-permute-start.2) | collective-permute-done | bytes 49184 | tf_op jit(solution)/shard_map/ppermute | solution.py:301
  61.8 1.3 %collective-permute-start.20 = (bf16[8,128,128]{2,1,0:T(8,128)(2,1)S(1)}, bf16[8,128,128]{2,1,0:T(8,128)(2,1)S(1)}, u32[]{:S(2)}, u32[]{:S(2)}) collective-permute-start(bf16[8,128,128]{2,1,0:T(8,128)(2,1)S(1)} %slice.109), channel_id=1, source_target_pairs={{0,1},{1,0},{2,3},{3,2},{4,5},{5,4},{6,7},{7,6},{8,9},{9,8},{10,11... | collective-permute-start | bytes 786440 | tf_op jit(solution)/shard_map/ppermute | solution.py:301
  63.3 5.6 %shard_map.55 = (bf16[14,16,128,128]{3,2,1,0:T(8,128)(2,1)S(1)}, bf16[14,16,128,128]{3,2,1,0:T(8,128)(2,1)S(1)}) custom-call(bf16[16,128,128]{2,1,0:T(8,128)(2,1)S(1)} %bitcast.32, bf16[16,128,128]{2,1,0:T(8,128)(2,1)S(1)} %shard_map.51.refs_0_.refs_1_, bf16[16,128,128]{2,1,0:T(8,128)(2,1)S(1)} %collective-permute-done.6.refs_1_.refs_2_, ...), custom_call_target="tpu_custom_call" | custom-call | bytes 22020096 | tf_op jit(solution)/shard_map/pallas_call | solution.py:214
  70.2 0.9 collective-permute-done.21.refs_2_
  71.5 15.0 %shard_map.58 = bf16[16,2,16,256]{3,2,1,0:T(8,128)(2,1)S(1)} custom-call(s32[16,16]{1,0:T(8,128)S(1)} %maximum_convert_fusion.ids_ref, bf16[16,2,16,128]{3,2,1,0:T(8,128)(2,1)S(1)} %bitcast.33, bf16[14,16,128,128]{3,2,1,0:T(8,128)(2,1)S(1)} %get-tuple-element.10.refs_1_.se_ref, bf16[14,16,128,128]{3,2,1,0:T(8,128)(2,1)S(1)} %get-tuple-element.11.ste_ref, ...), custom_call_target="tpu_custom_call" | custom-call | tf_op jit(solution)/shard_map/pallas_call | solution.py:363
  86.5 14.1 %all_to_all.5 = bf16[16,2,16,256]{3,2,1,0:T(8,128)(2,1)S(1)} all-to-all(bf16[16,2,16,256]{3,2,1,0:T(8,128)(2,1)S(1)} %shard_map.58), channel_id=1, replica_groups=mesh['dom'=2,'col'=4,'row'=4] {'col','row'}, dimensions={0} | all-to-all | bytes 524288 | tf_op jit(solution)/shard_map/all_to_all | solution.py:382
  100.7 0.8 copy.11
  101.6 0.8 copy.12
  (70 shorter events, 6.3 us)
Async XLA Ops:
  0.6 62.7 %copy-start.1 = (bf16[1,1,16,128,128]{4,3,2,1,0:T(8,128)(2,1)S(1)}, bf16[1,1,16,128,128]{4,3,2,1,0:T(8,128)(2,1)}, u32[]{:S(2)}) copy-start(bf16[1,1,16,128,128]{4,3,2,1,0:T(8,128)(2,1)} %param.4) | copy-start | bytes 1572868
  2.4 5.4 %collective-permute-start = (bf16[17,16,128]{2,1,0:T(8,128)(2,1)S(1)}, bf16[17,16,128]{2,1,0:T(8,128)(2,1)S(1)}, u32[]{:S(2)}, u32[]{:S(2)}) collective-permute-start(bf16[17,16,128]{2,1,0:T(8,128)(2,1)S(1)} %pad_maximum_fusion.13), channel_id=1, source_target_pairs={{0,4},{1,5},{2,6},{3,7},{4,0},{5,1},{6,2},{7,3},{8,12},{9,13},{10,... | collective-permute-start | bytes 208904 | tf_op jit(solution)/shard_map/ppermute | solution.py:301
  2.9 15.4 %collective-permute-start.5 = (bf16[16,128,128]{2,1,0:T(8,128)(2,1)}, bf16[16,128,128]{2,1,0:T(8,128)(2,1)S(1)}, u32[]{:S(2)}, u32[]{:S(2)}) collective-permute-start(bf16[16,128,128]{2,1,0:T(8,128)(2,1)} %bitcast.27), channel_id=1, source_target_pairs={{0,1},{1,0},{2,3},{3,2},{4,5},{5,4},{6,7},{7,6},{8,9},{9,8},{10,11... | collective-permute-start | bytes 1572872 | tf_op jit(solution)/shard_map/ppermute | solution.py:301
  5.6 15.0 %collective-permute-start.6 = (bf16[16,128,128]{2,1,0:T(8,128)(2,1)}, bf16[16,128,128]{2,1,0:T(8,128)(2,1)S(1)}, u32[]{:S(2)}, u32[]{:S(2)}) collective-permute-start(bf16[16,128,128]{2,1,0:T(8,128)(2,1)} %bitcast.28), channel_id=1, source_target_pairs={{0,8},{1,9},{2,10},{3,11},{4,12},{5,13},{6,14},{7,15},{8,0},{9,1},... | collective-permute-start | bytes 1572872 | tf_op jit(solution)/shard_map/ppermute | solution.py:301
  7.1 20.6 %collective-permute-start.7 = (bf16[16,128,128]{2,1,0:T(8,128)(2,1)}, bf16[16,128,128]{2,1,0:T(8,128)(2,1)S(1)}, u32[]{:S(2)}, u32[]{:S(2)}) collective-permute-start(bf16[16,128,128]{2,1,0:T(8,128)(2,1)} %bitcast.29), channel_id=1, source_target_pairs={{1,2},{2,1},{5,6},{6,5},{9,10},{10,9},{13,14},{14,13},{17,18},{18,... | collective-permute-start | bytes 1572872 | tf_op jit(solution)/shard_map/ppermute | solution.py:301
  7.9 19.7 %collective-permute-start.1 = (bf16[18,16,128]{2,1,0:T(8,128)(2,1)S(1)}, bf16[18,16,128]{2,1,0:T(8,128)(2,1)S(1)}, u32[]{:S(2)}, u32[]{:S(2)}) collective-permute-start(bf16[18,16,128]{2,1,0:T(8,128)(2,1)S(1)} %pad_maximum_fusion.12), channel_id=1, source_target_pairs={{0,8},{1,9},{2,10},{3,11},{4,12},{5,13},{6,14},{7,15},{8,0},{9,1},... | collective-permute-start | bytes 221192 | tf_op jit(solution)/shard_map/ppermute | solution.py:301
  8.5 19.8 %collective-permute-start.10 = (bf16[16,128,128]{2,1,0:T(8,128)(2,1)}, bf16[16,128,128]{2,1,0:T(8,128)(2,1)S(1)}, u32[]{:S(2)}, u32[]{:S(2)}) collective-permute-start(bf16[16,128,128]{2,1,0:T(8,128)(2,1)} %bitcast.30), channel_id=1, source_target_pairs={{0,4},{1,5},{2,6},{3,7},{4,0},{5,1},{6,2},{7,3},{8,12},{9,13},{10,... | collective-permute-start | bytes 1572872 | tf_op jit(solution)/shard_map/ppermute | solution.py:301
  21.6 17.4 %collective-permute-start.9 = (bf16[16,128,128]{2,1,0:T(8,128)(2,1)S(1)}, bf16[16,128,128]{2,1,0:T(8,128)(2,1)S(1)}, u32[]{:S(2)}, u32[]{:S(2)}) collective-permute-start(bf16[16,128,128]{2,1,0:T(8,128)(2,1)S(1)} %shard_map.51.refs_0_.refs_1_), channel_id=1, source_target_pairs={{0,8},{1,9},{2,10},{3,11},{4,12},{5,13},{6,14},{7,15},{8,0},{9,1},... | collective-permute-start | bytes 1572872 | tf_op jit(solution)/shard_map/ppermute | solution.py:301
  23.2 15.8 %collective-permute-start.8 = (bf16[16,128,128]{2,1,0:T(8,128)(2,1)S(1)}, bf16[16,128,128]{2,1,0:T(8,128)(2,1)S(1)}, u32[]{:S(2)}, u32[]{:S(2)}) collective-permute-start(bf16[16,128,128]{2,1,0:T(8,128)(2,1)S(1)} %shard_map.52), channel_id=1, source_target_pairs={{0,3},{3,0},{4,7},{7,4},{8,11},{11,8},{12,15},{15,12},{16,19},{19,... | collective-permute-start | bytes 1572872 | tf_op jit(solution)/shard_map/ppermute | solution.py:301
  27.6 11.4 %collective-permute-start.11 = (bf16[16,128,128]{2,1,0:T(8,128)(2,1)S(1)}, bf16[16,128,128]{2,1,0:T(8,128)(2,1)S(1)}, u32[]{:S(2)}, u32[]{:S(2)}) collective-permute-start(bf16[16,128,128]{2,1,0:T(8,128)(2,1)S(1)} %shard_map.51.refs_0_.refs_1_), channel_id=1, source_target_pairs={{0,4},{1,5},{2,6},{3,7},{4,0},{5,1},{6,2},{7,3},{8,12},{9,13},{10,... | collective-permute-start | bytes 1572872 | tf_op jit(solution)/shard_map/ppermute | solution.py:301
  27.7 11.3 %collective-permute-start.12 = (bf16[16,128,128]{2,1,0:T(8,128)(2,1)S(1)}, bf16[16,128,128]{2,1,0:T(8,128)(2,1)S(1)}, u32[]{:S(2)}, u32[]{:S(2)}) collective-permute-start(bf16[16,128,128]{2,1,0:T(8,128)(2,1)S(1)} %collective-permute-done.6.refs_1_.refs_2_), channel_id=1, source_target_pairs={{0,4},{1,5},{2,6},{3,7},{4,0},{5,1},{6,2},{7,3},{8,12},{9,13},{10,... | collective-permute-start | bytes 1572872 | tf_op jit(solution)/shard_map/ppermute | solution.py:301
  39.1 21.4 %collective-permute-start.13 = (bf16[16,128,128]{2,1,0:T(8,128)(2,1)S(1)}, bf16[16,128,128]{2,1,0:T(8,128)(2,1)S(1)}, u32[]{:S(2)}, u32[]{:S(2)}) collective-permute-start(bf16[16,128,128]{2,1,0:T(8,128)(2,1)S(1)} %shard_map.53.refs_3_), channel_id=1, source_target_pairs={{0,1},{1,0},{2,3},{3,2},{4,5},{5,4},{6,7},{7,6},{8,9},{9,8},{10,11... | collective-permute-start | bytes 1572872 | tf_op jit(solution)/shard_map/ppermute | solution.py:301
  39.2 21.4 %collective-permute-start.14 = (bf16[16,128,128]{2,1,0:T(8,128)(2,1)S(1)}, bf16[16,128,128]{2,1,0:T(8,128)(2,1)S(1)}, u32[]{:S(2)}, u32[]{:S(2)}) collective-permute-start(bf16[16,128,128]{2,1,0:T(8,128)(2,1)S(1)} %shard_map.53.refs_3_), channel_id=1, source_target_pairs={{0,8},{1,9},{2,10},{3,11},{4,12},{5,13},{6,14},{7,15},{8,0},{9,1},... | collective-permute-start | bytes 1572872 | tf_op jit(solution)/shard_map/ppermute | solution.py:301
  39.8 20.8 %collective-permute-start.15 = (bf16[16,128,128]{2,1,0:T(8,128)(2,1)S(1)}, bf16[16,128,128]{2,1,0:T(8,128)(2,1)S(1)}, u32[]{:S(2)}, u32[]{:S(2)}) collective-permute-start(bf16[16,128,128]{2,1,0:T(8,128)(2,1)S(1)} %shard_map.53.refs_3_), channel_id=1, source_target_pairs={{0,4},{1,5},{2,6},{3,7},{4,0},{5,1},{6,2},{7,3},{8,12},{9,13},{10,... | collective-permute-start | bytes 1572872 | tf_op jit(solution)/shard_map/ppermute | solution.py:301
  39.8 20.8 %collective-permute-start.16 = (bf16[16,128,128]{2,1,0:T(8,128)(2,1)S(1)}, bf16[16,128,128]{2,1,0:T(8,128)(2,1)S(1)}, u32[]{:S(2)}, u32[]{:S(2)}) collective-permute-start(bf16[16,128,128]{2,1,0:T(8,128)(2,1)S(1)} %collective-permute-done.9.refs_0_.refs_4_), channel_id=1, source_target_pairs={{0,4},{1,5},{2,6},{3,7},{4,0},{5,1},{6,2},{7,3},{8,12},{9,13},{10,... | collective-permute-start | bytes 1572872 | tf_op jit(solution)/shard_map/ppermute | solution.py:301
  40.3 9.9 %collective-permute-start.4 = (bf16[12,16,128]{2,1,0:T(8,128)(2,1)S(1)}, bf16[12,16,128]{2,1,0:T(8,128)(2,1)S(1)}, u32[]{:S(2)}, u32[]{:S(2)}) collective-permute-start(bf16[12,16,128]{2,1,0:T(8,128)(2,1)S(1)} %get-tuple-element.26), channel_id=1, source_target_pairs={{0,2},{1,3},{2,0},{3,1},{4,6},{5,7},{6,4},{7,5},{8,10},{9,11},{10,... | collective-permute-start | bytes 147464 | tf_op jit(solution)/shard_map/ppermute | solution.py:301
  50.2 6.2 %collective-permute-start.3 = (bf16[12,16,128]{2,1,0:T(8,128)(2,1)S(1)}, bf16[12,16,128]{2,1,0:T(8,128)(2,1)S(1)}, u32[]{:S(2)}, u32[]{:S(2)}) collective-permute-start(bf16[12,16,128]{2,1,0:T(8,128)(2,1)S(1)} %get-tuple-element.25), channel_id=1, source_target_pairs={{0,3},{1,2},{2,1},{3,0},{4,7},{5,6},{6,5},{7,4},{8,11},{9,10},{10,... | collective-permute-start | bytes 147464 | tf_op jit(solution)/shard_map/ppermute | solution.py:301
  56.4 4.1 %collective-permute-start.2 = (bf16[12,16,128]{2,1,0:T(8,128)(2,1)S(1)}, bf16[12,16,128]{2,1,0:T(8,128)(2,1)S(1)}, u32[]{:S(2)}, u32[]{:S(2)}) collective-permute-start(bf16[12,16,128]{2,1,0:T(8,128)(2,1)S(1)} %get-tuple-element.24), channel_id=1, source_target_pairs={{0,1},{1,0},{2,3},{3,2},{4,5},{5,4},{6,7},{7,6},{8,9},{9,8},{10,11... | collective-permute-start | bytes 147464 | tf_op jit(solution)/shard_map/ppermute | solution.py:301
  60.6 2.5 %collective-permute-start.17 = (bf16[16,128,128]{2,1,0:T(8,128)(2,1)S(1)}, bf16[16,128,128]{2,1,0:T(8,128)(2,1)S(1)}, u32[]{:S(2)}, u32[]{:S(2)}) collective-permute-start(bf16[16,128,128]{2,1,0:T(8,128)(2,1)S(1)} %shard_map.54.refs_5_), channel_id=1, source_target_pairs={{0,4},{1,5},{2,6},{3,7},{4,0},{5,1},{6,2},{7,3},{8,12},{9,13},{10,... | collective-permute-start | bytes 1572872 | tf_op jit(solution)/shard_map/ppermute | solution.py:301
  60.7 2.6 %collective-permute-start.18 = (bf16[16,128,128]{2,1,0:T(8,128)(2,1)S(1)}, bf16[16,128,128]{2,1,0:T(8,128)(2,1)S(1)}, u32[]{:S(2)}, u32[]{:S(2)}) collective-permute-start(bf16[16,128,128]{2,1,0:T(8,128)(2,1)S(1)} %collective-permute-done.14.refs_1_.refs_6_), channel_id=1, source_target_pairs={{0,4},{1,5},{2,6},{3,7},{4,0},{5,1},{6,2},{7,3},{8,12},{9,13},{10,... | collective-permute-start | bytes 1572872 | tf_op jit(solution)/shard_map/ppermute | solution.py:301
  61.2 8.4 %collective-permute-start.19 = (bf16[8,128,128]{2,1,0:T(8,128)(2,1)S(1)}, bf16[8,128,128]{2,1,0:T(8,128)(2,1)S(1)}, u32[]{:S(2)}, u32[]{:S(2)}) collective-permute-start(bf16[8,128,128]{2,1,0:T(8,128)(2,1)S(1)} %slice.108), channel_id=1, source_target_pairs={{0,8},{1,9},{2,10},{3,11},{4,12},{5,13},{6,14},{7,15},{8,0},{9,1},... | collective-permute-start | bytes 786440 | tf_op jit(solution)/shard_map/ppermute | solution.py:301
  61.8 8.1 %collective-permute-start.20 = (bf16[8,128,128]{2,1,0:T(8,128)(2,1)S(1)}, bf16[8,128,128]{2,1,0:T(8,128)(2,1)S(1)}, u32[]{:S(2)}, u32[]{:S(2)}) collective-permute-start(bf16[8,128,128]{2,1,0:T(8,128)(2,1)S(1)} %slice.109), channel_id=1, source_target_pairs={{0,1},{1,0},{2,3},{3,2},{4,5},{5,4},{6,7},{7,6},{8,9},{9,8},{10,11... | collective-permute-start | bytes 786440 | tf_op jit(solution)/shard_map/ppermute | solution.py:301
  69.6 1.5 %collective-permute-start.21 = (bf16[8,128,128]{2,1,0:T(8,128)(2,1)S(1)}, bf16[8,128,128]{2,1,0:T(8,128)(2,1)S(1)}, u32[]{:S(2)}, u32[]{:S(2)}) collective-permute-start(bf16[8,128,128]{2,1,0:T(8,128)(2,1)S(1)} %shard_map.56.refs_0_), channel_id=1, source_target_pairs={{0,4},{1,5},{2,6},{3,7},{4,0},{5,1},{6,2},{7,3},{8,12},{9,13},{10,... | collective-permute-start | bytes 786440 | tf_op jit(solution)/shard_map/ppermute | solution.py:301
  69.9 1.6 %collective-permute-start.22 = (bf16[8,128,128]{2,1,0:T(8,128)(2,1)S(1)}, bf16[8,128,128]{2,1,0:T(8,128)(2,1)S(1)}, u32[]{:S(2)}, u32[]{:S(2)}) collective-permute-start(bf16[8,128,128]{2,1,0:T(8,128)(2,1)S(1)} %shard_map.57.refs_1_), channel_id=1, source_target_pairs={{0,4},{1,5},{2,6},{3,7},{4,0},{5,1},{6,2},{7,3},{8,12},{9,13},{10,... | collective-permute-start | bytes 786440 | tf_op jit(solution)/shard_map/ppermute | solution.py:301
  (2 other events, 1.9 us)

commit v12 on v7

--- a/solution.py
+++ b/solution.py
@@ -66,16 +66,18 @@
     return (now, prev)
 
 
-def filter_kernel(per_piece, n_row, starts, ids_ref, where_ref, zt_ref, *refs):
-    bufs, (out_ref, s_ref, st_ref, z, now, prev, straight, *scattered, sems) = refs[: len(starts)], refs[len(starts) :]
+def filter_kernel(per_piece, n_row, ids_ref, zt_ref, lower_ref, upper_ref, *refs):
+    out_ref, s_ref, st_ref, z, now, prev, straight, *scattered, sems = refs
     tiles, slots = s_ref.shape[:2]
     orb = s_ref.shape[2]
     tile_rows = slots // PER_ROW
     pieces = zt_ref.shape[0]
 
-    for buf, start, i in zip(bufs, starts, range(len(bufs))):
-        tile = where_ref[i]
-        pltpu.make_async_copy(buf, s_ref.at[tile, pl.ds(start, buf.shape[0])], sems.at[tile]).start()
+    half = slots // 2
+    for tile in range(tiles):
+        other = tile % n_row * (tiles // n_row) + tile // n_row
+        pltpu.make_async_copy(lower_ref.at[tile], s_ref.at[tile, pl.ds(0, half)], sems.at[tile]).start()
+        pltpu.make_async_copy(upper_ref.at[other], s_ref.at[tile, pl.ds(half, half)], sems.at[tile]).start()
 
     for p in range(pieces):
         for b in range(per_piece):
@@ -131,52 +133,19 @@
             out_ref[p, 1, :, b * orb : (b + 1) * orb] = prev[g].astype(out_ref.dtype)
 
 
-def gather_tiles(own, n_col, n_row):
-    col, row = lax.axis_index("col"), lax.axis_index("row")
-    half = own.shape[0] // 2
-
-    def send(buf, flip_col, flip_row):
-        pairs = [
-            (c * n_row + r, (c ^ flip_col) * n_row + (r ^ flip_row))
-            for c in range(n_col)
-            for r in range(n_row)
-        ]
-        return lax.ppermute(buf, LANES, pairs)
-
-    near = send(own, 0, 1)
-    over_own = send(own, 2, 0)
-    far = send(own, 0, 3)
-    over_near = send(near, 2, 0)
-    last = send(far, 0, 1)
-    over_far = send(far, 2, 0)
-    over_last = send(last[:half], 2, 0)
-    side_last = send(over_far[half:], 0, 1)
-    held = [
-        (own, 0, 0, 0),
-        (near, 0, 1, 0),
-        (over_own, 2, 0, 0),
-        (far, 0, 3, 0),
-        (over_near, 2, 1, 0),
-        (last, 0, 2, 0),
-        (over_far, 2, 3, 0),
-        (over_last, 2, 2, 0),
-        (side_last, 2, 2, half),
-    ]
-    held += [(send(buf, 1, 0), c ^ 1, r, slot) for buf, c, r, slot in held]
-    where = jnp.stack([(col ^ c) * n_row + (row ^ r) for _, c, r, _ in held]).astype(jnp.int32)
-    return [buf for buf, _, _, _ in held], [slot for _, _, _, slot in held], where
-
-
 def gather_plan(vectors, blocks, cols):
     n_dev = lax.axis_size(LANES)
-    n_col, n_row = lax.axis_size("col"), lax.axis_size("row")
+    n_row = lax.axis_size("row")
     rows, width = vectors.shape
     slots, orb = blocks.shape[2:4]
     share = width // n_dev
     per_piece = rows // orb
     n_blocks = n_dev * per_piece
-
-    bufs, starts, where = gather_tiles(blocks[0, 0], n_col, n_row)
+    half = slots // 2
+    bufs = [
+        lax.all_gather(blocks[0, 0, :half], LANES, axis=0),
+        lax.all_gather(blocks[0, 0, half:], LANES[::-1], axis=0),
+    ]
 
     turned = vectors.T.reshape(n_dev, share, rows)
     own_ids = jnp.pad(cols[0, 0].astype(jnp.bfloat16), (0, rows - slots))
@@ -190,10 +159,9 @@
     ids = (local // per_piece * n_row + down) * per_piece + local % per_piece
 
     done = pl.pallas_call(
-        functools.partial(filter_kernel, per_piece, n_row, starts),
+        functools.partial(filter_kernel, per_piece, n_row),
         out_shape=jax.ShapeDtypeStruct((n_dev, 2, share, rows), jnp.bfloat16),
         in_specs=[
-            pl.BlockSpec(memory_space=pltpu.SMEM),
             pl.BlockSpec(memory_space=pltpu.SMEM),
             pl.BlockSpec(memory_space=pltpu.VMEM),
         ]
@@ -206,8 +174,8 @@
             *[pltpu.VMEM((n_blocks, share, orb), jnp.float32)] * (3 + SPLIT),
             pltpu.SemaphoreType.DMA((n_dev,)),
         ],
-        compiler_params=pltpu.CompilerParams(vmem_limit_bytes=32 * 2**20),
-    )(ids, where, zt, *bufs)
+        compiler_params=pltpu.CompilerParams(vmem_limit_bytes=58 * 2**20),
+    )(ids, zt, *bufs)
     back = lax.all_to_all(done, LANES, split_axis=0, concat_axis=0, tiled=True)
     outs = jnp.transpose(back, (1, 3, 0, 2)).reshape(2, rows, width).astype(jnp.float32)
     return outs[0], outs[1]

time: 97.4 us -> 159 us (1.63)
  waiting for transfers between devices: 28 us -> 98.9 us
  starting transfers between devices: 29 us -> 7.46 us
  between operations: 0.78 us -> 14.1 us
  blocking collectives: 16.5 us -> 13.6 us
  Pallas kernels: 15.9 us -> 17.5 us
    all_gather x0 -> x2, waiting for transfers between devices: none -> 85.6 us  [the longest x1 51.3 us: gather_plan(): lax.all_gather(blocks[0, 0, :half], LANES, axis=0)]
    ppermute x17 -> x0, waiting for transfers between devices: 28 us -> none  [send(): return lax.ppermute(buf, LANES, pairs)]
    ppermute x17 -> x0, starting transfers between devices: 24.6 us -> none  [send(): return lax.ppermute(buf, LANES, pairs)]
    all_to_all x1, waiting for transfers between devices: 0.01 us -> 12.6 us  [gather_plan(): lax.all_to_all(jnp.concatenate([turned, own_ids], axis=1), LANES, split_a...]
    all_to_all x1, starting transfers between devices: 4.4 us -> 7.39 us  [gather_plan(): lax.all_to_all(jnp.concatenate([turned, own_ids], axis=1), LANES, split_a...]
    all_to_all x1, blocking collectives: 16.5 us -> 13.6 us  [gather_plan(): back = lax.all_to_all(done, LANES, split_axis=0, concat_axis=0, tiled=True)]
  transfers between devices with their start and end apart: 18 -> 3, of which waited for: 4 -> 3; matrix products, arithmetic and copies ran while one was open for 5% -> 2% of each run, Pallas kernels for 0% -> 0%
where the time goes in v12:
time: 159 us
  waiting for transfers between devices  98.9 us (62%)
  Pallas kernels  17.5 us (11%)
  between operations  14.1 us (9%)
  blocking collectives  13.6 us (9%)
  starting transfers between devices  7.46 us (5%)
  local copies, waits for them, and re-layouts  5.29 us (3%)
  other arithmetic  2.12 us (1%)
    all_gather x1, waiting for transfers between devices, gather_plan(): lax.all_gather(blocks[0, 0, :half], LANES, axis=0)  51.3 us
    all_gather x1, waiting for transfers between devices, gather_plan(): lax.all_gather(blocks[0, 0, half:], LANES[::-1], axis=0)  34.3 us
    pallas_call x1, Pallas kernels, gather_plan(): pl.pallas_call(functools.partial(filter_kernel, per_piece, n_row), out_sh...  17.5 us
    all_to_all x1, blocking collectives, gather_plan(): back = lax.all_to_all(done, LANES, split_axis=0, concat_axis=0, tiled=True)  13.6 us
    all_to_all x1, waiting for transfers between devices, gather_plan(): lax.all_to_all(jnp.concatenate([turned, own_ids], axis=1), LANES, split_a...  12.6 us
    all_to_all x1, starting transfers between devices, gather_plan(): lax.all_to_all(jnp.concatenate([turned, own_ids], axis=1), LANES, split_a...  7.39 us
  transfers between devices with their start and end apart: 3, of which 3 were waited for; matrix products, arithmetic and copies ran while one was open for 2% of the time, Pallas kernels for 0%

profile of v12, /device:TPU:0, one launch (start us, length us, event | category | flops | bytes accessed | tf_op | source)
XLA Modules:
  0.0 158.9 jit_solution(1485747492108396104)
XLA Ops:
  7.2 0.0 all-gather.7.cloned.1.call-start
  7.2 1.9 %fusion.9 = (bf16[1,1,8,128,128]{4,3,2,1,0:T(8,128)(2,1)}, bf16[1,1,8,128,128]{4,3,2,1,0:T(8,128)(2,1)}) fusion(bf16[1,1,16,128,128]{4,3,2,1,0:T(8,128)(2,1)} %param.4), kind=kLoop, calls=%fused_computation.20 | loop fusion | bytes 1048576 | tf_op jit(solution)/shard_map/slice | solution.py:147
  9.1 0.0 all-gather.7.cloned.1.call-update
  9.1 0.0 all-gather.5.cloned.1.call-start
  9.2 0.7 all-gather.5.cloned.1.call-update
  9.9 1.0 copy.10
  10.9 0.7 convert_bitcast_fusion.1
  11.6 0.7 pad_maximum_fusion
  12.3 7.4 %all-to-all-start = ((bf16[16,32,256]{2,1,0:T(8,128)(2,1)}), bf16[16,32,256]{2,1,0:T(8,128)(2,1)S(1)}, u32[]{:S(2)}, u32[]{:S(2)}) async-start(bf16[16,32,256]{2,1,0:T(8,128)(2,1)} %pad_maximum_fusion), calls=%async_computation | async-start | bytes 524288 | tf_op jit(solution)/shard_map/all_to_all | solution.py:153
  19.7 12.6 %all-to-all-done = bf16[16,32,256]{2,1,0:T(8,128)(2,1)S(1)} async-done(((bf16[16,32,256]{2,1,0:T(8,128)(2,1)}), bf16[16,32,256]{2,1,0:T(8,128)(2,1)S(1)}, u32[]{:S(2)}, u32[]{:S(2)}) %all-to-all-start) | async-done | bytes 262176 | tf_op jit(solution)/shard_map/all_to_all | solution.py:153
  32.3 0.7 slice.27.zt_ref
  33.0 0.7 fusion.3.ids_ref
  33.7 34.3 %all-gather.7.cloned.1.call-done = bf16[16,1,8,128,128]{4,3,2,1,0:T(8,128)(2,1)} async-done(((bf16[1,1,8,128,128]{4,3,2,1,0:T(8,128)(2,1)}), bf16[16,1,8,128,128]{4,3,2,1,0:T(8,128)(2,1)}) %all-gather.7.cloned.1.call-update) | async-done | bytes 4194320 | tf_op jit(solution)/shard_map/all_gather | solution.py:147
  68.0 51.3 %all-gather.5.cloned.1.call-done = bf16[16,1,8,128,128]{4,3,2,1,0:T(8,128)(2,1)} async-done(((bf16[1,1,8,128,128]{4,3,2,1,0:T(8,128)(2,1)}), bf16[16,1,8,128,128]{4,3,2,1,0:T(8,128)(2,1)}) %all-gather.5.cloned.1.call-update) | async-done | bytes 4194320 | tf_op jit(solution)/shard_map/all_gather | solution.py:146
  119.3 17.5 %shard_map.50 = bf16[16,2,16,256]{3,2,1,0:T(8,128)(2,1)} custom-call(s32[16,16]{1,0:T(8,128)} %fusion.3.ids_ref, bf16[16,16,256]{2,1,0:T(8,128)(2,1)} %slice.27.zt_ref, bf16[16,8,128,128]{3,2,1,0:T(8,128)(2,1)} %bitcast.12, bf16[16,8,128,128]{3,2,1,0:T(8,128)(2,1)} %bitcast.11), custom_call_target="tpu_custom_call" | custom-call | tf_op jit(solution)/shard_map/pallas_call | solution.py:161
  136.8 13.6 %all_to_all.10 = bf16[16,2,16,256]{3,2,1,0:T(8,128)(2,1)S(1)} all-to-all(bf16[16,2,16,256]{3,2,1,0:T(8,128)(2,1)} %shard_map.50), channel_id=1, replica_groups=mesh['dom'=2,'col'=4,'row'=4] {'col','row'}, dimensions={0} | all-to-all | bytes 524288 | tf_op jit(solution)/shard_map/all_to_all | solution.py:179
  150.4 0.8 copy.12
  151.3 0.8 copy.11
  (6 shorter events, 0.1 us)
Async XLA Ops:
  7.2 60.8 %all-gather.7.cloned.1.call-start = ((), (), s32[]{:S(2)}) async-start(), calls=%async_computation.3 | async-start | bytes 4456448 | tf_op jit(solution)/shard_map/all_gather | solution.py:147
  9.1 110.2 %all-gather.5.cloned.1.call-start = ((), (), s32[]{:S(2)}) async-start(), calls=%async_computation.2 | async-start | bytes 4456448 | tf_op jit(solution)/shard_map/all_gather | solution.py:146
  12.3 20.0 %all-to-all-start = ((bf16[16,32,256]{2,1,0:T(8,128)(2,1)}), bf16[16,32,256]{2,1,0:T(8,128)(2,1)S(1)}, u32[]{:S(2)}, u32[]{:S(2)}) async-start(bf16[16,32,256]{2,1,0:T(8,128)(2,1)} %pad_maximum_fusion), calls=%async_computation | async-start | bytes 524288 | tf_op jit(solution)/shard_map/all_to_all | solution.py:153
Sparse Core Ops, SparseCore 0:
  10.7 57.2 all-gather.6
  70.2 49.0 all-gather.4

commit v13 on v11

--- a/solution.py
+++ b/solution.py
@@ -140,26 +140,62 @@
     )(one, other, *others)
 
 
-def split_kernel(n_col, n_row, vectors_ref, cols_ref, keep_ref, go_ref, known_ref, turned):
+def split_kernel(n_col, n_row, vectors_ref, cols_ref, stay_ref, go_ref, turned):
     col, row = lax.axis_index("col"), lax.axis_index("row")
     count, share, rows = turned.shape
-    orb = keep_ref.shape[2]
+    orb = stay_ref.shape[2]
     per_piece = rows // orb
     whole = vectors_ref[...].T
     for d in range(count):
         turned[d] = whole[d * share : (d + 1) * share]
     orders = [(y, one, three) for y in range(2) for one in range(2) for three in range(2)]
-    for core, out_ref in enumerate((keep_ref, go_ref)):
-        for k, (y, one, three) in enumerate(orders):
-            peer = (col ^ (core + 2 * y)) * n_row + (row ^ one ^ 3 * three)
-            for b in range(per_piece):
-                out_ref[k * per_piece + b] = turned[peer, :, b * orb : (b + 1) * orb]
     ids = cols_ref[...]
     piece = jnp.zeros_like(ids)
     for c in range(1, n_col):
         piece += (ids >= c * per_piece).astype(jnp.int32)
     ids = ids - piece * per_piece + (piece * n_row + row) * per_piece
-    known_ref[0] = ids.astype(jnp.float32).astype(known_ref.dtype)
+    for core, out_ref in enumerate((stay_ref, go_ref)):
+        for k, (y, one, three) in enumerate(orders):
+            peer = (col ^ (core + 2 * y)) * n_row + (row ^ one ^ 3 * three)
+            for b in range(per_piece):
+                out_ref[k * per_piece + b] = turned[peer, :, b * orb : (b + 1) * orb]
+        out_ref[len(orders) * per_piece] = ids.astype(jnp.float32).astype(out_ref.dtype)
+
+
+def regroup_kernel(sources, count, stay_ref, came_ref, *outs):
+    per_piece = (stay_ref.shape[0] - sources) // (sources * count)
+    kept = max(count // 2, 1)
+    for h, out_ref in enumerate(outs):
+        for s in range(2 * sources):
+            ref = stay_ref if s < sources else came_ref
+            ids = ref[sources * count * per_piece + s % sources]
+            if h == 1 and count == 1:
+                out_ref[s : s + 1] = ids.astype(jnp.float32)[:1].astype(jnp.int32)
+                continue
+            for k in range(kept * per_piece):
+                out_ref[s * kept * per_piece + k] = ref[(s % sources * count + h * kept) * per_piece + k]
+            if count > 1:
+                out_ref[2 * sources * kept * per_piece + s] = ids
+
+
+def regroup(stay, came, sources, per_piece):
+    count = (stay.shape[0] // sources - 1) // per_piece
+    _, share, orb = stay.shape
+    if count > 1:
+        out = jax.ShapeDtypeStruct((sources * count * per_piece + 2 * sources, share, orb), stay.dtype)
+        outs = [out, out]
+    else:
+        outs = [
+            jax.ShapeDtypeStruct((2 * sources * per_piece, share, orb), stay.dtype),
+            jax.ShapeDtypeStruct((2 * sources, orb), jnp.int32),
+        ]
+    return pl.pallas_call(
+        functools.partial(regroup_kernel, sources, count),
+        out_shape=outs,
+        in_specs=vmem(2),
+        out_specs=vmem(2),
+        compiler_params=pltpu.CompilerParams(vmem_limit_bytes=2**20),
+    )(stay, came)
 
 
 def place(g, f):
@@ -282,6 +318,13 @@
             out_ref[p, 1, :, b * orb : (b + 1) * orb] = prev[u].astype(out_ref.dtype)
 
 
+def result_kernel(back_ref, last_ref, before_ref):
+    count, _, share, rows = back_ref.shape
+    for i, out_ref in enumerate((last_ref, before_ref)):
+        whole = jnp.concatenate([back_ref[d, i] for d in range(count)], axis=0)
+        out_ref[...] = whole.astype(jnp.float32).T
+
+
 def gather_plan(vectors, blocks, cols):
     n_dev = lax.axis_size(LANES)
     n_col, n_row = lax.axis_size("col"), lax.axis_size("row")
@@ -309,44 +352,29 @@
     over_own = send(own, 2, 0)
 
     own_cols = jnp.broadcast_to(jnp.pad(cols[0, 0], (0, orb - slots)), (share, orb))
-    shares = jax.ShapeDtypeStruct((n_dev // 2 * per_piece, share, orb), vectors.dtype)
-    keep, go, known = pl.pallas_call(
+    shares = jax.ShapeDtypeStruct((n_dev // 2 * per_piece + 1, share, orb), vectors.dtype)
+    stay, go = pl.pallas_call(
         functools.partial(split_kernel, n_col, n_row),
-        out_shape=[shares, shares, jax.ShapeDtypeStruct((1, share, orb), vectors.dtype)],
+        out_shape=[shares, shares],
         in_specs=vmem(2),
-        out_specs=vmem(3),
+        out_specs=vmem(2),
         scratch_shapes=[pltpu.VMEM((n_dev, share, rows), vectors.dtype)],
         compiler_params=pltpu.CompilerParams(vmem_limit_bytes=4 * 2**20),
     )(vectors, own_cols)
-
-    def swap(keep, go, flip_col, flip_row):
-        (keep, known), count = keep, go.shape[0]
-        came = send(jnp.concatenate([go, known]), flip_col, flip_row)
-        return jnp.concatenate([keep, came[:count]]), jnp.concatenate([known, came[count:]])
-
-    parts = swap((keep, known), go, 1, 0)
-
-    near = after(near, over_own, parts[0])
+    stay, go = regroup(stay, send(go, 1, 0), 1, per_piece)
+
+    near = after(near, over_own)
     outer = send(copy_after(own, near), 0, 3, (0, 3))
     over_near = send(near, 2, 0)
-    mine, known = parts
-    mine = mine.reshape(2, 2, -1, share, orb)
-    parts = swap((mine[:, 0].reshape(-1, share, orb), known), mine[:, 1].reshape(-1, share, orb), 2, 0)
+    stay, go = regroup(stay, send(go, 2, 0), 2, per_piece)
+    stay, go = regroup(stay, send(go, 0, 1), 4, per_piece)
     mates = to_mate(own, near, over_own)
-    far = pick((1, 2), inner, outer, over_near, parts[0], *mates)
+    far = pick((1, 2), inner, outer, over_near, go, *mates)
 
     over_far = send(far, 2, 0)
     last = send(far, 0, 1)
-    mine, known = parts
-    mine = mine.reshape(n_col, n_row, -1, share, orb)
-    parts = [(mine[:, 0].reshape(-1, share, orb), known)]
-    for one, three in ((1, 0), (0, 1), (1, 1)):
-        go = mine[:, 2 * one + three].reshape(-1, share, orb)
-        came = send(jnp.concatenate([go, known]), 0, one ^ 3 * three)
-        parts.append((came[: go.shape[0]], came[go.shape[0] :]))
-    mine = jnp.concatenate([part for part, _ in parts])
-    ids = jnp.concatenate([known[:, 0, :slots].astype(jnp.int32) for _, known in parts])
     mates += to_mate(far, over_near)
+    mine, ids = regroup(stay, send(go, 0, 3), 8, per_piece)
     last = after(last, over_far, mine, *mates[3:])
 
     over_last = send(last[:half], 2, 0)
@@ -380,8 +408,14 @@
         *late_bufs,
     )
     back = lax.all_to_all(done, LANES, split_axis=0, concat_axis=0, tiled=True)
-    outs = jnp.transpose(back, (1, 3, 0, 2)).reshape(2, rows, width).astype(jnp.float32)
-    return outs[0], outs[1]
+    whole = jax.ShapeDtypeStruct((rows, width), jnp.float32)
+    return pl.pallas_call(
+        result_kernel,
+        out_shape=[whole, whole],
+        in_specs=vmem(),
+        out_specs=vmem(2),
+        compiler_params=pltpu.CompilerParams(vmem_limit_bytes=4 * 2**20),
+    )(back)
 
 
 def per_device(vectors, blocks, cols):

time: 103 us -> 98.1 us (0.952)
  starting transfers between devices: 23.4 us -> 20.2 us
  local copies, waits for them, and re-layouts: 4.5 us -> 2.65 us
    ppermute x23 -> x22, starting transfers between devices: 23.4 us -> 20.2 us  [send(): return lax.ppermute(buf, LANES, pairs)]
    unnamed x12 -> x6, local copies, waits for them, and re-layouts: 3.64 us -> 1.95 us
    ppermute x23 -> x22, waiting for transfers between devices: 38.5 us -> 38.6 us  [send(): return lax.ppermute(buf, LANES, pairs)]
  transfers between devices with their start and end apart: 23 -> 22, of which waited for: 11 -> 10; matrix products, arithmetic and copies ran while one was open for 0% -> 1% of each run, Pallas kernels for 5% -> 6%
where the time goes in v13:
time: 98.1 us; the launch traced here: 97.9 us
  waiting for transfers between devices  38.6 us (39%)
  Pallas kernels  21.8 us (22%)
  starting transfers between devices  20.2 us (21%)
  blocking collectives  13.8 us (14%)
  local copies, waits for them, and re-layouts  2.65 us (3%)
    ppermute x22, waiting for transfers between devices, send(): return lax.ppermute(buf, LANES, pairs)  38.6 us
    ppermute x22, starting transfers between devices, send(): return lax.ppermute(buf, LANES, pairs)  20.2 us
    pallas_call x1, Pallas kernels, gather_plan(): pl.pallas_call(functools.partial(filter_kernel, early, late, n_col, n_row...  15 us
    all_to_all x1, blocking collectives, gather_plan(): back = lax.all_to_all(done, LANES, split_axis=0, concat_axis=0, tiled=True)  13.8 us
    pallas_call x1, Pallas kernels, load(): pl.pallas_call(functools.partial(load_kernel, len(bufs)), out_shape=[out,...  5.57 us
  transfers between devices with their start and end apart: 22, of which 10 were waited for; matrix products, arithmetic and copies ran while one was open for 1% of the time, Pallas kernels for 6%

profile of v13, /device:TPU:0, one launch (start us, length us, event | category | flops | bytes accessed | tf_op | source)
XLA Modules:
  0.0 97.9 jit_solution(16744343376233244407)
XLA Ops:
  0.6 3.1 %collective-permute-start.4 = (bf16[16,128,128]{2,1,0:T(8,128)(2,1)}, bf16[16,128,128]{2,1,0:T(8,128)(2,1)S(1)}, u32[]{:S(2)}, u32[]{:S(2)}) collective-permute-start(bf16[16,128,128]{2,1,0:T(8,128)(2,1)} %bitcast.3), channel_id=1, source_target_pairs={{0,1},{1,0},{2,3},{3,2},{4,5},{5,4},{6,7},{7,6},{8,9},{9,8},{10,11... | collective-permute-start | bytes 1572872 | tf_op jit(solution)/shard_map/ppermute | solution.py:344
  3.7 1.5 %collective-permute-start.5 = (bf16[16,128,128]{2,1,0:T(8,128)(2,1)}, bf16[16,128,128]{2,1,0:T(8,128)(2,1)S(1)}, u32[]{:S(2)}, u32[]{:S(2)}) collective-permute-start(bf16[16,128,128]{2,1,0:T(8,128)(2,1)} %bitcast.4), channel_id=1, source_target_pairs={{0,8},{1,9},{2,10},{3,11},{4,12},{5,13},{6,14},{7,15},{8,0},{9,1},... | collective-permute-start | bytes 1572872 | tf_op jit(solution)/shard_map/ppermute | solution.py:344
  5.3 0.7 collective-permute-start.6
  5.9 0.7 pad.4
  6.6 0.9 copy-done.2
  7.7 1.2 %collective-permute-done.came_ref = bf16[17,16,128]{2,1,0:T(8,128)(2,1)S(1)} collective-permute-done((bf16[17,16,128]{2,1,0:T(8,128)(2,1)S(1)}, bf16[17,16,128]{2,1,0:T(8,128)(2,1)S(1)}, u32[]{:S(2)}, u32[]{:S(2)}) %collective-permute-start) | collective-permute-done | bytes 69664 | tf_op jit(solution)/shard_map/ppermute | solution.py:344
  9.0 0.6 collective-permute-start.1
  9.5 9.4 %collective-permute-done.1.came_ref = bf16[18,16,128]{2,1,0:T(8,128)(2,1)S(1)} collective-permute-done((bf16[18,16,128]{2,1,0:T(8,128)(2,1)S(1)}, bf16[18,16,128]{2,1,0:T(8,128)(2,1)S(1)}, u32[]{:S(2)}, u32[]{:S(2)}) %collective-permute-start.1) | collective-permute-done | bytes 73760 | tf_op jit(solution)/shard_map/ppermute | solution.py:344
  19.4 1.0 %copy-done = bf16[1,1,16,128,128]{4,3,2,1,0:T(8,128)(2,1)S(1)} copy-done((bf16[1,1,16,128,128]{4,3,2,1,0:T(8,128)(2,1)S(1)}, bf16[1,1,16,128,128]{4,3,2,1,0:T(8,128)(2,1)}, u32[]{:S(2)}) %copy-start) | copy-done | bytes 524312
  20.5 1.7 %collective-permute-start.8 = (bf16[16,128,128]{2,1,0:T(8,128)(2,1)S(1)}, bf16[16,128,128]{2,1,0:T(8,128)(2,1)S(1)}, u32[]{:S(2)}, u32[]{:S(2)}) collective-permute-start(bf16[16,128,128]{2,1,0:T(8,128)(2,1)S(1)} %shard_map.55.refs_0_.refs_1_), channel_id=1, source_target_pairs={{0,8},{1,9},{2,10},{3,11},{4,12},{5,13},{6,14},{7,15},{8,0},{9,1},... | collective-permute-start | bytes 1572872 | tf_op jit(solution)/shard_map/ppermute | solution.py:344
  22.1 5.5 %collective-permute-start.7 = (bf16[16,128,128]{2,1,0:T(8,128)(2,1)S(1)}, bf16[16,128,128]{2,1,0:T(8,128)(2,1)S(1)}, u32[]{:S(2)}, u32[]{:S(2)}) collective-permute-start(bf16[16,128,128]{2,1,0:T(8,128)(2,1)S(1)} %shard_map.56), channel_id=1, source_target_pairs={{0,3},{3,0},{4,7},{7,4},{8,11},{11,8},{12,15},{15,12},{16,19},{19,... | collective-permute-start | bytes 1572872 | tf_op jit(solution)/shard_map/ppermute | solution.py:344
  28.3 11.7 %collective-permute-done.7.other_ref = bf16[16,128,128]{2,1,0:T(8,128)(2,1)S(1)} collective-permute-done((bf16[16,128,128]{2,1,0:T(8,128)(2,1)S(1)}, bf16[16,128,128]{2,1,0:T(8,128)(2,1)S(1)}, u32[]{:S(2)}, u32[]{:S(2)}) %collective-permute-start.7) | collective-permute-done | bytes 524320 | tf_op jit(solution)/shard_map/ppermute | solution.py:344
  40.1 0.6 collective-permute-start.13
  41.2 3.5 %collective-permute-start.3 = (bf16[24,16,128]{2,1,0:T(8,128)(2,1)S(1)}, bf16[24,16,128]{2,1,0:T(8,128)(2,1)S(1)}, u32[]{:S(2)}, u32[]{:S(2)}) collective-permute-start(bf16[24,16,128]{2,1,0:T(8,128)(2,1)S(1)} %get-tuple-element.21.refs_1_), channel_id=1, source_target_pairs={{0,3},{1,2},{2,1},{3,0},{4,7},{5,6},{6,5},{7,4},{8,11},{9,10},{10,... | collective-permute-start | bytes 294920 | tf_op jit(solution)/shard_map/ppermute | solution.py:344
  44.7 12.5 %collective-permute-done.3.came_ref = bf16[24,16,128]{2,1,0:T(8,128)(2,1)S(1)} collective-permute-done((bf16[24,16,128]{2,1,0:T(8,128)(2,1)S(1)}, bf16[24,16,128]{2,1,0:T(8,128)(2,1)S(1)}, u32[]{:S(2)}, u32[]{:S(2)}) %collective-permute-start.3) | collective-permute-done | bytes 98336 | tf_op jit(solution)/shard_map/ppermute | solution.py:344
  57.9 0.6 collective-permute-start.18
  58.6 0.7 collective-permute-done.16.refs_12_
  59.3 0.7 collective-permute-done.17.refs_13_
  60.0 5.6 %shard_map.59 = (bf16[14,16,128,128]{3,2,1,0:T(8,128)(2,1)S(1)}, bf16[14,16,128,128]{3,2,1,0:T(8,128)(2,1)S(1)}) custom-call(bf16[16,128,128]{2,1,0:T(8,128)(2,1)S(1)} %bitcast.8, bf16[16,128,128]{2,1,0:T(8,128)(2,1)S(1)} %shard_map.55.refs_0_.refs_1_, bf16[16,128,128]{2,1,0:T(8,128)(2,1)S(1)} %collective-permute-done.5.refs_1_.refs_2_, ...), custom_call_target="tpu_custom_call" | custom-call | bytes 22020096 | tf_op jit(solution)/shard_map/pallas_call | solution.py:250
  65.6 0.6 collective-permute-done.18.refs_0_
  66.8 1.0 %collective-permute-done.20.refs_2_ = bf16[8,128,128]{2,1,0:T(8,128)(2,1)S(1)} collective-permute-done((bf16[8,128,128]{2,1,0:T(8,128)(2,1)S(1)}, bf16[8,128,128]{2,1,0:T(8,128)(2,1)S(1)}, u32[]{:S(2)}, u32[]{:S(2)}) %collective-permute-start.20) | collective-permute-done | bytes 262176 | tf_op jit(solution)/shard_map/ppermute | solution.py:344
  68.1 15.0 %shard_map.62 = bf16[16,2,16,256]{3,2,1,0:T(8,128)(2,1)S(1)} custom-call(s32[16,128]{1,0:T(8,128)S(1)} %get-tuple-element.22.ids_ref, bf16[16,2,16,128]{3,2,1,0:T(8,128)(2,1)S(1)} %bitcast.9, bf16[14,16,128,128]{3,2,1,0:T(8,128)(2,1)S(1)} %get-tuple-element.24.refs_1_.se_ref, bf16[14,16,128,128]{3,2,1,0:T(8,128)(2,1)S(1)} %get-tuple-element.25.ste_ref, ...), custom_call_target="tpu_custom_call" | custom-call | tf_op jit(solution)/shard_map/pallas_call | solution.py:391
  83.2 13.8 %all_to_all.5.back_ref = bf16[16,2,16,256]{3,2,1,0:T(8,128)(2,1)S(1)} all-to-all(bf16[16,2,16,256]{3,2,1,0:T(8,128)(2,1)S(1)} %shard_map.62), channel_id=1, replica_groups=mesh['dom'=2,'col'=4,'row'=4] {'col','row'}, dimensions={0} | all-to-all | bytes 524288 | tf_op jit(solution)/shard_map/all_to_all | solution.py:410
  97.0 0.9 shard_map.63
  (45 shorter events, 3.5 us)
Async XLA Ops:
  0.6 59.4 %copy-start.1 = (bf16[1,1,16,128,128]{4,3,2,1,0:T(8,128)(2,1)S(1)}, bf16[1,1,16,128,128]{4,3,2,1,0:T(8,128)(2,1)}, u32[]{:S(2)}) copy-start(bf16[1,1,16,128,128]{4,3,2,1,0:T(8,128)(2,1)} %param.4) | copy-start | bytes 1572868
  0.6 18.7 %collective-permute-start.4 = (bf16[16,128,128]{2,1,0:T(8,128)(2,1)}, bf16[16,128,128]{2,1,0:T(8,128)(2,1)S(1)}, u32[]{:S(2)}, u32[]{:S(2)}) collective-permute-start(bf16[16,128,128]{2,1,0:T(8,128)(2,1)} %bitcast.3), channel_id=1, source_target_pairs={{0,1},{1,0},{2,3},{3,2},{4,5},{5,4},{6,7},{7,6},{8,9},{9,8},{10,11... | collective-permute-start | bytes 1572872 | tf_op jit(solution)/shard_map/ppermute | solution.py:344
  3.7 15.6 %collective-permute-start.5 = (bf16[16,128,128]{2,1,0:T(8,128)(2,1)}, bf16[16,128,128]{2,1,0:T(8,128)(2,1)S(1)}, u32[]{:S(2)}, u32[]{:S(2)}) collective-permute-start(bf16[16,128,128]{2,1,0:T(8,128)(2,1)} %bitcast.4), channel_id=1, source_target_pairs={{0,8},{1,9},{2,10},{3,11},{4,12},{5,13},{6,14},{7,15},{8,0},{9,1},... | collective-permute-start | bytes 1572872 | tf_op jit(solution)/shard_map/ppermute | solution.py:344
  5.3 22.5 %collective-permute-start.6 = (bf16[16,128,128]{2,1,0:T(8,128)(2,1)}, bf16[16,128,128]{2,1,0:T(8,128)(2,1)S(1)}, u32[]{:S(2)}, u32[]{:S(2)}) collective-permute-start(bf16[16,128,128]{2,1,0:T(8,128)(2,1)} %bitcast.5), channel_id=1, source_target_pairs={{1,2},{2,1},{5,6},{6,5},{9,10},{10,9},{13,14},{14,13},{17,18},{18,... | collective-permute-start | bytes 1572872 | tf_op jit(solution)/shard_map/ppermute | solution.py:344
  7.6 1.3 %collective-permute-start = (bf16[17,16,128]{2,1,0:T(8,128)(2,1)S(1)}, bf16[17,16,128]{2,1,0:T(8,128)(2,1)S(1)}, u32[]{:S(2)}, u32[]{:S(2)}) collective-permute-start(bf16[17,16,128]{2,1,0:T(8,128)(2,1)S(1)} %get-tuple-element.15), channel_id=1, source_target_pairs={{0,4},{1,5},{2,6},{3,7},{4,0},{5,1},{6,2},{7,3},{8,12},{9,13},{10,... | collective-permute-start | bytes 208904 | tf_op jit(solution)/shard_map/ppermute | solution.py:344
  9.0 9.9 %collective-permute-start.1 = (bf16[18,16,128]{2,1,0:T(8,128)(2,1)S(1)}, bf16[18,16,128]{2,1,0:T(8,128)(2,1)S(1)}, u32[]{:S(2)}, u32[]{:S(2)}) collective-permute-start(bf16[18,16,128]{2,1,0:T(8,128)(2,1)S(1)} %get-tuple-element.17), channel_id=1, source_target_pairs={{0,8},{1,9},{2,10},{3,11},{4,12},{5,13},{6,14},{7,15},{8,0},{9,1},... | collective-permute-start | bytes 221192 | tf_op jit(solution)/shard_map/ppermute | solution.py:344
  18.9 8.7 %collective-permute-start.2 = (bf16[20,16,128]{2,1,0:T(8,128)(2,1)S(1)}, bf16[20,16,128]{2,1,0:T(8,128)(2,1)S(1)}, u32[]{:S(2)}, u32[]{:S(2)}) collective-permute-start(bf16[20,16,128]{2,1,0:T(8,128)(2,1)S(1)} %get-tuple-element.19), channel_id=1, source_target_pairs={{0,1},{1,0},{2,3},{3,2},{4,5},{5,4},{6,7},{7,6},{8,9},{9,8},{10,11... | collective-permute-start | bytes 245768 | tf_op jit(solution)/shard_map/ppermute | solution.py:344
  19.3 8.9 %collective-permute-start.9 = (bf16[16,128,128]{2,1,0:T(8,128)(2,1)}, bf16[16,128,128]{2,1,0:T(8,128)(2,1)S(1)}, u32[]{:S(2)}, u32[]{:S(2)}) collective-permute-start(bf16[16,128,128]{2,1,0:T(8,128)(2,1)} %bitcast.6), channel_id=1, source_target_pairs={{0,4},{1,5},{2,6},{3,7},{4,0},{5,1},{6,2},{7,3},{8,12},{9,13},{10,... | collective-permute-start | bytes 1572872 | tf_op jit(solution)/shard_map/ppermute | solution.py:344
  19.4 1.0 %copy-start = (bf16[1,1,16,128,128]{4,3,2,1,0:T(8,128)(2,1)S(1)}, bf16[1,1,16,128,128]{4,3,2,1,0:T(8,128)(2,1)}, u32[]{:S(2)}) copy-start(bf16[1,1,16,128,128]{4,3,2,1,0:T(8,128)(2,1)} %param.4) | copy-start | bytes 1572868
  20.5 19.5 %collective-permute-start.8 = (bf16[16,128,128]{2,1,0:T(8,128)(2,1)S(1)}, bf16[16,128,128]{2,1,0:T(8,128)(2,1)S(1)}, u32[]{:S(2)}, u32[]{:S(2)}) collective-permute-start(bf16[16,128,128]{2,1,0:T(8,128)(2,1)S(1)} %shard_map.55.refs_0_.refs_1_), channel_id=1, source_target_pairs={{0,8},{1,9},{2,10},{3,11},{4,12},{5,13},{6,14},{7,15},{8,0},{9,1},... | collective-permute-start | bytes 1572872 | tf_op jit(solution)/shard_map/ppermute | solution.py:344
  22.1 17.8 %collective-permute-start.7 = (bf16[16,128,128]{2,1,0:T(8,128)(2,1)S(1)}, bf16[16,128,128]{2,1,0:T(8,128)(2,1)S(1)}, u32[]{:S(2)}, u32[]{:S(2)}) collective-permute-start(bf16[16,128,128]{2,1,0:T(8,128)(2,1)S(1)} %shard_map.56), channel_id=1, source_target_pairs={{0,3},{3,0},{4,7},{7,4},{8,11},{11,8},{12,15},{15,12},{16,19},{19,... | collective-permute-start | bytes 1572872 | tf_op jit(solution)/shard_map/ppermute | solution.py:344
  27.7 12.3 %collective-permute-start.10 = (bf16[16,128,128]{2,1,0:T(8,128)(2,1)S(1)}, bf16[16,128,128]{2,1,0:T(8,128)(2,1)S(1)}, u32[]{:S(2)}, u32[]{:S(2)}) collective-permute-start(bf16[16,128,128]{2,1,0:T(8,128)(2,1)S(1)} %shard_map.55.refs_0_.refs_1_), channel_id=1, source_target_pairs={{0,4},{1,5},{2,6},{3,7},{4,0},{5,1},{6,2},{7,3},{8,12},{9,13},{10,... | collective-permute-start | bytes 1572872 | tf_op jit(solution)/shard_map/ppermute | solution.py:344
  27.8 12.2 %collective-permute-start.11 = (bf16[16,128,128]{2,1,0:T(8,128)(2,1)S(1)}, bf16[16,128,128]{2,1,0:T(8,128)(2,1)S(1)}, u32[]{:S(2)}, u32[]{:S(2)}) collective-permute-start(bf16[16,128,128]{2,1,0:T(8,128)(2,1)S(1)} %collective-permute-done.5.refs_1_.refs_2_), channel_id=1, source_target_pairs={{0,4},{1,5},{2,6},{3,7},{4,0},{5,1},{6,2},{7,3},{8,12},{9,13},{10,... | collective-permute-start | bytes 1572872 | tf_op jit(solution)/shard_map/ppermute | solution.py:344
  40.0 17.2 %collective-permute-start.12 = (bf16[16,128,128]{2,1,0:T(8,128)(2,1)S(1)}, bf16[16,128,128]{2,1,0:T(8,128)(2,1)S(1)}, u32[]{:S(2)}, u32[]{:S(2)}) collective-permute-start(bf16[16,128,128]{2,1,0:T(8,128)(2,1)S(1)} %shard_map.57.refs_3_), channel_id=1, source_target_pairs={{0,1},{1,0},{2,3},{3,2},{4,5},{5,4},{6,7},{7,6},{8,9},{9,8},{10,11... | collective-permute-start | bytes 1572872 | tf_op jit(solution)/shard_map/ppermute | solution.py:344
  40.1 17.1 %collective-permute-start.13 = (bf16[16,128,128]{2,1,0:T(8,128)(2,1)S(1)}, bf16[16,128,128]{2,1,0:T(8,128)(2,1)S(1)}, u32[]{:S(2)}, u32[]{:S(2)}) collective-permute-start(bf16[16,128,128]{2,1,0:T(8,128)(2,1)S(1)} %shard_map.57.refs_3_), channel_id=1, source_target_pairs={{0,8},{1,9},{2,10},{3,11},{4,12},{5,13},{6,14},{7,15},{8,0},{9,1},... | collective-permute-start | bytes 1572872 | tf_op jit(solution)/shard_map/ppermute | solution.py:344
  40.7 16.6 %collective-permute-start.14 = (bf16[16,128,128]{2,1,0:T(8,128)(2,1)S(1)}, bf16[16,128,128]{2,1,0:T(8,128)(2,1)S(1)}, u32[]{:S(2)}, u32[]{:S(2)}) collective-permute-start(bf16[16,128,128]{2,1,0:T(8,128)(2,1)S(1)} %shard_map.57.refs_3_), channel_id=1, source_target_pairs={{0,4},{1,5},{2,6},{3,7},{4,0},{5,1},{6,2},{7,3},{8,12},{9,13},{10,... | collective-permute-start | bytes 1572872 | tf_op jit(solution)/shard_map/ppermute | solution.py:344
  40.7 16.6 %collective-permute-start.15 = (bf16[16,128,128]{2,1,0:T(8,128)(2,1)S(1)}, bf16[16,128,128]{2,1,0:T(8,128)(2,1)S(1)}, u32[]{:S(2)}, u32[]{:S(2)}) collective-permute-start(bf16[16,128,128]{2,1,0:T(8,128)(2,1)S(1)} %collective-permute-done.8.refs_0_.refs_4_), channel_id=1, source_target_pairs={{0,4},{1,5},{2,6},{3,7},{4,0},{5,1},{6,2},{7,3},{8,12},{9,13},{10,... | collective-permute-start | bytes 1572872 | tf_op jit(solution)/shard_map/ppermute | solution.py:344
  41.2 16.0 %collective-permute-start.3 = (bf16[24,16,128]{2,1,0:T(8,128)(2,1)S(1)}, bf16[24,16,128]{2,1,0:T(8,128)(2,1)S(1)}, u32[]{:S(2)}, u32[]{:S(2)}) collective-permute-start(bf16[24,16,128]{2,1,0:T(8,128)(2,1)S(1)} %get-tuple-element.21.refs_1_), channel_id=1, source_target_pairs={{0,3},{1,2},{2,1},{3,0},{4,7},{5,6},{6,5},{7,4},{8,11},{9,10},{10,... | collective-permute-start | bytes 294920 | tf_op jit(solution)/shard_map/ppermute | solution.py:344
  57.3 2.0 %collective-permute-start.16 = (bf16[16,128,128]{2,1,0:T(8,128)(2,1)S(1)}, bf16[16,128,128]{2,1,0:T(8,128)(2,1)S(1)}, u32[]{:S(2)}, u32[]{:S(2)}) collective-permute-start(bf16[16,128,128]{2,1,0:T(8,128)(2,1)S(1)} %shard_map.58.refs_5_), channel_id=1, source_target_pairs={{0,4},{1,5},{2,6},{3,7},{4,0},{5,1},{6,2},{7,3},{8,12},{9,13},{10,... | collective-permute-start | bytes 1572872 | tf_op jit(solution)/shard_map/ppermute | solution.py:344
  57.4 2.6 %collective-permute-start.17 = (bf16[16,128,128]{2,1,0:T(8,128)(2,1)S(1)}, bf16[16,128,128]{2,1,0:T(8,128)(2,1)S(1)}, u32[]{:S(2)}, u32[]{:S(2)}) collective-permute-start(bf16[16,128,128]{2,1,0:T(8,128)(2,1)S(1)} %collective-permute-done.13.refs_1_.refs_6_), channel_id=1, source_target_pairs={{0,4},{1,5},{2,6},{3,7},{4,0},{5,1},{6,2},{7,3},{8,12},{9,13},{10,... | collective-permute-start | bytes 1572872 | tf_op jit(solution)/shard_map/ppermute | solution.py:344
  57.9 8.4 %collective-permute-start.18 = (bf16[8,128,128]{2,1,0:T(8,128)(2,1)S(1)}, bf16[8,128,128]{2,1,0:T(8,128)(2,1)S(1)}, u32[]{:S(2)}, u32[]{:S(2)}) collective-permute-start(bf16[8,128,128]{2,1,0:T(8,128)(2,1)S(1)} %slice.8), channel_id=1, source_target_pairs={{0,8},{1,9},{2,10},{3,11},{4,12},{5,13},{6,14},{7,15},{8,0},{9,1},... | collective-permute-start | bytes 786440 | tf_op jit(solution)/shard_map/ppermute | solution.py:344
  58.5 8.1 %collective-permute-start.19 = (bf16[8,128,128]{2,1,0:T(8,128)(2,1)S(1)}, bf16[8,128,128]{2,1,0:T(8,128)(2,1)S(1)}, u32[]{:S(2)}, u32[]{:S(2)}) collective-permute-start(bf16[8,128,128]{2,1,0:T(8,128)(2,1)S(1)} %slice.9), channel_id=1, source_target_pairs={{0,1},{1,0},{2,3},{3,2},{4,5},{5,4},{6,7},{7,6},{8,9},{9,8},{10,11... | collective-permute-start | bytes 786440 | tf_op jit(solution)/shard_map/ppermute | solution.py:344
  66.2 1.5 %collective-permute-start.20 = (bf16[8,128,128]{2,1,0:T(8,128)(2,1)S(1)}, bf16[8,128,128]{2,1,0:T(8,128)(2,1)S(1)}, u32[]{:S(2)}, u32[]{:S(2)}) collective-permute-start(bf16[8,128,128]{2,1,0:T(8,128)(2,1)S(1)} %shard_map.60.refs_0_), channel_id=1, source_target_pairs={{0,4},{1,5},{2,6},{3,7},{4,0},{5,1},{6,2},{7,3},{8,12},{9,13},{10,... | collective-permute-start | bytes 786440 | tf_op jit(solution)/shard_map/ppermute | solution.py:344
  66.6 1.6 %collective-permute-start.21 = (bf16[8,128,128]{2,1,0:T(8,128)(2,1)S(1)}, bf16[8,128,128]{2,1,0:T(8,128)(2,1)S(1)}, u32[]{:S(2)}, u32[]{:S(2)}) collective-permute-start(bf16[8,128,128]{2,1,0:T(8,128)(2,1)S(1)} %shard_map.61.refs_1_), channel_id=1, source_target_pairs={{0,4},{1,5},{2,6},{3,7},{4,0},{5,1},{6,2},{7,3},{8,12},{9,13},{10,... | collective-permute-start | bytes 786440 | tf_op jit(solution)/shard_map/ppermute | solution.py:344
  (1 other events, 0.9 us)

commit v14 on v13

--- a/solution.py
+++ b/solution.py
@@ -12,6 +12,7 @@
 SPLIT = 4
 GATHER_LIMIT = 12 * 2**20
 LANES = ("col", "row")
+INNER = (1, 2)
 
 
 def onehot_sum(selected, high_part, low_part):
@@ -93,24 +94,6 @@
     )(value, *others)
 
 
-def copy_kernel(value_ref, *refs):
-    out_ref, sem = refs[-2:]
-    copy = pltpu.make_async_copy(value_ref, out_ref, sem)
-    copy.start()
-    copy.wait()
-
-
-def copy_after(value, *others):
-    return pl.pallas_call(
-        copy_kernel,
-        out_shape=jax.ShapeDtypeStruct(value.shape, value.dtype),
-        in_specs=[pl.BlockSpec(memory_space=pltpu.HBM)] + anywhere(len(others)),
-        out_specs=anywhere()[0],
-        scratch_shapes=[pltpu.SemaphoreType.DMA(())],
-        compiler_params=pltpu.CompilerParams(vmem_limit_bytes=2**20),
-    )(value, *others)
-
-
 def pick_kernel(rows, one_ref, other_ref, *refs):
     out_ref, sem = refs[-2:]
     row = lax.axis_index("row")
@@ -348,7 +331,7 @@
 
     own = blocks[0, 0]
     near = send(own, 0, 1)
-    inner = send(own, 0, 3, (1, 2))
+    inner = send(own, 0, 3, INNER)
     over_own = send(own, 2, 0)
 
     own_cols = jnp.broadcast_to(jnp.pad(cols[0, 0], (0, orb - slots)), (share, orb))
@@ -364,29 +347,30 @@
     stay, go = regroup(stay, send(go, 1, 0), 1, per_piece)
 
     near = after(near, over_own)
-    outer = send(copy_after(own, near), 0, 3, (0, 3))
     over_near = send(near, 2, 0)
+    crossed = send(near, 0, 3, INNER)
+    outward = send(inner, 0, 1, INNER)
     stay, go = regroup(stay, send(go, 2, 0), 2, per_piece)
     stay, go = regroup(stay, send(go, 0, 1), 4, per_piece)
     mates = to_mate(own, near, over_own)
-    far = pick((1, 2), inner, outer, over_near, go, *mates)
-
-    over_far = send(far, 2, 0)
-    last = send(far, 0, 1)
-    mates += to_mate(far, over_near)
+    two = pick(INNER, crossed, outward, over_near, go, *mates)
+
+    over_two = send(two, 2, 0)
+    outer = send(crossed, 0, 1, INNER)
+    mates += to_mate(two, over_near)
     mine, ids = regroup(stay, send(go, 0, 3), 8, per_piece)
-    last = after(last, over_far, mine, *mates[3:])
-
-    over_last = send(last[:half], 2, 0)
-    side_last = send(over_far[half:], 0, 1)
-    mates += to_mate(last, over_far)
-    se, ste = load([own, near, over_own, far, over_near, last, over_far, *mates])
-    over_last, side_last = after(over_last, se), after(side_last, se)
-
-    early = [(0, 0), (0, 1), (2, 0), (0, 3), (2, 1), (0, 2), (2, 3)]
+    three = pick(INNER, inner, outer, over_two, mine, *mates[3:])
+
+    over_three = send(three[:half], 2, 0)
+    side_three = send(over_two[half:], 0, 1)
+    mates += to_mate(three, over_two)
+    se, ste = load([own, near, over_own, two, over_near, three, over_two, *mates])
+    over_three, side_three = after(over_three, se), after(side_three, se)
+
+    early = [(0, 0), (0, 1), (2, 0), (0, 2), (2, 1), (0, 3), (2, 2)]
     early += [(g ^ 1, f) for g, f in early]
-    late = [(2, 2, 0), (2, 2, half), (3, 2, 0), (3, 2, half)]
-    late_bufs = [over_last, side_last, *to_mate(over_last, side_last)]
+    late = [(2, 3, 0), (2, 3, half), (3, 3, 0), (3, 3, half)]
+    late_bufs = [over_three, side_three, *to_mate(over_three, side_three)]
 
     done = pl.pallas_call(
         functools.partial(filter_kernel, early, late, n_col, n_row),

time: 98.1 us -> 91.8 us (0.936)
  starting transfers between devices: 20.2 us -> 15.7 us
  local copies, waits for them, and re-layouts: 2.65 us -> 1.61 us
  waiting for transfers between devices: 38.6 us -> 37.6 us
    ppermute x22 -> x23, starting transfers between devices: 20.2 us -> 15.7 us  [send(): return lax.ppermute(buf, LANES, pairs)]
    unnamed x6 -> x4, local copies, waits for them, and re-layouts: 1.95 us -> 0.91 us
    ppermute x22 -> x23, waiting for transfers between devices: 38.6 us -> 37.6 us  [send(): return lax.ppermute(buf, LANES, pairs)]
  transfers between devices with their start and end apart: 22 -> 23, of which waited for: 10 -> 12; matrix products, arithmetic and copies ran while one was open for 1% -> 1% of each run, Pallas kernels for 6% -> 6%
where the time goes in v14:
time: 91.8 us; the launch traced here: 91.5 us
  waiting for transfers between devices  37.6 us (41%)
  Pallas kernels  21.8 us (24%)
  starting transfers between devices  15.7 us (17%)
  blocking collectives  14 us (15%)
  local copies, waits for them, and re-layouts  1.61 us (2%)
    ppermute x23, waiting for transfers between devices, send(): return lax.ppermute(buf, LANES, pairs)  37.6 us
    ppermute x23, starting transfers between devices, send(): return lax.ppermute(buf, LANES, pairs)  15.7 us
    pallas_call x1, Pallas kernels, gather_plan(): pl.pallas_call(functools.partial(filter_kernel, early, late, n_col, n_row...  15.1 us
    all_to_all x1, blocking collectives, gather_plan(): back = lax.all_to_all(done, LANES, split_axis=0, concat_axis=0, tiled=True)  14 us
    pallas_call x1, Pallas kernels, load(): pl.pallas_call(functools.partial(load_kernel, len(bufs)), out_shape=[out,...  5.57 us
  transfers between devices with their start and end apart: 23, of which 12 were waited for; matrix products, arithmetic and copies ran while one was open for 1% of the time, Pallas kernels for 6%

profile of v14, /device:TPU:0, one launch (start us, length us, event | category | flops | bytes accessed | tf_op | source)
XLA Modules:
  0.0 91.5 jit_solution(17300242753957955541)
XLA Ops:
  0.6 3.1 %collective-permute-start.4 = (bf16[16,128,128]{2,1,0:T(8,128)(2,1)}, bf16[16,128,128]{2,1,0:T(8,128)(2,1)S(1)}, u32[]{:S(2)}, u32[]{:S(2)}) collective-permute-start(bf16[16,128,128]{2,1,0:T(8,128)(2,1)} %bitcast.4), channel_id=1, source_target_pairs={{0,1},{1,0},{2,3},{3,2},{4,5},{5,4},{6,7},{7,6},{8,9},{9,8},{10,11... | collective-permute-start | bytes 1572872 | tf_op jit(solution)/shard_map/ppermute | solution.py:327
  3.7 1.5 %collective-permute-start.5 = (bf16[16,128,128]{2,1,0:T(8,128)(2,1)}, bf16[16,128,128]{2,1,0:T(8,128)(2,1)S(1)}, u32[]{:S(2)}, u32[]{:S(2)}) collective-permute-start(bf16[16,128,128]{2,1,0:T(8,128)(2,1)} %bitcast.5), channel_id=1, source_target_pairs={{0,8},{1,9},{2,10},{3,11},{4,12},{5,13},{6,14},{7,15},{8,0},{9,1},... | collective-permute-start | bytes 1572872 | tf_op jit(solution)/shard_map/ppermute | solution.py:327
  5.2 0.7 collective-permute-start.7
  6.0 0.7 pad.4
  6.7 0.9 copy-done.1
  8.3 0.9 collective-permute-done.came_ref
  9.8 9.1 %collective-permute-done.1.came_ref = bf16[18,16,128]{2,1,0:T(8,128)(2,1)S(1)} collective-permute-done((bf16[18,16,128]{2,1,0:T(8,128)(2,1)S(1)}, bf16[18,16,128]{2,1,0:T(8,128)(2,1)S(1)}, u32[]{:S(2)}, u32[]{:S(2)}) %collective-permute-start.1) | collective-permute-done | bytes 73760 | tf_op jit(solution)/shard_map/ppermute | solution.py:327
  19.4 0.7 collective-permute-start.6
  20.0 1.7 %collective-permute-start.9 = (bf16[16,128,128]{2,1,0:T(8,128)(2,1)S(1)}, bf16[16,128,128]{2,1,0:T(8,128)(2,1)S(1)}, u32[]{:S(2)}, u32[]{:S(2)}) collective-permute-start(bf16[16,128,128]{2,1,0:T(8,128)(2,1)S(1)} %shard_map.55.refs_1_), channel_id=1, source_target_pairs={{0,8},{1,9},{2,10},{3,11},{4,12},{5,13},{6,14},{7,15},{8,0},{9,1},... | collective-permute-start | bytes 1572872 | tf_op jit(solution)/shard_map/ppermute | solution.py:327
  21.7 1.3 %collective-permute-start.8 = (bf16[16,128,128]{2,1,0:T(8,128)(2,1)S(1)}, bf16[16,128,128]{2,1,0:T(8,128)(2,1)S(1)}, u32[]{:S(2)}, u32[]{:S(2)}) collective-permute-start(bf16[16,128,128]{2,1,0:T(8,128)(2,1)S(1)} %collective-permute-done.7.one_ref), channel_id=1, source_target_pairs={{1,0},{2,3},{5,4},{6,7},{9,8},{10,11},{13,12},{14,15},{17,16},{18,... | collective-permute-start | bytes 1572872 | tf_op jit(solution)/shard_map/ppermute | solution.py:327
  24.0 1.3 %collective-permute-start.13 = (bf16[16,128,128]{2,1,0:T(8,128)(2,1)S(1)}, bf16[16,128,128]{2,1,0:T(8,128)(2,1)S(1)}, u32[]{:S(2)}, u32[]{:S(2)}) collective-permute-start(bf16[16,128,128]{2,1,0:T(8,128)(2,1)S(1)} %collective-permute-done.6.one_ref), channel_id=1, source_target_pairs={{1,0},{2,3},{5,4},{6,7},{9,8},{10,11},{13,12},{14,15},{17,16},{18,... | collective-permute-start | bytes 1572872 | tf_op jit(solution)/shard_map/ppermute | solution.py:327
  25.3 14.5 %collective-permute-done.8.other_ref = bf16[16,128,128]{2,1,0:T(8,128)(2,1)S(1)} collective-permute-done((bf16[16,128,128]{2,1,0:T(8,128)(2,1)S(1)}, bf16[16,128,128]{2,1,0:T(8,128)(2,1)S(1)}, u32[]{:S(2)}, u32[]{:S(2)}) %collective-permute-start.8) | collective-permute-done | bytes 524320 | tf_op jit(solution)/shard_map/ppermute | solution.py:327
  40.5 1.3 %collective-permute-start.3 = (bf16[24,16,128]{2,1,0:T(8,128)(2,1)S(1)}, bf16[24,16,128]{2,1,0:T(8,128)(2,1)S(1)}, u32[]{:S(2)}, u32[]{:S(2)}) collective-permute-start(bf16[24,16,128]{2,1,0:T(8,128)(2,1)S(1)} %get-tuple-element.21.refs_1_), channel_id=1, source_target_pairs={{0,3},{1,2},{2,1},{3,0},{4,7},{5,6},{6,5},{7,4},{8,11},{9,10},{10,... | collective-permute-start | bytes 294920 | tf_op jit(solution)/shard_map/ppermute | solution.py:327
  41.8 5.4 %collective-permute-done.3.came_ref = bf16[24,16,128]{2,1,0:T(8,128)(2,1)S(1)} collective-permute-done((bf16[24,16,128]{2,1,0:T(8,128)(2,1)S(1)}, bf16[24,16,128]{2,1,0:T(8,128)(2,1)S(1)}, u32[]{:S(2)}, u32[]{:S(2)}) %collective-permute-start.3) | collective-permute-done | bytes 98336 | tf_op jit(solution)/shard_map/ppermute | solution.py:327
  47.2 3.4 %collective-permute-done.13.other_ref = bf16[16,128,128]{2,1,0:T(8,128)(2,1)S(1)} collective-permute-done((bf16[16,128,128]{2,1,0:T(8,128)(2,1)S(1)}, bf16[16,128,128]{2,1,0:T(8,128)(2,1)S(1)}, u32[]{:S(2)}, u32[]{:S(2)}) %collective-permute-start.13) | collective-permute-done | bytes 524320 | tf_op jit(solution)/shard_map/ppermute | solution.py:327
  51.3 0.6 collective-permute-start.19
  51.9 0.7 collective-permute-done.17.refs_12_
  52.6 0.7 collective-permute-done.18.refs_13_
  53.4 5.6 %shard_map.58 = (bf16[14,16,128,128]{3,2,1,0:T(8,128)(2,1)S(1)}, bf16[14,16,128,128]{3,2,1,0:T(8,128)(2,1)S(1)}) custom-call(bf16[16,128,128]{2,1,0:T(8,128)(2,1)S(1)} %bitcast.8, bf16[16,128,128]{2,1,0:T(8,128)(2,1)S(1)} %shard_map.55.refs_1_, bf16[16,128,128]{2,1,0:T(8,128)(2,1)S(1)} %collective-permute-done.5.refs_1_.refs_2_, ...), custom_call_target="tpu_custom_call" | custom-call | bytes 22020096 | tf_op jit(solution)/shard_map/pallas_call | solution.py:233
  59.0 0.6 collective-permute-done.19.refs_0_
  60.1 1.0 %collective-permute-done.21.refs_2_ = bf16[8,128,128]{2,1,0:T(8,128)(2,1)S(1)} collective-permute-done((bf16[8,128,128]{2,1,0:T(8,128)(2,1)S(1)}, bf16[8,128,128]{2,1,0:T(8,128)(2,1)S(1)}, u32[]{:S(2)}, u32[]{:S(2)}) %collective-permute-start.21) | collective-permute-done | bytes 262176 | tf_op jit(solution)/shard_map/ppermute | solution.py:327
  61.5 15.1 %shard_map.61 = bf16[16,2,16,256]{3,2,1,0:T(8,128)(2,1)S(1)} custom-call(s32[16,128]{1,0:T(8,128)S(1)} %get-tuple-element.22.ids_ref, bf16[16,2,16,128]{3,2,1,0:T(8,128)(2,1)S(1)} %bitcast.3, bf16[14,16,128,128]{3,2,1,0:T(8,128)(2,1)S(1)} %get-tuple-element.24.refs_1_.se_ref, bf16[14,16,128,128]{3,2,1,0:T(8,128)(2,1)S(1)} %get-tuple-element.25.ste_ref, ...), custom_call_target="tpu_custom_call" | custom-call | tf_op jit(solution)/shard_map/pallas_call | solution.py:375
  76.6 14.0 %all_to_all.5.back_ref = bf16[16,2,16,256]{3,2,1,0:T(8,128)(2,1)S(1)} all-to-all(bf16[16,2,16,256]{3,2,1,0:T(8,128)(2,1)S(1)} %shard_map.61), channel_id=1, replica_groups=mesh['dom'=2,'col'=4,'row'=4] {'col','row'}, dimensions={0} | all-to-all | bytes 524288 | tf_op jit(solution)/shard_map/all_to_all | solution.py:394
  90.6 0.9 shard_map.62
  (44 shorter events, 5.1 us)
Async XLA Ops:
  0.6 52.8 %copy-start = (bf16[1,1,16,128,128]{4,3,2,1,0:T(8,128)(2,1)S(1)}, bf16[1,1,16,128,128]{4,3,2,1,0:T(8,128)(2,1)}, u32[]{:S(2)}) copy-start(bf16[1,1,16,128,128]{4,3,2,1,0:T(8,128)(2,1)} %param.4) | copy-start | bytes 1572868
  0.6 18.7 %collective-permute-start.4 = (bf16[16,128,128]{2,1,0:T(8,128)(2,1)}, bf16[16,128,128]{2,1,0:T(8,128)(2,1)S(1)}, u32[]{:S(2)}, u32[]{:S(2)}) collective-permute-start(bf16[16,128,128]{2,1,0:T(8,128)(2,1)} %bitcast.4), channel_id=1, source_target_pairs={{0,1},{1,0},{2,3},{3,2},{4,5},{5,4},{6,7},{7,6},{8,9},{9,8},{10,11... | collective-permute-start | bytes 1572872 | tf_op jit(solution)/shard_map/ppermute | solution.py:327
  3.7 15.6 %collective-permute-start.5 = (bf16[16,128,128]{2,1,0:T(8,128)(2,1)}, bf16[16,128,128]{2,1,0:T(8,128)(2,1)S(1)}, u32[]{:S(2)}, u32[]{:S(2)}) collective-permute-start(bf16[16,128,128]{2,1,0:T(8,128)(2,1)} %bitcast.5), channel_id=1, source_target_pairs={{0,8},{1,9},{2,10},{3,11},{4,12},{5,13},{6,14},{7,15},{8,0},{9,1},... | collective-permute-start | bytes 1572872 | tf_op jit(solution)/shard_map/ppermute | solution.py:327
  5.2 16.5 %collective-permute-start.7 = (bf16[16,128,128]{2,1,0:T(8,128)(2,1)}, bf16[16,128,128]{2,1,0:T(8,128)(2,1)S(1)}, u32[]{:S(2)}, u32[]{:S(2)}) collective-permute-start(bf16[16,128,128]{2,1,0:T(8,128)(2,1)} %bitcast.6), channel_id=1, source_target_pairs={{1,2},{2,1},{5,6},{6,5},{9,10},{10,9},{13,14},{14,13},{17,18},{18,... | collective-permute-start | bytes 1572872 | tf_op jit(solution)/shard_map/ppermute | solution.py:327
  5.9 17.5 %collective-permute-start.10 = (bf16[16,128,128]{2,1,0:T(8,128)(2,1)}, bf16[16,128,128]{2,1,0:T(8,128)(2,1)S(1)}, u32[]{:S(2)}, u32[]{:S(2)}) collective-permute-start(bf16[16,128,128]{2,1,0:T(8,128)(2,1)} %bitcast.7), channel_id=1, source_target_pairs={{0,4},{1,5},{2,6},{3,7},{4,0},{5,1},{6,2},{7,3},{8,12},{9,13},{10,... | collective-permute-start | bytes 1572872 | tf_op jit(solution)/shard_map/ppermute | solution.py:327
  7.7 1.5 %collective-permute-start = (bf16[17,16,128]{2,1,0:T(8,128)(2,1)S(1)}, bf16[17,16,128]{2,1,0:T(8,128)(2,1)S(1)}, u32[]{:S(2)}, u32[]{:S(2)}) collective-permute-start(bf16[17,16,128]{2,1,0:T(8,128)(2,1)S(1)} %get-tuple-element.15), channel_id=1, source_target_pairs={{0,4},{1,5},{2,6},{3,7},{4,0},{5,1},{6,2},{7,3},{8,12},{9,13},{10,... | collective-permute-start | bytes 208904 | tf_op jit(solution)/shard_map/ppermute | solution.py:327
  9.2 9.7 %collective-permute-start.1 = (bf16[18,16,128]{2,1,0:T(8,128)(2,1)S(1)}, bf16[18,16,128]{2,1,0:T(8,128)(2,1)S(1)}, u32[]{:S(2)}, u32[]{:S(2)}) collective-permute-start(bf16[18,16,128]{2,1,0:T(8,128)(2,1)S(1)} %get-tuple-element.17), channel_id=1, source_target_pairs={{0,8},{1,9},{2,10},{3,11},{4,12},{5,13},{6,14},{7,15},{8,0},{9,1},... | collective-permute-start | bytes 221192 | tf_op jit(solution)/shard_map/ppermute | solution.py:327
  18.9 4.5 %collective-permute-start.2 = (bf16[20,16,128]{2,1,0:T(8,128)(2,1)S(1)}, bf16[20,16,128]{2,1,0:T(8,128)(2,1)S(1)}, u32[]{:S(2)}, u32[]{:S(2)}) collective-permute-start(bf16[20,16,128]{2,1,0:T(8,128)(2,1)S(1)} %get-tuple-element.19), channel_id=1, source_target_pairs={{0,1},{1,0},{2,3},{3,2},{4,5},{5,4},{6,7},{7,6},{8,9},{9,8},{10,11... | collective-permute-start | bytes 245768 | tf_op jit(solution)/shard_map/ppermute | solution.py:327
  19.4 4.6 %collective-permute-start.6 = (bf16[16,128,128]{2,1,0:T(8,128)(2,1)S(1)}, bf16[16,128,128]{2,1,0:T(8,128)(2,1)S(1)}, u32[]{:S(2)}, u32[]{:S(2)}) collective-permute-start(bf16[16,128,128]{2,1,0:T(8,128)(2,1)S(1)} %shard_map.55.refs_1_), channel_id=1, source_target_pairs={{1,2},{2,1},{5,6},{6,5},{9,10},{10,9},{13,14},{14,13},{17,18},{18,... | collective-permute-start | bytes 1572872 | tf_op jit(solution)/shard_map/ppermute | solution.py:327
  20.0 19.7 %collective-permute-start.9 = (bf16[16,128,128]{2,1,0:T(8,128)(2,1)S(1)}, bf16[16,128,128]{2,1,0:T(8,128)(2,1)S(1)}, u32[]{:S(2)}, u32[]{:S(2)}) collective-permute-start(bf16[16,128,128]{2,1,0:T(8,128)(2,1)S(1)} %shard_map.55.refs_1_), channel_id=1, source_target_pairs={{0,8},{1,9},{2,10},{3,11},{4,12},{5,13},{6,14},{7,15},{8,0},{9,1},... | collective-permute-start | bytes 1572872 | tf_op jit(solution)/shard_map/ppermute | solution.py:327
  21.7 18.0 %collective-permute-start.8 = (bf16[16,128,128]{2,1,0:T(8,128)(2,1)S(1)}, bf16[16,128,128]{2,1,0:T(8,128)(2,1)S(1)}, u32[]{:S(2)}, u32[]{:S(2)}) collective-permute-start(bf16[16,128,128]{2,1,0:T(8,128)(2,1)S(1)} %collective-permute-done.7.one_ref), channel_id=1, source_target_pairs={{1,0},{2,3},{5,4},{6,7},{9,8},{10,11},{13,12},{14,15},{17,16},{18,... | collective-permute-start | bytes 1572872 | tf_op jit(solution)/shard_map/ppermute | solution.py:327
  23.4 16.3 %collective-permute-start.11 = (bf16[16,128,128]{2,1,0:T(8,128)(2,1)S(1)}, bf16[16,128,128]{2,1,0:T(8,128)(2,1)S(1)}, u32[]{:S(2)}, u32[]{:S(2)}) collective-permute-start(bf16[16,128,128]{2,1,0:T(8,128)(2,1)S(1)} %shard_map.55.refs_1_), channel_id=1, source_target_pairs={{0,4},{1,5},{2,6},{3,7},{4,0},{5,1},{6,2},{7,3},{8,12},{9,13},{10,... | collective-permute-start | bytes 1572872 | tf_op jit(solution)/shard_map/ppermute | solution.py:327
  23.4 16.3 %collective-permute-start.12 = (bf16[16,128,128]{2,1,0:T(8,128)(2,1)S(1)}, bf16[16,128,128]{2,1,0:T(8,128)(2,1)S(1)}, u32[]{:S(2)}, u32[]{:S(2)}) collective-permute-start(bf16[16,128,128]{2,1,0:T(8,128)(2,1)S(1)} %collective-permute-done.5.refs_1_.refs_2_), channel_id=1, source_target_pairs={{0,4},{1,5},{2,6},{3,7},{4,0},{5,1},{6,2},{7,3},{8,12},{9,13},{10,... | collective-permute-start | bytes 1572872 | tf_op jit(solution)/shard_map/ppermute | solution.py:327
  24.0 26.6 %collective-permute-start.13 = (bf16[16,128,128]{2,1,0:T(8,128)(2,1)S(1)}, bf16[16,128,128]{2,1,0:T(8,128)(2,1)S(1)}, u32[]{:S(2)}, u32[]{:S(2)}) collective-permute-start(bf16[16,128,128]{2,1,0:T(8,128)(2,1)S(1)} %collective-permute-done.6.one_ref), channel_id=1, source_target_pairs={{1,0},{2,3},{5,4},{6,7},{9,8},{10,11},{13,12},{14,15},{17,16},{18,... | collective-permute-start | bytes 1572872 | tf_op jit(solution)/shard_map/ppermute | solution.py:327
  39.9 10.7 %collective-permute-start.14 = (bf16[16,128,128]{2,1,0:T(8,128)(2,1)S(1)}, bf16[16,128,128]{2,1,0:T(8,128)(2,1)S(1)}, u32[]{:S(2)}, u32[]{:S(2)}) collective-permute-start(bf16[16,128,128]{2,1,0:T(8,128)(2,1)S(1)} %shard_map.56.refs_3_), channel_id=1, source_target_pairs={{0,8},{1,9},{2,10},{3,11},{4,12},{5,13},{6,14},{7,15},{8,0},{9,1},... | collective-permute-start | bytes 1572872 | tf_op jit(solution)/shard_map/ppermute | solution.py:327
  39.9 10.7 %collective-permute-start.15 = (bf16[16,128,128]{2,1,0:T(8,128)(2,1)S(1)}, bf16[16,128,128]{2,1,0:T(8,128)(2,1)S(1)}, u32[]{:S(2)}, u32[]{:S(2)}) collective-permute-start(bf16[16,128,128]{2,1,0:T(8,128)(2,1)S(1)} %shard_map.56.refs_3_), channel_id=1, source_target_pairs={{0,4},{1,5},{2,6},{3,7},{4,0},{5,1},{6,2},{7,3},{8,12},{9,13},{10,... | collective-permute-start | bytes 1572872 | tf_op jit(solution)/shard_map/ppermute | solution.py:327
  40.0 10.6 %collective-permute-start.16 = (bf16[16,128,128]{2,1,0:T(8,128)(2,1)S(1)}, bf16[16,128,128]{2,1,0:T(8,128)(2,1)S(1)}, u32[]{:S(2)}, u32[]{:S(2)}) collective-permute-start(bf16[16,128,128]{2,1,0:T(8,128)(2,1)S(1)} %collective-permute-done.9.refs_0_.refs_4_), channel_id=1, source_target_pairs={{0,4},{1,5},{2,6},{3,7},{4,0},{5,1},{6,2},{7,3},{8,12},{9,13},{10,... | collective-permute-start | bytes 1572872 | tf_op jit(solution)/shard_map/ppermute | solution.py:327
  40.5 6.7 %collective-permute-start.3 = (bf16[24,16,128]{2,1,0:T(8,128)(2,1)S(1)}, bf16[24,16,128]{2,1,0:T(8,128)(2,1)S(1)}, u32[]{:S(2)}, u32[]{:S(2)}) collective-permute-start(bf16[24,16,128]{2,1,0:T(8,128)(2,1)S(1)} %get-tuple-element.21.refs_1_), channel_id=1, source_target_pairs={{0,3},{1,2},{2,1},{3,0},{4,7},{5,6},{6,5},{7,4},{8,11},{9,10},{10,... | collective-permute-start | bytes 294920 | tf_op jit(solution)/shard_map/ppermute | solution.py:327
  50.7 2.0 %collective-permute-start.17 = (bf16[16,128,128]{2,1,0:T(8,128)(2,1)S(1)}, bf16[16,128,128]{2,1,0:T(8,128)(2,1)S(1)}, u32[]{:S(2)}, u32[]{:S(2)}) collective-permute-start(bf16[16,128,128]{2,1,0:T(8,128)(2,1)S(1)} %shard_map.57.refs_5_), channel_id=1, source_target_pairs={{0,4},{1,5},{2,6},{3,7},{4,0},{5,1},{6,2},{7,3},{8,12},{9,13},{10,... | collective-permute-start | bytes 1572872 | tf_op jit(solution)/shard_map/ppermute | solution.py:327
  50.8 2.6 %collective-permute-start.18 = (bf16[16,128,128]{2,1,0:T(8,128)(2,1)S(1)}, bf16[16,128,128]{2,1,0:T(8,128)(2,1)S(1)}, u32[]{:S(2)}, u32[]{:S(2)}) collective-permute-start(bf16[16,128,128]{2,1,0:T(8,128)(2,1)S(1)} %collective-permute-done.14.refs_0_.refs_6_), channel_id=1, source_target_pairs={{0,4},{1,5},{2,6},{3,7},{4,0},{5,1},{6,2},{7,3},{8,12},{9,13},{10,... | collective-permute-start | bytes 1572872 | tf_op jit(solution)/shard_map/ppermute | solution.py:327
  51.3 8.4 %collective-permute-start.19 = (bf16[8,128,128]{2,1,0:T(8,128)(2,1)S(1)}, bf16[8,128,128]{2,1,0:T(8,128)(2,1)S(1)}, u32[]{:S(2)}, u32[]{:S(2)}) collective-permute-start(bf16[8,128,128]{2,1,0:T(8,128)(2,1)S(1)} %slice.8), channel_id=1, source_target_pairs={{0,8},{1,9},{2,10},{3,11},{4,12},{5,13},{6,14},{7,15},{8,0},{9,1},... | collective-permute-start | bytes 786440 | tf_op jit(solution)/shard_map/ppermute | solution.py:327
  51.9 8.1 %collective-permute-start.20 = (bf16[8,128,128]{2,1,0:T(8,128)(2,1)S(1)}, bf16[8,128,128]{2,1,0:T(8,128)(2,1)S(1)}, u32[]{:S(2)}, u32[]{:S(2)}) collective-permute-start(bf16[8,128,128]{2,1,0:T(8,128)(2,1)S(1)} %slice.9), channel_id=1, source_target_pairs={{0,1},{1,0},{2,3},{3,2},{4,5},{5,4},{6,7},{7,6},{8,9},{9,8},{10,11... | collective-permute-start | bytes 786440 | tf_op jit(solution)/shard_map/ppermute | solution.py:327
  59.6 1.5 %collective-permute-start.21 = (bf16[8,128,128]{2,1,0:T(8,128)(2,1)S(1)}, bf16[8,128,128]{2,1,0:T(8,128)(2,1)S(1)}, u32[]{:S(2)}, u32[]{:S(2)}) collective-permute-start(bf16[8,128,128]{2,1,0:T(8,128)(2,1)S(1)} %shard_map.59.refs_0_), channel_id=1, source_target_pairs={{0,4},{1,5},{2,6},{3,7},{4,0},{5,1},{6,2},{7,3},{8,12},{9,13},{10,... | collective-permute-start | bytes 786440 | tf_op jit(solution)/shard_map/ppermute | solution.py:327
  59.9 1.6 %collective-permute-start.22 = (bf16[8,128,128]{2,1,0:T(8,128)(2,1)S(1)}, bf16[8,128,128]{2,1,0:T(8,128)(2,1)S(1)}, u32[]{:S(2)}, u32[]{:S(2)}) collective-permute-start(bf16[8,128,128]{2,1,0:T(8,128)(2,1)S(1)} %shard_map.60.refs_1_), channel_id=1, source_target_pairs={{0,4},{1,5},{2,6},{3,7},{4,0},{5,1},{6,2},{7,3},{8,12},{9,13},{10,... | collective-permute-start | bytes 786440 | tf_op jit(solution)/shard_map/ppermute | solution.py:327
  (1 other events, 0.9 us)

commit v15 on v14

--- a/solution.py
+++ b/solution.py
@@ -83,7 +83,7 @@
     pass
 
 
-def after(value, *others):
+def after(value, *others, rank=0):
     return pl.pallas_call(
         nothing,
         out_shape=jax.ShapeDtypeStruct(value.shape, value.dtype),
@@ -91,6 +91,7 @@
         out_specs=anywhere()[0],
         input_output_aliases={0: 0},
         compiler_params=pltpu.CompilerParams(vmem_limit_bytes=2**20),
+        cost_estimate=pl.CostEstimate(flops=0, bytes_accessed=rank * 2**23, transcendentals=0),
     )(value, *others)
 
 
@@ -217,8 +218,7 @@
     lax.fori_loop(0, count // 4, four, 0)
 
 
-def load_kernel(count, *refs):
-    bufs, (s_ref, st_ref, sems) = refs[:count], refs[count:]
+def fill(bufs, s_ref, st_ref, sems):
     copies = [pltpu.make_async_copy(buf, s_ref.at[i], sems.at[i]) for i, buf in enumerate(bufs)]
     for copy in copies:
         copy.start()
@@ -227,31 +227,55 @@
         turn(s_ref, st_ref, i, 0, s_ref.shape[1])
 
 
-def load(bufs):
-    out = jax.ShapeDtypeStruct((len(bufs), *bufs[0].shape), bufs[0].dtype)
-    size = len(bufs) * bufs[0].size
-    return pl.pallas_call(
-        functools.partial(load_kernel, len(bufs)),
-        out_shape=[out, out],
-        in_specs=anywhere(len(bufs)),
-        out_specs=vmem(2),
-        scratch_shapes=[pltpu.SemaphoreType.DMA((len(bufs),))],
-        compiler_params=pltpu.CompilerParams(vmem_limit_bytes=2**20),
-        cost_estimate=pl.CostEstimate(flops=0, bytes_accessed=6 * size, transcendentals=0),
-    )(*bufs)
-
-
-def filter_kernel(early, late, n_col, n_row, ids_ref, zt_ref, se_ref, ste_ref, *refs):
+def grouped(tiles, n_col, n_row):
+    return [[(f, *tiles[g, f]) for f in range(n_row) if (g, f) in tiles] for g in range(n_col)]
+
+
+def spread_vectors(parts_ref, z, n_col, n_row, now=None):
+    per_piece = z.shape[0] // (n_col * n_row)
+    across = [lax.axis_index("col") ^ g for g in range(n_col)]
+    down = [lax.axis_index("row") ^ f for f in range(n_row)]
+    for g in range(n_col):
+        for f in range(n_row):
+            for b in range(per_piece):
+                u = (across[g] * n_row + down[f]) * per_piece + b
+                own = parts_ref[place(g, f) * per_piece + b]
+                z[u] = own
+                if now is not None:
+                    now[u] = own.astype(jnp.float32)
+
+
+def sum_products(groups, n_col, ids_ref, z, straight, scattered):
+    across = [lax.axis_index("col") ^ g for g in range(n_col)]
+    clear(scattered)
+
+    def block_row(t, carry):
+        multiply(t, groups, across, ids_ref, z, straight, scattered)
+        return carry
+
+    lax.fori_loop(0, z.shape[0] // n_col, block_row, 0)
+    total = straight[...]
+    for ref in scattered:
+        total += ref[...]
+    return total
+
+
+def first_kernel(early, n_col, n_row, ids_ref, parts_ref, *refs):
+    bufs, (s_ref, st_ref, sum_ref, z, straight, *scattered, sems) = refs[: len(early)], refs[len(early) :]
+    spread_vectors(parts_ref, z, n_col, n_row)
+    fill(bufs, s_ref, st_ref, sems)
+    tiles = {at: (s_ref, i, st_ref, i) for i, at in enumerate(early)}
+    clear([straight])
+    sum_ref[...] = sum_products(grouped(tiles, n_col, n_row), n_col, ids_ref, z, straight, scattered)
+
+
+def filter_kernel(early, late, n_col, n_row, ids_ref, parts_ref, sum_ref, se_ref, ste_ref, *refs):
     bufs, (out_ref, s_ref, st_ref, z, now, prev, straight, *scattered, sems) = (
         refs[: len(late)],
         refs[len(late) :],
     )
     n_blocks, share, orb = z.shape
-    slots = s_ref.shape[1]
     per_piece = n_blocks // (n_col * n_row)
-    tile_rows = slots // PER_ROW
-    across = [lax.axis_index("col") ^ g for g in range(n_col)]
-    down = [lax.axis_index("row") ^ f for f in range(n_row)]
     rest = sorted({(g, f) for g, f, _ in late})
 
     copies = []
@@ -259,41 +283,30 @@
         target = s_ref.at[rest.index((g, f)), pl.ds(start, buf.shape[0])]
         copies.append(pltpu.make_async_copy(buf, target, sems.at[i]))
         copies[-1].start()
-    for g in range(n_col):
-        for f in range(n_row):
-            for b in range(per_piece):
-                u = (across[g] * n_row + down[f]) * per_piece + b
-                own = zt_ref[place(g, f), b]
-                z[u] = own
-                now[u] = own.astype(jnp.float32)
-    clear([prev])
+    spread_vectors(parts_ref, z, n_col, n_row, prev)
     for copy, buf, (g, f, start) in zip(copies, bufs, late):
         copy.wait()
         turn(s_ref, st_ref, rest.index((g, f)), start, buf.shape[0])
 
-    tiles = {at: (se_ref, i, ste_ref, i) for i, at in enumerate(early)}
-    tiles.update({at: (s_ref, i, st_ref, i) for i, at in enumerate(rest)})
-    groups = [[(f, *tiles[g, f]) for f in range(n_row)] for g in range(n_col)]
+    tiles = {at: (s_ref, i, st_ref, i) for i, at in enumerate(rest)}
+    clear([straight])
+    total = sum_products(grouped(tiles, n_col, n_row), n_col, ids_ref, z, straight, scattered)
+    total += sum_ref[...]
+    now[...] = total
+    z[...] = total.astype(z.dtype)
+
+    tiles.update({at: (se_ref, i, ste_ref, i) for i, at in enumerate(early)})
+    groups = grouped(tiles, n_col, n_row)
 
     def one_step(step, carry):
-        clear(scattered)
-
-        def block_row(t, carry):
-            multiply(t, groups, across, ids_ref, z, straight, scattered)
-            return carry
-
-        lax.fori_loop(0, tile_rows, block_row, 0)
-        total = straight[...]
-        for ref in scattered:
-            total += ref[...]
-        later = step > 0
-        total = jnp.where(later, 2.0, 1.0) * total - jnp.where(later, 1.0, 0.0) * prev[...]
+        total = sum_products(groups, n_col, ids_ref, z, straight, scattered)
+        total = 2.0 * total - prev[...]
         prev[...] = now[...]
         now[...] = total
         z[...] = total.astype(z.dtype)
         return carry
 
-    lax.fori_loop(0, DEG, one_step, 0)
+    lax.fori_loop(1, DEG, one_step, 0)
     for p in range(n_col * n_row):
         for b in range(per_piece):
             u = p * per_piece + b
@@ -346,17 +359,19 @@
     )(vectors, own_cols)
     stay, go = regroup(stay, send(go, 1, 0), 1, per_piece)
 
-    near = after(near, over_own)
-    over_near = send(near, 2, 0)
-    crossed = send(near, 0, 3, INNER)
-    outward = send(inner, 0, 1, INNER)
     stay, go = regroup(stay, send(go, 2, 0), 2, per_piece)
+    mates = to_mate(own)
+    near = after(near, over_own, go, *mates)
+    over_near = after(send(near, 2, 0), rank=3)
+    crossed = after(send(near, 0, 3, INNER), rank=1)
+    inner = after(inner, near)
+    outward = after(send(inner, 0, 1, INNER), rank=1)
     stay, go = regroup(stay, send(go, 0, 1), 4, per_piece)
-    mates = to_mate(own, near, over_own)
+    mates += to_mate(near, over_own)
     two = pick(INNER, crossed, outward, over_near, go, *mates)
 
     over_two = send(two, 2, 0)
-    outer = send(crossed, 0, 1, INNER)
+    outer = after(send(crossed, 0, 1, INNER), rank=1)
     mates += to_mate(two, over_near)
     mine, ids = regroup(stay, send(go, 0, 3), 8, per_piece)
     three = pick(INNER, inner, outer, over_two, mine, *mates[3:])
@@ -364,33 +379,44 @@
     over_three = send(three[:half], 2, 0)
     side_three = send(over_two[half:], 0, 1)
     mates += to_mate(three, over_two)
-    se, ste = load([own, near, over_own, two, over_near, three, over_two, *mates])
-    over_three, side_three = after(over_three, se), after(side_three, se)
-
     early = [(0, 0), (0, 1), (2, 0), (0, 2), (2, 1), (0, 3), (2, 2)]
     early += [(g ^ 1, f) for g, f in early]
+    tiles_of = jax.ShapeDtypeStruct((len(early), slots, orb, orb), blocks.dtype)
+    sums = jax.ShapeDtypeStruct((n_blocks, share, orb), jnp.float32)
+    se, ste, total = pl.pallas_call(
+        functools.partial(first_kernel, early, n_col, n_row),
+        out_shape=[tiles_of, tiles_of, sums],
+        in_specs=smem() + vmem() + anywhere(len(early)),
+        out_specs=vmem(3),
+        scratch_shapes=[
+            pltpu.VMEM((n_blocks, share, orb), jnp.bfloat16),
+            *[pltpu.VMEM((n_blocks, share, orb), jnp.float32)] * (1 + SPLIT),
+            pltpu.SemaphoreType.DMA((len(early),)),
+        ],
+        compiler_params=pltpu.CompilerParams(vmem_limit_bytes=6 * 2**20),
+        cost_estimate=pl.CostEstimate(
+            flops=4 * len(early) * slots * orb * orb * share,
+            bytes_accessed=6 * len(early) * own.size,
+            transcendentals=0,
+        ),
+    )(ids, mine, own, near, over_own, two, over_near, three, over_two, *mates)
+    over_three, side_three = after(over_three, se), after(side_three, se)
     late = [(2, 3, 0), (2, 3, half), (3, 3, 0), (3, 3, half)]
     late_bufs = [over_three, side_three, *to_mate(over_three, side_three)]
 
     done = pl.pallas_call(
         functools.partial(filter_kernel, early, late, n_col, n_row),
         out_shape=jax.ShapeDtypeStruct((n_dev, 2, share, rows), jnp.bfloat16),
-        in_specs=smem() + vmem(3) + anywhere(len(late)),
+        in_specs=smem() + vmem(4) + anywhere(len(late)),
         out_specs=vmem()[0],
         scratch_shapes=[
-            *[pltpu.VMEM((n_dev - len(early), slots, orb, orb), blocks.dtype)] * 2,
+            *[pltpu.VMEM((2, slots, orb, orb), blocks.dtype)] * 2,
             pltpu.VMEM((n_blocks, share, orb), jnp.bfloat16),
             *[pltpu.VMEM((n_blocks, share, orb), jnp.float32)] * (3 + SPLIT),
             pltpu.SemaphoreType.DMA((len(late),)),
         ],
         compiler_params=pltpu.CompilerParams(vmem_limit_bytes=12 * 2**20),
-    )(
-        ids,
-        mine.reshape(n_dev, per_piece, share, orb),
-        se,
-        ste,
-        *late_bufs,
-    )
+    )(ids, mine, total, se, ste, *late_bufs)
     back = lax.all_to_all(done, LANES, split_axis=0, concat_axis=0, tiled=True)
     whole = jax.ShapeDtypeStruct((rows, width), jnp.float32)
     return pl.pallas_call(

time: 91.8 us -> 91.6 us (level)
  waiting for transfers between devices: 37.6 us -> 32.7 us
  starting transfers between devices: 15.7 us -> 19 us
  Pallas kernels: 21.8 us -> 23.6 us
    ppermute x23, waiting for transfers between devices: 37.6 us -> 32.7 us  [send(): return lax.ppermute(buf, LANES, pairs)]
    pallas_call x1, Pallas kernels: 5.57 us -> 9.32 us  [gather_plan(): pl.pallas_call(functools.partial(first_kernel, early, n_col, n_row), out_...]
    ppermute x23, starting transfers between devices: 15.7 us -> 19 us  [send(): return lax.ppermute(buf, LANES, pairs)]
    pallas_call x1, Pallas kernels: 15.1 us -> 13.1 us  [gather_plan(): pl.pallas_call(functools.partial(filter_kernel, early, late, n_col, n_row...]
  transfers between devices with their start and end apart: 23 -> 23, of which waited for: 12 -> 8; matrix products, arithmetic and copies ran while one was open for 1% -> 1% of each run, Pallas kernels for 6% -> 10%
where the time goes in v15:
time: 91.6 us; the launch traced here: 91.4 us
  waiting for transfers between devices  32.7 us (36%)
  Pallas kernels  23.6 us (26%)
  starting transfers between devices  19 us (21%)
  blocking collectives  13.7 us (15%)
  local copies, waits for them, and re-layouts  1.61 us (2%)
    ppermute x23, waiting for transfers between devices, send(): return lax.ppermute(buf, LANES, pairs)  32.7 us
    ppermute x23, starting transfers between devices, send(): return lax.ppermute(buf, LANES, pairs)  19 us
    all_to_all x1, blocking collectives, gather_plan(): back = lax.all_to_all(done, LANES, split_axis=0, concat_axis=0, tiled=True)  13.7 us
    pallas_call x1, Pallas kernels, gather_plan(): pl.pallas_call(functools.partial(filter_kernel, early, late, n_col, n_row...  13.1 us
    pallas_call x1, Pallas kernels, gather_plan(): pl.pallas_call(functools.partial(first_kernel, early, n_col, n_row), out_...  9.32 us
  transfers between devices with their start and end apart: 23, of which 8 were waited for; matrix products, arithmetic and copies ran while one was open for 1% of the time, Pallas kernels for 10%

profile of v15, /device:TPU:0, one launch (start us, length us, event | category | flops | bytes accessed | tf_op | source)
XLA Modules:
  0.0 91.4 jit_solution(7947598640403678628)
XLA Ops:
  0.6 3.0 %collective-permute-start.5 = (bf16[16,128,128]{2,1,0:T(8,128)(2,1)}, bf16[16,128,128]{2,1,0:T(8,128)(2,1)S(1)}, u32[]{:S(2)}, u32[]{:S(2)}) collective-permute-start(bf16[16,128,128]{2,1,0:T(8,128)(2,1)} %bitcast.2), channel_id=1, source_target_pairs={{0,8},{1,9},{2,10},{3,11},{4,12},{5,13},{6,14},{7,15},{8,0},{9,1},... | collective-permute-start | bytes 1572872 | tf_op jit(solution)/shard_map/ppermute | solution.py:340
  3.7 1.6 %collective-permute-start.4 = (bf16[16,128,128]{2,1,0:T(8,128)(2,1)}, bf16[16,128,128]{2,1,0:T(8,128)(2,1)S(1)}, u32[]{:S(2)}, u32[]{:S(2)}) collective-permute-start(bf16[16,128,128]{2,1,0:T(8,128)(2,1)} %bitcast.4), channel_id=1, source_target_pairs={{0,1},{1,0},{2,3},{3,2},{4,5},{5,4},{6,7},{7,6},{8,9},{9,8},{10,11... | collective-permute-start | bytes 1572872 | tf_op jit(solution)/shard_map/ppermute | solution.py:340
  5.2 0.7 collective-permute-start.8
  5.9 0.7 pad.4
  6.6 0.9 copy-done.1
  7.9 1.0 %collective-permute-done.came_ref = bf16[17,16,128]{2,1,0:T(8,128)(2,1)S(1)} collective-permute-done((bf16[17,16,128]{2,1,0:T(8,128)(2,1)S(1)}, bf16[17,16,128]{2,1,0:T(8,128)(2,1)S(1)}, u32[]{:S(2)}, u32[]{:S(2)}) %collective-permute-start) | collective-permute-done | bytes 69664 | tf_op jit(solution)/shard_map/ppermute | solution.py:340
  9.0 0.6 collective-permute-start.1
  9.5 7.8 %collective-permute-done.1.came_ref = bf16[18,16,128]{2,1,0:T(8,128)(2,1)S(1)} collective-permute-done((bf16[18,16,128]{2,1,0:T(8,128)(2,1)S(1)}, bf16[18,16,128]{2,1,0:T(8,128)(2,1)S(1)}, u32[]{:S(2)}, u32[]{:S(2)}) %collective-permute-start.1) | collective-permute-done | bytes 73760 | tf_op jit(solution)/shard_map/ppermute | solution.py:340
  17.4 1.9 %collective-permute-start.2 = (bf16[20,16,128]{2,1,0:T(8,128)(2,1)S(1)}, bf16[20,16,128]{2,1,0:T(8,128)(2,1)S(1)}, u32[]{:S(2)}, u32[]{:S(2)}) collective-permute-start(bf16[20,16,128]{2,1,0:T(8,128)(2,1)S(1)} %get-tuple-element.20.refs_2_), channel_id=1, source_target_pairs={{0,1},{1,0},{2,3},{3,2},{4,5},{5,4},{6,7},{7,6},{8,9},{9,8},{10,11... | collective-permute-start | bytes 245768 | tf_op jit(solution)/shard_map/ppermute | solution.py:340
  19.3 0.8 collective-permute-start.7
  20.1 1.3 %collective-permute-start.9 = (bf16[16,128,128]{2,1,0:T(8,128)(2,1)S(1)}, bf16[16,128,128]{2,1,0:T(8,128)(2,1)S(1)}, u32[]{:S(2)}, u32[]{:S(2)}) collective-permute-start(bf16[16,128,128]{2,1,0:T(8,128)(2,1)S(1)} %shard_map.57.one_ref), channel_id=1, source_target_pairs={{1,0},{2,3},{5,4},{6,7},{9,8},{10,11},{13,12},{14,15},{17,16},{18,... | collective-permute-start | bytes 1572872 | tf_op jit(solution)/shard_map/ppermute | solution.py:340
  21.4 1.6 %collective-permute-start.10 = (bf16[16,128,128]{2,1,0:T(8,128)(2,1)S(1)}, bf16[16,128,128]{2,1,0:T(8,128)(2,1)S(1)}, u32[]{:S(2)}, u32[]{:S(2)}) collective-permute-start(bf16[16,128,128]{2,1,0:T(8,128)(2,1)S(1)} %shard_map.55.refs_1_), channel_id=1, source_target_pairs={{0,8},{1,9},{2,10},{3,11},{4,12},{5,13},{6,14},{7,15},{8,0},{9,1},... | collective-permute-start | bytes 1572872 | tf_op jit(solution)/shard_map/ppermute | solution.py:340
  23.0 0.5 collective-permute-start.12
  23.6 1.3 %collective-permute-start.13 = (bf16[16,128,128]{2,1,0:T(8,128)(2,1)S(1)}, bf16[16,128,128]{2,1,0:T(8,128)(2,1)S(1)}, u32[]{:S(2)}, u32[]{:S(2)}) collective-permute-start(bf16[16,128,128]{2,1,0:T(8,128)(2,1)S(1)} %shard_map.56.one_ref), channel_id=1, source_target_pairs={{1,0},{2,3},{5,4},{6,7},{9,8},{10,11},{13,12},{14,15},{17,16},{18,... | collective-permute-start | bytes 1572872 | tf_op jit(solution)/shard_map/ppermute | solution.py:340
  24.9 12.0 %collective-permute-done.9.refs_0_ = bf16[16,128,128]{2,1,0:T(8,128)(2,1)S(1)} collective-permute-done((bf16[16,128,128]{2,1,0:T(8,128)(2,1)S(1)}, bf16[16,128,128]{2,1,0:T(8,128)(2,1)S(1)}, u32[]{:S(2)}, u32[]{:S(2)}) %collective-permute-start.9) | collective-permute-done | bytes 524320 | tf_op jit(solution)/shard_map/ppermute | solution.py:340
  37.0 1.8 %collective-permute-start.14 = (bf16[16,128,128]{2,1,0:T(8,128)(2,1)S(1)}, bf16[16,128,128]{2,1,0:T(8,128)(2,1)S(1)}, u32[]{:S(2)}, u32[]{:S(2)}) collective-permute-start(bf16[16,128,128]{2,1,0:T(8,128)(2,1)S(1)} %shard_map.60.refs_3_), channel_id=1, source_target_pairs={{0,8},{1,9},{2,10},{3,11},{4,12},{5,13},{6,14},{7,15},{8,0},{9,1},... | collective-permute-start | bytes 1572872 | tf_op jit(solution)/shard_map/ppermute | solution.py:340
  39.7 6.3 %collective-permute-done.3.came_ref = bf16[24,16,128]{2,1,0:T(8,128)(2,1)S(1)} collective-permute-done((bf16[24,16,128]{2,1,0:T(8,128)(2,1)S(1)}, bf16[24,16,128]{2,1,0:T(8,128)(2,1)S(1)}, u32[]{:S(2)}, u32[]{:S(2)}) %collective-permute-start.3) | collective-permute-done | bytes 98336 | tf_op jit(solution)/shard_map/ppermute | solution.py:340
  45.9 3.7 %collective-permute-done.13.refs_0_ = bf16[16,128,128]{2,1,0:T(8,128)(2,1)S(1)} collective-permute-done((bf16[16,128,128]{2,1,0:T(8,128)(2,1)S(1)}, bf16[16,128,128]{2,1,0:T(8,128)(2,1)S(1)}, u32[]{:S(2)}, u32[]{:S(2)}) %collective-permute-start.13) | collective-permute-done | bytes 524320 | tf_op jit(solution)/shard_map/ppermute | solution.py:340
  50.4 1.6 %collective-permute-start.19 = (bf16[8,128,128]{2,1,0:T(8,128)(2,1)S(1)}, bf16[8,128,128]{2,1,0:T(8,128)(2,1)S(1)}, u32[]{:S(2)}, u32[]{:S(2)}) collective-permute-start(bf16[8,128,128]{2,1,0:T(8,128)(2,1)S(1)} %slice.8), channel_id=1, source_target_pairs={{0,8},{1,9},{2,10},{3,11},{4,12},{5,13},{6,14},{7,15},{8,0},{9,1},... | collective-permute-start | bytes 786440 | tf_op jit(solution)/shard_map/ppermute | solution.py:340
  52.4 9.3 %shard_map.63 = (bf16[14,16,128,128]{3,2,1,0:T(8,128)(2,1)S(1)}, bf16[14,16,128,128]{3,2,1,0:T(8,128)(2,1)S(1)}, f32[32,16,128]{2,1,0:T(8,128)S(1)}) custom-call(s32[16,128]{1,0:T(8,128)S(1)} %get-tuple-element.23.ids_ref, bf16[32,16,128]{2,1,0:T(8,128)(2,1)S(1)} %get-tuple-element.24.refs_1_.parts_ref, bf16[16,128,128]{2,1,0:T(8,128)(2,1)S(1)} %bitcast.6, ...), custom_call_target="tpu_custom_call" | custom-call | flops 234881024 | bytes 22020096 | tf_op jit(solution)/shard_map/pallas_call | solution.py:386
  62.4 1.0 %collective-permute-done.22.refs_3_ = bf16[8,128,128]{2,1,0:T(8,128)(2,1)S(1)} collective-permute-done((bf16[8,128,128]{2,1,0:T(8,128)(2,1)S(1)}, bf16[8,128,128]{2,1,0:T(8,128)(2,1)S(1)}, u32[]{:S(2)}, u32[]{:S(2)}) %collective-permute-start.22) | collective-permute-done | bytes 262176 | tf_op jit(solution)/shard_map/ppermute | solution.py:340
  63.8 13.1 %shard_map.66 = bf16[16,2,16,256]{3,2,1,0:T(8,128)(2,1)S(1)} custom-call(s32[16,128]{1,0:T(8,128)S(1)} %get-tuple-element.23.ids_ref, bf16[32,16,128]{2,1,0:T(8,128)(2,1)S(1)} %get-tuple-element.24.refs_1_.parts_ref, f32[32,16,128]{2,1,0:T(8,128)S(1)} %get-tuple-element.25.sum_ref, bf16[14,16,128,128]{3,2,1,0:T(8,128)(2,1)S(1)} %get-tuple-element.26.refs_1_.se_ref, ...), custom_call_target="tpu_custom_call" | custom-call | tf_op jit(solution)/shard_map/pallas_call | solution.py:407
  76.8 13.7 %all_to_all.5.back_ref = bf16[16,2,16,256]{3,2,1,0:T(8,128)(2,1)S(1)} all-to-all(bf16[16,2,16,256]{3,2,1,0:T(8,128)(2,1)S(1)} %shard_map.66), channel_id=1, replica_groups=mesh['dom'=2,'col'=4,'row'=4] {'col','row'}, dimensions={0} | all-to-all | bytes 524288 | tf_op jit(solution)/shard_map/all_to_all | solution.py:420
  90.5 0.9 shard_map.67
  (49 shorter events, 3.6 us)
Async XLA Ops:
  0.6 18.6 %collective-permute-start.5 = (bf16[16,128,128]{2,1,0:T(8,128)(2,1)}, bf16[16,128,128]{2,1,0:T(8,128)(2,1)S(1)}, u32[]{:S(2)}, u32[]{:S(2)}) collective-permute-start(bf16[16,128,128]{2,1,0:T(8,128)(2,1)} %bitcast.2), channel_id=1, source_target_pairs={{0,8},{1,9},{2,10},{3,11},{4,12},{5,13},{6,14},{7,15},{8,0},{9,1},... | collective-permute-start | bytes 1572872 | tf_op jit(solution)/shard_map/ppermute | solution.py:340
  3.7 15.6 %collective-permute-start.6 = (bf16[16,128,128]{2,1,0:T(8,128)(2,1)}, bf16[16,128,128]{2,1,0:T(8,128)(2,1)S(1)}, u32[]{:S(2)}, u32[]{:S(2)}) collective-permute-start(bf16[16,128,128]{2,1,0:T(8,128)(2,1)} %bitcast.3), channel_id=1, source_target_pairs={{0,4},{1,5},{2,6},{3,7},{4,0},{5,1},{6,2},{7,3},{8,12},{9,13},{10,... | collective-permute-start | bytes 1572872 | tf_op jit(solution)/shard_map/ppermute | solution.py:340
  3.7 15.6 %collective-permute-start.4 = (bf16[16,128,128]{2,1,0:T(8,128)(2,1)}, bf16[16,128,128]{2,1,0:T(8,128)(2,1)S(1)}, u32[]{:S(2)}, u32[]{:S(2)}) collective-permute-start(bf16[16,128,128]{2,1,0:T(8,128)(2,1)} %bitcast.4), channel_id=1, source_target_pairs={{0,1},{1,0},{2,3},{3,2},{4,5},{5,4},{6,7},{7,6},{8,9},{9,8},{10,11... | collective-permute-start | bytes 1572872 | tf_op jit(solution)/shard_map/ppermute | solution.py:340
  5.2 14.9 %collective-permute-start.8 = (bf16[16,128,128]{2,1,0:T(8,128)(2,1)}, bf16[16,128,128]{2,1,0:T(8,128)(2,1)S(1)}, u32[]{:S(2)}, u32[]{:S(2)}) collective-permute-start(bf16[16,128,128]{2,1,0:T(8,128)(2,1)} %bitcast.5), channel_id=1, source_target_pairs={{1,2},{2,1},{5,6},{6,5},{9,10},{10,9},{13,14},{14,13},{17,18},{18,... | collective-permute-start | bytes 1572872 | tf_op jit(solution)/shard_map/ppermute | solution.py:340
  7.6 1.3 %collective-permute-start = (bf16[17,16,128]{2,1,0:T(8,128)(2,1)S(1)}, bf16[17,16,128]{2,1,0:T(8,128)(2,1)S(1)}, u32[]{:S(2)}, u32[]{:S(2)}) collective-permute-start(bf16[17,16,128]{2,1,0:T(8,128)(2,1)S(1)} %get-tuple-element.16), channel_id=1, source_target_pairs={{0,4},{1,5},{2,6},{3,7},{4,0},{5,1},{6,2},{7,3},{8,12},{9,13},{10,... | collective-permute-start | bytes 208904 | tf_op jit(solution)/shard_map/ppermute | solution.py:340
  9.0 8.4 %collective-permute-start.1 = (bf16[18,16,128]{2,1,0:T(8,128)(2,1)S(1)}, bf16[18,16,128]{2,1,0:T(8,128)(2,1)S(1)}, u32[]{:S(2)}, u32[]{:S(2)}) collective-permute-start(bf16[18,16,128]{2,1,0:T(8,128)(2,1)S(1)} %get-tuple-element.18), channel_id=1, source_target_pairs={{0,8},{1,9},{2,10},{3,11},{4,12},{5,13},{6,14},{7,15},{8,0},{9,1},... | collective-permute-start | bytes 221192 | tf_op jit(solution)/shard_map/ppermute | solution.py:340
  17.4 5.6 %collective-permute-start.2 = (bf16[20,16,128]{2,1,0:T(8,128)(2,1)S(1)}, bf16[20,16,128]{2,1,0:T(8,128)(2,1)S(1)}, u32[]{:S(2)}, u32[]{:S(2)}) collective-permute-start(bf16[20,16,128]{2,1,0:T(8,128)(2,1)S(1)} %get-tuple-element.20.refs_2_), channel_id=1, source_target_pairs={{0,1},{1,0},{2,3},{3,2},{4,5},{5,4},{6,7},{7,6},{8,9},{9,8},{10,11... | collective-permute-start | bytes 245768 | tf_op jit(solution)/shard_map/ppermute | solution.py:340
  19.3 33.2 %copy-start = (bf16[1,1,16,128,128]{4,3,2,1,0:T(8,128)(2,1)S(1)}, bf16[1,1,16,128,128]{4,3,2,1,0:T(8,128)(2,1)}, u32[]{:S(2)}) copy-start(bf16[1,1,16,128,128]{4,3,2,1,0:T(8,128)(2,1)} %param.4) | copy-start | bytes 1572868
  19.3 4.3 %collective-permute-start.7 = (bf16[16,128,128]{2,1,0:T(8,128)(2,1)S(1)}, bf16[16,128,128]{2,1,0:T(8,128)(2,1)S(1)}, u32[]{:S(2)}, u32[]{:S(2)}) collective-permute-start(bf16[16,128,128]{2,1,0:T(8,128)(2,1)S(1)} %shard_map.55.refs_1_), channel_id=1, source_target_pairs={{1,2},{2,1},{5,6},{6,5},{9,10},{10,9},{13,14},{14,13},{17,18},{18,... | collective-permute-start | bytes 1572872 | tf_op jit(solution)/shard_map/ppermute | solution.py:340
  20.1 16.7 %collective-permute-start.9 = (bf16[16,128,128]{2,1,0:T(8,128)(2,1)S(1)}, bf16[16,128,128]{2,1,0:T(8,128)(2,1)S(1)}, u32[]{:S(2)}, u32[]{:S(2)}) collective-permute-start(bf16[16,128,128]{2,1,0:T(8,128)(2,1)S(1)} %shard_map.57.one_ref), channel_id=1, source_target_pairs={{1,0},{2,3},{5,4},{6,7},{9,8},{10,11},{13,12},{14,15},{17,16},{18,... | collective-permute-start | bytes 1572872 | tf_op jit(solution)/shard_map/ppermute | solution.py:340
  21.4 15.4 %collective-permute-start.10 = (bf16[16,128,128]{2,1,0:T(8,128)(2,1)S(1)}, bf16[16,128,128]{2,1,0:T(8,128)(2,1)S(1)}, u32[]{:S(2)}, u32[]{:S(2)}) collective-permute-start(bf16[16,128,128]{2,1,0:T(8,128)(2,1)S(1)} %shard_map.55.refs_1_), channel_id=1, source_target_pairs={{0,8},{1,9},{2,10},{3,11},{4,12},{5,13},{6,14},{7,15},{8,0},{9,1},... | collective-permute-start | bytes 1572872 | tf_op jit(solution)/shard_map/ppermute | solution.py:340
  23.0 13.8 %collective-permute-start.11 = (bf16[16,128,128]{2,1,0:T(8,128)(2,1)S(1)}, bf16[16,128,128]{2,1,0:T(8,128)(2,1)S(1)}, u32[]{:S(2)}, u32[]{:S(2)}) collective-permute-start(bf16[16,128,128]{2,1,0:T(8,128)(2,1)S(1)} %shard_map.55.refs_1_), channel_id=1, source_target_pairs={{0,4},{1,5},{2,6},{3,7},{4,0},{5,1},{6,2},{7,3},{8,12},{9,13},{10,... | collective-permute-start | bytes 1572872 | tf_op jit(solution)/shard_map/ppermute | solution.py:340
  23.0 13.8 %collective-permute-start.12 = (bf16[16,128,128]{2,1,0:T(8,128)(2,1)S(1)}, bf16[16,128,128]{2,1,0:T(8,128)(2,1)S(1)}, u32[]{:S(2)}, u32[]{:S(2)}) collective-permute-start(bf16[16,128,128]{2,1,0:T(8,128)(2,1)S(1)} %collective-permute-done.5.refs_1_.refs_2_), channel_id=1, source_target_pairs={{0,4},{1,5},{2,6},{3,7},{4,0},{5,1},{6,2},{7,3},{8,12},{9,13},{10,... | collective-permute-start | bytes 1572872 | tf_op jit(solution)/shard_map/ppermute | solution.py:340
  23.6 26.0 %collective-permute-start.13 = (bf16[16,128,128]{2,1,0:T(8,128)(2,1)S(1)}, bf16[16,128,128]{2,1,0:T(8,128)(2,1)S(1)}, u32[]{:S(2)}, u32[]{:S(2)}) collective-permute-start(bf16[16,128,128]{2,1,0:T(8,128)(2,1)S(1)} %shard_map.56.one_ref), channel_id=1, source_target_pairs={{1,0},{2,3},{5,4},{6,7},{9,8},{10,11},{13,12},{14,15},{17,16},{18,... | collective-permute-start | bytes 1572872 | tf_op jit(solution)/shard_map/ppermute | solution.py:340
  37.0 12.7 %collective-permute-start.14 = (bf16[16,128,128]{2,1,0:T(8,128)(2,1)S(1)}, bf16[16,128,128]{2,1,0:T(8,128)(2,1)S(1)}, u32[]{:S(2)}, u32[]{:S(2)}) collective-permute-start(bf16[16,128,128]{2,1,0:T(8,128)(2,1)S(1)} %shard_map.60.refs_3_), channel_id=1, source_target_pairs={{0,8},{1,9},{2,10},{3,11},{4,12},{5,13},{6,14},{7,15},{8,0},{9,1},... | collective-permute-start | bytes 1572872 | tf_op jit(solution)/shard_map/ppermute | solution.py:340
  38.8 10.9 %collective-permute-start.15 = (bf16[16,128,128]{2,1,0:T(8,128)(2,1)S(1)}, bf16[16,128,128]{2,1,0:T(8,128)(2,1)S(1)}, u32[]{:S(2)}, u32[]{:S(2)}) collective-permute-start(bf16[16,128,128]{2,1,0:T(8,128)(2,1)S(1)} %shard_map.60.refs_3_), channel_id=1, source_target_pairs={{0,4},{1,5},{2,6},{3,7},{4,0},{5,1},{6,2},{7,3},{8,12},{9,13},{10,... | collective-permute-start | bytes 1572872 | tf_op jit(solution)/shard_map/ppermute | solution.py:340
  38.8 10.9 %collective-permute-start.16 = (bf16[16,128,128]{2,1,0:T(8,128)(2,1)S(1)}, bf16[16,128,128]{2,1,0:T(8,128)(2,1)S(1)}, u32[]{:S(2)}, u32[]{:S(2)}) collective-permute-start(bf16[16,128,128]{2,1,0:T(8,128)(2,1)S(1)} %shard_map.59.refs_0_.refs_4_), channel_id=1, source_target_pairs={{0,4},{1,5},{2,6},{3,7},{4,0},{5,1},{6,2},{7,3},{8,12},{9,13},{10,... | collective-permute-start | bytes 1572872 | tf_op jit(solution)/shard_map/ppermute | solution.py:340
  39.3 6.7 %collective-permute-start.3 = (bf16[24,16,128]{2,1,0:T(8,128)(2,1)S(1)}, bf16[24,16,128]{2,1,0:T(8,128)(2,1)S(1)}, u32[]{:S(2)}, u32[]{:S(2)}) collective-permute-start(bf16[24,16,128]{2,1,0:T(8,128)(2,1)S(1)} %get-tuple-element.22.refs_1_), channel_id=1, source_target_pairs={{0,3},{1,2},{2,1},{3,0},{4,7},{5,6},{6,5},{7,4},{8,11},{9,10},{10,... | collective-permute-start | bytes 294920 | tf_op jit(solution)/shard_map/ppermute | solution.py:340
  49.7 2.3 %collective-permute-start.17 = (bf16[16,128,128]{2,1,0:T(8,128)(2,1)S(1)}, bf16[16,128,128]{2,1,0:T(8,128)(2,1)S(1)}, u32[]{:S(2)}, u32[]{:S(2)}) collective-permute-start(bf16[16,128,128]{2,1,0:T(8,128)(2,1)S(1)} %shard_map.62.refs_5_), channel_id=1, source_target_pairs={{0,4},{1,5},{2,6},{3,7},{4,0},{5,1},{6,2},{7,3},{8,12},{9,13},{10,... | collective-permute-start | bytes 1572872 | tf_op jit(solution)/shard_map/ppermute | solution.py:340
  49.8 2.6 %collective-permute-start.18 = (bf16[16,128,128]{2,1,0:T(8,128)(2,1)S(1)}, bf16[16,128,128]{2,1,0:T(8,128)(2,1)S(1)}, u32[]{:S(2)}, u32[]{:S(2)}) collective-permute-start(bf16[16,128,128]{2,1,0:T(8,128)(2,1)S(1)} %collective-permute-done.14.refs_0_.refs_6_), channel_id=1, source_target_pairs={{0,4},{1,5},{2,6},{3,7},{4,0},{5,1},{6,2},{7,3},{8,12},{9,13},{10,... | collective-permute-start | bytes 1572872 | tf_op jit(solution)/shard_map/ppermute | solution.py:340
  50.3 11.5 %collective-permute-start.20 = (bf16[8,128,128]{2,1,0:T(8,128)(2,1)S(1)}, bf16[8,128,128]{2,1,0:T(8,128)(2,1)S(1)}, u32[]{:S(2)}, u32[]{:S(2)}) collective-permute-start(bf16[8,128,128]{2,1,0:T(8,128)(2,1)S(1)} %slice.9), channel_id=1, source_target_pairs={{0,1},{1,0},{2,3},{3,2},{4,5},{5,4},{6,7},{7,6},{8,9},{9,8},{10,11... | collective-permute-start | bytes 786440 | tf_op jit(solution)/shard_map/ppermute | solution.py:340
  50.4 11.6 %collective-permute-start.19 = (bf16[8,128,128]{2,1,0:T(8,128)(2,1)S(1)}, bf16[8,128,128]{2,1,0:T(8,128)(2,1)S(1)}, u32[]{:S(2)}, u32[]{:S(2)}) collective-permute-start(bf16[8,128,128]{2,1,0:T(8,128)(2,1)S(1)} %slice.8), channel_id=1, source_target_pairs={{0,8},{1,9},{2,10},{3,11},{4,12},{5,13},{6,14},{7,15},{8,0},{9,1},... | collective-permute-start | bytes 786440 | tf_op jit(solution)/shard_map/ppermute | solution.py:340
  61.8 1.6 %collective-permute-start.22 = (bf16[8,128,128]{2,1,0:T(8,128)(2,1)S(1)}, bf16[8,128,128]{2,1,0:T(8,128)(2,1)S(1)}, u32[]{:S(2)}, u32[]{:S(2)}) collective-permute-start(bf16[8,128,128]{2,1,0:T(8,128)(2,1)S(1)} %shard_map.65.refs_1_), channel_id=1, source_target_pairs={{0,4},{1,5},{2,6},{3,7},{4,0},{5,1},{6,2},{7,3},{8,12},{9,13},{10,... | collective-permute-start | bytes 786440 | tf_op jit(solution)/shard_map/ppermute | solution.py:340
  62.0 1.8 %collective-permute-start.21 = (bf16[8,128,128]{2,1,0:T(8,128)(2,1)S(1)}, bf16[8,128,128]{2,1,0:T(8,128)(2,1)S(1)}, u32[]{:S(2)}, u32[]{:S(2)}) collective-permute-start(bf16[8,128,128]{2,1,0:T(8,128)(2,1)S(1)} %shard_map.64.refs_0_), channel_id=1, source_target_pairs={{0,4},{1,5},{2,6},{3,7},{4,0},{5,1},{6,2},{7,3},{8,12},{9,13},{10,... | collective-permute-start | bytes 786440 | tf_op jit(solution)/shard_map/ppermute | solution.py:340
  (1 other events, 0.9 us)

commit v16 on v15

--- a/solution.py
+++ b/solution.py
@@ -260,16 +260,36 @@
     return total
 
 
-def first_kernel(early, n_col, n_row, ids_ref, parts_ref, *refs):
-    bufs, (s_ref, st_ref, sum_ref, z, straight, *scattered, sems) = refs[: len(early)], refs[len(early) :]
+def load_kernel(count, *refs):
+    bufs, (s_ref, st_ref, sems) = refs[:count], refs[count:]
+    fill(bufs, s_ref, st_ref, sems)
+
+
+def load(*bufs):
+    out = jax.ShapeDtypeStruct((len(bufs), *bufs[0].shape), bufs[0].dtype)
+    return pl.pallas_call(
+        functools.partial(load_kernel, len(bufs)),
+        out_shape=[out, out],
+        in_specs=anywhere(len(bufs)),
+        out_specs=vmem(2),
+        scratch_shapes=[pltpu.SemaphoreType.DMA((len(bufs),))],
+        compiler_params=pltpu.CompilerParams(vmem_limit_bytes=2**20),
+        cost_estimate=pl.CostEstimate(flops=0, bytes_accessed=6 * out.size, transcendentals=0),
+    )(*bufs)
+
+
+def first_kernel(early, later, n_col, n_row, ids_ref, parts_ref, sa_ref, sta_ref, *refs):
+    bufs, (s_ref, st_ref, sum_ref, z, straight, *scattered, sems) = refs[: len(later)], refs[len(later) :]
     spread_vectors(parts_ref, z, n_col, n_row)
     fill(bufs, s_ref, st_ref, sems)
-    tiles = {at: (s_ref, i, st_ref, i) for i, at in enumerate(early)}
+    tiles = {at: (sa_ref, i, sta_ref, i) for i, at in enumerate(early)}
+    tiles.update({at: (s_ref, i, st_ref, i) for i, at in enumerate(later)})
     clear([straight])
     sum_ref[...] = sum_products(grouped(tiles, n_col, n_row), n_col, ids_ref, z, straight, scattered)
 
 
-def filter_kernel(early, late, n_col, n_row, ids_ref, parts_ref, sum_ref, se_ref, ste_ref, *refs):
+def filter_kernel(early, later, late, n_col, n_row, ids_ref, parts_ref, sum_ref, *refs):
+    (sa_ref, sta_ref, sb_ref, stb_ref), refs = refs[:4], refs[4:]
     bufs, (out_ref, s_ref, st_ref, z, now, prev, straight, *scattered, sems) = (
         refs[: len(late)],
         refs[len(late) :],
@@ -295,7 +315,8 @@
     now[...] = total
     z[...] = total.astype(z.dtype)
 
-    tiles.update({at: (se_ref, i, ste_ref, i) for i, at in enumerate(early)})
+    tiles.update({at: (sa_ref, i, sta_ref, i) for i, at in enumerate(early)})
+    tiles.update({at: (sb_ref, i, stb_ref, i) for i, at in enumerate(later)})
     groups = grouped(tiles, n_col, n_row)
 
     def one_step(step, carry):
@@ -374,40 +395,41 @@
     outer = after(send(crossed, 0, 1, INNER), rank=1)
     mates += to_mate(two, over_near)
     mine, ids = regroup(stay, send(go, 0, 3), 8, per_piece)
-    three = pick(INNER, inner, outer, over_two, mine, *mates[3:])
+    sa, sta = load(own, near, over_own, over_near, *mates[:3])
+    three = pick(INNER, inner, outer, over_two, mine, sa, *mates[3:])
 
     over_three = send(three[:half], 2, 0)
     side_three = send(over_two[half:], 0, 1)
     mates += to_mate(three, over_two)
-    early = [(0, 0), (0, 1), (2, 0), (0, 2), (2, 1), (0, 3), (2, 2)]
-    early += [(g ^ 1, f) for g, f in early]
-    tiles_of = jax.ShapeDtypeStruct((len(early), slots, orb, orb), blocks.dtype)
+    early = [(0, 0), (0, 1), (2, 0), (2, 1), (1, 0), (1, 1), (3, 0)]
+    later = [(0, 2), (2, 2), (0, 3), (1, 2), (3, 1), (1, 3), (3, 2)]
+    tiles_of = jax.ShapeDtypeStruct((len(later), slots, orb, orb), blocks.dtype)
     sums = jax.ShapeDtypeStruct((n_blocks, share, orb), jnp.float32)
-    se, ste, total = pl.pallas_call(
-        functools.partial(first_kernel, early, n_col, n_row),
+    sb, stb, total = pl.pallas_call(
+        functools.partial(first_kernel, early, later, n_col, n_row),
         out_shape=[tiles_of, tiles_of, sums],
-        in_specs=smem() + vmem() + anywhere(len(early)),
+        in_specs=smem() + vmem(3) + anywhere(len(later)),
         out_specs=vmem(3),
         scratch_shapes=[
             pltpu.VMEM((n_blocks, share, orb), jnp.bfloat16),
             *[pltpu.VMEM((n_blocks, share, orb), jnp.float32)] * (1 + SPLIT),
-            pltpu.SemaphoreType.DMA((len(early),)),
+            pltpu.SemaphoreType.DMA((len(later),)),
         ],
         compiler_params=pltpu.CompilerParams(vmem_limit_bytes=6 * 2**20),
         cost_estimate=pl.CostEstimate(
-            flops=4 * len(early) * slots * orb * orb * share,
-            bytes_accessed=6 * len(early) * own.size,
+            flops=4 * len(early + later) * slots * orb * orb * share,
+            bytes_accessed=6 * len(later) * own.size,
             transcendentals=0,
         ),
-    )(ids, mine, own, near, over_own, two, over_near, three, over_two, *mates)
-    over_three, side_three = after(over_three, se), after(side_three, se)
+    )(ids, mine, sa, sta, two, over_two, three, *mates[3:])
+    over_three, side_three = after(over_three, sb), after(side_three, sb)
     late = [(2, 3, 0), (2, 3, half), (3, 3, 0), (3, 3, half)]
     late_bufs = [over_three, side_three, *to_mate(over_three, side_three)]
 
     done = pl.pallas_call(
-        functools.partial(filter_kernel, early, late, n_col, n_row),
+        functools.partial(filter_kernel, early, later, late, n_col, n_row),
         out_shape=jax.ShapeDtypeStruct((n_dev, 2, share, rows), jnp.bfloat16),
-        in_specs=smem() + vmem(4) + anywhere(len(late)),
+        in_specs=smem() + vmem(6) + anywhere(len(late)),
         out_specs=vmem()[0],
         scratch_shapes=[
             *[pltpu.VMEM((2, slots, orb, orb), blocks.dtype)] * 2,
@@ -416,7 +438,7 @@
             pltpu.SemaphoreType.DMA((len(late),)),
         ],
         compiler_params=pltpu.CompilerParams(vmem_limit_bytes=12 * 2**20),
-    )(ids, mine, total, se, ste, *late_bufs)
+    )(ids, mine, total, sa, sta, sb, stb, *late_bufs)
     back = lax.all_to_all(done, LANES, split_axis=0, concat_axis=0, tiled=True)
     whole = jax.ShapeDtypeStruct((rows, width), jnp.float32)
     return pl.pallas_call(

time: 91.6 us -> 88.9 us (0.971)
  waiting for transfers between devices: 32.7 us -> 29.9 us
    ppermute x23, waiting for transfers between devices: 32.7 us -> 29.9 us  [send(): return lax.ppermute(buf, LANES, pairs)]
    pallas_call x2 -> x3, Pallas kernels: 22.4 us -> 22.4 us  [the longest x1 13.1 us: gather_plan(): pl.pallas_call(functools.partial(filter_kernel, early, later, late, n_col...]
  transfers between devices with their start and end apart: 23 -> 23, of which waited for: 8 -> 8; matrix products, arithmetic and copies ran while one was open for 1% -> 1% of each run, Pallas kernels for 10% -> 11%
where the time goes in v16:
time: 88.9 us; the launch traced here: 88.7 us
  waiting for transfers between devices  29.9 us (34%)
  Pallas kernels  23.6 us (27%)
  starting transfers between devices  19 us (21%)
  blocking collectives  13.7 us (15%)
  local copies, waits for them, and re-layouts  1.61 us (2%)
    ppermute x23, waiting for transfers between devices, send(): return lax.ppermute(buf, LANES, pairs)  29.9 us
    ppermute x23, starting transfers between devices, send(): return lax.ppermute(buf, LANES, pairs)  19 us
    all_to_all x1, blocking collectives, gather_plan(): back = lax.all_to_all(done, LANES, split_axis=0, concat_axis=0, tiled=True)  13.7 us
    pallas_call x1, Pallas kernels, gather_plan(): pl.pallas_call(functools.partial(filter_kernel, early, later, late, n_col...  13.1 us
    pallas_call x1, Pallas kernels, gather_plan(): pl.pallas_call(functools.partial(first_kernel, early, later, n_col, n_row...  6.55 us
    pallas_call x1, Pallas kernels, load(): pl.pallas_call(functools.partial(load_kernel, len(bufs)), out_shape=[out,...  2.79 us
  transfers between devices with their start and end apart: 23, of which 8 were waited for; matrix products, arithmetic and copies ran while one was open for 1% of the time, Pallas kernels for 11%

profile of v16, /device:TPU:0, one launch (start us, length us, event | category | flops | bytes accessed | tf_op | source)
XLA Modules:
  0.0 88.7 jit_solution(17266268537306356053)
XLA Ops:
  0.6 3.0 %collective-permute-start.5 = (bf16[16,128,128]{2,1,0:T(8,128)(2,1)}, bf16[16,128,128]{2,1,0:T(8,128)(2,1)S(1)}, u32[]{:S(2)}, u32[]{:S(2)}) collective-permute-start(bf16[16,128,128]{2,1,0:T(8,128)(2,1)} %bitcast.2), channel_id=1, source_target_pairs={{0,8},{1,9},{2,10},{3,11},{4,12},{5,13},{6,14},{7,15},{8,0},{9,1},... | collective-permute-start | bytes 1572872 | tf_op jit(solution)/shard_map/ppermute | solution.py:361
  3.7 1.6 %collective-permute-start.4 = (bf16[16,128,128]{2,1,0:T(8,128)(2,1)}, bf16[16,128,128]{2,1,0:T(8,128)(2,1)S(1)}, u32[]{:S(2)}, u32[]{:S(2)}) collective-permute-start(bf16[16,128,128]{2,1,0:T(8,128)(2,1)} %bitcast.4), channel_id=1, source_target_pairs={{0,1},{1,0},{2,3},{3,2},{4,5},{5,4},{6,7},{7,6},{8,9},{9,8},{10,11... | collective-permute-start | bytes 1572872 | tf_op jit(solution)/shard_map/ppermute | solution.py:361
  5.2 0.7 collective-permute-start.11
  5.9 0.7 pad.4
  6.6 0.9 %copy-done.1 = bf16[256,256]{1,0:T(8,128)(2,1)S(1)} copy-done((bf16[256,256]{1,0:T(8,128)(2,1)S(1)}, bf16[256,256]{1,0:T(8,128)(2,1)}, u32[]{:S(2)}) %copy-start.1) | copy-done | bytes 131096
  7.9 1.0 %collective-permute-done.came_ref = bf16[17,16,128]{2,1,0:T(8,128)(2,1)S(1)} collective-permute-done((bf16[17,16,128]{2,1,0:T(8,128)(2,1)S(1)}, bf16[17,16,128]{2,1,0:T(8,128)(2,1)S(1)}, u32[]{:S(2)}, u32[]{:S(2)}) %collective-permute-start) | collective-permute-done | bytes 69664 | tf_op jit(solution)/shard_map/ppermute | solution.py:361
  9.0 0.6 collective-permute-start.1
  9.5 7.8 %collective-permute-done.1.came_ref = bf16[18,16,128]{2,1,0:T(8,128)(2,1)S(1)} collective-permute-done((bf16[18,16,128]{2,1,0:T(8,128)(2,1)S(1)}, bf16[18,16,128]{2,1,0:T(8,128)(2,1)S(1)}, u32[]{:S(2)}, u32[]{:S(2)}) %collective-permute-start.1) | collective-permute-done | bytes 73760 | tf_op jit(solution)/shard_map/ppermute | solution.py:361
  17.4 1.9 %collective-permute-start.2 = (bf16[20,16,128]{2,1,0:T(8,128)(2,1)S(1)}, bf16[20,16,128]{2,1,0:T(8,128)(2,1)S(1)}, u32[]{:S(2)}, u32[]{:S(2)}) collective-permute-start(bf16[20,16,128]{2,1,0:T(8,128)(2,1)S(1)} %get-tuple-element.22.refs_2_), channel_id=1, source_target_pairs={{0,1},{1,0},{2,3},{3,2},{4,5},{5,4},{6,7},{7,6},{8,9},{9,8},{10,11... | collective-permute-start | bytes 245768 | tf_op jit(solution)/shard_map/ppermute | solution.py:361
  19.3 0.7 collective-permute-start.10
  20.0 1.4 %collective-permute-start.12 = (bf16[16,128,128]{2,1,0:T(8,128)(2,1)S(1)}, bf16[16,128,128]{2,1,0:T(8,128)(2,1)S(1)}, u32[]{:S(2)}, u32[]{:S(2)}) collective-permute-start(bf16[16,128,128]{2,1,0:T(8,128)(2,1)S(1)} %shard_map.59.one_ref), channel_id=1, source_target_pairs={{1,0},{2,3},{5,4},{6,7},{9,8},{10,11},{13,12},{14,15},{17,16},{18,... | collective-permute-start | bytes 1572872 | tf_op jit(solution)/shard_map/ppermute | solution.py:361
  21.4 1.6 %collective-permute-start.7 = (bf16[16,128,128]{2,1,0:T(8,128)(2,1)S(1)}, bf16[16,128,128]{2,1,0:T(8,128)(2,1)S(1)}, u32[]{:S(2)}, u32[]{:S(2)}) collective-permute-start(bf16[16,128,128]{2,1,0:T(8,128)(2,1)S(1)} %shard_map.55.refs_1_), channel_id=1, source_target_pairs={{0,8},{1,9},{2,10},{3,11},{4,12},{5,13},{6,14},{7,15},{8,0},{9,1},... | collective-permute-start | bytes 1572872 | tf_op jit(solution)/shard_map/ppermute | solution.py:361
  23.6 1.3 %collective-permute-start.14 = (bf16[16,128,128]{2,1,0:T(8,128)(2,1)S(1)}, bf16[16,128,128]{2,1,0:T(8,128)(2,1)S(1)}, u32[]{:S(2)}, u32[]{:S(2)}) collective-permute-start(bf16[16,128,128]{2,1,0:T(8,128)(2,1)S(1)} %shard_map.58.one_ref), channel_id=1, source_target_pairs={{1,0},{2,3},{5,4},{6,7},{9,8},{10,11},{13,12},{14,15},{17,16},{18,... | collective-permute-start | bytes 1572872 | tf_op jit(solution)/shard_map/ppermute | solution.py:361
  24.9 12.1 %collective-permute-done.12.refs_0_ = bf16[16,128,128]{2,1,0:T(8,128)(2,1)S(1)} collective-permute-done((bf16[16,128,128]{2,1,0:T(8,128)(2,1)S(1)}, bf16[16,128,128]{2,1,0:T(8,128)(2,1)S(1)}, u32[]{:S(2)}, u32[]{:S(2)}) %collective-permute-start.12) | collective-permute-done | bytes 524320 | tf_op jit(solution)/shard_map/ppermute | solution.py:361
  37.1 1.8 %collective-permute-start.13 = (bf16[16,128,128]{2,1,0:T(8,128)(2,1)S(1)}, bf16[16,128,128]{2,1,0:T(8,128)(2,1)S(1)}, u32[]{:S(2)}, u32[]{:S(2)}) collective-permute-start(bf16[16,128,128]{2,1,0:T(8,128)(2,1)S(1)} %shard_map.61.refs_0_), channel_id=1, source_target_pairs={{0,8},{1,9},{2,10},{3,11},{4,12},{5,13},{6,14},{7,15},{8,0},{9,1},... | collective-permute-start | bytes 1572872 | tf_op jit(solution)/shard_map/ppermute | solution.py:361
  39.7 6.3 %collective-permute-done.3.came_ref = bf16[24,16,128]{2,1,0:T(8,128)(2,1)S(1)} collective-permute-done((bf16[24,16,128]{2,1,0:T(8,128)(2,1)S(1)}, bf16[24,16,128]{2,1,0:T(8,128)(2,1)S(1)}, u32[]{:S(2)}, u32[]{:S(2)}) %collective-permute-start.3) | collective-permute-done | bytes 98336 | tf_op jit(solution)/shard_map/ppermute | solution.py:361
  46.1 2.8 %shard_map.57 = (bf16[7,16,128,128]{3,2,1,0:T(8,128)(2,1)S(1)}, bf16[7,16,128,128]{3,2,1,0:T(8,128)(2,1)S(1)}) custom-call(bf16[16,128,128]{2,1,0:T(8,128)(2,1)S(1)} %bitcast.6, bf16[16,128,128]{2,1,0:T(8,128)(2,1)S(1)} %shard_map.55.refs_1_, bf16[16,128,128]{2,1,0:T(8,128)(2,1)S(1)} %collective-permute-done.5.refs_1_.refs_2_, ...), custom_call_target="tpu_custom_call" | custom-call | bytes 11010048 | tf_op jit(solution)/shard_map/pallas_call | solution.py:270
  48.9 0.7 collective-permute-done.14.refs_0_
  50.8 1.2 %collective-permute-start.19 = (bf16[8,128,128]{2,1,0:T(8,128)(2,1)S(1)}, bf16[8,128,128]{2,1,0:T(8,128)(2,1)S(1)}, u32[]{:S(2)}, u32[]{:S(2)}) collective-permute-start(bf16[8,128,128]{2,1,0:T(8,128)(2,1)S(1)} %slice.8), channel_id=1, source_target_pairs={{0,8},{1,9},{2,10},{3,11},{4,12},{5,13},{6,14},{7,15},{8,0},{9,1},... | collective-permute-start | bytes 786440 | tf_op jit(solution)/shard_map/ppermute | solution.py:361
  52.4 6.5 %shard_map.64 = (bf16[7,16,128,128]{3,2,1,0:T(8,128)(2,1)S(1)}, bf16[7,16,128,128]{3,2,1,0:T(8,128)(2,1)S(1)}, f32[32,16,128]{2,1,0:T(8,128)S(1)}) custom-call(s32[16,128]{1,0:T(8,128)S(1)} %get-tuple-element.25.ids_ref, bf16[32,16,128]{2,1,0:T(8,128)(2,1)S(1)} %get-tuple-element.26.refs_1_.parts_ref, ...), custom_call_target="tpu_custom_call" | custom-call | flops 234881024 | bytes 11010048 | tf_op jit(solution)/shard_map/pallas_call | solution.py:408
  59.6 1.0 %collective-permute-done.22.refs_7_ = bf16[8,128,128]{2,1,0:T(8,128)(2,1)S(1)} collective-permute-done((bf16[8,128,128]{2,1,0:T(8,128)(2,1)S(1)}, bf16[8,128,128]{2,1,0:T(8,128)(2,1)S(1)}, u32[]{:S(2)}, u32[]{:S(2)}) %collective-permute-start.22) | collective-permute-done | bytes 262176 | tf_op jit(solution)/shard_map/ppermute | solution.py:361
  61.0 13.1 %shard_map.67 = bf16[16,2,16,256]{3,2,1,0:T(8,128)(2,1)S(1)} custom-call(s32[16,128]{1,0:T(8,128)S(1)} %get-tuple-element.25.ids_ref, bf16[32,16,128]{2,1,0:T(8,128)(2,1)S(1)} %get-tuple-element.26.refs_1_.parts_ref, f32[32,16,128]{2,1,0:T(8,128)S(1)} %get-tuple-element.29.sum_ref, bf16[7,16,128,128]{3,2,1,0:T(8,128)(2,1)S(1)} %get-tuple-element.27.refs_2_.sa_ref.refs_0_, ...), custom_call_target="tpu_custom_call" | custom-call | tf_op jit(solution)/shard_map/pallas_call | solution.py:429
  74.1 13.7 %all_to_all.5.back_ref = bf16[16,2,16,256]{3,2,1,0:T(8,128)(2,1)S(1)} all-to-all(bf16[16,2,16,256]{3,2,1,0:T(8,128)(2,1)S(1)} %shard_map.67), channel_id=1, replica_groups=mesh['dom'=2,'col'=4,'row'=4] {'col','row'}, dimensions={0} | all-to-all | bytes 524288 | tf_op jit(solution)/shard_map/all_to_all | solution.py:442
  87.8 0.9 %shard_map.68 = (f32[256,256]{1,0:T(8,128)}, f32[256,256]{1,0:T(8,128)}) custom-call(bf16[16,2,16,256]{3,2,1,0:T(8,128)(2,1)S(1)} %all_to_all.5.back_ref), custom_call_target="tpu_custom_call" | custom-call | tf_op jit(solution)/shard_map/pallas_call | solution.py:444
  (50 shorter events, 4.4 us)
Async XLA Ops:
  0.6 18.6 %collective-permute-start.5 = (bf16[16,128,128]{2,1,0:T(8,128)(2,1)}, bf16[16,128,128]{2,1,0:T(8,128)(2,1)S(1)}, u32[]{:S(2)}, u32[]{:S(2)}) collective-permute-start(bf16[16,128,128]{2,1,0:T(8,128)(2,1)} %bitcast.2), channel_id=1, source_target_pairs={{0,8},{1,9},{2,10},{3,11},{4,12},{5,13},{6,14},{7,15},{8,0},{9,1},... | collective-permute-start | bytes 1572872 | tf_op jit(solution)/shard_map/ppermute | solution.py:361
  3.7 15.6 %collective-permute-start.6 = (bf16[16,128,128]{2,1,0:T(8,128)(2,1)}, bf16[16,128,128]{2,1,0:T(8,128)(2,1)S(1)}, u32[]{:S(2)}, u32[]{:S(2)}) collective-permute-start(bf16[16,128,128]{2,1,0:T(8,128)(2,1)} %bitcast.3), channel_id=1, source_target_pairs={{0,4},{1,5},{2,6},{3,7},{4,0},{5,1},{6,2},{7,3},{8,12},{9,13},{10,... | collective-permute-start | bytes 1572872 | tf_op jit(solution)/shard_map/ppermute | solution.py:361
  3.7 15.6 %collective-permute-start.4 = (bf16[16,128,128]{2,1,0:T(8,128)(2,1)}, bf16[16,128,128]{2,1,0:T(8,128)(2,1)S(1)}, u32[]{:S(2)}, u32[]{:S(2)}) collective-permute-start(bf16[16,128,128]{2,1,0:T(8,128)(2,1)} %bitcast.4), channel_id=1, source_target_pairs={{0,1},{1,0},{2,3},{3,2},{4,5},{5,4},{6,7},{7,6},{8,9},{9,8},{10,11... | collective-permute-start | bytes 1572872 | tf_op jit(solution)/shard_map/ppermute | solution.py:361
  5.2 14.7 %collective-permute-start.11 = (bf16[16,128,128]{2,1,0:T(8,128)(2,1)}, bf16[16,128,128]{2,1,0:T(8,128)(2,1)S(1)}, u32[]{:S(2)}, u32[]{:S(2)}) collective-permute-start(bf16[16,128,128]{2,1,0:T(8,128)(2,1)} %bitcast.5), channel_id=1, source_target_pairs={{1,2},{2,1},{5,6},{6,5},{9,10},{10,9},{13,14},{14,13},{17,18},{18,... | collective-permute-start | bytes 1572872 | tf_op jit(solution)/shard_map/ppermute | solution.py:361
  7.6 1.3 %collective-permute-start = (bf16[17,16,128]{2,1,0:T(8,128)(2,1)S(1)}, bf16[17,16,128]{2,1,0:T(8,128)(2,1)S(1)}, u32[]{:S(2)}, u32[]{:S(2)}) collective-permute-start(bf16[17,16,128]{2,1,0:T(8,128)(2,1)S(1)} %get-tuple-element.18), channel_id=1, source_target_pairs={{0,4},{1,5},{2,6},{3,7},{4,0},{5,1},{6,2},{7,3},{8,12},{9,13},{10,... | collective-permute-start | bytes 208904 | tf_op jit(solution)/shard_map/ppermute | solution.py:361
  9.0 8.4 %collective-permute-start.1 = (bf16[18,16,128]{2,1,0:T(8,128)(2,1)S(1)}, bf16[18,16,128]{2,1,0:T(8,128)(2,1)S(1)}, u32[]{:S(2)}, u32[]{:S(2)}) collective-permute-start(bf16[18,16,128]{2,1,0:T(8,128)(2,1)S(1)} %get-tuple-element.20), channel_id=1, source_target_pairs={{0,8},{1,9},{2,10},{3,11},{4,12},{5,13},{6,14},{7,15},{8,0},{9,1},... | collective-permute-start | bytes 221192 | tf_op jit(solution)/shard_map/ppermute | solution.py:361
  17.4 5.6 %collective-permute-start.2 = (bf16[20,16,128]{2,1,0:T(8,128)(2,1)S(1)}, bf16[20,16,128]{2,1,0:T(8,128)(2,1)S(1)}, u32[]{:S(2)}, u32[]{:S(2)}) collective-permute-start(bf16[20,16,128]{2,1,0:T(8,128)(2,1)S(1)} %get-tuple-element.22.refs_2_), channel_id=1, source_target_pairs={{0,1},{1,0},{2,3},{3,2},{4,5},{5,4},{6,7},{7,6},{8,9},{9,8},{10,11... | collective-permute-start | bytes 245768 | tf_op jit(solution)/shard_map/ppermute | solution.py:361
  19.3 4.3 %collective-permute-start.10 = (bf16[16,128,128]{2,1,0:T(8,128)(2,1)S(1)}, bf16[16,128,128]{2,1,0:T(8,128)(2,1)S(1)}, u32[]{:S(2)}, u32[]{:S(2)}) collective-permute-start(bf16[16,128,128]{2,1,0:T(8,128)(2,1)S(1)} %shard_map.55.refs_1_), channel_id=1, source_target_pairs={{1,2},{2,1},{5,6},{6,5},{9,10},{10,9},{13,14},{14,13},{17,18},{18,... | collective-permute-start | bytes 1572872 | tf_op jit(solution)/shard_map/ppermute | solution.py:361
  20.0 26.1 %copy-start = (bf16[1,1,16,128,128]{4,3,2,1,0:T(8,128)(2,1)S(1)}, bf16[1,1,16,128,128]{4,3,2,1,0:T(8,128)(2,1)}, u32[]{:S(2)}) copy-start(bf16[1,1,16,128,128]{4,3,2,1,0:T(8,128)(2,1)} %param.4) | copy-start | bytes 1572868
  20.0 17.0 %collective-permute-start.12 = (bf16[16,128,128]{2,1,0:T(8,128)(2,1)S(1)}, bf16[16,128,128]{2,1,0:T(8,128)(2,1)S(1)}, u32[]{:S(2)}, u32[]{:S(2)}) collective-permute-start(bf16[16,128,128]{2,1,0:T(8,128)(2,1)S(1)} %shard_map.59.one_ref), channel_id=1, source_target_pairs={{1,0},{2,3},{5,4},{6,7},{9,8},{10,11},{13,12},{14,15},{17,16},{18,... | collective-permute-start | bytes 1572872 | tf_op jit(solution)/shard_map/ppermute | solution.py:361
  21.4 15.5 %collective-permute-start.7 = (bf16[16,128,128]{2,1,0:T(8,128)(2,1)S(1)}, bf16[16,128,128]{2,1,0:T(8,128)(2,1)S(1)}, u32[]{:S(2)}, u32[]{:S(2)}) collective-permute-start(bf16[16,128,128]{2,1,0:T(8,128)(2,1)S(1)} %shard_map.55.refs_1_), channel_id=1, source_target_pairs={{0,8},{1,9},{2,10},{3,11},{4,12},{5,13},{6,14},{7,15},{8,0},{9,1},... | collective-permute-start | bytes 1572872 | tf_op jit(solution)/shard_map/ppermute | solution.py:361
  23.0 14.0 %collective-permute-start.8 = (bf16[16,128,128]{2,1,0:T(8,128)(2,1)S(1)}, bf16[16,128,128]{2,1,0:T(8,128)(2,1)S(1)}, u32[]{:S(2)}, u32[]{:S(2)}) collective-permute-start(bf16[16,128,128]{2,1,0:T(8,128)(2,1)S(1)} %shard_map.55.refs_1_), channel_id=1, source_target_pairs={{0,4},{1,5},{2,6},{3,7},{4,0},{5,1},{6,2},{7,3},{8,12},{9,13},{10,... | collective-permute-start | bytes 1572872 | tf_op jit(solution)/shard_map/ppermute | solution.py:361
  23.0 14.0 %collective-permute-start.9 = (bf16[16,128,128]{2,1,0:T(8,128)(2,1)S(1)}, bf16[16,128,128]{2,1,0:T(8,128)(2,1)S(1)}, u32[]{:S(2)}, u32[]{:S(2)}) collective-permute-start(bf16[16,128,128]{2,1,0:T(8,128)(2,1)S(1)} %collective-permute-done.5.refs_1_.refs_2_), channel_id=1, source_target_pairs={{0,4},{1,5},{2,6},{3,7},{4,0},{5,1},{6,2},{7,3},{8,12},{9,13},{10,... | collective-permute-start | bytes 1572872 | tf_op jit(solution)/shard_map/ppermute | solution.py:361
  23.6 26.0 %collective-permute-start.14 = (bf16[16,128,128]{2,1,0:T(8,128)(2,1)S(1)}, bf16[16,128,128]{2,1,0:T(8,128)(2,1)S(1)}, u32[]{:S(2)}, u32[]{:S(2)}) collective-permute-start(bf16[16,128,128]{2,1,0:T(8,128)(2,1)S(1)} %shard_map.58.one_ref), channel_id=1, source_target_pairs={{1,0},{2,3},{5,4},{6,7},{9,8},{10,11},{13,12},{14,15},{17,16},{18,... | collective-permute-start | bytes 1572872 | tf_op jit(solution)/shard_map/ppermute | solution.py:361
  37.1 12.6 %collective-permute-start.13 = (bf16[16,128,128]{2,1,0:T(8,128)(2,1)S(1)}, bf16[16,128,128]{2,1,0:T(8,128)(2,1)S(1)}, u32[]{:S(2)}, u32[]{:S(2)}) collective-permute-start(bf16[16,128,128]{2,1,0:T(8,128)(2,1)S(1)} %shard_map.61.refs_0_), channel_id=1, source_target_pairs={{0,8},{1,9},{2,10},{3,11},{4,12},{5,13},{6,14},{7,15},{8,0},{9,1},... | collective-permute-start | bytes 1572872 | tf_op jit(solution)/shard_map/ppermute | solution.py:361
  38.9 10.7 %collective-permute-start.15 = (bf16[16,128,128]{2,1,0:T(8,128)(2,1)S(1)}, bf16[16,128,128]{2,1,0:T(8,128)(2,1)S(1)}, u32[]{:S(2)}, u32[]{:S(2)}) collective-permute-start(bf16[16,128,128]{2,1,0:T(8,128)(2,1)S(1)} %shard_map.61.refs_0_), channel_id=1, source_target_pairs={{0,4},{1,5},{2,6},{3,7},{4,0},{5,1},{6,2},{7,3},{8,12},{9,13},{10,... | collective-permute-start | bytes 1572872 | tf_op jit(solution)/shard_map/ppermute | solution.py:361
  38.9 10.7 %collective-permute-start.16 = (bf16[16,128,128]{2,1,0:T(8,128)(2,1)S(1)}, bf16[16,128,128]{2,1,0:T(8,128)(2,1)S(1)}, u32[]{:S(2)}, u32[]{:S(2)}) collective-permute-start(bf16[16,128,128]{2,1,0:T(8,128)(2,1)S(1)} %shard_map.56.refs_3_.refs_0_), channel_id=1, source_target_pairs={{0,4},{1,5},{2,6},{3,7},{4,0},{5,1},{6,2},{7,3},{8,12},{9,13},{10,... | collective-permute-start | bytes 1572872 | tf_op jit(solution)/shard_map/ppermute | solution.py:361
  39.4 6.7 %collective-permute-start.3 = (bf16[24,16,128]{2,1,0:T(8,128)(2,1)S(1)}, bf16[24,16,128]{2,1,0:T(8,128)(2,1)S(1)}, u32[]{:S(2)}, u32[]{:S(2)}) collective-permute-start(bf16[24,16,128]{2,1,0:T(8,128)(2,1)S(1)} %get-tuple-element.24.refs_1_), channel_id=1, source_target_pairs={{0,3},{1,2},{2,1},{3,0},{4,7},{5,6},{6,5},{7,4},{8,11},{9,10},{10,... | collective-permute-start | bytes 294920 | tf_op jit(solution)/shard_map/ppermute | solution.py:361
  49.7 2.3 %collective-permute-start.17 = (bf16[16,128,128]{2,1,0:T(8,128)(2,1)S(1)}, bf16[16,128,128]{2,1,0:T(8,128)(2,1)S(1)}, u32[]{:S(2)}, u32[]{:S(2)}) collective-permute-start(bf16[16,128,128]{2,1,0:T(8,128)(2,1)S(1)} %shard_map.63.refs_2_), channel_id=1, source_target_pairs={{0,4},{1,5},{2,6},{3,7},{4,0},{5,1},{6,2},{7,3},{8,12},{9,13},{10,... | collective-permute-start | bytes 1572872 | tf_op jit(solution)/shard_map/ppermute | solution.py:361
  49.8 2.6 %collective-permute-start.18 = (bf16[16,128,128]{2,1,0:T(8,128)(2,1)S(1)}, bf16[16,128,128]{2,1,0:T(8,128)(2,1)S(1)}, u32[]{:S(2)}, u32[]{:S(2)}) collective-permute-start(bf16[16,128,128]{2,1,0:T(8,128)(2,1)S(1)} %collective-permute-done.13.refs_0_.refs_1_), channel_id=1, source_target_pairs={{0,4},{1,5},{2,6},{3,7},{4,0},{5,1},{6,2},{7,3},{8,12},{9,13},{10,... | collective-permute-start | bytes 1572872 | tf_op jit(solution)/shard_map/ppermute | solution.py:361
  50.3 8.7 %collective-permute-start.20 = (bf16[8,128,128]{2,1,0:T(8,128)(2,1)S(1)}, bf16[8,128,128]{2,1,0:T(8,128)(2,1)S(1)}, u32[]{:S(2)}, u32[]{:S(2)}) collective-permute-start(bf16[8,128,128]{2,1,0:T(8,128)(2,1)S(1)} %slice.9), channel_id=1, source_target_pairs={{0,1},{1,0},{2,3},{3,2},{4,5},{5,4},{6,7},{7,6},{8,9},{9,8},{10,11... | collective-permute-start | bytes 786440 | tf_op jit(solution)/shard_map/ppermute | solution.py:361
  50.8 8.4 %collective-permute-start.19 = (bf16[8,128,128]{2,1,0:T(8,128)(2,1)S(1)}, bf16[8,128,128]{2,1,0:T(8,128)(2,1)S(1)}, u32[]{:S(2)}, u32[]{:S(2)}) collective-permute-start(bf16[8,128,128]{2,1,0:T(8,128)(2,1)S(1)} %slice.8), channel_id=1, source_target_pairs={{0,8},{1,9},{2,10},{3,11},{4,12},{5,13},{6,14},{7,15},{8,0},{9,1},... | collective-permute-start | bytes 786440 | tf_op jit(solution)/shard_map/ppermute | solution.py:361
  59.0 1.6 %collective-permute-start.22 = (bf16[8,128,128]{2,1,0:T(8,128)(2,1)S(1)}, bf16[8,128,128]{2,1,0:T(8,128)(2,1)S(1)}, u32[]{:S(2)}, u32[]{:S(2)}) collective-permute-start(bf16[8,128,128]{2,1,0:T(8,128)(2,1)S(1)} %shard_map.66.refs_5_), channel_id=1, source_target_pairs={{0,4},{1,5},{2,6},{3,7},{4,0},{5,1},{6,2},{7,3},{8,12},{9,13},{10,... | collective-permute-start | bytes 786440 | tf_op jit(solution)/shard_map/ppermute | solution.py:361
  59.2 1.8 %collective-permute-start.21 = (bf16[8,128,128]{2,1,0:T(8,128)(2,1)S(1)}, bf16[8,128,128]{2,1,0:T(8,128)(2,1)S(1)}, u32[]{:S(2)}, u32[]{:S(2)}) collective-permute-start(bf16[8,128,128]{2,1,0:T(8,128)(2,1)S(1)} %shard_map.65.refs_4_), channel_id=1, source_target_pairs={{0,4},{1,5},{2,6},{3,7},{4,0},{5,1},{6,2},{7,3},{8,12},{9,13},{10,... | collective-permute-start | bytes 786440 | tf_op jit(solution)/shard_map/ppermute | solution.py:361
  (1 other events, 0.9 us)

commit v17 on v16

--- a/solution.py
+++ b/solution.py
@@ -10,6 +10,7 @@
 PER_ROW = 2
 DEG = 4
 SPLIT = 4
+UNROLL = 2
 GATHER_LIMIT = 12 * 2**20
 LANES = ("col", "row")
 INNER = (1, 2)
@@ -194,8 +195,8 @@
             continue
         here = across[g] * tile_rows + t
         places = [(tile, t * PER_ROW + p) for tile in group for p in range(PER_ROW)]
-        strip = jnp.concatenate([s[i, slot] for (_, s, i, _, _), slot in places], axis=1)
-        turned = jnp.concatenate([st[i, slot] for (_, _, _, st, i), slot in places], axis=0)
+        strip = jnp.concatenate([s[slot] for (_, s, _, _), slot in places], axis=1)
+        turned = jnp.concatenate([st[i, slot] for (_, _, st, i), slot in places], axis=0)
         where = [ids_ref[place(g, f), slot] for (f, *_), slot in places]
         wide = jnp.concatenate([z[u] for u in where], axis=1)
         straight[here] = jnp.dot(wide, turned, preferred_element_type=jnp.float32)
@@ -218,13 +219,14 @@
     lax.fori_loop(0, count // 4, four, 0)
 
 
-def fill(bufs, s_ref, st_ref, sems):
-    copies = [pltpu.make_async_copy(buf, s_ref.at[i], sems.at[i]) for i, buf in enumerate(bufs)]
-    for copy in copies:
-        copy.start()
-    for i, copy in enumerate(copies):
-        copy.wait()
-        turn(s_ref, st_ref, i, 0, s_ref.shape[1])
+def turn_all(bufs, st_ref):
+    def four(k, carry):
+        for i, buf in enumerate(bufs):
+            for m in range(4):
+                st_ref[i, 4 * k + m] = buf[4 * k + m].T
+        return carry
+
+    lax.fori_loop(0, st_ref.shape[1] // 4, four, 0)
 
 
 def grouped(tiles, n_col, n_row):
@@ -249,47 +251,49 @@
     across = [lax.axis_index("col") ^ g for g in range(n_col)]
     clear(scattered)
 
-    def block_row(t, carry):
-        multiply(t, groups, across, ids_ref, z, straight, scattered)
+    def block_rows(k, carry):
+        for t in range(UNROLL):
+            multiply(k * UNROLL + t, groups, across, ids_ref, z, straight, scattered)
         return carry
 
-    lax.fori_loop(0, z.shape[0] // n_col, block_row, 0)
+    lax.fori_loop(0, z.shape[0] // n_col // UNROLL, block_rows, 0)
     total = straight[...]
     for ref in scattered:
         total += ref[...]
     return total
 
 
-def load_kernel(count, *refs):
-    bufs, (s_ref, st_ref, sems) = refs[:count], refs[count:]
-    fill(bufs, s_ref, st_ref, sems)
-
-
-def load(*bufs):
-    out = jax.ShapeDtypeStruct((len(bufs), *bufs[0].shape), bufs[0].dtype)
+def turned_kernel(*refs):
+    turn_all(refs[:-1], refs[-1])
+
+
+def turned_tiles(*bufs):
+    size = len(bufs) * bufs[0].size
     return pl.pallas_call(
-        functools.partial(load_kernel, len(bufs)),
-        out_shape=[out, out],
-        in_specs=anywhere(len(bufs)),
-        out_specs=vmem(2),
-        scratch_shapes=[pltpu.SemaphoreType.DMA((len(bufs),))],
+        turned_kernel,
+        out_shape=jax.ShapeDtypeStruct((len(bufs), *bufs[0].shape), bufs[0].dtype),
+        in_specs=vmem(len(bufs)),
+        out_specs=vmem()[0],
         compiler_params=pltpu.CompilerParams(vmem_limit_bytes=2**20),
-        cost_estimate=pl.CostEstimate(flops=0, bytes_accessed=6 * out.size, transcendentals=0),
+        cost_estimate=pl.CostEstimate(flops=0, bytes_accessed=6 * size, transcendentals=0),
     )(*bufs)
 
 
-def first_kernel(early, later, n_col, n_row, ids_ref, parts_ref, sa_ref, sta_ref, *refs):
-    bufs, (s_ref, st_ref, sum_ref, z, straight, *scattered, sems) = refs[: len(later)], refs[len(later) :]
+def first_kernel(early, later, n_col, n_row, ids_ref, parts_ref, sta_ref, *refs):
+    sa, refs = refs[: len(early)], refs[len(early) :]
+    sb, (stb_ref, sum_ref, z, straight, *scattered) = refs[: len(later)], refs[len(later) :]
     spread_vectors(parts_ref, z, n_col, n_row)
-    fill(bufs, s_ref, st_ref, sems)
-    tiles = {at: (sa_ref, i, sta_ref, i) for i, at in enumerate(early)}
-    tiles.update({at: (s_ref, i, st_ref, i) for i, at in enumerate(later)})
+    turn_all(sb, stb_ref)
+    tiles = {at: (s, sta_ref, i) for i, (at, s) in enumerate(zip(early, sa))}
+    tiles.update({at: (s, stb_ref, i) for i, (at, s) in enumerate(zip(later, sb))})
     clear([straight])
     sum_ref[...] = sum_products(grouped(tiles, n_col, n_row), n_col, ids_ref, z, straight, scattered)
 
 
 def filter_kernel(early, later, late, n_col, n_row, ids_ref, parts_ref, sum_ref, *refs):
-    (sa_ref, sta_ref, sb_ref, stb_ref), refs = refs[:4], refs[4:]
+    (sta_ref, stb_ref), refs = refs[:2], refs[2:]
+    sa, refs = refs[: len(early)], refs[len(early) :]
+    sb, refs = refs[: len(later)], refs[len(later) :]
     bufs, (out_ref, s_ref, st_ref, z, now, prev, straight, *scattered, sems) = (
         refs[: len(late)],
         refs[len(late) :],
@@ -308,15 +312,15 @@
         copy.wait()
         turn(s_ref, st_ref, rest.index((g, f)), start, buf.shape[0])
 
-    tiles = {at: (s_ref, i, st_ref, i) for i, at in enumerate(rest)}
+    tiles = {at: (s_ref.at[i], st_ref, i) for i, at in enumerate(rest)}
     clear([straight])
     total = sum_products(grouped(tiles, n_col, n_row), n_col, ids_ref, z, straight, scattered)
     total += sum_ref[...]
     now[...] = total
     z[...] = total.astype(z.dtype)
 
-    tiles.update({at: (sa_ref, i, sta_ref, i) for i, at in enumerate(early)})
-    tiles.update({at: (sb_ref, i, stb_ref, i) for i, at in enumerate(later)})
+    tiles.update({at: (s, sta_ref, i) for i, (at, s) in enumerate(zip(early, sa))})
+    tiles.update({at: (s, stb_ref, i) for i, (at, s) in enumerate(zip(later, sb))})
     groups = grouped(tiles, n_col, n_row)
 
     def one_step(step, carry):
@@ -395,8 +399,9 @@
     outer = after(send(crossed, 0, 1, INNER), rank=1)
     mates += to_mate(two, over_near)
     mine, ids = regroup(stay, send(go, 0, 3), 8, per_piece)
-    sa, sta = load(own, near, over_own, over_near, *mates[:3])
-    three = pick(INNER, inner, outer, over_two, mine, sa, *mates[3:])
+    sa = [own, near, over_own, over_near, *mates[:3]]
+    sta = turned_tiles(*sa)
+    three = pick(INNER, inner, outer, over_two, mine, sta, *mates[3:])
 
     over_three = send(three[:half], 2, 0)
     side_three = send(over_two[half:], 0, 1)
@@ -405,15 +410,15 @@
     later = [(0, 2), (2, 2), (0, 3), (1, 2), (3, 1), (1, 3), (3, 2)]
     tiles_of = jax.ShapeDtypeStruct((len(later), slots, orb, orb), blocks.dtype)
     sums = jax.ShapeDtypeStruct((n_blocks, share, orb), jnp.float32)
-    sb, stb, total = pl.pallas_call(
+    sb = [two, over_two, three, *mates[3:]]
+    stb, total = pl.pallas_call(
         functools.partial(first_kernel, early, later, n_col, n_row),
-        out_shape=[tiles_of, tiles_of, sums],
-        in_specs=smem() + vmem(3) + anywhere(len(later)),
-        out_specs=vmem(3),
+        out_shape=[tiles_of, sums],
+        in_specs=smem() + vmem(2 + len(early + later)),
+        out_specs=vmem(2),
         scratch_shapes=[
             pltpu.VMEM((n_blocks, share, orb), jnp.bfloat16),
             *[pltpu.VMEM((n_blocks, share, orb), jnp.float32)] * (1 + SPLIT),
-            pltpu.SemaphoreType.DMA((len(later),)),
         ],
         compiler_params=pltpu.CompilerParams(vmem_limit_bytes=6 * 2**20),
         cost_estimate=pl.CostEstimate(
@@ -421,15 +426,15 @@
             bytes_accessed=6 * len(later) * own.size,
             transcendentals=0,
         ),
-    )(ids, mine, sa, sta, two, over_two, three, *mates[3:])
-    over_three, side_three = after(over_three, sb), after(side_three, sb)
+    )(ids, mine, sta, *sa, *sb)
+    over_three, side_three = after(over_three, stb), after(side_three, stb)
     late = [(2, 3, 0), (2, 3, half), (3, 3, 0), (3, 3, half)]
     late_bufs = [over_three, side_three, *to_mate(over_three, side_three)]
 
     done = pl.pallas_call(
         functools.partial(filter_kernel, early, later, late, n_col, n_row),
         out_shape=jax.ShapeDtypeStruct((n_dev, 2, share, rows), jnp.bfloat16),
-        in_specs=smem() + vmem(6) + anywhere(len(late)),
+        in_specs=smem() + vmem(4 + len(early + later)) + anywhere(len(late)),
         out_specs=vmem()[0],
         scratch_shapes=[
             *[pltpu.VMEM((2, slots, orb, orb), blocks.dtype)] * 2,
@@ -438,7 +443,7 @@
             pltpu.SemaphoreType.DMA((len(late),)),
         ],
         compiler_params=pltpu.CompilerParams(vmem_limit_bytes=12 * 2**20),
-    )(ids, mine, total, sa, sta, sb, stb, *late_bufs)
+    )(ids, mine, total, sta, stb, *sa, *sb, *late_bufs)
     back = lax.all_to_all(done, LANES, split_axis=0, concat_axis=0, tiled=True)
     whole = jax.ShapeDtypeStruct((rows, width), jnp.float32)
     return pl.pallas_call(

time: 88.9 us -> 88.7 us (level)
  Pallas kernels: 23.6 us -> 18.2 us
  waiting for transfers between devices: 29.9 us -> 35.2 us
    ppermute x23, waiting for transfers between devices: 29.9 us -> 35.2 us  [send(): return lax.ppermute(buf, LANES, pairs)]
    pallas_call x1, Pallas kernels: 6.55 us -> 4.45 us  [gather_plan(): pl.pallas_call(functools.partial(first_kernel, early, later, n_col, n_row...]
    pallas_call x1, Pallas kernels: 13.1 us -> 11.4 us  [gather_plan(): pl.pallas_call(functools.partial(filter_kernel, early, later, late, n_col...]
    pallas_call x1, Pallas kernels: 2.79 us -> 1.16 us  [turned_tiles(): pl.pallas_call(turned_kernel, out_shape=jax.ShapeDtypeStruct((len(bufs),...]
  transfers between devices with their start and end apart: 23 -> 23, of which waited for: 8 -> 9; matrix products, arithmetic and copies ran while one was open for 1% -> 1% of each run, Pallas kernels for 11% -> 7%
where the time goes in v17:
time: 88.7 us; the launch traced here: 88.4 us
  waiting for transfers between devices  35.2 us (40%)
  starting transfers between devices  19.3 us (22%)
  Pallas kernels  18.2 us (21%)
  blocking collectives  13.3 us (15%)
  local copies, waits for them, and re-layouts  1.61 us (2%)
    ppermute x23, waiting for transfers between devices, send(): return lax.ppermute(buf, LANES, pairs)  35.2 us
    ppermute x23, starting transfers between devices, send(): return lax.ppermute(buf, LANES, pairs)  19.3 us
    all_to_all x1, blocking collectives, gather_plan(): back = lax.all_to_all(done, LANES, split_axis=0, concat_axis=0, tiled=True)  13.3 us
    pallas_call x1, Pallas kernels, gather_plan(): pl.pallas_call(functools.partial(filter_kernel, early, later, late, n_col...  11.4 us
    pallas_call x1, Pallas kernels, gather_plan(): pl.pallas_call(functools.partial(first_kernel, early, later, n_col, n_row...  4.45 us
  transfers between devices with their start and end apart: 23, of which 9 were waited for; matrix products, arithmetic and copies ran while one was open for 1% of the time, Pallas kernels for 7%

profile of v17, /device:TPU:0, one launch (start us, length us, event | category | flops | bytes accessed | tf_op | source)
XLA Modules:
  0.0 88.4 jit_solution(3531374505784346222)
XLA Ops:
  1.1 2.6 %collective-permute-start.5 = (bf16[16,128,128]{2,1,0:T(8,128)(2,1)}, bf16[16,128,128]{2,1,0:T(8,128)(2,1)S(1)}, u32[]{:S(2)}, u32[]{:S(2)}) collective-permute-start(bf16[16,128,128]{2,1,0:T(8,128)(2,1)} %bitcast.3), channel_id=1, source_target_pairs={{0,8},{1,9},{2,10},{3,11},{4,12},{5,13},{6,14},{7,15},{8,0},{9,1},... | collective-permute-start | bytes 1572872 | tf_op jit(solution)/shard_map/ppermute | solution.py:365
  3.7 1.6 %collective-permute-start.4 = (bf16[16,128,128]{2,1,0:T(8,128)(2,1)}, bf16[16,128,128]{2,1,0:T(8,128)(2,1)S(1)}, u32[]{:S(2)}, u32[]{:S(2)}) collective-permute-start(bf16[16,128,128]{2,1,0:T(8,128)(2,1)} %bitcast.4), channel_id=1, source_target_pairs={{0,1},{1,0},{2,3},{3,2},{4,5},{5,4},{6,7},{7,6},{8,9},{9,8},{10,11... | collective-permute-start | bytes 1572872 | tf_op jit(solution)/shard_map/ppermute | solution.py:365
  6.7 0.9 %copy-done.1 = bf16[256,256]{1,0:T(8,128)(2,1)S(1)} copy-done((bf16[256,256]{1,0:T(8,128)(2,1)S(1)}, bf16[256,256]{1,0:T(8,128)(2,1)}, u32[]{:S(2)}) %copy-start.1) | copy-done | bytes 131096
  7.8 1.2 %collective-permute-done.came_ref = bf16[17,16,128]{2,1,0:T(8,128)(2,1)S(1)} collective-permute-done((bf16[17,16,128]{2,1,0:T(8,128)(2,1)S(1)}, bf16[17,16,128]{2,1,0:T(8,128)(2,1)S(1)}, u32[]{:S(2)}, u32[]{:S(2)}) %collective-permute-start) | collective-permute-done | bytes 69664 | tf_op jit(solution)/shard_map/ppermute | solution.py:365
  9.6 8.4 %collective-permute-done.1.came_ref = bf16[18,16,128]{2,1,0:T(8,128)(2,1)S(1)} collective-permute-done((bf16[18,16,128]{2,1,0:T(8,128)(2,1)S(1)}, bf16[18,16,128]{2,1,0:T(8,128)(2,1)S(1)}, u32[]{:S(2)}, u32[]{:S(2)}) %collective-permute-start.1) | collective-permute-done | bytes 73760 | tf_op jit(solution)/shard_map/ppermute | solution.py:365
  18.1 1.9 %collective-permute-start.2 = (bf16[20,16,128]{2,1,0:T(8,128)(2,1)S(1)}, bf16[20,16,128]{2,1,0:T(8,128)(2,1)S(1)}, u32[]{:S(2)}, u32[]{:S(2)}) collective-permute-start(bf16[20,16,128]{2,1,0:T(8,128)(2,1)S(1)} %get-tuple-element.19.refs_2_), channel_id=1, source_target_pairs={{0,1},{1,0},{2,3},{3,2},{4,5},{5,4},{6,7},{7,6},{8,9},{9,8},{10,11... | collective-permute-start | bytes 245768 | tf_op jit(solution)/shard_map/ppermute | solution.py:365
  20.7 1.4 %collective-permute-start.12 = (bf16[16,128,128]{2,1,0:T(8,128)(2,1)S(1)}, bf16[16,128,128]{2,1,0:T(8,128)(2,1)S(1)}, u32[]{:S(2)}, u32[]{:S(2)}) collective-permute-start(bf16[16,128,128]{2,1,0:T(8,128)(2,1)S(1)} %shard_map.59.one_ref), channel_id=1, source_target_pairs={{1,0},{2,3},{5,4},{6,7},{9,8},{10,11},{13,12},{14,15},{17,16},{18,... | collective-permute-start | bytes 1572872 | tf_op jit(solution)/shard_map/ppermute | solution.py:365
  22.1 1.6 %collective-permute-start.7 = (bf16[16,128,128]{2,1,0:T(8,128)(2,1)S(1)}, bf16[16,128,128]{2,1,0:T(8,128)(2,1)S(1)}, u32[]{:S(2)}, u32[]{:S(2)}) collective-permute-start(bf16[16,128,128]{2,1,0:T(8,128)(2,1)S(1)} %shard_map.55.refs_1_.refs_3_), channel_id=1, source_target_pairs={{0,8},{1,9},{2,10},{3,11},{4,12},{5,13},{6,14},{7,15},{8,0},{9,1},... | collective-permute-start | bytes 1572872 | tf_op jit(solution)/shard_map/ppermute | solution.py:365
  24.3 1.3 %collective-permute-start.14 = (bf16[16,128,128]{2,1,0:T(8,128)(2,1)S(1)}, bf16[16,128,128]{2,1,0:T(8,128)(2,1)S(1)}, u32[]{:S(2)}, u32[]{:S(2)}) collective-permute-start(bf16[16,128,128]{2,1,0:T(8,128)(2,1)S(1)} %shard_map.58.one_ref), channel_id=1, source_target_pairs={{1,0},{2,3},{5,4},{6,7},{9,8},{10,11},{13,12},{14,15},{17,16},{18,... | collective-permute-start | bytes 1572872 | tf_op jit(solution)/shard_map/ppermute | solution.py:365
  25.6 12.3 %collective-permute-done.12.refs_0_ = bf16[16,128,128]{2,1,0:T(8,128)(2,1)S(1)} collective-permute-done((bf16[16,128,128]{2,1,0:T(8,128)(2,1)S(1)}, bf16[16,128,128]{2,1,0:T(8,128)(2,1)S(1)}, u32[]{:S(2)}, u32[]{:S(2)}) %collective-permute-start.12) | collective-permute-done | bytes 524320 | tf_op jit(solution)/shard_map/ppermute | solution.py:365
  38.0 1.6 %collective-permute-start.13 = (bf16[16,128,128]{2,1,0:T(8,128)(2,1)S(1)}, bf16[16,128,128]{2,1,0:T(8,128)(2,1)S(1)}, u32[]{:S(2)}, u32[]{:S(2)}) collective-permute-start(bf16[16,128,128]{2,1,0:T(8,128)(2,1)S(1)} %shard_map.61.refs_7_.refs_9_), channel_id=1, source_target_pairs={{0,8},{1,9},{2,10},{3,11},{4,12},{5,13},{6,14},{7,15},{8,0},{9,1},... | collective-permute-start | bytes 1572872 | tf_op jit(solution)/shard_map/ppermute | solution.py:365
  40.1 1.0 %collective-permute-start.3 = (bf16[24,16,128]{2,1,0:T(8,128)(2,1)S(1)}, bf16[24,16,128]{2,1,0:T(8,128)(2,1)S(1)}, u32[]{:S(2)}, u32[]{:S(2)}) collective-permute-start(bf16[24,16,128]{2,1,0:T(8,128)(2,1)S(1)} %get-tuple-element.21.refs_1_), channel_id=1, source_target_pairs={{0,3},{1,2},{2,1},{3,0},{4,7},{5,6},{6,5},{7,4},{8,11},{9,10},{10,... | collective-permute-start | bytes 294920 | tf_op jit(solution)/shard_map/ppermute | solution.py:365
  41.0 5.7 %collective-permute-done.3.came_ref = bf16[24,16,128]{2,1,0:T(8,128)(2,1)S(1)} collective-permute-done((bf16[24,16,128]{2,1,0:T(8,128)(2,1)S(1)}, bf16[24,16,128]{2,1,0:T(8,128)(2,1)S(1)}, u32[]{:S(2)}, u32[]{:S(2)}) %collective-permute-start.3) | collective-permute-done | bytes 98336 | tf_op jit(solution)/shard_map/ppermute | solution.py:365
  46.8 1.2 %shard_map.57.refs_2_.sta_ref.refs_0_ = bf16[7,16,128,128]{3,2,1,0:T(8,128)(2,1)S(1)} custom-call(bf16[16,128,128]{2,1,0:T(8,128)(2,1)S(1)} %bitcast.6, bf16[16,128,128]{2,1,0:T(8,128)(2,1)S(1)} %shard_map.55.refs_1_.refs_3_, bf16[16,128,128]{2,1,0:T(8,128)(2,1)S(1)} %collective-permute-done.5.refs_1_.refs_2_.refs_4_, ...), custom_call_target="tpu_custom_call" | custom-call | bytes 11010048 | tf_op jit(solution)/shard_map/pallas_call | solution.py:272
  47.9 3.1 %collective-permute-done.14.refs_0_ = bf16[16,128,128]{2,1,0:T(8,128)(2,1)S(1)} collective-permute-done((bf16[16,128,128]{2,1,0:T(8,128)(2,1)S(1)}, bf16[16,128,128]{2,1,0:T(8,128)(2,1)S(1)}, u32[]{:S(2)}, u32[]{:S(2)}) %collective-permute-start.14) | collective-permute-done | bytes 524320 | tf_op jit(solution)/shard_map/ppermute | solution.py:365
  51.7 1.6 %collective-permute-start.19 = (bf16[8,128,128]{2,1,0:T(8,128)(2,1)S(1)}, bf16[8,128,128]{2,1,0:T(8,128)(2,1)S(1)}, u32[]{:S(2)}, u32[]{:S(2)}) collective-permute-start(bf16[8,128,128]{2,1,0:T(8,128)(2,1)S(1)} %slice.8), channel_id=1, source_target_pairs={{0,8},{1,9},{2,10},{3,11},{4,12},{5,13},{6,14},{7,15},{8,0},{9,1},... | collective-permute-start | bytes 786440 | tf_op jit(solution)/shard_map/ppermute | solution.py:365
  53.3 0.7 collective-permute-start.20
  54.0 4.5 %shard_map.64 = (bf16[7,16,128,128]{3,2,1,0:T(8,128)(2,1)S(1)}, f32[32,16,128]{2,1,0:T(8,128)S(1)}) custom-call(s32[16,128]{1,0:T(8,128)S(1)} %get-tuple-element.22.ids_ref, bf16[32,16,128]{2,1,0:T(8,128)(2,1)S(1)} %get-tuple-element.23.refs_1_.parts_ref, bf16[7,16,128,128]{3,2,1,0:T(8,128)(2,1)S(1)} %shard_map.57.refs_2_.sta_ref.refs_0_, ...), custom_call_target="tpu_custom_call" | custom-call | flops 234881024 | bytes 11010048 | tf_op jit(solution)/shard_map/pallas_call | solution.py:414
  58.5 1.5 %collective-permute-done.19.refs_0_ = bf16[8,128,128]{2,1,0:T(8,128)(2,1)S(1)} collective-permute-done((bf16[8,128,128]{2,1,0:T(8,128)(2,1)S(1)}, bf16[8,128,128]{2,1,0:T(8,128)(2,1)S(1)}, u32[]{:S(2)}, u32[]{:S(2)}) %collective-permute-start.19) | collective-permute-done | bytes 262176 | tf_op jit(solution)/shard_map/ppermute | solution.py:365
  60.0 1.3 %collective-permute-done.20.refs_0_ = bf16[8,128,128]{2,1,0:T(8,128)(2,1)S(1)} collective-permute-done((bf16[8,128,128]{2,1,0:T(8,128)(2,1)S(1)}, bf16[8,128,128]{2,1,0:T(8,128)(2,1)S(1)}, u32[]{:S(2)}, u32[]{:S(2)}) %collective-permute-start.20) | collective-permute-done | bytes 262176 | tf_op jit(solution)/shard_map/ppermute | solution.py:365
  61.5 1.3 %collective-permute-done.22.refs_19_ = bf16[8,128,128]{2,1,0:T(8,128)(2,1)S(1)} collective-permute-done((bf16[8,128,128]{2,1,0:T(8,128)(2,1)S(1)}, bf16[8,128,128]{2,1,0:T(8,128)(2,1)S(1)}, u32[]{:S(2)}, u32[]{:S(2)}) %collective-permute-start.22) | collective-permute-done | bytes 262176 | tf_op jit(solution)/shard_map/ppermute | solution.py:365
  62.8 11.4 %shard_map.67 = bf16[16,2,16,256]{3,2,1,0:T(8,128)(2,1)S(1)} custom-call(s32[16,128]{1,0:T(8,128)S(1)} %get-tuple-element.22.ids_ref, bf16[32,16,128]{2,1,0:T(8,128)(2,1)S(1)} %get-tuple-element.23.refs_1_.parts_ref, f32[32,16,128]{2,1,0:T(8,128)S(1)} %get-tuple-element.24.sum_ref, bf16[7,16,128,128]{3,2,1,0:T(8,128)(2,1)S(1)} %shard_map.57.refs_2_.sta_ref.refs_0_, ...), custom_call_target="tpu_custom_call" | custom-call | tf_op jit(solution)/shard_map/pallas_call | solution.py:434
  74.2 13.3 %all_to_all.5.back_ref = bf16[16,2,16,256]{3,2,1,0:T(8,128)(2,1)S(1)} all-to-all(bf16[16,2,16,256]{3,2,1,0:T(8,128)(2,1)S(1)} %shard_map.67), channel_id=1, replica_groups=mesh['dom'=2,'col'=4,'row'=4] {'col','row'}, dimensions={0} | all-to-all | bytes 524288 | tf_op jit(solution)/shard_map/all_to_all | solution.py:447
  87.5 0.9 %shard_map.68 = (f32[256,256]{1,0:T(8,128)}, f32[256,256]{1,0:T(8,128)}) custom-call(bf16[16,2,16,256]{3,2,1,0:T(8,128)(2,1)S(1)} %all_to_all.5.back_ref), custom_call_target="tpu_custom_call" | custom-call | tf_op jit(solution)/shard_map/pallas_call | solution.py:449
  (50 shorter events, 5.4 us)
Async XLA Ops:
  0.6 19.3 %collective-permute-start.6 = (bf16[16,128,128]{2,1,0:T(8,128)(2,1)}, bf16[16,128,128]{2,1,0:T(8,128)(2,1)S(1)}, u32[]{:S(2)}, u32[]{:S(2)}) collective-permute-start(bf16[16,128,128]{2,1,0:T(8,128)(2,1)} %bitcast.2), channel_id=1, source_target_pairs={{0,4},{1,5},{2,6},{3,7},{4,0},{5,1},{6,2},{7,3},{8,12},{9,13},{10,... | collective-permute-start | bytes 1572872 | tf_op jit(solution)/shard_map/ppermute | solution.py:365
  1.1 18.8 %collective-permute-start.5 = (bf16[16,128,128]{2,1,0:T(8,128)(2,1)}, bf16[16,128,128]{2,1,0:T(8,128)(2,1)S(1)}, u32[]{:S(2)}, u32[]{:S(2)}) collective-permute-start(bf16[16,128,128]{2,1,0:T(8,128)(2,1)} %bitcast.3), channel_id=1, source_target_pairs={{0,8},{1,9},{2,10},{3,11},{4,12},{5,13},{6,14},{7,15},{8,0},{9,1},... | collective-permute-start | bytes 1572872 | tf_op jit(solution)/shard_map/ppermute | solution.py:365
  3.7 16.2 %collective-permute-start.4 = (bf16[16,128,128]{2,1,0:T(8,128)(2,1)}, bf16[16,128,128]{2,1,0:T(8,128)(2,1)S(1)}, u32[]{:S(2)}, u32[]{:S(2)}) collective-permute-start(bf16[16,128,128]{2,1,0:T(8,128)(2,1)} %bitcast.4), channel_id=1, source_target_pairs={{0,1},{1,0},{2,3},{3,2},{4,5},{5,4},{6,7},{7,6},{8,9},{9,8},{10,11... | collective-permute-start | bytes 1572872 | tf_op jit(solution)/shard_map/ppermute | solution.py:365
  5.3 15.4 %collective-permute-start.11 = (bf16[16,128,128]{2,1,0:T(8,128)(2,1)}, bf16[16,128,128]{2,1,0:T(8,128)(2,1)S(1)}, u32[]{:S(2)}, u32[]{:S(2)}) collective-permute-start(bf16[16,128,128]{2,1,0:T(8,128)(2,1)} %bitcast.5), channel_id=1, source_target_pairs={{1,2},{2,1},{5,6},{6,5},{9,10},{10,9},{13,14},{14,13},{17,18},{18,... | collective-permute-start | bytes 1572872 | tf_op jit(solution)/shard_map/ppermute | solution.py:365
  7.7 1.3 %collective-permute-start = (bf16[17,16,128]{2,1,0:T(8,128)(2,1)S(1)}, bf16[17,16,128]{2,1,0:T(8,128)(2,1)S(1)}, u32[]{:S(2)}, u32[]{:S(2)}) collective-permute-start(bf16[17,16,128]{2,1,0:T(8,128)(2,1)S(1)} %get-tuple-element.15), channel_id=1, source_target_pairs={{0,4},{1,5},{2,6},{3,7},{4,0},{5,1},{6,2},{7,3},{8,12},{9,13},{10,... | collective-permute-start | bytes 208904 | tf_op jit(solution)/shard_map/ppermute | solution.py:365
  9.0 9.0 %collective-permute-start.1 = (bf16[18,16,128]{2,1,0:T(8,128)(2,1)S(1)}, bf16[18,16,128]{2,1,0:T(8,128)(2,1)S(1)}, u32[]{:S(2)}, u32[]{:S(2)}) collective-permute-start(bf16[18,16,128]{2,1,0:T(8,128)(2,1)S(1)} %get-tuple-element.17), channel_id=1, source_target_pairs={{0,8},{1,9},{2,10},{3,11},{4,12},{5,13},{6,14},{7,15},{8,0},{9,1},... | collective-permute-start | bytes 221192 | tf_op jit(solution)/shard_map/ppermute | solution.py:365
  18.1 5.7 %collective-permute-start.2 = (bf16[20,16,128]{2,1,0:T(8,128)(2,1)S(1)}, bf16[20,16,128]{2,1,0:T(8,128)(2,1)S(1)}, u32[]{:S(2)}, u32[]{:S(2)}) collective-permute-start(bf16[20,16,128]{2,1,0:T(8,128)(2,1)S(1)} %get-tuple-element.19.refs_2_), channel_id=1, source_target_pairs={{0,1},{1,0},{2,3},{3,2},{4,5},{5,4},{6,7},{7,6},{8,9},{9,8},{10,11... | collective-permute-start | bytes 245768 | tf_op jit(solution)/shard_map/ppermute | solution.py:365
  20.0 4.3 %collective-permute-start.10 = (bf16[16,128,128]{2,1,0:T(8,128)(2,1)S(1)}, bf16[16,128,128]{2,1,0:T(8,128)(2,1)S(1)}, u32[]{:S(2)}, u32[]{:S(2)}) collective-permute-start(bf16[16,128,128]{2,1,0:T(8,128)(2,1)S(1)} %shard_map.55.refs_1_.refs_3_), channel_id=1, source_target_pairs={{1,2},{2,1},{5,6},{6,5},{9,10},{10,9},{13,14},{14,13},{17,18},{18,... | collective-permute-start | bytes 1572872 | tf_op jit(solution)/shard_map/ppermute | solution.py:365
  20.7 26.1 %copy-start = (bf16[1,1,16,128,128]{4,3,2,1,0:T(8,128)(2,1)S(1)}, bf16[1,1,16,128,128]{4,3,2,1,0:T(8,128)(2,1)}, u32[]{:S(2)}) copy-start(bf16[1,1,16,128,128]{4,3,2,1,0:T(8,128)(2,1)} %param.4) | copy-start | bytes 1572868
  20.7 17.2 %collective-permute-start.12 = (bf16[16,128,128]{2,1,0:T(8,128)(2,1)S(1)}, bf16[16,128,128]{2,1,0:T(8,128)(2,1)S(1)}, u32[]{:S(2)}, u32[]{:S(2)}) collective-permute-start(bf16[16,128,128]{2,1,0:T(8,128)(2,1)S(1)} %shard_map.59.one_ref), channel_id=1, source_target_pairs={{1,0},{2,3},{5,4},{6,7},{9,8},{10,11},{13,12},{14,15},{17,16},{18,... | collective-permute-start | bytes 1572872 | tf_op jit(solution)/shard_map/ppermute | solution.py:365
  22.1 15.8 %collective-permute-start.7 = (bf16[16,128,128]{2,1,0:T(8,128)(2,1)S(1)}, bf16[16,128,128]{2,1,0:T(8,128)(2,1)S(1)}, u32[]{:S(2)}, u32[]{:S(2)}) collective-permute-start(bf16[16,128,128]{2,1,0:T(8,128)(2,1)S(1)} %shard_map.55.refs_1_.refs_3_), channel_id=1, source_target_pairs={{0,8},{1,9},{2,10},{3,11},{4,12},{5,13},{6,14},{7,15},{8,0},{9,1},... | collective-permute-start | bytes 1572872 | tf_op jit(solution)/shard_map/ppermute | solution.py:365
  23.7 14.2 %collective-permute-start.9 = (bf16[16,128,128]{2,1,0:T(8,128)(2,1)S(1)}, bf16[16,128,128]{2,1,0:T(8,128)(2,1)S(1)}, u32[]{:S(2)}, u32[]{:S(2)}) collective-permute-start(bf16[16,128,128]{2,1,0:T(8,128)(2,1)S(1)} %collective-permute-done.5.refs_1_.refs_2_.refs_4_), channel_id=1, source_target_pairs={{0,4},{1,5},{2,6},{3,7},{4,0},{5,1},{6,2},{7,3},{8,12},{9,13},{10,... | collective-permute-start | bytes 1572872 | tf_op jit(solution)/shard_map/ppermute | solution.py:365
  23.7 14.2 %collective-permute-start.8 = (bf16[16,128,128]{2,1,0:T(8,128)(2,1)S(1)}, bf16[16,128,128]{2,1,0:T(8,128)(2,1)S(1)}, u32[]{:S(2)}, u32[]{:S(2)}) collective-permute-start(bf16[16,128,128]{2,1,0:T(8,128)(2,1)S(1)} %shard_map.55.refs_1_.refs_3_), channel_id=1, source_target_pairs={{0,4},{1,5},{2,6},{3,7},{4,0},{5,1},{6,2},{7,3},{8,12},{9,13},{10,... | collective-permute-start | bytes 1572872 | tf_op jit(solution)/shard_map/ppermute | solution.py:365
  24.3 26.7 %collective-permute-start.14 = (bf16[16,128,128]{2,1,0:T(8,128)(2,1)S(1)}, bf16[16,128,128]{2,1,0:T(8,128)(2,1)S(1)}, u32[]{:S(2)}, u32[]{:S(2)}) collective-permute-start(bf16[16,128,128]{2,1,0:T(8,128)(2,1)S(1)} %shard_map.58.one_ref), channel_id=1, source_target_pairs={{1,0},{2,3},{5,4},{6,7},{9,8},{10,11},{13,12},{14,15},{17,16},{18,... | collective-permute-start | bytes 1572872 | tf_op jit(solution)/shard_map/ppermute | solution.py:365
  38.0 13.0 %collective-permute-start.13 = (bf16[16,128,128]{2,1,0:T(8,128)(2,1)S(1)}, bf16[16,128,128]{2,1,0:T(8,128)(2,1)S(1)}, u32[]{:S(2)}, u32[]{:S(2)}) collective-permute-start(bf16[16,128,128]{2,1,0:T(8,128)(2,1)S(1)} %shard_map.61.refs_7_.refs_9_), channel_id=1, source_target_pairs={{0,8},{1,9},{2,10},{3,11},{4,12},{5,13},{6,14},{7,15},{8,0},{9,1},... | collective-permute-start | bytes 1572872 | tf_op jit(solution)/shard_map/ppermute | solution.py:365
  39.6 11.4 %collective-permute-start.15 = (bf16[16,128,128]{2,1,0:T(8,128)(2,1)S(1)}, bf16[16,128,128]{2,1,0:T(8,128)(2,1)S(1)}, u32[]{:S(2)}, u32[]{:S(2)}) collective-permute-start(bf16[16,128,128]{2,1,0:T(8,128)(2,1)S(1)} %shard_map.61.refs_7_.refs_9_), channel_id=1, source_target_pairs={{0,4},{1,5},{2,6},{3,7},{4,0},{5,1},{6,2},{7,3},{8,12},{9,13},{10,... | collective-permute-start | bytes 1572872 | tf_op jit(solution)/shard_map/ppermute | solution.py:365
  39.6 11.5 %collective-permute-start.16 = (bf16[16,128,128]{2,1,0:T(8,128)(2,1)S(1)}, bf16[16,128,128]{2,1,0:T(8,128)(2,1)S(1)}, u32[]{:S(2)}, u32[]{:S(2)}) collective-permute-start(bf16[16,128,128]{2,1,0:T(8,128)(2,1)S(1)} %shard_map.56.refs_3_.refs_0_.refs_5_), channel_id=1, source_target_pairs={{0,4},{1,5},{2,6},{3,7},{4,0},{5,1},{6,2},{7,3},{8,12},{9,13},{10,... | collective-permute-start | bytes 1572872 | tf_op jit(solution)/shard_map/ppermute | solution.py:365
  40.1 6.7 %collective-permute-start.3 = (bf16[24,16,128]{2,1,0:T(8,128)(2,1)S(1)}, bf16[24,16,128]{2,1,0:T(8,128)(2,1)S(1)}, u32[]{:S(2)}, u32[]{:S(2)}) collective-permute-start(bf16[24,16,128]{2,1,0:T(8,128)(2,1)S(1)} %get-tuple-element.21.refs_1_), channel_id=1, source_target_pairs={{0,3},{1,2},{2,1},{3,0},{4,7},{5,6},{6,5},{7,4},{8,11},{9,10},{10,... | collective-permute-start | bytes 294920 | tf_op jit(solution)/shard_map/ppermute | solution.py:365
  51.0 3.0 %collective-permute-start.18 = (bf16[16,128,128]{2,1,0:T(8,128)(2,1)S(1)}, bf16[16,128,128]{2,1,0:T(8,128)(2,1)S(1)}, u32[]{:S(2)}, u32[]{:S(2)}) collective-permute-start(bf16[16,128,128]{2,1,0:T(8,128)(2,1)S(1)} %collective-permute-done.13.refs_0_.refs_8_.refs_10_), channel_id=1, source_target_pairs={{0,4},{1,5},{2,6},{3,7},{4,0},{5,1},{6,2},{7,3},{8,12},{9,13},{10,... | collective-permute-start | bytes 1572872 | tf_op jit(solution)/shard_map/ppermute | solution.py:365
  51.1 2.9 %collective-permute-start.17 = (bf16[16,128,128]{2,1,0:T(8,128)(2,1)S(1)}, bf16[16,128,128]{2,1,0:T(8,128)(2,1)S(1)}, u32[]{:S(2)}, u32[]{:S(2)}) collective-permute-start(bf16[16,128,128]{2,1,0:T(8,128)(2,1)S(1)} %shard_map.63.refs_9_.refs_11_), channel_id=1, source_target_pairs={{0,4},{1,5},{2,6},{3,7},{4,0},{5,1},{6,2},{7,3},{8,12},{9,13},{10,... | collective-permute-start | bytes 1572872 | tf_op jit(solution)/shard_map/ppermute | solution.py:365
  51.7 8.3 %collective-permute-start.19 = (bf16[8,128,128]{2,1,0:T(8,128)(2,1)S(1)}, bf16[8,128,128]{2,1,0:T(8,128)(2,1)S(1)}, u32[]{:S(2)}, u32[]{:S(2)}) collective-permute-start(bf16[8,128,128]{2,1,0:T(8,128)(2,1)S(1)} %slice.8), channel_id=1, source_target_pairs={{0,8},{1,9},{2,10},{3,11},{4,12},{5,13},{6,14},{7,15},{8,0},{9,1},... | collective-permute-start | bytes 786440 | tf_op jit(solution)/shard_map/ppermute | solution.py:365
  53.3 8.0 %collective-permute-start.20 = (bf16[8,128,128]{2,1,0:T(8,128)(2,1)S(1)}, bf16[8,128,128]{2,1,0:T(8,128)(2,1)S(1)}, u32[]{:S(2)}, u32[]{:S(2)}) collective-permute-start(bf16[8,128,128]{2,1,0:T(8,128)(2,1)S(1)} %slice.9), channel_id=1, source_target_pairs={{0,1},{1,0},{2,3},{3,2},{4,5},{5,4},{6,7},{7,6},{8,9},{9,8},{10,11... | collective-permute-start | bytes 786440 | tf_op jit(solution)/shard_map/ppermute | solution.py:365
  60.0 1.5 %collective-permute-start.21 = (bf16[8,128,128]{2,1,0:T(8,128)(2,1)S(1)}, bf16[8,128,128]{2,1,0:T(8,128)(2,1)S(1)}, u32[]{:S(2)}, u32[]{:S(2)}) collective-permute-start(bf16[8,128,128]{2,1,0:T(8,128)(2,1)S(1)} %shard_map.65.refs_16_), channel_id=1, source_target_pairs={{0,4},{1,5},{2,6},{3,7},{4,0},{5,1},{6,2},{7,3},{8,12},{9,13},{10,... | collective-permute-start | bytes 786440 | tf_op jit(solution)/shard_map/ppermute | solution.py:365
  61.3 1.5 %collective-permute-start.22 = (bf16[8,128,128]{2,1,0:T(8,128)(2,1)S(1)}, bf16[8,128,128]{2,1,0:T(8,128)(2,1)S(1)}, u32[]{:S(2)}, u32[]{:S(2)}) collective-permute-start(bf16[8,128,128]{2,1,0:T(8,128)(2,1)S(1)} %shard_map.66.refs_17_), channel_id=1, source_target_pairs={{0,4},{1,5},{2,6},{3,7},{4,0},{5,1},{6,2},{7,3},{8,12},{9,13},{10,... | collective-permute-start | bytes 786440 | tf_op jit(solution)/shard_map/ppermute | solution.py:365
  (1 other events, 0.9 us)

commit v18 on v17

--- a/solution.py
+++ b/solution.py
@@ -10,7 +10,7 @@
 PER_ROW = 2
 DEG = 4
 SPLIT = 4
-UNROLL = 2
+UNROLL = 4
 GATHER_LIMIT = 12 * 2**20
 LANES = ("col", "row")
 INNER = (1, 2)
@@ -370,7 +370,7 @@
     own = blocks[0, 0]
     near = send(own, 0, 1)
     inner = send(own, 0, 3, INNER)
-    over_own = send(own, 2, 0)
+    over_own = after(send(own, 2, 0), rank=1)
 
     own_cols = jnp.broadcast_to(jnp.pad(cols[0, 0], (0, orb - slots)), (share, orb))
     shares = jax.ShapeDtypeStruct((n_dev // 2 * per_piece + 1, share, orb), vectors.dtype)

time: 88.7 us -> 86.2 us (0.972)
  Pallas kernels: 18.2 us -> 16.9 us
  starting transfers between devices: 19.3 us -> 18.4 us
    pallas_call x1, Pallas kernels: 11.4 us -> 10.3 us  [gather_plan(): pl.pallas_call(functools.partial(filter_kernel, early, later, late, n_col...]
    ppermute x23, starting transfers between devices: 19.3 us -> 18.4 us  [send(): return lax.ppermute(buf, LANES, pairs)]
  transfers between devices with their start and end apart: 23 -> 23, of which waited for: 9 -> 10; matrix products, arithmetic and copies ran while one was open for 1% -> 1% of each run, Pallas kernels for 7% -> 7%
where the time goes in v18:
time: 86.2 us; the launch traced here: 85.9 us
  waiting for transfers between devices  34.9 us (40%)
  starting transfers between devices  18.4 us (21%)
  Pallas kernels  16.9 us (20%)
  blocking collectives  13.2 us (15%)
  local copies, waits for them, and re-layouts  1.61 us (2%)
    ppermute x23, waiting for transfers between devices, send(): return lax.ppermute(buf, LANES, pairs)  34.9 us
    ppermute x23, starting transfers between devices, send(): return lax.ppermute(buf, LANES, pairs)  18.4 us
    all_to_all x1, blocking collectives, gather_plan(): back = lax.all_to_all(done, LANES, split_axis=0, concat_axis=0, tiled=True)  13.2 us
    pallas_call x1, Pallas kernels, gather_plan(): pl.pallas_call(functools.partial(filter_kernel, early, later, late, n_col...  10.3 us
    pallas_call x1, Pallas kernels, gather_plan(): pl.pallas_call(functools.partial(first_kernel, early, later, n_col, n_row...  4.22 us
  transfers between devices with their start and end apart: 23, of which 10 were waited for; matrix products, arithmetic and copies ran while one was open for 1% of the time, Pallas kernels for 7%

profile of v18, /device:TPU:0, one launch (start us, length us, event | category | flops | bytes accessed | tf_op | source)
XLA Modules:
  0.0 85.9 jit_solution(11806961540252985089)
XLA Ops:
  0.6 3.0 %collective-permute-start.5 = (bf16[16,128,128]{2,1,0:T(8,128)(2,1)}, bf16[16,128,128]{2,1,0:T(8,128)(2,1)S(1)}, u32[]{:S(2)}, u32[]{:S(2)}) collective-permute-start(bf16[16,128,128]{2,1,0:T(8,128)(2,1)} %bitcast.2), channel_id=1, source_target_pairs={{0,8},{1,9},{2,10},{3,11},{4,12},{5,13},{6,14},{7,15},{8,0},{9,1},... | collective-permute-start | bytes 1572872 | tf_op jit(solution)/shard_map/ppermute | solution.py:365
  3.7 1.6 %collective-permute-start.4 = (bf16[16,128,128]{2,1,0:T(8,128)(2,1)}, bf16[16,128,128]{2,1,0:T(8,128)(2,1)S(1)}, u32[]{:S(2)}, u32[]{:S(2)}) collective-permute-start(bf16[16,128,128]{2,1,0:T(8,128)(2,1)} %bitcast.4), channel_id=1, source_target_pairs={{0,1},{1,0},{2,3},{3,2},{4,5},{5,4},{6,7},{7,6},{8,9},{9,8},{10,11... | collective-permute-start | bytes 1572872 | tf_op jit(solution)/shard_map/ppermute | solution.py:365
  5.2 0.7 collective-permute-start.11
  6.6 0.9 %copy-done.1 = bf16[256,256]{1,0:T(8,128)(2,1)S(1)} copy-done((bf16[256,256]{1,0:T(8,128)(2,1)S(1)}, bf16[256,256]{1,0:T(8,128)(2,1)}, u32[]{:S(2)}) %copy-start.1) | copy-done | bytes 131096
  7.9 1.0 %collective-permute-done.came_ref = bf16[17,16,128]{2,1,0:T(8,128)(2,1)S(1)} collective-permute-done((bf16[17,16,128]{2,1,0:T(8,128)(2,1)S(1)}, bf16[17,16,128]{2,1,0:T(8,128)(2,1)S(1)}, u32[]{:S(2)}, u32[]{:S(2)}) %collective-permute-start) | collective-permute-done | bytes 69664 | tf_op jit(solution)/shard_map/ppermute | solution.py:365
  9.5 7.8 %collective-permute-done.1.came_ref = bf16[18,16,128]{2,1,0:T(8,128)(2,1)S(1)} collective-permute-done((bf16[18,16,128]{2,1,0:T(8,128)(2,1)S(1)}, bf16[18,16,128]{2,1,0:T(8,128)(2,1)S(1)}, u32[]{:S(2)}, u32[]{:S(2)}) %collective-permute-start.1) | collective-permute-done | bytes 73760 | tf_op jit(solution)/shard_map/ppermute | solution.py:365
  17.4 1.9 %collective-permute-start.2 = (bf16[20,16,128]{2,1,0:T(8,128)(2,1)S(1)}, bf16[20,16,128]{2,1,0:T(8,128)(2,1)S(1)}, u32[]{:S(2)}, u32[]{:S(2)}) collective-permute-start(bf16[20,16,128]{2,1,0:T(8,128)(2,1)S(1)} %get-tuple-element.19.refs_2_), channel_id=1, source_target_pairs={{0,1},{1,0},{2,3},{3,2},{4,5},{5,4},{6,7},{7,6},{8,9},{9,8},{10,11... | collective-permute-start | bytes 245768 | tf_op jit(solution)/shard_map/ppermute | solution.py:365
  19.3 0.7 collective-permute-start.10
  20.0 1.4 %collective-permute-start.12 = (bf16[16,128,128]{2,1,0:T(8,128)(2,1)S(1)}, bf16[16,128,128]{2,1,0:T(8,128)(2,1)S(1)}, u32[]{:S(2)}, u32[]{:S(2)}) collective-permute-start(bf16[16,128,128]{2,1,0:T(8,128)(2,1)S(1)} %shard_map.60.one_ref), channel_id=1, source_target_pairs={{1,0},{2,3},{5,4},{6,7},{9,8},{10,11},{13,12},{14,15},{17,16},{18,... | collective-permute-start | bytes 1572872 | tf_op jit(solution)/shard_map/ppermute | solution.py:365
  21.4 1.6 %collective-permute-start.7 = (bf16[16,128,128]{2,1,0:T(8,128)(2,1)S(1)}, bf16[16,128,128]{2,1,0:T(8,128)(2,1)S(1)}, u32[]{:S(2)}, u32[]{:S(2)}) collective-permute-start(bf16[16,128,128]{2,1,0:T(8,128)(2,1)S(1)} %shard_map.56.refs_1_.refs_3_), channel_id=1, source_target_pairs={{0,8},{1,9},{2,10},{3,11},{4,12},{5,13},{6,14},{7,15},{8,0},{9,1},... | collective-permute-start | bytes 1572872 | tf_op jit(solution)/shard_map/ppermute | solution.py:365
  23.6 1.3 %collective-permute-start.14 = (bf16[16,128,128]{2,1,0:T(8,128)(2,1)S(1)}, bf16[16,128,128]{2,1,0:T(8,128)(2,1)S(1)}, u32[]{:S(2)}, u32[]{:S(2)}) collective-permute-start(bf16[16,128,128]{2,1,0:T(8,128)(2,1)S(1)} %shard_map.59.one_ref), channel_id=1, source_target_pairs={{1,0},{2,3},{5,4},{6,7},{9,8},{10,11},{13,12},{14,15},{17,16},{18,... | collective-permute-start | bytes 1572872 | tf_op jit(solution)/shard_map/ppermute | solution.py:365
  24.9 12.1 %collective-permute-done.12.refs_0_ = bf16[16,128,128]{2,1,0:T(8,128)(2,1)S(1)} collective-permute-done((bf16[16,128,128]{2,1,0:T(8,128)(2,1)S(1)}, bf16[16,128,128]{2,1,0:T(8,128)(2,1)S(1)}, u32[]{:S(2)}, u32[]{:S(2)}) %collective-permute-start.12) | collective-permute-done | bytes 524320 | tf_op jit(solution)/shard_map/ppermute | solution.py:365
  37.1 1.8 %collective-permute-start.13 = (bf16[16,128,128]{2,1,0:T(8,128)(2,1)S(1)}, bf16[16,128,128]{2,1,0:T(8,128)(2,1)S(1)}, u32[]{:S(2)}, u32[]{:S(2)}) collective-permute-start(bf16[16,128,128]{2,1,0:T(8,128)(2,1)S(1)} %shard_map.62.refs_7_.refs_9_), channel_id=1, source_target_pairs={{0,8},{1,9},{2,10},{3,11},{4,12},{5,13},{6,14},{7,15},{8,0},{9,1},... | collective-permute-start | bytes 1572872 | tf_op jit(solution)/shard_map/ppermute | solution.py:365
  39.7 6.3 %collective-permute-done.3.came_ref = bf16[24,16,128]{2,1,0:T(8,128)(2,1)S(1)} collective-permute-done((bf16[24,16,128]{2,1,0:T(8,128)(2,1)S(1)}, bf16[24,16,128]{2,1,0:T(8,128)(2,1)S(1)}, u32[]{:S(2)}, u32[]{:S(2)}) %collective-permute-start.3) | collective-permute-done | bytes 98336 | tf_op jit(solution)/shard_map/ppermute | solution.py:365
  46.1 1.2 %shard_map.58.refs_2_.sta_ref.refs_0_ = bf16[7,16,128,128]{3,2,1,0:T(8,128)(2,1)S(1)} custom-call(bf16[16,128,128]{2,1,0:T(8,128)(2,1)S(1)} %bitcast.6, bf16[16,128,128]{2,1,0:T(8,128)(2,1)S(1)} %shard_map.56.refs_1_.refs_3_, bf16[16,128,128]{2,1,0:T(8,128)(2,1)S(1)} %shard_map.55.refs_1_.refs_2_.refs_4_, ...), custom_call_target="tpu_custom_call" | custom-call | bytes 11010048 | tf_op jit(solution)/shard_map/pallas_call | solution.py:272
  47.3 2.3 %collective-permute-done.14.refs_0_ = bf16[16,128,128]{2,1,0:T(8,128)(2,1)S(1)} collective-permute-done((bf16[16,128,128]{2,1,0:T(8,128)(2,1)S(1)}, bf16[16,128,128]{2,1,0:T(8,128)(2,1)S(1)}, u32[]{:S(2)}, u32[]{:S(2)}) %collective-permute-start.14) | collective-permute-done | bytes 524320 | tf_op jit(solution)/shard_map/ppermute | solution.py:365
  50.3 1.6 %collective-permute-start.19 = (bf16[8,128,128]{2,1,0:T(8,128)(2,1)S(1)}, bf16[8,128,128]{2,1,0:T(8,128)(2,1)S(1)}, u32[]{:S(2)}, u32[]{:S(2)}) collective-permute-start(bf16[8,128,128]{2,1,0:T(8,128)(2,1)S(1)} %slice.8), channel_id=1, source_target_pairs={{0,8},{1,9},{2,10},{3,11},{4,12},{5,13},{6,14},{7,15},{8,0},{9,1},... | collective-permute-start | bytes 786440 | tf_op jit(solution)/shard_map/ppermute | solution.py:365
  52.3 4.2 %shard_map.65 = (bf16[7,16,128,128]{3,2,1,0:T(8,128)(2,1)S(1)}, f32[32,16,128]{2,1,0:T(8,128)S(1)}) custom-call(s32[16,128]{1,0:T(8,128)S(1)} %get-tuple-element.22.ids_ref, bf16[32,16,128]{2,1,0:T(8,128)(2,1)S(1)} %get-tuple-element.23.refs_1_.parts_ref, bf16[7,16,128,128]{3,2,1,0:T(8,128)(2,1)S(1)} %shard_map.58.refs_2_.sta_ref.refs_0_, ...), custom_call_target="tpu_custom_call" | custom-call | flops 234881024 | bytes 11010048 | tf_op jit(solution)/shard_map/pallas_call | solution.py:414
  56.5 2.1 %collective-permute-done.19.refs_0_ = bf16[8,128,128]{2,1,0:T(8,128)(2,1)S(1)} collective-permute-done((bf16[8,128,128]{2,1,0:T(8,128)(2,1)S(1)}, bf16[8,128,128]{2,1,0:T(8,128)(2,1)S(1)}, u32[]{:S(2)}, u32[]{:S(2)}) %collective-permute-start.19) | collective-permute-done | bytes 262176 | tf_op jit(solution)/shard_map/ppermute | solution.py:365
  58.6 1.3 %collective-permute-done.20.refs_0_ = bf16[8,128,128]{2,1,0:T(8,128)(2,1)S(1)} collective-permute-done((bf16[8,128,128]{2,1,0:T(8,128)(2,1)S(1)}, bf16[8,128,128]{2,1,0:T(8,128)(2,1)S(1)}, u32[]{:S(2)}, u32[]{:S(2)}) %collective-permute-start.20) | collective-permute-done | bytes 262176 | tf_op jit(solution)/shard_map/ppermute | solution.py:365
  60.1 1.3 %collective-permute-done.22.refs_19_ = bf16[8,128,128]{2,1,0:T(8,128)(2,1)S(1)} collective-permute-done((bf16[8,128,128]{2,1,0:T(8,128)(2,1)S(1)}, bf16[8,128,128]{2,1,0:T(8,128)(2,1)S(1)}, u32[]{:S(2)}, u32[]{:S(2)}) %collective-permute-start.22) | collective-permute-done | bytes 262176 | tf_op jit(solution)/shard_map/ppermute | solution.py:365
  61.5 10.3 %shard_map.68 = bf16[16,2,16,256]{3,2,1,0:T(8,128)(2,1)S(1)} custom-call(s32[16,128]{1,0:T(8,128)S(1)} %get-tuple-element.22.ids_ref, bf16[32,16,128]{2,1,0:T(8,128)(2,1)S(1)} %get-tuple-element.23.refs_1_.parts_ref, f32[32,16,128]{2,1,0:T(8,128)S(1)} %get-tuple-element.24.sum_ref, bf16[7,16,128,128]{3,2,1,0:T(8,128)(2,1)S(1)} %shard_map.58.refs_2_.sta_ref.refs_0_, ...), custom_call_target="tpu_custom_call" | custom-call | tf_op jit(solution)/shard_map/pallas_call | solution.py:434
  71.8 13.2 %all_to_all.5.back_ref = bf16[16,2,16,256]{3,2,1,0:T(8,128)(2,1)S(1)} all-to-all(bf16[16,2,16,256]{3,2,1,0:T(8,128)(2,1)S(1)} %shard_map.68), channel_id=1, replica_groups=mesh['dom'=2,'col'=4,'row'=4] {'col','row'}, dimensions={0} | all-to-all | bytes 524288 | tf_op jit(solution)/shard_map/all_to_all | solution.py:447
  85.0 0.9 %shard_map.69 = (f32[256,256]{1,0:T(8,128)}, f32[256,256]{1,0:T(8,128)}) custom-call(bf16[16,2,16,256]{3,2,1,0:T(8,128)(2,1)S(1)} %all_to_all.5.back_ref), custom_call_target="tpu_custom_call" | custom-call | tf_op jit(solution)/shard_map/pallas_call | solution.py:449
  (51 shorter events, 4.4 us)
Async XLA Ops:
  0.6 18.6 %collective-permute-start.5 = (bf16[16,128,128]{2,1,0:T(8,128)(2,1)}, bf16[16,128,128]{2,1,0:T(8,128)(2,1)S(1)}, u32[]{:S(2)}, u32[]{:S(2)}) collective-permute-start(bf16[16,128,128]{2,1,0:T(8,128)(2,1)} %bitcast.2), channel_id=1, source_target_pairs={{0,8},{1,9},{2,10},{3,11},{4,12},{5,13},{6,14},{7,15},{8,0},{9,1},... | collective-permute-start | bytes 1572872 | tf_op jit(solution)/shard_map/ppermute | solution.py:365
  3.7 15.6 %collective-permute-start.6 = (bf16[16,128,128]{2,1,0:T(8,128)(2,1)}, bf16[16,128,128]{2,1,0:T(8,128)(2,1)S(1)}, u32[]{:S(2)}, u32[]{:S(2)}) collective-permute-start(bf16[16,128,128]{2,1,0:T(8,128)(2,1)} %bitcast.3), channel_id=1, source_target_pairs={{0,4},{1,5},{2,6},{3,7},{4,0},{5,1},{6,2},{7,3},{8,12},{9,13},{10,... | collective-permute-start | bytes 1572872 | tf_op jit(solution)/shard_map/ppermute | solution.py:365
  3.7 15.6 %collective-permute-start.4 = (bf16[16,128,128]{2,1,0:T(8,128)(2,1)}, bf16[16,128,128]{2,1,0:T(8,128)(2,1)S(1)}, u32[]{:S(2)}, u32[]{:S(2)}) collective-permute-start(bf16[16,128,128]{2,1,0:T(8,128)(2,1)} %bitcast.4), channel_id=1, source_target_pairs={{0,1},{1,0},{2,3},{3,2},{4,5},{5,4},{6,7},{7,6},{8,9},{9,8},{10,11... | collective-permute-start | bytes 1572872 | tf_op jit(solution)/shard_map/ppermute | solution.py:365
  5.2 14.7 %collective-permute-start.11 = (bf16[16,128,128]{2,1,0:T(8,128)(2,1)}, bf16[16,128,128]{2,1,0:T(8,128)(2,1)S(1)}, u32[]{:S(2)}, u32[]{:S(2)}) collective-permute-start(bf16[16,128,128]{2,1,0:T(8,128)(2,1)} %bitcast.5), channel_id=1, source_target_pairs={{1,2},{2,1},{5,6},{6,5},{9,10},{10,9},{13,14},{14,13},{17,18},{18,... | collective-permute-start | bytes 1572872 | tf_op jit(solution)/shard_map/ppermute | solution.py:365
  7.6 1.3 %collective-permute-start = (bf16[17,16,128]{2,1,0:T(8,128)(2,1)S(1)}, bf16[17,16,128]{2,1,0:T(8,128)(2,1)S(1)}, u32[]{:S(2)}, u32[]{:S(2)}) collective-permute-start(bf16[17,16,128]{2,1,0:T(8,128)(2,1)S(1)} %get-tuple-element.15), channel_id=1, source_target_pairs={{0,4},{1,5},{2,6},{3,7},{4,0},{5,1},{6,2},{7,3},{8,12},{9,13},{10,... | collective-permute-start | bytes 208904 | tf_op jit(solution)/shard_map/ppermute | solution.py:365
  9.0 8.4 %collective-permute-start.1 = (bf16[18,16,128]{2,1,0:T(8,128)(2,1)S(1)}, bf16[18,16,128]{2,1,0:T(8,128)(2,1)S(1)}, u32[]{:S(2)}, u32[]{:S(2)}) collective-permute-start(bf16[18,16,128]{2,1,0:T(8,128)(2,1)S(1)} %get-tuple-element.17), channel_id=1, source_target_pairs={{0,8},{1,9},{2,10},{3,11},{4,12},{5,13},{6,14},{7,15},{8,0},{9,1},... | collective-permute-start | bytes 221192 | tf_op jit(solution)/shard_map/ppermute | solution.py:365
  17.4 5.6 %collective-permute-start.2 = (bf16[20,16,128]{2,1,0:T(8,128)(2,1)S(1)}, bf16[20,16,128]{2,1,0:T(8,128)(2,1)S(1)}, u32[]{:S(2)}, u32[]{:S(2)}) collective-permute-start(bf16[20,16,128]{2,1,0:T(8,128)(2,1)S(1)} %get-tuple-element.19.refs_2_), channel_id=1, source_target_pairs={{0,1},{1,0},{2,3},{3,2},{4,5},{5,4},{6,7},{7,6},{8,9},{9,8},{10,11... | collective-permute-start | bytes 245768 | tf_op jit(solution)/shard_map/ppermute | solution.py:365
  19.3 4.3 %collective-permute-start.10 = (bf16[16,128,128]{2,1,0:T(8,128)(2,1)S(1)}, bf16[16,128,128]{2,1,0:T(8,128)(2,1)S(1)}, u32[]{:S(2)}, u32[]{:S(2)}) collective-permute-start(bf16[16,128,128]{2,1,0:T(8,128)(2,1)S(1)} %shard_map.56.refs_1_.refs_3_), channel_id=1, source_target_pairs={{1,2},{2,1},{5,6},{6,5},{9,10},{10,9},{13,14},{14,13},{17,18},{18,... | collective-permute-start | bytes 1572872 | tf_op jit(solution)/shard_map/ppermute | solution.py:365
  20.0 26.1 %copy-start = (bf16[1,1,16,128,128]{4,3,2,1,0:T(8,128)(2,1)S(1)}, bf16[1,1,16,128,128]{4,3,2,1,0:T(8,128)(2,1)}, u32[]{:S(2)}) copy-start(bf16[1,1,16,128,128]{4,3,2,1,0:T(8,128)(2,1)} %param.4) | copy-start | bytes 1572868
  20.0 17.0 %collective-permute-start.12 = (bf16[16,128,128]{2,1,0:T(8,128)(2,1)S(1)}, bf16[16,128,128]{2,1,0:T(8,128)(2,1)S(1)}, u32[]{:S(2)}, u32[]{:S(2)}) collective-permute-start(bf16[16,128,128]{2,1,0:T(8,128)(2,1)S(1)} %shard_map.60.one_ref), channel_id=1, source_target_pairs={{1,0},{2,3},{5,4},{6,7},{9,8},{10,11},{13,12},{14,15},{17,16},{18,... | collective-permute-start | bytes 1572872 | tf_op jit(solution)/shard_map/ppermute | solution.py:365
  21.4 15.5 %collective-permute-start.7 = (bf16[16,128,128]{2,1,0:T(8,128)(2,1)S(1)}, bf16[16,128,128]{2,1,0:T(8,128)(2,1)S(1)}, u32[]{:S(2)}, u32[]{:S(2)}) collective-permute-start(bf16[16,128,128]{2,1,0:T(8,128)(2,1)S(1)} %shard_map.56.refs_1_.refs_3_), channel_id=1, source_target_pairs={{0,8},{1,9},{2,10},{3,11},{4,12},{5,13},{6,14},{7,15},{8,0},{9,1},... | collective-permute-start | bytes 1572872 | tf_op jit(solution)/shard_map/ppermute | solution.py:365
  23.0 14.0 %collective-permute-start.9 = (bf16[16,128,128]{2,1,0:T(8,128)(2,1)S(1)}, bf16[16,128,128]{2,1,0:T(8,128)(2,1)S(1)}, u32[]{:S(2)}, u32[]{:S(2)}) collective-permute-start(bf16[16,128,128]{2,1,0:T(8,128)(2,1)S(1)} %shard_map.55.refs_1_.refs_2_.refs_4_), channel_id=1, source_target_pairs={{0,4},{1,5},{2,6},{3,7},{4,0},{5,1},{6,2},{7,3},{8,12},{9,13},{10,... | collective-permute-start | bytes 1572872 | tf_op jit(solution)/shard_map/ppermute | solution.py:365
  23.0 14.0 %collective-permute-start.8 = (bf16[16,128,128]{2,1,0:T(8,128)(2,1)S(1)}, bf16[16,128,128]{2,1,0:T(8,128)(2,1)S(1)}, u32[]{:S(2)}, u32[]{:S(2)}) collective-permute-start(bf16[16,128,128]{2,1,0:T(8,128)(2,1)S(1)} %shard_map.56.refs_1_.refs_3_), channel_id=1, source_target_pairs={{0,4},{1,5},{2,6},{3,7},{4,0},{5,1},{6,2},{7,3},{8,12},{9,13},{10,... | collective-permute-start | bytes 1572872 | tf_op jit(solution)/shard_map/ppermute | solution.py:365
  23.6 26.0 %collective-permute-start.14 = (bf16[16,128,128]{2,1,0:T(8,128)(2,1)S(1)}, bf16[16,128,128]{2,1,0:T(8,128)(2,1)S(1)}, u32[]{:S(2)}, u32[]{:S(2)}) collective-permute-start(bf16[16,128,128]{2,1,0:T(8,128)(2,1)S(1)} %shard_map.59.one_ref), channel_id=1, source_target_pairs={{1,0},{2,3},{5,4},{6,7},{9,8},{10,11},{13,12},{14,15},{17,16},{18,... | collective-permute-start | bytes 1572872 | tf_op jit(solution)/shard_map/ppermute | solution.py:365
  37.1 12.6 %collective-permute-start.13 = (bf16[16,128,128]{2,1,0:T(8,128)(2,1)S(1)}, bf16[16,128,128]{2,1,0:T(8,128)(2,1)S(1)}, u32[]{:S(2)}, u32[]{:S(2)}) collective-permute-start(bf16[16,128,128]{2,1,0:T(8,128)(2,1)S(1)} %shard_map.62.refs_7_.refs_9_), channel_id=1, source_target_pairs={{0,8},{1,9},{2,10},{3,11},{4,12},{5,13},{6,14},{7,15},{8,0},{9,1},... | collective-permute-start | bytes 1572872 | tf_op jit(solution)/shard_map/ppermute | solution.py:365
  38.9 10.7 %collective-permute-start.15 = (bf16[16,128,128]{2,1,0:T(8,128)(2,1)S(1)}, bf16[16,128,128]{2,1,0:T(8,128)(2,1)S(1)}, u32[]{:S(2)}, u32[]{:S(2)}) collective-permute-start(bf16[16,128,128]{2,1,0:T(8,128)(2,1)S(1)} %shard_map.62.refs_7_.refs_9_), channel_id=1, source_target_pairs={{0,4},{1,5},{2,6},{3,7},{4,0},{5,1},{6,2},{7,3},{8,12},{9,13},{10,... | collective-permute-start | bytes 1572872 | tf_op jit(solution)/shard_map/ppermute | solution.py:365
  38.9 10.7 %collective-permute-start.16 = (bf16[16,128,128]{2,1,0:T(8,128)(2,1)S(1)}, bf16[16,128,128]{2,1,0:T(8,128)(2,1)S(1)}, u32[]{:S(2)}, u32[]{:S(2)}) collective-permute-start(bf16[16,128,128]{2,1,0:T(8,128)(2,1)S(1)} %shard_map.57.refs_3_.refs_0_.refs_5_), channel_id=1, source_target_pairs={{0,4},{1,5},{2,6},{3,7},{4,0},{5,1},{6,2},{7,3},{8,12},{9,13},{10,... | collective-permute-start | bytes 1572872 | tf_op jit(solution)/shard_map/ppermute | solution.py:365
  39.4 6.7 %collective-permute-start.3 = (bf16[24,16,128]{2,1,0:T(8,128)(2,1)S(1)}, bf16[24,16,128]{2,1,0:T(8,128)(2,1)S(1)}, u32[]{:S(2)}, u32[]{:S(2)}) collective-permute-start(bf16[24,16,128]{2,1,0:T(8,128)(2,1)S(1)} %get-tuple-element.21.refs_1_), channel_id=1, source_target_pairs={{0,3},{1,2},{2,1},{3,0},{4,7},{5,6},{6,5},{7,4},{8,11},{9,10},{10,... | collective-permute-start | bytes 294920 | tf_op jit(solution)/shard_map/ppermute | solution.py:365
  49.6 2.3 %collective-permute-start.18 = (bf16[16,128,128]{2,1,0:T(8,128)(2,1)S(1)}, bf16[16,128,128]{2,1,0:T(8,128)(2,1)S(1)}, u32[]{:S(2)}, u32[]{:S(2)}) collective-permute-start(bf16[16,128,128]{2,1,0:T(8,128)(2,1)S(1)} %collective-permute-done.13.refs_0_.refs_8_.refs_10_), channel_id=1, source_target_pairs={{0,4},{1,5},{2,6},{3,7},{4,0},{5,1},{6,2},{7,3},{8,12},{9,13},{10,... | collective-permute-start | bytes 1572872 | tf_op jit(solution)/shard_map/ppermute | solution.py:365
  49.7 2.6 %collective-permute-start.17 = (bf16[16,128,128]{2,1,0:T(8,128)(2,1)S(1)}, bf16[16,128,128]{2,1,0:T(8,128)(2,1)S(1)}, u32[]{:S(2)}, u32[]{:S(2)}) collective-permute-start(bf16[16,128,128]{2,1,0:T(8,128)(2,1)S(1)} %shard_map.64.refs_9_.refs_11_), channel_id=1, source_target_pairs={{0,4},{1,5},{2,6},{3,7},{4,0},{5,1},{6,2},{7,3},{8,12},{9,13},{10,... | collective-permute-start | bytes 1572872 | tf_op jit(solution)/shard_map/ppermute | solution.py:365
  50.3 8.3 %collective-permute-start.19 = (bf16[8,128,128]{2,1,0:T(8,128)(2,1)S(1)}, bf16[8,128,128]{2,1,0:T(8,128)(2,1)S(1)}, u32[]{:S(2)}, u32[]{:S(2)}) collective-permute-start(bf16[8,128,128]{2,1,0:T(8,128)(2,1)S(1)} %slice.8), channel_id=1, source_target_pairs={{0,8},{1,9},{2,10},{3,11},{4,12},{5,13},{6,14},{7,15},{8,0},{9,1},... | collective-permute-start | bytes 786440 | tf_op jit(solution)/shard_map/ppermute | solution.py:365
  51.9 8.0 %collective-permute-start.20 = (bf16[8,128,128]{2,1,0:T(8,128)(2,1)S(1)}, bf16[8,128,128]{2,1,0:T(8,128)(2,1)S(1)}, u32[]{:S(2)}, u32[]{:S(2)}) collective-permute-start(bf16[8,128,128]{2,1,0:T(8,128)(2,1)S(1)} %slice.9), channel_id=1, source_target_pairs={{0,1},{1,0},{2,3},{3,2},{4,5},{5,4},{6,7},{7,6},{8,9},{9,8},{10,11... | collective-permute-start | bytes 786440 | tf_op jit(solution)/shard_map/ppermute | solution.py:365
  58.6 1.5 %collective-permute-start.21 = (bf16[8,128,128]{2,1,0:T(8,128)(2,1)S(1)}, bf16[8,128,128]{2,1,0:T(8,128)(2,1)S(1)}, u32[]{:S(2)}, u32[]{:S(2)}) collective-permute-start(bf16[8,128,128]{2,1,0:T(8,128)(2,1)S(1)} %shard_map.66.refs_16_), channel_id=1, source_target_pairs={{0,4},{1,5},{2,6},{3,7},{4,0},{5,1},{6,2},{7,3},{8,12},{9,13},{10,... | collective-permute-start | bytes 786440 | tf_op jit(solution)/shard_map/ppermute | solution.py:365
  59.9 1.5 %collective-permute-start.22 = (bf16[8,128,128]{2,1,0:T(8,128)(2,1)S(1)}, bf16[8,128,128]{2,1,0:T(8,128)(2,1)S(1)}, u32[]{:S(2)}, u32[]{:S(2)}) collective-permute-start(bf16[8,128,128]{2,1,0:T(8,128)(2,1)S(1)} %shard_map.67.refs_17_), channel_id=1, source_target_pairs={{0,4},{1,5},{2,6},{3,7},{4,0},{5,1},{6,2},{7,3},{8,12},{9,13},{10,... | collective-permute-start | bytes 786440 | tf_op jit(solution)/shard_map/ppermute | solution.py:365
  (1 other events, 0.9 us)

commit v19 on v18

--- a/solution.py
+++ b/solution.py
@@ -10,7 +10,7 @@
 PER_ROW = 2
 DEG = 4
 SPLIT = 4
-UNROLL = 4
+UNROLL = 8
 GATHER_LIMIT = 12 * 2**20
 LANES = ("col", "row")
 INNER = (1, 2)
@@ -339,7 +339,7 @@
             out_ref[p, 1, :, b * orb : (b + 1) * orb] = prev[u].astype(out_ref.dtype)
 
 
-def result_kernel(back_ref, last_ref, before_ref):
+def result_kernel(back_ref, marker_ref, last_ref, before_ref):
     count, _, share, rows = back_ref.shape
     for i, out_ref in enumerate((last_ref, before_ref)):
         whole = jnp.concatenate([back_ref[d, i] for d in range(count)], axis=0)
@@ -449,10 +449,10 @@
     return pl.pallas_call(
         result_kernel,
         out_shape=[whole, whole],
-        in_specs=vmem(),
+        in_specs=vmem() + anywhere(),
         out_specs=vmem(2),
         compiler_params=pltpu.CompilerParams(vmem_limit_bytes=4 * 2**20),
-    )(back)
+    )(back, after(ids, done, rank=8))
 
 
 def per_device(vectors, blocks, cols):

time: 86.2 us -> 86.5 us (level)
  blocking collectives: 13.2 us -> 0 us
  waiting for transfers between devices: 34.9 us -> 45.1 us
  starting transfers between devices: 18.4 us -> 21.9 us
    all_to_all x1 -> x0, blocking collectives: 13.2 us -> none  [gather_plan(): back = lax.all_to_all(done, LANES, split_axis=0, concat_axis=0, tiled=True)]
    all_to_all x0 -> x1, waiting for transfers between devices: none -> 10 us  [gather_plan(): back = lax.all_to_all(done, LANES, split_axis=0, concat_axis=0, tiled=True)]
    all_to_all x0 -> x1, starting transfers between devices: none -> 3.55 us  [gather_plan(): back = lax.all_to_all(done, LANES, split_axis=0, concat_axis=0, tiled=True)]
  transfers between devices with their start and end apart: 23 -> 24, of which waited for: 10 -> 11; matrix products, arithmetic and copies ran while one was open for 1% -> 1% of each run, Pallas kernels for 7% -> 6%
where the time goes in v19:
time: 86.5 us; the launch traced here: 86.2 us
  waiting for transfers between devices  45.1 us (52%)
  starting transfers between devices  21.9 us (25%)
  Pallas kernels  16.7 us (19%)
  local copies, waits for them, and re-layouts  1.61 us (2%)
    ppermute x23, waiting for transfers between devices, send(): return lax.ppermute(buf, LANES, pairs)  35.1 us
    ppermute x23, starting transfers between devices, send(): return lax.ppermute(buf, LANES, pairs)  18.4 us
    pallas_call x1, Pallas kernels, gather_plan(): pl.pallas_call(functools.partial(filter_kernel, early, later, late, n_col...  10.3 us
    all_to_all x1, waiting for transfers between devices, gather_plan(): back = lax.all_to_all(done, LANES, split_axis=0, concat_axis=0, tiled=True)  10 us
    pallas_call x1, Pallas kernels, gather_plan(): pl.pallas_call(functools.partial(first_kernel, early, later, n_col, n_row...  4.05 us
    all_to_all x1, starting transfers between devices, gather_plan(): back = lax.all_to_all(done, LANES, split_axis=0, concat_axis=0, tiled=True)  3.55 us
  transfers between devices with their start and end apart: 24, of which 11 were waited for; matrix products, arithmetic and copies ran while one was open for 1% of the time, Pallas kernels for 6%

profile of v19, /device:TPU:0, one launch (start us, length us, event | category | flops | bytes accessed | tf_op | source)
XLA Modules:
  0.0 86.2 jit_solution(3467754762137699852)
XLA Ops:
  0.6 3.0 %collective-permute-start.5 = (bf16[16,128,128]{2,1,0:T(8,128)(2,1)}, bf16[16,128,128]{2,1,0:T(8,128)(2,1)S(1)}, u32[]{:S(2)}, u32[]{:S(2)}) collective-permute-start(bf16[16,128,128]{2,1,0:T(8,128)(2,1)} %bitcast.2), channel_id=1, source_target_pairs={{0,8},{1,9},{2,10},{3,11},{4,12},{5,13},{6,14},{7,15},{8,0},{9,1},... | collective-permute-start | bytes 1572872 | tf_op jit(solution)/shard_map/ppermute | solution.py:365
  3.7 1.6 %collective-permute-start.4 = (bf16[16,128,128]{2,1,0:T(8,128)(2,1)}, bf16[16,128,128]{2,1,0:T(8,128)(2,1)S(1)}, u32[]{:S(2)}, u32[]{:S(2)}) collective-permute-start(bf16[16,128,128]{2,1,0:T(8,128)(2,1)} %bitcast.4), channel_id=1, source_target_pairs={{0,1},{1,0},{2,3},{3,2},{4,5},{5,4},{6,7},{7,6},{8,9},{9,8},{10,11... | collective-permute-start | bytes 1572872 | tf_op jit(solution)/shard_map/ppermute | solution.py:365
  6.6 0.9 %copy-done.1 = bf16[256,256]{1,0:T(8,128)(2,1)S(1)} copy-done((bf16[256,256]{1,0:T(8,128)(2,1)S(1)}, bf16[256,256]{1,0:T(8,128)(2,1)}, u32[]{:S(2)}) %copy-start.1) | copy-done | bytes 131096
  7.9 1.0 %collective-permute-done.came_ref = bf16[17,16,128]{2,1,0:T(8,128)(2,1)S(1)} collective-permute-done((bf16[17,16,128]{2,1,0:T(8,128)(2,1)S(1)}, bf16[17,16,128]{2,1,0:T(8,128)(2,1)S(1)}, u32[]{:S(2)}, u32[]{:S(2)}) %collective-permute-start) | collective-permute-done | bytes 69664 | tf_op jit(solution)/shard_map/ppermute | solution.py:365
  9.5 7.8 %collective-permute-done.1.came_ref = bf16[18,16,128]{2,1,0:T(8,128)(2,1)S(1)} collective-permute-done((bf16[18,16,128]{2,1,0:T(8,128)(2,1)S(1)}, bf16[18,16,128]{2,1,0:T(8,128)(2,1)S(1)}, u32[]{:S(2)}, u32[]{:S(2)}) %collective-permute-start.1) | collective-permute-done | bytes 73760 | tf_op jit(solution)/shard_map/ppermute | solution.py:365
  17.4 1.9 %collective-permute-start.2 = (bf16[20,16,128]{2,1,0:T(8,128)(2,1)S(1)}, bf16[20,16,128]{2,1,0:T(8,128)(2,1)S(1)}, u32[]{:S(2)}, u32[]{:S(2)}) collective-permute-start(bf16[20,16,128]{2,1,0:T(8,128)(2,1)S(1)} %get-tuple-element.19.refs_2_), channel_id=1, source_target_pairs={{0,1},{1,0},{2,3},{3,2},{4,5},{5,4},{6,7},{7,6},{8,9},{9,8},{10,11... | collective-permute-start | bytes 245768 | tf_op jit(solution)/shard_map/ppermute | solution.py:365
  19.3 0.7 collective-permute-start.10
  20.0 1.4 %collective-permute-start.12 = (bf16[16,128,128]{2,1,0:T(8,128)(2,1)S(1)}, bf16[16,128,128]{2,1,0:T(8,128)(2,1)S(1)}, u32[]{:S(2)}, u32[]{:S(2)}) collective-permute-start(bf16[16,128,128]{2,1,0:T(8,128)(2,1)S(1)} %shard_map.60.one_ref), channel_id=1, source_target_pairs={{1,0},{2,3},{5,4},{6,7},{9,8},{10,11},{13,12},{14,15},{17,16},{18,... | collective-permute-start | bytes 1572872 | tf_op jit(solution)/shard_map/ppermute | solution.py:365
  21.4 1.6 %collective-permute-start.7 = (bf16[16,128,128]{2,1,0:T(8,128)(2,1)S(1)}, bf16[16,128,128]{2,1,0:T(8,128)(2,1)S(1)}, u32[]{:S(2)}, u32[]{:S(2)}) collective-permute-start(bf16[16,128,128]{2,1,0:T(8,128)(2,1)S(1)} %shard_map.56.refs_1_.refs_3_), channel_id=1, source_target_pairs={{0,8},{1,9},{2,10},{3,11},{4,12},{5,13},{6,14},{7,15},{8,0},{9,1},... | collective-permute-start | bytes 1572872 | tf_op jit(solution)/shard_map/ppermute | solution.py:365
  23.6 1.3 %collective-permute-start.14 = (bf16[16,128,128]{2,1,0:T(8,128)(2,1)S(1)}, bf16[16,128,128]{2,1,0:T(8,128)(2,1)S(1)}, u32[]{:S(2)}, u32[]{:S(2)}) collective-permute-start(bf16[16,128,128]{2,1,0:T(8,128)(2,1)S(1)} %shard_map.59.one_ref), channel_id=1, source_target_pairs={{1,0},{2,3},{5,4},{6,7},{9,8},{10,11},{13,12},{14,15},{17,16},{18,... | collective-permute-start | bytes 1572872 | tf_op jit(solution)/shard_map/ppermute | solution.py:365
  24.9 12.1 %collective-permute-done.12.refs_0_ = bf16[16,128,128]{2,1,0:T(8,128)(2,1)S(1)} collective-permute-done((bf16[16,128,128]{2,1,0:T(8,128)(2,1)S(1)}, bf16[16,128,128]{2,1,0:T(8,128)(2,1)S(1)}, u32[]{:S(2)}, u32[]{:S(2)}) %collective-permute-start.12) | collective-permute-done | bytes 524320 | tf_op jit(solution)/shard_map/ppermute | solution.py:365
  37.1 1.8 %collective-permute-start.13 = (bf16[16,128,128]{2,1,0:T(8,128)(2,1)S(1)}, bf16[16,128,128]{2,1,0:T(8,128)(2,1)S(1)}, u32[]{:S(2)}, u32[]{:S(2)}) collective-permute-start(bf16[16,128,128]{2,1,0:T(8,128)(2,1)S(1)} %shard_map.62.refs_7_.refs_9_), channel_id=1, source_target_pairs={{0,8},{1,9},{2,10},{3,11},{4,12},{5,13},{6,14},{7,15},{8,0},{9,1},... | collective-permute-start | bytes 1572872 | tf_op jit(solution)/shard_map/ppermute | solution.py:365
  39.7 6.3 %collective-permute-done.3.came_ref = bf16[24,16,128]{2,1,0:T(8,128)(2,1)S(1)} collective-permute-done((bf16[24,16,128]{2,1,0:T(8,128)(2,1)S(1)}, bf16[24,16,128]{2,1,0:T(8,128)(2,1)S(1)}, u32[]{:S(2)}, u32[]{:S(2)}) %collective-permute-start.3) | collective-permute-done | bytes 98336 | tf_op jit(solution)/shard_map/ppermute | solution.py:365
  46.1 1.2 %shard_map.58.refs_2_.sta_ref.refs_0_ = bf16[7,16,128,128]{3,2,1,0:T(8,128)(2,1)S(1)} custom-call(bf16[16,128,128]{2,1,0:T(8,128)(2,1)S(1)} %bitcast.6, bf16[16,128,128]{2,1,0:T(8,128)(2,1)S(1)} %shard_map.56.refs_1_.refs_3_, bf16[16,128,128]{2,1,0:T(8,128)(2,1)S(1)} %shard_map.55.refs_1_.refs_2_.refs_4_, ...), custom_call_target="tpu_custom_call" | custom-call | bytes 11010048 | tf_op jit(solution)/shard_map/pallas_call | solution.py:272
  47.3 2.3 %collective-permute-done.14.refs_0_ = bf16[16,128,128]{2,1,0:T(8,128)(2,1)S(1)} collective-permute-done((bf16[16,128,128]{2,1,0:T(8,128)(2,1)S(1)}, bf16[16,128,128]{2,1,0:T(8,128)(2,1)S(1)}, u32[]{:S(2)}, u32[]{:S(2)}) %collective-permute-start.14) | collective-permute-done | bytes 524320 | tf_op jit(solution)/shard_map/ppermute | solution.py:365
  50.3 1.6 %collective-permute-start.19 = (bf16[8,128,128]{2,1,0:T(8,128)(2,1)S(1)}, bf16[8,128,128]{2,1,0:T(8,128)(2,1)S(1)}, u32[]{:S(2)}, u32[]{:S(2)}) collective-permute-start(bf16[8,128,128]{2,1,0:T(8,128)(2,1)S(1)} %slice.8), channel_id=1, source_target_pairs={{0,8},{1,9},{2,10},{3,11},{4,12},{5,13},{6,14},{7,15},{8,0},{9,1},... | collective-permute-start | bytes 786440 | tf_op jit(solution)/shard_map/ppermute | solution.py:365
  52.3 4.0 %shard_map.65 = (bf16[7,16,128,128]{3,2,1,0:T(8,128)(2,1)S(1)}, f32[32,16,128]{2,1,0:T(8,128)S(1)}) custom-call(s32[16,128]{1,0:T(8,128)S(1)} %get-tuple-element.22.ids_ref.refs_0_, bf16[32,16,128]{2,1,0:T(8,128)(2,1)S(1)} %get-tuple-element.23.refs_1_.parts_ref, bf16[7,16,128,128]{3,2,1,0:T(8,128)(2,1)S(1)} %shard_map.58.refs_2_.sta_ref.refs_0_, ...), custom_call_target="tpu_custom_call" | custom-call | flops 234881024 | bytes 11010048 | tf_op jit(solution)/shard_map/pallas_call | solution.py:414
  56.3 2.2 %collective-permute-done.19.refs_0_ = bf16[8,128,128]{2,1,0:T(8,128)(2,1)S(1)} collective-permute-done((bf16[8,128,128]{2,1,0:T(8,128)(2,1)S(1)}, bf16[8,128,128]{2,1,0:T(8,128)(2,1)S(1)}, u32[]{:S(2)}, u32[]{:S(2)}) %collective-permute-start.19) | collective-permute-done | bytes 262176 | tf_op jit(solution)/shard_map/ppermute | solution.py:365
  58.6 1.3 %collective-permute-done.20.refs_0_ = bf16[8,128,128]{2,1,0:T(8,128)(2,1)S(1)} collective-permute-done((bf16[8,128,128]{2,1,0:T(8,128)(2,1)S(1)}, bf16[8,128,128]{2,1,0:T(8,128)(2,1)S(1)}, u32[]{:S(2)}, u32[]{:S(2)}) %collective-permute-start.20) | collective-permute-done | bytes 262176 | tf_op jit(solution)/shard_map/ppermute | solution.py:365
  60.1 1.3 %collective-permute-done.22.refs_19_ = bf16[8,128,128]{2,1,0:T(8,128)(2,1)S(1)} collective-permute-done((bf16[8,128,128]{2,1,0:T(8,128)(2,1)S(1)}, bf16[8,128,128]{2,1,0:T(8,128)(2,1)S(1)}, u32[]{:S(2)}, u32[]{:S(2)}) %collective-permute-start.22) | collective-permute-done | bytes 262176 | tf_op jit(solution)/shard_map/ppermute | solution.py:365
  61.5 10.3 %shard_map.68.refs_1_ = bf16[16,2,16,256]{3,2,1,0:T(8,128)(2,1)} custom-call(s32[16,128]{1,0:T(8,128)S(1)} %get-tuple-element.22.ids_ref.refs_0_, bf16[32,16,128]{2,1,0:T(8,128)(2,1)S(1)} %get-tuple-element.23.refs_1_.parts_ref, f32[32,16,128]{2,1,0:T(8,128)S(1)} %get-tuple-element.24.sum_ref, ...), custom_call_target="tpu_custom_call" | custom-call | tf_op jit(solution)/shard_map/pallas_call | solution.py:434
  71.7 3.5 %all-to-all-start = ((bf16[16,2,16,256]{3,2,1,0:T(8,128)(2,1)}), bf16[16,2,16,256]{3,2,1,0:T(8,128)(2,1)S(1)}, u32[]{:S(2)}, u32[]{:S(2)}) async-start(bf16[16,2,16,256]{3,2,1,0:T(8,128)(2,1)} %shard_map.68.refs_1_), calls=%async_computation | async-start | bytes 524288 | tf_op jit(solution)/shard_map/all_to_all | solution.py:447
  75.3 10.0 %all-to-all-done.back_ref = bf16[16,2,16,256]{3,2,1,0:T(8,128)(2,1)S(1)} async-done(((bf16[16,2,16,256]{3,2,1,0:T(8,128)(2,1)}), bf16[16,2,16,256]{3,2,1,0:T(8,128)(2,1)S(1)}, u32[]{:S(2)}, u32[]{:S(2)}) %all-to-all-start) | async-done | bytes 262176 | tf_op jit(solution)/shard_map/all_to_all | solution.py:447
  85.3 0.9 %shard_map.70 = (f32[256,256]{1,0:T(8,128)}, f32[256,256]{1,0:T(8,128)}) custom-call(bf16[16,2,16,256]{3,2,1,0:T(8,128)(2,1)S(1)} %all-to-all-done.back_ref, s32[16,128]{1,0:T(8,128)S(1)} %shard_map.69.marker_ref), custom_call_target="tpu_custom_call" | custom-call | tf_op jit(solution)/shard_map/pallas_call | solution.py:449
  (53 shorter events, 5.1 us)
Async XLA Ops:
  0.6 18.6 %collective-permute-start.5 = (bf16[16,128,128]{2,1,0:T(8,128)(2,1)}, bf16[16,128,128]{2,1,0:T(8,128)(2,1)S(1)}, u32[]{:S(2)}, u32[]{:S(2)}) collective-permute-start(bf16[16,128,128]{2,1,0:T(8,128)(2,1)} %bitcast.2), channel_id=1, source_target_pairs={{0,8},{1,9},{2,10},{3,11},{4,12},{5,13},{6,14},{7,15},{8,0},{9,1},... | collective-permute-start | bytes 1572872 | tf_op jit(solution)/shard_map/ppermute | solution.py:365
  3.7 15.6 %collective-permute-start.6 = (bf16[16,128,128]{2,1,0:T(8,128)(2,1)}, bf16[16,128,128]{2,1,0:T(8,128)(2,1)S(1)}, u32[]{:S(2)}, u32[]{:S(2)}) collective-permute-start(bf16[16,128,128]{2,1,0:T(8,128)(2,1)} %bitcast.3), channel_id=1, source_target_pairs={{0,4},{1,5},{2,6},{3,7},{4,0},{5,1},{6,2},{7,3},{8,12},{9,13},{10,... | collective-permute-start | bytes 1572872 | tf_op jit(solution)/shard_map/ppermute | solution.py:365
  3.7 15.6 %collective-permute-start.4 = (bf16[16,128,128]{2,1,0:T(8,128)(2,1)}, bf16[16,128,128]{2,1,0:T(8,128)(2,1)S(1)}, u32[]{:S(2)}, u32[]{:S(2)}) collective-permute-start(bf16[16,128,128]{2,1,0:T(8,128)(2,1)} %bitcast.4), channel_id=1, source_target_pairs={{0,1},{1,0},{2,3},{3,2},{4,5},{5,4},{6,7},{7,6},{8,9},{9,8},{10,11... | collective-permute-start | bytes 1572872 | tf_op jit(solution)/shard_map/ppermute | solution.py:365
  5.2 14.7 %collective-permute-start.11 = (bf16[16,128,128]{2,1,0:T(8,128)(2,1)}, bf16[16,128,128]{2,1,0:T(8,128)(2,1)S(1)}, u32[]{:S(2)}, u32[]{:S(2)}) collective-permute-start(bf16[16,128,128]{2,1,0:T(8,128)(2,1)} %bitcast.5), channel_id=1, source_target_pairs={{1,2},{2,1},{5,6},{6,5},{9,10},{10,9},{13,14},{14,13},{17,18},{18,... | collective-permute-start | bytes 1572872 | tf_op jit(solution)/shard_map/ppermute | solution.py:365
  7.6 1.3 %collective-permute-start = (bf16[17,16,128]{2,1,0:T(8,128)(2,1)S(1)}, bf16[17,16,128]{2,1,0:T(8,128)(2,1)S(1)}, u32[]{:S(2)}, u32[]{:S(2)}) collective-permute-start(bf16[17,16,128]{2,1,0:T(8,128)(2,1)S(1)} %get-tuple-element.15), channel_id=1, source_target_pairs={{0,4},{1,5},{2,6},{3,7},{4,0},{5,1},{6,2},{7,3},{8,12},{9,13},{10,... | collective-permute-start | bytes 208904 | tf_op jit(solution)/shard_map/ppermute | solution.py:365
  9.0 8.4 %collective-permute-start.1 = (bf16[18,16,128]{2,1,0:T(8,128)(2,1)S(1)}, bf16[18,16,128]{2,1,0:T(8,128)(2,1)S(1)}, u32[]{:S(2)}, u32[]{:S(2)}) collective-permute-start(bf16[18,16,128]{2,1,0:T(8,128)(2,1)S(1)} %get-tuple-element.17), channel_id=1, source_target_pairs={{0,8},{1,9},{2,10},{3,11},{4,12},{5,13},{6,14},{7,15},{8,0},{9,1},... | collective-permute-start | bytes 221192 | tf_op jit(solution)/shard_map/ppermute | solution.py:365
  17.4 5.6 %collective-permute-start.2 = (bf16[20,16,128]{2,1,0:T(8,128)(2,1)S(1)}, bf16[20,16,128]{2,1,0:T(8,128)(2,1)S(1)}, u32[]{:S(2)}, u32[]{:S(2)}) collective-permute-start(bf16[20,16,128]{2,1,0:T(8,128)(2,1)S(1)} %get-tuple-element.19.refs_2_), channel_id=1, source_target_pairs={{0,1},{1,0},{2,3},{3,2},{4,5},{5,4},{6,7},{7,6},{8,9},{9,8},{10,11... | collective-permute-start | bytes 245768 | tf_op jit(solution)/shard_map/ppermute | solution.py:365
  19.3 4.3 %collective-permute-start.10 = (bf16[16,128,128]{2,1,0:T(8,128)(2,1)S(1)}, bf16[16,128,128]{2,1,0:T(8,128)(2,1)S(1)}, u32[]{:S(2)}, u32[]{:S(2)}) collective-permute-start(bf16[16,128,128]{2,1,0:T(8,128)(2,1)S(1)} %shard_map.56.refs_1_.refs_3_), channel_id=1, source_target_pairs={{1,2},{2,1},{5,6},{6,5},{9,10},{10,9},{13,14},{14,13},{17,18},{18,... | collective-permute-start | bytes 1572872 | tf_op jit(solution)/shard_map/ppermute | solution.py:365
  20.0 17.0 %collective-permute-start.12 = (bf16[16,128,128]{2,1,0:T(8,128)(2,1)S(1)}, bf16[16,128,128]{2,1,0:T(8,128)(2,1)S(1)}, u32[]{:S(2)}, u32[]{:S(2)}) collective-permute-start(bf16[16,128,128]{2,1,0:T(8,128)(2,1)S(1)} %shard_map.60.one_ref), channel_id=1, source_target_pairs={{1,0},{2,3},{5,4},{6,7},{9,8},{10,11},{13,12},{14,15},{17,16},{18,... | collective-permute-start | bytes 1572872 | tf_op jit(solution)/shard_map/ppermute | solution.py:365
  21.4 15.5 %collective-permute-start.7 = (bf16[16,128,128]{2,1,0:T(8,128)(2,1)S(1)}, bf16[16,128,128]{2,1,0:T(8,128)(2,1)S(1)}, u32[]{:S(2)}, u32[]{:S(2)}) collective-permute-start(bf16[16,128,128]{2,1,0:T(8,128)(2,1)S(1)} %shard_map.56.refs_1_.refs_3_), channel_id=1, source_target_pairs={{0,8},{1,9},{2,10},{3,11},{4,12},{5,13},{6,14},{7,15},{8,0},{9,1},... | collective-permute-start | bytes 1572872 | tf_op jit(solution)/shard_map/ppermute | solution.py:365
  23.0 14.0 %collective-permute-start.9 = (bf16[16,128,128]{2,1,0:T(8,128)(2,1)S(1)}, bf16[16,128,128]{2,1,0:T(8,128)(2,1)S(1)}, u32[]{:S(2)}, u32[]{:S(2)}) collective-permute-start(bf16[16,128,128]{2,1,0:T(8,128)(2,1)S(1)} %shard_map.55.refs_1_.refs_2_.refs_4_), channel_id=1, source_target_pairs={{0,4},{1,5},{2,6},{3,7},{4,0},{5,1},{6,2},{7,3},{8,12},{9,13},{10,... | collective-permute-start | bytes 1572872 | tf_op jit(solution)/shard_map/ppermute | solution.py:365
  23.0 14.0 %collective-permute-start.8 = (bf16[16,128,128]{2,1,0:T(8,128)(2,1)S(1)}, bf16[16,128,128]{2,1,0:T(8,128)(2,1)S(1)}, u32[]{:S(2)}, u32[]{:S(2)}) collective-permute-start(bf16[16,128,128]{2,1,0:T(8,128)(2,1)S(1)} %shard_map.56.refs_1_.refs_3_), channel_id=1, source_target_pairs={{0,4},{1,5},{2,6},{3,7},{4,0},{5,1},{6,2},{7,3},{8,12},{9,13},{10,... | collective-permute-start | bytes 1572872 | tf_op jit(solution)/shard_map/ppermute | solution.py:365
  23.6 26.0 %collective-permute-start.14 = (bf16[16,128,128]{2,1,0:T(8,128)(2,1)S(1)}, bf16[16,128,128]{2,1,0:T(8,128)(2,1)S(1)}, u32[]{:S(2)}, u32[]{:S(2)}) collective-permute-start(bf16[16,128,128]{2,1,0:T(8,128)(2,1)S(1)} %shard_map.59.one_ref), channel_id=1, source_target_pairs={{1,0},{2,3},{5,4},{6,7},{9,8},{10,11},{13,12},{14,15},{17,16},{18,... | collective-permute-start | bytes 1572872 | tf_op jit(solution)/shard_map/ppermute | solution.py:365
  37.1 12.6 %collective-permute-start.13 = (bf16[16,128,128]{2,1,0:T(8,128)(2,1)S(1)}, bf16[16,128,128]{2,1,0:T(8,128)(2,1)S(1)}, u32[]{:S(2)}, u32[]{:S(2)}) collective-permute-start(bf16[16,128,128]{2,1,0:T(8,128)(2,1)S(1)} %shard_map.62.refs_7_.refs_9_), channel_id=1, source_target_pairs={{0,8},{1,9},{2,10},{3,11},{4,12},{5,13},{6,14},{7,15},{8,0},{9,1},... | collective-permute-start | bytes 1572872 | tf_op jit(solution)/shard_map/ppermute | solution.py:365
  38.9 10.7 %collective-permute-start.15 = (bf16[16,128,128]{2,1,0:T(8,128)(2,1)S(1)}, bf16[16,128,128]{2,1,0:T(8,128)(2,1)S(1)}, u32[]{:S(2)}, u32[]{:S(2)}) collective-permute-start(bf16[16,128,128]{2,1,0:T(8,128)(2,1)S(1)} %shard_map.62.refs_7_.refs_9_), channel_id=1, source_target_pairs={{0,4},{1,5},{2,6},{3,7},{4,0},{5,1},{6,2},{7,3},{8,12},{9,13},{10,... | collective-permute-start | bytes 1572872 | tf_op jit(solution)/shard_map/ppermute | solution.py:365
  38.9 10.7 %collective-permute-start.16 = (bf16[16,128,128]{2,1,0:T(8,128)(2,1)S(1)}, bf16[16,128,128]{2,1,0:T(8,128)(2,1)S(1)}, u32[]{:S(2)}, u32[]{:S(2)}) collective-permute-start(bf16[16,128,128]{2,1,0:T(8,128)(2,1)S(1)} %shard_map.57.refs_3_.refs_0_.refs_5_), channel_id=1, source_target_pairs={{0,4},{1,5},{2,6},{3,7},{4,0},{5,1},{6,2},{7,3},{8,12},{9,13},{10,... | collective-permute-start | bytes 1572872 | tf_op jit(solution)/shard_map/ppermute | solution.py:365
  39.4 6.7 %collective-permute-start.3 = (bf16[24,16,128]{2,1,0:T(8,128)(2,1)S(1)}, bf16[24,16,128]{2,1,0:T(8,128)(2,1)S(1)}, u32[]{:S(2)}, u32[]{:S(2)}) collective-permute-start(bf16[24,16,128]{2,1,0:T(8,128)(2,1)S(1)} %get-tuple-element.21.refs_1_), channel_id=1, source_target_pairs={{0,3},{1,2},{2,1},{3,0},{4,7},{5,6},{6,5},{7,4},{8,11},{9,10},{10,... | collective-permute-start | bytes 294920 | tf_op jit(solution)/shard_map/ppermute | solution.py:365
  49.6 2.3 %collective-permute-start.18 = (bf16[16,128,128]{2,1,0:T(8,128)(2,1)S(1)}, bf16[16,128,128]{2,1,0:T(8,128)(2,1)S(1)}, u32[]{:S(2)}, u32[]{:S(2)}) collective-permute-start(bf16[16,128,128]{2,1,0:T(8,128)(2,1)S(1)} %collective-permute-done.13.refs_0_.refs_8_.refs_10_), channel_id=1, source_target_pairs={{0,4},{1,5},{2,6},{3,7},{4,0},{5,1},{6,2},{7,3},{8,12},{9,13},{10,... | collective-permute-start | bytes 1572872 | tf_op jit(solution)/shard_map/ppermute | solution.py:365
  49.7 2.6 %collective-permute-start.17 = (bf16[16,128,128]{2,1,0:T(8,128)(2,1)S(1)}, bf16[16,128,128]{2,1,0:T(8,128)(2,1)S(1)}, u32[]{:S(2)}, u32[]{:S(2)}) collective-permute-start(bf16[16,128,128]{2,1,0:T(8,128)(2,1)S(1)} %shard_map.64.refs_9_.refs_11_), channel_id=1, source_target_pairs={{0,4},{1,5},{2,6},{3,7},{4,0},{5,1},{6,2},{7,3},{8,12},{9,13},{10,... | collective-permute-start | bytes 1572872 | tf_op jit(solution)/shard_map/ppermute | solution.py:365
  50.3 8.3 %collective-permute-start.19 = (bf16[8,128,128]{2,1,0:T(8,128)(2,1)S(1)}, bf16[8,128,128]{2,1,0:T(8,128)(2,1)S(1)}, u32[]{:S(2)}, u32[]{:S(2)}) collective-permute-start(bf16[8,128,128]{2,1,0:T(8,128)(2,1)S(1)} %slice.8), channel_id=1, source_target_pairs={{0,8},{1,9},{2,10},{3,11},{4,12},{5,13},{6,14},{7,15},{8,0},{9,1},... | collective-permute-start | bytes 786440 | tf_op jit(solution)/shard_map/ppermute | solution.py:365
  51.9 8.0 %collective-permute-start.20 = (bf16[8,128,128]{2,1,0:T(8,128)(2,1)S(1)}, bf16[8,128,128]{2,1,0:T(8,128)(2,1)S(1)}, u32[]{:S(2)}, u32[]{:S(2)}) collective-permute-start(bf16[8,128,128]{2,1,0:T(8,128)(2,1)S(1)} %slice.9), channel_id=1, source_target_pairs={{0,1},{1,0},{2,3},{3,2},{4,5},{5,4},{6,7},{7,6},{8,9},{9,8},{10,11... | collective-permute-start | bytes 786440 | tf_op jit(solution)/shard_map/ppermute | solution.py:365
  58.6 1.5 %collective-permute-start.21 = (bf16[8,128,128]{2,1,0:T(8,128)(2,1)S(1)}, bf16[8,128,128]{2,1,0:T(8,128)(2,1)S(1)}, u32[]{:S(2)}, u32[]{:S(2)}) collective-permute-start(bf16[8,128,128]{2,1,0:T(8,128)(2,1)S(1)} %shard_map.66.refs_16_), channel_id=1, source_target_pairs={{0,4},{1,5},{2,6},{3,7},{4,0},{5,1},{6,2},{7,3},{8,12},{9,13},{10,... | collective-permute-start | bytes 786440 | tf_op jit(solution)/shard_map/ppermute | solution.py:365
  59.9 1.5 %collective-permute-start.22 = (bf16[8,128,128]{2,1,0:T(8,128)(2,1)S(1)}, bf16[8,128,128]{2,1,0:T(8,128)(2,1)S(1)}, u32[]{:S(2)}, u32[]{:S(2)}) collective-permute-start(bf16[8,128,128]{2,1,0:T(8,128)(2,1)S(1)} %shard_map.67.refs_17_), channel_id=1, source_target_pairs={{0,4},{1,5},{2,6},{3,7},{4,0},{5,1},{6,2},{7,3},{8,12},{9,13},{10,... | collective-permute-start | bytes 786440 | tf_op jit(solution)/shard_map/ppermute | solution.py:365
  71.7 13.6 %all-to-all-start = ((bf16[16,2,16,256]{3,2,1,0:T(8,128)(2,1)}), bf16[16,2,16,256]{3,2,1,0:T(8,128)(2,1)S(1)}, u32[]{:S(2)}, u32[]{:S(2)}) async-start(bf16[16,2,16,256]{3,2,1,0:T(8,128)(2,1)} %shard_map.68.refs_1_), calls=%async_computation | async-start | bytes 524288 | tf_op jit(solution)/shard_map/all_to_all | solution.py:447
  (2 other events, 27.0 us)

commit v20 on v19

--- a/solution.py
+++ b/solution.py
@@ -386,14 +386,14 @@
 
     stay, go = regroup(stay, send(go, 2, 0), 2, per_piece)
     mates = to_mate(own)
-    near = after(near, over_own, go, *mates)
-    over_near = after(send(near, 2, 0), rank=3)
+    near = after(near, over_own, go, inner, *mates)
+    over_near = after(send(near, 2, 0), rank=8)
     crossed = after(send(near, 0, 3, INNER), rank=1)
     inner = after(inner, near)
-    outward = after(send(inner, 0, 1, INNER), rank=1)
-    stay, go = regroup(stay, send(go, 0, 1), 4, per_piece)
+    outward = after(send(inner, 0, 1, INNER), rank=8)
+    stay, go = regroup(stay, send(after(go, near), 0, 1), 4, per_piece)
     mates += to_mate(near, over_own)
-    two = pick(INNER, crossed, outward, over_near, go, *mates)
+    two = pick(INNER, crossed, outward, over_near, *mates)
 
     over_two = send(two, 2, 0)
     outer = after(send(crossed, 0, 1, INNER), rank=1)
@@ -401,7 +401,7 @@
     mine, ids = regroup(stay, send(go, 0, 3), 8, per_piece)
     sa = [own, near, over_own, over_near, *mates[:3]]
     sta = turned_tiles(*sa)
-    three = pick(INNER, inner, outer, over_two, mine, sta, *mates[3:])
+    three = pick(INNER, inner, outer, over_two, mine, *mates[3:])
 
     over_three = send(three[:half], 2, 0)
     side_three = send(over_two[half:], 0, 1)

time: 86.5 us -> 94.8 us (1.096)
  waiting for transfers between devices: 45.1 us -> 52.1 us
  starting transfers between devices: 21.9 us -> 23.1 us
    ppermute x23, waiting for transfers between devices: 35.1 us -> 42.1 us  [send(): return lax.ppermute(buf, LANES, pairs)]
  transfers between devices with their start and end apart: 24 -> 24, of which waited for: 11 -> 12; matrix products, arithmetic and copies ran while one was open for 1% -> 1% of each run, Pallas kernels for 6% -> 6%
where the time goes in v20:
time: 94.8 us; the launch traced here: 94.5 us
  waiting for transfers between devices  52.1 us (55%)
  starting transfers between devices  23.1 us (24%)
  Pallas kernels  16.8 us (18%)
  local copies, waits for them, and re-layouts  1.61 us (2%)
    ppermute x23, waiting for transfers between devices, send(): return lax.ppermute(buf, LANES, pairs)  42.1 us
    ppermute x23, starting transfers between devices, send(): return lax.ppermute(buf, LANES, pairs)  19.2 us
    pallas_call x1, Pallas kernels, gather_plan(): pl.pallas_call(functools.partial(filter_kernel, early, later, late, n_col...  10.3 us
    all_to_all x1, waiting for transfers between devices, gather_plan(): back = lax.all_to_all(done, LANES, split_axis=0, concat_axis=0, tiled=True)  10.1 us
    pallas_call x1, Pallas kernels, gather_plan(): pl.pallas_call(functools.partial(first_kernel, early, later, n_col, n_row...  4.07 us
    all_to_all x1, starting transfers between devices, gather_plan(): back = lax.all_to_all(done, LANES, split_axis=0, concat_axis=0, tiled=True)  3.91 us
  transfers between devices with their start and end apart: 24, of which 12 were waited for; matrix products, arithmetic and copies ran while one was open for 1% of the time, Pallas kernels for 6%

profile of v20, /device:TPU:0, one launch (start us, length us, event | category | flops | bytes accessed | tf_op | source)
XLA Modules:
  0.0 94.5 jit_solution(951698844168236452)
XLA Ops:
  0.6 3.0 %collective-permute-start.3 = (bf16[16,128,128]{2,1,0:T(8,128)(2,1)}, bf16[16,128,128]{2,1,0:T(8,128)(2,1)S(1)}, u32[]{:S(2)}, u32[]{:S(2)}) collective-permute-start(bf16[16,128,128]{2,1,0:T(8,128)(2,1)} %bitcast.2), channel_id=1, source_target_pairs={{0,8},{1,9},{2,10},{3,11},{4,12},{5,13},{6,14},{7,15},{8,0},{9,1},... | collective-permute-start | bytes 1572872 | tf_op jit(solution)/shard_map/ppermute | solution.py:365
  3.7 0.7 collective-permute-start.4
  4.4 4.4 %collective-permute-start.2 = (bf16[16,128,128]{2,1,0:T(8,128)(2,1)}, bf16[16,128,128]{2,1,0:T(8,128)(2,1)S(1)}, u32[]{:S(2)}, u32[]{:S(2)}) collective-permute-start(bf16[16,128,128]{2,1,0:T(8,128)(2,1)} %bitcast.5), channel_id=1, source_target_pairs={{0,1},{1,0},{2,3},{3,2},{4,5},{5,4},{6,7},{7,6},{8,9},{9,8},{10,11... | collective-permute-start | bytes 1572872 | tf_op jit(solution)/shard_map/ppermute | solution.py:365
  8.8 0.7 pad.4
  9.5 0.9 copy-done.1
  10.6 1.2 %collective-permute-done.came_ref = bf16[17,16,128]{2,1,0:T(8,128)(2,1)S(1)} collective-permute-done((bf16[17,16,128]{2,1,0:T(8,128)(2,1)S(1)}, bf16[17,16,128]{2,1,0:T(8,128)(2,1)S(1)}, u32[]{:S(2)}, u32[]{:S(2)}) %collective-permute-start) | collective-permute-done | bytes 69664 | tf_op jit(solution)/shard_map/ppermute | solution.py:365
  12.4 5.0 %collective-permute-done.1.came_ref = bf16[18,16,128]{2,1,0:T(8,128)(2,1)S(1)} collective-permute-done((bf16[18,16,128]{2,1,0:T(8,128)(2,1)S(1)}, bf16[18,16,128]{2,1,0:T(8,128)(2,1)S(1)}, u32[]{:S(2)}, u32[]{:S(2)}) %collective-permute-start.1) | collective-permute-done | bytes 73760 | tf_op jit(solution)/shard_map/ppermute | solution.py:365
  17.4 3.9 %collective-permute-done.2.refs_0_ = bf16[16,128,128]{2,1,0:T(8,128)(2,1)S(1)} collective-permute-done((bf16[16,128,128]{2,1,0:T(8,128)(2,1)}, bf16[16,128,128]{2,1,0:T(8,128)(2,1)S(1)}, u32[]{:S(2)}, u32[]{:S(2)}) %collective-permute-start.2) | collective-permute-done | bytes 524320 | tf_op jit(solution)/shard_map/ppermute | solution.py:365
  21.3 0.7 collective-permute-start.11
  22.0 1.3 %collective-permute-start.12 = (bf16[16,128,128]{2,1,0:T(8,128)(2,1)S(1)}, bf16[16,128,128]{2,1,0:T(8,128)(2,1)S(1)}, u32[]{:S(2)}, u32[]{:S(2)}) collective-permute-start(bf16[16,128,128]{2,1,0:T(8,128)(2,1)S(1)} %shard_map.61.one_ref), channel_id=1, source_target_pairs={{1,0},{2,3},{5,4},{6,7},{9,8},{10,11},{13,12},{14,15},{17,16},{18,... | collective-permute-start | bytes 1572872 | tf_op jit(solution)/shard_map/ppermute | solution.py:365
  24.4 1.3 %collective-permute-start.14 = (bf16[16,128,128]{2,1,0:T(8,128)(2,1)S(1)}, bf16[16,128,128]{2,1,0:T(8,128)(2,1)S(1)}, u32[]{:S(2)}, u32[]{:S(2)}) collective-permute-start(bf16[16,128,128]{2,1,0:T(8,128)(2,1)S(1)} %shard_map.60.one_ref), channel_id=1, source_target_pairs={{1,0},{2,3},{5,4},{6,7},{9,8},{10,11},{13,12},{14,15},{17,16},{18,... | collective-permute-start | bytes 1572872 | tf_op jit(solution)/shard_map/ppermute | solution.py:365
  25.7 12.3 %collective-permute-done.12.refs_0_ = bf16[16,128,128]{2,1,0:T(8,128)(2,1)S(1)} collective-permute-done((bf16[16,128,128]{2,1,0:T(8,128)(2,1)S(1)}, bf16[16,128,128]{2,1,0:T(8,128)(2,1)S(1)}, u32[]{:S(2)}, u32[]{:S(2)}) %collective-permute-start.12) | collective-permute-done | bytes 524320 | tf_op jit(solution)/shard_map/ppermute | solution.py:365
  39.2 1.8 %collective-permute-start.6 = (bf16[20,16,128]{2,1,0:T(8,128)(2,1)S(1)}, bf16[20,16,128]{2,1,0:T(8,128)(2,1)S(1)}, u32[]{:S(2)}, u32[]{:S(2)}) collective-permute-start(bf16[20,16,128]{2,1,0:T(8,128)(2,1)S(1)} %shard_map.55), channel_id=1, source_target_pairs={{0,1},{1,0},{2,3},{3,2},{4,5},{5,4},{6,7},{7,6},{8,9},{9,8},{10,11... | collective-permute-start | bytes 245768 | tf_op jit(solution)/shard_map/ppermute | solution.py:365
  41.0 10.8 %collective-permute-done.6.came_ref = bf16[20,16,128]{2,1,0:T(8,128)(2,1)S(1)} collective-permute-done((bf16[20,16,128]{2,1,0:T(8,128)(2,1)S(1)}, bf16[20,16,128]{2,1,0:T(8,128)(2,1)S(1)}, u32[]{:S(2)}, u32[]{:S(2)}) %collective-permute-start.6) | collective-permute-done | bytes 81952 | tf_op jit(solution)/shard_map/ppermute | solution.py:365
  51.8 1.7 %collective-permute-start.7 = (bf16[24,16,128]{2,1,0:T(8,128)(2,1)S(1)}, bf16[24,16,128]{2,1,0:T(8,128)(2,1)S(1)}, u32[]{:S(2)}, u32[]{:S(2)}) collective-permute-start(bf16[24,16,128]{2,1,0:T(8,128)(2,1)S(1)} %get-tuple-element.21), channel_id=1, source_target_pairs={{0,3},{1,2},{2,1},{3,0},{4,7},{5,6},{6,5},{7,4},{8,11},{9,10},{10,... | collective-permute-start | bytes 294920 | tf_op jit(solution)/shard_map/ppermute | solution.py:365
  53.5 4.8 %collective-permute-done.7.came_ref = bf16[24,16,128]{2,1,0:T(8,128)(2,1)S(1)} collective-permute-done((bf16[24,16,128]{2,1,0:T(8,128)(2,1)S(1)}, bf16[24,16,128]{2,1,0:T(8,128)(2,1)S(1)}, u32[]{:S(2)}, u32[]{:S(2)}) %collective-permute-start.7) | collective-permute-done | bytes 98336 | tf_op jit(solution)/shard_map/ppermute | solution.py:365
  59.7 1.2 %shard_map.59.sta_ref.refs_0_ = bf16[7,16,128,128]{3,2,1,0:T(8,128)(2,1)S(1)} custom-call(bf16[16,128,128]{2,1,0:T(8,128)(2,1)S(1)} %bitcast.6, bf16[16,128,128]{2,1,0:T(8,128)(2,1)S(1)} %shard_map.54.refs_1_.refs_3_, bf16[16,128,128]{2,1,0:T(8,128)(2,1)S(1)} %shard_map.53.refs_1_.refs_2_.refs_4_, ...), custom_call_target="tpu_custom_call" | custom-call | bytes 11010048 | tf_op jit(solution)/shard_map/pallas_call | solution.py:272
  61.1 4.1 %shard_map.66 = (bf16[7,16,128,128]{3,2,1,0:T(8,128)(2,1)S(1)}, f32[32,16,128]{2,1,0:T(8,128)S(1)}) custom-call(s32[16,128]{1,0:T(8,128)S(1)} %get-tuple-element.22.ids_ref.refs_0_, bf16[32,16,128]{2,1,0:T(8,128)(2,1)S(1)} %get-tuple-element.23.refs_1_.parts_ref, bf16[7,16,128,128]{3,2,1,0:T(8,128)(2,1)S(1)} %shard_map.59.sta_ref.refs_0_, ...), custom_call_target="tpu_custom_call" | custom-call | flops 234881024 | bytes 11010048 | tf_op jit(solution)/shard_map/pallas_call | solution.py:414
  65.1 2.2 %collective-permute-done.19.refs_0_ = bf16[8,128,128]{2,1,0:T(8,128)(2,1)S(1)} collective-permute-done((bf16[8,128,128]{2,1,0:T(8,128)(2,1)S(1)}, bf16[8,128,128]{2,1,0:T(8,128)(2,1)S(1)}, u32[]{:S(2)}, u32[]{:S(2)}) %collective-permute-start.19) | collective-permute-done | bytes 262176 | tf_op jit(solution)/shard_map/ppermute | solution.py:365
  67.9 1.0 %collective-permute-done.21.refs_18_ = bf16[8,128,128]{2,1,0:T(8,128)(2,1)S(1)} collective-permute-done((bf16[8,128,128]{2,1,0:T(8,128)(2,1)S(1)}, bf16[8,128,128]{2,1,0:T(8,128)(2,1)S(1)}, u32[]{:S(2)}, u32[]{:S(2)}) %collective-permute-start.21) | collective-permute-done | bytes 262176 | tf_op jit(solution)/shard_map/ppermute | solution.py:365
  69.3 10.3 %shard_map.69.refs_1_ = bf16[16,2,16,256]{3,2,1,0:T(8,128)(2,1)} custom-call(s32[16,128]{1,0:T(8,128)S(1)} %get-tuple-element.22.ids_ref.refs_0_, bf16[32,16,128]{2,1,0:T(8,128)(2,1)S(1)} %get-tuple-element.23.refs_1_.parts_ref, f32[32,16,128]{2,1,0:T(8,128)S(1)} %get-tuple-element.24.sum_ref, bf16[7,16,128,128]{3,2,1,0:T(8,128)(2,1)S(1)} %shard_map.59.sta_ref.refs_0_, ...), custom_call_target="tpu_custom_call" | custom-call | tf_op jit(solution)/shard_map/pallas_call | solution.py:434
  79.6 3.9 %all-to-all-start = ((bf16[16,2,16,256]{3,2,1,0:T(8,128)(2,1)}), bf16[16,2,16,256]{3,2,1,0:T(8,128)(2,1)S(1)}, u32[]{:S(2)}, u32[]{:S(2)}) async-start(bf16[16,2,16,256]{3,2,1,0:T(8,128)(2,1)} %shard_map.69.refs_1_), calls=%async_computation | async-start | bytes 524288 | tf_op jit(solution)/shard_map/all_to_all | solution.py:447
  83.5 10.1 %all-to-all-done.back_ref = bf16[16,2,16,256]{3,2,1,0:T(8,128)(2,1)S(1)} async-done(((bf16[16,2,16,256]{3,2,1,0:T(8,128)(2,1)}), bf16[16,2,16,256]{3,2,1,0:T(8,128)(2,1)S(1)}, u32[]{:S(2)}, u32[]{:S(2)}) %all-to-all-start) | async-done | bytes 262176 | tf_op jit(solution)/shard_map/all_to_all | solution.py:447
  93.6 0.9 shard_map.71
  (54 shorter events, 5.5 us)
Async XLA Ops:
  0.6 16.8 %collective-permute-start.3 = (bf16[16,128,128]{2,1,0:T(8,128)(2,1)}, bf16[16,128,128]{2,1,0:T(8,128)(2,1)S(1)}, u32[]{:S(2)}, u32[]{:S(2)}) collective-permute-start(bf16[16,128,128]{2,1,0:T(8,128)(2,1)} %bitcast.2), channel_id=1, source_target_pairs={{0,8},{1,9},{2,10},{3,11},{4,12},{5,13},{6,14},{7,15},{8,0},{9,1},... | collective-permute-start | bytes 1572872 | tf_op jit(solution)/shard_map/ppermute | solution.py:365
  3.7 13.8 %collective-permute-start.5 = (bf16[16,128,128]{2,1,0:T(8,128)(2,1)}, bf16[16,128,128]{2,1,0:T(8,128)(2,1)S(1)}, u32[]{:S(2)}, u32[]{:S(2)}) collective-permute-start(bf16[16,128,128]{2,1,0:T(8,128)(2,1)} %bitcast.3), channel_id=1, source_target_pairs={{0,4},{1,5},{2,6},{3,7},{4,0},{5,1},{6,2},{7,3},{8,12},{9,13},{10,... | collective-permute-start | bytes 1572872 | tf_op jit(solution)/shard_map/ppermute | solution.py:365
  3.7 13.8 %collective-permute-start.4 = (bf16[16,128,128]{2,1,0:T(8,128)(2,1)}, bf16[16,128,128]{2,1,0:T(8,128)(2,1)S(1)}, u32[]{:S(2)}, u32[]{:S(2)}) collective-permute-start(bf16[16,128,128]{2,1,0:T(8,128)(2,1)} %bitcast.4), channel_id=1, source_target_pairs={{1,2},{2,1},{5,6},{6,5},{9,10},{10,9},{13,14},{14,13},{17,18},{18,... | collective-permute-start | bytes 1572872 | tf_op jit(solution)/shard_map/ppermute | solution.py:365
  4.4 17.0 %collective-permute-start.2 = (bf16[16,128,128]{2,1,0:T(8,128)(2,1)}, bf16[16,128,128]{2,1,0:T(8,128)(2,1)S(1)}, u32[]{:S(2)}, u32[]{:S(2)}) collective-permute-start(bf16[16,128,128]{2,1,0:T(8,128)(2,1)} %bitcast.5), channel_id=1, source_target_pairs={{0,1},{1,0},{2,3},{3,2},{4,5},{5,4},{6,7},{7,6},{8,9},{9,8},{10,11... | collective-permute-start | bytes 1572872 | tf_op jit(solution)/shard_map/ppermute | solution.py:365
  10.5 1.3 %collective-permute-start = (bf16[17,16,128]{2,1,0:T(8,128)(2,1)S(1)}, bf16[17,16,128]{2,1,0:T(8,128)(2,1)S(1)}, u32[]{:S(2)}, u32[]{:S(2)}) collective-permute-start(bf16[17,16,128]{2,1,0:T(8,128)(2,1)S(1)} %get-tuple-element.15), channel_id=1, source_target_pairs={{0,4},{1,5},{2,6},{3,7},{4,0},{5,1},{6,2},{7,3},{8,12},{9,13},{10,... | collective-permute-start | bytes 208904 | tf_op jit(solution)/shard_map/ppermute | solution.py:365
  11.8 5.6 %collective-permute-start.1 = (bf16[18,16,128]{2,1,0:T(8,128)(2,1)S(1)}, bf16[18,16,128]{2,1,0:T(8,128)(2,1)S(1)}, u32[]{:S(2)}, u32[]{:S(2)}) collective-permute-start(bf16[18,16,128]{2,1,0:T(8,128)(2,1)S(1)} %get-tuple-element.17), channel_id=1, source_target_pairs={{0,8},{1,9},{2,10},{3,11},{4,12},{5,13},{6,14},{7,15},{8,0},{9,1},... | collective-permute-start | bytes 221192 | tf_op jit(solution)/shard_map/ppermute | solution.py:365
  21.3 3.1 %collective-permute-start.11 = (bf16[16,128,128]{2,1,0:T(8,128)(2,1)S(1)}, bf16[16,128,128]{2,1,0:T(8,128)(2,1)S(1)}, u32[]{:S(2)}, u32[]{:S(2)}) collective-permute-start(bf16[16,128,128]{2,1,0:T(8,128)(2,1)S(1)} %shard_map.54.refs_1_.refs_3_), channel_id=1, source_target_pairs={{1,2},{2,1},{5,6},{6,5},{9,10},{10,9},{13,14},{14,13},{17,18},{18,... | collective-permute-start | bytes 1572872 | tf_op jit(solution)/shard_map/ppermute | solution.py:365
  22.0 16.0 %collective-permute-start.12 = (bf16[16,128,128]{2,1,0:T(8,128)(2,1)S(1)}, bf16[16,128,128]{2,1,0:T(8,128)(2,1)S(1)}, u32[]{:S(2)}, u32[]{:S(2)}) collective-permute-start(bf16[16,128,128]{2,1,0:T(8,128)(2,1)S(1)} %shard_map.61.one_ref), channel_id=1, source_target_pairs={{1,0},{2,3},{5,4},{6,7},{9,8},{10,11},{13,12},{14,15},{17,16},{18,... | collective-permute-start | bytes 1572872 | tf_op jit(solution)/shard_map/ppermute | solution.py:365
  23.3 14.7 %collective-permute-start.8 = (bf16[16,128,128]{2,1,0:T(8,128)(2,1)S(1)}, bf16[16,128,128]{2,1,0:T(8,128)(2,1)S(1)}, u32[]{:S(2)}, u32[]{:S(2)}) collective-permute-start(bf16[16,128,128]{2,1,0:T(8,128)(2,1)S(1)} %shard_map.54.refs_1_.refs_3_), channel_id=1, source_target_pairs={{0,8},{1,9},{2,10},{3,11},{4,12},{5,13},{6,14},{7,15},{8,0},{9,1},... | collective-permute-start | bytes 1572872 | tf_op jit(solution)/shard_map/ppermute | solution.py:365
  23.9 14.1 %collective-permute-start.10 = (bf16[16,128,128]{2,1,0:T(8,128)(2,1)S(1)}, bf16[16,128,128]{2,1,0:T(8,128)(2,1)S(1)}, u32[]{:S(2)}, u32[]{:S(2)}) collective-permute-start(bf16[16,128,128]{2,1,0:T(8,128)(2,1)S(1)} %shard_map.53.refs_1_.refs_2_.refs_4_), channel_id=1, source_target_pairs={{0,4},{1,5},{2,6},{3,7},{4,0},{5,1},{6,2},{7,3},{8,12},{9,13},{10,... | collective-permute-start | bytes 1572872 | tf_op jit(solution)/shard_map/ppermute | solution.py:365
  23.9 14.1 %collective-permute-start.9 = (bf16[16,128,128]{2,1,0:T(8,128)(2,1)S(1)}, bf16[16,128,128]{2,1,0:T(8,128)(2,1)S(1)}, u32[]{:S(2)}, u32[]{:S(2)}) collective-permute-start(bf16[16,128,128]{2,1,0:T(8,128)(2,1)S(1)} %shard_map.54.refs_1_.refs_3_), channel_id=1, source_target_pairs={{0,4},{1,5},{2,6},{3,7},{4,0},{5,1},{6,2},{7,3},{8,12},{9,13},{10,... | collective-permute-start | bytes 1572872 | tf_op jit(solution)/shard_map/ppermute | solution.py:365
  24.4 33.9 %collective-permute-start.14 = (bf16[16,128,128]{2,1,0:T(8,128)(2,1)S(1)}, bf16[16,128,128]{2,1,0:T(8,128)(2,1)S(1)}, u32[]{:S(2)}, u32[]{:S(2)}) collective-permute-start(bf16[16,128,128]{2,1,0:T(8,128)(2,1)S(1)} %shard_map.60.one_ref), channel_id=1, source_target_pairs={{1,0},{2,3},{5,4},{6,7},{9,8},{10,11},{13,12},{14,15},{17,16},{18,... | collective-permute-start | bytes 1572872 | tf_op jit(solution)/shard_map/ppermute | solution.py:365
  38.1 20.2 %collective-permute-start.13 = (bf16[16,128,128]{2,1,0:T(8,128)(2,1)S(1)}, bf16[16,128,128]{2,1,0:T(8,128)(2,1)S(1)}, u32[]{:S(2)}, u32[]{:S(2)}) collective-permute-start(bf16[16,128,128]{2,1,0:T(8,128)(2,1)S(1)} %shard_map.63.refs_7_.refs_9_), channel_id=1, source_target_pairs={{0,8},{1,9},{2,10},{3,11},{4,12},{5,13},{6,14},{7,15},{8,0},{9,1},... | collective-permute-start | bytes 1572872 | tf_op jit(solution)/shard_map/ppermute | solution.py:365
  38.7 19.8 %collective-permute-start.15 = (bf16[16,128,128]{2,1,0:T(8,128)(2,1)S(1)}, bf16[16,128,128]{2,1,0:T(8,128)(2,1)S(1)}, u32[]{:S(2)}, u32[]{:S(2)}) collective-permute-start(bf16[16,128,128]{2,1,0:T(8,128)(2,1)S(1)} %shard_map.63.refs_7_.refs_9_), channel_id=1, source_target_pairs={{0,4},{1,5},{2,6},{3,7},{4,0},{5,1},{6,2},{7,3},{8,12},{9,13},{10,... | collective-permute-start | bytes 1572872 | tf_op jit(solution)/shard_map/ppermute | solution.py:365
  38.7 19.8 %collective-permute-start.16 = (bf16[16,128,128]{2,1,0:T(8,128)(2,1)S(1)}, bf16[16,128,128]{2,1,0:T(8,128)(2,1)S(1)}, u32[]{:S(2)}, u32[]{:S(2)}) collective-permute-start(bf16[16,128,128]{2,1,0:T(8,128)(2,1)S(1)} %shard_map.58.refs_3_.refs_0_.refs_5_), channel_id=1, source_target_pairs={{0,4},{1,5},{2,6},{3,7},{4,0},{5,1},{6,2},{7,3},{8,12},{9,13},{10,... | collective-permute-start | bytes 1572872 | tf_op jit(solution)/shard_map/ppermute | solution.py:365
  39.2 12.6 %collective-permute-start.6 = (bf16[20,16,128]{2,1,0:T(8,128)(2,1)S(1)}, bf16[20,16,128]{2,1,0:T(8,128)(2,1)S(1)}, u32[]{:S(2)}, u32[]{:S(2)}) collective-permute-start(bf16[20,16,128]{2,1,0:T(8,128)(2,1)S(1)} %shard_map.55), channel_id=1, source_target_pairs={{0,1},{1,0},{2,3},{3,2},{4,5},{5,4},{6,7},{7,6},{8,9},{9,8},{10,11... | collective-permute-start | bytes 245768 | tf_op jit(solution)/shard_map/ppermute | solution.py:365
  51.8 6.5 %collective-permute-start.7 = (bf16[24,16,128]{2,1,0:T(8,128)(2,1)S(1)}, bf16[24,16,128]{2,1,0:T(8,128)(2,1)S(1)}, u32[]{:S(2)}, u32[]{:S(2)}) collective-permute-start(bf16[24,16,128]{2,1,0:T(8,128)(2,1)S(1)} %get-tuple-element.21), channel_id=1, source_target_pairs={{0,3},{1,2},{2,1},{3,0},{4,7},{5,6},{6,5},{7,4},{8,11},{9,10},{10,... | collective-permute-start | bytes 294920 | tf_op jit(solution)/shard_map/ppermute | solution.py:365
  58.3 2.6 %collective-permute-start.18 = (bf16[16,128,128]{2,1,0:T(8,128)(2,1)S(1)}, bf16[16,128,128]{2,1,0:T(8,128)(2,1)S(1)}, u32[]{:S(2)}, u32[]{:S(2)}) collective-permute-start(bf16[16,128,128]{2,1,0:T(8,128)(2,1)S(1)} %collective-permute-done.13.refs_0_.refs_8_.refs_10_), channel_id=1, source_target_pairs={{0,4},{1,5},{2,6},{3,7},{4,0},{5,1},{6,2},{7,3},{8,12},{9,13},{10,... | collective-permute-start | bytes 1572872 | tf_op jit(solution)/shard_map/ppermute | solution.py:365
  58.5 2.6 %collective-permute-start.17 = (bf16[16,128,128]{2,1,0:T(8,128)(2,1)S(1)}, bf16[16,128,128]{2,1,0:T(8,128)(2,1)S(1)}, u32[]{:S(2)}, u32[]{:S(2)}) collective-permute-start(bf16[16,128,128]{2,1,0:T(8,128)(2,1)S(1)} %shard_map.65.refs_9_.refs_11_), channel_id=1, source_target_pairs={{0,4},{1,5},{2,6},{3,7},{4,0},{5,1},{6,2},{7,3},{8,12},{9,13},{10,... | collective-permute-start | bytes 1572872 | tf_op jit(solution)/shard_map/ppermute | solution.py:365
  59.0 8.3 %collective-permute-start.19 = (bf16[8,128,128]{2,1,0:T(8,128)(2,1)S(1)}, bf16[8,128,128]{2,1,0:T(8,128)(2,1)S(1)}, u32[]{:S(2)}, u32[]{:S(2)}) collective-permute-start(bf16[8,128,128]{2,1,0:T(8,128)(2,1)S(1)} %slice.8), channel_id=1, source_target_pairs={{0,8},{1,9},{2,10},{3,11},{4,12},{5,13},{6,14},{7,15},{8,0},{9,1},... | collective-permute-start | bytes 786440 | tf_op jit(solution)/shard_map/ppermute | solution.py:365
  59.6 8.0 %collective-permute-start.20 = (bf16[8,128,128]{2,1,0:T(8,128)(2,1)S(1)}, bf16[8,128,128]{2,1,0:T(8,128)(2,1)S(1)}, u32[]{:S(2)}, u32[]{:S(2)}) collective-permute-start(bf16[8,128,128]{2,1,0:T(8,128)(2,1)S(1)} %slice.9), channel_id=1, source_target_pairs={{0,1},{1,0},{2,3},{3,2},{4,5},{5,4},{6,7},{7,6},{8,9},{9,8},{10,11... | collective-permute-start | bytes 786440 | tf_op jit(solution)/shard_map/ppermute | solution.py:365
  67.4 1.5 %collective-permute-start.21 = (bf16[8,128,128]{2,1,0:T(8,128)(2,1)S(1)}, bf16[8,128,128]{2,1,0:T(8,128)(2,1)S(1)}, u32[]{:S(2)}, u32[]{:S(2)}) collective-permute-start(bf16[8,128,128]{2,1,0:T(8,128)(2,1)S(1)} %shard_map.67.refs_16_), channel_id=1, source_target_pairs={{0,4},{1,5},{2,6},{3,7},{4,0},{5,1},{6,2},{7,3},{8,12},{9,13},{10,... | collective-permute-start | bytes 786440 | tf_op jit(solution)/shard_map/ppermute | solution.py:365
  67.7 1.6 %collective-permute-start.22 = (bf16[8,128,128]{2,1,0:T(8,128)(2,1)S(1)}, bf16[8,128,128]{2,1,0:T(8,128)(2,1)S(1)}, u32[]{:S(2)}, u32[]{:S(2)}) collective-permute-start(bf16[8,128,128]{2,1,0:T(8,128)(2,1)S(1)} %shard_map.68.refs_17_), channel_id=1, source_target_pairs={{0,4},{1,5},{2,6},{3,7},{4,0},{5,1},{6,2},{7,3},{8,12},{9,13},{10,... | collective-permute-start | bytes 786440 | tf_op jit(solution)/shard_map/ppermute | solution.py:365
  79.6 14.0 %all-to-all-start = ((bf16[16,2,16,256]{3,2,1,0:T(8,128)(2,1)}), bf16[16,2,16,256]{3,2,1,0:T(8,128)(2,1)S(1)}, u32[]{:S(2)}, u32[]{:S(2)}) async-start(bf16[16,2,16,256]{3,2,1,0:T(8,128)(2,1)} %shard_map.69.refs_1_), calls=%async_computation | async-start | bytes 524288 | tf_op jit(solution)/shard_map/all_to_all | solution.py:447
  (2 other events, 22.6 us)

commit v21 on v19

--- a/solution.py
+++ b/solution.py
@@ -10,7 +10,6 @@
 PER_ROW = 2
 DEG = 4
 SPLIT = 4
-UNROLL = 8
 GATHER_LIMIT = 12 * 2**20
 LANES = ("col", "row")
 INNER = (1, 2)
@@ -148,31 +147,33 @@
 
 
 def regroup_kernel(sources, count, stay_ref, came_ref, *outs):
-    per_piece = (stay_ref.shape[0] - sources) // (sources * count)
+    per_piece = (stay_ref.shape[0] - 1) // (sources * count)
     kept = max(count // 2, 1)
+    ids = stay_ref[sources * count * per_piece].astype(jnp.float32)
+    came = came_ref[sources * count * per_piece].astype(jnp.float32)
+    line = lax.broadcasted_iota(jnp.int32, ids.shape, 0)
+    ids = jnp.where(line < sources, ids, pltpu.roll(came, sources, 0))
     for h, out_ref in enumerate(outs):
+        if h == 1 and count == 1:
+            out_ref[...] = ids.astype(jnp.int32)
+            continue
         for s in range(2 * sources):
             ref = stay_ref if s < sources else came_ref
-            ids = ref[sources * count * per_piece + s % sources]
-            if h == 1 and count == 1:
-                out_ref[s : s + 1] = ids.astype(jnp.float32)[:1].astype(jnp.int32)
-                continue
             for k in range(kept * per_piece):
                 out_ref[s * kept * per_piece + k] = ref[(s % sources * count + h * kept) * per_piece + k]
-            if count > 1:
-                out_ref[2 * sources * kept * per_piece + s] = ids
+        if count > 1:
+            out_ref[2 * sources * kept * per_piece] = ids.astype(out_ref.dtype)
 
 
 def regroup(stay, came, sources, per_piece):
-    count = (stay.shape[0] // sources - 1) // per_piece
+    count = (stay.shape[0] - 1) // (sources * per_piece)
     _, share, orb = stay.shape
     if count > 1:
-        out = jax.ShapeDtypeStruct((sources * count * per_piece + 2 * sources, share, orb), stay.dtype)
-        outs = [out, out]
+        outs = [jax.ShapeDtypeStruct(stay.shape, stay.dtype)] * 2
     else:
         outs = [
             jax.ShapeDtypeStruct((2 * sources * per_piece, share, orb), stay.dtype),
-            jax.ShapeDtypeStruct((2 * sources, orb), jnp.int32),
+            jax.ShapeDtypeStruct((share, orb), jnp.int32),
         ]
     return pl.pallas_call(
         functools.partial(regroup_kernel, sources, count),
@@ -195,7 +196,7 @@
             continue
         here = across[g] * tile_rows + t
         places = [(tile, t * PER_ROW + p) for tile in group for p in range(PER_ROW)]
-        strip = jnp.concatenate([s[slot] for (_, s, _, _), slot in places], axis=1)
+        strip = jnp.concatenate([s[slot][...] for (_, s, _, _), slot in places], axis=1)
         turned = jnp.concatenate([st[i, slot] for (_, _, st, i), slot in places], axis=0)
         where = [ids_ref[place(g, f), slot] for (f, *_), slot in places]
         wide = jnp.concatenate([z[u] for u in where], axis=1)
@@ -208,15 +209,6 @@
 def clear(refs):
     for ref in refs:
         ref[...] = jnp.zeros_like(ref)
-
-
-def turn(s_ref, st_ref, i, start, count):
-    def four(k, carry):
-        for m in range(4):
-            st_ref[i, start + 4 * k + m] = s_ref[i, start + 4 * k + m].T
-        return carry
-
-    lax.fori_loop(0, count // 4, four, 0)
 
 
 def turn_all(bufs, st_ref):
@@ -251,12 +243,8 @@
     across = [lax.axis_index("col") ^ g for g in range(n_col)]
     clear(scattered)
 
-    def block_rows(k, carry):
-        for t in range(UNROLL):
-            multiply(k * UNROLL + t, groups, across, ids_ref, z, straight, scattered)
-        return carry
-
-    lax.fori_loop(0, z.shape[0] // n_col // UNROLL, block_rows, 0)
+    for t in range(z.shape[0] // n_col):
+        multiply(t, groups, across, ids_ref, z, straight, scattered)
     total = straight[...]
     for ref in scattered:
         total += ref[...]
@@ -294,25 +282,20 @@
     (sta_ref, stb_ref), refs = refs[:2], refs[2:]
     sa, refs = refs[: len(early)], refs[len(early) :]
     sb, refs = refs[: len(later)], refs[len(later) :]
-    bufs, (out_ref, s_ref, st_ref, z, now, prev, straight, *scattered, sems) = (
-        refs[: len(late)],
-        refs[len(late) :],
-    )
+    bufs, (out_ref, st_ref, z, now, prev, straight, *scattered) = refs[: len(late)], refs[len(late) :]
     n_blocks, share, orb = z.shape
     per_piece = n_blocks // (n_col * n_row)
     rest = sorted({(g, f) for g, f, _ in late})
-
-    copies = []
-    for i, (buf, (g, f, start)) in enumerate(zip(bufs, late)):
-        target = s_ref.at[rest.index((g, f)), pl.ds(start, buf.shape[0])]
-        copies.append(pltpu.make_async_copy(buf, target, sems.at[i]))
-        copies[-1].start()
     spread_vectors(parts_ref, z, n_col, n_row, prev)
-    for copy, buf, (g, f, start) in zip(copies, bufs, late):
-        copy.wait()
-        turn(s_ref, st_ref, rest.index((g, f)), start, buf.shape[0])
-
-    tiles = {at: (s_ref.at[i], st_ref, i) for i, at in enumerate(rest)}
+    slots = {at: {} for at in rest}
+    for buf, (g, f, start) in zip(bufs, late):
+        for k in range(buf.shape[0]):
+            slots[g, f][start + k] = buf.at[k]
+    for i, at in enumerate(rest):
+        for slot, block in slots[at].items():
+            st_ref[i, slot] = block[...].T
+
+    tiles = {at: (slots[at], st_ref, i) for i, at in enumerate(rest)}
     clear([straight])
     total = sum_products(grouped(tiles, n_col, n_row), n_col, ids_ref, z, straight, scattered)
     total += sum_ref[...]
@@ -434,13 +417,12 @@
     done = pl.pallas_call(
         functools.partial(filter_kernel, early, later, late, n_col, n_row),
         out_shape=jax.ShapeDtypeStruct((n_dev, 2, share, rows), jnp.bfloat16),
-        in_specs=smem() + vmem(4 + len(early + later)) + anywhere(len(late)),
+        in_specs=smem() + vmem(4 + len(early + later + late)),
         out_specs=vmem()[0],
         scratch_shapes=[
-            *[pltpu.VMEM((2, slots, orb, orb), blocks.dtype)] * 2,
+            pltpu.VMEM((2, slots, orb, orb), blocks.dtype),
             pltpu.VMEM((n_blocks, share, orb), jnp.bfloat16),
             *[pltpu.VMEM((n_blocks, share, orb), jnp.float32)] * (3 + SPLIT),
-            pltpu.SemaphoreType.DMA((len(late),)),
         ],
         compiler_params=pltpu.CompilerParams(vmem_limit_bytes=12 * 2**20),
     )(ids, mine, total, sta, stb, *sa, *sb, *late_bufs)
@@ -458,6 +440,7 @@
 def per_device(vectors, blocks, cols):
     n_dev = lax.axis_size(LANES)
     line_of_four = lax.axis_size("col") == 4 and lax.axis_size("row") == 4
+    line_of_four = line_of_four and vectors.shape[1] // n_dev == n_dev
     if line_of_four and n_dev * blocks.size * blocks.dtype.itemsize <= GATHER_LIMIT:
         return gather_plan(vectors, blocks, cols)
     return spread_plan(vectors, blocks, cols)

time: 86.5 us -> 85.2 us (0.985)
  waiting for transfers between devices: 45.1 us -> 43.8 us
    ppermute x23, waiting for transfers between devices: 35.1 us -> 33.8 us  [send(): return lax.ppermute(buf, LANES, pairs)]
  transfers between devices with their start and end apart: 24 -> 24, of which waited for: 11 -> 10; matrix products, arithmetic and copies ran while one was open for 1% -> 1% of each run, Pallas kernels for 6% -> 6%
where the time goes in v21:
time: 85.2 us; the launch traced here: 84.9 us
  waiting for transfers between devices  43.8 us (51%)
  starting transfers between devices  22.7 us (27%)
  Pallas kernels  16 us (19%)
  local copies, waits for them, and re-layouts  1.61 us (2%)
    ppermute x23, waiting for transfers between devices, send(): return lax.ppermute(buf, LANES, pairs)  33.8 us
    ppermute x23, starting transfers between devices, send(): return lax.ppermute(buf, LANES, pairs)  19.1 us
    all_to_all x1, waiting for transfers between devices, gather_plan(): back = lax.all_to_all(done, LANES, split_axis=0, concat_axis=0, tiled=True)  10.1 us
    pallas_call x1, Pallas kernels, gather_plan(): pl.pallas_call(functools.partial(filter_kernel, early, later, late, n_col...  9.59 us
    pallas_call x1, Pallas kernels, gather_plan(): pl.pallas_call(functools.partial(first_kernel, early, later, n_col, n_row...  4.04 us
    all_to_all x1, starting transfers between devices, gather_plan(): back = lax.all_to_all(done, LANES, split_axis=0, concat_axis=0, tiled=True)  3.59 us
  transfers between devices with their start and end apart: 24, of which 10 were waited for; matrix products, arithmetic and copies ran while one was open for 1% of the time, Pallas kernels for 6%

profile of v21, /device:TPU:0, one launch (start us, length us, event | category | flops | bytes accessed | tf_op | source)
XLA Modules:
  0.0 84.9 jit_solution(13683089718720189310)
XLA Ops:
  0.6 3.0 %collective-permute-start.5 = (bf16[16,128,128]{2,1,0:T(8,128)(2,1)}, bf16[16,128,128]{2,1,0:T(8,128)(2,1)S(1)}, u32[]{:S(2)}, u32[]{:S(2)}) collective-permute-start(bf16[16,128,128]{2,1,0:T(8,128)(2,1)} %bitcast.2), channel_id=1, source_target_pairs={{0,8},{1,9},{2,10},{3,11},{4,12},{5,13},{6,14},{7,15},{8,0},{9,1},... | collective-permute-start | bytes 1572872 | tf_op jit(solution)/shard_map/ppermute | solution.py:348
  3.7 1.6 %collective-permute-start.4 = (bf16[16,128,128]{2,1,0:T(8,128)(2,1)}, bf16[16,128,128]{2,1,0:T(8,128)(2,1)S(1)}, u32[]{:S(2)}, u32[]{:S(2)}) collective-permute-start(bf16[16,128,128]{2,1,0:T(8,128)(2,1)} %bitcast.4), channel_id=1, source_target_pairs={{0,1},{1,0},{2,3},{3,2},{4,5},{5,4},{6,7},{7,6},{8,9},{9,8},{10,11... | collective-permute-start | bytes 1572872 | tf_op jit(solution)/shard_map/ppermute | solution.py:348
  6.6 0.9 %copy-done.1 = bf16[256,256]{1,0:T(8,128)(2,1)S(1)} copy-done((bf16[256,256]{1,0:T(8,128)(2,1)S(1)}, bf16[256,256]{1,0:T(8,128)(2,1)}, u32[]{:S(2)}) %copy-start.1) | copy-done | bytes 131096
  7.9 1.0 %collective-permute-done.came_ref = bf16[17,16,128]{2,1,0:T(8,128)(2,1)S(1)} collective-permute-done((bf16[17,16,128]{2,1,0:T(8,128)(2,1)S(1)}, bf16[17,16,128]{2,1,0:T(8,128)(2,1)S(1)}, u32[]{:S(2)}, u32[]{:S(2)}) %collective-permute-start) | collective-permute-done | bytes 69664 | tf_op jit(solution)/shard_map/ppermute | solution.py:348
  9.5 7.8 %collective-permute-done.1.came_ref = bf16[17,16,128]{2,1,0:T(8,128)(2,1)S(1)} collective-permute-done((bf16[17,16,128]{2,1,0:T(8,128)(2,1)S(1)}, bf16[17,16,128]{2,1,0:T(8,128)(2,1)S(1)}, u32[]{:S(2)}, u32[]{:S(2)}) %collective-permute-start.1) | collective-permute-done | bytes 69664 | tf_op jit(solution)/shard_map/ppermute | solution.py:348
  17.3 1.9 %collective-permute-start.2 = (bf16[17,16,128]{2,1,0:T(8,128)(2,1)S(1)}, bf16[17,16,128]{2,1,0:T(8,128)(2,1)S(1)}, u32[]{:S(2)}, u32[]{:S(2)}) collective-permute-start(bf16[17,16,128]{2,1,0:T(8,128)(2,1)S(1)} %get-tuple-element.19.refs_2_), channel_id=1, source_target_pairs={{0,1},{1,0},{2,3},{3,2},{4,5},{5,4},{6,7},{7,6},{8,9},{9,8},{10,11... | collective-permute-start | bytes 208904 | tf_op jit(solution)/shard_map/ppermute | solution.py:348
  19.2 0.7 collective-permute-start.10
  19.9 1.4 %collective-permute-start.12 = (bf16[16,128,128]{2,1,0:T(8,128)(2,1)S(1)}, bf16[16,128,128]{2,1,0:T(8,128)(2,1)S(1)}, u32[]{:S(2)}, u32[]{:S(2)}) collective-permute-start(bf16[16,128,128]{2,1,0:T(8,128)(2,1)S(1)} %shard_map.60.one_ref), channel_id=1, source_target_pairs={{1,0},{2,3},{5,4},{6,7},{9,8},{10,11},{13,12},{14,15},{17,16},{18,... | collective-permute-start | bytes 1572872 | tf_op jit(solution)/shard_map/ppermute | solution.py:348
  21.4 1.6 %collective-permute-start.7 = (bf16[16,128,128]{2,1,0:T(8,128)(2,1)S(1)}, bf16[16,128,128]{2,1,0:T(8,128)(2,1)S(1)}, u32[]{:S(2)}, u32[]{:S(2)}) collective-permute-start(bf16[16,128,128]{2,1,0:T(8,128)(2,1)S(1)} %shard_map.56.refs_1_.refs_3_), channel_id=1, source_target_pairs={{0,8},{1,9},{2,10},{3,11},{4,12},{5,13},{6,14},{7,15},{8,0},{9,1},... | collective-permute-start | bytes 1572872 | tf_op jit(solution)/shard_map/ppermute | solution.py:348
  23.5 1.3 %collective-permute-start.14 = (bf16[16,128,128]{2,1,0:T(8,128)(2,1)S(1)}, bf16[16,128,128]{2,1,0:T(8,128)(2,1)S(1)}, u32[]{:S(2)}, u32[]{:S(2)}) collective-permute-start(bf16[16,128,128]{2,1,0:T(8,128)(2,1)S(1)} %shard_map.59.one_ref), channel_id=1, source_target_pairs={{1,0},{2,3},{5,4},{6,7},{9,8},{10,11},{13,12},{14,15},{17,16},{18,... | collective-permute-start | bytes 1572872 | tf_op jit(solution)/shard_map/ppermute | solution.py:348
  24.8 12.0 %collective-permute-done.12.refs_0_ = bf16[16,128,128]{2,1,0:T(8,128)(2,1)S(1)} collective-permute-done((bf16[16,128,128]{2,1,0:T(8,128)(2,1)S(1)}, bf16[16,128,128]{2,1,0:T(8,128)(2,1)S(1)}, u32[]{:S(2)}, u32[]{:S(2)}) %collective-permute-start.12) | collective-permute-done | bytes 524320 | tf_op jit(solution)/shard_map/ppermute | solution.py:348
  36.9 1.9 %collective-permute-start.13 = (bf16[16,128,128]{2,1,0:T(8,128)(2,1)S(1)}, bf16[16,128,128]{2,1,0:T(8,128)(2,1)S(1)}, u32[]{:S(2)}, u32[]{:S(2)}) collective-permute-start(bf16[16,128,128]{2,1,0:T(8,128)(2,1)S(1)} %shard_map.62.refs_7_.refs_9_), channel_id=1, source_target_pairs={{0,8},{1,9},{2,10},{3,11},{4,12},{5,13},{6,14},{7,15},{8,0},{9,1},... | collective-permute-start | bytes 1572872 | tf_op jit(solution)/shard_map/ppermute | solution.py:348
  39.7 5.8 %collective-permute-done.3.came_ref = bf16[17,16,128]{2,1,0:T(8,128)(2,1)S(1)} collective-permute-done((bf16[17,16,128]{2,1,0:T(8,128)(2,1)S(1)}, bf16[17,16,128]{2,1,0:T(8,128)(2,1)S(1)}, u32[]{:S(2)}, u32[]{:S(2)}) %collective-permute-start.3) | collective-permute-done | bytes 69664 | tf_op jit(solution)/shard_map/ppermute | solution.py:348
  45.5 1.2 %shard_map.58.refs_2_.sta_ref.refs_0_ = bf16[7,16,128,128]{3,2,1,0:T(8,128)(2,1)S(1)} custom-call(bf16[16,128,128]{2,1,0:T(8,128)(2,1)S(1)} %bitcast.6, bf16[16,128,128]{2,1,0:T(8,128)(2,1)S(1)} %shard_map.56.refs_1_.refs_3_, bf16[16,128,128]{2,1,0:T(8,128)(2,1)S(1)} %shard_map.55.refs_1_.refs_2_.refs_4_, ...), custom_call_target="tpu_custom_call" | custom-call | bytes 11010048 | tf_op jit(solution)/shard_map/pallas_call | solution.py:260
  46.7 2.3 %collective-permute-done.14.refs_0_ = bf16[16,128,128]{2,1,0:T(8,128)(2,1)S(1)} collective-permute-done((bf16[16,128,128]{2,1,0:T(8,128)(2,1)S(1)}, bf16[16,128,128]{2,1,0:T(8,128)(2,1)S(1)}, u32[]{:S(2)}, u32[]{:S(2)}) %collective-permute-start.14) | collective-permute-done | bytes 524320 | tf_op jit(solution)/shard_map/ppermute | solution.py:348
  49.6 1.5 %collective-permute-start.19 = (bf16[8,128,128]{2,1,0:T(8,128)(2,1)S(1)}, bf16[8,128,128]{2,1,0:T(8,128)(2,1)S(1)}, u32[]{:S(2)}, u32[]{:S(2)}) collective-permute-start(bf16[8,128,128]{2,1,0:T(8,128)(2,1)S(1)} %slice.8), channel_id=1, source_target_pairs={{0,8},{1,9},{2,10},{3,11},{4,12},{5,13},{6,14},{7,15},{8,0},{9,1},... | collective-permute-start | bytes 786440 | tf_op jit(solution)/shard_map/ppermute | solution.py:348
  51.8 4.0 %shard_map.65 = (bf16[7,16,128,128]{3,2,1,0:T(8,128)(2,1)S(1)}, f32[32,16,128]{2,1,0:T(8,128)S(1)}) custom-call(s32[16,128]{1,0:T(8,128)S(1)} %get-tuple-element.22.ids_ref.refs_0_, bf16[32,16,128]{2,1,0:T(8,128)(2,1)S(1)} %get-tuple-element.23.refs_1_.parts_ref, bf16[7,16,128,128]{3,2,1,0:T(8,128)(2,1)S(1)} %shard_map.58.refs_2_.sta_ref.refs_0_, ...), custom_call_target="tpu_custom_call" | custom-call | flops 234881024 | bytes 11010048 | tf_op jit(solution)/shard_map/pallas_call | solution.py:397
  55.9 2.1 %collective-permute-done.19.refs_0_ = bf16[8,128,128]{2,1,0:T(8,128)(2,1)S(1)} collective-permute-done((bf16[8,128,128]{2,1,0:T(8,128)(2,1)S(1)}, bf16[8,128,128]{2,1,0:T(8,128)(2,1)S(1)}, u32[]{:S(2)}, u32[]{:S(2)}) %collective-permute-start.19) | collective-permute-done | bytes 262176 | tf_op jit(solution)/shard_map/ppermute | solution.py:348
  57.9 1.3 %collective-permute-done.20.refs_0_ = bf16[8,128,128]{2,1,0:T(8,128)(2,1)S(1)} collective-permute-done((bf16[8,128,128]{2,1,0:T(8,128)(2,1)S(1)}, bf16[8,128,128]{2,1,0:T(8,128)(2,1)S(1)}, u32[]{:S(2)}, u32[]{:S(2)}) %collective-permute-start.20) | collective-permute-done | bytes 262176 | tf_op jit(solution)/shard_map/ppermute | solution.py:348
  59.5 1.3 %collective-permute-done.22.refs_19_ = bf16[8,128,128]{2,1,0:T(8,128)(2,1)S(1)} collective-permute-done((bf16[8,128,128]{2,1,0:T(8,128)(2,1)S(1)}, bf16[8,128,128]{2,1,0:T(8,128)(2,1)S(1)}, u32[]{:S(2)}, u32[]{:S(2)}) %collective-permute-start.22) | collective-permute-done | bytes 262176 | tf_op jit(solution)/shard_map/ppermute | solution.py:348
  60.7 9.6 %shard_map.68.refs_1_ = bf16[16,2,16,256]{3,2,1,0:T(8,128)(2,1)} custom-call(s32[16,128]{1,0:T(8,128)S(1)} %get-tuple-element.22.ids_ref.refs_0_, bf16[32,16,128]{2,1,0:T(8,128)(2,1)S(1)} %get-tuple-element.23.refs_1_.parts_ref, f32[32,16,128]{2,1,0:T(8,128)S(1)} %get-tuple-element.24.sum_ref, ...), custom_call_target="tpu_custom_call" | custom-call | tf_op jit(solution)/shard_map/pallas_call | solution.py:417
  70.3 3.6 %all-to-all-start = ((bf16[16,2,16,256]{3,2,1,0:T(8,128)(2,1)}), bf16[16,2,16,256]{3,2,1,0:T(8,128)(2,1)S(1)}, u32[]{:S(2)}, u32[]{:S(2)}) async-start(bf16[16,2,16,256]{3,2,1,0:T(8,128)(2,1)} %shard_map.68.refs_1_), calls=%async_computation | async-start | bytes 524288 | tf_op jit(solution)/shard_map/all_to_all | solution.py:429
  73.9 10.1 %all-to-all-done.back_ref = bf16[16,2,16,256]{3,2,1,0:T(8,128)(2,1)S(1)} async-done(((bf16[16,2,16,256]{3,2,1,0:T(8,128)(2,1)}), bf16[16,2,16,256]{3,2,1,0:T(8,128)(2,1)S(1)}, u32[]{:S(2)}, u32[]{:S(2)}) %all-to-all-start) | async-done | bytes 262176 | tf_op jit(solution)/shard_map/all_to_all | solution.py:429
  84.0 0.9 %shard_map.70 = (f32[256,256]{1,0:T(8,128)}, f32[256,256]{1,0:T(8,128)}) custom-call(bf16[16,2,16,256]{3,2,1,0:T(8,128)(2,1)S(1)} %all-to-all-done.back_ref, s32[16,128]{1,0:T(8,128)S(1)} %shard_map.69.marker_ref), custom_call_target="tpu_custom_call" | custom-call | tf_op jit(solution)/shard_map/pallas_call | solution.py:431
  (53 shorter events, 5.5 us)
Async XLA Ops:
  0.6 18.5 %collective-permute-start.5 = (bf16[16,128,128]{2,1,0:T(8,128)(2,1)}, bf16[16,128,128]{2,1,0:T(8,128)(2,1)S(1)}, u32[]{:S(2)}, u32[]{:S(2)}) collective-permute-start(bf16[16,128,128]{2,1,0:T(8,128)(2,1)} %bitcast.2), channel_id=1, source_target_pairs={{0,8},{1,9},{2,10},{3,11},{4,12},{5,13},{6,14},{7,15},{8,0},{9,1},... | collective-permute-start | bytes 1572872 | tf_op jit(solution)/shard_map/ppermute | solution.py:348
  3.7 15.5 %collective-permute-start.6 = (bf16[16,128,128]{2,1,0:T(8,128)(2,1)}, bf16[16,128,128]{2,1,0:T(8,128)(2,1)S(1)}, u32[]{:S(2)}, u32[]{:S(2)}) collective-permute-start(bf16[16,128,128]{2,1,0:T(8,128)(2,1)} %bitcast.3), channel_id=1, source_target_pairs={{0,4},{1,5},{2,6},{3,7},{4,0},{5,1},{6,2},{7,3},{8,12},{9,13},{10,... | collective-permute-start | bytes 1572872 | tf_op jit(solution)/shard_map/ppermute | solution.py:348
  3.7 15.5 %collective-permute-start.4 = (bf16[16,128,128]{2,1,0:T(8,128)(2,1)}, bf16[16,128,128]{2,1,0:T(8,128)(2,1)S(1)}, u32[]{:S(2)}, u32[]{:S(2)}) collective-permute-start(bf16[16,128,128]{2,1,0:T(8,128)(2,1)} %bitcast.4), channel_id=1, source_target_pairs={{0,1},{1,0},{2,3},{3,2},{4,5},{5,4},{6,7},{7,6},{8,9},{9,8},{10,11... | collective-permute-start | bytes 1572872 | tf_op jit(solution)/shard_map/ppermute | solution.py:348
  5.2 14.7 %collective-permute-start.11 = (bf16[16,128,128]{2,1,0:T(8,128)(2,1)}, bf16[16,128,128]{2,1,0:T(8,128)(2,1)S(1)}, u32[]{:S(2)}, u32[]{:S(2)}) collective-permute-start(bf16[16,128,128]{2,1,0:T(8,128)(2,1)} %bitcast.5), channel_id=1, source_target_pairs={{1,2},{2,1},{5,6},{6,5},{9,10},{10,9},{13,14},{14,13},{17,18},{18,... | collective-permute-start | bytes 1572872 | tf_op jit(solution)/shard_map/ppermute | solution.py:348
  7.6 1.3 %collective-permute-start = (bf16[17,16,128]{2,1,0:T(8,128)(2,1)S(1)}, bf16[17,16,128]{2,1,0:T(8,128)(2,1)S(1)}, u32[]{:S(2)}, u32[]{:S(2)}) collective-permute-start(bf16[17,16,128]{2,1,0:T(8,128)(2,1)S(1)} %get-tuple-element.15), channel_id=1, source_target_pairs={{0,4},{1,5},{2,6},{3,7},{4,0},{5,1},{6,2},{7,3},{8,12},{9,13},{10,... | collective-permute-start | bytes 208904 | tf_op jit(solution)/shard_map/ppermute | solution.py:348
  9.0 8.3 %collective-permute-start.1 = (bf16[17,16,128]{2,1,0:T(8,128)(2,1)S(1)}, bf16[17,16,128]{2,1,0:T(8,128)(2,1)S(1)}, u32[]{:S(2)}, u32[]{:S(2)}) collective-permute-start(bf16[17,16,128]{2,1,0:T(8,128)(2,1)S(1)} %get-tuple-element.17), channel_id=1, source_target_pairs={{0,8},{1,9},{2,10},{3,11},{4,12},{5,13},{6,14},{7,15},{8,0},{9,1},... | collective-permute-start | bytes 208904 | tf_op jit(solution)/shard_map/ppermute | solution.py:348
  17.3 5.6 %collective-permute-start.2 = (bf16[17,16,128]{2,1,0:T(8,128)(2,1)S(1)}, bf16[17,16,128]{2,1,0:T(8,128)(2,1)S(1)}, u32[]{:S(2)}, u32[]{:S(2)}) collective-permute-start(bf16[17,16,128]{2,1,0:T(8,128)(2,1)S(1)} %get-tuple-element.19.refs_2_), channel_id=1, source_target_pairs={{0,1},{1,0},{2,3},{3,2},{4,5},{5,4},{6,7},{7,6},{8,9},{9,8},{10,11... | collective-permute-start | bytes 208904 | tf_op jit(solution)/shard_map/ppermute | solution.py:348
  19.2 4.3 %collective-permute-start.10 = (bf16[16,128,128]{2,1,0:T(8,128)(2,1)S(1)}, bf16[16,128,128]{2,1,0:T(8,128)(2,1)S(1)}, u32[]{:S(2)}, u32[]{:S(2)}) collective-permute-start(bf16[16,128,128]{2,1,0:T(8,128)(2,1)S(1)} %shard_map.56.refs_1_.refs_3_), channel_id=1, source_target_pairs={{1,2},{2,1},{5,6},{6,5},{9,10},{10,9},{13,14},{14,13},{17,18},{18,... | collective-permute-start | bytes 1572872 | tf_op jit(solution)/shard_map/ppermute | solution.py:348
  19.9 16.9 %collective-permute-start.12 = (bf16[16,128,128]{2,1,0:T(8,128)(2,1)S(1)}, bf16[16,128,128]{2,1,0:T(8,128)(2,1)S(1)}, u32[]{:S(2)}, u32[]{:S(2)}) collective-permute-start(bf16[16,128,128]{2,1,0:T(8,128)(2,1)S(1)} %shard_map.60.one_ref), channel_id=1, source_target_pairs={{1,0},{2,3},{5,4},{6,7},{9,8},{10,11},{13,12},{14,15},{17,16},{18,... | collective-permute-start | bytes 1572872 | tf_op jit(solution)/shard_map/ppermute | solution.py:348
  21.4 15.5 %collective-permute-start.7 = (bf16[16,128,128]{2,1,0:T(8,128)(2,1)S(1)}, bf16[16,128,128]{2,1,0:T(8,128)(2,1)S(1)}, u32[]{:S(2)}, u32[]{:S(2)}) collective-permute-start(bf16[16,128,128]{2,1,0:T(8,128)(2,1)S(1)} %shard_map.56.refs_1_.refs_3_), channel_id=1, source_target_pairs={{0,8},{1,9},{2,10},{3,11},{4,12},{5,13},{6,14},{7,15},{8,0},{9,1},... | collective-permute-start | bytes 1572872 | tf_op jit(solution)/shard_map/ppermute | solution.py:348
  22.9 13.9 %collective-permute-start.9 = (bf16[16,128,128]{2,1,0:T(8,128)(2,1)S(1)}, bf16[16,128,128]{2,1,0:T(8,128)(2,1)S(1)}, u32[]{:S(2)}, u32[]{:S(2)}) collective-permute-start(bf16[16,128,128]{2,1,0:T(8,128)(2,1)S(1)} %shard_map.55.refs_1_.refs_2_.refs_4_), channel_id=1, source_target_pairs={{0,4},{1,5},{2,6},{3,7},{4,0},{5,1},{6,2},{7,3},{8,12},{9,13},{10,... | collective-permute-start | bytes 1572872 | tf_op jit(solution)/shard_map/ppermute | solution.py:348
  22.9 13.9 %collective-permute-start.8 = (bf16[16,128,128]{2,1,0:T(8,128)(2,1)S(1)}, bf16[16,128,128]{2,1,0:T(8,128)(2,1)S(1)}, u32[]{:S(2)}, u32[]{:S(2)}) collective-permute-start(bf16[16,128,128]{2,1,0:T(8,128)(2,1)S(1)} %shard_map.56.refs_1_.refs_3_), channel_id=1, source_target_pairs={{0,4},{1,5},{2,6},{3,7},{4,0},{5,1},{6,2},{7,3},{8,12},{9,13},{10,... | collective-permute-start | bytes 1572872 | tf_op jit(solution)/shard_map/ppermute | solution.py:348
  23.5 25.5 %collective-permute-start.14 = (bf16[16,128,128]{2,1,0:T(8,128)(2,1)S(1)}, bf16[16,128,128]{2,1,0:T(8,128)(2,1)S(1)}, u32[]{:S(2)}, u32[]{:S(2)}) collective-permute-start(bf16[16,128,128]{2,1,0:T(8,128)(2,1)S(1)} %shard_map.59.one_ref), channel_id=1, source_target_pairs={{1,0},{2,3},{5,4},{6,7},{9,8},{10,11},{13,12},{14,15},{17,16},{18,... | collective-permute-start | bytes 1572872 | tf_op jit(solution)/shard_map/ppermute | solution.py:348
  36.9 12.1 %collective-permute-start.13 = (bf16[16,128,128]{2,1,0:T(8,128)(2,1)S(1)}, bf16[16,128,128]{2,1,0:T(8,128)(2,1)S(1)}, u32[]{:S(2)}, u32[]{:S(2)}) collective-permute-start(bf16[16,128,128]{2,1,0:T(8,128)(2,1)S(1)} %shard_map.62.refs_7_.refs_9_), channel_id=1, source_target_pairs={{0,8},{1,9},{2,10},{3,11},{4,12},{5,13},{6,14},{7,15},{8,0},{9,1},... | collective-permute-start | bytes 1572872 | tf_op jit(solution)/shard_map/ppermute | solution.py:348
  38.8 10.2 %collective-permute-start.15 = (bf16[16,128,128]{2,1,0:T(8,128)(2,1)S(1)}, bf16[16,128,128]{2,1,0:T(8,128)(2,1)S(1)}, u32[]{:S(2)}, u32[]{:S(2)}) collective-permute-start(bf16[16,128,128]{2,1,0:T(8,128)(2,1)S(1)} %shard_map.62.refs_7_.refs_9_), channel_id=1, source_target_pairs={{0,4},{1,5},{2,6},{3,7},{4,0},{5,1},{6,2},{7,3},{8,12},{9,13},{10,... | collective-permute-start | bytes 1572872 | tf_op jit(solution)/shard_map/ppermute | solution.py:348
  38.8 10.2 %collective-permute-start.16 = (bf16[16,128,128]{2,1,0:T(8,128)(2,1)S(1)}, bf16[16,128,128]{2,1,0:T(8,128)(2,1)S(1)}, u32[]{:S(2)}, u32[]{:S(2)}) collective-permute-start(bf16[16,128,128]{2,1,0:T(8,128)(2,1)S(1)} %shard_map.57.refs_3_.refs_0_.refs_5_), channel_id=1, source_target_pairs={{0,4},{1,5},{2,6},{3,7},{4,0},{5,1},{6,2},{7,3},{8,12},{9,13},{10,... | collective-permute-start | bytes 1572872 | tf_op jit(solution)/shard_map/ppermute | solution.py:348
  39.3 6.2 %collective-permute-start.3 = (bf16[17,16,128]{2,1,0:T(8,128)(2,1)S(1)}, bf16[17,16,128]{2,1,0:T(8,128)(2,1)S(1)}, u32[]{:S(2)}, u32[]{:S(2)}) collective-permute-start(bf16[17,16,128]{2,1,0:T(8,128)(2,1)S(1)} %get-tuple-element.21.refs_1_), channel_id=1, source_target_pairs={{0,3},{1,2},{2,1},{3,0},{4,7},{5,6},{6,5},{7,4},{8,11},{9,10},{10,... | collective-permute-start | bytes 208904 | tf_op jit(solution)/shard_map/ppermute | solution.py:348
  49.0 2.9 %collective-permute-start.18 = (bf16[16,128,128]{2,1,0:T(8,128)(2,1)S(1)}, bf16[16,128,128]{2,1,0:T(8,128)(2,1)S(1)}, u32[]{:S(2)}, u32[]{:S(2)}) collective-permute-start(bf16[16,128,128]{2,1,0:T(8,128)(2,1)S(1)} %collective-permute-done.13.refs_0_.refs_8_.refs_10_), channel_id=1, source_target_pairs={{0,4},{1,5},{2,6},{3,7},{4,0},{5,1},{6,2},{7,3},{8,12},{9,13},{10,... | collective-permute-start | bytes 1572872 | tf_op jit(solution)/shard_map/ppermute | solution.py:348
  49.1 2.8 %collective-permute-start.17 = (bf16[16,128,128]{2,1,0:T(8,128)(2,1)S(1)}, bf16[16,128,128]{2,1,0:T(8,128)(2,1)S(1)}, u32[]{:S(2)}, u32[]{:S(2)}) collective-permute-start(bf16[16,128,128]{2,1,0:T(8,128)(2,1)S(1)} %shard_map.64.refs_9_.refs_11_), channel_id=1, source_target_pairs={{0,4},{1,5},{2,6},{3,7},{4,0},{5,1},{6,2},{7,3},{8,12},{9,13},{10,... | collective-permute-start | bytes 1572872 | tf_op jit(solution)/shard_map/ppermute | solution.py:348
  49.6 8.3 %collective-permute-start.19 = (bf16[8,128,128]{2,1,0:T(8,128)(2,1)S(1)}, bf16[8,128,128]{2,1,0:T(8,128)(2,1)S(1)}, u32[]{:S(2)}, u32[]{:S(2)}) collective-permute-start(bf16[8,128,128]{2,1,0:T(8,128)(2,1)S(1)} %slice.8), channel_id=1, source_target_pairs={{0,8},{1,9},{2,10},{3,11},{4,12},{5,13},{6,14},{7,15},{8,0},{9,1},... | collective-permute-start | bytes 786440 | tf_op jit(solution)/shard_map/ppermute | solution.py:348
  51.2 8.0 %collective-permute-start.20 = (bf16[8,128,128]{2,1,0:T(8,128)(2,1)S(1)}, bf16[8,128,128]{2,1,0:T(8,128)(2,1)S(1)}, u32[]{:S(2)}, u32[]{:S(2)}) collective-permute-start(bf16[8,128,128]{2,1,0:T(8,128)(2,1)S(1)} %slice.9), channel_id=1, source_target_pairs={{0,1},{1,0},{2,3},{3,2},{4,5},{5,4},{6,7},{7,6},{8,9},{9,8},{10,11... | collective-permute-start | bytes 786440 | tf_op jit(solution)/shard_map/ppermute | solution.py:348
  57.9 1.5 %collective-permute-start.21 = (bf16[8,128,128]{2,1,0:T(8,128)(2,1)S(1)}, bf16[8,128,128]{2,1,0:T(8,128)(2,1)S(1)}, u32[]{:S(2)}, u32[]{:S(2)}) collective-permute-start(bf16[8,128,128]{2,1,0:T(8,128)(2,1)S(1)} %shard_map.66.refs_16_), channel_id=1, source_target_pairs={{0,4},{1,5},{2,6},{3,7},{4,0},{5,1},{6,2},{7,3},{8,12},{9,13},{10,... | collective-permute-start | bytes 786440 | tf_op jit(solution)/shard_map/ppermute | solution.py:348
  59.2 1.5 %collective-permute-start.22 = (bf16[8,128,128]{2,1,0:T(8,128)(2,1)S(1)}, bf16[8,128,128]{2,1,0:T(8,128)(2,1)S(1)}, u32[]{:S(2)}, u32[]{:S(2)}) collective-permute-start(bf16[8,128,128]{2,1,0:T(8,128)(2,1)S(1)} %shard_map.67.refs_17_), channel_id=1, source_target_pairs={{0,4},{1,5},{2,6},{3,7},{4,0},{5,1},{6,2},{7,3},{8,12},{9,13},{10,... | collective-permute-start | bytes 786440 | tf_op jit(solution)/shard_map/ppermute | solution.py:348
  70.3 13.7 %all-to-all-start = ((bf16[16,2,16,256]{3,2,1,0:T(8,128)(2,1)}), bf16[16,2,16,256]{3,2,1,0:T(8,128)(2,1)S(1)}, u32[]{:S(2)}, u32[]{:S(2)}) async-start(bf16[16,2,16,256]{3,2,1,0:T(8,128)(2,1)} %shard_map.68.refs_1_), calls=%async_computation | async-start | bytes 524288 | tf_op jit(solution)/shard_map/all_to_all | solution.py:429
  (2 other events, 26.5 us)

commit v22 on v21

--- a/solution.py
+++ b/solution.py
@@ -95,6 +95,24 @@
     )(value, *others)
 
 
+def copy_kernel(value_ref, *refs):
+    out_ref, sem = refs[-2:]
+    copy = pltpu.make_async_copy(value_ref, out_ref, sem)
+    copy.start()
+    copy.wait()
+
+
+def copy_after(value, *others):
+    return pl.pallas_call(
+        copy_kernel,
+        out_shape=jax.ShapeDtypeStruct(value.shape, value.dtype),
+        in_specs=anywhere(1 + len(others)),
+        out_specs=anywhere()[0],
+        scratch_shapes=[pltpu.SemaphoreType.DMA(())],
+        compiler_params=pltpu.CompilerParams(vmem_limit_bytes=2**20),
+    )(value, *others)
+
+
 def pick_kernel(rows, one_ref, other_ref, *refs):
     out_ref, sem = refs[-2:]
     row = lax.axis_index("row")
@@ -371,11 +389,12 @@
     mates = to_mate(own)
     near = after(near, over_own, go, *mates)
     over_near = after(send(near, 2, 0), rank=3)
-    crossed = after(send(near, 0, 3, INNER), rank=1)
+    mates += to_mate(near)
+    crossed = after(send(copy_after(near, mates[1]), 0, 3, INNER), rank=1)
     inner = after(inner, near)
     outward = after(send(inner, 0, 1, INNER), rank=1)
     stay, go = regroup(stay, send(go, 0, 1), 4, per_piece)
-    mates += to_mate(near, over_own)
+    mates += to_mate(over_own)
     two = pick(INNER, crossed, outward, over_near, go, *mates)
 
     over_two = send(two, 2, 0)

time: 85.2 us -> 93.2 us (1.094)
  starting transfers between devices: 22.7 us -> 32.6 us
  waiting for transfers between devices: 43.8 us -> 41.8 us
    ppermute x23, starting transfers between devices: 19.1 us -> 28.6 us  [send(): return lax.ppermute(buf, LANES, pairs)]
    ppermute x23, waiting for transfers between devices: 33.8 us -> 31.7 us  [send(): return lax.ppermute(buf, LANES, pairs)]
  transfers between devices with their start and end apart: 24 -> 24, of which waited for: 10 -> 12; matrix products, arithmetic and copies ran while one was open for 1% -> 1% of each run, Pallas kernels for 6% -> 6%
where the time goes in v22:
time: 93.2 us; the launch traced here: 92.9 us
  waiting for transfers between devices  41.8 us (45%)
  starting transfers between devices  32.6 us (35%)
  Pallas kernels  16 us (17%)
  local copies, waits for them, and re-layouts  1.61 us (2%)
    ppermute x23, waiting for transfers between devices, send(): return lax.ppermute(buf, LANES, pairs)  31.7 us
    ppermute x23, starting transfers between devices, send(): return lax.ppermute(buf, LANES, pairs)  28.6 us
    all_to_all x1, waiting for transfers between devices, gather_plan(): back = lax.all_to_all(done, LANES, split_axis=0, concat_axis=0, tiled=True)  10.1 us
    pallas_call x1, Pallas kernels, gather_plan(): pl.pallas_call(functools.partial(filter_kernel, early, later, late, n_col...  9.59 us
    pallas_call x1, Pallas kernels, gather_plan(): pl.pallas_call(functools.partial(first_kernel, early, later, n_col, n_row...  4.05 us
    all_to_all x1, starting transfers between devices, gather_plan(): back = lax.all_to_all(done, LANES, split_axis=0, concat_axis=0, tiled=True)  4 us
  transfers between devices with their start and end apart: 24, of which 12 were waited for; matrix products, arithmetic and copies ran while one was open for 1% of the time, Pallas kernels for 6%

profile of v22, /device:TPU:0, one launch (start us, length us, event | category | flops | bytes accessed | tf_op | source)
XLA Modules:
  0.0 92.9 jit_solution(12509316518192681804)
XLA Ops:
  0.6 3.0 %collective-permute-start.5 = (bf16[16,128,128]{2,1,0:T(8,128)(2,1)}, bf16[16,128,128]{2,1,0:T(8,128)(2,1)S(1)}, u32[]{:S(2)}, u32[]{:S(2)}) collective-permute-start(bf16[16,128,128]{2,1,0:T(8,128)(2,1)} %bitcast.2), channel_id=1, source_target_pairs={{0,8},{1,9},{2,10},{3,11},{4,12},{5,13},{6,14},{7,15},{8,0},{9,1},... | collective-permute-start | bytes 1572872 | tf_op jit(solution)/shard_map/ppermute | solution.py:366
  3.7 1.6 %collective-permute-start.4 = (bf16[16,128,128]{2,1,0:T(8,128)(2,1)}, bf16[16,128,128]{2,1,0:T(8,128)(2,1)S(1)}, u32[]{:S(2)}, u32[]{:S(2)}) collective-permute-start(bf16[16,128,128]{2,1,0:T(8,128)(2,1)} %bitcast.4), channel_id=1, source_target_pairs={{0,1},{1,0},{2,3},{3,2},{4,5},{5,4},{6,7},{7,6},{8,9},{9,8},{10,11... | collective-permute-start | bytes 1572872 | tf_op jit(solution)/shard_map/ppermute | solution.py:366
  5.9 0.9 copy-done.1
  7.2 1.0 %collective-permute-done.came_ref = bf16[17,16,128]{2,1,0:T(8,128)(2,1)S(1)} collective-permute-done((bf16[17,16,128]{2,1,0:T(8,128)(2,1)S(1)}, bf16[17,16,128]{2,1,0:T(8,128)(2,1)S(1)}, u32[]{:S(2)}, u32[]{:S(2)}) %collective-permute-start) | collective-permute-done | bytes 69664 | tf_op jit(solution)/shard_map/ppermute | solution.py:366
  9.5 7.8 %collective-permute-done.1.came_ref = bf16[17,16,128]{2,1,0:T(8,128)(2,1)S(1)} collective-permute-done((bf16[17,16,128]{2,1,0:T(8,128)(2,1)S(1)}, bf16[17,16,128]{2,1,0:T(8,128)(2,1)S(1)}, u32[]{:S(2)}, u32[]{:S(2)}) %collective-permute-start.1) | collective-permute-done | bytes 69664 | tf_op jit(solution)/shard_map/ppermute | solution.py:366
  17.3 0.9 collective-permute-done.4.refs_0_
  18.2 1.3 %collective-permute-start.12 = (bf16[16,128,128]{2,1,0:T(8,128)(2,1)S(1)}, bf16[16,128,128]{2,1,0:T(8,128)(2,1)S(1)}, u32[]{:S(2)}, u32[]{:S(2)}) collective-permute-start(bf16[16,128,128]{2,1,0:T(8,128)(2,1)S(1)} %shard_map.61.one_ref), channel_id=1, source_target_pairs={{1,0},{2,3},{5,4},{6,7},{9,8},{10,11},{13,12},{14,15},{17,16},{18,... | collective-permute-start | bytes 1572872 | tf_op jit(solution)/shard_map/ppermute | solution.py:366
  19.5 1.0 %collective-permute-start.7 = (bf16[16,128,128]{2,1,0:T(8,128)(2,1)S(1)}, bf16[16,128,128]{2,1,0:T(8,128)(2,1)S(1)}, u32[]{:S(2)}, u32[]{:S(2)}) collective-permute-start(bf16[16,128,128]{2,1,0:T(8,128)(2,1)S(1)} %shard_map.56.refs_1_.value_ref.refs_3_), channel_id=1, source_target_pairs={{0,8},{1,9},{2,10},{3,11},{4,12},{5,13},{6,14},{7,15},{8,0},{9,1},... | collective-permute-start | bytes 1572872 | tf_op jit(solution)/shard_map/ppermute | solution.py:366
  21.7 11.3 %collective-permute-start.2 = (bf16[17,16,128]{2,1,0:T(8,128)(2,1)S(1)}, bf16[17,16,128]{2,1,0:T(8,128)(2,1)S(1)}, u32[]{:S(2)}, u32[]{:S(2)}) collective-permute-start(bf16[17,16,128]{2,1,0:T(8,128)(2,1)S(1)} %get-tuple-element.19.refs_2_), channel_id=1, source_target_pairs={{0,1},{1,0},{2,3},{3,2},{4,5},{5,4},{6,7},{7,6},{8,9},{9,8},{10,11... | collective-permute-start | bytes 208904 | tf_op jit(solution)/shard_map/ppermute | solution.py:366
  33.0 7.4 %collective-permute-done.2.came_ref = bf16[17,16,128]{2,1,0:T(8,128)(2,1)S(1)} collective-permute-done((bf16[17,16,128]{2,1,0:T(8,128)(2,1)S(1)}, bf16[17,16,128]{2,1,0:T(8,128)(2,1)S(1)}, u32[]{:S(2)}, u32[]{:S(2)}) %collective-permute-start.2) | collective-permute-done | bytes 69664 | tf_op jit(solution)/shard_map/ppermute | solution.py:366
  40.5 1.3 %collective-permute-start.14 = (bf16[16,128,128]{2,1,0:T(8,128)(2,1)S(1)}, bf16[16,128,128]{2,1,0:T(8,128)(2,1)S(1)}, u32[]{:S(2)}, u32[]{:S(2)}) collective-permute-start(bf16[16,128,128]{2,1,0:T(8,128)(2,1)S(1)} %shard_map.60.one_ref), channel_id=1, source_target_pairs={{1,0},{2,3},{5,4},{6,7},{9,8},{10,11},{13,12},{14,15},{17,16},{18,... | collective-permute-start | bytes 1572872 | tf_op jit(solution)/shard_map/ppermute | solution.py:366
  41.8 1.6 %collective-permute-start.13 = (bf16[16,128,128]{2,1,0:T(8,128)(2,1)S(1)}, bf16[16,128,128]{2,1,0:T(8,128)(2,1)S(1)}, u32[]{:S(2)}, u32[]{:S(2)}) collective-permute-start(bf16[16,128,128]{2,1,0:T(8,128)(2,1)S(1)} %shard_map.63.refs_7_.refs_9_), channel_id=1, source_target_pairs={{0,8},{1,9},{2,10},{3,11},{4,12},{5,13},{6,14},{7,15},{8,0},{9,1},... | collective-permute-start | bytes 1572872 | tf_op jit(solution)/shard_map/ppermute | solution.py:366
  43.9 2.3 %collective-permute-start.3 = (bf16[17,16,128]{2,1,0:T(8,128)(2,1)S(1)}, bf16[17,16,128]{2,1,0:T(8,128)(2,1)S(1)}, u32[]{:S(2)}, u32[]{:S(2)}) collective-permute-start(bf16[17,16,128]{2,1,0:T(8,128)(2,1)S(1)} %get-tuple-element.21.refs_1_), channel_id=1, source_target_pairs={{0,3},{1,2},{2,1},{3,0},{4,7},{5,6},{6,5},{7,4},{8,11},{9,10},{10,... | collective-permute-start | bytes 208904 | tf_op jit(solution)/shard_map/ppermute | solution.py:366
  46.3 3.9 %collective-permute-done.3.came_ref = bf16[17,16,128]{2,1,0:T(8,128)(2,1)S(1)} collective-permute-done((bf16[17,16,128]{2,1,0:T(8,128)(2,1)S(1)}, bf16[17,16,128]{2,1,0:T(8,128)(2,1)S(1)}, u32[]{:S(2)}, u32[]{:S(2)}) %collective-permute-start.3) | collective-permute-done | bytes 69664 | tf_op jit(solution)/shard_map/ppermute | solution.py:366
  50.2 1.2 %shard_map.58.refs_2_.sta_ref.refs_0_ = bf16[7,16,128,128]{3,2,1,0:T(8,128)(2,1)S(1)} custom-call(bf16[16,128,128]{2,1,0:T(8,128)(2,1)S(1)} %bitcast.6, bf16[16,128,128]{2,1,0:T(8,128)(2,1)S(1)} %shard_map.56.refs_1_.value_ref.refs_3_, bf16[16,128,128]{2,1,0:T(8,128)(2,1)S(1)} %shard_map.55.refs_1_.refs_2_.refs_4_, ...), custom_call_target="tpu_custom_call" | custom-call | bytes 11010048 | tf_op jit(solution)/shard_map/pallas_call | solution.py:278
  51.3 5.8 %collective-permute-done.14.refs_0_ = bf16[16,128,128]{2,1,0:T(8,128)(2,1)S(1)} collective-permute-done((bf16[16,128,128]{2,1,0:T(8,128)(2,1)S(1)}, bf16[16,128,128]{2,1,0:T(8,128)(2,1)S(1)}, u32[]{:S(2)}, u32[]{:S(2)}) %collective-permute-start.14) | collective-permute-done | bytes 524320 | tf_op jit(solution)/shard_map/ppermute | solution.py:366
  57.8 0.9 collective-permute-start.19
  59.8 4.0 %shard_map.66 = (bf16[7,16,128,128]{3,2,1,0:T(8,128)(2,1)S(1)}, f32[32,16,128]{2,1,0:T(8,128)S(1)}) custom-call(s32[16,128]{1,0:T(8,128)S(1)} %get-tuple-element.22.ids_ref.refs_0_, bf16[32,16,128]{2,1,0:T(8,128)(2,1)S(1)} %get-tuple-element.23.refs_1_.parts_ref, bf16[7,16,128,128]{3,2,1,0:T(8,128)(2,1)S(1)} %shard_map.58.refs_2_.sta_ref.refs_0_, ...), custom_call_target="tpu_custom_call" | custom-call | flops 234881024 | bytes 11010048 | tf_op jit(solution)/shard_map/pallas_call | solution.py:416
  63.9 2.2 %collective-permute-done.19.refs_0_ = bf16[8,128,128]{2,1,0:T(8,128)(2,1)S(1)} collective-permute-done((bf16[8,128,128]{2,1,0:T(8,128)(2,1)S(1)}, bf16[8,128,128]{2,1,0:T(8,128)(2,1)S(1)}, u32[]{:S(2)}, u32[]{:S(2)}) %collective-permute-start.19) | collective-permute-done | bytes 262176 | tf_op jit(solution)/shard_map/ppermute | solution.py:366
  66.8 0.9 collective-permute-done.21.refs_18_
  68.3 9.6 %shard_map.69.refs_1_ = bf16[16,2,16,256]{3,2,1,0:T(8,128)(2,1)} custom-call(s32[16,128]{1,0:T(8,128)S(1)} %get-tuple-element.22.ids_ref.refs_0_, bf16[32,16,128]{2,1,0:T(8,128)(2,1)S(1)} %get-tuple-element.23.refs_1_.parts_ref, f32[32,16,128]{2,1,0:T(8,128)S(1)} %get-tuple-element.24.sum_ref, ...), custom_call_target="tpu_custom_call" | custom-call | tf_op jit(solution)/shard_map/pallas_call | solution.py:436
  77.9 4.0 %all-to-all-start = ((bf16[16,2,16,256]{3,2,1,0:T(8,128)(2,1)}), bf16[16,2,16,256]{3,2,1,0:T(8,128)(2,1)S(1)}, u32[]{:S(2)}, u32[]{:S(2)}) async-start(bf16[16,2,16,256]{3,2,1,0:T(8,128)(2,1)} %shard_map.69.refs_1_), calls=%async_computation | async-start | bytes 524288 | tf_op jit(solution)/shard_map/all_to_all | solution.py:448
  81.9 10.1 %all-to-all-done.back_ref = bf16[16,2,16,256]{3,2,1,0:T(8,128)(2,1)S(1)} async-done(((bf16[16,2,16,256]{3,2,1,0:T(8,128)(2,1)}), bf16[16,2,16,256]{3,2,1,0:T(8,128)(2,1)S(1)}, u32[]{:S(2)}, u32[]{:S(2)}) %all-to-all-start) | async-done | bytes 262176 | tf_op jit(solution)/shard_map/all_to_all | solution.py:448
  92.0 0.9 shard_map.71
  (54 shorter events, 7.1 us)
Async XLA Ops:
  0.6 16.7 %collective-permute-start.5 = (bf16[16,128,128]{2,1,0:T(8,128)(2,1)}, bf16[16,128,128]{2,1,0:T(8,128)(2,1)S(1)}, u32[]{:S(2)}, u32[]{:S(2)}) collective-permute-start(bf16[16,128,128]{2,1,0:T(8,128)(2,1)} %bitcast.2), channel_id=1, source_target_pairs={{0,8},{1,9},{2,10},{3,11},{4,12},{5,13},{6,14},{7,15},{8,0},{9,1},... | collective-permute-start | bytes 1572872 | tf_op jit(solution)/shard_map/ppermute | solution.py:366
  3.7 13.7 %collective-permute-start.6 = (bf16[16,128,128]{2,1,0:T(8,128)(2,1)}, bf16[16,128,128]{2,1,0:T(8,128)(2,1)S(1)}, u32[]{:S(2)}, u32[]{:S(2)}) collective-permute-start(bf16[16,128,128]{2,1,0:T(8,128)(2,1)} %bitcast.3), channel_id=1, source_target_pairs={{0,4},{1,5},{2,6},{3,7},{4,0},{5,1},{6,2},{7,3},{8,12},{9,13},{10,... | collective-permute-start | bytes 1572872 | tf_op jit(solution)/shard_map/ppermute | solution.py:366
  3.7 14.5 %collective-permute-start.4 = (bf16[16,128,128]{2,1,0:T(8,128)(2,1)}, bf16[16,128,128]{2,1,0:T(8,128)(2,1)S(1)}, u32[]{:S(2)}, u32[]{:S(2)}) collective-permute-start(bf16[16,128,128]{2,1,0:T(8,128)(2,1)} %bitcast.4), channel_id=1, source_target_pairs={{0,1},{1,0},{2,3},{3,2},{4,5},{5,4},{6,7},{7,6},{8,9},{9,8},{10,11... | collective-permute-start | bytes 1572872 | tf_op jit(solution)/shard_map/ppermute | solution.py:366
  6.9 1.3 %collective-permute-start = (bf16[17,16,128]{2,1,0:T(8,128)(2,1)S(1)}, bf16[17,16,128]{2,1,0:T(8,128)(2,1)S(1)}, u32[]{:S(2)}, u32[]{:S(2)}) collective-permute-start(bf16[17,16,128]{2,1,0:T(8,128)(2,1)S(1)} %get-tuple-element.15), channel_id=1, source_target_pairs={{0,4},{1,5},{2,6},{3,7},{4,0},{5,1},{6,2},{7,3},{8,12},{9,13},{10,... | collective-permute-start | bytes 208904 | tf_op jit(solution)/shard_map/ppermute | solution.py:366
  8.3 9.0 %collective-permute-start.1 = (bf16[17,16,128]{2,1,0:T(8,128)(2,1)S(1)}, bf16[17,16,128]{2,1,0:T(8,128)(2,1)S(1)}, u32[]{:S(2)}, u32[]{:S(2)}) collective-permute-start(bf16[17,16,128]{2,1,0:T(8,128)(2,1)S(1)} %get-tuple-element.17), channel_id=1, source_target_pairs={{0,8},{1,9},{2,10},{3,11},{4,12},{5,13},{6,14},{7,15},{8,0},{9,1},... | collective-permute-start | bytes 208904 | tf_op jit(solution)/shard_map/ppermute | solution.py:366
  8.8 9.4 %collective-permute-start.11 = (bf16[16,128,128]{2,1,0:T(8,128)(2,1)}, bf16[16,128,128]{2,1,0:T(8,128)(2,1)S(1)}, u32[]{:S(2)}, u32[]{:S(2)}) collective-permute-start(bf16[16,128,128]{2,1,0:T(8,128)(2,1)} %bitcast.5), channel_id=1, source_target_pairs={{1,2},{2,1},{5,6},{6,5},{9,10},{10,9},{13,14},{14,13},{17,18},{18,... | collective-permute-start | bytes 1572872 | tf_op jit(solution)/shard_map/ppermute | solution.py:366
  18.2 2.3 %collective-permute-start.8 = (bf16[16,128,128]{2,1,0:T(8,128)(2,1)S(1)}, bf16[16,128,128]{2,1,0:T(8,128)(2,1)S(1)}, u32[]{:S(2)}, u32[]{:S(2)}) collective-permute-start(bf16[16,128,128]{2,1,0:T(8,128)(2,1)S(1)} %shard_map.56.refs_1_.value_ref.refs_3_), channel_id=1, source_target_pairs={{0,4},{1,5},{2,6},{3,7},{4,0},{5,1},{6,2},{7,3},{8,12},{9,13},{10,... | collective-permute-start | bytes 1572872 | tf_op jit(solution)/shard_map/ppermute | solution.py:366
  18.2 22.2 %collective-permute-start.12 = (bf16[16,128,128]{2,1,0:T(8,128)(2,1)S(1)}, bf16[16,128,128]{2,1,0:T(8,128)(2,1)S(1)}, u32[]{:S(2)}, u32[]{:S(2)}) collective-permute-start(bf16[16,128,128]{2,1,0:T(8,128)(2,1)S(1)} %shard_map.61.one_ref), channel_id=1, source_target_pairs={{1,0},{2,3},{5,4},{6,7},{9,8},{10,11},{13,12},{14,15},{17,16},{18,... | collective-permute-start | bytes 1572872 | tf_op jit(solution)/shard_map/ppermute | solution.py:366
  19.5 20.9 %collective-permute-start.7 = (bf16[16,128,128]{2,1,0:T(8,128)(2,1)S(1)}, bf16[16,128,128]{2,1,0:T(8,128)(2,1)S(1)}, u32[]{:S(2)}, u32[]{:S(2)}) collective-permute-start(bf16[16,128,128]{2,1,0:T(8,128)(2,1)S(1)} %shard_map.56.refs_1_.value_ref.refs_3_), channel_id=1, source_target_pairs={{0,8},{1,9},{2,10},{3,11},{4,12},{5,13},{6,14},{7,15},{8,0},{9,1},... | collective-permute-start | bytes 1572872 | tf_op jit(solution)/shard_map/ppermute | solution.py:366
  20.6 19.8 %collective-permute-start.10 = (bf16[16,128,128]{2,1,0:T(8,128)(2,1)S(1)}, bf16[16,128,128]{2,1,0:T(8,128)(2,1)S(1)}, u32[]{:S(2)}, u32[]{:S(2)}) collective-permute-start(bf16[16,128,128]{2,1,0:T(8,128)(2,1)S(1)} %shard_map.59), channel_id=1, source_target_pairs={{1,2},{2,1},{5,6},{6,5},{9,10},{10,9},{13,14},{14,13},{17,18},{18,... | collective-permute-start | bytes 1572872 | tf_op jit(solution)/shard_map/ppermute | solution.py:366
  21.5 20.3 %collective-permute-start.9 = (bf16[16,128,128]{2,1,0:T(8,128)(2,1)S(1)}, bf16[16,128,128]{2,1,0:T(8,128)(2,1)S(1)}, u32[]{:S(2)}, u32[]{:S(2)}) collective-permute-start(bf16[16,128,128]{2,1,0:T(8,128)(2,1)S(1)} %shard_map.55.refs_1_.refs_2_.refs_4_), channel_id=1, source_target_pairs={{0,4},{1,5},{2,6},{3,7},{4,0},{5,1},{6,2},{7,3},{8,12},{9,13},{10,... | collective-permute-start | bytes 1572872 | tf_op jit(solution)/shard_map/ppermute | solution.py:366
  21.7 18.7 %collective-permute-start.2 = (bf16[17,16,128]{2,1,0:T(8,128)(2,1)S(1)}, bf16[17,16,128]{2,1,0:T(8,128)(2,1)S(1)}, u32[]{:S(2)}, u32[]{:S(2)}) collective-permute-start(bf16[17,16,128]{2,1,0:T(8,128)(2,1)S(1)} %get-tuple-element.19.refs_2_), channel_id=1, source_target_pairs={{0,1},{1,0},{2,3},{3,2},{4,5},{5,4},{6,7},{7,6},{8,9},{9,8},{10,11... | collective-permute-start | bytes 208904 | tf_op jit(solution)/shard_map/ppermute | solution.py:366
  40.5 16.7 %collective-permute-start.14 = (bf16[16,128,128]{2,1,0:T(8,128)(2,1)S(1)}, bf16[16,128,128]{2,1,0:T(8,128)(2,1)S(1)}, u32[]{:S(2)}, u32[]{:S(2)}) collective-permute-start(bf16[16,128,128]{2,1,0:T(8,128)(2,1)S(1)} %shard_map.60.one_ref), channel_id=1, source_target_pairs={{1,0},{2,3},{5,4},{6,7},{9,8},{10,11},{13,12},{14,15},{17,16},{18,... | collective-permute-start | bytes 1572872 | tf_op jit(solution)/shard_map/ppermute | solution.py:366
  41.8 15.3 %collective-permute-start.13 = (bf16[16,128,128]{2,1,0:T(8,128)(2,1)S(1)}, bf16[16,128,128]{2,1,0:T(8,128)(2,1)S(1)}, u32[]{:S(2)}, u32[]{:S(2)}) collective-permute-start(bf16[16,128,128]{2,1,0:T(8,128)(2,1)S(1)} %shard_map.63.refs_7_.refs_9_), channel_id=1, source_target_pairs={{0,8},{1,9},{2,10},{3,11},{4,12},{5,13},{6,14},{7,15},{8,0},{9,1},... | collective-permute-start | bytes 1572872 | tf_op jit(solution)/shard_map/ppermute | solution.py:366
  43.4 13.7 %collective-permute-start.16 = (bf16[16,128,128]{2,1,0:T(8,128)(2,1)S(1)}, bf16[16,128,128]{2,1,0:T(8,128)(2,1)S(1)}, u32[]{:S(2)}, u32[]{:S(2)}) collective-permute-start(bf16[16,128,128]{2,1,0:T(8,128)(2,1)S(1)} %shard_map.57.refs_3_.refs_0_.refs_5_), channel_id=1, source_target_pairs={{0,4},{1,5},{2,6},{3,7},{4,0},{5,1},{6,2},{7,3},{8,12},{9,13},{10,... | collective-permute-start | bytes 1572872 | tf_op jit(solution)/shard_map/ppermute | solution.py:366
  43.4 13.7 %collective-permute-start.15 = (bf16[16,128,128]{2,1,0:T(8,128)(2,1)S(1)}, bf16[16,128,128]{2,1,0:T(8,128)(2,1)S(1)}, u32[]{:S(2)}, u32[]{:S(2)}) collective-permute-start(bf16[16,128,128]{2,1,0:T(8,128)(2,1)S(1)} %shard_map.63.refs_7_.refs_9_), channel_id=1, source_target_pairs={{0,4},{1,5},{2,6},{3,7},{4,0},{5,1},{6,2},{7,3},{8,12},{9,13},{10,... | collective-permute-start | bytes 1572872 | tf_op jit(solution)/shard_map/ppermute | solution.py:366
  43.9 6.2 %collective-permute-start.3 = (bf16[17,16,128]{2,1,0:T(8,128)(2,1)S(1)}, bf16[17,16,128]{2,1,0:T(8,128)(2,1)S(1)}, u32[]{:S(2)}, u32[]{:S(2)}) collective-permute-start(bf16[17,16,128]{2,1,0:T(8,128)(2,1)S(1)} %get-tuple-element.21.refs_1_), channel_id=1, source_target_pairs={{0,3},{1,2},{2,1},{3,0},{4,7},{5,6},{6,5},{7,4},{8,11},{9,10},{10,... | collective-permute-start | bytes 208904 | tf_op jit(solution)/shard_map/ppermute | solution.py:366
  57.2 2.1 %collective-permute-start.18 = (bf16[16,128,128]{2,1,0:T(8,128)(2,1)S(1)}, bf16[16,128,128]{2,1,0:T(8,128)(2,1)S(1)}, u32[]{:S(2)}, u32[]{:S(2)}) collective-permute-start(bf16[16,128,128]{2,1,0:T(8,128)(2,1)S(1)} %collective-permute-done.13.refs_0_.refs_8_.refs_10_), channel_id=1, source_target_pairs={{0,4},{1,5},{2,6},{3,7},{4,0},{5,1},{6,2},{7,3},{8,12},{9,13},{10,... | collective-permute-start | bytes 1572872 | tf_op jit(solution)/shard_map/ppermute | solution.py:366
  57.2 2.6 %collective-permute-start.17 = (bf16[16,128,128]{2,1,0:T(8,128)(2,1)S(1)}, bf16[16,128,128]{2,1,0:T(8,128)(2,1)S(1)}, u32[]{:S(2)}, u32[]{:S(2)}) collective-permute-start(bf16[16,128,128]{2,1,0:T(8,128)(2,1)S(1)} %shard_map.65.refs_9_.refs_11_), channel_id=1, source_target_pairs={{0,4},{1,5},{2,6},{3,7},{4,0},{5,1},{6,2},{7,3},{8,12},{9,13},{10,... | collective-permute-start | bytes 1572872 | tf_op jit(solution)/shard_map/ppermute | solution.py:366
  57.8 8.3 %collective-permute-start.19 = (bf16[8,128,128]{2,1,0:T(8,128)(2,1)S(1)}, bf16[8,128,128]{2,1,0:T(8,128)(2,1)S(1)}, u32[]{:S(2)}, u32[]{:S(2)}) collective-permute-start(bf16[8,128,128]{2,1,0:T(8,128)(2,1)S(1)} %slice.8), channel_id=1, source_target_pairs={{0,8},{1,9},{2,10},{3,11},{4,12},{5,13},{6,14},{7,15},{8,0},{9,1},... | collective-permute-start | bytes 786440 | tf_op jit(solution)/shard_map/ppermute | solution.py:366
  58.8 8.0 %collective-permute-start.20 = (bf16[8,128,128]{2,1,0:T(8,128)(2,1)S(1)}, bf16[8,128,128]{2,1,0:T(8,128)(2,1)S(1)}, u32[]{:S(2)}, u32[]{:S(2)}) collective-permute-start(bf16[8,128,128]{2,1,0:T(8,128)(2,1)S(1)} %slice.9), channel_id=1, source_target_pairs={{0,1},{1,0},{2,3},{3,2},{4,5},{5,4},{6,7},{7,6},{8,9},{9,8},{10,11... | collective-permute-start | bytes 786440 | tf_op jit(solution)/shard_map/ppermute | solution.py:366
  66.1 1.5 %collective-permute-start.21 = (bf16[8,128,128]{2,1,0:T(8,128)(2,1)S(1)}, bf16[8,128,128]{2,1,0:T(8,128)(2,1)S(1)}, u32[]{:S(2)}, u32[]{:S(2)}) collective-permute-start(bf16[8,128,128]{2,1,0:T(8,128)(2,1)S(1)} %shard_map.67.refs_16_), channel_id=1, source_target_pairs={{0,4},{1,5},{2,6},{3,7},{4,0},{5,1},{6,2},{7,3},{8,12},{9,13},{10,... | collective-permute-start | bytes 786440 | tf_op jit(solution)/shard_map/ppermute | solution.py:366
  66.8 1.5 %collective-permute-start.22 = (bf16[8,128,128]{2,1,0:T(8,128)(2,1)S(1)}, bf16[8,128,128]{2,1,0:T(8,128)(2,1)S(1)}, u32[]{:S(2)}, u32[]{:S(2)}) collective-permute-start(bf16[8,128,128]{2,1,0:T(8,128)(2,1)S(1)} %shard_map.68.refs_17_), channel_id=1, source_target_pairs={{0,4},{1,5},{2,6},{3,7},{4,0},{5,1},{6,2},{7,3},{8,12},{9,13},{10,... | collective-permute-start | bytes 786440 | tf_op jit(solution)/shard_map/ppermute | solution.py:366
  77.9 14.1 %all-to-all-start = ((bf16[16,2,16,256]{3,2,1,0:T(8,128)(2,1)}), bf16[16,2,16,256]{3,2,1,0:T(8,128)(2,1)S(1)}, u32[]{:S(2)}, u32[]{:S(2)}) async-start(bf16[16,2,16,256]{3,2,1,0:T(8,128)(2,1)} %shard_map.69.refs_1_), calls=%async_computation | async-start | bytes 524288 | tf_op jit(solution)/shard_map/all_to_all | solution.py:448
  (2 other events, 30.4 us)

commit v23 on v21

--- a/solution.py
+++ b/solution.py
@@ -372,8 +372,7 @@
     near = after(near, over_own, go, *mates)
     over_near = after(send(near, 2, 0), rank=3)
     crossed = after(send(near, 0, 3, INNER), rank=1)
-    inner = after(inner, near)
-    outward = after(send(inner, 0, 1, INNER), rank=1)
+    outward = send(inner, 0, 1, INNER)
     stay, go = regroup(stay, send(go, 0, 1), 4, per_piece)
     mates += to_mate(near, over_own)
     two = pick(INNER, crossed, outward, over_near, go, *mates)

time: 85.2 us -> 88.4 us (1.038)
  waiting for transfers between devices: 43.8 us -> 49.2 us
  starting transfers between devices: 22.7 us -> 20.5 us
    ppermute x23, waiting for transfers between devices: 33.8 us -> 39.2 us  [send(): return lax.ppermute(buf, LANES, pairs)]
    ppermute x23, starting transfers between devices: 19.1 us -> 17 us  [send(): return lax.ppermute(buf, LANES, pairs)]
  transfers between devices with their start and end apart: 24 -> 24, of which waited for: 10 -> 14; matrix products, arithmetic and copies ran while one was open for 1% -> 1% of each run, Pallas kernels for 6% -> 6%
where the time goes in v23:
time: 88.4 us; the launch traced here: 88.1 us
  waiting for transfers between devices  49.2 us (56%)
  starting transfers between devices  20.5 us (23%)
  Pallas kernels  16 us (18%)
  local copies, waits for them, and re-layouts  1.61 us (2%)
    ppermute x23, waiting for transfers between devices, send(): return lax.ppermute(buf, LANES, pairs)  39.2 us
    ppermute x23, starting transfers between devices, send(): return lax.ppermute(buf, LANES, pairs)  17 us
    all_to_all x1, waiting for transfers between devices, gather_plan(): back = lax.all_to_all(done, LANES, split_axis=0, concat_axis=0, tiled=True)  10 us
    pallas_call x1, Pallas kernels, gather_plan(): pl.pallas_call(functools.partial(filter_kernel, early, later, late, n_col...  9.61 us
    pallas_call x1, Pallas kernels, gather_plan(): pl.pallas_call(functools.partial(first_kernel, early, later, n_col, n_row...  4.05 us
    all_to_all x1, starting transfers between devices, gather_plan(): back = lax.all_to_all(done, LANES, split_axis=0, concat_axis=0, tiled=True)  3.53 us
  transfers between devices with their start and end apart: 24, of which 14 were waited for; matrix products, arithmetic and copies ran while one was open for 1% of the time, Pallas kernels for 6%

profile of v23, /device:TPU:0, one launch (start us, length us, event | category | flops | bytes accessed | tf_op | source)
XLA Modules:
  0.0 88.1 jit_solution(2008345701456766816)
XLA Ops:
  0.6 3.0 %collective-permute-start.5 = (bf16[16,128,128]{2,1,0:T(8,128)(2,1)}, bf16[16,128,128]{2,1,0:T(8,128)(2,1)S(1)}, u32[]{:S(2)}, u32[]{:S(2)}) collective-permute-start(bf16[16,128,128]{2,1,0:T(8,128)(2,1)} %bitcast.2), channel_id=1, source_target_pairs={{0,8},{1,9},{2,10},{3,11},{4,12},{5,13},{6,14},{7,15},{8,0},{9,1},... | collective-permute-start | bytes 1572872 | tf_op jit(solution)/shard_map/ppermute | solution.py:348
  3.7 1.6 %collective-permute-start.4 = (bf16[16,128,128]{2,1,0:T(8,128)(2,1)}, bf16[16,128,128]{2,1,0:T(8,128)(2,1)S(1)}, u32[]{:S(2)}, u32[]{:S(2)}) collective-permute-start(bf16[16,128,128]{2,1,0:T(8,128)(2,1)} %bitcast.4), channel_id=1, source_target_pairs={{0,1},{1,0},{2,3},{3,2},{4,5},{5,4},{6,7},{7,6},{8,9},{9,8},{10,11... | collective-permute-start | bytes 1572872 | tf_op jit(solution)/shard_map/ppermute | solution.py:348
  6.6 0.9 %copy-done.1 = bf16[256,256]{1,0:T(8,128)(2,1)S(1)} copy-done((bf16[256,256]{1,0:T(8,128)(2,1)S(1)}, bf16[256,256]{1,0:T(8,128)(2,1)}, u32[]{:S(2)}) %copy-start.1) | copy-done | bytes 131096
  7.9 1.0 %collective-permute-done.came_ref = bf16[17,16,128]{2,1,0:T(8,128)(2,1)S(1)} collective-permute-done((bf16[17,16,128]{2,1,0:T(8,128)(2,1)S(1)}, bf16[17,16,128]{2,1,0:T(8,128)(2,1)S(1)}, u32[]{:S(2)}, u32[]{:S(2)}) %collective-permute-start) | collective-permute-done | bytes 69664 | tf_op jit(solution)/shard_map/ppermute | solution.py:348
  9.5 7.8 %collective-permute-done.1.came_ref = bf16[17,16,128]{2,1,0:T(8,128)(2,1)S(1)} collective-permute-done((bf16[17,16,128]{2,1,0:T(8,128)(2,1)S(1)}, bf16[17,16,128]{2,1,0:T(8,128)(2,1)S(1)}, u32[]{:S(2)}, u32[]{:S(2)}) %collective-permute-start.1) | collective-permute-done | bytes 69664 | tf_op jit(solution)/shard_map/ppermute | solution.py:348
  17.3 1.9 %collective-permute-start.2 = (bf16[17,16,128]{2,1,0:T(8,128)(2,1)S(1)}, bf16[17,16,128]{2,1,0:T(8,128)(2,1)S(1)}, u32[]{:S(2)}, u32[]{:S(2)}) collective-permute-start(bf16[17,16,128]{2,1,0:T(8,128)(2,1)S(1)} %get-tuple-element.19.refs_2_), channel_id=1, source_target_pairs={{0,1},{1,0},{2,3},{3,2},{4,5},{5,4},{6,7},{7,6},{8,9},{9,8},{10,11... | collective-permute-start | bytes 208904 | tf_op jit(solution)/shard_map/ppermute | solution.py:348
  19.2 0.8 collective-permute-start.10
  20.1 1.6 %collective-permute-start.7 = (bf16[16,128,128]{2,1,0:T(8,128)(2,1)S(1)}, bf16[16,128,128]{2,1,0:T(8,128)(2,1)S(1)}, u32[]{:S(2)}, u32[]{:S(2)}) collective-permute-start(bf16[16,128,128]{2,1,0:T(8,128)(2,1)S(1)} %shard_map.56.refs_1_.refs_3_), channel_id=1, source_target_pairs={{0,8},{1,9},{2,10},{3,11},{4,12},{5,13},{6,14},{7,15},{8,0},{9,1},... | collective-permute-start | bytes 1572872 | tf_op jit(solution)/shard_map/ppermute | solution.py:348
  21.7 1.3 %collective-permute-start.12 = (bf16[16,128,128]{2,1,0:T(8,128)(2,1)S(1)}, bf16[16,128,128]{2,1,0:T(8,128)(2,1)S(1)}, u32[]{:S(2)}, u32[]{:S(2)}) collective-permute-start(bf16[16,128,128]{2,1,0:T(8,128)(2,1)S(1)} %collective-permute-done.11.one_ref), channel_id=1, source_target_pairs={{1,0},{2,3},{5,4},{6,7},{9,8},{10,11},{13,12},{14,15},{17,16},{18,... | collective-permute-start | bytes 1572872 | tf_op jit(solution)/shard_map/ppermute | solution.py:348
  23.3 1.3 %collective-permute-start.14 = (bf16[16,128,128]{2,1,0:T(8,128)(2,1)S(1)}, bf16[16,128,128]{2,1,0:T(8,128)(2,1)S(1)}, u32[]{:S(2)}, u32[]{:S(2)}) collective-permute-start(bf16[16,128,128]{2,1,0:T(8,128)(2,1)S(1)} %shard_map.59.one_ref), channel_id=1, source_target_pairs={{1,0},{2,3},{5,4},{6,7},{9,8},{10,11},{13,12},{14,15},{17,16},{18,... | collective-permute-start | bytes 1572872 | tf_op jit(solution)/shard_map/ppermute | solution.py:348
  24.6 9.9 %collective-permute-done.7.refs_0_ = bf16[16,128,128]{2,1,0:T(8,128)(2,1)S(1)} collective-permute-done((bf16[16,128,128]{2,1,0:T(8,128)(2,1)S(1)}, bf16[16,128,128]{2,1,0:T(8,128)(2,1)S(1)}, u32[]{:S(2)}, u32[]{:S(2)}) %collective-permute-start.7) | collective-permute-done | bytes 524320 | tf_op jit(solution)/shard_map/ppermute | solution.py:348
  34.5 5.6 %collective-permute-done.12.other_ref = bf16[16,128,128]{2,1,0:T(8,128)(2,1)S(1)} collective-permute-done((bf16[16,128,128]{2,1,0:T(8,128)(2,1)S(1)}, bf16[16,128,128]{2,1,0:T(8,128)(2,1)S(1)}, u32[]{:S(2)}, u32[]{:S(2)}) %collective-permute-start.12) | collective-permute-done | bytes 524320 | tf_op jit(solution)/shard_map/ppermute | solution.py:348
  41.2 0.9 %collective-permute-start.3 = (bf16[17,16,128]{2,1,0:T(8,128)(2,1)S(1)}, bf16[17,16,128]{2,1,0:T(8,128)(2,1)S(1)}, u32[]{:S(2)}, u32[]{:S(2)}) collective-permute-start(bf16[17,16,128]{2,1,0:T(8,128)(2,1)S(1)} %get-tuple-element.21.refs_1_), channel_id=1, source_target_pairs={{0,3},{1,2},{2,1},{3,0},{4,7},{5,6},{6,5},{7,4},{8,11},{9,10},{10,... | collective-permute-start | bytes 208904 | tf_op jit(solution)/shard_map/ppermute | solution.py:348
  42.1 5.3 %collective-permute-done.3.came_ref = bf16[17,16,128]{2,1,0:T(8,128)(2,1)S(1)} collective-permute-done((bf16[17,16,128]{2,1,0:T(8,128)(2,1)S(1)}, bf16[17,16,128]{2,1,0:T(8,128)(2,1)S(1)}, u32[]{:S(2)}, u32[]{:S(2)}) %collective-permute-start.3) | collective-permute-done | bytes 69664 | tf_op jit(solution)/shard_map/ppermute | solution.py:348
  47.4 1.2 %shard_map.58.refs_2_.sta_ref.refs_0_ = bf16[7,16,128,128]{3,2,1,0:T(8,128)(2,1)S(1)} custom-call(bf16[16,128,128]{2,1,0:T(8,128)(2,1)S(1)} %bitcast.6, bf16[16,128,128]{2,1,0:T(8,128)(2,1)S(1)} %shard_map.56.refs_1_.refs_3_, bf16[16,128,128]{2,1,0:T(8,128)(2,1)S(1)} %shard_map.55.refs_1_.refs_2_.refs_4_, ...), custom_call_target="tpu_custom_call" | custom-call | bytes 11010048 | tf_op jit(solution)/shard_map/pallas_call | solution.py:260
  48.5 3.8 %collective-permute-done.14.refs_0_ = bf16[16,128,128]{2,1,0:T(8,128)(2,1)S(1)} collective-permute-done((bf16[16,128,128]{2,1,0:T(8,128)(2,1)S(1)}, bf16[16,128,128]{2,1,0:T(8,128)(2,1)S(1)}, u32[]{:S(2)}, u32[]{:S(2)}) %collective-permute-start.14) | collective-permute-done | bytes 524320 | tf_op jit(solution)/shard_map/ppermute | solution.py:348
  52.3 0.9 %collective-permute-done.13.refs_0_.refs_8_.refs_10_ = bf16[16,128,128]{2,1,0:T(8,128)(2,1)S(1)} collective-permute-done((bf16[16,128,128]{2,1,0:T(8,128)(2,1)S(1)}, bf16[16,128,128]{2,1,0:T(8,128)(2,1)S(1)}, u32[]{:S(2)}, u32[]{:S(2)}) %collective-permute-start.13) | collective-permute-done | bytes 524320 | tf_op jit(solution)/shard_map/ppermute | solution.py:348
  55.9 4.0 %shard_map.63 = (bf16[7,16,128,128]{3,2,1,0:T(8,128)(2,1)S(1)}, f32[32,16,128]{2,1,0:T(8,128)S(1)}) custom-call(s32[16,128]{1,0:T(8,128)S(1)} %get-tuple-element.22.ids_ref.refs_0_, bf16[32,16,128]{2,1,0:T(8,128)(2,1)S(1)} %get-tuple-element.23.refs_1_.parts_ref, bf16[7,16,128,128]{3,2,1,0:T(8,128)(2,1)S(1)} %shard_map.58.refs_2_.sta_ref.refs_0_, ...), custom_call_target="tpu_custom_call" | custom-call | flops 234881024 | bytes 11010048 | tf_op jit(solution)/shard_map/pallas_call | solution.py:396
  59.9 2.2 %collective-permute-done.19.refs_0_ = bf16[8,128,128]{2,1,0:T(8,128)(2,1)S(1)} collective-permute-done((bf16[8,128,128]{2,1,0:T(8,128)(2,1)S(1)}, bf16[8,128,128]{2,1,0:T(8,128)(2,1)S(1)}, u32[]{:S(2)}, u32[]{:S(2)}) %collective-permute-start.19) | collective-permute-done | bytes 262176 | tf_op jit(solution)/shard_map/ppermute | solution.py:348
  62.7 1.0 %collective-permute-done.21.refs_18_ = bf16[8,128,128]{2,1,0:T(8,128)(2,1)S(1)} collective-permute-done((bf16[8,128,128]{2,1,0:T(8,128)(2,1)S(1)}, bf16[8,128,128]{2,1,0:T(8,128)(2,1)S(1)}, u32[]{:S(2)}, u32[]{:S(2)}) %collective-permute-start.21) | collective-permute-done | bytes 262176 | tf_op jit(solution)/shard_map/ppermute | solution.py:348
  64.1 9.6 %shard_map.66.refs_1_ = bf16[16,2,16,256]{3,2,1,0:T(8,128)(2,1)} custom-call(s32[16,128]{1,0:T(8,128)S(1)} %get-tuple-element.22.ids_ref.refs_0_, bf16[32,16,128]{2,1,0:T(8,128)(2,1)S(1)} %get-tuple-element.23.refs_1_.parts_ref, f32[32,16,128]{2,1,0:T(8,128)S(1)} %get-tuple-element.24.sum_ref, ...), custom_call_target="tpu_custom_call" | custom-call | tf_op jit(solution)/shard_map/pallas_call | solution.py:416
  73.7 3.5 %all-to-all-start = ((bf16[16,2,16,256]{3,2,1,0:T(8,128)(2,1)}), bf16[16,2,16,256]{3,2,1,0:T(8,128)(2,1)S(1)}, u32[]{:S(2)}, u32[]{:S(2)}) async-start(bf16[16,2,16,256]{3,2,1,0:T(8,128)(2,1)} %shard_map.66.refs_1_), calls=%async_computation | async-start | bytes 524288 | tf_op jit(solution)/shard_map/all_to_all | solution.py:428
  77.2 10.0 %all-to-all-done.back_ref = bf16[16,2,16,256]{3,2,1,0:T(8,128)(2,1)S(1)} async-done(((bf16[16,2,16,256]{3,2,1,0:T(8,128)(2,1)}), bf16[16,2,16,256]{3,2,1,0:T(8,128)(2,1)S(1)}, u32[]{:S(2)}, u32[]{:S(2)}) %all-to-all-start) | async-done | bytes 262176 | tf_op jit(solution)/shard_map/all_to_all | solution.py:428
  87.2 0.9 %shard_map.68 = (f32[256,256]{1,0:T(8,128)}, f32[256,256]{1,0:T(8,128)}) custom-call(bf16[16,2,16,256]{3,2,1,0:T(8,128)(2,1)S(1)} %all-to-all-done.back_ref, s32[16,128]{1,0:T(8,128)S(1)} %shard_map.67.marker_ref), custom_call_target="tpu_custom_call" | custom-call | tf_op jit(solution)/shard_map/pallas_call | solution.py:430
  (51 shorter events, 7.4 us)
Async XLA Ops:
  0.6 18.5 %collective-permute-start.5 = (bf16[16,128,128]{2,1,0:T(8,128)(2,1)}, bf16[16,128,128]{2,1,0:T(8,128)(2,1)S(1)}, u32[]{:S(2)}, u32[]{:S(2)}) collective-permute-start(bf16[16,128,128]{2,1,0:T(8,128)(2,1)} %bitcast.2), channel_id=1, source_target_pairs={{0,8},{1,9},{2,10},{3,11},{4,12},{5,13},{6,14},{7,15},{8,0},{9,1},... | collective-permute-start | bytes 1572872 | tf_op jit(solution)/shard_map/ppermute | solution.py:348
  3.7 15.5 %collective-permute-start.6 = (bf16[16,128,128]{2,1,0:T(8,128)(2,1)}, bf16[16,128,128]{2,1,0:T(8,128)(2,1)S(1)}, u32[]{:S(2)}, u32[]{:S(2)}) collective-permute-start(bf16[16,128,128]{2,1,0:T(8,128)(2,1)} %bitcast.3), channel_id=1, source_target_pairs={{0,4},{1,5},{2,6},{3,7},{4,0},{5,1},{6,2},{7,3},{8,12},{9,13},{10,... | collective-permute-start | bytes 1572872 | tf_op jit(solution)/shard_map/ppermute | solution.py:348
  3.7 15.5 %collective-permute-start.4 = (bf16[16,128,128]{2,1,0:T(8,128)(2,1)}, bf16[16,128,128]{2,1,0:T(8,128)(2,1)S(1)}, u32[]{:S(2)}, u32[]{:S(2)}) collective-permute-start(bf16[16,128,128]{2,1,0:T(8,128)(2,1)} %bitcast.4), channel_id=1, source_target_pairs={{0,1},{1,0},{2,3},{3,2},{4,5},{5,4},{6,7},{7,6},{8,9},{9,8},{10,11... | collective-permute-start | bytes 1572872 | tf_op jit(solution)/shard_map/ppermute | solution.py:348
  5.2 16.5 %collective-permute-start.11 = (bf16[16,128,128]{2,1,0:T(8,128)(2,1)}, bf16[16,128,128]{2,1,0:T(8,128)(2,1)S(1)}, u32[]{:S(2)}, u32[]{:S(2)}) collective-permute-start(bf16[16,128,128]{2,1,0:T(8,128)(2,1)} %bitcast.5), channel_id=1, source_target_pairs={{1,2},{2,1},{5,6},{6,5},{9,10},{10,9},{13,14},{14,13},{17,18},{18,... | collective-permute-start | bytes 1572872 | tf_op jit(solution)/shard_map/ppermute | solution.py:348
  7.6 1.3 %collective-permute-start = (bf16[17,16,128]{2,1,0:T(8,128)(2,1)S(1)}, bf16[17,16,128]{2,1,0:T(8,128)(2,1)S(1)}, u32[]{:S(2)}, u32[]{:S(2)}) collective-permute-start(bf16[17,16,128]{2,1,0:T(8,128)(2,1)S(1)} %get-tuple-element.15), channel_id=1, source_target_pairs={{0,4},{1,5},{2,6},{3,7},{4,0},{5,1},{6,2},{7,3},{8,12},{9,13},{10,... | collective-permute-start | bytes 208904 | tf_op jit(solution)/shard_map/ppermute | solution.py:348
  9.0 8.3 %collective-permute-start.1 = (bf16[17,16,128]{2,1,0:T(8,128)(2,1)S(1)}, bf16[17,16,128]{2,1,0:T(8,128)(2,1)S(1)}, u32[]{:S(2)}, u32[]{:S(2)}) collective-permute-start(bf16[17,16,128]{2,1,0:T(8,128)(2,1)S(1)} %get-tuple-element.17), channel_id=1, source_target_pairs={{0,8},{1,9},{2,10},{3,11},{4,12},{5,13},{6,14},{7,15},{8,0},{9,1},... | collective-permute-start | bytes 208904 | tf_op jit(solution)/shard_map/ppermute | solution.py:348
  17.3 5.7 %collective-permute-start.2 = (bf16[17,16,128]{2,1,0:T(8,128)(2,1)S(1)}, bf16[17,16,128]{2,1,0:T(8,128)(2,1)S(1)}, u32[]{:S(2)}, u32[]{:S(2)}) collective-permute-start(bf16[17,16,128]{2,1,0:T(8,128)(2,1)S(1)} %get-tuple-element.19.refs_2_), channel_id=1, source_target_pairs={{0,1},{1,0},{2,3},{3,2},{4,5},{5,4},{6,7},{7,6},{8,9},{9,8},{10,11... | collective-permute-start | bytes 208904 | tf_op jit(solution)/shard_map/ppermute | solution.py:348
  19.2 4.0 %collective-permute-start.10 = (bf16[16,128,128]{2,1,0:T(8,128)(2,1)S(1)}, bf16[16,128,128]{2,1,0:T(8,128)(2,1)S(1)}, u32[]{:S(2)}, u32[]{:S(2)}) collective-permute-start(bf16[16,128,128]{2,1,0:T(8,128)(2,1)S(1)} %shard_map.56.refs_1_.refs_3_), channel_id=1, source_target_pairs={{1,2},{2,1},{5,6},{6,5},{9,10},{10,9},{13,14},{14,13},{17,18},{18,... | collective-permute-start | bytes 1572872 | tf_op jit(solution)/shard_map/ppermute | solution.py:348
  20.0 20.0 %collective-permute-start.9 = (bf16[16,128,128]{2,1,0:T(8,128)(2,1)S(1)}, bf16[16,128,128]{2,1,0:T(8,128)(2,1)S(1)}, u32[]{:S(2)}, u32[]{:S(2)}) collective-permute-start(bf16[16,128,128]{2,1,0:T(8,128)(2,1)S(1)} %shard_map.55.refs_1_.refs_2_.refs_4_), channel_id=1, source_target_pairs={{0,4},{1,5},{2,6},{3,7},{4,0},{5,1},{6,2},{7,3},{8,12},{9,13},{10,... | collective-permute-start | bytes 1572872 | tf_op jit(solution)/shard_map/ppermute | solution.py:348
  20.1 14.3 %collective-permute-start.7 = (bf16[16,128,128]{2,1,0:T(8,128)(2,1)S(1)}, bf16[16,128,128]{2,1,0:T(8,128)(2,1)S(1)}, u32[]{:S(2)}, u32[]{:S(2)}) collective-permute-start(bf16[16,128,128]{2,1,0:T(8,128)(2,1)S(1)} %shard_map.56.refs_1_.refs_3_), channel_id=1, source_target_pairs={{0,8},{1,9},{2,10},{3,11},{4,12},{5,13},{6,14},{7,15},{8,0},{9,1},... | collective-permute-start | bytes 1572872 | tf_op jit(solution)/shard_map/ppermute | solution.py:348
  21.7 18.3 %collective-permute-start.12 = (bf16[16,128,128]{2,1,0:T(8,128)(2,1)S(1)}, bf16[16,128,128]{2,1,0:T(8,128)(2,1)S(1)}, u32[]{:S(2)}, u32[]{:S(2)}) collective-permute-start(bf16[16,128,128]{2,1,0:T(8,128)(2,1)S(1)} %collective-permute-done.11.one_ref), channel_id=1, source_target_pairs={{1,0},{2,3},{5,4},{6,7},{9,8},{10,11},{13,12},{14,15},{17,16},{18,... | collective-permute-start | bytes 1572872 | tf_op jit(solution)/shard_map/ppermute | solution.py:348
  23.0 17.0 %collective-permute-start.8 = (bf16[16,128,128]{2,1,0:T(8,128)(2,1)S(1)}, bf16[16,128,128]{2,1,0:T(8,128)(2,1)S(1)}, u32[]{:S(2)}, u32[]{:S(2)}) collective-permute-start(bf16[16,128,128]{2,1,0:T(8,128)(2,1)S(1)} %shard_map.56.refs_1_.refs_3_), channel_id=1, source_target_pairs={{0,4},{1,5},{2,6},{3,7},{4,0},{5,1},{6,2},{7,3},{8,12},{9,13},{10,... | collective-permute-start | bytes 1572872 | tf_op jit(solution)/shard_map/ppermute | solution.py:348
  23.3 29.0 %collective-permute-start.14 = (bf16[16,128,128]{2,1,0:T(8,128)(2,1)S(1)}, bf16[16,128,128]{2,1,0:T(8,128)(2,1)S(1)}, u32[]{:S(2)}, u32[]{:S(2)}) collective-permute-start(bf16[16,128,128]{2,1,0:T(8,128)(2,1)S(1)} %shard_map.59.one_ref), channel_id=1, source_target_pairs={{1,0},{2,3},{5,4},{6,7},{9,8},{10,11},{13,12},{14,15},{17,16},{18,... | collective-permute-start | bytes 1572872 | tf_op jit(solution)/shard_map/ppermute | solution.py:348
  40.1 13.1 %collective-permute-start.13 = (bf16[16,128,128]{2,1,0:T(8,128)(2,1)S(1)}, bf16[16,128,128]{2,1,0:T(8,128)(2,1)S(1)}, u32[]{:S(2)}, u32[]{:S(2)}) collective-permute-start(bf16[16,128,128]{2,1,0:T(8,128)(2,1)S(1)} %shard_map.60.refs_7_.refs_9_), channel_id=1, source_target_pairs={{0,8},{1,9},{2,10},{3,11},{4,12},{5,13},{6,14},{7,15},{8,0},{9,1},... | collective-permute-start | bytes 1572872 | tf_op jit(solution)/shard_map/ppermute | solution.py:348
  40.7 12.5 %collective-permute-start.15 = (bf16[16,128,128]{2,1,0:T(8,128)(2,1)S(1)}, bf16[16,128,128]{2,1,0:T(8,128)(2,1)S(1)}, u32[]{:S(2)}, u32[]{:S(2)}) collective-permute-start(bf16[16,128,128]{2,1,0:T(8,128)(2,1)S(1)} %shard_map.60.refs_7_.refs_9_), channel_id=1, source_target_pairs={{0,4},{1,5},{2,6},{3,7},{4,0},{5,1},{6,2},{7,3},{8,12},{9,13},{10,... | collective-permute-start | bytes 1572872 | tf_op jit(solution)/shard_map/ppermute | solution.py:348
  40.7 12.5 %collective-permute-start.16 = (bf16[16,128,128]{2,1,0:T(8,128)(2,1)S(1)}, bf16[16,128,128]{2,1,0:T(8,128)(2,1)S(1)}, u32[]{:S(2)}, u32[]{:S(2)}) collective-permute-start(bf16[16,128,128]{2,1,0:T(8,128)(2,1)S(1)} %shard_map.57.refs_3_.refs_0_.refs_5_), channel_id=1, source_target_pairs={{0,4},{1,5},{2,6},{3,7},{4,0},{5,1},{6,2},{7,3},{8,12},{9,13},{10,... | collective-permute-start | bytes 1572872 | tf_op jit(solution)/shard_map/ppermute | solution.py:348
  41.2 6.2 %collective-permute-start.3 = (bf16[17,16,128]{2,1,0:T(8,128)(2,1)S(1)}, bf16[17,16,128]{2,1,0:T(8,128)(2,1)S(1)}, u32[]{:S(2)}, u32[]{:S(2)}) collective-permute-start(bf16[17,16,128]{2,1,0:T(8,128)(2,1)S(1)} %get-tuple-element.21.refs_1_), channel_id=1, source_target_pairs={{0,3},{1,2},{2,1},{3,0},{4,7},{5,6},{6,5},{7,4},{8,11},{9,10},{10,... | collective-permute-start | bytes 208904 | tf_op jit(solution)/shard_map/ppermute | solution.py:348
  53.2 1.9 %collective-permute-start.18 = (bf16[16,128,128]{2,1,0:T(8,128)(2,1)S(1)}, bf16[16,128,128]{2,1,0:T(8,128)(2,1)S(1)}, u32[]{:S(2)}, u32[]{:S(2)}) collective-permute-start(bf16[16,128,128]{2,1,0:T(8,128)(2,1)S(1)} %collective-permute-done.13.refs_0_.refs_8_.refs_10_), channel_id=1, source_target_pairs={{0,4},{1,5},{2,6},{3,7},{4,0},{5,1},{6,2},{7,3},{8,12},{9,13},{10,... | collective-permute-start | bytes 1572872 | tf_op jit(solution)/shard_map/ppermute | solution.py:348
  53.3 2.6 %collective-permute-start.17 = (bf16[16,128,128]{2,1,0:T(8,128)(2,1)S(1)}, bf16[16,128,128]{2,1,0:T(8,128)(2,1)S(1)}, u32[]{:S(2)}, u32[]{:S(2)}) collective-permute-start(bf16[16,128,128]{2,1,0:T(8,128)(2,1)S(1)} %shard_map.62.refs_9_.refs_11_), channel_id=1, source_target_pairs={{0,4},{1,5},{2,6},{3,7},{4,0},{5,1},{6,2},{7,3},{8,12},{9,13},{10,... | collective-permute-start | bytes 1572872 | tf_op jit(solution)/shard_map/ppermute | solution.py:348
  53.9 8.3 %collective-permute-start.19 = (bf16[8,128,128]{2,1,0:T(8,128)(2,1)S(1)}, bf16[8,128,128]{2,1,0:T(8,128)(2,1)S(1)}, u32[]{:S(2)}, u32[]{:S(2)}) collective-permute-start(bf16[8,128,128]{2,1,0:T(8,128)(2,1)S(1)} %slice.8), channel_id=1, source_target_pairs={{0,8},{1,9},{2,10},{3,11},{4,12},{5,13},{6,14},{7,15},{8,0},{9,1},... | collective-permute-start | bytes 786440 | tf_op jit(solution)/shard_map/ppermute | solution.py:348
  54.5 8.0 %collective-permute-start.20 = (bf16[8,128,128]{2,1,0:T(8,128)(2,1)S(1)}, bf16[8,128,128]{2,1,0:T(8,128)(2,1)S(1)}, u32[]{:S(2)}, u32[]{:S(2)}) collective-permute-start(bf16[8,128,128]{2,1,0:T(8,128)(2,1)S(1)} %slice.9), channel_id=1, source_target_pairs={{0,1},{1,0},{2,3},{3,2},{4,5},{5,4},{6,7},{7,6},{8,9},{9,8},{10,11... | collective-permute-start | bytes 786440 | tf_op jit(solution)/shard_map/ppermute | solution.py:348
  62.2 1.5 %collective-permute-start.21 = (bf16[8,128,128]{2,1,0:T(8,128)(2,1)S(1)}, bf16[8,128,128]{2,1,0:T(8,128)(2,1)S(1)}, u32[]{:S(2)}, u32[]{:S(2)}) collective-permute-start(bf16[8,128,128]{2,1,0:T(8,128)(2,1)S(1)} %shard_map.64.refs_16_), channel_id=1, source_target_pairs={{0,4},{1,5},{2,6},{3,7},{4,0},{5,1},{6,2},{7,3},{8,12},{9,13},{10,... | collective-permute-start | bytes 786440 | tf_op jit(solution)/shard_map/ppermute | solution.py:348
  62.5 1.6 %collective-permute-start.22 = (bf16[8,128,128]{2,1,0:T(8,128)(2,1)S(1)}, bf16[8,128,128]{2,1,0:T(8,128)(2,1)S(1)}, u32[]{:S(2)}, u32[]{:S(2)}) collective-permute-start(bf16[8,128,128]{2,1,0:T(8,128)(2,1)S(1)} %shard_map.65.refs_17_), channel_id=1, source_target_pairs={{0,4},{1,5},{2,6},{3,7},{4,0},{5,1},{6,2},{7,3},{8,12},{9,13},{10,... | collective-permute-start | bytes 786440 | tf_op jit(solution)/shard_map/ppermute | solution.py:348
  73.7 13.6 %all-to-all-start = ((bf16[16,2,16,256]{3,2,1,0:T(8,128)(2,1)}), bf16[16,2,16,256]{3,2,1,0:T(8,128)(2,1)S(1)}, u32[]{:S(2)}, u32[]{:S(2)}) async-start(bf16[16,2,16,256]{3,2,1,0:T(8,128)(2,1)} %shard_map.66.refs_1_), calls=%async_computation | async-start | bytes 524288 | tf_op jit(solution)/shard_map/all_to_all | solution.py:428
  (2 other events, 29.1 us)

commit v24 on v22

--- a/solution.py
+++ b/solution.py
@@ -391,8 +391,7 @@
     over_near = after(send(near, 2, 0), rank=3)
     mates += to_mate(near)
     crossed = after(send(copy_after(near, mates[1]), 0, 3, INNER), rank=1)
-    inner = after(inner, near)
-    outward = after(send(inner, 0, 1, INNER), rank=1)
+    outward = send(inner, 0, 1, INNER)
     stay, go = regroup(stay, send(go, 0, 1), 4, per_piece)
     mates += to_mate(over_own)
     two = pick(INNER, crossed, outward, over_near, go, *mates)

time: 93.2 us -> 103 us (1.11)
  waiting for transfers between devices: 41.8 us -> 46.8 us
  starting transfers between devices: 32.6 us -> 37.1 us
    ppermute x23, waiting for transfers between devices: 31.7 us -> 36.8 us  [send(): return lax.ppermute(buf, LANES, pairs)]
    ppermute x23, starting transfers between devices: 28.6 us -> 32.8 us  [send(): return lax.ppermute(buf, LANES, pairs)]
  transfers between devices with their start and end apart: 24 -> 24, of which waited for: 12 -> 12; matrix products, arithmetic and copies ran while one was open for 1% -> 1% of each run, Pallas kernels for 6% -> 5%
where the time goes in v24:
time: 103 us; the launch traced here: 102 us
  waiting for transfers between devices  46.8 us (45%)
  starting transfers between devices  37.1 us (36%)
  Pallas kernels  16 us (16%)
  local copies, waits for them, and re-layouts  1.61 us (2%)
    ppermute x23, waiting for transfers between devices, send(): return lax.ppermute(buf, LANES, pairs)  36.8 us
    ppermute x23, starting transfers between devices, send(): return lax.ppermute(buf, LANES, pairs)  32.8 us
    all_to_all x1, waiting for transfers between devices, gather_plan(): back = lax.all_to_all(done, LANES, split_axis=0, concat_axis=0, tiled=True)  10.1 us
    pallas_call x1, Pallas kernels, gather_plan(): pl.pallas_call(functools.partial(filter_kernel, early, later, late, n_col...  9.59 us
    all_to_all x1, starting transfers between devices, gather_plan(): back = lax.all_to_all(done, LANES, split_axis=0, concat_axis=0, tiled=True)  4.39 us
    pallas_call x1, Pallas kernels, gather_plan(): pl.pallas_call(functools.partial(first_kernel, early, later, n_col, n_row...  4.04 us
  transfers between devices with their start and end apart: 24, of which 12 were waited for; matrix products, arithmetic and copies ran while one was open for 1% of the time, Pallas kernels for 5%

profile of v24, /device:TPU:0, one launch (start us, length us, event | category | flops | bytes accessed | tf_op | source)
XLA Modules:
  0.0 102.5 jit_solution(9783302854841753994)
XLA Ops:
  0.6 3.0 %collective-permute-start.5 = (bf16[16,128,128]{2,1,0:T(8,128)(2,1)}, bf16[16,128,128]{2,1,0:T(8,128)(2,1)S(1)}, u32[]{:S(2)}, u32[]{:S(2)}) collective-permute-start(bf16[16,128,128]{2,1,0:T(8,128)(2,1)} %bitcast.2), channel_id=1, source_target_pairs={{0,8},{1,9},{2,10},{3,11},{4,12},{5,13},{6,14},{7,15},{8,0},{9,1},... | collective-permute-start | bytes 1572872 | tf_op jit(solution)/shard_map/ppermute | solution.py:366
  3.7 1.6 %collective-permute-start.4 = (bf16[16,128,128]{2,1,0:T(8,128)(2,1)}, bf16[16,128,128]{2,1,0:T(8,128)(2,1)S(1)}, u32[]{:S(2)}, u32[]{:S(2)}) collective-permute-start(bf16[16,128,128]{2,1,0:T(8,128)(2,1)} %bitcast.4), channel_id=1, source_target_pairs={{0,1},{1,0},{2,3},{3,2},{4,5},{5,4},{6,7},{7,6},{8,9},{9,8},{10,11... | collective-permute-start | bytes 1572872 | tf_op jit(solution)/shard_map/ppermute | solution.py:366
  5.9 0.9 copy-done.1
  7.2 1.0 %collective-permute-done.came_ref = bf16[17,16,128]{2,1,0:T(8,128)(2,1)S(1)} collective-permute-done((bf16[17,16,128]{2,1,0:T(8,128)(2,1)S(1)}, bf16[17,16,128]{2,1,0:T(8,128)(2,1)S(1)}, u32[]{:S(2)}, u32[]{:S(2)}) %collective-permute-start) | collective-permute-done | bytes 69664 | tf_op jit(solution)/shard_map/ppermute | solution.py:366
  8.8 8.4 %collective-permute-done.1.came_ref = bf16[17,16,128]{2,1,0:T(8,128)(2,1)S(1)} collective-permute-done((bf16[17,16,128]{2,1,0:T(8,128)(2,1)S(1)}, bf16[17,16,128]{2,1,0:T(8,128)(2,1)S(1)}, u32[]{:S(2)}, u32[]{:S(2)}) %collective-permute-start.1) | collective-permute-done | bytes 69664 | tf_op jit(solution)/shard_map/ppermute | solution.py:366
  17.3 0.9 collective-permute-done.4.refs_0_
  18.2 0.8 collective-permute-start.11
  19.0 1.0 %collective-permute-start.7 = (bf16[16,128,128]{2,1,0:T(8,128)(2,1)S(1)}, bf16[16,128,128]{2,1,0:T(8,128)(2,1)S(1)}, u32[]{:S(2)}, u32[]{:S(2)}) collective-permute-start(bf16[16,128,128]{2,1,0:T(8,128)(2,1)S(1)} %shard_map.56.refs_1_.value_ref.refs_3_), channel_id=1, source_target_pairs={{0,8},{1,9},{2,10},{3,11},{4,12},{5,13},{6,14},{7,15},{8,0},{9,1},... | collective-permute-start | bytes 1572872 | tf_op jit(solution)/shard_map/ppermute | solution.py:366
  20.9 1.3 %collective-permute-start.12 = (bf16[16,128,128]{2,1,0:T(8,128)(2,1)S(1)}, bf16[16,128,128]{2,1,0:T(8,128)(2,1)S(1)}, u32[]{:S(2)}, u32[]{:S(2)}) collective-permute-start(bf16[16,128,128]{2,1,0:T(8,128)(2,1)S(1)} %collective-permute-done.11.one_ref), channel_id=1, source_target_pairs={{1,0},{2,3},{5,4},{6,7},{9,8},{10,11},{13,12},{14,15},{17,16},{18,... | collective-permute-start | bytes 1572872 | tf_op jit(solution)/shard_map/ppermute | solution.py:366
  22.4 15.8 %collective-permute-start.2 = (bf16[17,16,128]{2,1,0:T(8,128)(2,1)S(1)}, bf16[17,16,128]{2,1,0:T(8,128)(2,1)S(1)}, u32[]{:S(2)}, u32[]{:S(2)}) collective-permute-start(bf16[17,16,128]{2,1,0:T(8,128)(2,1)S(1)} %get-tuple-element.19.refs_2_), channel_id=1, source_target_pairs={{0,1},{1,0},{2,3},{3,2},{4,5},{5,4},{6,7},{7,6},{8,9},{9,8},{10,11... | collective-permute-start | bytes 208904 | tf_op jit(solution)/shard_map/ppermute | solution.py:366
  38.2 12.4 %collective-permute-done.2.came_ref = bf16[17,16,128]{2,1,0:T(8,128)(2,1)S(1)} collective-permute-done((bf16[17,16,128]{2,1,0:T(8,128)(2,1)S(1)}, bf16[17,16,128]{2,1,0:T(8,128)(2,1)S(1)}, u32[]{:S(2)}, u32[]{:S(2)}) %collective-permute-start.2) | collective-permute-done | bytes 69664 | tf_op jit(solution)/shard_map/ppermute | solution.py:366
  50.7 1.3 %collective-permute-start.14 = (bf16[16,128,128]{2,1,0:T(8,128)(2,1)S(1)}, bf16[16,128,128]{2,1,0:T(8,128)(2,1)S(1)}, u32[]{:S(2)}, u32[]{:S(2)}) collective-permute-start(bf16[16,128,128]{2,1,0:T(8,128)(2,1)S(1)} %shard_map.60.one_ref), channel_id=1, source_target_pairs={{1,0},{2,3},{5,4},{6,7},{9,8},{10,11},{13,12},{14,15},{17,16},{18,... | collective-permute-start | bytes 1572872 | tf_op jit(solution)/shard_map/ppermute | solution.py:366
  52.1 1.0 collective-permute-start.13
  53.6 2.5 %collective-permute-start.3 = (bf16[17,16,128]{2,1,0:T(8,128)(2,1)S(1)}, bf16[17,16,128]{2,1,0:T(8,128)(2,1)S(1)}, u32[]{:S(2)}, u32[]{:S(2)}) collective-permute-start(bf16[17,16,128]{2,1,0:T(8,128)(2,1)S(1)} %get-tuple-element.21.refs_1_), channel_id=1, source_target_pairs={{0,3},{1,2},{2,1},{3,0},{4,7},{5,6},{6,5},{7,4},{8,11},{9,10},{10,... | collective-permute-start | bytes 208904 | tf_op jit(solution)/shard_map/ppermute | solution.py:366
  56.1 3.7 %collective-permute-done.3.came_ref = bf16[17,16,128]{2,1,0:T(8,128)(2,1)S(1)} collective-permute-done((bf16[17,16,128]{2,1,0:T(8,128)(2,1)S(1)}, bf16[17,16,128]{2,1,0:T(8,128)(2,1)S(1)}, u32[]{:S(2)}, u32[]{:S(2)}) %collective-permute-start.3) | collective-permute-done | bytes 69664 | tf_op jit(solution)/shard_map/ppermute | solution.py:366
  59.8 1.2 %shard_map.58.refs_2_.sta_ref.refs_0_ = bf16[7,16,128,128]{3,2,1,0:T(8,128)(2,1)S(1)} custom-call(bf16[16,128,128]{2,1,0:T(8,128)(2,1)S(1)} %bitcast.6, bf16[16,128,128]{2,1,0:T(8,128)(2,1)S(1)} %shard_map.56.refs_1_.value_ref.refs_3_, bf16[16,128,128]{2,1,0:T(8,128)(2,1)S(1)} %shard_map.55.refs_1_.refs_2_.refs_4_, ...), custom_call_target="tpu_custom_call" | custom-call | bytes 11010048 | tf_op jit(solution)/shard_map/pallas_call | solution.py:278
  61.0 5.3 %collective-permute-done.14.refs_0_ = bf16[16,128,128]{2,1,0:T(8,128)(2,1)S(1)} collective-permute-done((bf16[16,128,128]{2,1,0:T(8,128)(2,1)S(1)}, bf16[16,128,128]{2,1,0:T(8,128)(2,1)S(1)}, u32[]{:S(2)}, u32[]{:S(2)}) %collective-permute-start.14) | collective-permute-done | bytes 524320 | tf_op jit(solution)/shard_map/ppermute | solution.py:366
  66.9 1.0 collective-permute-start.19
  68.9 4.0 %shard_map.64 = (bf16[7,16,128,128]{3,2,1,0:T(8,128)(2,1)S(1)}, f32[32,16,128]{2,1,0:T(8,128)S(1)}) custom-call(s32[16,128]{1,0:T(8,128)S(1)} %get-tuple-element.22.ids_ref.refs_0_, bf16[32,16,128]{2,1,0:T(8,128)(2,1)S(1)} %get-tuple-element.23.refs_1_.parts_ref, bf16[7,16,128,128]{3,2,1,0:T(8,128)(2,1)S(1)} %shard_map.58.refs_2_.sta_ref.refs_0_, ...), custom_call_target="tpu_custom_call" | custom-call | flops 234881024 | bytes 11010048 | tf_op jit(solution)/shard_map/pallas_call | solution.py:415
  73.0 2.3 %collective-permute-done.19.refs_0_ = bf16[8,128,128]{2,1,0:T(8,128)(2,1)S(1)} collective-permute-done((bf16[8,128,128]{2,1,0:T(8,128)(2,1)S(1)}, bf16[8,128,128]{2,1,0:T(8,128)(2,1)S(1)}, u32[]{:S(2)}, u32[]{:S(2)}) %collective-permute-start.19) | collective-permute-done | bytes 262176 | tf_op jit(solution)/shard_map/ppermute | solution.py:366
  77.5 9.6 %shard_map.67.refs_1_ = bf16[16,2,16,256]{3,2,1,0:T(8,128)(2,1)} custom-call(s32[16,128]{1,0:T(8,128)S(1)} %get-tuple-element.22.ids_ref.refs_0_, bf16[32,16,128]{2,1,0:T(8,128)(2,1)S(1)} %get-tuple-element.23.refs_1_.parts_ref, f32[32,16,128]{2,1,0:T(8,128)S(1)} %get-tuple-element.24.sum_ref, ...), custom_call_target="tpu_custom_call" | custom-call | tf_op jit(solution)/shard_map/pallas_call | solution.py:435
  87.1 4.4 %all-to-all-start = ((bf16[16,2,16,256]{3,2,1,0:T(8,128)(2,1)}), bf16[16,2,16,256]{3,2,1,0:T(8,128)(2,1)S(1)}, u32[]{:S(2)}, u32[]{:S(2)}) async-start(bf16[16,2,16,256]{3,2,1,0:T(8,128)(2,1)} %shard_map.67.refs_1_), calls=%async_computation | async-start | bytes 524288 | tf_op jit(solution)/shard_map/all_to_all | solution.py:447
  91.5 10.1 %all-to-all-done.back_ref = bf16[16,2,16,256]{3,2,1,0:T(8,128)(2,1)S(1)} async-done(((bf16[16,2,16,256]{3,2,1,0:T(8,128)(2,1)}), bf16[16,2,16,256]{3,2,1,0:T(8,128)(2,1)S(1)}, u32[]{:S(2)}, u32[]{:S(2)}) %all-to-all-start) | async-done | bytes 262176 | tf_op jit(solution)/shard_map/all_to_all | solution.py:447
  101.6 0.9 shard_map.69
  (52 shorter events, 7.2 us)
Async XLA Ops:
  0.6 16.7 %collective-permute-start.5 = (bf16[16,128,128]{2,1,0:T(8,128)(2,1)}, bf16[16,128,128]{2,1,0:T(8,128)(2,1)S(1)}, u32[]{:S(2)}, u32[]{:S(2)}) collective-permute-start(bf16[16,128,128]{2,1,0:T(8,128)(2,1)} %bitcast.2), channel_id=1, source_target_pairs={{0,8},{1,9},{2,10},{3,11},{4,12},{5,13},{6,14},{7,15},{8,0},{9,1},... | collective-permute-start | bytes 1572872 | tf_op jit(solution)/shard_map/ppermute | solution.py:366
  3.7 13.7 %collective-permute-start.6 = (bf16[16,128,128]{2,1,0:T(8,128)(2,1)}, bf16[16,128,128]{2,1,0:T(8,128)(2,1)S(1)}, u32[]{:S(2)}, u32[]{:S(2)}) collective-permute-start(bf16[16,128,128]{2,1,0:T(8,128)(2,1)} %bitcast.3), channel_id=1, source_target_pairs={{0,4},{1,5},{2,6},{3,7},{4,0},{5,1},{6,2},{7,3},{8,12},{9,13},{10,... | collective-permute-start | bytes 1572872 | tf_op jit(solution)/shard_map/ppermute | solution.py:366
  3.7 14.5 %collective-permute-start.4 = (bf16[16,128,128]{2,1,0:T(8,128)(2,1)}, bf16[16,128,128]{2,1,0:T(8,128)(2,1)S(1)}, u32[]{:S(2)}, u32[]{:S(2)}) collective-permute-start(bf16[16,128,128]{2,1,0:T(8,128)(2,1)} %bitcast.4), channel_id=1, source_target_pairs={{0,1},{1,0},{2,3},{3,2},{4,5},{5,4},{6,7},{7,6},{8,9},{9,8},{10,11... | collective-permute-start | bytes 1572872 | tf_op jit(solution)/shard_map/ppermute | solution.py:366
  6.9 1.3 %collective-permute-start = (bf16[17,16,128]{2,1,0:T(8,128)(2,1)S(1)}, bf16[17,16,128]{2,1,0:T(8,128)(2,1)S(1)}, u32[]{:S(2)}, u32[]{:S(2)}) collective-permute-start(bf16[17,16,128]{2,1,0:T(8,128)(2,1)S(1)} %get-tuple-element.15), channel_id=1, source_target_pairs={{0,4},{1,5},{2,6},{3,7},{4,0},{5,1},{6,2},{7,3},{8,12},{9,13},{10,... | collective-permute-start | bytes 208904 | tf_op jit(solution)/shard_map/ppermute | solution.py:366
  8.3 9.0 %collective-permute-start.1 = (bf16[17,16,128]{2,1,0:T(8,128)(2,1)S(1)}, bf16[17,16,128]{2,1,0:T(8,128)(2,1)S(1)}, u32[]{:S(2)}, u32[]{:S(2)}) collective-permute-start(bf16[17,16,128]{2,1,0:T(8,128)(2,1)S(1)} %get-tuple-element.17), channel_id=1, source_target_pairs={{0,8},{1,9},{2,10},{3,11},{4,12},{5,13},{6,14},{7,15},{8,0},{9,1},... | collective-permute-start | bytes 208904 | tf_op jit(solution)/shard_map/ppermute | solution.py:366
  18.2 1.9 %collective-permute-start.8 = (bf16[16,128,128]{2,1,0:T(8,128)(2,1)S(1)}, bf16[16,128,128]{2,1,0:T(8,128)(2,1)S(1)}, u32[]{:S(2)}, u32[]{:S(2)}) collective-permute-start(bf16[16,128,128]{2,1,0:T(8,128)(2,1)S(1)} %shard_map.56.refs_1_.value_ref.refs_3_), channel_id=1, source_target_pairs={{0,4},{1,5},{2,6},{3,7},{4,0},{5,1},{6,2},{7,3},{8,12},{9,13},{10,... | collective-permute-start | bytes 1572872 | tf_op jit(solution)/shard_map/ppermute | solution.py:366
  18.2 2.7 %collective-permute-start.11 = (bf16[16,128,128]{2,1,0:T(8,128)(2,1)}, bf16[16,128,128]{2,1,0:T(8,128)(2,1)S(1)}, u32[]{:S(2)}, u32[]{:S(2)}) collective-permute-start(bf16[16,128,128]{2,1,0:T(8,128)(2,1)} %bitcast.5), channel_id=1, source_target_pairs={{1,2},{2,1},{5,6},{6,5},{9,10},{10,9},{13,14},{14,13},{17,18},{18,... | collective-permute-start | bytes 1572872 | tf_op jit(solution)/shard_map/ppermute | solution.py:366
  19.0 31.6 %collective-permute-start.7 = (bf16[16,128,128]{2,1,0:T(8,128)(2,1)S(1)}, bf16[16,128,128]{2,1,0:T(8,128)(2,1)S(1)}, u32[]{:S(2)}, u32[]{:S(2)}) collective-permute-start(bf16[16,128,128]{2,1,0:T(8,128)(2,1)S(1)} %shard_map.56.refs_1_.value_ref.refs_3_), channel_id=1, source_target_pairs={{0,8},{1,9},{2,10},{3,11},{4,12},{5,13},{6,14},{7,15},{8,0},{9,1},... | collective-permute-start | bytes 1572872 | tf_op jit(solution)/shard_map/ppermute | solution.py:366
  20.2 30.5 %collective-permute-start.10 = (bf16[16,128,128]{2,1,0:T(8,128)(2,1)S(1)}, bf16[16,128,128]{2,1,0:T(8,128)(2,1)S(1)}, u32[]{:S(2)}, u32[]{:S(2)}) collective-permute-start(bf16[16,128,128]{2,1,0:T(8,128)(2,1)S(1)} %shard_map.59), channel_id=1, source_target_pairs={{1,2},{2,1},{5,6},{6,5},{9,10},{10,9},{13,14},{14,13},{17,18},{18,... | collective-permute-start | bytes 1572872 | tf_op jit(solution)/shard_map/ppermute | solution.py:366
  20.9 31.1 %collective-permute-start.12 = (bf16[16,128,128]{2,1,0:T(8,128)(2,1)S(1)}, bf16[16,128,128]{2,1,0:T(8,128)(2,1)S(1)}, u32[]{:S(2)}, u32[]{:S(2)}) collective-permute-start(bf16[16,128,128]{2,1,0:T(8,128)(2,1)S(1)} %collective-permute-done.11.one_ref), channel_id=1, source_target_pairs={{1,0},{2,3},{5,4},{6,7},{9,8},{10,11},{13,12},{14,15},{17,16},{18,... | collective-permute-start | bytes 1572872 | tf_op jit(solution)/shard_map/ppermute | solution.py:366
  22.2 29.8 %collective-permute-start.9 = (bf16[16,128,128]{2,1,0:T(8,128)(2,1)S(1)}, bf16[16,128,128]{2,1,0:T(8,128)(2,1)S(1)}, u32[]{:S(2)}, u32[]{:S(2)}) collective-permute-start(bf16[16,128,128]{2,1,0:T(8,128)(2,1)S(1)} %shard_map.55.refs_1_.refs_2_.refs_4_), channel_id=1, source_target_pairs={{0,4},{1,5},{2,6},{3,7},{4,0},{5,1},{6,2},{7,3},{8,12},{9,13},{10,... | collective-permute-start | bytes 1572872 | tf_op jit(solution)/shard_map/ppermute | solution.py:366
  22.4 28.2 %collective-permute-start.2 = (bf16[17,16,128]{2,1,0:T(8,128)(2,1)S(1)}, bf16[17,16,128]{2,1,0:T(8,128)(2,1)S(1)}, u32[]{:S(2)}, u32[]{:S(2)}) collective-permute-start(bf16[17,16,128]{2,1,0:T(8,128)(2,1)S(1)} %get-tuple-element.19.refs_2_), channel_id=1, source_target_pairs={{0,1},{1,0},{2,3},{3,2},{4,5},{5,4},{6,7},{7,6},{8,9},{9,8},{10,11... | collective-permute-start | bytes 208904 | tf_op jit(solution)/shard_map/ppermute | solution.py:366
  50.7 15.6 %collective-permute-start.14 = (bf16[16,128,128]{2,1,0:T(8,128)(2,1)S(1)}, bf16[16,128,128]{2,1,0:T(8,128)(2,1)S(1)}, u32[]{:S(2)}, u32[]{:S(2)}) collective-permute-start(bf16[16,128,128]{2,1,0:T(8,128)(2,1)S(1)} %shard_map.60.one_ref), channel_id=1, source_target_pairs={{1,0},{2,3},{5,4},{6,7},{9,8},{10,11},{13,12},{14,15},{17,16},{18,... | collective-permute-start | bytes 1572872 | tf_op jit(solution)/shard_map/ppermute | solution.py:366
  52.1 14.2 %collective-permute-start.13 = (bf16[16,128,128]{2,1,0:T(8,128)(2,1)S(1)}, bf16[16,128,128]{2,1,0:T(8,128)(2,1)S(1)}, u32[]{:S(2)}, u32[]{:S(2)}) collective-permute-start(bf16[16,128,128]{2,1,0:T(8,128)(2,1)S(1)} %shard_map.61.refs_7_.refs_9_), channel_id=1, source_target_pairs={{0,8},{1,9},{2,10},{3,11},{4,12},{5,13},{6,14},{7,15},{8,0},{9,1},... | collective-permute-start | bytes 1572872 | tf_op jit(solution)/shard_map/ppermute | solution.py:366
  53.1 13.2 %collective-permute-start.16 = (bf16[16,128,128]{2,1,0:T(8,128)(2,1)S(1)}, bf16[16,128,128]{2,1,0:T(8,128)(2,1)S(1)}, u32[]{:S(2)}, u32[]{:S(2)}) collective-permute-start(bf16[16,128,128]{2,1,0:T(8,128)(2,1)S(1)} %shard_map.57.refs_3_.refs_0_.refs_5_), channel_id=1, source_target_pairs={{0,4},{1,5},{2,6},{3,7},{4,0},{5,1},{6,2},{7,3},{8,12},{9,13},{10,... | collective-permute-start | bytes 1572872 | tf_op jit(solution)/shard_map/ppermute | solution.py:366
  53.1 13.2 %collective-permute-start.15 = (bf16[16,128,128]{2,1,0:T(8,128)(2,1)S(1)}, bf16[16,128,128]{2,1,0:T(8,128)(2,1)S(1)}, u32[]{:S(2)}, u32[]{:S(2)}) collective-permute-start(bf16[16,128,128]{2,1,0:T(8,128)(2,1)S(1)} %shard_map.61.refs_7_.refs_9_), channel_id=1, source_target_pairs={{0,4},{1,5},{2,6},{3,7},{4,0},{5,1},{6,2},{7,3},{8,12},{9,13},{10,... | collective-permute-start | bytes 1572872 | tf_op jit(solution)/shard_map/ppermute | solution.py:366
  53.6 6.2 %collective-permute-start.3 = (bf16[17,16,128]{2,1,0:T(8,128)(2,1)S(1)}, bf16[17,16,128]{2,1,0:T(8,128)(2,1)S(1)}, u32[]{:S(2)}, u32[]{:S(2)}) collective-permute-start(bf16[17,16,128]{2,1,0:T(8,128)(2,1)S(1)} %get-tuple-element.21.refs_1_), channel_id=1, source_target_pairs={{0,3},{1,2},{2,1},{3,0},{4,7},{5,6},{6,5},{7,4},{8,11},{9,10},{10,... | collective-permute-start | bytes 208904 | tf_op jit(solution)/shard_map/ppermute | solution.py:366
  66.3 2.2 %collective-permute-start.18 = (bf16[16,128,128]{2,1,0:T(8,128)(2,1)S(1)}, bf16[16,128,128]{2,1,0:T(8,128)(2,1)S(1)}, u32[]{:S(2)}, u32[]{:S(2)}) collective-permute-start(bf16[16,128,128]{2,1,0:T(8,128)(2,1)S(1)} %collective-permute-done.13.refs_0_.refs_8_.refs_10_), channel_id=1, source_target_pairs={{0,4},{1,5},{2,6},{3,7},{4,0},{5,1},{6,2},{7,3},{8,12},{9,13},{10,... | collective-permute-start | bytes 1572872 | tf_op jit(solution)/shard_map/ppermute | solution.py:366
  66.4 2.6 %collective-permute-start.17 = (bf16[16,128,128]{2,1,0:T(8,128)(2,1)S(1)}, bf16[16,128,128]{2,1,0:T(8,128)(2,1)S(1)}, u32[]{:S(2)}, u32[]{:S(2)}) collective-permute-start(bf16[16,128,128]{2,1,0:T(8,128)(2,1)S(1)} %shard_map.63.refs_9_.refs_11_), channel_id=1, source_target_pairs={{0,4},{1,5},{2,6},{3,7},{4,0},{5,1},{6,2},{7,3},{8,12},{9,13},{10,... | collective-permute-start | bytes 1572872 | tf_op jit(solution)/shard_map/ppermute | solution.py:366
  66.9 8.3 %collective-permute-start.19 = (bf16[8,128,128]{2,1,0:T(8,128)(2,1)S(1)}, bf16[8,128,128]{2,1,0:T(8,128)(2,1)S(1)}, u32[]{:S(2)}, u32[]{:S(2)}) collective-permute-start(bf16[8,128,128]{2,1,0:T(8,128)(2,1)S(1)} %slice.8), channel_id=1, source_target_pairs={{0,8},{1,9},{2,10},{3,11},{4,12},{5,13},{6,14},{7,15},{8,0},{9,1},... | collective-permute-start | bytes 786440 | tf_op jit(solution)/shard_map/ppermute | solution.py:366
  67.9 8.0 %collective-permute-start.20 = (bf16[8,128,128]{2,1,0:T(8,128)(2,1)S(1)}, bf16[8,128,128]{2,1,0:T(8,128)(2,1)S(1)}, u32[]{:S(2)}, u32[]{:S(2)}) collective-permute-start(bf16[8,128,128]{2,1,0:T(8,128)(2,1)S(1)} %slice.9), channel_id=1, source_target_pairs={{0,1},{1,0},{2,3},{3,2},{4,5},{5,4},{6,7},{7,6},{8,9},{9,8},{10,11... | collective-permute-start | bytes 786440 | tf_op jit(solution)/shard_map/ppermute | solution.py:366
  75.2 1.5 %collective-permute-start.21 = (bf16[8,128,128]{2,1,0:T(8,128)(2,1)S(1)}, bf16[8,128,128]{2,1,0:T(8,128)(2,1)S(1)}, u32[]{:S(2)}, u32[]{:S(2)}) collective-permute-start(bf16[8,128,128]{2,1,0:T(8,128)(2,1)S(1)} %shard_map.65.refs_16_), channel_id=1, source_target_pairs={{0,4},{1,5},{2,6},{3,7},{4,0},{5,1},{6,2},{7,3},{8,12},{9,13},{10,... | collective-permute-start | bytes 786440 | tf_op jit(solution)/shard_map/ppermute | solution.py:366
  76.0 1.5 %collective-permute-start.22 = (bf16[8,128,128]{2,1,0:T(8,128)(2,1)S(1)}, bf16[8,128,128]{2,1,0:T(8,128)(2,1)S(1)}, u32[]{:S(2)}, u32[]{:S(2)}) collective-permute-start(bf16[8,128,128]{2,1,0:T(8,128)(2,1)S(1)} %shard_map.66.refs_17_), channel_id=1, source_target_pairs={{0,4},{1,5},{2,6},{3,7},{4,0},{5,1},{6,2},{7,3},{8,12},{9,13},{10,... | collective-permute-start | bytes 786440 | tf_op jit(solution)/shard_map/ppermute | solution.py:366
  87.1 14.5 %all-to-all-start = ((bf16[16,2,16,256]{3,2,1,0:T(8,128)(2,1)}), bf16[16,2,16,256]{3,2,1,0:T(8,128)(2,1)S(1)}, u32[]{:S(2)}, u32[]{:S(2)}) async-start(bf16[16,2,16,256]{3,2,1,0:T(8,128)(2,1)} %shard_map.67.refs_1_), calls=%async_computation | async-start | bytes 524288 | tf_op jit(solution)/shard_map/all_to_all | solution.py:447
  (2 other events, 42.5 us)

commit v25 on v21

--- a/solution.py
+++ b/solution.py
@@ -9,7 +9,7 @@
 
 PER_ROW = 2
 DEG = 4
-SPLIT = 4
+SPLIT = 8
 GATHER_LIMIT = 12 * 2**20
 LANES = ("col", "row")
 INNER = (1, 2)

time: 85.2 us -> 85.7 us (level)
  transfers between devices with their start and end apart: 24 -> 24, of which waited for: 10 -> 10; matrix products, arithmetic and copies ran while one was open for 1% -> 1% of each run, Pallas kernels for 6% -> 7%
where the time goes in v25:
time: 85.7 us; the launch traced here: 85.3 us
  waiting for transfers between devices  43.7 us (51%)
  starting transfers between devices  22.6 us (26%)
  Pallas kernels  16.6 us (19%)
  local copies, waits for them, and re-layouts  1.61 us (2%)
    ppermute x23, waiting for transfers between devices, send(): return lax.ppermute(buf, LANES, pairs)  33.6 us
    ppermute x23, starting transfers between devices, send(): return lax.ppermute(buf, LANES, pairs)  19.1 us
    all_to_all x1, waiting for transfers between devices, gather_plan(): back = lax.all_to_all(done, LANES, split_axis=0, concat_axis=0, tiled=True)  10.1 us
    pallas_call x1, Pallas kernels, gather_plan(): pl.pallas_call(functools.partial(filter_kernel, early, later, late, n_col...  10 us
    pallas_call x1, Pallas kernels, gather_plan(): pl.pallas_call(functools.partial(first_kernel, early, later, n_col, n_row...  4.17 us
    all_to_all x1, starting transfers between devices, gather_plan(): back = lax.all_to_all(done, LANES, split_axis=0, concat_axis=0, tiled=True)  3.59 us
  transfers between devices with their start and end apart: 24, of which 10 were waited for; matrix products, arithmetic and copies ran while one was open for 1% of the time, Pallas kernels for 7%

profile of v25, /device:TPU:0, one launch (start us, length us, event | category | flops | bytes accessed | tf_op | source)
XLA Modules:
  0.0 85.3 jit_solution(11670428438536859153)
XLA Ops:
  0.6 3.0 %collective-permute-start.5 = (bf16[16,128,128]{2,1,0:T(8,128)(2,1)}, bf16[16,128,128]{2,1,0:T(8,128)(2,1)S(1)}, u32[]{:S(2)}, u32[]{:S(2)}) collective-permute-start(bf16[16,128,128]{2,1,0:T(8,128)(2,1)} %bitcast.2), channel_id=1, source_target_pairs={{0,8},{1,9},{2,10},{3,11},{4,12},{5,13},{6,14},{7,15},{8,0},{9,1},... | collective-permute-start | bytes 1572872 | tf_op jit(solution)/shard_map/ppermute | solution.py:348
  3.7 1.6 %collective-permute-start.4 = (bf16[16,128,128]{2,1,0:T(8,128)(2,1)}, bf16[16,128,128]{2,1,0:T(8,128)(2,1)S(1)}, u32[]{:S(2)}, u32[]{:S(2)}) collective-permute-start(bf16[16,128,128]{2,1,0:T(8,128)(2,1)} %bitcast.4), channel_id=1, source_target_pairs={{0,1},{1,0},{2,3},{3,2},{4,5},{5,4},{6,7},{7,6},{8,9},{9,8},{10,11... | collective-permute-start | bytes 1572872 | tf_op jit(solution)/shard_map/ppermute | solution.py:348
  6.6 0.9 %copy-done.1 = bf16[256,256]{1,0:T(8,128)(2,1)S(1)} copy-done((bf16[256,256]{1,0:T(8,128)(2,1)S(1)}, bf16[256,256]{1,0:T(8,128)(2,1)}, u32[]{:S(2)}) %copy-start.1) | copy-done | bytes 131096
  7.9 1.0 %collective-permute-done.came_ref = bf16[17,16,128]{2,1,0:T(8,128)(2,1)S(1)} collective-permute-done((bf16[17,16,128]{2,1,0:T(8,128)(2,1)S(1)}, bf16[17,16,128]{2,1,0:T(8,128)(2,1)S(1)}, u32[]{:S(2)}, u32[]{:S(2)}) %collective-permute-start) | collective-permute-done | bytes 69664 | tf_op jit(solution)/shard_map/ppermute | solution.py:348
  9.5 7.8 %collective-permute-done.1.came_ref = bf16[17,16,128]{2,1,0:T(8,128)(2,1)S(1)} collective-permute-done((bf16[17,16,128]{2,1,0:T(8,128)(2,1)S(1)}, bf16[17,16,128]{2,1,0:T(8,128)(2,1)S(1)}, u32[]{:S(2)}, u32[]{:S(2)}) %collective-permute-start.1) | collective-permute-done | bytes 69664 | tf_op jit(solution)/shard_map/ppermute | solution.py:348
  17.3 1.9 %collective-permute-start.2 = (bf16[17,16,128]{2,1,0:T(8,128)(2,1)S(1)}, bf16[17,16,128]{2,1,0:T(8,128)(2,1)S(1)}, u32[]{:S(2)}, u32[]{:S(2)}) collective-permute-start(bf16[17,16,128]{2,1,0:T(8,128)(2,1)S(1)} %get-tuple-element.19.refs_2_), channel_id=1, source_target_pairs={{0,1},{1,0},{2,3},{3,2},{4,5},{5,4},{6,7},{7,6},{8,9},{9,8},{10,11... | collective-permute-start | bytes 208904 | tf_op jit(solution)/shard_map/ppermute | solution.py:348
  19.2 0.7 collective-permute-start.10
  19.9 1.4 %collective-permute-start.12 = (bf16[16,128,128]{2,1,0:T(8,128)(2,1)S(1)}, bf16[16,128,128]{2,1,0:T(8,128)(2,1)S(1)}, u32[]{:S(2)}, u32[]{:S(2)}) collective-permute-start(bf16[16,128,128]{2,1,0:T(8,128)(2,1)S(1)} %shard_map.60.one_ref), channel_id=1, source_target_pairs={{1,0},{2,3},{5,4},{6,7},{9,8},{10,11},{13,12},{14,15},{17,16},{18,... | collective-permute-start | bytes 1572872 | tf_op jit(solution)/shard_map/ppermute | solution.py:348
  21.4 1.6 %collective-permute-start.7 = (bf16[16,128,128]{2,1,0:T(8,128)(2,1)S(1)}, bf16[16,128,128]{2,1,0:T(8,128)(2,1)S(1)}, u32[]{:S(2)}, u32[]{:S(2)}) collective-permute-start(bf16[16,128,128]{2,1,0:T(8,128)(2,1)S(1)} %shard_map.56.refs_1_.refs_3_), channel_id=1, source_target_pairs={{0,8},{1,9},{2,10},{3,11},{4,12},{5,13},{6,14},{7,15},{8,0},{9,1},... | collective-permute-start | bytes 1572872 | tf_op jit(solution)/shard_map/ppermute | solution.py:348
  23.5 1.3 %collective-permute-start.14 = (bf16[16,128,128]{2,1,0:T(8,128)(2,1)S(1)}, bf16[16,128,128]{2,1,0:T(8,128)(2,1)S(1)}, u32[]{:S(2)}, u32[]{:S(2)}) collective-permute-start(bf16[16,128,128]{2,1,0:T(8,128)(2,1)S(1)} %shard_map.59.one_ref), channel_id=1, source_target_pairs={{1,0},{2,3},{5,4},{6,7},{9,8},{10,11},{13,12},{14,15},{17,16},{18,... | collective-permute-start | bytes 1572872 | tf_op jit(solution)/shard_map/ppermute | solution.py:348
  24.8 12.0 %collective-permute-done.12.refs_0_ = bf16[16,128,128]{2,1,0:T(8,128)(2,1)S(1)} collective-permute-done((bf16[16,128,128]{2,1,0:T(8,128)(2,1)S(1)}, bf16[16,128,128]{2,1,0:T(8,128)(2,1)S(1)}, u32[]{:S(2)}, u32[]{:S(2)}) %collective-permute-start.12) | collective-permute-done | bytes 524320 | tf_op jit(solution)/shard_map/ppermute | solution.py:348
  36.9 1.9 %collective-permute-start.13 = (bf16[16,128,128]{2,1,0:T(8,128)(2,1)S(1)}, bf16[16,128,128]{2,1,0:T(8,128)(2,1)S(1)}, u32[]{:S(2)}, u32[]{:S(2)}) collective-permute-start(bf16[16,128,128]{2,1,0:T(8,128)(2,1)S(1)} %shard_map.62.refs_7_.refs_9_), channel_id=1, source_target_pairs={{0,8},{1,9},{2,10},{3,11},{4,12},{5,13},{6,14},{7,15},{8,0},{9,1},... | collective-permute-start | bytes 1572872 | tf_op jit(solution)/shard_map/ppermute | solution.py:348
  39.7 5.8 %collective-permute-done.3.came_ref = bf16[17,16,128]{2,1,0:T(8,128)(2,1)S(1)} collective-permute-done((bf16[17,16,128]{2,1,0:T(8,128)(2,1)S(1)}, bf16[17,16,128]{2,1,0:T(8,128)(2,1)S(1)}, u32[]{:S(2)}, u32[]{:S(2)}) %collective-permute-start.3) | collective-permute-done | bytes 69664 | tf_op jit(solution)/shard_map/ppermute | solution.py:348
  45.5 1.2 %shard_map.58.refs_2_.sta_ref.refs_0_ = bf16[7,16,128,128]{3,2,1,0:T(8,128)(2,1)S(1)} custom-call(bf16[16,128,128]{2,1,0:T(8,128)(2,1)S(1)} %bitcast.6, bf16[16,128,128]{2,1,0:T(8,128)(2,1)S(1)} %shard_map.56.refs_1_.refs_3_, bf16[16,128,128]{2,1,0:T(8,128)(2,1)S(1)} %shard_map.55.refs_1_.refs_2_.refs_4_, ...), custom_call_target="tpu_custom_call" | custom-call | bytes 11010048 | tf_op jit(solution)/shard_map/pallas_call | solution.py:260
  46.7 2.3 %collective-permute-done.14.refs_0_ = bf16[16,128,128]{2,1,0:T(8,128)(2,1)S(1)} collective-permute-done((bf16[16,128,128]{2,1,0:T(8,128)(2,1)S(1)}, bf16[16,128,128]{2,1,0:T(8,128)(2,1)S(1)}, u32[]{:S(2)}, u32[]{:S(2)}) %collective-permute-start.14) | collective-permute-done | bytes 524320 | tf_op jit(solution)/shard_map/ppermute | solution.py:348
  49.6 1.5 %collective-permute-start.19 = (bf16[8,128,128]{2,1,0:T(8,128)(2,1)S(1)}, bf16[8,128,128]{2,1,0:T(8,128)(2,1)S(1)}, u32[]{:S(2)}, u32[]{:S(2)}) collective-permute-start(bf16[8,128,128]{2,1,0:T(8,128)(2,1)S(1)} %slice.8), channel_id=1, source_target_pairs={{0,8},{1,9},{2,10},{3,11},{4,12},{5,13},{6,14},{7,15},{8,0},{9,1},... | collective-permute-start | bytes 786440 | tf_op jit(solution)/shard_map/ppermute | solution.py:348
  51.8 4.2 %shard_map.65 = (bf16[7,16,128,128]{3,2,1,0:T(8,128)(2,1)S(1)}, f32[32,16,128]{2,1,0:T(8,128)S(1)}) custom-call(s32[16,128]{1,0:T(8,128)S(1)} %get-tuple-element.22.ids_ref.refs_0_, bf16[32,16,128]{2,1,0:T(8,128)(2,1)S(1)} %get-tuple-element.23.refs_1_.parts_ref, bf16[7,16,128,128]{3,2,1,0:T(8,128)(2,1)S(1)} %shard_map.58.refs_2_.sta_ref.refs_0_, ...), custom_call_target="tpu_custom_call" | custom-call | flops 234881024 | bytes 11010048 | tf_op jit(solution)/shard_map/pallas_call | solution.py:397
  56.0 1.9 %collective-permute-done.19.refs_0_ = bf16[8,128,128]{2,1,0:T(8,128)(2,1)S(1)} collective-permute-done((bf16[8,128,128]{2,1,0:T(8,128)(2,1)S(1)}, bf16[8,128,128]{2,1,0:T(8,128)(2,1)S(1)}, u32[]{:S(2)}, u32[]{:S(2)}) %collective-permute-start.19) | collective-permute-done | bytes 262176 | tf_op jit(solution)/shard_map/ppermute | solution.py:348
  57.9 1.3 %collective-permute-done.20.refs_0_ = bf16[8,128,128]{2,1,0:T(8,128)(2,1)S(1)} collective-permute-done((bf16[8,128,128]{2,1,0:T(8,128)(2,1)S(1)}, bf16[8,128,128]{2,1,0:T(8,128)(2,1)S(1)}, u32[]{:S(2)}, u32[]{:S(2)}) %collective-permute-start.20) | collective-permute-done | bytes 262176 | tf_op jit(solution)/shard_map/ppermute | solution.py:348
  59.5 1.3 %collective-permute-done.22.refs_19_ = bf16[8,128,128]{2,1,0:T(8,128)(2,1)S(1)} collective-permute-done((bf16[8,128,128]{2,1,0:T(8,128)(2,1)S(1)}, bf16[8,128,128]{2,1,0:T(8,128)(2,1)S(1)}, u32[]{:S(2)}, u32[]{:S(2)}) %collective-permute-start.22) | collective-permute-done | bytes 262176 | tf_op jit(solution)/shard_map/ppermute | solution.py:348
  60.7 10.0 %shard_map.68.refs_1_ = bf16[16,2,16,256]{3,2,1,0:T(8,128)(2,1)} custom-call(s32[16,128]{1,0:T(8,128)S(1)} %get-tuple-element.22.ids_ref.refs_0_, bf16[32,16,128]{2,1,0:T(8,128)(2,1)S(1)} %get-tuple-element.23.refs_1_.parts_ref, f32[32,16,128]{2,1,0:T(8,128)S(1)} %get-tuple-element.24.sum_ref, ...), custom_call_target="tpu_custom_call" | custom-call | tf_op jit(solution)/shard_map/pallas_call | solution.py:417
  70.8 3.6 %all-to-all-start = ((bf16[16,2,16,256]{3,2,1,0:T(8,128)(2,1)}), bf16[16,2,16,256]{3,2,1,0:T(8,128)(2,1)S(1)}, u32[]{:S(2)}, u32[]{:S(2)}) async-start(bf16[16,2,16,256]{3,2,1,0:T(8,128)(2,1)} %shard_map.68.refs_1_), calls=%async_computation | async-start | bytes 524288 | tf_op jit(solution)/shard_map/all_to_all | solution.py:429
  74.4 10.1 %all-to-all-done.back_ref = bf16[16,2,16,256]{3,2,1,0:T(8,128)(2,1)S(1)} async-done(((bf16[16,2,16,256]{3,2,1,0:T(8,128)(2,1)}), bf16[16,2,16,256]{3,2,1,0:T(8,128)(2,1)S(1)}, u32[]{:S(2)}, u32[]{:S(2)}) %all-to-all-start) | async-done | bytes 262176 | tf_op jit(solution)/shard_map/all_to_all | solution.py:429
  84.4 0.9 %shard_map.70 = (f32[256,256]{1,0:T(8,128)}, f32[256,256]{1,0:T(8,128)}) custom-call(bf16[16,2,16,256]{3,2,1,0:T(8,128)(2,1)S(1)} %all-to-all-done.back_ref, s32[16,128]{1,0:T(8,128)S(1)} %shard_map.69.marker_ref), custom_call_target="tpu_custom_call" | custom-call | tf_op jit(solution)/shard_map/pallas_call | solution.py:431
  (53 shorter events, 5.5 us)
Async XLA Ops:
  0.6 18.5 %collective-permute-start.5 = (bf16[16,128,128]{2,1,0:T(8,128)(2,1)}, bf16[16,128,128]{2,1,0:T(8,128)(2,1)S(1)}, u32[]{:S(2)}, u32[]{:S(2)}) collective-permute-start(bf16[16,128,128]{2,1,0:T(8,128)(2,1)} %bitcast.2), channel_id=1, source_target_pairs={{0,8},{1,9},{2,10},{3,11},{4,12},{5,13},{6,14},{7,15},{8,0},{9,1},... | collective-permute-start | bytes 1572872 | tf_op jit(solution)/shard_map/ppermute | solution.py:348
  3.7 15.5 %collective-permute-start.6 = (bf16[16,128,128]{2,1,0:T(8,128)(2,1)}, bf16[16,128,128]{2,1,0:T(8,128)(2,1)S(1)}, u32[]{:S(2)}, u32[]{:S(2)}) collective-permute-start(bf16[16,128,128]{2,1,0:T(8,128)(2,1)} %bitcast.3), channel_id=1, source_target_pairs={{0,4},{1,5},{2,6},{3,7},{4,0},{5,1},{6,2},{7,3},{8,12},{9,13},{10,... | collective-permute-start | bytes 1572872 | tf_op jit(solution)/shard_map/ppermute | solution.py:348
  3.7 15.5 %collective-permute-start.4 = (bf16[16,128,128]{2,1,0:T(8,128)(2,1)}, bf16[16,128,128]{2,1,0:T(8,128)(2,1)S(1)}, u32[]{:S(2)}, u32[]{:S(2)}) collective-permute-start(bf16[16,128,128]{2,1,0:T(8,128)(2,1)} %bitcast.4), channel_id=1, source_target_pairs={{0,1},{1,0},{2,3},{3,2},{4,5},{5,4},{6,7},{7,6},{8,9},{9,8},{10,11... | collective-permute-start | bytes 1572872 | tf_op jit(solution)/shard_map/ppermute | solution.py:348
  5.2 14.7 %collective-permute-start.11 = (bf16[16,128,128]{2,1,0:T(8,128)(2,1)}, bf16[16,128,128]{2,1,0:T(8,128)(2,1)S(1)}, u32[]{:S(2)}, u32[]{:S(2)}) collective-permute-start(bf16[16,128,128]{2,1,0:T(8,128)(2,1)} %bitcast.5), channel_id=1, source_target_pairs={{1,2},{2,1},{5,6},{6,5},{9,10},{10,9},{13,14},{14,13},{17,18},{18,... | collective-permute-start | bytes 1572872 | tf_op jit(solution)/shard_map/ppermute | solution.py:348
  7.6 1.3 %collective-permute-start = (bf16[17,16,128]{2,1,0:T(8,128)(2,1)S(1)}, bf16[17,16,128]{2,1,0:T(8,128)(2,1)S(1)}, u32[]{:S(2)}, u32[]{:S(2)}) collective-permute-start(bf16[17,16,128]{2,1,0:T(8,128)(2,1)S(1)} %get-tuple-element.15), channel_id=1, source_target_pairs={{0,4},{1,5},{2,6},{3,7},{4,0},{5,1},{6,2},{7,3},{8,12},{9,13},{10,... | collective-permute-start | bytes 208904 | tf_op jit(solution)/shard_map/ppermute | solution.py:348
  9.0 8.3 %collective-permute-start.1 = (bf16[17,16,128]{2,1,0:T(8,128)(2,1)S(1)}, bf16[17,16,128]{2,1,0:T(8,128)(2,1)S(1)}, u32[]{:S(2)}, u32[]{:S(2)}) collective-permute-start(bf16[17,16,128]{2,1,0:T(8,128)(2,1)S(1)} %get-tuple-element.17), channel_id=1, source_target_pairs={{0,8},{1,9},{2,10},{3,11},{4,12},{5,13},{6,14},{7,15},{8,0},{9,1},... | collective-permute-start | bytes 208904 | tf_op jit(solution)/shard_map/ppermute | solution.py:348
  17.3 5.6 %collective-permute-start.2 = (bf16[17,16,128]{2,1,0:T(8,128)(2,1)S(1)}, bf16[17,16,128]{2,1,0:T(8,128)(2,1)S(1)}, u32[]{:S(2)}, u32[]{:S(2)}) collective-permute-start(bf16[17,16,128]{2,1,0:T(8,128)(2,1)S(1)} %get-tuple-element.19.refs_2_), channel_id=1, source_target_pairs={{0,1},{1,0},{2,3},{3,2},{4,5},{5,4},{6,7},{7,6},{8,9},{9,8},{10,11... | collective-permute-start | bytes 208904 | tf_op jit(solution)/shard_map/ppermute | solution.py:348
  19.2 4.3 %collective-permute-start.10 = (bf16[16,128,128]{2,1,0:T(8,128)(2,1)S(1)}, bf16[16,128,128]{2,1,0:T(8,128)(2,1)S(1)}, u32[]{:S(2)}, u32[]{:S(2)}) collective-permute-start(bf16[16,128,128]{2,1,0:T(8,128)(2,1)S(1)} %shard_map.56.refs_1_.refs_3_), channel_id=1, source_target_pairs={{1,2},{2,1},{5,6},{6,5},{9,10},{10,9},{13,14},{14,13},{17,18},{18,... | collective-permute-start | bytes 1572872 | tf_op jit(solution)/shard_map/ppermute | solution.py:348
  19.9 16.9 %collective-permute-start.12 = (bf16[16,128,128]{2,1,0:T(8,128)(2,1)S(1)}, bf16[16,128,128]{2,1,0:T(8,128)(2,1)S(1)}, u32[]{:S(2)}, u32[]{:S(2)}) collective-permute-start(bf16[16,128,128]{2,1,0:T(8,128)(2,1)S(1)} %shard_map.60.one_ref), channel_id=1, source_target_pairs={{1,0},{2,3},{5,4},{6,7},{9,8},{10,11},{13,12},{14,15},{17,16},{18,... | collective-permute-start | bytes 1572872 | tf_op jit(solution)/shard_map/ppermute | solution.py:348
  21.4 15.5 %collective-permute-start.7 = (bf16[16,128,128]{2,1,0:T(8,128)(2,1)S(1)}, bf16[16,128,128]{2,1,0:T(8,128)(2,1)S(1)}, u32[]{:S(2)}, u32[]{:S(2)}) collective-permute-start(bf16[16,128,128]{2,1,0:T(8,128)(2,1)S(1)} %shard_map.56.refs_1_.refs_3_), channel_id=1, source_target_pairs={{0,8},{1,9},{2,10},{3,11},{4,12},{5,13},{6,14},{7,15},{8,0},{9,1},... | collective-permute-start | bytes 1572872 | tf_op jit(solution)/shard_map/ppermute | solution.py:348
  22.9 13.9 %collective-permute-start.9 = (bf16[16,128,128]{2,1,0:T(8,128)(2,1)S(1)}, bf16[16,128,128]{2,1,0:T(8,128)(2,1)S(1)}, u32[]{:S(2)}, u32[]{:S(2)}) collective-permute-start(bf16[16,128,128]{2,1,0:T(8,128)(2,1)S(1)} %shard_map.55.refs_1_.refs_2_.refs_4_), channel_id=1, source_target_pairs={{0,4},{1,5},{2,6},{3,7},{4,0},{5,1},{6,2},{7,3},{8,12},{9,13},{10,... | collective-permute-start | bytes 1572872 | tf_op jit(solution)/shard_map/ppermute | solution.py:348
  22.9 13.9 %collective-permute-start.8 = (bf16[16,128,128]{2,1,0:T(8,128)(2,1)S(1)}, bf16[16,128,128]{2,1,0:T(8,128)(2,1)S(1)}, u32[]{:S(2)}, u32[]{:S(2)}) collective-permute-start(bf16[16,128,128]{2,1,0:T(8,128)(2,1)S(1)} %shard_map.56.refs_1_.refs_3_), channel_id=1, source_target_pairs={{0,4},{1,5},{2,6},{3,7},{4,0},{5,1},{6,2},{7,3},{8,12},{9,13},{10,... | collective-permute-start | bytes 1572872 | tf_op jit(solution)/shard_map/ppermute | solution.py:348
  23.5 25.5 %collective-permute-start.14 = (bf16[16,128,128]{2,1,0:T(8,128)(2,1)S(1)}, bf16[16,128,128]{2,1,0:T(8,128)(2,1)S(1)}, u32[]{:S(2)}, u32[]{:S(2)}) collective-permute-start(bf16[16,128,128]{2,1,0:T(8,128)(2,1)S(1)} %shard_map.59.one_ref), channel_id=1, source_target_pairs={{1,0},{2,3},{5,4},{6,7},{9,8},{10,11},{13,12},{14,15},{17,16},{18,... | collective-permute-start | bytes 1572872 | tf_op jit(solution)/shard_map/ppermute | solution.py:348
  36.9 12.1 %collective-permute-start.13 = (bf16[16,128,128]{2,1,0:T(8,128)(2,1)S(1)}, bf16[16,128,128]{2,1,0:T(8,128)(2,1)S(1)}, u32[]{:S(2)}, u32[]{:S(2)}) collective-permute-start(bf16[16,128,128]{2,1,0:T(8,128)(2,1)S(1)} %shard_map.62.refs_7_.refs_9_), channel_id=1, source_target_pairs={{0,8},{1,9},{2,10},{3,11},{4,12},{5,13},{6,14},{7,15},{8,0},{9,1},... | collective-permute-start | bytes 1572872 | tf_op jit(solution)/shard_map/ppermute | solution.py:348
  38.8 10.2 %collective-permute-start.15 = (bf16[16,128,128]{2,1,0:T(8,128)(2,1)S(1)}, bf16[16,128,128]{2,1,0:T(8,128)(2,1)S(1)}, u32[]{:S(2)}, u32[]{:S(2)}) collective-permute-start(bf16[16,128,128]{2,1,0:T(8,128)(2,1)S(1)} %shard_map.62.refs_7_.refs_9_), channel_id=1, source_target_pairs={{0,4},{1,5},{2,6},{3,7},{4,0},{5,1},{6,2},{7,3},{8,12},{9,13},{10,... | collective-permute-start | bytes 1572872 | tf_op jit(solution)/shard_map/ppermute | solution.py:348
  38.8 10.2 %collective-permute-start.16 = (bf16[16,128,128]{2,1,0:T(8,128)(2,1)S(1)}, bf16[16,128,128]{2,1,0:T(8,128)(2,1)S(1)}, u32[]{:S(2)}, u32[]{:S(2)}) collective-permute-start(bf16[16,128,128]{2,1,0:T(8,128)(2,1)S(1)} %shard_map.57.refs_3_.refs_0_.refs_5_), channel_id=1, source_target_pairs={{0,4},{1,5},{2,6},{3,7},{4,0},{5,1},{6,2},{7,3},{8,12},{9,13},{10,... | collective-permute-start | bytes 1572872 | tf_op jit(solution)/shard_map/ppermute | solution.py:348
  39.3 6.2 %collective-permute-start.3 = (bf16[17,16,128]{2,1,0:T(8,128)(2,1)S(1)}, bf16[17,16,128]{2,1,0:T(8,128)(2,1)S(1)}, u32[]{:S(2)}, u32[]{:S(2)}) collective-permute-start(bf16[17,16,128]{2,1,0:T(8,128)(2,1)S(1)} %get-tuple-element.21.refs_1_), channel_id=1, source_target_pairs={{0,3},{1,2},{2,1},{3,0},{4,7},{5,6},{6,5},{7,4},{8,11},{9,10},{10,... | collective-permute-start | bytes 208904 | tf_op jit(solution)/shard_map/ppermute | solution.py:348
  49.0 2.9 %collective-permute-start.18 = (bf16[16,128,128]{2,1,0:T(8,128)(2,1)S(1)}, bf16[16,128,128]{2,1,0:T(8,128)(2,1)S(1)}, u32[]{:S(2)}, u32[]{:S(2)}) collective-permute-start(bf16[16,128,128]{2,1,0:T(8,128)(2,1)S(1)} %collective-permute-done.13.refs_0_.refs_8_.refs_10_), channel_id=1, source_target_pairs={{0,4},{1,5},{2,6},{3,7},{4,0},{5,1},{6,2},{7,3},{8,12},{9,13},{10,... | collective-permute-start | bytes 1572872 | tf_op jit(solution)/shard_map/ppermute | solution.py:348
  49.1 2.8 %collective-permute-start.17 = (bf16[16,128,128]{2,1,0:T(8,128)(2,1)S(1)}, bf16[16,128,128]{2,1,0:T(8,128)(2,1)S(1)}, u32[]{:S(2)}, u32[]{:S(2)}) collective-permute-start(bf16[16,128,128]{2,1,0:T(8,128)(2,1)S(1)} %shard_map.64.refs_9_.refs_11_), channel_id=1, source_target_pairs={{0,4},{1,5},{2,6},{3,7},{4,0},{5,1},{6,2},{7,3},{8,12},{9,13},{10,... | collective-permute-start | bytes 1572872 | tf_op jit(solution)/shard_map/ppermute | solution.py:348
  49.6 8.3 %collective-permute-start.19 = (bf16[8,128,128]{2,1,0:T(8,128)(2,1)S(1)}, bf16[8,128,128]{2,1,0:T(8,128)(2,1)S(1)}, u32[]{:S(2)}, u32[]{:S(2)}) collective-permute-start(bf16[8,128,128]{2,1,0:T(8,128)(2,1)S(1)} %slice.8), channel_id=1, source_target_pairs={{0,8},{1,9},{2,10},{3,11},{4,12},{5,13},{6,14},{7,15},{8,0},{9,1},... | collective-permute-start | bytes 786440 | tf_op jit(solution)/shard_map/ppermute | solution.py:348
  51.2 8.0 %collective-permute-start.20 = (bf16[8,128,128]{2,1,0:T(8,128)(2,1)S(1)}, bf16[8,128,128]{2,1,0:T(8,128)(2,1)S(1)}, u32[]{:S(2)}, u32[]{:S(2)}) collective-permute-start(bf16[8,128,128]{2,1,0:T(8,128)(2,1)S(1)} %slice.9), channel_id=1, source_target_pairs={{0,1},{1,0},{2,3},{3,2},{4,5},{5,4},{6,7},{7,6},{8,9},{9,8},{10,11... | collective-permute-start | bytes 786440 | tf_op jit(solution)/shard_map/ppermute | solution.py:348
  57.9 1.5 %collective-permute-start.21 = (bf16[8,128,128]{2,1,0:T(8,128)(2,1)S(1)}, bf16[8,128,128]{2,1,0:T(8,128)(2,1)S(1)}, u32[]{:S(2)}, u32[]{:S(2)}) collective-permute-start(bf16[8,128,128]{2,1,0:T(8,128)(2,1)S(1)} %shard_map.66.refs_16_), channel_id=1, source_target_pairs={{0,4},{1,5},{2,6},{3,7},{4,0},{5,1},{6,2},{7,3},{8,12},{9,13},{10,... | collective-permute-start | bytes 786440 | tf_op jit(solution)/shard_map/ppermute | solution.py:348
  59.2 1.5 %collective-permute-start.22 = (bf16[8,128,128]{2,1,0:T(8,128)(2,1)S(1)}, bf16[8,128,128]{2,1,0:T(8,128)(2,1)S(1)}, u32[]{:S(2)}, u32[]{:S(2)}) collective-permute-start(bf16[8,128,128]{2,1,0:T(8,128)(2,1)S(1)} %shard_map.67.refs_17_), channel_id=1, source_target_pairs={{0,4},{1,5},{2,6},{3,7},{4,0},{5,1},{6,2},{7,3},{8,12},{9,13},{10,... | collective-permute-start | bytes 786440 | tf_op jit(solution)/shard_map/ppermute | solution.py:348
  70.8 13.7 %all-to-all-start = ((bf16[16,2,16,256]{3,2,1,0:T(8,128)(2,1)}), bf16[16,2,16,256]{3,2,1,0:T(8,128)(2,1)S(1)}, u32[]{:S(2)}, u32[]{:S(2)}) async-start(bf16[16,2,16,256]{3,2,1,0:T(8,128)(2,1)} %shard_map.68.refs_1_), calls=%async_computation | async-start | bytes 524288 | tf_op jit(solution)/shard_map/all_to_all | solution.py:429
  (2 other events, 26.5 us)
